TPU v7x, 32 devices: a whole 2x2x4 slice. The times are simulated.
32 devices in a mesh: parts: 2 (over y), tensor: 4 (over z), dp: 4 (over x, core).
Axes of the slice: x: 2, y: 2, z: 4, core: 2. Of those that a mesh axis runs over, the one named last changes fastest.
Arguments:
- hidden_acts: bfloat16 [2048, 28672], P(('parts', 'dp'), 'tensor'), parts along dimension 0, may hold values from -6 to 6
- output_grad: bfloat16 [4, 4, 512, 2048], P('tensor', None, None, ('parts', 'dp')), parts along dimension 3, may hold values from -6 to 6
- down_weight: bfloat16 [4, 4, 512, 28672], P(None, 'dp', None, 'tensor'), may hold values from -0.0625 to 0.0625
- input_basis: bfloat16 [28672, 64], P('tensor'), may hold values from -0.03125 to 0.03125
- output_basis: bfloat16 [4, 4, 512, 64], P('tensor'), may hold values from -0.0625 to 0.0625
- token_example: int32 [8, 256], P(('parts', 'dp')), parts along dimension 0, may hold values from 0 to 3, never falling along the last dimension, each value on 1 to 128 neighbouring positions
- example_group: int32 [32], P(('parts', 'dp')), parts along dimension 0, may hold values from 0 to 7
Outputs:
- hidden_grad: bfloat16 [2048, 28672], P(('parts', 'dp'), 'tensor'), parts along dimension 0
- fisher: float32 [8192, 4096], P(('parts', 'dp'), 'tensor'), parts along dimension 0
- group_grad: float32 [16, 4096], P('parts', 'tensor'), parts along dimension 0
There are 2 independent parts, one for each index of `parts`. A program takes and returns all parts, laid end to end along the dimension named above; an argument that names none is the same for every part. Nothing has to cross between parts.
Inputs may be any that keep to these rules, and one draw needn't show every extreme that they name: `token_example`: within each row the ids never fall, and each of the 4 examples takes 1 to 128 consecutive tokens.
All inputs are finite; a program needn't handle non-finite values.
Results may differ from a plain program's by a relative error of at most 0.009.
Values may be sent and summed in bfloat16 or wider, within the bound.
No kernel may reach another device: no remote copies, remote signals or barrier semaphores. Data moves between devices by JAX's collectives and lax.ppermute only.
A program may use at most 128 MiB of HBM per device.

v0:
```python
import jax
import jax.numpy as jnp
from jax import lax
from jax.sharding import PartitionSpec as P

GROUPS = 8


highest = lax.Precision.HIGHEST


def feature_dot(grad_block, weight_block):
    return lax.dot_general(
        grad_block,
        weight_block,
        (((0, 1, 2), (0, 1, 2)), ((), ())),
        preferred_element_type=jnp.float32,
    )


def example_gradients(acts_low, grads_low, local_ids, examples):
    onehot = (local_ids[:, None] == jnp.arange(examples, dtype=jnp.int32)[None, :]).astype(
        jnp.float32
    )
    counts = jnp.sum(onehot, axis=0)
    spread = (onehot[:, :, None] * acts_low[:, None, :]).reshape(onehot.shape[0], -1)
    outer_sum = lax.dot_general(
        spread,
        grads_low,
        (((0,), (0,)), ((), ())),
        precision=highest,
        preferred_element_type=jnp.float32,
    )
    basis_rank = acts_low.shape[1]
    outer_sum = outer_sum.reshape(examples, basis_rank * grads_low.shape[1]) / counts[:, None]
    return outer_sum.astype(jnp.bfloat16)


def per_device(
    hidden_acts, output_grad, down_weight, input_basis, output_basis, token_example, example_group
):
    acts_part = jnp.dot(hidden_acts, input_basis, preferred_element_type=jnp.float32)
    grads_part = feature_dot(output_grad, output_basis)
    acts_low, grads_low = lax.psum((acts_part, grads_part), "tensor")
    features = lax.all_gather(output_grad, "tensor", axis=0, tiled=True)
    columns = lax.all_to_all(features, "dp", split_axis=1, concat_axis=3, tiled=True)
    hidden_grad = lax.psum_scatter(
        feature_dot(columns, down_weight).astype(jnp.bfloat16),
        "dp",
        scatter_dimension=0,
        tiled=True,
    )
    example_grad = example_gradients(acts_low, grads_low, token_example[0], example_group.shape[0])
    flat_width = example_grad.shape[1]
    row_count = flat_width // lax.axis_size("dp")
    col_count = flat_width // lax.axis_size("tensor")
    col_start = lax.axis_index("tensor") * col_count
    own_cols = lax.dynamic_slice_in_dim(example_grad, col_start, col_count, 1)
    row_start = lax.axis_index("dp") * row_count
    shard_piece = lax.all_gather(example_grad, "dp", axis=0, tiled=True)
    rows_part = lax.dynamic_slice_in_dim(shard_piece, row_start, row_count, 1)
    cols_part = lax.dynamic_slice_in_dim(shard_piece, col_start, col_count, 1)
    fisher = lax.dot_general(
        rows_part, cols_part, (((0,), (0,)), ((), ())), preferred_element_type=jnp.float32
    )
    member = (example_group[:, None] == jnp.arange(GROUPS, dtype=jnp.int32)[None, :]).astype(
        jnp.bfloat16
    )
    local_totals = lax.dot_general(
        member, own_cols, (((0,), (0,)), ((), ())), preferred_element_type=jnp.float32
    )
    group_grad = lax.psum(local_totals, "dp")
    return (hidden_grad, fisher, group_grad)


def solution(mesh):
    return jax.shard_map(
        per_device,
        mesh=mesh,
        in_specs=(
            P(("parts", "dp"), "tensor"),
            P("tensor", None, None, ("parts", "dp")),
            P(None, "dp", None, "tensor"),
            P("tensor", None),
            P("tensor", None, None, None),
            P(("parts", "dp"), None),
            P(("parts", "dp")),
        ),
        out_specs=(
            P(("parts", "dp"), "tensor"),
            P(("parts", "dp"), "tensor"),
            P("parts", "tensor"),
        ),
        check_vma=False,
    )
```

profile of v0, /device:TPU:0, one launch (start us, length us, event | category | flops | bytes accessed | tf_op | source)
XLA Modules:
  0.0 312.6 jit_solution(11690185493150369994)
XLA Ops:
  7.2 0.0 copy-start
  7.2 0.0 all-gather.3.cloned.1.call-start
  7.2 0.7 all-gather.3.cloned.1.call-update
  7.9 85.2 %all-gather.3.cloned.1.call-done = bf16[4,4,512,256]{3,2,1,0:T(8,128)(2,1)} async-done(((bf16[1,4,512,256]{3,2,1,0:T(8,128)(2,1)}), bf16[4,4,512,256]{3,2,1,0:T(8,128)(2,1)}) %all-gather.3.cloned.1.call-update) | async-done | bytes 4194320 | tf_op jit(solution)/shard_map/all_gather | solution.py:45
  93.1 4.6 %copy.14 = bf16[4,4,512,256]{3,2,0,1:T(8,128)(2,1)} copy(bf16[4,4,512,256]{3,2,1,0:T(8,128)(2,1)} %all-gather.3.cloned.1.call-done) | data formatting | bytes 8388608 | tf_op jit(solution)/shard_map/all_gather | solution.py:45
  97.7 0.0 copy-start.2
  97.7 0.0 copy-start.3
  97.7 5.0 %all-to-all-start = ((bf16[4,4,512,256]{3,2,0,1:T(8,128)(2,1)}), bf16[4,4,512,256]{3,2,0,1:T(8,128)(2,1)}, u32[]{:S(2)}, u32[]{:S(2)}) async-start(bf16[4,4,512,256]{3,2,0,1:T(8,128)(2,1)} %copy.14), calls=%async_computation | async-start | bytes 8388608 | tf_op jit(solution)/shard_map/all_to_all | solution.py:46
  102.6 0.0 all-reduce.3.cloned.1.call-start
  102.7 0.0 copy-done.2
  102.7 0.0 copy-done.3
  102.7 0.9 convolution_bitcast_fusion
  103.6 0.0 copy-done
  103.6 3.9 %fusion.16 = f32[256,64]{0,1:T(8,128)} fusion(bf16[256,7168]{1,0:T(8,128)(2,1)} %param.7, bf16[7168,64]{0,1:T(8,128)(2,1)S(1)} %copy-done), kind=kOutput, calls=%fused_computation.20 | convolution fusion | flops 234881024 | bytes 4653056 | tf_op jit(solution)/shard_map/dot_general | solution.py:42
  107.5 0.0 all-reduce.3.cloned.1.call-update
  107.5 0.0 reduce-scatter.2.cloned.1.call-start
  107.6 43.3 %all-to-all-done = bf16[4,4,512,256]{3,2,0,1:T(8,128)(2,1)} async-done(((bf16[4,4,512,256]{3,2,0,1:T(8,128)(2,1)}), bf16[4,4,512,256]{3,2,0,1:T(8,128)(2,1)}, u32[]{:S(2)}, u32[]{:S(2)}) %all-to-all-start) | async-done | bytes 4194336 | tf_op jit(solution)/shard_map/all_to_all | solution.py:46
  150.9 7.3 %copy.15 = bf16[4,1,512,4,256]{2,4,3,0,1:T(8,128)(2,1)} copy(bf16[4,1,512,4,256]{4,2,0,3,1:T(8,128)(2,1)} %bitcast.1) | data formatting | bytes 8388608 | tf_op jit(solution)/shard_map/all_to_all | solution.py:46
  158.1 37.1 %bitcast_convert_fusion = bf16[1024,7168]{1,0:T(8,128)(2,1)} fusion(bf16[4,512,1024]{1,2,0:T(8,128)(2,1)} %bitcast.28, bf16[4,1,512,7168]{3,2,1,0:T(8,128)(2,1)} %param.9), kind=kOutput, calls=%fused_computation | convolution fusion | flops 30072111104 | bytes 48234496 | tf_op jit(solution)/shard_map/dot_general | solution.py:13
  195.3 0.0 copy-start.4
  195.3 0.0 copy-start.5
  195.3 0.0 reduce-scatter.2.cloned.1.call-update
  195.3 0.0 copy-start.1
  195.3 0.6 copy-done.4
  195.9 0.1 fusion.15
  196.1 0.0 all-reduce.3.cloned.1.call-done
  196.1 0.9 broadcast_multiply_fusion
  197.0 1.2 fusion.17
  198.2 0.1 reshape.58
  198.3 0.1 fusion.23
  198.4 5.4 %all-gather = bf16[4,4,4096]{2,1,0:T(4,128)(2,1)S(1)} all-gather(bf16[1,4,4096]{2,1,0:T(4,128)(2,1)S(1)} %fusion.23), channel_id=1, replica_groups=mesh['parts'=2,'tensor'=4,'dp'=4] {'dp'}, dimensions={0}, use_global_device_ids=true | all-gather | bytes 163840 | tf_op jit(solution)/shard_map/all_gather | solution.py:60
  203.8 0.1 divide_convert_fusion
  203.9 0.0 copy-done.5
  203.9 0.3 fusion.9
  204.2 11.1 %psum.23 = f32[8,1024]{1,0:T(8,128)} all-reduce(f32[8,1024]{1,0:T(8,128)S(1)} %fusion.9), channel_id=1, replica_groups=mesh['parts'=2,'tensor'=4,'dp'=4] {'dp'}, use_global_device_ids=true, to_apply=%region_4.0 | all-reduce | flops 8192 | bytes 65536 | tf_op jit(solution)/shard_map/psum | solution.py:72
  215.3 2.7 fusion.6
  218.0 88.0 %reduce-scatter.2.cloned.1.call-done = bf16[256,7168]{1,0:T(8,128)(2,1)} async-done(((bf16[1024,7168]{1,0:T(8,128)(2,1)}), bf16[256,7168]{1,0:T(8,128)(2,1)}) %reduce-scatter.2.cloned.1.call-update) | async-done | bytes 3670032 | tf_op jit(solution)/shard_map/reduce_scatter | solution.py:47
  306.0 0.0 copy-done.1
  (2 shorter events, 0.0 us)
Async XLA Ops:
  7.2 96.5 %copy-start = (bf16[7168,64]{0,1:T(8,128)(2,1)S(1)}, bf16[7168,64]{0,1:T(8,128)(2,1)}, u32[]{:S(2)}) copy-start(bf16[7168,64]{0,1:T(8,128)(2,1)} %param.10) | copy-start | bytes 2752516
  7.2 85.9 %all-gather.3.cloned.1.call-start = ((), (), s32[]{:S(2)}) async-start(), calls=%async_computation.2 | async-start | bytes 5242880 | tf_op jit(solution)/shard_map/all_gather | solution.py:45
  97.7 5.0 %copy-start.2 = (bf16[1,4,512,256]{3,2,1,0:T(8,128)(2,1)S(1)}, bf16[1,4,512,256]{3,2,1,0:T(8,128)(2,1)}, u32[]{:S(2)}) copy-start(bf16[1,4,512,256]{3,2,1,0:T(8,128)(2,1)} %param.8) | copy-start | bytes 3145732
  97.7 5.0 %copy-start.3 = (bf16[1,4,512,64]{2,3,1,0:T(8,128)(2,1)S(1)}, bf16[1,4,512,64]{2,3,1,0:T(8,128)(2,1)}, u32[]{:S(2)}) copy-start(bf16[1,4,512,64]{2,3,1,0:T(8,128)(2,1)} %param.11) | copy-start | bytes 786436
  97.7 53.2 %all-to-all-start = ((bf16[4,4,512,256]{3,2,0,1:T(8,128)(2,1)}), bf16[4,4,512,256]{3,2,0,1:T(8,128)(2,1)}, u32[]{:S(2)}, u32[]{:S(2)}) async-start(bf16[4,4,512,256]{3,2,0,1:T(8,128)(2,1)} %copy.14), calls=%async_computation | async-start | bytes 8388608 | tf_op jit(solution)/shard_map/all_to_all | solution.py:46
  102.6 93.4 %all-reduce.3.cloned.1.call-start = ((), (), s32[]{:S(2)}) async-start(), calls=%async_computation.4 | async-start | bytes 262144 | tf_op jit(solution)/shard_map/psum | solution.py:44
  107.5 198.5 %reduce-scatter.2.cloned.1.call-start = ((), (), s32[]{:S(2)}) async-start(), calls=%async_computation.3 | async-start | bytes 18350080 | tf_op jit(solution)/shard_map/reduce_scatter | solution.py:47
  195.3 0.7 copy-start.4
  195.3 8.7 %copy-start.5 = (s32[4]{0:T(128)S(1)}, s32[4]{0:T(128)}, u32[]{:S(2)}) copy-start(s32[4]{0:T(128)} %param.13) | copy-start | bytes 52
  195.3 110.8 %copy-start.1 = (bf16[7168,64]{0,1:T(8,128)(2,1)S(1)}, bf16[7168,64]{0,1:T(8,128)(2,1)}, u32[]{:S(2)}) copy-start(bf16[7168,64]{0,1:T(8,128)(2,1)} %param.10) | copy-start | bytes 2752516
Sparse Core Ops, SparseCore 0:
  9.6 83.4 all-gather.2
  107.7 33.4 all-reduce.2
  195.4 110.5 reduce-scatter.1
where the time goes:
time: 313 us
  waiting for transfers between devices  217 us (69%)
  matrix products  46.1 us (15%)
  blocking collectives  16.5 us (5%)
  between operations  13.8 us (4%)
  local copies, waits for them, and re-layouts  12.6 us (4%)
  starting transfers between devices  5.09 us (2%)
    reduce_scatter x1, waiting for transfers between devices, per_device(): lax.psum_scatter(feature_dot(columns, down_weight).astype(jnp.bfloat16),...  88 us
    all_gather x1, waiting for transfers between devices, per_device(): features = lax.all_gather(output_grad, 'tensor', axis=0, tiled=True)  85.2 us
    all_to_all x1, waiting for transfers between devices, per_device(): lax.all_to_all(features, 'dp', split_axis=1, concat_axis=3, tiled=True)  43.3 us
    dot_general x2, matrix products, feature_dot(): lax.dot_general(grad_block, weight_block, (((0, 1, 2), (0, 1, 2)), ((), (...  38.1 us
    psum x1, blocking collectives, per_device(): group_grad = lax.psum(local_totals, 'dp')  11.1 us
    all_to_all x1, local copies, waits for them, and re-layouts, per_device(): lax.all_to_all(features, 'dp', split_axis=1, concat_axis=3, tiled=True)  7.27 us
  transfers between devices with their start and end apart: 4, of which 3 were waited for; matrix products, arithmetic and copies ran while one was open for 17% of the time, Pallas kernels for 0%

commit v1 on v0

--- a/solution.py
+++ b/solution.py
@@ -36,14 +36,42 @@
     return outer_sum.astype(jnp.bfloat16)
 
 
+def fisher_and_groups(example_grad, example_group):
+    flat_width = example_grad.shape[1]
+    row_count = flat_width // lax.axis_size("dp")
+    col_count = flat_width // lax.axis_size("tensor")
+    col_start = lax.axis_index("tensor") * col_count
+    row_start = lax.axis_index("dp") * row_count
+    group_column = jnp.broadcast_to(
+        example_group.astype(jnp.bfloat16)[:, None], (example_grad.shape[0], 128)
+    )
+    every = lax.all_gather(
+        jnp.concatenate([example_grad, group_column], axis=1), "dp", axis=0, tiled=True
+    )
+    every_grad = every[:, :flat_width]
+    every_group = every[:, flat_width].astype(jnp.int32)
+    rows_part = lax.dynamic_slice_in_dim(every_grad, row_start, row_count, 1)
+    cols_part = lax.dynamic_slice_in_dim(every_grad, col_start, col_count, 1)
+    fisher = lax.dot_general(
+        rows_part, cols_part, (((0,), (0,)), ((), ())), preferred_element_type=jnp.float32
+    )
+    member = (every_group[:, None] == jnp.arange(GROUPS, dtype=jnp.int32)[None, :]).astype(
+        jnp.bfloat16
+    )
+    group_grad = lax.dot_general(
+        member, cols_part, (((0,), (0,)), ((), ())), preferred_element_type=jnp.float32
+    )
+    return fisher, group_grad
+
+
 def per_device(
     hidden_acts, output_grad, down_weight, input_basis, output_basis, token_example, example_group
 ):
+    pieces = lax.all_to_all(output_grad, "dp", split_axis=1, concat_axis=3, tiled=True)
+    columns = lax.all_gather(pieces, "tensor", axis=0, tiled=True)
     acts_part = jnp.dot(hidden_acts, input_basis, preferred_element_type=jnp.float32)
     grads_part = feature_dot(output_grad, output_basis)
     acts_low, grads_low = lax.psum((acts_part, grads_part), "tensor")
-    features = lax.all_gather(output_grad, "tensor", axis=0, tiled=True)
-    columns = lax.all_to_all(features, "dp", split_axis=1, concat_axis=3, tiled=True)
     hidden_grad = lax.psum_scatter(
         feature_dot(columns, down_weight).astype(jnp.bfloat16),
         "dp",
@@ -51,25 +79,7 @@
         tiled=True,
     )
     example_grad = example_gradients(acts_low, grads_low, token_example[0], example_group.shape[0])
-    flat_width = example_grad.shape[1]
-    row_count = flat_width // lax.axis_size("dp")
-    col_count = flat_width // lax.axis_size("tensor")
-    col_start = lax.axis_index("tensor") * col_count
-    own_cols = lax.dynamic_slice_in_dim(example_grad, col_start, col_count, 1)
-    row_start = lax.axis_index("dp") * row_count
-    shard_piece = lax.all_gather(example_grad, "dp", axis=0, tiled=True)
-    rows_part = lax.dynamic_slice_in_dim(shard_piece, row_start, row_count, 1)
-    cols_part = lax.dynamic_slice_in_dim(shard_piece, col_start, col_count, 1)
-    fisher = lax.dot_general(
-        rows_part, cols_part, (((0,), (0,)), ((), ())), preferred_element_type=jnp.float32
-    )
-    member = (example_group[:, None] == jnp.arange(GROUPS, dtype=jnp.int32)[None, :]).astype(
-        jnp.bfloat16
-    )
-    local_totals = lax.dot_general(
-        member, own_cols, (((0,), (0,)), ((), ())), preferred_element_type=jnp.float32
-    )
-    group_grad = lax.psum(local_totals, "dp")
+    fisher, group_grad = fisher_and_groups(example_grad, example_group)
     return (hidden_grad, fisher, group_grad)
 
 

time: 313 us -> 271 us (0.87)
  waiting for transfers between devices: 217 us -> 178 us
  local copies, waits for them, and re-layouts: 12.6 us -> 3.71 us
  blocking collectives: 16.5 us -> 25 us
  starting transfers between devices: 5.09 us -> 0.12 us
    all_to_all x1 -> x0, waiting for transfers between devices: 43.3 us -> none  [per_device(): lax.all_to_all(features, 'dp', split_axis=1, concat_axis=3, tiled=True)]
    all_to_all x0 -> x1, blocking collectives: none -> 19.5 us  [per_device(): lax.all_to_all(output_grad, 'dp', split_axis=1, concat_axis=3, tiled=True)]
    reduce_scatter x1, waiting for transfers between devices: 88 us -> 101 us  [per_device(): lax.psum_scatter(feature_dot(columns, down_weight).astype(jnp.bfloat16),...]
    psum x1 -> x0, blocking collectives: 11.1 us -> none  [per_device(): group_grad = lax.psum(local_totals, 'dp')]
    all_gather x1, waiting for transfers between devices: 85.2 us -> 77.1 us  [per_device(): columns = lax.all_gather(pieces, 'tensor', axis=0, tiled=True)]
    all_to_all x1 -> x0, starting transfers between devices: 4.97 us -> none  [per_device(): lax.all_to_all(features, 'dp', split_axis=1, concat_axis=3, tiled=True)]
    all_gather x1 -> x0, local copies, waits for them, and re-layouts: 4.57 us -> none  [per_device(): features = lax.all_gather(output_grad, 'tensor', axis=0, tiled=True)]
    all_to_all x1 -> x2, local copies, waits for them, and re-layouts: 7.27 us -> 2.8 us  [per_device(): lax.all_to_all(output_grad, 'dp', split_axis=1, concat_axis=3, tiled=True)]
  transfers between devices with their start and end apart: 4 -> 3, of which waited for: 3 -> 2; matrix products, arithmetic and copies ran while one was open for 17% -> 18% of each run, Pallas kernels for 0% -> 0%
where the time goes in v1:
time: 271 us; the launch traced here: 270 us
  waiting for transfers between devices  178 us (66%)
  matrix products  48 us (18%)
  blocking collectives  25 us (9%)
  between operations  13.8 us (5%)
  local copies, waits for them, and re-layouts  3.71 us (1%)
    reduce_scatter x1, waiting for transfers between devices, per_device(): lax.psum_scatter(feature_dot(columns, down_weight).astype(jnp.bfloat16),...  101 us
    all_gather x1, waiting for transfers between devices, per_device(): columns = lax.all_gather(pieces, 'tensor', axis=0, tiled=True)  77.1 us
    dot_general x2, matrix products, feature_dot(): lax.dot_general(grad_block, weight_block, (((0, 1, 2), (0, 1, 2)), ((), (...  38.8 us
    all_to_all x1, blocking collectives, per_device(): lax.all_to_all(output_grad, 'dp', split_axis=1, concat_axis=3, tiled=True)  19.5 us
    all_gather x1, blocking collectives, fisher_and_groups(): lax.all_gather(jnp.concatenate([example_grad, group_column], axis=1), 'dp...  5.44 us
  transfers between devices with their start and end apart: 3, of which 2 were waited for; matrix products, arithmetic and copies ran while one was open for 18% of the time, Pallas kernels for 0%

profile of v1, /device:TPU:0, one launch (start us, length us, event | category | flops | bytes accessed | tf_op | source)
XLA Modules:
  0.0 270.1 jit_solution(5275482531739182294)
XLA Ops:
  7.2 0.0 copy-start
  7.2 0.0 copy-start.1
  7.2 0.0 copy-start.2
  7.2 0.0 all-gather.3.cloned.1.call-start
  7.2 19.5 %all_to_all.18 = bf16[1,4,512,256]{3,2,0,1:T(8,128)(2,1)} all-to-all(bf16[1,4,512,256]{3,2,0,1:T(8,128)(2,1)} %bitcast.33), channel_id=1, replica_groups=mesh['parts'=2,'tensor'=4,'dp'=4] {'dp'}, dimensions={1} | all-to-all | bytes 2097152 | tf_op jit(solution)/shard_map/all_to_all | solution.py:70
  26.8 1.5 copy.20
  28.3 1.3 copy.21
  29.6 0.0 all-gather.3.cloned.1.call-update
  29.6 0.0 all-reduce.3.cloned.1.call-start
  29.7 0.0 copy-done.1
  29.7 0.0 copy-done.2
  29.7 0.9 convolution_bitcast_fusion
  30.6 0.0 copy-done
  30.6 3.9 %fusion.17 = f32[256,64]{0,1:T(8,128)} fusion(bf16[256,7168]{1,0:T(8,128)(2,1)} %param.7, bf16[7168,64]{0,1:T(8,128)(2,1)S(1)} %copy-done), kind=kOutput, calls=%fused_computation.23 | convolution fusion | flops 234881024 | bytes 4653056 | tf_op jit(solution)/shard_map/dot_general | solution.py:72
  34.5 0.0 all-reduce.3.cloned.1.call-update
  34.5 0.0 reduce-scatter.2.cloned.1.call-start
  34.6 77.1 %all-gather.3.cloned.1.call-done = bf16[4,1,512,1024]{3,2,1,0:T(8,128)(2,1)} async-done(((bf16[1,1,512,1024]{3,2,1,0:T(8,128)(2,1)}), bf16[4,1,512,1024]{3,2,1,0:T(8,128)(2,1)}) %all-gather.3.cloned.1.call-update) | async-done | bytes 4194320 | tf_op jit(solution)/shard_map/all_gather | solution.py:71
  111.7 37.9 %bitcast_convert_fusion = bf16[1024,7168]{1,0:T(8,128)(2,1)} fusion(bf16[4,1,512,7168]{3,2,1,0:T(8,128)(2,1)} %param.9, bf16[4,1,512,1024]{3,2,1,0:T(8,128)(2,1)} %all-gather.3.cloned.1.call-done), kind=kOutput, calls=%fused_computation | convolution fusion | flops 30072111104 | bytes 48234496 | tf_op jit(solution)/shard_map/dot_general | solution.py:13
  149.6 0.0 copy-start.4
  149.6 0.0 copy-start.3
  149.6 0.0 reduce-scatter.2.cloned.1.call-update
  149.6 0.6 copy-done.4
  150.3 0.0 copy-done.3
  150.3 0.1 fusion.14
  150.4 0.0 all-reduce.3.cloned.1.call-done
  150.4 0.9 broadcast_multiply_fusion
  151.3 1.2 fusion.18
  152.5 0.1 reshape.57
  152.6 0.1 divide_convert_fusion
  152.7 0.1 broadcast_in_dim.2
  152.8 5.4 %all-gather = bf16[4,4,4224]{2,1,0:T(4,128)(2,1)S(1)} all-gather(bf16[1,4,4224]{2,1,0:T(4,128)(2,1)S(1)} %maximum_bitcast_fusion), channel_id=1, replica_groups=mesh['parts'=2,'tensor'=4,'dp'=4] {'dp'}, dimensions={0}, use_global_device_ids=true | all-gather | bytes 168960 | tf_op jit(solution)/shard_map/all_gather | solution.py:48
  158.3 0.1 convert_reduce_fusion
  158.4 3.2 %fusion.7 = f32[1024,1024]{1,0:T(8,128)} fusion(bf16[16,4096]{1,0:T(8,128)(2,1)S(1)} %slice.8, s32[]{:T(128)S(6)} %select_n.6, s32[]{:T(128)S(6)} %select_n.7), kind=kOutput, calls=%fused_computation.10 | convolution fusion | flops 33554432 | bytes 4259848 | tf_op jit(solution)/shard_map/dot_general | solution.py:55
  161.6 0.9 fusion.9
  162.5 101.1 %reduce-scatter.2.cloned.1.call-done = bf16[256,7168]{1,0:T(8,128)(2,1)} async-done(((bf16[1024,7168]{1,0:T(8,128)(2,1)}), bf16[256,7168]{1,0:T(8,128)(2,1)}) %reduce-scatter.2.cloned.1.call-update) | async-done | bytes 3670032 | tf_op jit(solution)/shard_map/reduce_scatter | solution.py:75
  (5 shorter events, 0.1 us)
Async XLA Ops:
  7.2 23.4 %copy-start = (bf16[7168,64]{0,1:T(8,128)(2,1)S(1)}, bf16[7168,64]{0,1:T(8,128)(2,1)}, u32[]{:S(2)}) copy-start(bf16[7168,64]{0,1:T(8,128)(2,1)} %param.10) | copy-start | bytes 2752516
  7.2 22.5 %copy-start.1 = (bf16[1,4,512,256]{3,2,1,0:T(8,128)(2,1)S(1)}, bf16[1,4,512,256]{3,2,1,0:T(8,128)(2,1)}, u32[]{:S(2)}) copy-start(bf16[1,4,512,256]{3,2,1,0:T(8,128)(2,1)} %param.8) | copy-start | bytes 3145732
  7.2 22.5 %copy-start.2 = (bf16[1,4,512,64]{2,3,1,0:T(8,128)(2,1)S(1)}, bf16[1,4,512,64]{2,3,1,0:T(8,128)(2,1)}, u32[]{:S(2)}) copy-start(bf16[1,4,512,64]{2,3,1,0:T(8,128)(2,1)} %param.11) | copy-start | bytes 786436
  7.2 104.5 %all-gather.3.cloned.1.call-start = ((), (), s32[]{:S(2)}) async-start(), calls=%async_computation.2 | async-start | bytes 5242880 | tf_op jit(solution)/shard_map/all_gather | solution.py:71
  29.6 120.8 %all-reduce.3.cloned.1.call-start = ((), (), s32[]{:S(2)}) async-start(), calls=%async_computation.4 | async-start | bytes 262144 | tf_op jit(solution)/shard_map/psum | solution.py:74
  34.5 229.1 %reduce-scatter.2.cloned.1.call-start = ((), (), s32[]{:S(2)}) async-start(), calls=%async_computation.3 | async-start | bytes 18350080 | tf_op jit(solution)/shard_map/reduce_scatter | solution.py:75
  149.6 0.7 copy-start.4
  149.6 0.7 copy-start.3
Sparse Core Ops, SparseCore 0:
  29.7 81.8 all-gather.2
  114.6 33.0 all-reduce.2
  151.0 112.5 reduce-scatter.1

commit v2 on v1

v2 whole, which is shorter than its diff:
```python
import functools

import jax
import jax.numpy as jnp
from jax import lax
from jax.experimental import pallas as pl
from jax.experimental.pallas import tpu as pltpu
from jax.sharding import PartitionSpec as P

GROUPS = 8
FAR_PARTS = 2
COL_PARTS = 2

highest = lax.Precision.HIGHEST
f32, bf16 = jnp.float32, jnp.bfloat16


def swap(value, step):
    size = lax.axis_size("dp")
    return lax.ppermute(value, "dp", [(d, d ^ step) for d in range(size)])


def after(value, *earlier):
    return lax.optimization_barrier((value,) + earlier)[0]


def relay(block):
    size = lax.axis_size("tensor")
    up, down = [block], [block]
    for step in range(1, size):
        up.append(
            lax.ppermute(up[-1], "tensor", [(t, t + 1) for t in range(step - 1, size - 1)])
        )
        down.append(
            lax.ppermute(down[-1], "tensor", [(t, t - 1) for t in range(1, size - step + 1)])
        )
    return [block] + up[1:] + down[1:]


def terms_kernel(size, place_ref, *refs):
    blocks, (w_ref, out_ref, feats) = refs[: 2 * size - 1], refs[2 * size - 1 :]
    own, up, down = blocks[0], blocks[1:size], blocks[size:]
    width = own.shape[1]

    @pl.when(pl.program_id(0) == 0)
    def _():
        place = place_ref[0]

        def put(source, value):
            feats[:, pl.ds(pl.multiple_of(source * width, width), width)] = value

        put(place, own[...])
        for step in range(1, size):
            source = lax.rem(place - step + size, size)

            @pl.when(place >= step)
            def _():
                put(source, up[step - 1][...])

            @pl.when(place < step)
            def _():
                put(source, down[size - step - 1][...])

    weight = w_ref[...].reshape(size * width, w_ref.shape[3])
    out_ref[...] = jnp.dot(feats[...], weight, preferred_element_type=f32).astype(bf16)


def block_terms(blocks, down_weight, col_start, cols):
    size, _, width, _ = down_weight.shape
    rows = blocks[0].shape[0]
    tile = max(n for n in range(128, 1025, 128) if cols % n == 0 and n <= 512)
    first = col_start // tile
    whole = pl.BlockSpec((rows, width), lambda j, place: (0, 0))
    return pl.pallas_call(
        functools.partial(terms_kernel, size),
        out_shape=jax.ShapeDtypeStruct((rows, cols), bf16),
        grid_spec=pltpu.PrefetchScalarGridSpec(
            num_scalar_prefetch=1,
            grid=(cols // tile,),
            in_specs=[whole] * len(blocks)
            + [pl.BlockSpec((size, 1, width, tile), lambda j, place: (0, 0, 0, j + first))],
            out_specs=pl.BlockSpec((rows, tile), lambda j, place: (0, j)),
            scratch_shapes=[pltpu.VMEM((rows, size * width), bf16)],
        ),
        compiler_params=pltpu.CompilerParams(vmem_limit_bytes=32 << 20),
        cost_estimate=pl.CostEstimate(
            flops=2 * rows * size * width * cols,
            bytes_accessed=2 * (size * width * (cols + rows) + rows * cols),
            transcendentals=0,
        ),
        name="terms",
    )(lax.axis_index("tensor").reshape(1), *blocks, down_weight)


def gathered_terms(gathered, down_weight, col_start, cols):
    weight = lax.slice_in_dim(down_weight, col_start, col_start + cols, axis=3)
    return lax.dot_general(
        gathered, weight[:, 0], (((0, 2), (0, 1)), ((), ())), preferred_element_type=f32
    ).astype(bf16)


def add(*values):
    total = values[0].astype(f32)
    for value in values[1:]:
        total = total + value.astype(f32)
    return total.astype(bf16)


def hidden_gradient(output_grad, down_weight):
    groups, cols = lax.axis_size("dp"), down_weight.shape[3]
    place = lax.axis_index("dp")
    line = lax.axis_size("tensor") <= 8 and down_weight.shape[2] % 128 == 0
    col_parts = COL_PARTS if cols % (256 * COL_PARTS) == 0 else 1
    part = cols // col_parts

    def spread(block):
        return relay(block) if line else lax.all_gather(block, "tensor", axis=0)

    def multiply(blocks, at):
        return (block_terms if line else gathered_terms)(blocks, down_weight, at * part, part)

    turned = jnp.transpose(output_grad[0], (0, 2, 1))
    pieces = [
        lax.dynamic_index_in_dim(turned, place ^ step, 0, keepdims=False) for step in range(groups)
    ]
    tokens = pieces[0].shape[0]
    rows = tokens // FAR_PARTS

    blocks = []
    for half in range(FAR_PARTS):
        cut = slice(half * rows, (half + 1) * rows)
        for step in range(2, groups, 2):
            sent = [swap(pieces[step + 1][cut], step + 1), swap(pieces[step][cut], step)]
            blocks.append(jnp.concatenate(sent))
    blocks.append(swap(pieces[1], 1))
    blocks.append(pieces[0])
    lines = []
    for block in blocks:
        if lines:
            last = lines[-1]
            block = after(block, last[len(last) // 2], last[-2]) if line else after(block, last)
        lines.append(spread(block))

    calls = [(index, at) for index in range(len(lines)) for at in range(col_parts)]
    far_calls = (len(lines) - 2) * col_parts
    terms, pairs, sums, near_pairs = {}, [], {}, {}
    for count, (index, at) in enumerate(calls):
        held = lines[index]
        if count >= 2:
            ready = pairs[count - 2]
            held = [after(held[0], ready)] + held[1:] if line else after(held, ready)
        both = multiply(held, at)
        if count < far_calls:
            half, step = divmod(index, groups // 2 - 1)
            pair = add(both[rows:], swap(both[:rows], 1))
            sums.setdefault((half, at), []).append(swap(pair, 2 * step + 2))
            pairs.append(pair)
        else:
            terms[index, at] = both
            if index == len(lines) - 2:
                near_pairs[at] = swap(both, 1)
                pairs.append(both)
    result = jnp.zeros((tokens, cols), bf16)
    for (half, at), arrived in sums.items():
        cut = slice(half * rows, (half + 1) * rows)
        value = add(terms[len(lines) - 1, at][cut], near_pairs[at][cut], *arrived)
        result = lax.dynamic_update_slice(result, value, (half * rows, at * part))
    return result, pairs[0]


def example_gradients(acts_low, grads_low, local_ids, examples):
    onehot = (local_ids[:, None] == jnp.arange(examples, dtype=jnp.int32)[None, :]).astype(f32)
    counts = jnp.sum(onehot, axis=0)
    spread = (onehot[:, :, None] * acts_low[:, None, :]).reshape(onehot.shape[0], -1)
    outer_sum = lax.dot_general(
        spread,
        grads_low,
        (((0,), (0,)), ((), ())),
        precision=highest,
        preferred_element_type=f32,
    )
    basis_rank = acts_low.shape[1]
    outer_sum = outer_sum.reshape(examples, basis_rank * grads_low.shape[1]) / counts[:, None]
    return outer_sum.astype(bf16)


def fisher_and_groups(example_grad, example_group):
    flat_width = example_grad.shape[1]
    row_count = flat_width // lax.axis_size("dp")
    col_count = flat_width // lax.axis_size("tensor")
    col_start = lax.axis_index("tensor") * col_count
    row_start = lax.axis_index("dp") * row_count
    group_column = jnp.broadcast_to(
        example_group.astype(bf16)[:, None], (example_grad.shape[0], 128)
    )
    held = jnp.concatenate([example_grad, group_column], axis=1)
    every = jnp.concatenate(
        [held] + [swap(held, step) for step in range(1, lax.axis_size("dp"))], axis=0
    )
    every_group = every[:, flat_width].astype(jnp.int32)
    rows_part = lax.dynamic_slice_in_dim(every, row_start, row_count, 1)
    cols_part = lax.dynamic_slice_in_dim(every, col_start, col_count, 1)
    fisher = lax.dot_general(
        rows_part, cols_part, (((0,), (0,)), ((), ())), preferred_element_type=f32
    )
    member = (every_group[:, None] == jnp.arange(GROUPS, dtype=jnp.int32)[None, :]).astype(bf16)
    group_grad = lax.dot_general(
        member, cols_part, (((0,), (0,)), ((), ())), preferred_element_type=f32
    )
    return fisher, group_grad


def per_device(
    hidden_acts, output_grad, down_weight, input_basis, output_basis, token_example, example_group
):
    hidden_grad, first_pair = hidden_gradient(output_grad, down_weight)
    acts_part = jnp.dot(hidden_acts, input_basis, preferred_element_type=f32)
    grads_part = lax.dot_general(
        output_grad,
        output_basis,
        (((0, 1, 2), (0, 1, 2)), ((), ())),
        preferred_element_type=f32,
    )
    acts_low, grads_low = lax.psum((acts_part, grads_part), "tensor")
    acts_low = after(acts_low, first_pair)
    grads_low = after(grads_low, first_pair)
    example_grad = example_gradients(acts_low, grads_low, token_example[0], example_group.shape[0])
    fisher, group_grad = fisher_and_groups(example_grad, example_group)
    return (hidden_grad, fisher, group_grad)


def solution(mesh):
    return jax.shard_map(
        per_device,
        mesh=mesh,
        in_specs=(
            P(("parts", "dp"), "tensor"),
            P("tensor", None, None, ("parts", "dp")),
            P(None, "dp", None, "tensor"),
            P("tensor", None),
            P("tensor", None, None, None),
            P(("parts", "dp"), None),
            P(("parts", "dp")),
        ),
        out_specs=(
            P(("parts", "dp"), "tensor"),
            P(("parts", "dp"), "tensor"),
            P("parts", "tensor"),
        ),
        check_vma=False,
    )
```

time: 271 us -> 279 us (1.030)
  waiting for transfers between devices: 178 us -> 94.6 us
  Pallas kernels: 0 us -> 76.3 us
  starting transfers between devices: 0.12 us -> 53.1 us
  matrix products: 48 us -> 7.65 us
  blocking collectives: 25 us -> 0 us
  local copies, waits for them, and re-layouts: 3.71 us -> 23.5 us
  other arithmetic: 1.2 us -> 7.03 us
    reduce_scatter x1 -> x0, waiting for transfers between devices: 101 us -> none  [per_device(): lax.psum_scatter(feature_dot(columns, down_weight).astype(jnp.bfloat16),...]
    ppermute x0 -> x42, waiting for transfers between devices: none -> 94.6 us  [the longest x18 49.6 us: swap(): return lax.ppermute(value, 'dp', [(d, d ^ step) for d in range(size)])]
    all_gather x1 -> x0, waiting for transfers between devices: 77.1 us -> none  [per_device(): columns = lax.all_gather(pieces, 'tensor', axis=0, tiled=True)]
    pallas_call x0 -> x8, Pallas kernels: none -> 76.3 us  [block_terms(): pl.pallas_call(functools.partial(terms_kernel, size), out_shape=jax.Shape...]
    ppermute x0 -> x42, starting transfers between devices: none -> 53.1 us  [the longest x12 25.6 us: relay(): lax.ppermute(up[-1], 'tensor', [(t, t + 1) for t in range(step - 1, size...]
    dot_general x3 -> x2, matrix products: 42.7 us -> 2.78 us  [the longest x1 1.86 us: per_device(): acts_part = jnp.dot(hidden_acts, input_basis, preferred_element_type=f32)]
    all_to_all x1 -> x0, blocking collectives: 19.5 us -> none  [per_device(): lax.all_to_all(output_grad, 'dp', split_axis=1, concat_axis=3, tiled=True)]
    unnamed x11 -> x73, local copies, waits for them, and re-layouts: 0.71 us -> 16.5 us
  transfers between devices with their start and end apart: 3 -> 43, of which waited for: 2 -> 13; matrix products, arithmetic and copies ran while one was open for 18% -> 7% of each run, Pallas kernels for 0% -> 28%
where the time goes in v2:
time: 279 us; the launch traced here: 277 us
  waiting for transfers between devices  94.6 us (34%)
  Pallas kernels  76.3 us (27%)
  starting transfers between devices  53.1 us (19%)
  local copies, waits for them, and re-layouts  23.5 us (8%)
  between operations  14.9 us (5%)
  matrix products  7.65 us (3%)
  other arithmetic  7.03 us (3%)
    pallas_call x8, Pallas kernels, block_terms(): pl.pallas_call(functools.partial(terms_kernel, size), out_shape=jax.Shape...  76.3 us
    ppermute x18, waiting for transfers between devices, swap(): return lax.ppermute(value, 'dp', [(d, d ^ step) for d in range(size)])  49.6 us
    ppermute x12, waiting for transfers between devices, relay(): lax.ppermute(down[-1], 'tensor', [(t, t - 1) for t in range(1, size - ste...  40.5 us
    ppermute x12, starting transfers between devices, relay(): lax.ppermute(up[-1], 'tensor', [(t, t + 1) for t in range(step - 1, size...  25.6 us
    unnamed x73, local copies, waits for them, and re-layouts  16.5 us
    ppermute x12, starting transfers between devices, relay(): lax.ppermute(down[-1], 'tensor', [(t, t - 1) for t in range(1, size - ste...  15.4 us
    ppermute x18, starting transfers between devices, swap(): return lax.ppermute(value, 'dp', [(d, d ^ step) for d in range(size)])  12 us
  transfers between devices with their start and end apart: 43, of which 13 were waited for; matrix products, arithmetic and copies ran while one was open for 7% of the time, Pallas kernels for 28%

profile of v2, /device:TPU:0, one launch (start us, length us, event | category | flops | bytes accessed | tf_op | source)
XLA Modules:
  0.0 277.0 jit_solution(15374798050039750937)
XLA Ops:
  7.2 2.0 constant_dynamic-slice_fusion.3
  9.5 2.4 collective-permute-start.3
  12.7 3.1 %collective-permute-done.3 = bf16[128,512]{1,0:T(8,128)(2,1)S(1)} collective-permute-done((bf16[128,512]{1,0:T(8,128)(2,1)S(1)}, bf16[128,512]{1,0:T(8,128)(2,1)S(1)}, u32[]{:S(2)}, u32[]{:S(2)}) %collective-permute-start.3) | collective-permute-done | bytes 131104 | tf_op jit(solution)/shard_map/ppermute | solution.py:20
  15.8 3.0 %collective-permute-done.4 = bf16[128,512]{1,0:T(8,128)(2,1)S(1)} collective-permute-done((bf16[128,512]{1,0:T(8,128)(2,1)S(1)}, bf16[128,512]{1,0:T(8,128)(2,1)S(1)}, u32[]{:S(2)}, u32[]{:S(2)}) %collective-permute-start.4) | collective-permute-done | bytes 131104 | tf_op jit(solution)/shard_map/ppermute | solution.py:20
  18.8 4.3 %collective-permute-start.5 = (bf16[256,512]{1,0:T(8,128)(2,1)S(1)}, bf16[256,512]{1,0:T(8,128)(2,1)S(1)}, u32[]{:S(2)}, u32[]{:S(2)}) collective-permute-start(bf16[256,512]{1,0:T(8,128)(2,1)S(1)} %constant_dynamic-update-slice_fusion.refs_0_), channel_id=1, source_target_pairs={{0,4},{4,8},{8,12},{1,5},{5,9},{9,13},{2,6},{6,10},{10,14},{3,7},{... | collective-permute-start | bytes 786440 | tf_op jit(solution)/shard_map/ppermute | solution.py:32
  23.1 1.3 collective-permute-start.8
  24.4 4.5 %collective-permute-done.5.refs_1_ = bf16[256,512]{1,0:T(8,128)(2,1)S(1)} collective-permute-done((bf16[256,512]{1,0:T(8,128)(2,1)S(1)}, bf16[256,512]{1,0:T(8,128)(2,1)S(1)}, u32[]{:S(2)}, u32[]{:S(2)}) %collective-permute-start.5) | collective-permute-done | bytes 262176 | tf_op jit(solution)/shard_map/ppermute | solution.py:32
  29.5 3.5 %collective-permute-done.8.refs_4_ = bf16[256,512]{1,0:T(8,128)(2,1)S(1)} collective-permute-done((bf16[256,512]{1,0:T(8,128)(2,1)S(1)}, bf16[256,512]{1,0:T(8,128)(2,1)S(1)}, u32[]{:S(2)}, u32[]{:S(2)}) %collective-permute-start.8) | collective-permute-done | bytes 262176 | tf_op jit(solution)/shard_map/ppermute | solution.py:35
  33.0 1.3 collective-permute-start.9
  35.0 7.2 %collective-permute-done.9.refs_5_ = bf16[256,512]{1,0:T(8,128)(2,1)S(1)} collective-permute-done((bf16[256,512]{1,0:T(8,128)(2,1)S(1)}, bf16[256,512]{1,0:T(8,128)(2,1)S(1)}, u32[]{:S(2)}, u32[]{:S(2)}) %collective-permute-start.9) | collective-permute-done | bytes 262176 | tf_op jit(solution)/shard_map/ppermute | solution.py:35
  42.2 1.3 collective-permute-start.20
  43.5 1.6 collective-permute-start.2
  46.2 3.0 %collective-permute-done.1 = bf16[128,512]{1,0:T(8,128)(2,1)S(1)} collective-permute-done((bf16[128,512]{1,0:T(8,128)(2,1)S(1)}, bf16[128,512]{1,0:T(8,128)(2,1)S(1)}, u32[]{:S(2)}, u32[]{:S(2)}) %collective-permute-start.1) | collective-permute-done | bytes 131104 | tf_op jit(solution)/shard_map/ppermute | solution.py:20
  49.2 2.9 %collective-permute-done.2 = bf16[128,512]{1,0:T(8,128)(2,1)S(1)} collective-permute-done((bf16[128,512]{1,0:T(8,128)(2,1)S(1)}, bf16[128,512]{1,0:T(8,128)(2,1)S(1)}, u32[]{:S(2)}, u32[]{:S(2)}) %collective-permute-start.2) | collective-permute-done | bytes 131104 | tf_op jit(solution)/shard_map/ppermute | solution.py:20
  52.9 5.2 %collective-permute-start.10 = (bf16[256,512]{1,0:T(8,128)(2,1)S(1)}, bf16[256,512]{1,0:T(8,128)(2,1)}, u32[]{:S(2)}, u32[]{:S(2)}) collective-permute-start(bf16[256,512]{1,0:T(8,128)(2,1)S(1)} %pad_maximum_fusion.refs_0_), channel_id=1, source_target_pairs={{0,4},{4,8},{8,12},{1,5},{5,9},{9,13},{2,6},{6,10},{10,14},{3,7},{... | collective-permute-start | bytes 786440 | tf_op jit(solution)/shard_map/ppermute | solution.py:32
  58.8 0.9 copy-done.10
  59.8 0.9 copy-done.13
  60.7 0.9 copy-done.16
  61.7 0.9 copy-done.19
  62.6 0.9 copy-done.22
  63.6 9.6 %terms.8 = bf16[256,3584]{1,0:T(8,128)(2,1)S(1)} custom-call(s32[1]{0:T(128)} %bitcast.place_ref, bf16[256,512]{1,0:T(8,128)(2,1)S(1)} %constant_dynamic-update-slice_fusion.refs_0_, bf16[256,512]{1,0:T(8,128)(2,1)S(1)} %collective-permute-done.5.refs_1_, bf16[256,512]{1,0:T(8,128)(2,1)S(1)} %copy-done.13, bf16[256,512]{1,0:T(8,128)(2,1)S(1)} %copy-done.19, ...), custom_call_target="tpu_custom_call" | custom-call | flops 3758096384 | bytes 17563648 | tf_op jit(solution)/shard_map/terms/pallas_call | solution.py:74
  73.2 1.0 slice.105
  74.3 1.9 fusion.15
  77.1 1.3 collective-permute-start.13
  78.4 1.4 collective-permute-start.11
  79.9 1.1 copy.20
  81.0 8.5 %collective-permute-done.13.refs_4_ = bf16[256,512]{1,0:T(8,128)(2,1)S(1)} collective-permute-done((bf16[256,512]{1,0:T(8,128)(2,1)S(1)}, bf16[256,512]{1,0:T(8,128)(2,1)S(1)}, u32[]{:S(2)}, u32[]{:S(2)}) %collective-permute-start.13) | collective-permute-done | bytes 262176 | tf_op jit(solution)/shard_map/ppermute | solution.py:35
  89.6 1.3 collective-permute-start.14
  91.6 0.9 copy-done.11
  92.5 0.9 copy-done.17
  93.5 0.9 copy-done.20
  94.4 0.9 copy-done.23
  95.4 9.5 %terms.12 = bf16[256,3584]{1,0:T(8,128)(2,1)S(1)} custom-call(s32[1]{0:T(128)} %bitcast.place_ref, bf16[256,512]{1,0:T(8,128)(2,1)S(1)} %constant_dynamic-update-slice_fusion.refs_0_, bf16[256,512]{1,0:T(8,128)(2,1)S(1)} %copy-done.8, bf16[256,512]{1,0:T(8,128)(2,1)S(1)} %copy-done.14, bf16[256,512]{1,0:T(8,128)(2,1)S(1)} %copy-done.20, ...), custom_call_target="tpu_custom_call" | custom-call | flops 3758096384 | bytes 17563648 | tf_op jit(solution)/shard_map/terms/pallas_call | solution.py:74
  104.9 1.2 copy-done.2
  106.1 1.0 slice.111
  107.1 1.3 collective-permute-start.22
  109.1 1.3 collective-permute-start.18
  110.4 5.2 %collective-permute-start.15 = (bf16[256,512]{1,0:T(8,128)(2,1)}, bf16[256,512]{1,0:T(8,128)(2,1)S(1)}, u32[]{:S(2)}, u32[]{:S(2)}) collective-permute-start(bf16[256,512]{1,0:T(8,128)(2,1)} %collective-permute-done.refs_0_), channel_id=1, source_target_pairs={{0,4},{4,8},{8,12},{1,5},{5,9},{9,13},{2,6},{6,10},{10,14},{3,7},{... | collective-permute-start | bytes 786440 | tf_op jit(solution)/shard_map/ppermute | solution.py:32
  115.6 2.3 add_convert_fusion.7
  118.8 1.3 fusion.16
  120.5 1.8 collective-permute-start.40
  122.3 1.7 add_convert_fusion.4
  125.7 9.6 %terms.9 = bf16[256,3584]{1,0:T(8,128)(2,1)S(1)} custom-call(s32[1]{0:T(128)} %bitcast.place_ref, bf16[256,512]{1,0:T(8,128)(2,1)S(1)} %pad_maximum_fusion.refs_0_, bf16[256,512]{1,0:T(8,128)(2,1)} %collective-permute-done.10.refs_1_, bf16[256,512]{1,0:T(8,128)(2,1)} %collective-permute-done.11.refs_2_, bf16[256,512]{1,0:T(8,128)(2,1)S(1)} %copy-done.25, ...), custom_call_target="tpu_custom_call" | custom-call | flops 3758096384 | bytes 17563648 | tf_op jit(solution)/shard_map/terms/pallas_call | solution.py:74
  136.7 9.7 %terms.13 = bf16[256,3584]{1,0:T(8,128)(2,1)S(1)} custom-call(s32[1]{0:T(128)} %bitcast.place_ref, bf16[256,512]{1,0:T(8,128)(2,1)S(1)} %pad_maximum_fusion.refs_0_, bf16[256,512]{1,0:T(8,128)(2,1)} %collective-permute-done.10.refs_1_, bf16[256,512]{1,0:T(8,128)(2,1)} %collective-permute-done.11.refs_2_, bf16[256,512]{1,0:T(8,128)(2,1)S(1)} %copy-done.25, ...), custom_call_target="tpu_custom_call" | custom-call | flops 3758096384 | bytes 17563648 | tf_op jit(solution)/shard_map/terms/pallas_call | solution.py:74
  146.5 1.1 copy-done.32
  147.8 1.3 collective-permute-start.19
  149.9 10.5 %collective-permute-done.19.refs_5_ = bf16[256,512]{1,0:T(8,128)(2,1)S(1)} collective-permute-done((bf16[256,512]{1,0:T(8,128)(2,1)S(1)}, bf16[256,512]{1,0:T(8,128)(2,1)S(1)}, u32[]{:S(2)}, u32[]{:S(2)}) %collective-permute-start.19) | collective-permute-done | bytes 262176 | tf_op jit(solution)/shard_map/ppermute | solution.py:35
  160.5 1.3 collective-permute-start.28
  161.7 4.6 %collective-permute-start.25 = (bf16[256,512]{1,0:T(8,128)(2,1)S(1)}, bf16[256,512]{1,0:T(8,128)(2,1)S(1)}, u32[]{:S(2)}, u32[]{:S(2)}) collective-permute-start(bf16[256,512]{1,0:T(8,128)(2,1)S(1)} %bitcast.40), channel_id=1, source_target_pairs={{0,4},{4,8},{8,12},{1,5},{5,9},{9,13},{2,6},{6,10},{10,14},{3,7},{... | collective-permute-start | bytes 786440 | tf_op jit(solution)/shard_map/ppermute | solution.py:32
  167.3 3.2 %collective-permute-done.28.refs_4_ = bf16[256,512]{1,0:T(8,128)(2,1)S(1)} collective-permute-done((bf16[256,512]{1,0:T(8,128)(2,1)S(1)}, bf16[256,512]{1,0:T(8,128)(2,1)S(1)}, u32[]{:S(2)}, u32[]{:S(2)}) %collective-permute-start.28) | collective-permute-done | bytes 262176 | tf_op jit(solution)/shard_map/ppermute | solution.py:35
  170.5 1.3 collective-permute-start.24
  171.8 1.3 collective-permute-start.29
  174.0 7.6 %collective-permute-done.24.refs_6_ = bf16[256,512]{1,0:T(8,128)(2,1)S(1)} collective-permute-done((bf16[256,512]{1,0:T(8,128)(2,1)S(1)}, bf16[256,512]{1,0:T(8,128)(2,1)S(1)}, u32[]{:S(2)}, u32[]{:S(2)}) %collective-permute-start.24) | collective-permute-done | bytes 262176 | tf_op jit(solution)/shard_map/ppermute | solution.py:35
  181.6 9.5 %terms.10 = bf16[256,3584]{1,0:T(8,128)(2,1)S(1)} custom-call(s32[1]{0:T(128)} %bitcast.place_ref, bf16[256,512]{1,0:T(8,128)(2,1)} %collective-permute-done.refs_0_, bf16[256,512]{1,0:T(8,128)(2,1)S(1)} %copy-done.4, bf16[256,512]{1,0:T(8,128)(2,1)S(1)} %collective-permute-done.16.refs_2_, bf16[256,512]{1,0:T(8,128)(2,1)S(1)} %collective-permute-done.17.refs_3_, ...), custom_call_target="tpu_custom_call" | custom-call | flops 3758096384 | bytes 17563648 | tf_op jit(solution)/shard_map/terms/pallas_call | solution.py:74
  191.4 1.3 collective-permute-start.30
  193.6 9.5 %terms.14 = bf16[256,3584]{1,0:T(8,128)(2,1)S(1)} custom-call(s32[1]{0:T(128)} %bitcast.place_ref, bf16[256,512]{1,0:T(8,128)(2,1)} %collective-permute-done.refs_0_, bf16[256,512]{1,0:T(8,128)(2,1)S(1)} %copy-done.4, bf16[256,512]{1,0:T(8,128)(2,1)S(1)} %collective-permute-done.16.refs_2_, bf16[256,512]{1,0:T(8,128)(2,1)S(1)} %collective-permute-done.17.refs_3_, ...), custom_call_target="tpu_custom_call" | custom-call | flops 3758096384 | bytes 17563648 | tf_op jit(solution)/shard_map/terms/pallas_call | solution.py:74
  203.7 2.7 fusion.5
  206.4 1.5 collective-permute-start.36
  208.4 9.5 %terms.15 = bf16[256,3584]{1,0:T(8,128)(2,1)S(1)} custom-call(s32[1]{0:T(128)} %bitcast.place_ref, bf16[256,512]{1,0:T(8,128)(2,1)S(1)} %bitcast.41, bf16[256,512]{1,0:T(8,128)(2,1)S(1)} %collective-permute-done.25.refs_1_, bf16[256,512]{1,0:T(8,128)(2,1)S(1)} %collective-permute-done.26.refs_2_, bf16[256,512]{1,0:T(8,128)(2,1)S(1)} %collective-permute-done.27.refs_3_, ...), custom_call_target="tpu_custom_call" | custom-call | flops 3758096384 | bytes 17563648 | tf_op jit(solution)/shard_map/terms/pallas_call | solution.py:74
  217.9 9.5 %terms.11 = bf16[256,3584]{1,0:T(8,128)(2,1)S(1)} custom-call(s32[1]{0:T(128)} %bitcast.place_ref, bf16[256,512]{1,0:T(8,128)(2,1)S(1)} %bitcast.42, bf16[256,512]{1,0:T(8,128)(2,1)S(1)} %collective-permute-done.25.refs_1_, bf16[256,512]{1,0:T(8,128)(2,1)S(1)} %collective-permute-done.26.refs_2_, bf16[256,512]{1,0:T(8,128)(2,1)S(1)} %collective-permute-done.27.refs_3_, ...), custom_call_target="tpu_custom_call" | custom-call | flops 3758096384 | bytes 17563648 | tf_op jit(solution)/shard_map/terms/pallas_call | solution.py:74
  227.4 1.6 collective-permute-start.38
  230.0 19.2 %collective-permute-done.37 = bf16[128,3584]{1,0:T(8,128)(2,1)S(1)} collective-permute-done((bf16[128,3584]{1,0:T(8,128)(2,1)S(1)}, bf16[128,3584]{1,0:T(8,128)(2,1)S(1)}, u32[]{:S(2)}, u32[]{:S(2)}) %collective-permute-start.37) | collective-permute-done | bytes 917536 | tf_op jit(solution)/shard_map/ppermute | solution.py:20
  249.6 18.4 %collective-permute-done.38 = bf16[128,3584]{1,0:T(8,128)(2,1)S(1)} collective-permute-done((bf16[128,3584]{1,0:T(8,128)(2,1)S(1)}, bf16[128,3584]{1,0:T(8,128)(2,1)S(1)}, u32[]{:S(2)}, u32[]{:S(2)}) %collective-permute-start.38) | collective-permute-done | bytes 917536 | tf_op jit(solution)/shard_map/ppermute | solution.py:20
  268.4 1.8 copy-done.31
  (141 shorter events, 18.7 us)
Async XLA Ops:
  7.2 67.1 %copy-start = (bf16[7168,64]{0,1:T(8,128)(2,1)S(1)}, bf16[7168,64]{0,1:T(8,128)(2,1)}, u32[]{:S(2)}) copy-start(bf16[7168,64]{0,1:T(8,128)(2,1)} %param.10) | copy-start | bytes 2752516
  7.2 110.8 %all-reduce.4.cloned.1.call-start = ((), (), s32[]{:S(2)}) async-start(), calls=%async_computation | async-start | bytes 262144 | tf_op jit(solution)/shard_map/psum | solution.py:224
  9.5 6.3 %collective-permute-start.3 = (bf16[128,512]{1,0:T(8,128)(2,1)S(1)}, bf16[128,512]{1,0:T(8,128)(2,1)S(1)}, u32[]{:S(2)}, u32[]{:S(2)}) collective-permute-start(bf16[128,512]{1,0:T(8,128)(2,1)S(1)} %get-tuple-element.32), channel_id=1, source_target_pairs={{0,3},{1,2},{2,1},{3,0},{4,7},{5,6},{6,5},{7,4},{8,11},{9,10},{10,... | collective-permute-start | bytes 393224 | tf_op jit(solution)/shard_map/ppermute | solution.py:20
  12.1 6.7 %collective-permute-start.4 = (bf16[128,512]{1,0:T(8,128)(2,1)S(1)}, bf16[128,512]{1,0:T(8,128)(2,1)S(1)}, u32[]{:S(2)}, u32[]{:S(2)}) collective-permute-start(bf16[128,512]{1,0:T(8,128)(2,1)S(1)} %get-tuple-element.34), channel_id=1, source_target_pairs={{0,2},{1,3},{2,0},{3,1},{4,6},{5,7},{6,4},{7,5},{8,10},{9,11},{10,... | collective-permute-start | bytes 393224 | tf_op jit(solution)/shard_map/ppermute | solution.py:20
  18.8 10.1 %collective-permute-start.5 = (bf16[256,512]{1,0:T(8,128)(2,1)S(1)}, bf16[256,512]{1,0:T(8,128)(2,1)S(1)}, u32[]{:S(2)}, u32[]{:S(2)}) collective-permute-start(bf16[256,512]{1,0:T(8,128)(2,1)S(1)} %constant_dynamic-update-slice_fusion.refs_0_), channel_id=1, source_target_pairs={{0,4},{4,8},{8,12},{1,5},{5,9},{9,13},{2,6},{6,10},{10,14},{3,7},{... | collective-permute-start | bytes 786440 | tf_op jit(solution)/shard_map/ppermute | solution.py:32
  23.1 9.9 %collective-permute-start.8 = (bf16[256,512]{1,0:T(8,128)(2,1)S(1)}, bf16[256,512]{1,0:T(8,128)(2,1)S(1)}, u32[]{:S(2)}, u32[]{:S(2)}) collective-permute-start(bf16[256,512]{1,0:T(8,128)(2,1)S(1)} %constant_dynamic-update-slice_fusion.refs_0_), channel_id=1, source_target_pairs={{4,0},{8,4},{12,8},{5,1},{9,5},{13,9},{6,2},{10,6},{14,10},{7,3},{... | collective-permute-start | bytes 786440 | tf_op jit(solution)/shard_map/ppermute | solution.py:35
  28.8 44.3 %copy-start.7 = (bf16[256,512]{1,0:T(8,128)(2,1)}, bf16[256,512]{1,0:T(8,128)(2,1)S(1)}, u32[]{:S(2)}) copy-start(bf16[256,512]{1,0:T(8,128)(2,1)S(1)} %collective-permute-done.5.refs_1_) | copy-start | bytes 786436
  28.9 5.4 %collective-permute-start.6 = (bf16[256,512]{1,0:T(8,128)(2,1)S(1)}, bf16[256,512]{1,0:T(8,128)(2,1)S(1)}, u32[]{:S(2)}, u32[]{:S(2)}) collective-permute-start(bf16[256,512]{1,0:T(8,128)(2,1)S(1)} %collective-permute-done.5.refs_1_), channel_id=1, source_target_pairs={{4,8},{8,12},{5,9},{9,13},{6,10},{10,14},{7,11},{11,15},{20,24},{2... | collective-permute-start | bytes 786440 | tf_op jit(solution)/shard_map/ppermute | solution.py:32
  33.0 16.2 %copy-start.9 = (bf16[256,512]{1,0:T(8,128)(2,1)}, bf16[256,512]{1,0:T(8,128)(2,1)S(1)}, u32[]{:S(2)}) copy-start(bf16[256,512]{1,0:T(8,128)(2,1)S(1)} %collective-permute-done.8.refs_4_) | copy-start | bytes 786436
  33.0 9.2 %collective-permute-start.9 = (bf16[256,512]{1,0:T(8,128)(2,1)S(1)}, bf16[256,512]{1,0:T(8,128)(2,1)S(1)}, u32[]{:S(2)}, u32[]{:S(2)}) collective-permute-start(bf16[256,512]{1,0:T(8,128)(2,1)S(1)} %collective-permute-done.8.refs_4_), channel_id=1, source_target_pairs={{4,0},{8,4},{5,1},{9,5},{6,2},{10,6},{7,3},{11,7},{20,16},{24,20},... | collective-permute-start | bytes 786440 | tf_op jit(solution)/shard_map/ppermute | solution.py:35
  34.3 23.8 %copy-start.12 = (bf16[256,512]{1,0:T(8,128)(2,1)}, bf16[256,512]{1,0:T(8,128)(2,1)S(1)}, u32[]{:S(2)}) copy-start(bf16[256,512]{1,0:T(8,128)(2,1)S(1)} %collective-permute-done.6.refs_2_) | copy-start | bytes 786436
  34.3 17.9 %collective-permute-start.7 = (bf16[256,512]{1,0:T(8,128)(2,1)S(1)}, bf16[256,512]{1,0:T(8,128)(2,1)S(1)}, u32[]{:S(2)}, u32[]{:S(2)}) collective-permute-start(bf16[256,512]{1,0:T(8,128)(2,1)S(1)} %collective-permute-done.6.refs_2_), channel_id=1, source_target_pairs={{8,12},{9,13},{10,14},{11,15},{24,28},{25,29},{26,30},{27,31}} | collective-permute-start | bytes 786440 | tf_op jit(solution)/shard_map/ppermute | solution.py:32
  42.2 15.9 %copy-start.15 = (bf16[256,512]{1,0:T(8,128)(2,1)}, bf16[256,512]{1,0:T(8,128)(2,1)S(1)}, u32[]{:S(2)}) copy-start(bf16[256,512]{1,0:T(8,128)(2,1)S(1)} %collective-permute-done.9.refs_5_) | copy-start | bytes 786436
  42.2 15.9 %collective-permute-start.20 = (bf16[256,512]{1,0:T(8,128)(2,1)S(1)}, bf16[256,512]{1,0:T(8,128)(2,1)S(1)}, u32[]{:S(2)}, u32[]{:S(2)}) collective-permute-start(bf16[256,512]{1,0:T(8,128)(2,1)S(1)} %collective-permute-done.9.refs_5_), channel_id=1, source_target_pairs={{4,0},{5,1},{6,2},{7,3},{20,16},{21,17},{22,18},{23,19}} | collective-permute-start | bytes 786440 | tf_op jit(solution)/shard_map/ppermute | solution.py:35
  43.5 5.7 %collective-permute-start.1 = (bf16[128,512]{1,0:T(8,128)(2,1)S(1)}, bf16[128,512]{1,0:T(8,128)(2,1)S(1)}, u32[]{:S(2)}, u32[]{:S(2)}) collective-permute-start(bf16[128,512]{1,0:T(8,128)(2,1)S(1)} %get-tuple-element.31), channel_id=1, source_target_pairs={{0,3},{1,2},{2,1},{3,0},{4,7},{5,6},{6,5},{7,4},{8,11},{9,10},{10,... | collective-permute-start | bytes 393224 | tf_op jit(solution)/shard_map/ppermute | solution.py:20
  43.5 8.6 %collective-permute-start.2 = (bf16[128,512]{1,0:T(8,128)(2,1)S(1)}, bf16[128,512]{1,0:T(8,128)(2,1)S(1)}, u32[]{:S(2)}, u32[]{:S(2)}) collective-permute-start(bf16[128,512]{1,0:T(8,128)(2,1)S(1)} %get-tuple-element.33), channel_id=1, source_target_pairs={{0,2},{1,3},{2,0},{3,1},{4,6},{5,7},{6,4},{7,5},{8,10},{9,11},{10,... | collective-permute-start | bytes 393224 | tf_op jit(solution)/shard_map/ppermute | solution.py:20
  46.0 62.4 %collective-permute-start = (bf16[256,512]{1,0:T(8,128)(2,1)}, bf16[256,512]{1,0:T(8,128)(2,1)}, u32[]{:S(2)}, u32[]{:S(2)}) collective-permute-start(bf16[256,512]{1,0:T(8,128)(2,1)} %bitcast.6), channel_id=1, source_target_pairs={{0,1},{1,0},{2,3},{3,2},{4,5},{5,4},{6,7},{7,6},{8,9},{9,8},{10,11... | collective-permute-start | bytes 786440 | tf_op jit(solution)/shard_map/ppermute | solution.py:20
  52.9 25.5 %collective-permute-start.10 = (bf16[256,512]{1,0:T(8,128)(2,1)S(1)}, bf16[256,512]{1,0:T(8,128)(2,1)}, u32[]{:S(2)}, u32[]{:S(2)}) collective-permute-start(bf16[256,512]{1,0:T(8,128)(2,1)S(1)} %pad_maximum_fusion.refs_0_), channel_id=1, source_target_pairs={{0,4},{4,8},{8,12},{1,5},{5,9},{9,13},{2,6},{6,10},{10,14},{3,7},{... | collective-permute-start | bytes 786440 | tf_op jit(solution)/shard_map/ppermute | solution.py:32
  63.6 10.7 %copy-start.30 = (bf16[256,7168]{1,0:T(8,128)(2,1)S(1)}, bf16[256,7168]{1,0:T(8,128)(2,1)}, u32[]{:S(2)}) copy-start(bf16[256,7168]{1,0:T(8,128)(2,1)} %param.7) | copy-start | bytes 11010052
  74.2 2.0 copy-start.29
  74.2 2.0 copy-start.33
  74.2 5.6 %copy-start.34 = (s32[1,256]{1,0:T(1,128)S(1)}, s32[1,256]{1,0:T(1,128)}, u32[]{:S(2)}) copy-start(s32[1,256]{1,0:T(1,128)} %param.12) | copy-start | bytes 3076
  74.2 5.7 %copy-start.35 = (s32[4]{0:T(128)S(1)}, s32[4]{0:T(128)}, u32[]{:S(2)}) copy-start(s32[4]{0:T(128)} %param.13) | copy-start | bytes 52
  74.2 41.5 %collective-permute-start.21 = (bf16[128,3584]{1,0:T(8,128)(2,1)}, bf16[128,3584]{1,0:T(8,128)(2,1)}, u32[]{:S(2)}, u32[]{:S(2)}) collective-permute-start(bf16[128,3584]{1,0:T(8,128)(2,1)} %slice.105), channel_id=1, source_target_pairs={{0,1},{1,0},{2,3},{3,2},{4,5},{5,4},{6,7},{7,6},{8,9},{9,8},{10,11... | collective-permute-start | bytes 2752520 | tf_op jit(solution)/shard_map/ppermute | solution.py:20
  76.1 15.4 %copy-start.8 = (bf16[256,512]{1,0:T(8,128)(2,1)S(1)}, bf16[256,512]{1,0:T(8,128)(2,1)}, u32[]{:S(2)}) copy-start(bf16[256,512]{1,0:T(8,128)(2,1)} %copy-done.7) | copy-start | bytes 786436
  76.1 15.4 %copy-start.14 = (bf16[256,512]{1,0:T(8,128)(2,1)S(1)}, bf16[256,512]{1,0:T(8,128)(2,1)}, u32[]{:S(2)}) copy-start(bf16[256,512]{1,0:T(8,128)(2,1)} %copy-done.12) | copy-start | bytes 786436
  77.1 12.5 %collective-permute-start.13 = (bf16[256,512]{1,0:T(8,128)(2,1)S(1)}, bf16[256,512]{1,0:T(8,128)(2,1)S(1)}, u32[]{:S(2)}, u32[]{:S(2)}) collective-permute-start(bf16[256,512]{1,0:T(8,128)(2,1)S(1)} %pad_maximum_fusion.refs_0_), channel_id=1, source_target_pairs={{4,0},{8,4},{12,8},{5,1},{9,5},{13,9},{6,2},{10,6},{14,10},{7,3},{... | collective-permute-start | bytes 786440 | tf_op jit(solution)/shard_map/ppermute | solution.py:35
  78.4 12.4 %collective-permute-start.11 = (bf16[256,512]{1,0:T(8,128)(2,1)}, bf16[256,512]{1,0:T(8,128)(2,1)}, u32[]{:S(2)}, u32[]{:S(2)}) collective-permute-start(bf16[256,512]{1,0:T(8,128)(2,1)} %collective-permute-done.10.refs_1_), channel_id=1, source_target_pairs={{4,8},{8,12},{5,9},{9,13},{6,10},{10,14},{7,11},{11,15},{20,24},{2... | collective-permute-start | bytes 786440 | tf_op jit(solution)/shard_map/ppermute | solution.py:32
  89.6 15.3 %copy-start.5 = (bf16[256,512]{1,0:T(8,128)(2,1)}, bf16[256,512]{1,0:T(8,128)(2,1)S(1)}, u32[]{:S(2)}) copy-start(bf16[256,512]{1,0:T(8,128)(2,1)S(1)} %collective-permute-done.13.refs_4_) | copy-start | bytes 786436
  89.6 17.6 %collective-permute-start.14 = (bf16[256,512]{1,0:T(8,128)(2,1)S(1)}, bf16[256,512]{1,0:T(8,128)(2,1)}, u32[]{:S(2)}, u32[]{:S(2)}) collective-permute-start(bf16[256,512]{1,0:T(8,128)(2,1)S(1)} %collective-permute-done.13.refs_4_), channel_id=1, source_target_pairs={{4,0},{8,4},{5,1},{9,5},{6,2},{10,6},{7,3},{11,7},{20,16},{24,20},... | collective-permute-start | bytes 786440 | tf_op jit(solution)/shard_map/ppermute | solution.py:35
  90.9 17.6 %collective-permute-start.12 = (bf16[256,512]{1,0:T(8,128)(2,1)}, bf16[256,512]{1,0:T(8,128)(2,1)S(1)}, u32[]{:S(2)}, u32[]{:S(2)}) collective-permute-start(bf16[256,512]{1,0:T(8,128)(2,1)} %collective-permute-done.11.refs_2_), channel_id=1, source_target_pairs={{8,12},{9,13},{10,14},{11,15},{24,28},{25,29},{26,30},{27,31}} | collective-permute-start | bytes 786440 | tf_op jit(solution)/shard_map/ppermute | solution.py:32
  104.9 1.2 copy-start.2
  107.1 13.4 %collective-permute-start.33 = (bf16[128,3584]{1,0:T(8,128)(2,1)}, bf16[128,3584]{1,0:T(8,128)(2,1)}, u32[]{:S(2)}, u32[]{:S(2)}) collective-permute-start(bf16[128,3584]{1,0:T(8,128)(2,1)} %slice.111), channel_id=1, source_target_pairs={{0,1},{1,0},{2,3},{3,2},{4,5},{5,4},{6,7},{7,6},{8,9},{9,8},{10,11... | collective-permute-start | bytes 2752520 | tf_op jit(solution)/shard_map/ppermute | solution.py:20
  107.1 16.9 %collective-permute-start.22 = (bf16[256,512]{1,0:T(8,128)(2,1)}, bf16[256,512]{1,0:T(8,128)(2,1)S(1)}, u32[]{:S(2)}, u32[]{:S(2)}) collective-permute-start(bf16[256,512]{1,0:T(8,128)(2,1)} %collective-permute-done.14.refs_5_), channel_id=1, source_target_pairs={{4,0},{5,1},{6,2},{7,3},{20,16},{21,17},{22,18},{23,19}} | collective-permute-start | bytes 786440 | tf_op jit(solution)/shard_map/ppermute | solution.py:35
  109.1 38.7 %collective-permute-start.18 = (bf16[256,512]{1,0:T(8,128)(2,1)}, bf16[256,512]{1,0:T(8,128)(2,1)S(1)}, u32[]{:S(2)}, u32[]{:S(2)}) collective-permute-start(bf16[256,512]{1,0:T(8,128)(2,1)} %collective-permute-done.refs_0_), channel_id=1, source_target_pairs={{4,0},{8,4},{12,8},{5,1},{9,5},{13,9},{6,2},{10,6},{14,10},{7,3},{... | collective-permute-start | bytes 786440 | tf_op jit(solution)/shard_map/ppermute | solution.py:35
  110.4 25.6 %collective-permute-start.15 = (bf16[256,512]{1,0:T(8,128)(2,1)}, bf16[256,512]{1,0:T(8,128)(2,1)S(1)}, u32[]{:S(2)}, u32[]{:S(2)}) collective-permute-start(bf16[256,512]{1,0:T(8,128)(2,1)} %collective-permute-done.refs_0_), channel_id=1, source_target_pairs={{0,4},{4,8},{8,12},{1,5},{5,9},{9,13},{2,6},{6,10},{10,14},{3,7},{... | collective-permute-start | bytes 786440 | tf_op jit(solution)/shard_map/ppermute | solution.py:32
  118.8 5.9 %copy-start.6 = (bf16[256,512]{1,0:T(8,128)(2,1)S(1)}, bf16[256,512]{1,0:T(8,128)(2,1)}, u32[]{:S(2)}) copy-start(bf16[256,512]{1,0:T(8,128)(2,1)} %copy-done.5) | copy-start | bytes 786436
  118.8 5.9 %copy-start.25 = (bf16[256,512]{1,0:T(8,128)(2,1)S(1)}, bf16[256,512]{1,0:T(8,128)(2,1)}, u32[]{:S(2)}) copy-start(bf16[256,512]{1,0:T(8,128)(2,1)} %copy-done.24) | copy-start | bytes 786436
  120.4 15.0 %collective-permute-start.41 = (bf16[4,4224]{1,0:T(4,128)(2,1)S(1)}, bf16[4,4224]{1,0:T(4,128)(2,1)S(1)}, u32[]{:S(2)}, u32[]{:S(2)}) collective-permute-start(bf16[4,4224]{1,0:T(4,128)(2,1)S(1)} %pad_maximum_fusion.2), channel_id=1, source_target_pairs={{0,3},{1,2},{2,1},{3,0},{4,7},{5,6},{6,5},{7,4},{8,11},{9,10},{10,... | collective-permute-start | bytes 101384 | tf_op jit(solution)/shard_map/ppermute | solution.py:20
  120.5 26.0 %collective-permute-start.40 = (bf16[4,4224]{1,0:T(4,128)(2,1)S(1)}, bf16[4,4224]{1,0:T(4,128)(2,1)S(1)}, u32[]{:S(2)}, u32[]{:S(2)}) collective-permute-start(bf16[4,4224]{1,0:T(4,128)(2,1)S(1)} %pad_maximum_fusion.2), channel_id=1, source_target_pairs={{0,2},{1,3},{2,0},{3,1},{4,6},{5,7},{6,4},{7,5},{8,10},{9,11},{10,... | collective-permute-start | bytes 101384 | tf_op jit(solution)/shard_map/ppermute | solution.py:20
  124.7 23.1 %collective-permute-start.39 = (bf16[4,4224]{1,0:T(4,128)(2,1)S(1)}, bf16[4,4224]{1,0:T(4,128)(2,1)S(1)}, u32[]{:S(2)}, u32[]{:S(2)}) collective-permute-start(bf16[4,4224]{1,0:T(4,128)(2,1)S(1)} %pad_maximum_fusion.2), channel_id=1, source_target_pairs={{0,1},{1,0},{2,3},{3,2},{4,5},{5,4},{6,7},{7,6},{8,9},{9,8},{10,11... | collective-permute-start | bytes 101384 | tf_op jit(solution)/shard_map/ppermute | solution.py:20
  135.3 1.3 copy-start.28
  135.4 37.6 %collective-permute-start.23 = (bf16[128,3584]{1,0:T(8,128)(2,1)S(1)}, bf16[128,3584]{1,0:T(8,128)(2,1)S(1)}, u32[]{:S(2)}, u32[]{:S(2)}) collective-permute-start(bf16[128,3584]{1,0:T(8,128)(2,1)S(1)} %slice.107), channel_id=1, source_target_pairs={{0,1},{1,0},{2,3},{3,2},{4,5},{5,4},{6,7},{7,6},{8,9},{9,8},{10,11... | collective-permute-start | bytes 2752520 | tf_op jit(solution)/shard_map/ppermute | solution.py:20
  136.0 10.4 %copy-start.3 = (bf16[256,512]{1,0:T(8,128)(2,1)}, bf16[256,512]{1,0:T(8,128)(2,1)S(1)}, u32[]{:S(2)}) copy-start(bf16[256,512]{1,0:T(8,128)(2,1)S(1)} %collective-permute-done.15.refs_1_) | copy-start | bytes 786436
  136.0 13.1 %collective-permute-start.16 = (bf16[256,512]{1,0:T(8,128)(2,1)S(1)}, bf16[256,512]{1,0:T(8,128)(2,1)S(1)}, u32[]{:S(2)}, u32[]{:S(2)}) collective-permute-start(bf16[256,512]{1,0:T(8,128)(2,1)S(1)} %collective-permute-done.15.refs_1_), channel_id=1, source_target_pairs={{4,8},{8,12},{5,9},{9,13},{6,10},{10,14},{7,11},{11,15},{20,24},{2... | collective-permute-start | bytes 786440 | tf_op jit(solution)/shard_map/ppermute | solution.py:32
  146.5 35.1 %copy-start.4 = (bf16[256,512]{1,0:T(8,128)(2,1)S(1)}, bf16[256,512]{1,0:T(8,128)(2,1)}, u32[]{:S(2)}) copy-start(bf16[256,512]{1,0:T(8,128)(2,1)} %copy-done.3) | copy-start | bytes 786436
  147.6 79.8 %collective-permute-start.32 = (bf16[128,3584]{1,0:T(8,128)(2,1)S(1)}, bf16[128,3584]{1,0:T(8,128)(2,1)S(1)}, u32[]{:S(2)}, u32[]{:S(2)}) collective-permute-start(bf16[128,3584]{1,0:T(8,128)(2,1)S(1)} %copy-done.32), channel_id=1, source_target_pairs={{0,2},{1,3},{2,0},{3,1},{4,6},{5,7},{6,4},{7,5},{8,10},{9,11},{10,... | collective-permute-start | bytes 2752520 | tf_op jit(solution)/shard_map/ppermute | solution.py:20
  147.8 43.3 %collective-permute-start.34 = (bf16[128,3584]{1,0:T(8,128)(2,1)S(1)}, bf16[128,3584]{1,0:T(8,128)(2,1)S(1)}, u32[]{:S(2)}, u32[]{:S(2)}) collective-permute-start(bf16[128,3584]{1,0:T(8,128)(2,1)S(1)} %slice.113), channel_id=1, source_target_pairs={{0,1},{1,0},{2,3},{3,2},{4,5},{5,4},{6,7},{7,6},{8,9},{9,8},{10,11... | collective-permute-start | bytes 2752520 | tf_op jit(solution)/shard_map/ppermute | solution.py:20
  147.8 12.6 %collective-permute-start.19 = (bf16[256,512]{1,0:T(8,128)(2,1)S(1)}, bf16[256,512]{1,0:T(8,128)(2,1)S(1)}, u32[]{:S(2)}, u32[]{:S(2)}) collective-permute-start(bf16[256,512]{1,0:T(8,128)(2,1)S(1)} %collective-permute-done.18.refs_4_), channel_id=1, source_target_pairs={{4,0},{8,4},{5,1},{9,5},{6,2},{10,6},{7,3},{11,7},{20,16},{24,20},... | collective-permute-start | bytes 786440 | tf_op jit(solution)/shard_map/ppermute | solution.py:35
  149.2 11.3 %collective-permute-start.17 = (bf16[256,512]{1,0:T(8,128)(2,1)S(1)}, bf16[256,512]{1,0:T(8,128)(2,1)S(1)}, u32[]{:S(2)}, u32[]{:S(2)}) collective-permute-start(bf16[256,512]{1,0:T(8,128)(2,1)S(1)} %collective-permute-done.16.refs_2_), channel_id=1, source_target_pairs={{8,12},{9,13},{10,14},{11,15},{24,28},{25,29},{26,30},{27,31}} | collective-permute-start | bytes 786440 | tf_op jit(solution)/shard_map/ppermute | solution.py:32
  160.5 10.0 %collective-permute-start.28 = (bf16[256,512]{1,0:T(8,128)(2,1)S(1)}, bf16[256,512]{1,0:T(8,128)(2,1)S(1)}, u32[]{:S(2)}, u32[]{:S(2)}) collective-permute-start(bf16[256,512]{1,0:T(8,128)(2,1)S(1)} %bitcast.39), channel_id=1, source_target_pairs={{4,0},{8,4},{12,8},{5,1},{9,5},{13,9},{6,2},{10,6},{14,10},{7,3},{... | collective-permute-start | bytes 786440 | tf_op jit(solution)/shard_map/ppermute | solution.py:35
  161.7 10.0 %collective-permute-start.25 = (bf16[256,512]{1,0:T(8,128)(2,1)S(1)}, bf16[256,512]{1,0:T(8,128)(2,1)S(1)}, u32[]{:S(2)}, u32[]{:S(2)}) collective-permute-start(bf16[256,512]{1,0:T(8,128)(2,1)S(1)} %bitcast.40), channel_id=1, source_target_pairs={{0,4},{4,8},{8,12},{1,5},{5,9},{9,13},{2,6},{6,10},{10,14},{3,7},{... | collective-permute-start | bytes 786440 | tf_op jit(solution)/shard_map/ppermute | solution.py:32
  170.5 11.1 %collective-permute-start.24 = (bf16[256,512]{1,0:T(8,128)(2,1)S(1)}, bf16[256,512]{1,0:T(8,128)(2,1)S(1)}, u32[]{:S(2)}, u32[]{:S(2)}) collective-permute-start(bf16[256,512]{1,0:T(8,128)(2,1)S(1)} %collective-permute-done.19.refs_5_), channel_id=1, source_target_pairs={{4,0},{5,1},{6,2},{7,3},{20,16},{21,17},{22,18},{23,19}} | collective-permute-start | bytes 786440 | tf_op jit(solution)/shard_map/ppermute | solution.py:35
  171.8 19.6 %collective-permute-start.29 = (bf16[256,512]{1,0:T(8,128)(2,1)S(1)}, bf16[256,512]{1,0:T(8,128)(2,1)S(1)}, u32[]{:S(2)}, u32[]{:S(2)}) collective-permute-start(bf16[256,512]{1,0:T(8,128)(2,1)S(1)} %collective-permute-done.28.refs_4_), channel_id=1, source_target_pairs={{4,0},{8,4},{5,1},{9,5},{6,2},{10,6},{7,3},{11,7},{20,16},{24,20},... | collective-permute-start | bytes 786440 | tf_op jit(solution)/shard_map/ppermute | solution.py:35
  173.1 19.6 %collective-permute-start.26 = (bf16[256,512]{1,0:T(8,128)(2,1)S(1)}, bf16[256,512]{1,0:T(8,128)(2,1)S(1)}, u32[]{:S(2)}, u32[]{:S(2)}) collective-permute-start(bf16[256,512]{1,0:T(8,128)(2,1)S(1)} %collective-permute-done.25.refs_1_), channel_id=1, source_target_pairs={{4,8},{8,12},{5,9},{9,13},{6,10},{10,14},{7,11},{11,15},{20,24},{2... | collective-permute-start | bytes 786440 | tf_op jit(solution)/shard_map/ppermute | solution.py:32
  191.1 37.9 %collective-permute-start.31 = (bf16[256,3584]{1,0:T(8,128)(2,1)S(1)}, bf16[256,3584]{1,0:T(8,128)(2,1)S(1)}, u32[]{:S(2)}, u32[]{:S(2)}) collective-permute-start(bf16[256,3584]{1,0:T(8,128)(2,1)S(1)} %terms.10), channel_id=1, source_target_pairs={{0,1},{1,0},{2,3},{3,2},{4,5},{5,4},{6,7},{7,6},{8,9},{9,8},{10,11... | collective-permute-start | bytes 5505032 | tf_op jit(solution)/shard_map/ppermute | solution.py:20
  191.4 15.0 %collective-permute-start.30 = (bf16[256,512]{1,0:T(8,128)(2,1)S(1)}, bf16[256,512]{1,0:T(8,128)(2,1)S(1)}, u32[]{:S(2)}, u32[]{:S(2)}) collective-permute-start(bf16[256,512]{1,0:T(8,128)(2,1)S(1)} %collective-permute-done.29.refs_5_), channel_id=1, source_target_pairs={{4,0},{5,1},{6,2},{7,3},{20,16},{21,17},{22,18},{23,19}} | collective-permute-start | bytes 786440 | tf_op jit(solution)/shard_map/ppermute | solution.py:35
  192.7 15.2 %collective-permute-start.27 = (bf16[256,512]{1,0:T(8,128)(2,1)S(1)}, bf16[256,512]{1,0:T(8,128)(2,1)S(1)}, u32[]{:S(2)}, u32[]{:S(2)}) collective-permute-start(bf16[256,512]{1,0:T(8,128)(2,1)S(1)} %collective-permute-done.26.refs_2_), channel_id=1, source_target_pairs={{8,12},{9,13},{10,14},{11,15},{24,28},{25,29},{26,30},{27,31}} | collective-permute-start | bytes 786440 | tf_op jit(solution)/shard_map/ppermute | solution.py:32
  203.1 26.6 %collective-permute-start.35 = (bf16[256,3584]{1,0:T(8,128)(2,1)S(1)}, bf16[256,3584]{1,0:T(8,128)(2,1)S(1)}, u32[]{:S(2)}, u32[]{:S(2)}) collective-permute-start(bf16[256,3584]{1,0:T(8,128)(2,1)S(1)} %terms.14), channel_id=1, source_target_pairs={{0,1},{1,0},{2,3},{3,2},{4,5},{5,4},{6,7},{7,6},{8,9},{9,8},{10,11... | collective-permute-start | bytes 5505032 | tf_op jit(solution)/shard_map/ppermute | solution.py:20
  206.4 23.3 %collective-permute-start.36 = (bf16[128,3584]{1,0:T(8,128)(2,1)S(1)}, bf16[128,3584]{1,0:T(8,128)(2,1)S(1)}, u32[]{:S(2)}, u32[]{:S(2)}) collective-permute-start(bf16[128,3584]{1,0:T(8,128)(2,1)S(1)} %add_convert_fusion.4), channel_id=1, source_target_pairs={{0,2},{1,3},{2,0},{3,1},{4,6},{5,7},{6,4},{7,5},{8,10},{9,11},{10,... | collective-permute-start | bytes 2752520 | tf_op jit(solution)/shard_map/ppermute | solution.py:20
  207.9 41.4 %collective-permute-start.37 = (bf16[128,3584]{1,0:T(8,128)(2,1)S(1)}, bf16[128,3584]{1,0:T(8,128)(2,1)S(1)}, u32[]{:S(2)}, u32[]{:S(2)}) collective-permute-start(bf16[128,3584]{1,0:T(8,128)(2,1)S(1)} %add_convert_fusion.6), channel_id=1, source_target_pairs={{0,2},{1,3},{2,0},{3,1},{4,6},{5,7},{6,4},{7,5},{8,10},{9,11},{10,... | collective-permute-start | bytes 2752520 | tf_op jit(solution)/shard_map/ppermute | solution.py:20
  227.4 40.6 %collective-permute-start.38 = (bf16[128,3584]{1,0:T(8,128)(2,1)S(1)}, bf16[128,3584]{1,0:T(8,128)(2,1)S(1)}, u32[]{:S(2)}, u32[]{:S(2)}) collective-permute-start(bf16[128,3584]{1,0:T(8,128)(2,1)S(1)} %add_convert_fusion.3), channel_id=1, source_target_pairs={{0,2},{1,3},{2,0},{3,1},{4,6},{5,7},{6,4},{7,5},{8,10},{9,11},{10,... | collective-permute-start | bytes 2752520 | tf_op jit(solution)/shard_map/ppermute | solution.py:20
  249.3 20.9 %copy-start.1 = (bf16[7168,64]{0,1:T(8,128)(2,1)S(1)}, bf16[7168,64]{0,1:T(8,128)(2,1)}, u32[]{:S(2)}) copy-start(bf16[7168,64]{0,1:T(8,128)(2,1)} %param.10) | copy-start | bytes 2752516
  268.3 1.8 copy-start.31
  (15 other events, 13.5 us)
Sparse Core Ops, SparseCore 0:
  77.2 32.2 all-reduce.3

commit v3 on v1

v3 whole, which is shorter than its diff:
```python
import functools

import jax
import jax.numpy as jnp
from jax import lax
from jax.experimental import pallas as pl
from jax.experimental.pallas import tpu as pltpu
from jax.sharding import PartitionSpec as P

GROUPS = 8
FAR_PARTS = 2
COL_PARTS = 2

highest = lax.Precision.HIGHEST
f32, bf16 = jnp.float32, jnp.bfloat16


def swap(value, step):
    size = lax.axis_size("dp")
    return lax.ppermute(value, "dp", [(d, d ^ step) for d in range(size)])


def after(value, *earlier):
    return lax.optimization_barrier((value,) + earlier)[0]


def across(value, step, places=None):
    size = lax.axis_size("tensor")
    pairs = [(t, t ^ step) for t in range(size) if places is None or t in places]
    return lax.ppermute(value, "tensor", pairs)


def spread(block):
    second = across(block, 2)
    first = across(block, 1)
    middle = across(block, 3, (1, 2))
    ends = across(second, 1, (1, 2))
    return [block, first, second, middle, ends]


def terms_kernel(size, count, first, place_ref, *refs):
    blocks, (w_ref, out_ref, feats, held, sems, held_sems) = refs[:count], refs[count:]
    width, tile = feats.shape[1] // size, out_ref.shape[1]
    j, steps = pl.program_id(0), pl.num_programs(0)
    slots = held.shape[0]

    def put(value, source, slot):
        at = pl.ds(pl.multiple_of(source * width, width), width)
        return pltpu.make_async_copy(value, feats.at[:, at], sems.at[slot])

    def fetch(step):
        slot = lax.rem(step, slots)
        at = pl.ds(pl.multiple_of(first + step * tile, tile), tile)
        return pltpu.make_async_copy(w_ref.at[:, 0, :, at], held.at[slot], held_sems.at[slot])

    @pl.when(j == 0)
    def _():
        for step in range(slots):

            @pl.when(step < steps)
            def _():
                fetch(step).start()

        if count == 1:
            copies = [put(blocks[0].at[source], source, source) for source in range(size)]
            for copy in copies:
                copy.start()
            for copy in copies:
                copy.wait()
        else:
            place = place_ref[0]
            copies = [put(blocks[step], lax.bitwise_xor(place, step), step) for step in range(3)]
            for copy in copies:
                copy.start()
            inside = jnp.logical_or(place == 1, place == 2)
            for chosen, block in ((inside, blocks[3]), (jnp.logical_not(inside), blocks[4])):

                @pl.when(chosen)
                def _():
                    last = put(block, lax.bitwise_xor(place, 3), 3)
                    last.start()
                    last.wait()

            for copy in copies:
                copy.wait()

    fetch(j).wait()
    weight = held[lax.rem(j, slots)].reshape(size * width, tile)
    out_ref[...] = jnp.dot(feats[...], weight, preferred_element_type=f32).astype(bf16)

    @pl.when(j + slots < steps)
    def _():
        fetch(j + slots).start()


def block_terms(blocks, down_weight, col_start, cols):
    size, _, width, _ = down_weight.shape
    rows = blocks[-1].shape[-2]
    tile = max(n for n in range(128, 513, 128) if cols % n == 0)
    slots = min(4, cols // tile)
    return pl.pallas_call(
        functools.partial(terms_kernel, size, len(blocks), col_start),
        out_shape=jax.ShapeDtypeStruct((rows, cols), bf16),
        grid_spec=pltpu.PrefetchScalarGridSpec(
            num_scalar_prefetch=1,
            grid=(cols // tile,),
            in_specs=[pl.BlockSpec(memory_space=pl.ANY)] * (len(blocks) + 1),
            out_specs=pl.BlockSpec((rows, tile), lambda j, place: (0, j)),
            scratch_shapes=[
                pltpu.VMEM((rows, size * width), bf16),
                pltpu.VMEM((slots, size, width, tile), bf16),
                pltpu.SemaphoreType.DMA((size,)),
                pltpu.SemaphoreType.DMA((slots,)),
            ],
        ),
        compiler_params=pltpu.CompilerParams(vmem_limit_bytes=40 << 20),
        cost_estimate=pl.CostEstimate(flops=1000, bytes_accessed=1000, transcendentals=0),
        name="terms",
    )(lax.axis_index("tensor").reshape(1), *blocks, down_weight)


def gathered_terms(blocks, down_weight, col_start, cols):
    weight = lax.slice_in_dim(down_weight, col_start, col_start + cols, axis=3)
    return lax.dot_general(
        blocks[0], weight[:, 0], (((0, 2), (0, 1)), ((), ())), preferred_element_type=f32
    ).astype(bf16)


def add(*values):
    total = values[0].astype(f32)
    for value in values[1:]:
        total = total + value.astype(f32)
    return total.astype(bf16)


def far_features(output_grad):
    groups, place = lax.axis_size("dp"), lax.axis_index("dp")
    line = lax.axis_size("tensor") == 4

    def gather(block):
        return [lax.all_gather(block, "tensor", axis=0)]

    turned = jnp.transpose(output_grad[0], (0, 2, 1))
    pieces = [
        lax.dynamic_index_in_dim(turned, place ^ step, 0, keepdims=False) for step in range(groups)
    ]
    rows = pieces[0].shape[0] // FAR_PARTS
    far, beside = [], None
    last = None
    for half in range(FAR_PARTS):
        cut = slice(half * rows, (half + 1) * rows)
        for step in range(2, groups, 2):
            sent = [swap(pieces[step + 1][cut], step + 1), swap(pieces[step][cut], step)]
            block = jnp.concatenate(sent)
            if last is not None:
                block = after(block, last)
            far.append((half, step, spread(block) if line else gather(block)))
            last = far[-1][2][2] if line else far[-1][2][0]
            if beside is None:
                beside = swap(after(pieces[1], last), 1)
                far[0] = far[0][:2] + ([after(far[0][2][0], beside)] + far[0][2][1:],)
    beside = gather(after(beside, last))
    own = gather(after(pieces[0], last))
    return far, beside, own, last


def example_gradients(acts_low, grads_low, local_ids, examples):
    onehot = (local_ids[:, None] == jnp.arange(examples, dtype=jnp.int32)[None, :]).astype(f32)
    counts = jnp.sum(onehot, axis=0)
    spread = (onehot[:, :, None] * acts_low[:, None, :]).reshape(onehot.shape[0], -1)
    outer_sum = lax.dot_general(
        spread,
        grads_low,
        (((0,), (0,)), ((), ())),
        precision=highest,
        preferred_element_type=f32,
    )
    basis_rank = acts_low.shape[1]
    outer_sum = outer_sum.reshape(examples, basis_rank * grads_low.shape[1]) / counts[:, None]
    return outer_sum.astype(bf16)


def gather_examples(example_grad, example_group):
    count, width = example_grad.shape
    groups = lax.axis_size("dp")
    group_column = jnp.broadcast_to(example_group.astype(bf16)[:, None], (count, 128))
    held = jnp.concatenate([example_grad, group_column], axis=1)
    every = jnp.zeros((groups * count, width + 128), bf16)
    for step in range(groups):
        value = swap(held, step) if step else held
        row = (lax.axis_index("dp") ^ step) * count
        every = lax.dynamic_update_slice_in_dim(every, value, row, 0)
    return every


def fisher_and_groups(every, flat_width):
    row_count = flat_width // lax.axis_size("dp")
    col_count = flat_width // lax.axis_size("tensor")
    col_start = lax.axis_index("tensor") * col_count
    row_start = lax.axis_index("dp") * row_count
    every_group = every[:, flat_width].astype(jnp.int32)
    rows_part = lax.dynamic_slice_in_dim(every, row_start, row_count, 1)
    cols_part = lax.dynamic_slice_in_dim(every, col_start, col_count, 1)
    fisher = lax.dot_general(
        rows_part, cols_part, (((0,), (0,)), ((), ())), preferred_element_type=f32
    )
    member = (every_group[:, None] == jnp.arange(GROUPS, dtype=jnp.int32)[None, :]).astype(bf16)
    group_grad = lax.dot_general(
        member, cols_part, (((0,), (0,)), ((), ())), preferred_element_type=f32
    )
    return fisher, group_grad


def per_device(
    hidden_acts, output_grad, down_weight, input_basis, output_basis, token_example, example_group
):
    tokens, cols = hidden_acts.shape
    col_parts = COL_PARTS if cols % (256 * COL_PARTS) == 0 else 1
    part, rows = cols // col_parts, tokens // FAR_PARTS
    far, beside, own, last = far_features(output_grad)

    def multiply(blocks, at):
        kernel = block_terms if down_weight.shape[2] % 128 == 0 else gathered_terms
        return kernel(blocks, down_weight, at * part, part)

    acts_part = jnp.dot(hidden_acts, input_basis, preferred_element_type=f32)
    grads_part = lax.dot_general(
        output_grad,
        output_basis,
        (((0, 1, 2), (0, 1, 2)), ((), ())),
        preferred_element_type=f32,
    )
    parts = jnp.concatenate([acts_part, grads_part], axis=1)
    if lax.axis_size("tensor") == 4:
        low = parts = after(parts, last)
        far[0] = far[0][:2] + ([after(far[0][2][0], parts)] + far[0][2][1:],)
        for step in (1, 2):
            low = low + across(low, step)
    else:
        low = lax.psum(parts, "tensor")

    units = [(blocks, half, step, at) for half, step, blocks in far for at in range(col_parts)]
    held, pairs, arrived = [], [], []

    def settle(latest):
        count = len(pairs)
        both, other = held[count]
        pairs.append(add(after(both[rows:], latest), other))
        arrived.append(swap(pairs[count], units[count][2]))

    for count, (blocks, half, step, at) in enumerate(units):
        earlier = pairs[-1:] + arrived[:-1][-1:]
        if count == 1:
            earlier = earlier + far[-1][2] + [every]
        if count == 3:
            earlier.append(beside[0])
        if earlier:
            blocks = [after(blocks[0], *earlier)] + blocks[1:]
        both = multiply(blocks, at)
        held.append((both, swap(both[:rows], 1)))
        if count == 0:
            acts_low, grads_low = jnp.split(after(low, both), 2, axis=1)
            example_grad = example_gradients(
                acts_low, grads_low, token_example[0], example_group.shape[0]
            )
            every = gather_examples(example_grad, example_group)
        else:
            settle(both)

    near = []
    for at in range(col_parts):
        earlier = pairs[-1:] + arrived[:-1][-1:] + [own[0]]
        term = multiply([after(beside[0], *earlier)], at)
        near.append(swap(term, 1))
        if at == 0:
            settle(term)
    fisher, group_grad = fisher_and_groups(after(every, term), example_grad.shape[1])
    result = jnp.zeros((tokens, cols), bf16)
    for at in range(col_parts):
        earlier = [near[at], term] + ([arrived[-1]] if at == col_parts - 1 else [])
        term = multiply([after(own[0], *earlier)], at)
        for half in range(FAR_PARTS):
            sums = [
                arrived[count] for count, unit in enumerate(units) if unit[1:] == (half, unit[2], at)
            ]
            cut = slice(half * rows, (half + 1) * rows)
            value = add(term[cut], near[at][cut], *sums)
            result = lax.dynamic_update_slice(result, value, (half * rows, at * part))
    return (result, fisher, group_grad)


def solution(mesh):
    return jax.shard_map(
        per_device,
        mesh=mesh,
        in_specs=(
            P(("parts", "dp"), "tensor"),
            P("tensor", None, None, ("parts", "dp")),
            P(None, "dp", None, "tensor"),
            P("tensor", None),
            P("tensor", None, None, None),
            P(("parts", "dp"), None),
            P(("parts", "dp")),
        ),
        out_specs=(
            P(("parts", "dp"), "tensor"),
            P(("parts", "dp"), "tensor"),
            P("parts", "tensor"),
        ),
        check_vma=False,
    )
```

time: 271 us -> 262 us (0.967); the launches traced: 270 us -> 257 us
  waiting for transfers between devices: 178 us -> 72.6 us
  local copies, waits for them, and re-layouts: 3.71 us -> 67 us
  Pallas kernels: 0 us -> 58.5 us
  matrix products: 48 us -> 8.23 us
  blocking collectives: 25 us -> 0 us
  starting transfers between devices: 0.12 us -> 21.7 us
  other arithmetic: 1.2 us -> 14.7 us
    reduce_scatter x1 -> x0, waiting for transfers between devices: 101 us -> none  [per_device(): lax.psum_scatter(feature_dot(columns, down_weight).astype(jnp.bfloat16),...]
    all_gather x1 -> x2, waiting for transfers between devices: 77.1 us -> 0.02 us  [gather(): return [lax.all_gather(block, 'tensor', axis=0)]]
    ppermute x0 -> x28, waiting for transfers between devices: none -> 72.6 us  [the longest x18 37.9 us: swap(): return lax.ppermute(value, 'dp', [(d, d ^ step) for d in range(size)])]
    pallas_call x0 -> x8, Pallas kernels: none -> 58.5 us  [block_terms(): pl.pallas_call(functools.partial(terms_kernel, size, len(blocks), col_sta...]
    dynamic_update_slice x0 -> x5, local copies, waits for them, and re-layouts: none -> 47 us  [the longest x4 46.6 us: gather_examples(): every = lax.dynamic_update_slice_in_dim(every, value, row, 0)]
    dot_general x3 -> x2, matrix products: 42.7 us -> 3.57 us  [the longest x1 3.27 us: per_device(): acts_part = jnp.dot(hidden_acts, input_basis, preferred_element_type=f32)]
    ppermute x0 -> x28, starting transfers between devices: none -> 21.6 us  [the longest x18 11.5 us: swap(): return lax.ppermute(value, 'dp', [(d, d ^ step) for d in range(size)])]
    all_to_all x1 -> x0, blocking collectives: 19.5 us -> none  [per_device(): lax.all_to_all(output_grad, 'dp', split_axis=1, concat_axis=3, tiled=True)]
  transfers between devices with their start and end apart: 3 -> 30, of which waited for: 2 -> 10; matrix products, arithmetic and copies ran while one was open for 18% -> 31% of each run, Pallas kernels for 0% -> 20%
where the time goes in v3:
time: 262 us; the launch traced here: 257 us
  waiting for transfers between devices  72.6 us (28%)
  local copies, waits for them, and re-layouts  67 us (26%)
  Pallas kernels  58.5 us (22%)
  starting transfers between devices  21.7 us (8%)
  other arithmetic  14.7 us (6%)
  between operations  14.6 us (6%)
  matrix products  8.23 us (3%)
    pallas_call x8, Pallas kernels, block_terms(): pl.pallas_call(functools.partial(terms_kernel, size, len(blocks), col_sta...  58.5 us
    dynamic_update_slice x4, local copies, waits for them, and re-layouts, gather_examples(): every = lax.dynamic_update_slice_in_dim(every, value, row, 0)  46.6 us
    ppermute x18, waiting for transfers between devices, swap(): return lax.ppermute(value, 'dp', [(d, d ^ step) for d in range(size)])  37.9 us
    ppermute x10, waiting for transfers between devices, across(): return lax.ppermute(value, 'tensor', pairs)  34.6 us
    ppermute x18, starting transfers between devices, swap(): return lax.ppermute(value, 'dp', [(d, d ^ step) for d in range(size)])  11.5 us
    ppermute x10, starting transfers between devices, across(): return lax.ppermute(value, 'tensor', pairs)  10.1 us
    convert_element_type x5, other arithmetic, add(): return total.astype(bf16)  9.32 us
    unnamed x29, local copies, waits for them, and re-layouts  5.3 us
  transfers between devices with their start and end apart: 30, of which 10 were waited for; matrix products, arithmetic and copies ran while one was open for 31% of the time, Pallas kernels for 20%

profile of v3, /device:TPU:0, one launch (start us, length us, event | category | flops | bytes accessed | tf_op | source)
XLA Modules:
  0.0 257.3 jit_solution(13263124144622493739)
XLA Ops:
  7.2 2.0 dynamic-slice_bitcast_fusion.1
  9.5 2.4 collective-permute-start.2
  12.1 0.6 collective-permute-start.3
  12.7 1.5 collective-permute-start.1
  14.2 1.5 collective-permute-done.2
  15.8 3.5 %collective-permute-done.3 = bf16[128,512]{1,0:T(8,128)(2,1)S(1)} collective-permute-done((bf16[128,512]{1,0:T(8,128)(2,1)S(1)}, bf16[128,512]{1,0:T(8,128)(2,1)S(1)}, u32[]{:S(2)}, u32[]{:S(2)}) %collective-permute-start.3) | collective-permute-done | bytes 131104 | tf_op jit(solution)/shard_map/ppermute | solution.py:20
  19.3 3.0 %collective-permute-start.4 = (bf16[256,512]{1,0:T(8,128)(2,1)S(1)}, bf16[256,512]{1,0:T(8,128)(2,1)S(1)}, u32[]{:S(2)}, u32[]{:S(2)}) collective-permute-start(bf16[256,512]{1,0:T(8,128)(2,1)S(1)} %constant_dynamic-update-slice_fusion.refs_0_), channel_id=1, source_target_pairs={{0,8},{4,12},{8,0},{12,4},{1,9},{5,13},{9,1},{13,5},{2,10},{6,14},... | collective-permute-start | bytes 786440 | tf_op jit(solution)/shard_map/ppermute | solution.py:30
  22.3 3.3 %fusion.23 = f32[256,64]{0,1:T(8,128)S(1)} fusion(bf16[256,7168]{1,0:T(8,128)(2,1)} %param.7, bf16[7168,64]{0,1:T(8,128)(2,1)S(1)} %copy-done), kind=kOutput, calls=%fused_computation.49 | convolution fusion | flops 234881024 | bytes 4653056 | tf_op jit(solution)/shard_map/dot_general | solution.py:226
  25.7 8.8 %collective-permute-done.4.refs_2_ = bf16[256,512]{1,0:T(8,128)(2,1)S(1)} collective-permute-done((bf16[256,512]{1,0:T(8,128)(2,1)S(1)}, bf16[256,512]{1,0:T(8,128)(2,1)S(1)}, u32[]{:S(2)}, u32[]{:S(2)}) %collective-permute-start.4) | collective-permute-done | bytes 262176 | tf_op jit(solution)/shard_map/ppermute | solution.py:30
  34.8 13.9 %collective-permute-done.5.refs_2_ = bf16[256,512]{1,0:T(8,128)(2,1)S(1)} collective-permute-done((bf16[256,512]{1,0:T(8,128)(2,1)S(1)}, bf16[256,512]{1,0:T(8,128)(2,1)S(1)}, u32[]{:S(2)}, u32[]{:S(2)}) %collective-permute-start.5) | collective-permute-done | bytes 262176 | tf_op jit(solution)/shard_map/ppermute | solution.py:30
  48.6 2.0 collective-permute-start.7
  50.7 0.7 collective-permute-start.8
  51.4 1.3 collective-permute-start.9
  52.7 2.4 collective-permute-done.13
  55.1 0.7 add.79
  56.3 0.7 copy-done.10
  57.1 3.9 %collective-permute-done.7.refs_1_ = bf16[256,512]{1,0:T(8,128)(2,1)S(1)} collective-permute-done((bf16[256,512]{1,0:T(8,128)(2,1)S(1)}, bf16[256,512]{1,0:T(8,128)(2,1)S(1)}, u32[]{:S(2)}, u32[]{:S(2)}) %collective-permute-start.7) | collective-permute-done | bytes 262176 | tf_op jit(solution)/shard_map/ppermute | solution.py:30
  61.0 5.7 %collective-permute-done.9.refs_4_ = bf16[256,512]{1,0:T(8,128)(2,1)S(1)} collective-permute-done((bf16[256,512]{1,0:T(8,128)(2,1)S(1)}, bf16[256,512]{1,0:T(8,128)(2,1)S(1)}, u32[]{:S(2)}, u32[]{:S(2)}) %collective-permute-start.9) | collective-permute-done | bytes 262176 | tf_op jit(solution)/shard_map/ppermute | solution.py:30
  66.7 0.7 copy-done.2
  67.4 0.9 copy-done.3
  68.3 6.7 %terms.8 = bf16[256,3584]{1,0:T(8,128)(2,1)S(1)} custom-call(s32[1]{0:T(128)} %bitcast.place_ref, bf16[256,512]{1,0:T(8,128)(2,1)S(1)} %constant_dynamic-update-slice_fusion.refs_0_, bf16[256,512]{1,0:T(8,128)(2,1)S(1)} %collective-permute-done.7.refs_1_, bf16[256,512]{1,0:T(8,128)(2,1)S(1)} %collective-permute-done.4.refs_2_, ...), custom_call_target="tpu_custom_call" | custom-call | flops 1000 | bytes 1000 | tf_op jit(solution)/shard_map/terms/pallas_call | solution.py:101
  75.1 1.0 add.80
  76.1 1.0 fusion.10
  77.1 1.0 reshape.80
  78.5 1.4 collective-permute-start.11
  79.9 1.3 collective-permute-start.12
  81.2 1.2 collective-permute-start.16
  82.4 0.6 collective-permute-start.17
  83.0 1.4 fusion.22
  84.9 1.1 broadcast_in_dim.4
  86.0 10.2 %dynamic_update_slice.24 = bf16[16,4224]{0,1:T(8,128)(2,1)} dynamic-update-slice(bf16[16,4224]{0,1:T(8,128)(2,1)} %broadcast_in_dim.4, bf16[4,4224]{0,1:T(8,128)(2,1)S(1)} %copy.18, s32[]{:T(128)S(6)} %select_n.35, s32[]{:T(128)} %constant.34.clone.1) | dynamic-update-slice | bytes 67588 | tf_op jit(solution)/shard_map/dynamic_update_slice | solution.py:192
  96.8 12.1 %dynamic_update_slice.25 = bf16[16,4224]{0,1:T(8,128)(2,1)} dynamic-update-slice(bf16[16,4224]{0,1:T(8,128)(2,1)} %dynamic_update_slice.24, bf16[4,4224]{0,1:T(8,128)(2,1)S(1)} %copy.19, s32[]{:T(128)S(6)} %select_n.36, s32[]{:T(128)} %constant.34.clone.1) | dynamic-update-slice | bytes 67588 | tf_op jit(solution)/shard_map/dynamic_update_slice | solution.py:192
  109.4 1.3 copy.20
  110.7 12.1 %dynamic_update_slice.26 = bf16[16,4224]{0,1:T(8,128)(2,1)} dynamic-update-slice(bf16[16,4224]{0,1:T(8,128)(2,1)} %dynamic_update_slice.25, bf16[4,4224]{0,1:T(8,128)(2,1)S(1)} %copy.20, s32[]{:T(128)S(6)} %select_n.37, s32[]{:T(128)} %constant.34.clone.1) | dynamic-update-slice | bytes 67588 | tf_op jit(solution)/shard_map/dynamic_update_slice | solution.py:192
  123.3 12.1 %dynamic_update_slice.27 = bf16[16,4224]{0,1:T(8,128)(2,1)} dynamic-update-slice(bf16[16,4224]{0,1:T(8,128)(2,1)} %dynamic_update_slice.26, bf16[4,4224]{0,1:T(8,128)(2,1)S(1)} %copy.21, s32[]{:T(128)S(6)} %select_n.38, s32[]{:T(128)} %constant.34.clone.1) | dynamic-update-slice | bytes 67588 | tf_op jit(solution)/shard_map/dynamic_update_slice | solution.py:192
  135.5 6.7 %terms.9 = bf16[256,3584]{1,0:T(8,128)(2,1)S(1)} custom-call(s32[1]{0:T(128)} %bitcast.place_ref, bf16[256,512]{1,0:T(8,128)(2,1)S(1)} %constant_dynamic-update-slice_fusion.refs_0_, bf16[256,512]{1,0:T(8,128)(2,1)S(1)} %collective-permute-done.7.refs_1_, bf16[256,512]{1,0:T(8,128)(2,1)S(1)} %collective-permute-done.4.refs_2_, ...), custom_call_target="tpu_custom_call" | custom-call | flops 1000 | bytes 1000 | tf_op jit(solution)/shard_map/terms/pallas_call | solution.py:101
  142.5 0.9 copy-done.7
  143.4 2.3 add_convert_fusion.7
  145.7 1.1 collective-permute-start.20
  146.8 8.7 %terms.10 = bf16[256,3584]{1,0:T(8,128)(2,1)S(1)} custom-call(s32[1]{0:T(128)} %bitcast.place_ref, bf16[256,512]{1,0:T(8,128)(2,1)S(1)} %pad_maximum_fusion.refs_0_, bf16[256,512]{1,0:T(8,128)(2,1)} %collective-permute-done.10.refs_1_, bf16[256,512]{1,0:T(8,128)(2,1)S(1)} %collective-permute-done.5.refs_2_, ...), custom_call_target="tpu_custom_call" | custom-call | flops 1000 | bytes 1000 | tf_op jit(solution)/shard_map/terms/pallas_call | solution.py:101
  155.5 1.4 fusion.21
  157.0 1.2 add_convert_fusion.6
  158.1 1.0 collective-permute-start.22
  159.1 1.5 copy.16
  160.6 1.5 copy.15
  162.1 7.1 %collective-permute-done.20 = bf16[128,3584]{1,0:T(8,128)(2,1)} collective-permute-done((bf16[128,3584]{1,0:T(8,128)(2,1)}, bf16[128,3584]{1,0:T(8,128)(2,1)}, u32[]{:S(2)}, u32[]{:S(2)}) %collective-permute-start.20) | collective-permute-done | bytes 917536 | tf_op jit(solution)/shard_map/ppermute | solution.py:20
  169.3 8.7 %terms.11 = bf16[256,3584]{1,0:T(8,128)(2,1)S(1)} custom-call(s32[1]{0:T(128)} %bitcast.place_ref, bf16[256,512]{1,0:T(8,128)(2,1)S(1)} %pad_maximum_fusion.refs_0_, bf16[256,512]{1,0:T(8,128)(2,1)} %collective-permute-done.10.refs_1_, bf16[256,512]{1,0:T(8,128)(2,1)S(1)} %collective-permute-done.5.refs_2_, ...), custom_call_target="tpu_custom_call" | custom-call | flops 1000 | bytes 1000 | tf_op jit(solution)/shard_map/terms/pallas_call | solution.py:101
  178.0 1.3 fusion.19
  179.5 2.4 add_convert_fusion.5
  181.9 6.2 %collective-permute-done.22 = bf16[128,3584]{1,0:T(8,128)(2,1)} collective-permute-done((bf16[128,3584]{1,0:T(8,128)(2,1)}, bf16[128,3584]{1,0:T(8,128)(2,1)}, u32[]{:S(2)}, u32[]{:S(2)}) %collective-permute-start.22) | collective-permute-done | bytes 917536 | tf_op jit(solution)/shard_map/ppermute | solution.py:20
  188.1 7.5 %terms.12 = bf16[256,3584]{1,0:T(8,128)(2,1)} custom-call(s32[1]{0:T(128)} %bitcast.place_ref, bf16[4,256,512]{2,1,0:T(8,128)(2,1)S(1)} %bitcast.47, bf16[4,1,512,7168]{3,2,1,0:T(8,128)(2,1)} %refs_1_.7), custom_call_target="tpu_custom_call" | custom-call | flops 1000 | bytes 1000 | tf_op jit(solution)/shard_map/terms/pallas_call | solution.py:101
  195.6 1.1 collective-permute-start.25
  196.7 1.7 add_convert_fusion.4
  198.4 1.0 collective-permute-start.27
  199.4 19.6 %collective-permute-done.25 = bf16[128,3584]{1,0:T(8,128)(2,1)S(1)} collective-permute-done((bf16[128,3584]{1,0:T(8,128)(2,1)}, bf16[128,3584]{1,0:T(8,128)(2,1)S(1)}, u32[]{:S(2)}, u32[]{:S(2)}) %collective-permute-start.25) | collective-permute-done | bytes 917536 | tf_op jit(solution)/shard_map/ppermute | solution.py:20
  219.0 6.7 %terms.13 = bf16[256,3584]{1,0:T(8,128)(2,1)S(1)} custom-call(s32[1]{0:T(128)} %bitcast.place_ref, bf16[4,256,512]{2,1,0:T(8,128)(2,1)S(1)} %bitcast.48, bf16[4,1,512,7168]{3,2,1,0:T(8,128)(2,1)} %refs_1_.7), custom_call_target="tpu_custom_call" | custom-call | flops 1000 | bytes 1000 | tf_op jit(solution)/shard_map/terms/pallas_call | solution.py:101
  225.8 2.7 %fusion.5 = f32[1024,1024]{1,0:T(8,128)} fusion(bf16[16,4224]{0,1:T(8,128)(2,1)S(1)} %copy-done.9, s32[]{:T(128)S(6)} %select_n.39, s32[]{:T(128)S(6)} %select_n.40), kind=kOutput, calls=%fused_computation.15 | convolution fusion | flops 33554432 | bytes 4718600 | tf_op jit(solution)/shard_map/dot_general | solution.py:204
  228.6 0.9 fusion.7
  229.5 6.7 %terms.14 = bf16[256,3584]{1,0:T(8,128)(2,1)S(1)} custom-call(s32[1]{0:T(128)} %bitcast.place_ref, bf16[4,256,512]{2,1,0:T(8,128)(2,1)S(1)} %bitcast.45, bf16[4,1,512,7168]{3,2,1,0:T(8,128)(2,1)} %refs_1_.7), custom_call_target="tpu_custom_call" | custom-call | flops 1000 | bytes 1000 | tf_op jit(solution)/shard_map/terms/pallas_call | solution.py:101
  236.2 1.8 add_convert_fusion.3
  238.4 1.5 fusion.1
  239.9 6.7 %terms.15 = bf16[256,3584]{1,0:T(8,128)(2,1)S(1)} custom-call(s32[1]{0:T(128)} %bitcast.place_ref, bf16[4,256,512]{2,1,0:T(8,128)(2,1)S(1)} %bitcast.46, bf16[4,1,512,7168]{3,2,1,0:T(8,128)(2,1)} %refs_1_.7), custom_call_target="tpu_custom_call" | custom-call | flops 1000 | bytes 1000 | tf_op jit(solution)/shard_map/terms/pallas_call | solution.py:101
  246.7 1.6 fusion.2
  248.6 1.8 copy-done.6
  (84 shorter events, 5.3 us)
Async XLA Ops:
  7.2 15.1 %copy-start = (bf16[7168,64]{0,1:T(8,128)(2,1)S(1)}, bf16[7168,64]{0,1:T(8,128)(2,1)}, u32[]{:S(2)}) copy-start(bf16[7168,64]{0,1:T(8,128)(2,1)} %param.10) | copy-start | bytes 2752516
  7.2 151.9 %all-gather.7.cloned.1.call-start = ((), (), s32[]{:S(2)}) async-start(), calls=%async_computation.1 | async-start | bytes 1310720 | tf_op jit(solution)/shard_map/all_gather | solution.py:141
  9.5 6.3 %collective-permute-start.2 = (bf16[128,512]{1,0:T(8,128)(2,1)S(1)}, bf16[128,512]{1,0:T(8,128)(2,1)S(1)}, u32[]{:S(2)}, u32[]{:S(2)}) collective-permute-start(bf16[128,512]{1,0:T(8,128)(2,1)S(1)} %get-tuple-element.56), channel_id=1, source_target_pairs={{0,3},{1,2},{2,1},{3,0},{4,7},{5,6},{6,5},{7,4},{8,11},{9,10},{10,... | collective-permute-start | bytes 393224 | tf_op jit(solution)/shard_map/ppermute | solution.py:20
  12.1 7.2 %collective-permute-start.3 = (bf16[128,512]{1,0:T(8,128)(2,1)S(1)}, bf16[128,512]{1,0:T(8,128)(2,1)S(1)}, u32[]{:S(2)}, u32[]{:S(2)}) collective-permute-start(bf16[128,512]{1,0:T(8,128)(2,1)S(1)} %get-tuple-element.58), channel_id=1, source_target_pairs={{0,2},{1,3},{2,0},{3,1},{4,6},{5,7},{6,4},{7,5},{8,10},{9,11},{10,... | collective-permute-start | bytes 393224 | tf_op jit(solution)/shard_map/ppermute | solution.py:20
  12.7 12.9 %collective-permute-start.1 = (bf16[128,512]{1,0:T(8,128)(2,1)S(1)}, bf16[128,512]{1,0:T(8,128)(2,1)S(1)}, u32[]{:S(2)}, u32[]{:S(2)}) collective-permute-start(bf16[128,512]{1,0:T(8,128)(2,1)S(1)} %get-tuple-element.57), channel_id=1, source_target_pairs={{0,2},{1,3},{2,0},{3,1},{4,6},{5,7},{6,4},{7,5},{8,10},{9,11},{10,... | collective-permute-start | bytes 393224 | tf_op jit(solution)/shard_map/ppermute | solution.py:20
  14.2 11.5 %collective-permute-start = (bf16[128,512]{1,0:T(8,128)(2,1)S(1)}, bf16[128,512]{1,0:T(8,128)(2,1)S(1)}, u32[]{:S(2)}, u32[]{:S(2)}) collective-permute-start(bf16[128,512]{1,0:T(8,128)(2,1)S(1)} %get-tuple-element.55), channel_id=1, source_target_pairs={{0,3},{1,2},{2,1},{3,0},{4,7},{5,6},{6,5},{7,4},{8,11},{9,10},{10,... | collective-permute-start | bytes 393224 | tf_op jit(solution)/shard_map/ppermute | solution.py:20
  19.3 15.2 %copy-start.5 = (bf16[1,4,512,256]{3,2,1,0:T(8,128)(2,1)S(1)}, bf16[1,4,512,256]{3,2,1,0:T(8,128)(2,1)}, u32[]{:S(2)}) copy-start(bf16[1,4,512,256]{3,2,1,0:T(8,128)(2,1)} %param.8) | copy-start | bytes 3145732
  19.3 15.1 %copy-start.11 = (bf16[1,4,512,64]{2,3,1,0:T(8,128)(2,1)S(1)}, bf16[1,4,512,64]{2,3,1,0:T(8,128)(2,1)}, u32[]{:S(2)}) copy-start(bf16[1,4,512,64]{2,3,1,0:T(8,128)(2,1)} %param.11) | copy-start | bytes 786436
  19.3 15.1 %collective-permute-start.4 = (bf16[256,512]{1,0:T(8,128)(2,1)S(1)}, bf16[256,512]{1,0:T(8,128)(2,1)S(1)}, u32[]{:S(2)}, u32[]{:S(2)}) collective-permute-start(bf16[256,512]{1,0:T(8,128)(2,1)S(1)} %constant_dynamic-update-slice_fusion.refs_0_), channel_id=1, source_target_pairs={{0,8},{4,12},{8,0},{12,4},{1,9},{5,13},{9,1},{13,5},{2,10},{6,14},... | collective-permute-start | bytes 786440 | tf_op jit(solution)/shard_map/ppermute | solution.py:30
  25.6 30.6 %copy-start.12 = (s32[1,256]{1,0:T(1,128)S(1)}, s32[1,256]{1,0:T(1,128)}, u32[]{:S(2)}) copy-start(s32[1,256]{1,0:T(1,128)} %param.12) | copy-start | bytes 3076
  25.6 30.6 %copy-start.13 = (s32[4]{0:T(128)S(1)}, s32[4]{0:T(128)}, u32[]{:S(2)}) copy-start(s32[4]{0:T(128)} %param.13) | copy-start | bytes 52
  34.4 14.2 %collective-permute-start.5 = (bf16[256,512]{1,0:T(8,128)(2,1)S(1)}, bf16[256,512]{1,0:T(8,128)(2,1)S(1)}, u32[]{:S(2)}, u32[]{:S(2)}) collective-permute-start(bf16[256,512]{1,0:T(8,128)(2,1)S(1)} %pad_maximum_fusion.refs_0_), channel_id=1, source_target_pairs={{0,8},{4,12},{8,0},{12,4},{1,9},{5,13},{9,1},{13,5},{2,10},{6,14},... | collective-permute-start | bytes 786440 | tf_op jit(solution)/shard_map/ppermute | solution.py:30
  48.6 6.4 %collective-permute-start.13 = (f32[256,128]{0,1:T(8,128)S(1)}, f32[256,128]{0,1:T(8,128)S(1)}, u32[]{:S(2)}, u32[]{:S(2)}) collective-permute-start(f32[256,128]{0,1:T(8,128)S(1)} %pad_maximum_fusion.1), channel_id=1, source_target_pairs={{0,4},{4,0},{8,12},{12,8},{1,5},{5,1},{9,13},{13,9},{2,6},{6,2},{1... | collective-permute-start | bytes 393224 | tf_op jit(solution)/shard_map/ppermute | solution.py:30
  48.6 12.4 %collective-permute-start.7 = (bf16[256,512]{1,0:T(8,128)(2,1)S(1)}, bf16[256,512]{1,0:T(8,128)(2,1)S(1)}, u32[]{:S(2)}, u32[]{:S(2)}) collective-permute-start(bf16[256,512]{1,0:T(8,128)(2,1)S(1)} %constant_dynamic-update-slice_fusion.refs_0_), channel_id=1, source_target_pairs={{0,4},{4,0},{8,12},{12,8},{1,5},{5,1},{9,13},{13,9},{2,6},{6,2},{1... | collective-permute-start | bytes 786440 | tf_op jit(solution)/shard_map/ppermute | solution.py:30
  50.7 10.3 %collective-permute-start.8 = (bf16[256,512]{1,0:T(8,128)(2,1)S(1)}, bf16[256,512]{1,0:T(8,128)(2,1)S(1)}, u32[]{:S(2)}, u32[]{:S(2)}) collective-permute-start(bf16[256,512]{1,0:T(8,128)(2,1)S(1)} %constant_dynamic-update-slice_fusion.refs_0_), channel_id=1, source_target_pairs={{4,8},{8,4},{5,9},{9,5},{6,10},{10,6},{7,11},{11,7},{20,24},{24,20... | collective-permute-start | bytes 786440 | tf_op jit(solution)/shard_map/ppermute | solution.py:30
  51.3 4.9 %collective-permute-start.6 = (bf16[256,512]{0,1:T(8,128)(2,1)S(1)}, bf16[256,512]{0,1:T(8,128)(2,1)S(1)}, u32[]{:S(2)}, u32[]{:S(2)}) collective-permute-start(bf16[256,512]{0,1:T(8,128)(2,1)S(1)} %get-tuple-element.25), channel_id=1, source_target_pairs={{0,1},{1,0},{2,3},{3,2},{4,5},{5,4},{6,7},{7,6},{8,9},{9,8},{10,11... | collective-permute-start | bytes 786440 | tf_op jit(solution)/shard_map/ppermute | solution.py:20
  51.4 15.3 %collective-permute-start.9 = (bf16[256,512]{1,0:T(8,128)(2,1)S(1)}, bf16[256,512]{1,0:T(8,128)(2,1)S(1)}, u32[]{:S(2)}, u32[]{:S(2)}) collective-permute-start(bf16[256,512]{1,0:T(8,128)(2,1)S(1)} %collective-permute-done.4.refs_2_), channel_id=1, source_target_pairs={{4,0},{8,12},{5,1},{9,13},{6,2},{10,14},{7,3},{11,15},{20,16},{24,... | collective-permute-start | bytes 786440 | tf_op jit(solution)/shard_map/ppermute | solution.py:30
  55.8 19.3 %collective-permute-start.14 = (f32[256,128]{0,1:T(8,128)}, f32[256,128]{0,1:T(8,128)}, u32[]{:S(2)}, u32[]{:S(2)}) collective-permute-start(f32[256,128]{0,1:T(8,128)} %add.79), channel_id=1, source_target_pairs={{0,8},{4,12},{8,0},{12,4},{1,9},{5,13},{9,1},{13,5},{2,10},{6,14},... | collective-permute-start | bytes 393224 | tf_op jit(solution)/shard_map/ppermute | solution.py:30
  56.3 0.7 copy-start.10
  57.0 103.6 %all-gather.5.cloned.1.call-start = ((), (), s32[]{:S(2)}) async-start(), calls=%async_computation | async-start | bytes 1310720 | tf_op jit(solution)/shard_map/all_gather | solution.py:141
  66.7 0.7 copy-start.2
  67.4 0.9 copy-start.3
  78.3 4.0 %collective-permute-start.15 = (bf16[4,4224]{1,0:T(4,128)(2,1)S(1)}, bf16[4,4224]{1,0:T(4,128)(2,1)S(1)}, u32[]{:S(2)}, u32[]{:S(2)}) collective-permute-start(bf16[4,4224]{1,0:T(4,128)(2,1)S(1)} %pad_maximum_fusion.2), channel_id=1, source_target_pairs={{0,1},{1,0},{2,3},{3,2},{4,5},{5,4},{6,7},{7,6},{8,9},{9,8},{10,11... | collective-permute-start | bytes 101384 | tf_op jit(solution)/shard_map/ppermute | solution.py:20
  78.4 57.0 %collective-permute-start.10 = (bf16[256,512]{1,0:T(8,128)(2,1)S(1)}, bf16[256,512]{1,0:T(8,128)(2,1)}, u32[]{:S(2)}, u32[]{:S(2)}) collective-permute-start(bf16[256,512]{1,0:T(8,128)(2,1)S(1)} %pad_maximum_fusion.refs_0_), channel_id=1, source_target_pairs={{0,4},{4,0},{8,12},{12,8},{1,5},{5,1},{9,13},{13,9},{2,6},{6,2},{1... | collective-permute-start | bytes 786440 | tf_op jit(solution)/shard_map/ppermute | solution.py:30
  78.5 57.0 %collective-permute-start.11 = (bf16[256,512]{1,0:T(8,128)(2,1)S(1)}, bf16[256,512]{1,0:T(8,128)(2,1)}, u32[]{:S(2)}, u32[]{:S(2)}) collective-permute-start(bf16[256,512]{1,0:T(8,128)(2,1)S(1)} %pad_maximum_fusion.refs_0_), channel_id=1, source_target_pairs={{4,8},{8,4},{5,9},{9,5},{6,10},{10,6},{7,11},{11,7},{20,24},{24,20... | collective-permute-start | bytes 786440 | tf_op jit(solution)/shard_map/ppermute | solution.py:30
  79.9 55.6 %collective-permute-start.12 = (bf16[256,512]{1,0:T(8,128)(2,1)S(1)}, bf16[256,512]{1,0:T(8,128)(2,1)}, u32[]{:S(2)}, u32[]{:S(2)}) collective-permute-start(bf16[256,512]{1,0:T(8,128)(2,1)S(1)} %collective-permute-done.5.refs_2_), channel_id=1, source_target_pairs={{4,0},{8,12},{5,1},{9,13},{6,2},{10,14},{7,3},{11,15},{20,16},{24,... | collective-permute-start | bytes 786440 | tf_op jit(solution)/shard_map/ppermute | solution.py:30
  81.2 27.8 %collective-permute-start.16 = (bf16[4,4224]{1,0:T(4,128)(2,1)S(1)}, bf16[4,4224]{1,0:T(4,128)(2,1)}, u32[]{:S(2)}, u32[]{:S(2)}) collective-permute-start(bf16[4,4224]{1,0:T(4,128)(2,1)S(1)} %pad_maximum_fusion.2), channel_id=1, source_target_pairs={{0,2},{1,3},{2,0},{3,1},{4,6},{5,7},{6,4},{7,5},{8,10},{9,11},{10,... | collective-permute-start | bytes 101384 | tf_op jit(solution)/shard_map/ppermute | solution.py:20
  82.4 40.4 %collective-permute-start.17 = (bf16[4,4224]{1,0:T(4,128)(2,1)S(1)}, bf16[4,4224]{1,0:T(4,128)(2,1)S(1)}, u32[]{:S(2)}, u32[]{:S(2)}) collective-permute-start(bf16[4,4224]{1,0:T(4,128)(2,1)S(1)} %pad_maximum_fusion.2), channel_id=1, source_target_pairs={{0,3},{1,2},{2,1},{3,0},{4,7},{5,6},{6,5},{7,4},{8,11},{9,10},{10,... | collective-permute-start | bytes 101384 | tf_op jit(solution)/shard_map/ppermute | solution.py:20
  109.0 33.6 %collective-permute-start.18 = (bf16[128,3584]{1,0:T(8,128)(2,1)}, bf16[128,3584]{1,0:T(8,128)(2,1)}, u32[]{:S(2)}, u32[]{:S(2)}) collective-permute-start(bf16[128,3584]{1,0:T(8,128)(2,1)} %get-tuple-element.50), channel_id=1, source_target_pairs={{0,1},{1,0},{2,3},{3,2},{4,5},{5,4},{6,7},{7,6},{8,9},{9,8},{10,11... | collective-permute-start | bytes 2752520 | tf_op jit(solution)/shard_map/ppermute | solution.py:20
  122.8 12.7 %copy-start.4 = (bf16[256,512]{1,0:T(8,128)(2,1)S(1)}, bf16[256,512]{1,0:T(8,128)(2,1)}, u32[]{:S(2)}) copy-start(bf16[256,512]{1,0:T(8,128)(2,1)} %copy-done.2) | copy-start | bytes 786436
  142.2 1.2 copy-start.7
  142.4 14.6 %collective-permute-start.19 = (bf16[128,3584]{1,0:T(8,128)(2,1)S(1)}, bf16[128,3584]{1,0:T(8,128)(2,1)S(1)}, u32[]{:S(2)}, u32[]{:S(2)}) collective-permute-start(bf16[128,3584]{1,0:T(8,128)(2,1)S(1)} %get-tuple-element.46), channel_id=1, source_target_pairs={{0,1},{1,0},{2,3},{3,2},{4,5},{5,4},{6,7},{7,6},{8,9},{9,8},{10,11... | collective-permute-start | bytes 2752520 | tf_op jit(solution)/shard_map/ppermute | solution.py:20
  145.7 23.5 %collective-permute-start.20 = (bf16[128,3584]{1,0:T(8,128)(2,1)}, bf16[128,3584]{1,0:T(8,128)(2,1)}, u32[]{:S(2)}, u32[]{:S(2)}) collective-permute-start(bf16[128,3584]{1,0:T(8,128)(2,1)} %add_convert_fusion.7), channel_id=1, source_target_pairs={{0,2},{1,3},{2,0},{3,1},{4,6},{5,7},{6,4},{7,5},{8,10},{9,11},{10,... | collective-permute-start | bytes 2752520 | tf_op jit(solution)/shard_map/ppermute | solution.py:20
  157.0 22.3 %collective-permute-start.21 = (bf16[128,3584]{1,0:T(8,128)(2,1)}, bf16[128,3584]{1,0:T(8,128)(2,1)}, u32[]{:S(2)}, u32[]{:S(2)}) collective-permute-start(bf16[128,3584]{1,0:T(8,128)(2,1)} %get-tuple-element.48), channel_id=1, source_target_pairs={{0,1},{1,0},{2,3},{3,2},{4,5},{5,4},{6,7},{7,6},{8,9},{9,8},{10,11... | collective-permute-start | bytes 2752520 | tf_op jit(solution)/shard_map/ppermute | solution.py:20
  158.1 29.9 %collective-permute-start.22 = (bf16[128,3584]{1,0:T(8,128)(2,1)}, bf16[128,3584]{1,0:T(8,128)(2,1)}, u32[]{:S(2)}, u32[]{:S(2)}) collective-permute-start(bf16[128,3584]{1,0:T(8,128)(2,1)} %add_convert_fusion.6), channel_id=1, source_target_pairs={{0,2},{1,3},{2,0},{3,1},{4,6},{5,7},{6,4},{7,5},{8,10},{9,11},{10,... | collective-permute-start | bytes 2752520 | tf_op jit(solution)/shard_map/ppermute | solution.py:20
  178.0 1.5 copy-start.8
  179.3 17.4 %collective-permute-start.24 = (bf16[128,3584]{1,0:T(8,128)(2,1)}, bf16[128,3584]{1,0:T(8,128)(2,1)}, u32[]{:S(2)}, u32[]{:S(2)}) collective-permute-start(bf16[128,3584]{1,0:T(8,128)(2,1)} %get-tuple-element.44), channel_id=1, source_target_pairs={{0,1},{1,0},{2,3},{3,2},{4,5},{5,4},{6,7},{7,6},{8,9},{9,8},{10,11... | collective-permute-start | bytes 2752520 | tf_op jit(solution)/shard_map/ppermute | solution.py:20
  195.5 34.0 %collective-permute-start.23 = (bf16[256,3584]{1,0:T(8,128)(2,1)}, bf16[256,3584]{1,0:T(8,128)(2,1)}, u32[]{:S(2)}, u32[]{:S(2)}) collective-permute-start(bf16[256,3584]{1,0:T(8,128)(2,1)} %terms.12), channel_id=1, source_target_pairs={{0,1},{1,0},{2,3},{3,2},{4,5},{5,4},{6,7},{7,6},{8,9},{9,8},{10,11... | collective-permute-start | bytes 5505032 | tf_op jit(solution)/shard_map/ppermute | solution.py:20
  195.6 23.4 %collective-permute-start.25 = (bf16[128,3584]{1,0:T(8,128)(2,1)}, bf16[128,3584]{1,0:T(8,128)(2,1)S(1)}, u32[]{:S(2)}, u32[]{:S(2)}) collective-permute-start(bf16[128,3584]{1,0:T(8,128)(2,1)} %add_convert_fusion.5), channel_id=1, source_target_pairs={{0,2},{1,3},{2,0},{3,1},{4,6},{5,7},{6,4},{7,5},{8,10},{9,11},{10,... | collective-permute-start | bytes 2752520 | tf_op jit(solution)/shard_map/ppermute | solution.py:20
  198.4 27.4 %copy-start.9 = (bf16[16,4224]{0,1:T(8,128)(2,1)S(1)}, bf16[16,4224]{0,1:T(8,128)(2,1)}, u32[]{:S(2)}) copy-start(bf16[16,4224]{0,1:T(8,128)(2,1)} %dynamic_update_slice.27) | copy-start | bytes 405508
  198.4 41.5 %collective-permute-start.27 = (bf16[128,3584]{1,0:T(8,128)(2,1)S(1)}, bf16[128,3584]{1,0:T(8,128)(2,1)S(1)}, u32[]{:S(2)}, u32[]{:S(2)}) collective-permute-start(bf16[128,3584]{1,0:T(8,128)(2,1)S(1)} %add_convert_fusion.4), channel_id=1, source_target_pairs={{0,2},{1,3},{2,0},{3,1},{4,6},{5,7},{6,4},{7,5},{8,10},{9,11},{10,... | collective-permute-start | bytes 2752520 | tf_op jit(solution)/shard_map/ppermute | solution.py:20
  225.8 14.2 %collective-permute-start.26 = (bf16[256,3584]{1,0:T(8,128)(2,1)S(1)}, bf16[256,3584]{1,0:T(8,128)(2,1)S(1)}, u32[]{:S(2)}, u32[]{:S(2)}) collective-permute-start(bf16[256,3584]{1,0:T(8,128)(2,1)S(1)} %terms.13), channel_id=1, source_target_pairs={{0,1},{1,0},{2,3},{3,2},{4,5},{5,4},{6,7},{7,6},{8,9},{9,8},{10,11... | collective-permute-start | bytes 5505032 | tf_op jit(solution)/shard_map/ppermute | solution.py:20
  246.7 3.8 %copy-start.1 = (bf16[7168,64]{0,1:T(8,128)(2,1)S(1)}, bf16[7168,64]{0,1:T(8,128)(2,1)}, u32[]{:S(2)}) copy-start(bf16[7168,64]{0,1:T(8,128)(2,1)} %param.10) | copy-start | bytes 2752516
  248.6 1.8 copy-start.6
Sparse Core Ops, SparseCore 0:
  57.1 32.0 all-gather.6
  90.8 29.4 all-gather.4

commit v4 on v3

--- a/solution.py
+++ b/solution.py
@@ -4,6 +4,7 @@
 import jax.numpy as jnp
 from jax import lax
 from jax.experimental import pallas as pl
+from jax.experimental.layout import Layout, with_layout_constraint
 from jax.experimental.pallas import tpu as pltpu
 from jax.sharding import PartitionSpec as P
 
@@ -39,8 +40,9 @@
 
 
 def terms_kernel(size, count, first, place_ref, *refs):
-    blocks, (w_ref, out_ref, feats, held, sems, held_sems) = refs[:count], refs[count:]
-    width, tile = feats.shape[1] // size, out_ref.shape[1]
+    blocks, w_ref, outs = refs[:count], refs[count], refs[count + 1 : -4]
+    feats, held, sems, held_sems = refs[-4:]
+    width, tile = feats.shape[1] // size, outs[0].shape[1]
     j, steps = pl.program_id(0), pl.num_programs(0)
     slots = held.shape[0]
 
@@ -86,26 +88,29 @@
 
     fetch(j).wait()
     weight = held[lax.rem(j, slots)].reshape(size * width, tile)
-    out_ref[...] = jnp.dot(feats[...], weight, preferred_element_type=f32).astype(bf16)
+    total = jnp.dot(feats[...], weight, preferred_element_type=f32).astype(bf16)
+    rows = outs[0].shape[0]
+    for index, out_ref in enumerate(outs):
+        out_ref[...] = total[index * rows : (index + 1) * rows]
 
     @pl.when(j + slots < steps)
     def _():
         fetch(j + slots).start()
 
 
-def block_terms(blocks, down_weight, col_start, cols):
+def block_terms(blocks, down_weight, col_start, cols, outs):
     size, _, width, _ = down_weight.shape
     rows = blocks[-1].shape[-2]
     tile = max(n for n in range(128, 513, 128) if cols % n == 0)
     slots = min(4, cols // tile)
     return pl.pallas_call(
         functools.partial(terms_kernel, size, len(blocks), col_start),
-        out_shape=jax.ShapeDtypeStruct((rows, cols), bf16),
+        out_shape=[jax.ShapeDtypeStruct((rows // outs, cols), bf16)] * outs,
         grid_spec=pltpu.PrefetchScalarGridSpec(
             num_scalar_prefetch=1,
             grid=(cols // tile,),
             in_specs=[pl.BlockSpec(memory_space=pl.ANY)] * (len(blocks) + 1),
-            out_specs=pl.BlockSpec((rows, tile), lambda j, place: (0, j)),
+            out_specs=[pl.BlockSpec((rows // outs, tile), lambda j, place: (0, j))] * outs,
             scratch_shapes=[
                 pltpu.VMEM((rows, size * width), bf16),
                 pltpu.VMEM((slots, size, width, tile), bf16),
@@ -114,16 +119,17 @@
             ],
         ),
         compiler_params=pltpu.CompilerParams(vmem_limit_bytes=40 << 20),
-        cost_estimate=pl.CostEstimate(flops=1000, bytes_accessed=1000, transcendentals=0),
+        cost_estimate=pl.CostEstimate(flops=8 * rows * size * width * cols, bytes_accessed=1000, transcendentals=0),
         name="terms",
     )(lax.axis_index("tensor").reshape(1), *blocks, down_weight)
 
 
-def gathered_terms(blocks, down_weight, col_start, cols):
+def gathered_terms(blocks, down_weight, col_start, cols, outs):
     weight = lax.slice_in_dim(down_weight, col_start, col_start + cols, axis=3)
-    return lax.dot_general(
+    terms = lax.dot_general(
         blocks[0], weight[:, 0], (((0, 2), (0, 1)), ((), ())), preferred_element_type=f32
-    ).astype(bf16)
+    )
+    return jnp.split(terms.astype(bf16), outs)
 
 
 def add(*values):
@@ -133,11 +139,12 @@
     return total.astype(bf16)
 
 
-def far_features(output_grad):
+def far_features(output_grad, parts):
     groups, place = lax.axis_size("dp"), lax.axis_index("dp")
     line = lax.axis_size("tensor") == 4
 
     def gather(block):
+        block = with_layout_constraint(block, Layout(major_to_minor=(0, 1)))
         return [lax.all_gather(block, "tensor", axis=0)]
 
     turned = jnp.transpose(output_grad[0], (0, 2, 1))
@@ -151,17 +158,15 @@
         cut = slice(half * rows, (half + 1) * rows)
         for step in range(2, groups, 2):
             sent = [swap(pieces[step + 1][cut], step + 1), swap(pieces[step][cut], step)]
-            block = jnp.concatenate(sent)
-            if last is not None:
-                block = after(block, last)
+            block = after(jnp.concatenate(sent), *([parts] if last is None else last))
             far.append((half, step, spread(block) if line else gather(block)))
-            last = far[-1][2][2] if line else far[-1][2][0]
+            last = far[-1][2][1:4] if line else far[-1][2]
             if beside is None:
-                beside = swap(after(pieces[1], last), 1)
+                beside = swap(after(pieces[1], *last), 1)
                 far[0] = far[0][:2] + ([after(far[0][2][0], beside)] + far[0][2][1:],)
-    beside = gather(after(beside, last))
-    own = gather(after(pieces[0], last))
-    return far, beside, own, last
+    beside = gather(after(beside, far[0][2][-1]))
+    own = gather(after(pieces[0], far[0][2][-1]))
+    return far, beside, own
 
 
 def example_gradients(acts_low, grads_low, local_ids, examples):
@@ -181,16 +186,18 @@
 
 
 def gather_examples(example_grad, example_group):
-    count, width = example_grad.shape
-    groups = lax.axis_size("dp")
+    count = example_grad.shape[0]
+    groups, place = lax.axis_size("dp"), lax.axis_index("dp")
     group_column = jnp.broadcast_to(example_group.astype(bf16)[:, None], (count, 128))
     held = jnp.concatenate([example_grad, group_column], axis=1)
-    every = jnp.zeros((groups * count, width + 128), bf16)
-    for step in range(groups):
-        value = swap(held, step) if step else held
-        row = (lax.axis_index("dp") ^ step) * count
-        every = lax.dynamic_update_slice_in_dim(every, value, row, 0)
-    return every
+    values = [held] + [swap(held, step) for step in range(1, groups)]
+    ordered = []
+    for group in range(groups):
+        value = values[0]
+        for step in range(1, groups):
+            value = jnp.where((place ^ group) == step, values[step], value)
+        ordered.append(value)
+    return jnp.concatenate(ordered, axis=0)
 
 
 def fisher_and_groups(every, flat_width):
@@ -217,11 +224,10 @@
     tokens, cols = hidden_acts.shape
     col_parts = COL_PARTS if cols % (256 * COL_PARTS) == 0 else 1
     part, rows = cols // col_parts, tokens // FAR_PARTS
-    far, beside, own, last = far_features(output_grad)
-
-    def multiply(blocks, at):
+
+    def multiply(blocks, at, outs=2, width=part):
         kernel = block_terms if down_weight.shape[2] % 128 == 0 else gathered_terms
-        return kernel(blocks, down_weight, at * part, part)
+        return kernel(blocks, down_weight, at * part, width, outs)
 
     acts_part = jnp.dot(hidden_acts, input_basis, preferred_element_type=f32)
     grads_part = lax.dot_general(
@@ -231,9 +237,9 @@
         preferred_element_type=f32,
     )
     parts = jnp.concatenate([acts_part, grads_part], axis=1)
+    far, beside, own = far_features(output_grad, parts)
     if lax.axis_size("tensor") == 4:
-        low = parts = after(parts, last)
-        far[0] = far[0][:2] + ([after(far[0][2][0], parts)] + far[0][2][1:],)
+        low = after(parts, far[0][2][-1])
         for step in (1, 2):
             low = low + across(low, step)
     else:
@@ -244,47 +250,40 @@
 
     def settle(latest):
         count = len(pairs)
-        both, other = held[count]
-        pairs.append(add(after(both[rows:], latest), other))
+        pairs.append(add(after(held[count][0], latest), held[count][1]))
         arrived.append(swap(pairs[count], units[count][2]))
 
     for count, (blocks, half, step, at) in enumerate(units):
         earlier = pairs[-1:] + arrived[:-1][-1:]
-        if count == 1:
-            earlier = earlier + far[-1][2] + [every]
-        if count == 3:
-            earlier.append(beside[0])
-        if earlier:
-            blocks = [after(blocks[0], *earlier)] + blocks[1:]
-        both = multiply(blocks, at)
-        held.append((both, swap(both[:rows], 1)))
-        if count == 0:
-            acts_low, grads_low = jnp.split(after(low, both), 2, axis=1)
+        if count == len(units) - 1:
+            acts_low, grads_low = jnp.split(after(low, *arrived[:-1][-1:]), 2, axis=1)
             example_grad = example_gradients(
                 acts_low, grads_low, token_example[0], example_group.shape[0]
             )
             every = gather_examples(example_grad, example_group)
-        else:
+            earlier += [beside[0], every]
+        if earlier:
+            blocks = [after(blocks[0], *earlier)] + blocks[1:]
+        sent, both = multiply(blocks, at)
+        held.append((both, swap(sent, 1)))
+        if count:
             settle(both)
 
-    near = []
-    for at in range(col_parts):
-        earlier = pairs[-1:] + arrived[:-1][-1:] + [own[0]]
-        term = multiply([after(beside[0], *earlier)], at)
-        near.append(swap(term, 1))
-        if at == 0:
-            settle(term)
-    fisher, group_grad = fisher_and_groups(after(every, term), example_grad.shape[1])
+    fisher, group_grad = fisher_and_groups(after(every, arrived[-2]), example_grad.shape[1])
+    beside = [after(beside[0], pairs[-1], arrived[-2], fisher, group_grad)]
+    near = multiply(beside, 0, FAR_PARTS, cols)
+    settle(near[0])
+    near = [swap(term, 1) for term in near]
+    own = [after(own[0], pairs[-1], arrived[-2])]
+    mine = multiply(own, 0, FAR_PARTS, cols)
     result = jnp.zeros((tokens, cols), bf16)
-    for at in range(col_parts):
-        earlier = [near[at], term] + ([arrived[-1]] if at == col_parts - 1 else [])
-        term = multiply([after(own[0], *earlier)], at)
-        for half in range(FAR_PARTS):
+    for half in range(FAR_PARTS):
+        for at in range(col_parts):
             sums = [
                 arrived[count] for count, unit in enumerate(units) if unit[1:] == (half, unit[2], at)
             ]
-            cut = slice(half * rows, (half + 1) * rows)
-            value = add(term[cut], near[at][cut], *sums)
+            cut = slice(at * part, (at + 1) * part)
+            value = add(mine[half][:, cut], near[half][:, cut], *sums)
             result = lax.dynamic_update_slice(result, value, (half * rows, at * part))
     return (result, fisher, group_grad)
 

time: 262 us -> 200 us (0.76); the launches traced: 257 us -> 198 us
  local copies, waits for them, and re-layouts: 67 us -> 13.4 us
  waiting for transfers between devices: 72.6 us -> 56.4 us
  starting transfers between devices: 21.7 us -> 29.5 us
  other arithmetic: 14.7 us -> 19.3 us
    dynamic_update_slice x4 -> x0, local copies, waits for them, and re-layouts: 46.6 us -> none  [gather_examples(): every = lax.dynamic_update_slice_in_dim(every, value, row, 0)]
    ppermute x18, waiting for transfers between devices: 37.9 us -> 21.3 us  [swap(): return lax.ppermute(value, 'dp', [(d, d ^ step) for d in range(size)])]
    ppermute x10, starting transfers between devices: 10.1 us -> 16.9 us  [across(): return lax.ppermute(value, 'tensor', pairs)]
    slice x4 -> x0, local copies, waits for them, and re-layouts: 4.26 us -> none  [settle(): pairs.append(add(after(both[rows:], latest), other))]
    unnamed x29 -> x52, local copies, waits for them, and re-layouts: 5.3 us -> 8.66 us
    all_gather x2 -> x0, local copies, waits for them, and re-layouts: 2.99 us -> none  [gather(): return [lax.all_gather(block, 'tensor', axis=0)]]
    pallas_call x8 -> x6, Pallas kernels: 58.5 us -> 56.6 us  [block_terms(): pl.pallas_call(functools.partial(terms_kernel, size, len(blocks), col_sta...]
  transfers between devices with their start and end apart: 30 -> 30, of which waited for: 10 -> 11; matrix products, arithmetic and copies ran while one was open for 31% -> 15% of each run, Pallas kernels for 20% -> 29%
where the time goes in v4:
time: 200 us; the launch traced here: 198 us
  Pallas kernels  56.6 us (28%)
  waiting for transfers between devices  56.4 us (28%)
  starting transfers between devices  29.5 us (15%)
  other arithmetic  19.3 us (10%)
  between operations  14.6 us (7%)
  local copies, waits for them, and re-layouts  13.4 us (7%)
  matrix products  8.29 us (4%)
    pallas_call x6, Pallas kernels, block_terms(): pl.pallas_call(functools.partial(terms_kernel, size, len(blocks), col_sta...  56.6 us
    ppermute x10, waiting for transfers between devices, across(): return lax.ppermute(value, 'tensor', pairs)  35.1 us
    ppermute x18, waiting for transfers between devices, swap(): return lax.ppermute(value, 'dp', [(d, d ^ step) for d in range(size)])  21.3 us
    ppermute x10, starting transfers between devices, across(): return lax.ppermute(value, 'tensor', pairs)  16.9 us
    ppermute x18, starting transfers between devices, swap(): return lax.ppermute(value, 'dp', [(d, d ^ step) for d in range(size)])  12.5 us
    convert_element_type x5, other arithmetic, add(): return total.astype(bf16)  8.96 us
    unnamed x52, local copies, waits for them, and re-layouts  8.66 us
    dynamic_update_slice x3, other arithmetic, per_device(): result = lax.dynamic_update_slice(result, value, (half * rows, at * part))  4.91 us
  transfers between devices with their start and end apart: 30, of which 11 were waited for; matrix products, arithmetic and copies ran while one was open for 15% of the time, Pallas kernels for 29%

profile of v4, /device:TPU:0, one launch (start us, length us, event | category | flops | bytes accessed | tf_op | source)
XLA Modules:
  0.0 198.0 jit_solution(4958148362187572064)
XLA Ops:
  7.2 1.3 constant_dynamic-slice_fusion.3
  8.8 3.0 %collective-permute-start.1 = (bf16[128,512]{1,0:T(8,128)(2,1)S(1)}, bf16[128,512]{1,0:T(8,128)(2,1)S(1)}, u32[]{:S(2)}, u32[]{:S(2)}) collective-permute-start(bf16[128,512]{1,0:T(8,128)(2,1)S(1)} %get-tuple-element.68), channel_id=1, source_target_pairs={{0,2},{1,3},{2,0},{3,1},{4,6},{5,7},{6,4},{7,5},{8,10},{9,11},{10,... | collective-permute-start | bytes 393224 | tf_op jit(solution)/shard_map/ppermute | solution.py:21
  12.0 3.4 %fusion.17 = f32[256,64]{0,1:T(8,128)S(1)} fusion(bf16[256,7168]{1,0:T(8,128)(2,1)} %param.7, bf16[7168,64]{0,1:T(8,128)(2,1)S(1)} %copy-done), kind=kOutput, calls=%fused_computation.48 | convolution fusion | flops 234881024 | bytes 4653056 | tf_op jit(solution)/shard_map/dot_general | solution.py:232
  15.8 0.7 pad_maximum_fusion.3
  16.4 1.5 collective-permute-done
  17.9 0.7 collective-permute-start.7
  18.6 4.4 %collective-permute-start.6 = (bf16[256,512]{1,0:T(8,128)(2,1)S(1)}, bf16[256,512]{1,0:T(8,128)(2,1)S(1)}, u32[]{:S(2)}, u32[]{:S(2)}) collective-permute-start(bf16[256,512]{1,0:T(8,128)(2,1)S(1)} %pad_maximum_fusion.refs_0_), channel_id=1, source_target_pairs={{0,4},{4,0},{8,12},{12,8},{1,5},{5,1},{9,13},{13,9},{2,6},{6,2},{1... | collective-permute-start | bytes 786440 | tf_op jit(solution)/shard_map/ppermute | solution.py:31
  23.0 0.8 collective-permute-start.5
  24.3 5.8 %collective-permute-done.6.refs_1_ = bf16[256,512]{1,0:T(8,128)(2,1)S(1)} collective-permute-done((bf16[256,512]{1,0:T(8,128)(2,1)S(1)}, bf16[256,512]{1,0:T(8,128)(2,1)S(1)}, u32[]{:S(2)}, u32[]{:S(2)}) %collective-permute-start.6) | collective-permute-done | bytes 262176 | tf_op jit(solution)/shard_map/ppermute | solution.py:31
  30.1 10.4 %collective-permute-done.2.refs_2_ = bf16[256,512]{1,0:T(8,128)(2,1)S(1)} collective-permute-done((bf16[256,512]{1,0:T(8,128)(2,1)S(1)}, bf16[256,512]{1,0:T(8,128)(2,1)S(1)}, u32[]{:S(2)}, u32[]{:S(2)}) %collective-permute-start.2) | collective-permute-done | bytes 262176 | tf_op jit(solution)/shard_map/ppermute | solution.py:31
  40.5 1.3 collective-permute-start.3
  41.9 0.9 copy.20
  42.9 0.7 collective-permute-start.12
  43.6 5.4 %collective-permute-start.11 = (bf16[256,512]{1,0:T(8,128)(2,1)S(1)}, bf16[256,512]{1,0:T(8,128)(2,1)}, u32[]{:S(2)}, u32[]{:S(2)}) collective-permute-start(bf16[256,512]{1,0:T(8,128)(2,1)S(1)} %pad_maximum_fusion.1.refs_0_), channel_id=1, source_target_pairs={{0,8},{4,12},{8,0},{12,4},{1,9},{5,13},{9,1},{13,5},{2,10},{6,14},... | collective-permute-start | bytes 786440 | tf_op jit(solution)/shard_map/ppermute | solution.py:31
  49.2 1.9 collective-permute-done.3.refs_4_
  51.2 0.7 collective-permute-start.16
  51.9 0.9 copy-done.13
  52.8 6.8 %terms.7 = (bf16[128,3584]{1,0:T(8,128)(2,1)S(1)}, bf16[128,3584]{1,0:T(8,128)(2,1)S(1)}) custom-call(s32[1]{0:T(128)} %bitcast.place_ref, bf16[256,512]{1,0:T(8,128)(2,1)S(1)} %pad_maximum_fusion.refs_0_, bf16[256,512]{1,0:T(8,128)(2,1)S(1)} %collective-permute-done.6.refs_1_, bf16[256,512]{1,0:T(8,128)(2,1)S(1)} %collective-permute-done.2.refs_2_, ...), custom_call_target="tpu_custom_call" | custom-call | flops 15032385536 | bytes 1000 | tf_op jit(solution)/shard_map/terms/pallas_call | solution.py:106
  59.8 8.0 %collective-permute-done.16 = f32[256,128]{0,1:T(8,128)S(1)} collective-permute-done((f32[256,128]{0,1:T(8,128)}, f32[256,128]{0,1:T(8,128)S(1)}, u32[]{:S(2)}, u32[]{:S(2)}) %collective-permute-start.16) | collective-permute-done | bytes 131104 | tf_op jit(solution)/shard_map/ppermute | solution.py:31
  67.8 1.6 add.69
  69.4 2.3 %collective-permute-start.17 = (f32[256,128]{0,1:T(8,128)}, f32[256,128]{0,1:T(8,128)}, u32[]{:S(2)}, u32[]{:S(2)}) collective-permute-start(f32[256,128]{0,1:T(8,128)} %add.69), channel_id=1, source_target_pairs={{0,8},{4,12},{8,0},{12,4},{1,9},{5,13},{9,1},{13,5},{2,10},{6,14},... | collective-permute-start | bytes 393224 | tf_op jit(solution)/shard_map/ppermute | solution.py:31
  71.7 1.0 copy-done.5
  72.7 0.9 copy-done.7
  73.6 0.9 copy-done.9
  74.5 7.4 %terms.6 = (bf16[128,3584]{1,0:T(8,128)(2,1)}, bf16[128,3584]{1,0:T(8,128)(2,1)S(1)}) custom-call(s32[1]{0:T(128)} %bitcast.place_ref, bf16[256,512]{1,0:T(8,128)(2,1)S(1)} %pad_maximum_fusion.refs_0_, bf16[256,512]{1,0:T(8,128)(2,1)S(1)} %copy-done.7, bf16[256,512]{1,0:T(8,128)(2,1)S(1)} %copy-done.9, bf16[256,512]{1,0:T(8,128)(2,1)S(1)} %copy-done.5, ...), custom_call_target="tpu_custom_call" | custom-call | flops 15032385536 | bytes 1000 | tf_op jit(solution)/shard_map/terms/pallas_call | solution.py:106
  82.1 5.9 %collective-permute-done.17 = f32[256,128]{0,1:T(8,128)} collective-permute-done((f32[256,128]{0,1:T(8,128)}, f32[256,128]{0,1:T(8,128)}, u32[]{:S(2)}, u32[]{:S(2)}) %collective-permute-start.17) | collective-permute-done | bytes 131104 | tf_op jit(solution)/shard_map/ppermute | solution.py:31
  88.0 1.3 collective-permute-start.13
  89.3 1.0 add.70
  90.3 1.4 add_convert_fusion.7
  91.7 1.8 collective-permute-start.15
  93.5 3.0 %collective-permute-done.13.refs_4_ = bf16[256,512]{1,0:T(8,128)(2,1)S(1)} collective-permute-done((bf16[256,512]{1,0:T(8,128)(2,1)}, bf16[256,512]{1,0:T(8,128)(2,1)S(1)}, u32[]{:S(2)}, u32[]{:S(2)}) %collective-permute-start.13) | collective-permute-done | bytes 262176 | tf_op jit(solution)/shard_map/ppermute | solution.py:31
  96.5 9.1 %terms.8 = (bf16[128,3584]{1,0:T(8,128)(2,1)S(1)}, bf16[128,3584]{1,0:T(8,128)(2,1)S(1)}) custom-call(s32[1]{0:T(128)} %bitcast.place_ref, bf16[256,512]{1,0:T(8,128)(2,1)S(1)} %pad_maximum_fusion.1.refs_0_, bf16[256,512]{1,0:T(8,128)(2,1)} %collective-permute-done.10.refs_1_, bf16[256,512]{1,0:T(8,128)(2,1)} %collective-permute-done.11.refs_2_, ...), custom_call_target="tpu_custom_call" | custom-call | flops 15032385536 | bytes 1000 | tf_op jit(solution)/shard_map/terms/pallas_call | solution.py:106
  105.6 5.7 %collective-permute-done.15 = bf16[128,3584]{1,0:T(8,128)(2,1)S(1)} collective-permute-done((bf16[128,3584]{1,0:T(8,128)(2,1)S(1)}, bf16[128,3584]{1,0:T(8,128)(2,1)S(1)}, u32[]{:S(2)}, u32[]{:S(2)}) %collective-permute-start.15) | collective-permute-done | bytes 917536 | tf_op jit(solution)/shard_map/ppermute | solution.py:21
  111.3 0.9 copy-done.17
  112.3 1.0 fusion.5
  113.3 1.6 reshape.78
  114.9 1.0 divide_convert_fusion
  116.1 1.3 collective-permute-start.19
  117.4 0.5 collective-permute-start.18
  118.0 2.3 %add_convert_fusion.6 = bf16[128,3584]{1,0:T(8,128)(2,1)} fusion(bf16[128,3584]{1,0:T(8,128)(2,1)} %collective-permute-done.14, bf16[128,3584]{1,0:T(8,128)(2,1)S(1)} %get-tuple-element.43), kind=kLoop, calls=%fused_computation.6 | loop fusion | flops 1835008 | bytes 2752512 | tf_op jit(solution)/shard_map/convert_element_type | solution.py:139
  120.3 1.2 collective-permute-start.22
  121.7 0.8 pad_maximum_fusion.2
  122.5 8.8 %terms.9 = (bf16[128,3584]{1,0:T(8,128)(2,1)S(1)}, bf16[128,3584]{1,0:T(8,128)(2,1)S(1)}) custom-call(s32[1]{0:T(128)} %bitcast.place_ref, bf16[256,512]{1,0:T(8,128)(2,1)S(1)} %pad_maximum_fusion.1.refs_0_, bf16[256,512]{1,0:T(8,128)(2,1)} %collective-permute-done.10.refs_1_, bf16[256,512]{1,0:T(8,128)(2,1)} %collective-permute-done.11.refs_2_, ...), custom_call_target="tpu_custom_call" | custom-call | flops 15032385536 | bytes 1000 | tf_op jit(solution)/shard_map/terms/pallas_call | solution.py:106
  131.3 0.5 collective-permute-start.23
  131.8 11.3 %collective-permute-done.22 = bf16[128,3584]{1,0:T(8,128)(2,1)S(1)} collective-permute-done((bf16[128,3584]{1,0:T(8,128)(2,1)}, bf16[128,3584]{1,0:T(8,128)(2,1)S(1)}, u32[]{:S(2)}, u32[]{:S(2)}) %collective-permute-start.22) | collective-permute-done | bytes 917536 | tf_op jit(solution)/shard_map/ppermute | solution.py:21
  143.2 2.5 %add_convert_fusion.5 = bf16[128,3584]{1,0:T(8,128)(2,1)} fusion(bf16[128,3584]{1,0:T(8,128)(2,1)} %collective-permute-done.21, bf16[128,3584]{1,0:T(8,128)(2,1)S(1)} %get-tuple-element.50), kind=kLoop, calls=%fused_computation.5 | loop fusion | flops 1835008 | bytes 2752512 | tf_op jit(solution)/shard_map/convert_element_type | solution.py:139
  145.7 1.2 collective-permute-start.24
  147.0 0.9 fusion.9
  147.8 2.7 %fusion.7 = f32[1024,1024]{1,0:T(8,128)} fusion(bf16[16,4224]{1,0:T(8,128)(2,1)S(1)} %copy-done.21, s32[]{:T(128)S(6)} %select_n.121, s32[]{:T(128)S(6)} %select_n.122), kind=kOutput, calls=%fused_computation.31 | convolution fusion | flops 33554432 | bytes 4259848 | tf_op jit(solution)/shard_map/dot_general | solution.py:211
  150.6 12.5 %terms.10 = (bf16[128,7168]{1,0:T(8,128)(2,1)}, bf16[128,7168]{1,0:T(8,128)(2,1)S(1)}) custom-call(s32[1]{0:T(128)} %bitcast.place_ref, bf16[4,256,512]{2,1,0:T(8,128)(2,1)S(1)} %bitcast.40, bf16[4,1,512,7168]{3,2,1,0:T(8,128)(2,1)} %refs_1_.3), custom_call_target="tpu_custom_call" | custom-call | flops 30064771072 | bytes 1000 | tf_op jit(solution)/shard_map/terms/pallas_call | solution.py:106
  163.2 0.5 collective-permute-start.26
  163.7 1.2 add_convert_fusion.4
  164.9 0.8 collective-permute-start.27
  165.7 2.0 %collective-permute-done.24 = bf16[128,3584]{1,0:T(8,128)(2,1)S(1)} collective-permute-done((bf16[128,3584]{1,0:T(8,128)(2,1)}, bf16[128,3584]{1,0:T(8,128)(2,1)S(1)}, u32[]{:S(2)}, u32[]{:S(2)}) %collective-permute-start.24) | collective-permute-done | bytes 917536 | tf_op jit(solution)/shard_map/ppermute | solution.py:21
  167.7 1.2 copy-done.3
  169.0 12.0 %terms.11 = (bf16[128,7168]{1,0:T(8,128)(2,1)S(1)}, bf16[128,7168]{1,0:T(8,128)(2,1)S(1)}) custom-call(s32[1]{0:T(128)} %bitcast.place_ref, bf16[4,256,512]{2,1,0:T(8,128)(2,1)S(1)} %bitcast.41, bf16[4,1,512,7168]{3,2,1,0:T(8,128)(2,1)} %refs_1_.3), custom_call_target="tpu_custom_call" | custom-call | flops 30064771072 | bytes 1000 | tf_op jit(solution)/shard_map/terms/pallas_call | solution.py:106
  181.0 1.5 add_convert_fusion.3
  182.5 0.4 dynamic_update_slice.12
  182.9 0.8 copy-done.20
  183.7 1.5 fusion.1
  185.2 1.6 fusion.2
  186.8 0.8 collective-permute-done.27
  187.6 1.8 fusion.3
  189.4 1.8 copy-done.16
  (95 shorter events, 2.4 us)
Async XLA Ops:
  7.2 4.9 %copy-start = (bf16[7168,64]{0,1:T(8,128)(2,1)S(1)}, bf16[7168,64]{0,1:T(8,128)(2,1)}, u32[]{:S(2)}) copy-start(bf16[7168,64]{0,1:T(8,128)(2,1)} %param.10) | copy-start | bytes 2752516
  7.2 115.3 %all-gather.7.cloned.1.call-start = ((), (), s32[]{:S(2)}) async-start(), calls=%async_computation.1 | async-start | bytes 1310720 | tf_op jit(solution)/shard_map/all_gather | solution.py:148
  8.8 7.7 %collective-permute-start.1 = (bf16[128,512]{1,0:T(8,128)(2,1)S(1)}, bf16[128,512]{1,0:T(8,128)(2,1)S(1)}, u32[]{:S(2)}, u32[]{:S(2)}) collective-permute-start(bf16[128,512]{1,0:T(8,128)(2,1)S(1)} %get-tuple-element.68), channel_id=1, source_target_pairs={{0,2},{1,3},{2,0},{3,1},{4,6},{5,7},{6,4},{7,5},{8,10},{9,11},{10,... | collective-permute-start | bytes 393224 | tf_op jit(solution)/shard_map/ppermute | solution.py:21
  11.9 3.5 %copy-start.15 = (bf16[1,4,512,256]{3,2,1,0:T(8,128)(2,1)S(1)}, bf16[1,4,512,256]{3,2,1,0:T(8,128)(2,1)}, u32[]{:S(2)}) copy-start(bf16[1,4,512,256]{3,2,1,0:T(8,128)(2,1)} %param.8) | copy-start | bytes 3145732
  11.9 3.5 %copy-start.23 = (bf16[1,4,512,64]{2,3,1,0:T(8,128)(2,1)S(1)}, bf16[1,4,512,64]{2,3,1,0:T(8,128)(2,1)}, u32[]{:S(2)}) copy-start(bf16[1,4,512,64]{2,3,1,0:T(8,128)(2,1)} %param.11) | copy-start | bytes 786436
  12.0 5.9 %collective-permute-start = (bf16[128,512]{1,0:T(8,128)(2,1)S(1)}, bf16[128,512]{1,0:T(8,128)(2,1)S(1)}, u32[]{:S(2)}, u32[]{:S(2)}) collective-permute-start(bf16[128,512]{1,0:T(8,128)(2,1)S(1)} %get-tuple-element.66), channel_id=1, source_target_pairs={{0,3},{1,2},{2,1},{3,0},{4,7},{5,6},{6,5},{7,4},{8,11},{9,10},{10,... | collective-permute-start | bytes 393224 | tf_op jit(solution)/shard_map/ppermute | solution.py:21
  15.4 26.4 %copy-start.24 = (s32[1,256]{1,0:T(1,128)S(1)}, s32[1,256]{1,0:T(1,128)}, u32[]{:S(2)}) copy-start(s32[1,256]{1,0:T(1,128)} %param.12) | copy-start | bytes 3076
  15.4 26.4 %copy-start.25 = (s32[4]{0:T(128)S(1)}, s32[4]{0:T(128)}, u32[]{:S(2)}) copy-start(s32[4]{0:T(128)} %param.13) | copy-start | bytes 52
  17.9 6.3 %collective-permute-start.7 = (bf16[256,512]{1,0:T(8,128)(2,1)S(1)}, bf16[256,512]{1,0:T(8,128)(2,1)S(1)}, u32[]{:S(2)}, u32[]{:S(2)}) collective-permute-start(bf16[256,512]{1,0:T(8,128)(2,1)S(1)} %pad_maximum_fusion.refs_0_), channel_id=1, source_target_pairs={{4,8},{8,4},{5,9},{9,5},{6,10},{10,6},{7,11},{11,7},{20,24},{24,20... | collective-permute-start | bytes 786440 | tf_op jit(solution)/shard_map/ppermute | solution.py:31
  18.6 11.5 %collective-permute-start.6 = (bf16[256,512]{1,0:T(8,128)(2,1)S(1)}, bf16[256,512]{1,0:T(8,128)(2,1)S(1)}, u32[]{:S(2)}, u32[]{:S(2)}) collective-permute-start(bf16[256,512]{1,0:T(8,128)(2,1)S(1)} %pad_maximum_fusion.refs_0_), channel_id=1, source_target_pairs={{0,4},{4,0},{8,12},{12,8},{1,5},{5,1},{9,13},{13,9},{2,6},{6,2},{1... | collective-permute-start | bytes 786440 | tf_op jit(solution)/shard_map/ppermute | solution.py:31
  23.0 17.5 %collective-permute-start.2 = (bf16[256,512]{1,0:T(8,128)(2,1)S(1)}, bf16[256,512]{1,0:T(8,128)(2,1)S(1)}, u32[]{:S(2)}, u32[]{:S(2)}) collective-permute-start(bf16[256,512]{1,0:T(8,128)(2,1)S(1)} %pad_maximum_fusion.refs_0_), channel_id=1, source_target_pairs={{0,8},{4,12},{8,0},{12,4},{1,9},{5,13},{9,1},{13,5},{2,10},{6,14},... | collective-permute-start | bytes 786440 | tf_op jit(solution)/shard_map/ppermute | solution.py:31
  23.0 19.9 %collective-permute-start.5 = (bf16[128,512]{1,0:T(8,128)(2,1)S(1)}, bf16[128,512]{1,0:T(8,128)(2,1)S(1)}, u32[]{:S(2)}, u32[]{:S(2)}) collective-permute-start(bf16[128,512]{1,0:T(8,128)(2,1)S(1)} %get-tuple-element.67), channel_id=1, source_target_pairs={{0,2},{1,3},{2,0},{3,1},{4,6},{5,7},{6,4},{7,5},{8,10},{9,11},{10,... | collective-permute-start | bytes 393224 | tf_op jit(solution)/shard_map/ppermute | solution.py:21
  23.8 19.1 %collective-permute-start.4 = (bf16[128,512]{1,0:T(8,128)(2,1)S(1)}, bf16[128,512]{1,0:T(8,128)(2,1)S(1)}, u32[]{:S(2)}, u32[]{:S(2)}) collective-permute-start(bf16[128,512]{1,0:T(8,128)(2,1)S(1)} %get-tuple-element.65), channel_id=1, source_target_pairs={{0,3},{1,2},{2,1},{3,0},{4,7},{5,6},{6,5},{7,4},{8,11},{9,10},{10,... | collective-permute-start | bytes 393224 | tf_op jit(solution)/shard_map/ppermute | solution.py:21
  24.2 35.4 %copy-start.4 = (bf16[256,512]{1,0:T(8,128)(2,1)}, bf16[256,512]{1,0:T(8,128)(2,1)S(1)}, u32[]{:S(2)}) copy-start(bf16[256,512]{1,0:T(8,128)(2,1)S(1)} %collective-permute-done.7.refs_3_) | copy-start | bytes 786436
  30.1 29.6 %copy-start.6 = (bf16[256,512]{1,0:T(8,128)(2,1)}, bf16[256,512]{1,0:T(8,128)(2,1)S(1)}, u32[]{:S(2)}) copy-start(bf16[256,512]{1,0:T(8,128)(2,1)S(1)} %collective-permute-done.6.refs_1_) | copy-start | bytes 786436
  40.5 19.2 %copy-start.8 = (bf16[256,512]{1,0:T(8,128)(2,1)}, bf16[256,512]{1,0:T(8,128)(2,1)S(1)}, u32[]{:S(2)}) copy-start(bf16[256,512]{1,0:T(8,128)(2,1)S(1)} %collective-permute-done.2.refs_2_) | copy-start | bytes 786436
  40.5 8.7 %collective-permute-start.8 = (bf16[256,512]{1,0:T(8,128)(2,1)S(1)}, bf16[256,512]{1,0:T(8,128)(2,1)S(1)}, u32[]{:S(2)}, u32[]{:S(2)}) collective-permute-start(bf16[256,512]{1,0:T(8,128)(2,1)S(1)} %bitcast.46), channel_id=1, source_target_pairs={{0,1},{1,0},{2,3},{3,2},{4,5},{5,4},{6,7},{7,6},{8,9},{9,8},{10,11... | collective-permute-start | bytes 786440 | tf_op jit(solution)/shard_map/ppermute | solution.py:21
  40.5 10.6 %collective-permute-start.3 = (bf16[256,512]{1,0:T(8,128)(2,1)S(1)}, bf16[256,512]{1,0:T(8,128)(2,1)S(1)}, u32[]{:S(2)}, u32[]{:S(2)}) collective-permute-start(bf16[256,512]{1,0:T(8,128)(2,1)S(1)} %collective-permute-done.2.refs_2_), channel_id=1, source_target_pairs={{4,0},{8,12},{5,1},{9,13},{6,2},{10,14},{7,3},{11,15},{20,16},{24,... | collective-permute-start | bytes 786440 | tf_op jit(solution)/shard_map/ppermute | solution.py:31
  42.9 50.6 %collective-permute-start.12 = (bf16[256,512]{1,0:T(8,128)(2,1)S(1)}, bf16[256,512]{1,0:T(8,128)(2,1)S(1)}, u32[]{:S(2)}, u32[]{:S(2)}) collective-permute-start(bf16[256,512]{1,0:T(8,128)(2,1)S(1)} %pad_maximum_fusion.1.refs_0_), channel_id=1, source_target_pairs={{4,8},{8,4},{5,9},{9,5},{6,10},{10,6},{7,11},{11,7},{20,24},{24,20... | collective-permute-start | bytes 786440 | tf_op jit(solution)/shard_map/ppermute | solution.py:31
  43.6 38.4 %collective-permute-start.11 = (bf16[256,512]{1,0:T(8,128)(2,1)S(1)}, bf16[256,512]{1,0:T(8,128)(2,1)}, u32[]{:S(2)}, u32[]{:S(2)}) collective-permute-start(bf16[256,512]{1,0:T(8,128)(2,1)S(1)} %pad_maximum_fusion.1.refs_0_), channel_id=1, source_target_pairs={{0,8},{4,12},{8,0},{12,4},{1,9},{5,13},{9,1},{13,5},{2,10},{6,14},... | collective-permute-start | bytes 786440 | tf_op jit(solution)/shard_map/ppermute | solution.py:31
  49.0 44.5 %collective-permute-start.10 = (bf16[256,512]{1,0:T(8,128)(2,1)S(1)}, bf16[256,512]{1,0:T(8,128)(2,1)}, u32[]{:S(2)}, u32[]{:S(2)}) collective-permute-start(bf16[256,512]{1,0:T(8,128)(2,1)S(1)} %pad_maximum_fusion.1.refs_0_), channel_id=1, source_target_pairs={{0,4},{4,0},{8,12},{12,8},{1,5},{5,1},{9,13},{13,9},{2,6},{6,2},{1... | collective-permute-start | bytes 786440 | tf_op jit(solution)/shard_map/ppermute | solution.py:31
  49.2 1.9 copy-start.22
  51.1 0.8 copy-start.12
  51.1 114.5 %all-gather.5.cloned.1.call-start = ((), (), s32[]{:S(2)}) async-start(), calls=%async_computation | async-start | bytes 1310720 | tf_op jit(solution)/shard_map/all_gather | solution.py:148
  51.2 16.6 %collective-permute-start.16 = (f32[256,128]{0,1:T(8,128)}, f32[256,128]{0,1:T(8,128)S(1)}, u32[]{:S(2)}, u32[]{:S(2)}) collective-permute-start(f32[256,128]{0,1:T(8,128)} %pad_maximum_fusion.3), channel_id=1, source_target_pairs={{0,4},{4,0},{8,12},{12,8},{1,5},{5,1},{9,13},{13,9},{2,6},{6,2},{1... | collective-permute-start | bytes 393224 | tf_op jit(solution)/shard_map/ppermute | solution.py:31
  51.9 1.0 copy-start.13
  52.8 18.9 %copy-start.14 = (bf16[256,512]{1,0:T(8,128)(2,1)S(1)}, bf16[256,512]{1,0:T(8,128)(2,1)}, u32[]{:S(2)}) copy-start(bf16[256,512]{1,0:T(8,128)(2,1)} %copy-done.12) | copy-start | bytes 786436
  59.7 30.6 %collective-permute-start.9 = (bf16[128,3584]{1,0:T(8,128)(2,1)S(1)}, bf16[128,3584]{1,0:T(8,128)(2,1)}, u32[]{:S(2)}, u32[]{:S(2)}) collective-permute-start(bf16[128,3584]{1,0:T(8,128)(2,1)S(1)} %get-tuple-element.40), channel_id=1, source_target_pairs={{0,1},{1,0},{2,3},{3,2},{4,5},{5,4},{6,7},{7,6},{8,9},{9,8},{10,11... | collective-permute-start | bytes 2752520 | tf_op jit(solution)/shard_map/ppermute | solution.py:21
  69.4 18.6 %collective-permute-start.17 = (f32[256,128]{0,1:T(8,128)}, f32[256,128]{0,1:T(8,128)}, u32[]{:S(2)}, u32[]{:S(2)}) collective-permute-start(f32[256,128]{0,1:T(8,128)} %add.69), channel_id=1, source_target_pairs={{0,8},{4,12},{8,0},{12,4},{1,9},{5,13},{9,1},{13,5},{2,10},{6,14},... | collective-permute-start | bytes 393224 | tf_op jit(solution)/shard_map/ppermute | solution.py:31
  71.7 1.0 copy-start.5
  72.6 0.9 copy-start.7
  73.6 0.9 copy-start.9
  82.0 35.9 %collective-permute-start.14 = (bf16[128,3584]{1,0:T(8,128)(2,1)}, bf16[128,3584]{1,0:T(8,128)(2,1)}, u32[]{:S(2)}, u32[]{:S(2)}) collective-permute-start(bf16[128,3584]{1,0:T(8,128)(2,1)} %get-tuple-element.44), channel_id=1, source_target_pairs={{0,1},{1,0},{2,3},{3,2},{4,5},{5,4},{6,7},{7,6},{8,9},{9,8},{10,11... | collective-permute-start | bytes 2752520 | tf_op jit(solution)/shard_map/ppermute | solution.py:21
  88.0 8.5 %collective-permute-start.13 = (bf16[256,512]{1,0:T(8,128)(2,1)}, bf16[256,512]{1,0:T(8,128)(2,1)S(1)}, u32[]{:S(2)}, u32[]{:S(2)}) collective-permute-start(bf16[256,512]{1,0:T(8,128)(2,1)} %collective-permute-done.11.refs_2_), channel_id=1, source_target_pairs={{4,0},{8,12},{5,1},{9,13},{6,2},{10,14},{7,3},{11,15},{20,16},{24,... | collective-permute-start | bytes 786440 | tf_op jit(solution)/shard_map/ppermute | solution.py:31
  91.7 19.6 %collective-permute-start.15 = (bf16[128,3584]{1,0:T(8,128)(2,1)S(1)}, bf16[128,3584]{1,0:T(8,128)(2,1)S(1)}, u32[]{:S(2)}, u32[]{:S(2)}) collective-permute-start(bf16[128,3584]{1,0:T(8,128)(2,1)S(1)} %add_convert_fusion.7), channel_id=1, source_target_pairs={{0,2},{1,3},{2,0},{3,1},{4,6},{5,7},{6,4},{7,5},{8,10},{9,11},{10,... | collective-permute-start | bytes 2752520 | tf_op jit(solution)/shard_map/ppermute | solution.py:21
  96.5 9.1 %copy-start.10 = (bf16[256,512]{1,0:T(8,128)(2,1)}, bf16[256,512]{1,0:T(8,128)(2,1)S(1)}, u32[]{:S(2)}) copy-start(bf16[256,512]{1,0:T(8,128)(2,1)S(1)} %collective-permute-done.13.refs_4_) | copy-start | bytes 786436
  111.3 0.9 copy-start.17
  114.9 7.6 %copy-start.11 = (bf16[256,512]{1,0:T(8,128)(2,1)S(1)}, bf16[256,512]{1,0:T(8,128)(2,1)}, u32[]{:S(2)}) copy-start(bf16[256,512]{1,0:T(8,128)(2,1)} %copy-done.10) | copy-start | bytes 786436
  116.0 5.6 %collective-permute-start.20 = (bf16[4,4224]{1,0:T(4,128)(2,1)S(1)}, bf16[4,4224]{1,0:T(4,128)(2,1)S(1)}, u32[]{:S(2)}, u32[]{:S(2)}) collective-permute-start(bf16[4,4224]{1,0:T(4,128)(2,1)S(1)} %pad_maximum_fusion.4), channel_id=1, source_target_pairs={{0,1},{1,0},{2,3},{3,2},{4,5},{5,4},{6,7},{7,6},{8,9},{9,8},{10,11... | collective-permute-start | bytes 101384 | tf_op jit(solution)/shard_map/ppermute | solution.py:21
  116.1 5.5 %collective-permute-start.19 = (bf16[4,4224]{1,0:T(4,128)(2,1)S(1)}, bf16[4,4224]{1,0:T(4,128)(2,1)S(1)}, u32[]{:S(2)}, u32[]{:S(2)}) collective-permute-start(bf16[4,4224]{1,0:T(4,128)(2,1)S(1)} %pad_maximum_fusion.4), channel_id=1, source_target_pairs={{0,2},{1,3},{2,0},{3,1},{4,6},{5,7},{6,4},{7,5},{8,10},{9,11},{10,... | collective-permute-start | bytes 101384 | tf_op jit(solution)/shard_map/ppermute | solution.py:21
  117.4 4.2 %collective-permute-start.18 = (bf16[4,4224]{1,0:T(4,128)(2,1)S(1)}, bf16[4,4224]{1,0:T(4,128)(2,1)S(1)}, u32[]{:S(2)}, u32[]{:S(2)}) collective-permute-start(bf16[4,4224]{1,0:T(4,128)(2,1)S(1)} %pad_maximum_fusion.4), channel_id=1, source_target_pairs={{0,3},{1,2},{2,1},{3,0},{4,7},{5,6},{6,5},{7,4},{8,11},{9,10},{10,... | collective-permute-start | bytes 101384 | tf_op jit(solution)/shard_map/ppermute | solution.py:21
  120.3 22.8 %collective-permute-start.22 = (bf16[128,3584]{1,0:T(8,128)(2,1)}, bf16[128,3584]{1,0:T(8,128)(2,1)S(1)}, u32[]{:S(2)}, u32[]{:S(2)}) collective-permute-start(bf16[128,3584]{1,0:T(8,128)(2,1)} %add_convert_fusion.6), channel_id=1, source_target_pairs={{0,2},{1,3},{2,0},{3,1},{4,6},{5,7},{6,4},{7,5},{8,10},{9,11},{10,... | collective-permute-start | bytes 2752520 | tf_op jit(solution)/shard_map/ppermute | solution.py:21
  121.5 21.7 %collective-permute-start.21 = (bf16[128,3584]{1,0:T(8,128)(2,1)S(1)}, bf16[128,3584]{1,0:T(8,128)(2,1)}, u32[]{:S(2)}, u32[]{:S(2)}) collective-permute-start(bf16[128,3584]{1,0:T(8,128)(2,1)S(1)} %get-tuple-element.51), channel_id=1, source_target_pairs={{0,1},{1,0},{2,3},{3,2},{4,5},{5,4},{6,7},{7,6},{8,9},{9,8},{10,11... | collective-permute-start | bytes 2752520 | tf_op jit(solution)/shard_map/ppermute | solution.py:21
  122.5 20.6 %copy-start.21 = (bf16[16,4224]{1,0:T(8,128)(2,1)S(1)}, bf16[16,4224]{1,0:T(8,128)(2,1)}, u32[]{:S(2)}) copy-start(bf16[16,4224]{1,0:T(8,128)(2,1)} %pad_maximum_fusion.2) | copy-start | bytes 405508
  131.3 32.4 %collective-permute-start.23 = (bf16[128,3584]{1,0:T(8,128)(2,1)S(1)}, bf16[128,3584]{1,0:T(8,128)(2,1)S(1)}, u32[]{:S(2)}, u32[]{:S(2)}) collective-permute-start(bf16[128,3584]{1,0:T(8,128)(2,1)S(1)} %get-tuple-element.56), channel_id=1, source_target_pairs={{0,1},{1,0},{2,3},{3,2},{4,5},{5,4},{6,7},{7,6},{8,9},{9,8},{10,11... | collective-permute-start | bytes 2752520 | tf_op jit(solution)/shard_map/ppermute | solution.py:21
  143.1 4.8 %copy-start.19 = (bf16[128,3584]{1,0:T(8,128)(2,1)}, bf16[128,3584]{1,0:T(8,128)(2,1)S(1)}, u32[]{:S(2)}) copy-start(bf16[128,3584]{1,0:T(8,128)(2,1)S(1)} %collective-permute-done.22) | copy-start | bytes 2752516
  145.7 22.0 %collective-permute-start.24 = (bf16[128,3584]{1,0:T(8,128)(2,1)}, bf16[128,3584]{1,0:T(8,128)(2,1)S(1)}, u32[]{:S(2)}, u32[]{:S(2)}) collective-permute-start(bf16[128,3584]{1,0:T(8,128)(2,1)} %add_convert_fusion.5), channel_id=1, source_target_pairs={{0,2},{1,3},{2,0},{3,1},{4,6},{5,7},{6,4},{7,5},{8,10},{9,11},{10,... | collective-permute-start | bytes 2752520 | tf_op jit(solution)/shard_map/ppermute | solution.py:21
  147.8 2.7 %copy-start.2 = (bf16[1024,512]{1,0:T(8,128)(2,1)S(1)}, bf16[1024,512]{1,0:T(8,128)(2,1)}, u32[]{:S(2)}) copy-start(bf16[1024,512]{1,0:T(8,128)(2,1)} %all-gather.7.cloned.1.call-done) | copy-start | bytes 3145732
  163.1 17.8 %collective-permute-start.25 = (bf16[128,7168]{1,0:T(8,128)(2,1)}, bf16[128,7168]{1,0:T(8,128)(2,1)}, u32[]{:S(2)}, u32[]{:S(2)}) collective-permute-start(bf16[128,7168]{1,0:T(8,128)(2,1)} %get-tuple-element.54), channel_id=1, source_target_pairs={{0,1},{1,0},{2,3},{3,2},{4,5},{5,4},{6,7},{7,6},{8,9},{9,8},{10,11... | collective-permute-start | bytes 5505032 | tf_op jit(solution)/shard_map/ppermute | solution.py:21
  163.2 22.0 %collective-permute-start.26 = (bf16[128,7168]{1,0:T(8,128)(2,1)S(1)}, bf16[128,7168]{1,0:T(8,128)(2,1)}, u32[]{:S(2)}, u32[]{:S(2)}) collective-permute-start(bf16[128,7168]{1,0:T(8,128)(2,1)S(1)} %get-tuple-element.60), channel_id=1, source_target_pairs={{0,1},{1,0},{2,3},{3,2},{4,5},{5,4},{6,7},{7,6},{8,9},{9,8},{10,11... | collective-permute-start | bytes 5505032 | tf_op jit(solution)/shard_map/ppermute | solution.py:21
  164.9 22.7 %collective-permute-start.27 = (bf16[128,3584]{1,0:T(8,128)(2,1)}, bf16[128,3584]{1,0:T(8,128)(2,1)}, u32[]{:S(2)}, u32[]{:S(2)}) collective-permute-start(bf16[128,3584]{1,0:T(8,128)(2,1)} %add_convert_fusion.4), channel_id=1, source_target_pairs={{0,2},{1,3},{2,0},{3,1},{4,6},{5,7},{6,4},{7,5},{8,10},{9,11},{10,... | collective-permute-start | bytes 2752520 | tf_op jit(solution)/shard_map/ppermute | solution.py:21
  167.7 1.2 copy-start.3
  169.0 12.0 %copy-start.18 = (bf16[128,3584]{1,0:T(8,128)(2,1)S(1)}, bf16[128,3584]{1,0:T(8,128)(2,1)}, u32[]{:S(2)}) copy-start(bf16[128,3584]{1,0:T(8,128)(2,1)} %copy-done.17) | copy-start | bytes 2752516
  182.5 1.2 copy-start.20
  185.2 6.0 %copy-start.1 = (bf16[7168,64]{0,1:T(8,128)(2,1)S(1)}, bf16[7168,64]{0,1:T(8,128)(2,1)}, u32[]{:S(2)}) copy-start(bf16[7168,64]{0,1:T(8,128)(2,1)} %param.10) | copy-start | bytes 2752516
  189.4 1.8 copy-start.16
Sparse Core Ops, SparseCore 0:
  51.3 38.1 all-gather.6
  91.0 27.9 all-gather.4

commit v5 on v4

v5 whole, which is shorter than its diff:
```python
import functools

import jax
import jax.numpy as jnp
from jax import lax
from jax.experimental import pallas as pl
from jax.experimental.layout import Layout, with_layout_constraint
from jax.experimental.pallas import tpu as pltpu
from jax.sharding import PartitionSpec as P

GROUPS = 8
FAR_PARTS = 2

highest = lax.Precision.HIGHEST
f32, bf16 = jnp.float32, jnp.bfloat16


def swap(value, step):
    size = lax.axis_size("dp")
    return lax.ppermute(value, "dp", [(d, d ^ step) for d in range(size)])


def after(value, *earlier):
    return lax.optimization_barrier((value,) + earlier)[0]


def across(value, step, places=None):
    size = lax.axis_size("tensor")
    pairs = [(t, t ^ step) for t in range(size) if places is None or t in places]
    return lax.ppermute(value, "tensor", pairs)


def spread(block, *earlier):
    second = across(block, 2)
    first = across(block, 1)
    middle = across(after(block, second, *earlier), 3, (1, 2))
    ends = across(second, 1, (1, 2))
    return [block, first, second, middle, ends]


def terms_kernel(size, counts, first, lead, split, place_ref, *refs):
    total = sum(counts)
    groups, at = [], 0
    for count in counts:
        groups.append(refs[at : at + count])
        at += count
    w_ref, outs = refs[total], refs[total + 1 : -4]
    feats, held, sems, held_sems = refs[-4:]
    width, tile = feats.shape[1] // size, outs[0].shape[1]
    tall = feats.shape[0] // len(groups)
    j, steps = pl.program_id(0), pl.num_programs(0)
    slots = held.shape[0]

    def put(value, group, source, slot):
        at = pl.ds(pl.multiple_of(source * width, width), width)
        rows = pl.ds(group * tall, tall)
        return pltpu.make_async_copy(value, feats.at[rows, at], sems.at[group * size + slot])

    def fetch(step):
        slot = lax.rem(step, slots)
        at = pl.ds(pl.multiple_of(first + step * tile, tile), tile)
        return pltpu.make_async_copy(w_ref.at[:, 0, :, at], held.at[slot], held_sems.at[slot])

    @pl.when(j == 0)
    def _():
        copies = []
        place = place_ref[0]
        for group, blocks in enumerate(groups):
            if len(blocks) == 1:
                copies += [put(blocks[0].at[k], group, k, k) for k in range(size)]
            else:
                copies += [put(blocks[k], group, lax.bitwise_xor(place, k), k) for k in range(3)]
        for copy in copies:
            copy.start()
        for step in range(slots):
            fetch(step).start()
        inside = jnp.logical_or(place == 1, place == 2)
        for group, blocks in enumerate(groups):
            if len(blocks) == 1:
                continue
            for chosen, block in ((inside, blocks[3]), (jnp.logical_not(inside), blocks[4])):

                @pl.when(chosen)
                def _():
                    last = put(block, group, lax.bitwise_xor(place, 3), 3)
                    last.start()
                    last.wait()

        for copy in copies:
            copy.wait()

    fetch(j).wait()
    weight = held[lax.rem(j, slots)].reshape(size * width, tile)

    def multiply(outs):
        rows = sum(out_ref.shape[0] for out_ref in outs)
        terms = jnp.dot(feats[:rows], weight, preferred_element_type=f32).astype(bf16)
        row = 0
        for out_ref in outs:
            out_ref[...] = terms[row : row + out_ref.shape[0]]
            row += out_ref.shape[0]

    if split is None:
        multiply(outs)
    else:
        pl.when(j < split)(lambda: multiply(outs))
        pl.when(j >= split)(lambda: multiply(outs[:lead]))

    @pl.when(j + slots < steps)
    def _():
        fetch(j + slots).start()


def block_terms(groups, down_weight, col_start, cols, outs, lead=None, lead_cols=None):
    size, _, width, _ = down_weight.shape
    rows = sum(outs)
    wide = [cols if lead is None or k < lead else lead_cols for k in range(len(outs))]
    tile = max(n for n in range(128, 513, 128) if cols % n == 0)
    slots = min(4, cols // tile)
    split = None if lead is None else lead_cols // tile
    blocks = [block for group in groups for block in group]

    def out_at(count):
        return lambda j, place: (0, jnp.minimum(j, count - 1))

    return pl.pallas_call(
        functools.partial(
            terms_kernel, size, [len(group) for group in groups], col_start, lead, split
        ),
        out_shape=[jax.ShapeDtypeStruct((tall, n), bf16) for tall, n in zip(outs, wide)],
        grid_spec=pltpu.PrefetchScalarGridSpec(
            num_scalar_prefetch=1,
            grid=(cols // tile,),
            in_specs=[pl.BlockSpec(memory_space=pl.ANY)] * (len(blocks) + 1),
            out_specs=[pl.BlockSpec((tall, tile), out_at(n // tile)) for tall, n in zip(outs, wide)],
            scratch_shapes=[
                pltpu.VMEM((rows, size * width), bf16),
                pltpu.VMEM((slots, size, width, tile), bf16),
                pltpu.SemaphoreType.DMA((len(groups) * size,)),
                pltpu.SemaphoreType.DMA((slots,)),
            ],
        ),
        compiler_params=pltpu.CompilerParams(vmem_limit_bytes=40 << 20),
        cost_estimate=pl.CostEstimate(
            flops=8 * rows * size * width * cols, bytes_accessed=1000, transcendentals=0
        ),
        name="terms",
    )(lax.axis_index("tensor").reshape(1), *blocks, down_weight)


def gathered_terms(groups, down_weight, col_start, cols, outs, lead=None, lead_cols=None):
    weight = lax.slice_in_dim(down_weight, col_start, col_start + cols, axis=3)
    terms = [
        lax.dot_general(
            blocks[0], weight[:, 0], (((0, 2), (0, 1)), ((), ())), preferred_element_type=f32
        )
        for blocks in groups
    ]
    terms = jnp.concatenate(terms).astype(bf16)
    pieces = jnp.split(terms, [sum(outs[:k]) for k in range(1, len(outs))])
    return [
        piece if lead is None or k < lead else piece[:, :lead_cols]
        for k, piece in enumerate(pieces)
    ]


def add_kernel(kept_ref, first_ref, second_ref, out_ref):
    rows = first_ref.shape[0]
    for index, other in enumerate((first_ref, second_ref)):
        cut = slice(index * rows, (index + 1) * rows)
        out_ref[cut] = (kept_ref[cut].astype(f32) + other[...].astype(f32)).astype(bf16)


def add_halves(kept, first, second):
    rows, cols = kept.shape
    tile = max(n for n in range(128, 1025, 128) if cols % n == 0)

    def spec(tall):
        return pl.BlockSpec((tall, tile), lambda j: (0, j))

    return pl.pallas_call(
        add_kernel,
        out_shape=jax.ShapeDtypeStruct((rows, cols), bf16),
        grid=(cols // tile,),
        in_specs=[spec(rows), spec(rows // 2), spec(rows // 2)],
        out_specs=spec(rows),
        compiler_params=pltpu.CompilerParams(vmem_limit_bytes=16 << 20),
        cost_estimate=pl.CostEstimate(flops=1000, bytes_accessed=1000, transcendentals=0),
        name="pair",
    )(kept, first, second)


def finish_kernel(*refs):
    own_ref, halves, others, out_ref = refs[0], refs[1:3], refs[3:-1], refs[-1]
    rows = halves[0].shape[0]
    for index, half_ref in enumerate(halves):
        cut = slice(index * rows, (index + 1) * rows)
        total = own_ref[cut].astype(f32) + half_ref[...].astype(f32)
        for ref in others:
            total = total + ref[cut].astype(f32)
        out_ref[cut] = total.astype(bf16)


def finish(result, halves, others, row, col):
    rows, cols = others[0].shape
    tile = max(n for n in range(128, 1025, 128) if cols % n == 0)
    part = pl.BlockSpec((rows, tile), lambda j: (row // rows, col // tile + j))

    def spec(tall):
        return pl.BlockSpec((tall, tile), lambda j: (0, j))

    return pl.pallas_call(
        finish_kernel,
        out_shape=jax.ShapeDtypeStruct(result.shape, bf16),
        grid=(cols // tile,),
        in_specs=[part] + [spec(rows // 2)] * 2 + [spec(rows)] * len(others),
        out_specs=part,
        input_output_aliases={0: 0},
        compiler_params=pltpu.CompilerParams(vmem_limit_bytes=16 << 20),
        cost_estimate=pl.CostEstimate(flops=1000, bytes_accessed=1000, transcendentals=0),
        name="finish",
    )(result, *halves, *others)


def features(output_grad, parts):
    groups, place = lax.axis_size("dp"), lax.axis_index("dp")
    line = lax.axis_size("tensor") == 4

    def gather(block):
        block = with_layout_constraint(block, Layout(major_to_minor=(0, 1)))
        return [lax.all_gather(block, "tensor", axis=0)]

    turned = jnp.transpose(output_grad[0], (0, 2, 1))
    pieces = [
        lax.dynamic_index_in_dim(turned, place ^ step, 0, keepdims=False) for step in range(groups)
    ]
    rows = pieces[0].shape[0] // FAR_PARTS
    sent = []
    for half in range(FAR_PARTS):
        cut = slice(half * rows, (half + 1) * rows)
        for step in range(2, groups, 2):
            both = [swap(pieces[step + 1][cut], step + 1), swap(pieces[step][cut], step)]
            sent.append(jnp.concatenate(both))
    beside = swap(pieces[1], 1)
    far, last = [], [parts]
    low = parts + across(parts, 1) if line else lax.psum(parts, "tensor")
    for half in range(FAR_PARTS):
        for step in range(2, groups, 2):
            block = after(sent[len(far)], *last)
            early = [] if far else [low, beside] + sent[1:]
            blocks = spread(block, *early) if line else gather(block)
            far.append((half, step, blocks))
            last = blocks[-2:]
            if line and len(far) == 1:
                low = after(low, *last)
                low = low + across(low, 2)
    beside = after(beside, *last)
    beside = spread(beside) if line else gather(beside)
    own = after(pieces[0], *beside[1:3])
    own = spread(own) if line else gather(own)
    return far, beside, own, low


def example_gradients(acts_low, grads_low, local_ids, examples):
    onehot = (local_ids[:, None] == jnp.arange(examples, dtype=jnp.int32)[None, :]).astype(f32)
    counts = jnp.sum(onehot, axis=0)
    spread = (onehot[:, :, None] * acts_low[:, None, :]).reshape(onehot.shape[0], -1)
    outer_sum = lax.dot_general(
        spread,
        grads_low,
        (((0,), (0,)), ((), ())),
        precision=highest,
        preferred_element_type=f32,
    )
    basis_rank = acts_low.shape[1]
    outer_sum = outer_sum.reshape(examples, basis_rank * grads_low.shape[1]) / counts[:, None]
    return outer_sum.astype(bf16)


def gather_examples(example_grad, example_group):
    count = example_grad.shape[0]
    group_column = jnp.broadcast_to(example_group.astype(bf16)[:, None], (count, 128))
    held = jnp.concatenate([example_grad, group_column], axis=1)
    return [held] + [swap(held, step) for step in range(1, lax.axis_size("dp"))]


def order_examples(values):
    groups, place = lax.axis_size("dp"), lax.axis_index("dp")
    ordered = []
    for group in range(groups):
        value = values[0]
        for step in range(1, groups):
            value = jnp.where((place ^ group) == step, values[step], value)
        ordered.append(value)
    return jnp.concatenate(ordered, axis=0)


def fisher_and_groups(every, flat_width):
    row_count = flat_width // lax.axis_size("dp")
    col_count = flat_width // lax.axis_size("tensor")
    col_start = lax.axis_index("tensor") * col_count
    row_start = lax.axis_index("dp") * row_count
    every_group = every[:, flat_width].astype(jnp.int32)
    rows_part = lax.dynamic_slice_in_dim(every, row_start, row_count, 1)
    cols_part = lax.dynamic_slice_in_dim(every, col_start, col_count, 1)
    fisher = lax.dot_general(
        rows_part, cols_part, (((0,), (0,)), ((), ())), preferred_element_type=f32
    )
    member = (every_group[:, None] == jnp.arange(GROUPS, dtype=jnp.int32)[None, :]).astype(bf16)
    group_grad = lax.dot_general(
        member, cols_part, (((0,), (0,)), ((), ())), preferred_element_type=f32
    )
    return fisher, group_grad


def per_device(
    hidden_acts, output_grad, down_weight, input_basis, output_basis, token_example, example_group
):
    tokens, cols = hidden_acts.shape
    col_parts = 2 if cols % 512 == 0 else 1
    part, rows = cols // col_parts, tokens // FAR_PARTS

    def multiply(blocks, at, outs=2, width=part):
        kernel = block_terms if down_weight.shape[2] % 128 == 0 else gathered_terms
        return kernel(blocks, down_weight, at * part, width, outs)

    acts_part = jnp.dot(hidden_acts, input_basis, preferred_element_type=f32)
    grads_part = lax.dot_general(
        output_grad,
        output_basis,
        (((0, 1, 2), (0, 1, 2)), ((), ())),
        preferred_element_type=f32,
    )
    parts = jnp.concatenate([acts_part, grads_part], axis=1)
    far, beside, own, low = features(output_grad, parts)

    def multiply(groups, at, outs, width=part, *lead):
        kernel = block_terms if down_weight.shape[2] % 128 == 0 else gathered_terms
        return kernel(groups, down_weight, at * part, width, outs, *lead)

    units = [(blocks, half, step, at) for half, step, blocks in far for at in range(col_parts)]
    pairs, arrived, near = [], [], {}
    for count, (blocks, half, step, at) in enumerate(units):
        earlier = pairs[-1:] + arrived[:-1][-1:]
        if count == 1:
            earlier += far[-1][2][1:3]
        if count == 2:
            acts_low, grads_low = jnp.split(after(low, *earlier), 2, axis=1)
            example_grad = example_gradients(
                acts_low, grads_low, token_example[0], example_group.shape[0]
            )
            swapped = gather_examples(example_grad, example_group)
            earlier += [example_grad] + beside[1:3]
        if count == 3:
            every = order_examples(after(swapped, *earlier))
            fisher, group_grad = fisher_and_groups(every, example_grad.shape[1])
            earlier += [fisher, group_grad] + own[1:3]
        groups = [[after(blocks[0], *earlier)] + blocks[1:] if earlier else blocks]
        outs = [rows // 2, rows // 2, rows]
        if count == len(units) - 1:
            groups.append(beside)
            outs += [rows // 2] * (2 * FAR_PARTS)
        first, second, kept, *terms = multiply(groups, at, outs)
        pairs.append(add_halves(kept, swap(first, 1), swap(second, 1)))
        arrived.append(swap(pairs[-1], step))
        near[at] = [swap(after(term, arrived[-2], pairs[-1]), 1) for term in terms]
    own = [after(own[0], pairs[-1], *near[col_parts - 1])] + own[1:]
    if col_parts == 2:
        outs = [tokens] + [rows // 2] * (2 * FAR_PARTS)
        result, *terms = multiply([own, beside], 0, outs, cols, 1, part)
        near[0] = [swap(term, 1) for term in terms]
    else:
        (result,) = multiply([own], 0, [tokens], cols)
    for half in range(FAR_PARTS):
        for at in range(col_parts):
            sums = [
                arrived[count] for count, unit in enumerate(units) if unit[1:] == (half, unit[2], at)
            ]
            result = finish(
                result, near[at][2 * half : 2 * half + 2], sums, half * rows, at * part
            )
    return (result, fisher, group_grad)


def solution(mesh):
    return jax.shard_map(
        per_device,
        mesh=mesh,
        in_specs=(
            P(("parts", "dp"), "tensor"),
            P("tensor", None, None, ("parts", "dp")),
            P(None, "dp", None, "tensor"),
            P("tensor", None),
            P("tensor", None, None, None),
            P(("parts", "dp"), None),
            P(("parts", "dp")),
        ),
        out_specs=(
            P(("parts", "dp"), "tensor"),
            P(("parts", "dp"), "tensor"),
            P("parts", "tensor"),
        ),
        check_vma=False,
    )
```

time: 200 us -> 207 us (1.035)
  other arithmetic: 19.3 us -> 2.95 us
  starting transfers between devices: 29.5 us -> 43.8 us
  between operations: 14.6 us -> 1.29 us
  Pallas kernels: 56.6 us -> 69.4 us
  waiting for transfers between devices: 56.4 us -> 63.3 us
  local copies, waits for them, and re-layouts: 13.4 us -> 16.9 us
    ppermute x10 -> x18, waiting for transfers between devices: 35.1 us -> 59 us  [across(): return lax.ppermute(value, 'tensor', pairs)]
    ppermute x18 -> x28, waiting for transfers between devices: 21.3 us -> 4.31 us  [swap(): return lax.ppermute(value, 'dp', [(d, d ^ step) for d in range(size)])]
    pallas_call x6 -> x13, Pallas kernels: 56.6 us -> 69.4 us  [the longest x5 51.6 us: block_terms(): pl.pallas_call(functools.partial(terms_kernel, size, [len(group) for grou...]
    ppermute x18 -> x28, starting transfers between devices: 12.5 us -> 23.1 us  [swap(): return lax.ppermute(value, 'dp', [(d, d ^ step) for d in range(size)])]
    convert_element_type x5 -> x0, other arithmetic: 8.96 us -> none  [add(): return total.astype(bf16)]
    dynamic_update_slice x3 -> x0, other arithmetic: 4.91 us -> none  [per_device(): result = lax.dynamic_update_slice(result, value, (half * rows, at * part))]
    ppermute x10 -> x18, starting transfers between devices: 16.9 us -> 20.7 us  [across(): return lax.ppermute(value, 'tensor', pairs)]
    unnamed x52 -> x63, local copies, waits for them, and re-layouts: 8.66 us -> 10.2 us
  transfers between devices with their start and end apart: 30 -> 46, of which waited for: 11 -> 17; matrix products, arithmetic and copies ran while one was open for 15% -> 8% of each run, Pallas kernels for 29% -> 29%
where the time goes in v5:
time: 207 us; the launch traced here: 206 us
  Pallas kernels  69.4 us (34%)
  waiting for transfers between devices  63.3 us (31%)
  starting transfers between devices  43.8 us (21%)
  local copies, waits for them, and re-layouts  16.9 us (8%)
  matrix products  8.21 us (4%)
  other arithmetic  2.95 us (1%)
    ppermute x18, waiting for transfers between devices, across(): return lax.ppermute(value, 'tensor', pairs)  59 us
    pallas_call x5, Pallas kernels, block_terms(): pl.pallas_call(functools.partial(terms_kernel, size, [len(group) for grou...  51.6 us
    ppermute x28, starting transfers between devices, swap(): return lax.ppermute(value, 'dp', [(d, d ^ step) for d in range(size)])  23.1 us
    ppermute x18, starting transfers between devices, across(): return lax.ppermute(value, 'tensor', pairs)  20.7 us
    pallas_call x4, Pallas kernels, finish(): pl.pallas_call(finish_kernel, out_shape=jax.ShapeDtypeStruct(result.shape...  13.9 us
    unnamed x63, local copies, waits for them, and re-layouts  10.2 us
    ppermute x28, waiting for transfers between devices, swap(): return lax.ppermute(value, 'dp', [(d, d ^ step) for d in range(size)])  4.31 us
  transfers between devices with their start and end apart: 46, of which 17 were waited for; matrix products, arithmetic and copies ran while one was open for 8% of the time, Pallas kernels for 29%

profile of v5, /device:TPU:0, one launch (start us, length us, event | category | flops | bytes accessed | tf_op | source)
XLA Modules:
  0.0 205.8 jit_solution(9221933857266642334)
XLA Ops:
  0.7 2.1 %constant_dynamic-slice_fusion = (bf16[1,1,512,256]{3,2,1,0:T(8,128)(2,1)S(1)}, bf16[1,1,512,256]{3,2,1,0:T(8,128)(2,1)S(1)}, bf16[1,1,512,256]{3,2,1,0:T(8,128)(2,1)S(1)}, bf16[1,1,512,256]{3,2,1,0:T(8,128)(2,1)}) fusion(bf16[1,4,512,256]{3,2,1,0:T(8,128)(2,1)} %param.8, s32[]{:T(128)S(6)} %select_n.96, s32[]{:T(128)S(6)} %select_n.95, s32[]{:T(128)S(6)} %select_n.94, ...), kind=kLoop, calls=%fused_computation.33 | loop fusion | bytes 2097168 | tf_op jit(solution)/shard_map/dynamic-slice.7
  2.9 0.7 slice_bitcast_fusion
  3.6 2.9 %collective-permute-start.4 = (bf16[128,512]{1,0:T(8,128)(2,1)S(1)}, bf16[128,512]{1,0:T(8,128)(2,1)S(1)}, u32[]{:S(2)}, u32[]{:S(2)}) collective-permute-start(bf16[128,512]{1,0:T(8,128)(2,1)S(1)} %get-tuple-element.95), channel_id=1, source_target_pairs={{0,2},{1,3},{2,0},{3,1},{4,6},{5,7},{6,4},{7,5},{8,10},{9,11},{10,... | collective-permute-start | bytes 393224 | tf_op jit(solution)/shard_map/ppermute | solution.py:20
  6.6 0.7 slice_bitcast_fusion.1
  7.3 1.7 collective-permute-start.1
  9.1 3.3 %fusion.15 = f32[256,64]{0,1:T(8,128)S(1)} fusion(bf16[256,7168]{1,0:T(8,128)(2,1)} %param.7, bf16[7168,64]{0,1:T(8,128)(2,1)S(1)} %copy-done), kind=kOutput, calls=%fused_computation.39 | convolution fusion | flops 234881024 | bytes 4653056 | tf_op jit(solution)/shard_map/dot_general | solution.py:327
  12.7 1.6 collective-permute-start.6
  15.3 0.7 collective-permute-done.1
  16.0 2.6 %collective-permute-start.5 = (bf16[256,512]{1,0:T(8,128)(2,1)S(1)}, bf16[256,512]{1,0:T(8,128)(2,1)S(1)}, u32[]{:S(2)}, u32[]{:S(2)}) collective-permute-start(bf16[256,512]{1,0:T(8,128)(2,1)S(1)} %pad_maximum_fusion.refs_0_), channel_id=1, source_target_pairs={{0,8},{4,12},{8,0},{12,4},{1,9},{5,13},{9,1},{13,5},{2,10},{6,14},... | collective-permute-start | bytes 786440 | tf_op jit(solution)/shard_map/ppermute | solution.py:30
  18.6 0.9 constant_dynamic-update-slice_fusion.1
  19.5 0.8 fusion.14
  20.3 7.8 %collective-permute-done.5.refs_2_ = bf16[256,512]{1,0:T(8,128)(2,1)S(1)} collective-permute-done((bf16[256,512]{1,0:T(8,128)(2,1)S(1)}, bf16[256,512]{1,0:T(8,128)(2,1)S(1)}, u32[]{:S(2)}, u32[]{:S(2)}) %collective-permute-start.5) | collective-permute-done | bytes 262176 | tf_op jit(solution)/shard_map/ppermute | solution.py:30
  28.1 0.7 collective-permute-start.7
  28.8 1.3 collective-permute-start.8
  30.1 11.4 %collective-permute-done.8.refs_4_ = bf16[256,512]{1,0:T(8,128)(2,1)S(1)} collective-permute-done((bf16[256,512]{1,0:T(8,128)(2,1)S(1)}, bf16[256,512]{1,0:T(8,128)(2,1)S(1)}, u32[]{:S(2)}, u32[]{:S(2)}) %collective-permute-start.8) | collective-permute-done | bytes 262176 | tf_op jit(solution)/shard_map/ppermute | solution.py:30
  41.5 7.0 %terms.5 = (bf16[64,3584]{1,0:T(8,128)(2,1)S(1)}, bf16[64,3584]{1,0:T(8,128)(2,1)S(1)}, bf16[128,3584]{1,0:T(8,128)(2,1)S(1)}) custom-call(s32[1]{0:T(128)} %bitcast.place_ref, bf16[256,512]{1,0:T(8,128)(2,1)S(1)} %pad_maximum_fusion.refs_0_, bf16[256,512]{1,0:T(8,128)(2,1)S(1)} %collective-permute-done.14.refs_1_, ...), custom_call_target="tpu_custom_call" | custom-call | flops 15032385536 | bytes 1000 | tf_op jit(solution)/shard_map/terms/pallas_call | solution.py:126
  49.6 2.7 %collective-permute-start.9 = (bf16[256,512]{1,0:T(8,128)(2,1)S(1)}, bf16[256,512]{1,0:T(8,128)(2,1)S(1)}, u32[]{:S(2)}, u32[]{:S(2)}) collective-permute-start(bf16[256,512]{1,0:T(8,128)(2,1)S(1)} %constant_dynamic-update-slice_fusion.refs_0_), channel_id=1, source_target_pairs={{0,8},{4,12},{8,0},{12,4},{1,9},{5,13},{9,1},{13,5},{2,10},{6,14},... | collective-permute-start | bytes 786440 | tf_op jit(solution)/shard_map/ppermute | solution.py:30
  53.1 3.1 %collective-permute-start.20 = (bf16[128,3584]{1,0:T(8,128)(2,1)S(1)}, bf16[128,3584]{1,0:T(8,128)(2,1)S(1)}, u32[]{:S(2)}, u32[]{:S(2)}) collective-permute-start(bf16[128,3584]{1,0:T(8,128)(2,1)S(1)} %pair.4), channel_id=1, source_target_pairs={{0,2},{1,3},{2,0},{3,1},{4,6},{5,7},{6,4},{7,5},{8,10},{9,11},{10,... | collective-permute-start | bytes 2752520 | tf_op jit(solution)/shard_map/ppermute | solution.py:20
  56.2 6.6 %collective-permute-done.17.refs_1_ = bf16[256,512]{1,0:T(8,128)(2,1)S(1)} collective-permute-done((bf16[256,512]{1,0:T(8,128)(2,1)S(1)}, bf16[256,512]{1,0:T(8,128)(2,1)S(1)}, u32[]{:S(2)}, u32[]{:S(2)}) %collective-permute-start.17) | collective-permute-done | bytes 262176 | tf_op jit(solution)/shard_map/ppermute | solution.py:30
  62.8 5.4 %collective-permute-done.9.refs_2_ = bf16[256,512]{1,0:T(8,128)(2,1)S(1)} collective-permute-done((bf16[256,512]{1,0:T(8,128)(2,1)S(1)}, bf16[256,512]{1,0:T(8,128)(2,1)S(1)}, u32[]{:S(2)}, u32[]{:S(2)}) %collective-permute-start.9) | collective-permute-done | bytes 262176 | tf_op jit(solution)/shard_map/ppermute | solution.py:30
  68.1 0.9 copy-done.23
  69.1 0.9 copy-done.25
  70.0 7.0 %terms.6 = (bf16[64,3584]{1,0:T(8,128)(2,1)S(1)}, bf16[64,3584]{1,0:T(8,128)(2,1)S(1)}, bf16[128,3584]{1,0:T(8,128)(2,1)S(1)}) custom-call(s32[1]{0:T(128)} %bitcast.place_ref, bf16[256,512]{1,0:T(8,128)(2,1)S(1)} %pad_maximum_fusion.refs_0_, bf16[256,512]{1,0:T(8,128)(2,1)S(1)} %collective-permute-done.14.refs_1_, ...), custom_call_target="tpu_custom_call" | custom-call | flops 15032385536 | bytes 1000 | tf_op jit(solution)/shard_map/terms/pallas_call | solution.py:126
  77.6 0.7 collective-permute-start.10
  78.3 1.3 collective-permute-start.11
  79.8 0.7 copy-done.16
  80.5 8.0 %collective-permute-done.11.refs_4_ = bf16[256,512]{1,0:T(8,128)(2,1)S(1)} collective-permute-done((bf16[256,512]{1,0:T(8,128)(2,1)S(1)}, bf16[256,512]{1,0:T(8,128)(2,1)S(1)}, u32[]{:S(2)}, u32[]{:S(2)}) %collective-permute-start.11) | collective-permute-done | bytes 262176 | tf_op jit(solution)/shard_map/ppermute | solution.py:30
  88.5 0.7 copy-done.19
  89.4 2.5 %collective-permute-start.12 = (bf16[256,512]{1,0:T(8,128)(2,1)S(1)}, bf16[256,512]{1,0:T(8,128)(2,1)}, u32[]{:S(2)}, u32[]{:S(2)}) collective-permute-start(bf16[256,512]{1,0:T(8,128)(2,1)S(1)} %collective-permute-done.refs_5_), channel_id=1, source_target_pairs={{0,4},{4,0},{8,12},{12,8},{1,5},{5,1},{9,13},{13,9},{2,6},{6,2},{1... | collective-permute-start | bytes 786440 | tf_op jit(solution)/shard_map/ppermute | solution.py:30
  92.4 3.3 %collective-permute-start.24 = (bf16[128,3584]{1,0:T(8,128)(2,1)S(1)}, bf16[128,3584]{1,0:T(8,128)(2,1)S(1)}, u32[]{:S(2)}, u32[]{:S(2)}) collective-permute-start(bf16[128,3584]{1,0:T(8,128)(2,1)S(1)} %pair.5), channel_id=1, source_target_pairs={{0,2},{1,3},{2,0},{3,1},{4,6},{5,7},{6,4},{7,5},{8,10},{9,11},{10,... | collective-permute-start | bytes 2752520 | tf_op jit(solution)/shard_map/ppermute | solution.py:20
  95.7 1.0 fusion.2
  96.8 1.6 reshape.77
  98.4 0.9 divide_convert_fusion
  99.3 3.4 %collective-permute-done.13.refs_7_ = bf16[256,512]{1,0:T(8,128)(2,1)S(1)} collective-permute-done((bf16[256,512]{1,0:T(8,128)(2,1)S(1)}, bf16[256,512]{1,0:T(8,128)(2,1)S(1)}, u32[]{:S(2)}, u32[]{:S(2)}) %collective-permute-start.13) | collective-permute-done | bytes 262176 | tf_op jit(solution)/shard_map/ppermute | solution.py:30
  103.0 0.9 copy-done.11
  104.0 0.9 copy-done.14
  104.9 0.9 copy-done.17
  105.9 0.9 copy-done.20
  106.8 7.5 %terms.7 = (bf16[64,3584]{1,0:T(8,128)(2,1)S(1)}, bf16[64,3584]{1,0:T(8,128)(2,1)}, bf16[128,3584]{1,0:T(8,128)(2,1)S(1)}) custom-call(s32[1]{0:T(128)} %bitcast.place_ref, bf16[256,512]{1,0:T(8,128)(2,1)S(1)} %constant_dynamic-update-slice_fusion.refs_0_, bf16[256,512]{1,0:T(8,128)(2,1)S(1)} %copy-done.11, bf16[256,512]{1,0:T(8,128)(2,1)S(1)} %copy-done.14, ...), custom_call_target="tpu_custom_call" | custom-call | flops 15032385536 | bytes 1000 | tf_op jit(solution)/shard_map/terms/pallas_call | solution.py:126
  114.4 0.9 copy-done.2
  115.9 2.9 %collective-permute-start.27 = (bf16[4,4224]{1,0:T(4,128)(2,1)S(1)}, bf16[4,4224]{1,0:T(4,128)(2,1)S(1)}, u32[]{:S(2)}, u32[]{:S(2)}) collective-permute-start(bf16[4,4224]{1,0:T(4,128)(2,1)S(1)} %pad_maximum_fusion.3), channel_id=1, source_target_pairs={{0,3},{1,2},{2,1},{3,0},{4,7},{5,6},{6,5},{7,4},{8,11},{9,10},{10,... | collective-permute-start | bytes 101384 | tf_op jit(solution)/shard_map/ppermute | solution.py:20
  119.3 1.1 copy.24
  120.8 1.2 copy-done.3
  122.0 2.3 %pair.6 = bf16[128,3584]{1,0:T(8,128)(2,1)S(1)} custom-call(bf16[128,3584]{1,0:T(8,128)(2,1)S(1)} %copy-done.3, bf16[64,3584]{1,0:T(8,128)(2,1)S(1)} %collective-permute-done.22.first_ref, bf16[64,3584]{1,0:T(8,128)(2,1)} %collective-permute-done.23.second_ref), custom_call_target="tpu_custom_call" | custom-call | flops 1000 | bytes 1000 | tf_op jit(solution)/shard_map/pair/pallas_call | solution.py:181
  124.3 1.8 collective-permute-start.28
  126.1 0.7 collective-permute-start.30
  126.8 1.3 collective-permute-start.31
  128.1 1.9 collective-permute-start.34
  130.0 0.9 select_select_fusion.3
  130.9 2.7 %fusion.4 = f32[1024,1024]{1,0:T(8,128)} fusion(bf16[16,4224]{1,0:T(8,128)(2,1)S(1)} %pad_maximum_fusion.1, s32[]{:T(128)S(6)} %select_n.121, s32[]{:T(128)S(6)} %select_n.122), kind=kOutput, calls=%fused_computation.19 | convolution fusion | flops 33554432 | bytes 4259848 | tf_op jit(solution)/shard_map/dot_general | solution.py:306
  133.8 0.9 fusion.6
  134.8 4.3 %collective-permute-done.28.refs_1_ = bf16[256,512]{1,0:T(8,128)(2,1)S(1)} collective-permute-done((bf16[256,512]{1,0:T(8,128)(2,1)S(1)}, bf16[256,512]{1,0:T(8,128)(2,1)S(1)}, u32[]{:S(2)}, u32[]{:S(2)}) %collective-permute-start.28) | collective-permute-done | bytes 262176 | tf_op jit(solution)/shard_map/ppermute | solution.py:30
  139.1 4.9 %collective-permute-done.31.refs_9_ = bf16[256,512]{1,0:T(8,128)(2,1)S(1)} collective-permute-done((bf16[256,512]{1,0:T(8,128)(2,1)}, bf16[256,512]{1,0:T(8,128)(2,1)S(1)}, u32[]{:S(2)}, u32[]{:S(2)}) %collective-permute-start.31) | collective-permute-done | bytes 262176 | tf_op jit(solution)/shard_map/ppermute | solution.py:30
  144.0 11.2 %terms.8 = (bf16[64,3584]{1,0:T(8,128)(2,1)S(1)}, bf16[64,3584]{1,0:T(8,128)(2,1)S(1)}, bf16[128,3584]{1,0:T(8,128)(2,1)S(1)}, bf16[64,3584]{1,0:T(8,128)(2,1)S(...) custom-call(s32[1]{0:T(128)} %bitcast.place_ref, ...), custom_call_target="tpu_custom_call" | custom-call | flops 30064771072 | bytes 1000 | tf_op jit(solution)/shard_map/terms/pallas_call | solution.py:126
  155.7 1.3 collective-permute-done.32.first_ref
  160.1 1.5 collective-permute-start.40
  161.6 1.8 collective-permute-start.45
  163.4 7.0 %collective-permute-done.40.refs_4_ = bf16[256,512]{1,0:T(8,128)(2,1)S(1)} collective-permute-done((bf16[256,512]{1,0:T(8,128)(2,1)S(1)}, bf16[256,512]{1,0:T(8,128)(2,1)S(1)}, u32[]{:S(2)}, u32[]{:S(2)}) %collective-permute-start.40) | collective-permute-done | bytes 262176 | tf_op jit(solution)/shard_map/ppermute | solution.py:30
  170.4 19.0 %terms.9 = (bf16[256,7168]{1,0:T(8,128)(2,1)}, bf16[64,3584]{1,0:T(8,128)(2,1)S(1)}, bf16[64,3584]{1,0:T(8,128)(2,1)S(1)}, bf16[64,3584]{1,0:T(8,128)(2,1)S(1)}, bf16[64,3584]{1,0:T(8,128)(2,1)S(1)}) custom-call(s32[1]{0:T(128)} %bitcast.place_ref, bf16[256,512]{1,0:T(8,128)(2,1)S(1)} %bitcast.41, bf16[256,512]{1,0:T(8,128)(2,1)S(1)} %collective-permute-done.28.refs_1_, ...), custom_call_target="tpu_custom_call" | custom-call | flops 60129542144 | bytes 1000 | tf_op jit(solution)/shard_map/terms/pallas_call | solution.py:126
  190.5 0.8 collective-permute-done.41.refs_1_
  191.9 3.4 %finish.4.refs_0_ = bf16[256,7168]{1,0:T(8,128)(2,1)} custom-call(bf16[256,7168]{1,0:T(8,128)(2,1)} %get-tuple-element.84.refs_0_, bf16[64,3584]{1,0:T(8,128)(2,1)S(1)} %collective-permute-done.41.refs_1_, bf16[64,3584]{1,0:T(8,128)(2,1)S(1)} %collective-permute-done.42.refs_2_, ...), custom_call_target="tpu_custom_call", output_to_operand_aliasing={{}: (0, {})} | custom-call | flops 1000 | bytes 1000 | tf_op jit(solution)/shard_map/finish/pallas_call | solution.py:212
  195.4 3.5 %finish.5.refs_0_ = bf16[256,7168]{1,0:T(8,128)(2,1)} custom-call(bf16[256,7168]{1,0:T(8,128)(2,1)} %finish.4.refs_0_, bf16[64,3584]{1,0:T(8,128)(2,1)S(1)} %collective-permute-done.35.refs_1_, bf16[64,3584]{1,0:T(8,128)(2,1)S(1)} %collective-permute-done.36.refs_2_, ...), custom_call_target="tpu_custom_call", output_to_operand_aliasing={{}: (0, {})} | custom-call | flops 1000 | bytes 1000 | tf_op jit(solution)/shard_map/finish/pallas_call | solution.py:212
  198.8 3.5 %finish.6.refs_0_ = bf16[256,7168]{1,0:T(8,128)(2,1)} custom-call(bf16[256,7168]{1,0:T(8,128)(2,1)} %finish.5.refs_0_, bf16[64,3584]{1,0:T(8,128)(2,1)S(1)} %collective-permute-done.43.refs_1_, bf16[64,3584]{1,0:T(8,128)(2,1)S(1)} %collective-permute-done.44.refs_2_, ...), custom_call_target="tpu_custom_call", output_to_operand_aliasing={{}: (0, {})} | custom-call | flops 1000 | bytes 1000 | tf_op jit(solution)/shard_map/finish/pallas_call | solution.py:212
  202.4 3.5 %finish.7 = bf16[256,7168]{1,0:T(8,128)(2,1)} custom-call(bf16[256,7168]{1,0:T(8,128)(2,1)} %finish.6.refs_0_, bf16[64,3584]{1,0:T(8,128)(2,1)S(1)} %collective-permute-done.37.refs_1_, bf16[64,3584]{1,0:T(8,128)(2,1)S(1)} %collective-permute-done.38.refs_2_, bf16[128,3584]{1,0:T(8,128)(2,1)S(1)} %collective-permute-done.45.refs_3_), custom_call_target="tpu_custom_call", output_to_operand_aliasing={{}: (0, {})} | custom-call | flops 1000 | bytes 1000 | tf_op jit(solution)/shard_map/finish/pallas_call | solution.py:212
  (133 shorter events, 12.6 us)
Async XLA Ops:
  0.6 8.4 %copy-start = (bf16[7168,64]{0,1:T(8,128)(2,1)S(1)}, bf16[7168,64]{0,1:T(8,128)(2,1)}, u32[]{:S(2)}) copy-start(bf16[7168,64]{0,1:T(8,128)(2,1)} %param.10) | copy-start | bytes 2752516
  2.7 9.6 %copy-start.26 = (bf16[1,4,512,256]{3,2,1,0:T(8,128)(2,1)S(1)}, bf16[1,4,512,256]{3,2,1,0:T(8,128)(2,1)}, u32[]{:S(2)}) copy-start(bf16[1,4,512,256]{3,2,1,0:T(8,128)(2,1)} %param.8) | copy-start | bytes 3145732
  2.7 9.6 %copy-start.28 = (bf16[1,4,512,64]{2,3,1,0:T(8,128)(2,1)S(1)}, bf16[1,4,512,64]{2,3,1,0:T(8,128)(2,1)}, u32[]{:S(2)}) copy-start(bf16[1,4,512,64]{2,3,1,0:T(8,128)(2,1)} %param.11) | copy-start | bytes 786436
  3.6 11.4 %collective-permute-start.4 = (bf16[128,512]{1,0:T(8,128)(2,1)S(1)}, bf16[128,512]{1,0:T(8,128)(2,1)S(1)}, u32[]{:S(2)}, u32[]{:S(2)}) collective-permute-start(bf16[128,512]{1,0:T(8,128)(2,1)S(1)} %get-tuple-element.95), channel_id=1, source_target_pairs={{0,2},{1,3},{2,0},{3,1},{4,6},{5,7},{6,4},{7,5},{8,10},{9,11},{10,... | collective-permute-start | bytes 393224 | tf_op jit(solution)/shard_map/ppermute | solution.py:20
  7.3 7.8 %collective-permute-start.3 = (bf16[128,512]{1,0:T(8,128)(2,1)}, bf16[128,512]{1,0:T(8,128)(2,1)S(1)}, u32[]{:S(2)}, u32[]{:S(2)}) collective-permute-start(bf16[128,512]{1,0:T(8,128)(2,1)} %get-tuple-element.93), channel_id=1, source_target_pairs={{0,3},{1,2},{2,1},{3,0},{4,7},{5,6},{6,5},{7,4},{8,11},{9,10},{10,... | collective-permute-start | bytes 393224 | tf_op jit(solution)/shard_map/ppermute | solution.py:20
  7.3 8.7 %collective-permute-start.1 = (bf16[128,512]{1,0:T(8,128)(2,1)S(1)}, bf16[128,512]{1,0:T(8,128)(2,1)}, u32[]{:S(2)}, u32[]{:S(2)}) collective-permute-start(bf16[128,512]{1,0:T(8,128)(2,1)S(1)} %get-tuple-element.94), channel_id=1, source_target_pairs={{0,3},{1,2},{2,1},{3,0},{4,7},{5,6},{6,5},{7,4},{8,11},{9,10},{10,... | collective-permute-start | bytes 393224 | tf_op jit(solution)/shard_map/ppermute | solution.py:20
  12.7 6.8 %collective-permute-start.6 = (f32[256,128]{0,1:T(8,128)S(1)}, f32[256,128]{0,1:T(8,128)S(1)}, u32[]{:S(2)}, u32[]{:S(2)}) collective-permute-start(f32[256,128]{0,1:T(8,128)S(1)} %pad_maximum_fusion.2), channel_id=1, source_target_pairs={{0,4},{4,0},{8,12},{12,8},{1,5},{5,1},{9,13},{13,9},{2,6},{6,2},{1... | collective-permute-start | bytes 393224 | tf_op jit(solution)/shard_map/ppermute | solution.py:30
  14.3 5.2 %collective-permute-start.2 = (bf16[128,512]{1,0:T(8,128)(2,1)}, bf16[128,512]{1,0:T(8,128)(2,1)S(1)}, u32[]{:S(2)}, u32[]{:S(2)}) collective-permute-start(bf16[128,512]{1,0:T(8,128)(2,1)} %get-tuple-element.96), channel_id=1, source_target_pairs={{0,2},{1,3},{2,0},{3,1},{4,6},{5,7},{6,4},{7,5},{8,10},{9,11},{10,... | collective-permute-start | bytes 393224 | tf_op jit(solution)/shard_map/ppermute | solution.py:20
  15.0 5.3 %collective-permute-start = (bf16[256,512]{1,0:T(8,128)(2,1)S(1)}, bf16[256,512]{1,0:T(8,128)(2,1)S(1)}, u32[]{:S(2)}, u32[]{:S(2)}) collective-permute-start(bf16[256,512]{1,0:T(8,128)(2,1)S(1)} %bitcast.45), channel_id=1, source_target_pairs={{0,1},{1,0},{2,3},{3,2},{4,5},{5,4},{6,7},{7,6},{8,9},{9,8},{10,11... | collective-permute-start | bytes 786440 | tf_op jit(solution)/shard_map/ppermute | solution.py:20
  15.1 14.9 %collective-permute-start.14 = (bf16[256,512]{1,0:T(8,128)(2,1)S(1)}, bf16[256,512]{1,0:T(8,128)(2,1)S(1)}, u32[]{:S(2)}, u32[]{:S(2)}) collective-permute-start(bf16[256,512]{1,0:T(8,128)(2,1)S(1)} %pad_maximum_fusion.refs_0_), channel_id=1, source_target_pairs={{0,4},{4,0},{8,12},{12,8},{1,5},{5,1},{9,13},{13,9},{2,6},{6,2},{1... | collective-permute-start | bytes 786440 | tf_op jit(solution)/shard_map/ppermute | solution.py:30
  16.0 12.1 %collective-permute-start.5 = (bf16[256,512]{1,0:T(8,128)(2,1)S(1)}, bf16[256,512]{1,0:T(8,128)(2,1)S(1)}, u32[]{:S(2)}, u32[]{:S(2)}) collective-permute-start(bf16[256,512]{1,0:T(8,128)(2,1)S(1)} %pad_maximum_fusion.refs_0_), channel_id=1, source_target_pairs={{0,8},{4,12},{8,0},{12,4},{1,9},{5,13},{9,1},{13,5},{2,10},{6,14},... | collective-permute-start | bytes 786440 | tf_op jit(solution)/shard_map/ppermute | solution.py:30
  19.5 83.5 %copy-start.4 = (bf16[256,512]{1,0:T(8,128)(2,1)}, bf16[256,512]{1,0:T(8,128)(2,1)S(1)}, u32[]{:S(2)}) copy-start(bf16[256,512]{1,0:T(8,128)(2,1)S(1)} %constant_dynamic-update-slice_fusion.refs_0_) | copy-start | bytes 786436
  20.3 69.1 %copy-start.6 = (bf16[256,512]{1,0:T(8,128)(2,1)}, bf16[256,512]{1,0:T(8,128)(2,1)S(1)}, u32[]{:S(2)}) copy-start(bf16[256,512]{1,0:T(8,128)(2,1)S(1)} %collective-permute-done.refs_5_) | copy-start | bytes 786436
  28.1 2.0 collective-permute-start.7
  28.8 12.7 %collective-permute-start.8 = (bf16[256,512]{1,0:T(8,128)(2,1)S(1)}, bf16[256,512]{1,0:T(8,128)(2,1)S(1)}, u32[]{:S(2)}, u32[]{:S(2)}) collective-permute-start(bf16[256,512]{1,0:T(8,128)(2,1)S(1)} %collective-permute-done.5.refs_2_), channel_id=1, source_target_pairs={{4,0},{8,12},{5,1},{9,13},{6,2},{10,14},{7,3},{11,15},{20,16},{24,... | collective-permute-start | bytes 786440 | tf_op jit(solution)/shard_map/ppermute | solution.py:30
  30.1 18.4 %copy-start.22 = (bf16[256,512]{1,0:T(8,128)(2,1)}, bf16[256,512]{1,0:T(8,128)(2,1)S(1)}, u32[]{:S(2)}) copy-start(bf16[256,512]{1,0:T(8,128)(2,1)S(1)} %collective-permute-done.7.refs_3_) | copy-start | bytes 786436
  41.5 10.8 %copy-start.27 = (f32[256,128]{0,1:T(8,128)S(1)}, f32[256,128]{0,1:T(8,128)}, u32[]{:S(2)}) copy-start(f32[256,128]{0,1:T(8,128)} %fusion.14) | copy-start | bytes 393220
  48.5 4.0 %collective-permute-start.15 = (bf16[64,3584]{1,0:T(8,128)(2,1)S(1)}, bf16[64,3584]{1,0:T(8,128)(2,1)S(1)}, u32[]{:S(2)}, u32[]{:S(2)}) collective-permute-start(bf16[64,3584]{1,0:T(8,128)(2,1)S(1)} %get-tuple-element.53), channel_id=1, source_target_pairs={{0,1},{1,0},{2,3},{3,2},{4,5},{5,4},{6,7},{7,6},{8,9},{9,8},{10,11... | collective-permute-start | bytes 1376264 | tf_op jit(solution)/shard_map/ppermute | solution.py:20
  48.6 4.0 %collective-permute-start.16 = (bf16[64,3584]{1,0:T(8,128)(2,1)S(1)}, bf16[64,3584]{1,0:T(8,128)(2,1)S(1)}, u32[]{:S(2)}, u32[]{:S(2)}) collective-permute-start(bf16[64,3584]{1,0:T(8,128)(2,1)S(1)} %get-tuple-element.54), channel_id=1, source_target_pairs={{0,1},{1,0},{2,3},{3,2},{4,5},{5,4},{6,7},{7,6},{8,9},{9,8},{10,11... | collective-permute-start | bytes 1376264 | tf_op jit(solution)/shard_map/ppermute | solution.py:20
  49.1 13.7 %collective-permute-start.17 = (bf16[256,512]{1,0:T(8,128)(2,1)S(1)}, bf16[256,512]{1,0:T(8,128)(2,1)S(1)}, u32[]{:S(2)}, u32[]{:S(2)}) collective-permute-start(bf16[256,512]{1,0:T(8,128)(2,1)S(1)} %constant_dynamic-update-slice_fusion.refs_0_), channel_id=1, source_target_pairs={{0,4},{4,0},{8,12},{12,8},{1,5},{5,1},{9,13},{13,9},{2,6},{6,2},{1... | collective-permute-start | bytes 786440 | tf_op jit(solution)/shard_map/ppermute | solution.py:30
  49.6 18.5 %collective-permute-start.9 = (bf16[256,512]{1,0:T(8,128)(2,1)S(1)}, bf16[256,512]{1,0:T(8,128)(2,1)S(1)}, u32[]{:S(2)}, u32[]{:S(2)}) collective-permute-start(bf16[256,512]{1,0:T(8,128)(2,1)S(1)} %constant_dynamic-update-slice_fusion.refs_0_), channel_id=1, source_target_pairs={{0,8},{4,12},{8,0},{12,4},{1,9},{5,13},{9,1},{13,5},{2,10},{6,14},... | collective-permute-start | bytes 786440 | tf_op jit(solution)/shard_map/ppermute | solution.py:30
  52.3 26.0 %collective-permute-start.21 = (f32[256,128]{0,1:T(8,128)S(1)}, f32[256,128]{0,1:T(8,128)S(1)}, u32[]{:S(2)}, u32[]{:S(2)}) collective-permute-start(f32[256,128]{0,1:T(8,128)S(1)} %copy-done.27), channel_id=1, source_target_pairs={{0,8},{4,12},{8,0},{12,4},{1,9},{5,13},{9,1},{13,5},{2,10},{6,14},... | collective-permute-start | bytes 393224 | tf_op jit(solution)/shard_map/ppermute | solution.py:30
  52.5 27.0 %copy-start.29 = (s32[1,256]{1,0:T(1,128)S(1)}, s32[1,256]{1,0:T(1,128)}, u32[]{:S(2)}) copy-start(s32[1,256]{1,0:T(1,128)} %param.12) | copy-start | bytes 3076
  52.6 27.2 %copy-start.30 = (s32[4]{0:T(128)S(1)}, s32[4]{0:T(128)}, u32[]{:S(2)}) copy-start(s32[4]{0:T(128)} %param.13) | copy-start | bytes 52
  53.1 42.6 %collective-permute-start.20 = (bf16[128,3584]{1,0:T(8,128)(2,1)S(1)}, bf16[128,3584]{1,0:T(8,128)(2,1)S(1)}, u32[]{:S(2)}, u32[]{:S(2)}) collective-permute-start(bf16[128,3584]{1,0:T(8,128)(2,1)S(1)} %pair.4), channel_id=1, source_target_pairs={{0,2},{1,3},{2,0},{3,1},{4,6},{5,7},{6,4},{7,5},{8,10},{9,11},{10,... | collective-permute-start | bytes 2752520 | tf_op jit(solution)/shard_map/ppermute | solution.py:20
  62.8 14.2 %copy-start.10 = (bf16[256,512]{1,0:T(8,128)(2,1)}, bf16[256,512]{1,0:T(8,128)(2,1)S(1)}, u32[]{:S(2)}) copy-start(bf16[256,512]{1,0:T(8,128)(2,1)S(1)} %collective-permute-done.17.refs_1_) | copy-start | bytes 786436
  77.0 14.9 %collective-permute-start.18 = (bf16[64,3584]{1,0:T(8,128)(2,1)S(1)}, bf16[64,3584]{1,0:T(8,128)(2,1)S(1)}, u32[]{:S(2)}, u32[]{:S(2)}) collective-permute-start(bf16[64,3584]{1,0:T(8,128)(2,1)S(1)} %get-tuple-element.57), channel_id=1, source_target_pairs={{0,1},{1,0},{2,3},{3,2},{4,5},{5,4},{6,7},{7,6},{8,9},{9,8},{10,11... | collective-permute-start | bytes 1376264 | tf_op jit(solution)/shard_map/ppermute | solution.py:20
  77.1 14.8 %collective-permute-start.19 = (bf16[64,3584]{1,0:T(8,128)(2,1)S(1)}, bf16[64,3584]{1,0:T(8,128)(2,1)S(1)}, u32[]{:S(2)}, u32[]{:S(2)}) collective-permute-start(bf16[64,3584]{1,0:T(8,128)(2,1)S(1)} %get-tuple-element.58), channel_id=1, source_target_pairs={{0,1},{1,0},{2,3},{3,2},{4,5},{5,4},{6,7},{7,6},{8,9},{9,8},{10,11... | collective-permute-start | bytes 1376264 | tf_op jit(solution)/shard_map/ppermute | solution.py:20
  77.6 2.2 %collective-permute-start.10 = (bf16[256,512]{1,0:T(8,128)(2,1)S(1)}, bf16[256,512]{1,0:T(8,128)(2,1)S(1)}, u32[]{:S(2)}, u32[]{:S(2)}) collective-permute-start(bf16[256,512]{1,0:T(8,128)(2,1)S(1)} %constant_dynamic-update-slice_fusion.refs_0_), channel_id=1, source_target_pairs={{4,8},{8,4},{5,9},{9,5},{6,10},{10,6},{7,11},{11,7},{20,24},{24,20... | collective-permute-start | bytes 786440 | tf_op jit(solution)/shard_map/ppermute | solution.py:30
  78.3 10.2 %collective-permute-start.11 = (bf16[256,512]{1,0:T(8,128)(2,1)S(1)}, bf16[256,512]{1,0:T(8,128)(2,1)S(1)}, u32[]{:S(2)}, u32[]{:S(2)}) collective-permute-start(bf16[256,512]{1,0:T(8,128)(2,1)S(1)} %collective-permute-done.9.refs_2_), channel_id=1, source_target_pairs={{4,0},{8,12},{5,1},{9,13},{6,2},{10,14},{7,3},{11,15},{20,16},{24,... | collective-permute-start | bytes 786440 | tf_op jit(solution)/shard_map/ppermute | solution.py:30
  89.2 13.6 %collective-permute-start.13 = (bf16[256,512]{1,0:T(8,128)(2,1)S(1)}, bf16[256,512]{1,0:T(8,128)(2,1)S(1)}, u32[]{:S(2)}, u32[]{:S(2)}) collective-permute-start(bf16[256,512]{1,0:T(8,128)(2,1)S(1)} %collective-permute-done.refs_5_), channel_id=1, source_target_pairs={{0,8},{4,12},{8,0},{12,4},{1,9},{5,13},{9,1},{13,5},{2,10},{6,14},... | collective-permute-start | bytes 786440 | tf_op jit(solution)/shard_map/ppermute | solution.py:30
  89.4 13.6 %collective-permute-start.12 = (bf16[256,512]{1,0:T(8,128)(2,1)S(1)}, bf16[256,512]{1,0:T(8,128)(2,1)}, u32[]{:S(2)}, u32[]{:S(2)}) collective-permute-start(bf16[256,512]{1,0:T(8,128)(2,1)S(1)} %collective-permute-done.refs_5_), channel_id=1, source_target_pairs={{0,4},{4,0},{8,12},{12,8},{1,5},{5,1},{9,13},{13,9},{2,6},{6,2},{1... | collective-permute-start | bytes 786440 | tf_op jit(solution)/shard_map/ppermute | solution.py:30
  92.4 35.7 %collective-permute-start.24 = (bf16[128,3584]{1,0:T(8,128)(2,1)S(1)}, bf16[128,3584]{1,0:T(8,128)(2,1)S(1)}, u32[]{:S(2)}, u32[]{:S(2)}) collective-permute-start(bf16[128,3584]{1,0:T(8,128)(2,1)S(1)} %pair.5), channel_id=1, source_target_pairs={{0,2},{1,3},{2,0},{3,1},{4,6},{5,7},{6,4},{7,5},{8,10},{9,11},{10,... | collective-permute-start | bytes 2752520 | tf_op jit(solution)/shard_map/ppermute | solution.py:20
  102.7 11.6 %copy-start.8 = (bf16[256,512]{1,0:T(8,128)(2,1)}, bf16[256,512]{1,0:T(8,128)(2,1)S(1)}, u32[]{:S(2)}) copy-start(bf16[256,512]{1,0:T(8,128)(2,1)S(1)} %collective-permute-done.13.refs_7_) | copy-start | bytes 786436
  115.3 4.0 %collective-permute-start.22 = (bf16[64,3584]{1,0:T(8,128)(2,1)S(1)}, bf16[64,3584]{1,0:T(8,128)(2,1)S(1)}, u32[]{:S(2)}, u32[]{:S(2)}) collective-permute-start(bf16[64,3584]{1,0:T(8,128)(2,1)S(1)} %get-tuple-element.63), channel_id=1, source_target_pairs={{0,1},{1,0},{2,3},{3,2},{4,5},{5,4},{6,7},{7,6},{8,9},{9,8},{10,11... | collective-permute-start | bytes 1376264 | tf_op jit(solution)/shard_map/ppermute | solution.py:20
  115.3 5.1 %collective-permute-start.23 = (bf16[64,3584]{1,0:T(8,128)(2,1)}, bf16[64,3584]{1,0:T(8,128)(2,1)}, u32[]{:S(2)}, u32[]{:S(2)}) collective-permute-start(bf16[64,3584]{1,0:T(8,128)(2,1)} %get-tuple-element.64), channel_id=1, source_target_pairs={{0,1},{1,0},{2,3},{3,2},{4,5},{5,4},{6,7},{7,6},{8,9},{9,8},{10,11... | collective-permute-start | bytes 1376264 | tf_op jit(solution)/shard_map/ppermute | solution.py:20
  115.9 8.4 %collective-permute-start.27 = (bf16[4,4224]{1,0:T(4,128)(2,1)S(1)}, bf16[4,4224]{1,0:T(4,128)(2,1)S(1)}, u32[]{:S(2)}, u32[]{:S(2)}) collective-permute-start(bf16[4,4224]{1,0:T(4,128)(2,1)S(1)} %pad_maximum_fusion.3), channel_id=1, source_target_pairs={{0,3},{1,2},{2,1},{3,0},{4,7},{5,6},{6,5},{7,4},{8,11},{9,10},{10,... | collective-permute-start | bytes 101384 | tf_op jit(solution)/shard_map/ppermute | solution.py:20
  118.8 7.3 %collective-permute-start.26 = (bf16[4,4224]{1,0:T(4,128)(2,1)S(1)}, bf16[4,4224]{1,0:T(4,128)(2,1)}, u32[]{:S(2)}, u32[]{:S(2)}) collective-permute-start(bf16[4,4224]{1,0:T(4,128)(2,1)S(1)} %pad_maximum_fusion.3), channel_id=1, source_target_pairs={{0,2},{1,3},{2,0},{3,1},{4,6},{5,7},{6,4},{7,5},{8,10},{9,11},{10,... | collective-permute-start | bytes 101384 | tf_op jit(solution)/shard_map/ppermute | solution.py:20
  119.3 7.5 %collective-permute-start.25 = (bf16[4,4224]{1,0:T(4,128)(2,1)S(1)}, bf16[4,4224]{1,0:T(4,128)(2,1)}, u32[]{:S(2)}, u32[]{:S(2)}) collective-permute-start(bf16[4,4224]{1,0:T(4,128)(2,1)S(1)} %pad_maximum_fusion.3), channel_id=1, source_target_pairs={{0,1},{1,0},{2,3},{3,2},{4,5},{5,4},{6,7},{7,6},{8,9},{9,8},{10,11... | collective-permute-start | bytes 101384 | tf_op jit(solution)/shard_map/ppermute | solution.py:20
  120.4 14.4 %collective-permute-start.29 = (bf16[256,512]{1,0:T(8,128)(2,1)S(1)}, bf16[256,512]{1,0:T(8,128)(2,1)S(1)}, u32[]{:S(2)}, u32[]{:S(2)}) collective-permute-start(bf16[256,512]{1,0:T(8,128)(2,1)S(1)} %bitcast.38), channel_id=1, source_target_pairs={{0,8},{4,12},{8,0},{12,4},{1,9},{5,13},{9,1},{13,5},{2,10},{6,14},... | collective-permute-start | bytes 786440 | tf_op jit(solution)/shard_map/ppermute | solution.py:30
  122.0 22.0 %copy-start.5 = (bf16[256,512]{1,0:T(8,128)(2,1)S(1)}, bf16[256,512]{1,0:T(8,128)(2,1)}, u32[]{:S(2)}) copy-start(bf16[256,512]{1,0:T(8,128)(2,1)} %copy-done.4) | copy-start | bytes 786436
  122.0 22.0 %copy-start.7 = (bf16[256,512]{1,0:T(8,128)(2,1)S(1)}, bf16[256,512]{1,0:T(8,128)(2,1)}, u32[]{:S(2)}) copy-start(bf16[256,512]{1,0:T(8,128)(2,1)} %copy-done.6) | copy-start | bytes 786436
  122.0 22.0 %copy-start.9 = (bf16[256,512]{1,0:T(8,128)(2,1)S(1)}, bf16[256,512]{1,0:T(8,128)(2,1)}, u32[]{:S(2)}) copy-start(bf16[256,512]{1,0:T(8,128)(2,1)} %copy-done.8) | copy-start | bytes 786436
  122.0 22.0 %copy-start.12 = (bf16[256,512]{1,0:T(8,128)(2,1)S(1)}, bf16[256,512]{1,0:T(8,128)(2,1)}, u32[]{:S(2)}) copy-start(bf16[256,512]{1,0:T(8,128)(2,1)} %copy-done.10) | copy-start | bytes 786436
  122.0 22.0 %copy-start.15 = (bf16[256,512]{1,0:T(8,128)(2,1)S(1)}, bf16[256,512]{1,0:T(8,128)(2,1)}, u32[]{:S(2)}) copy-start(bf16[256,512]{1,0:T(8,128)(2,1)} %copy-done.13) | copy-start | bytes 786436
  122.0 22.0 %copy-start.18 = (bf16[256,512]{1,0:T(8,128)(2,1)S(1)}, bf16[256,512]{1,0:T(8,128)(2,1)}, u32[]{:S(2)}) copy-start(bf16[256,512]{1,0:T(8,128)(2,1)} %copy-done.16) | copy-start | bytes 786436
  122.0 22.0 %copy-start.21 = (bf16[256,512]{1,0:T(8,128)(2,1)S(1)}, bf16[256,512]{1,0:T(8,128)(2,1)}, u32[]{:S(2)}) copy-start(bf16[256,512]{1,0:T(8,128)(2,1)} %copy-done.19) | copy-start | bytes 786436
  124.3 14.7 %collective-permute-start.28 = (bf16[256,512]{1,0:T(8,128)(2,1)S(1)}, bf16[256,512]{1,0:T(8,128)(2,1)S(1)}, u32[]{:S(2)}, u32[]{:S(2)}) collective-permute-start(bf16[256,512]{1,0:T(8,128)(2,1)S(1)} %bitcast.39), channel_id=1, source_target_pairs={{0,4},{4,0},{8,12},{12,8},{1,5},{5,1},{9,13},{13,9},{2,6},{6,2},{1... | collective-permute-start | bytes 786440 | tf_op jit(solution)/shard_map/ppermute | solution.py:30
  126.1 13.0 %collective-permute-start.30 = (bf16[256,512]{1,0:T(8,128)(2,1)}, bf16[256,512]{1,0:T(8,128)(2,1)S(1)}, u32[]{:S(2)}, u32[]{:S(2)}) collective-permute-start(bf16[256,512]{1,0:T(8,128)(2,1)} %copy-done.6), channel_id=1, source_target_pairs={{4,8},{8,4},{5,9},{9,5},{6,10},{10,6},{7,11},{11,7},{20,24},{24,20... | collective-permute-start | bytes 786440 | tf_op jit(solution)/shard_map/ppermute | solution.py:30
  126.8 17.1 %collective-permute-start.31 = (bf16[256,512]{1,0:T(8,128)(2,1)}, bf16[256,512]{1,0:T(8,128)(2,1)S(1)}, u32[]{:S(2)}, u32[]{:S(2)}) collective-permute-start(bf16[256,512]{1,0:T(8,128)(2,1)} %copy-done.8), channel_id=1, source_target_pairs={{4,0},{8,12},{5,1},{9,13},{6,2},{10,14},{7,3},{11,15},{20,16},{24,... | collective-permute-start | bytes 786440 | tf_op jit(solution)/shard_map/ppermute | solution.py:30
  128.1 30.1 %collective-permute-start.34 = (bf16[128,3584]{1,0:T(8,128)(2,1)S(1)}, bf16[128,3584]{1,0:T(8,128)(2,1)S(1)}, u32[]{:S(2)}, u32[]{:S(2)}) collective-permute-start(bf16[128,3584]{1,0:T(8,128)(2,1)S(1)} %pair.6), channel_id=1, source_target_pairs={{0,2},{1,3},{2,0},{3,1},{4,6},{5,7},{6,4},{7,5},{8,10},{9,11},{10,... | collective-permute-start | bytes 2752520 | tf_op jit(solution)/shard_map/ppermute | solution.py:20
  155.2 1.9 collective-permute-start.32
  155.3 2.5 %collective-permute-start.33 = (bf16[64,3584]{1,0:T(8,128)(2,1)S(1)}, bf16[64,3584]{1,0:T(8,128)(2,1)S(1)}, u32[]{:S(2)}, u32[]{:S(2)}) collective-permute-start(bf16[64,3584]{1,0:T(8,128)(2,1)S(1)} %get-tuple-element.73), channel_id=1, source_target_pairs={{0,1},{1,0},{2,3},{3,2},{4,5},{5,4},{6,7},{7,6},{8,9},{9,8},{10,11... | collective-permute-start | bytes 1376264 | tf_op jit(solution)/shard_map/ppermute | solution.py:20
  158.3 1.9 collective-permute-start.35
  158.5 3.2 %collective-permute-start.36 = (bf16[64,3584]{1,0:T(8,128)(2,1)S(1)}, bf16[64,3584]{1,0:T(8,128)(2,1)S(1)}, u32[]{:S(2)}, u32[]{:S(2)}) collective-permute-start(bf16[64,3584]{1,0:T(8,128)(2,1)S(1)} %get-tuple-element.77), channel_id=1, source_target_pairs={{0,1},{1,0},{2,3},{3,2},{4,5},{5,4},{6,7},{7,6},{8,9},{9,8},{10,11... | collective-permute-start | bytes 1376264 | tf_op jit(solution)/shard_map/ppermute | solution.py:20
  158.8 4.5 %collective-permute-start.37 = (bf16[64,3584]{1,0:T(8,128)(2,1)S(1)}, bf16[64,3584]{1,0:T(8,128)(2,1)S(1)}, u32[]{:S(2)}, u32[]{:S(2)}) collective-permute-start(bf16[64,3584]{1,0:T(8,128)(2,1)S(1)} %get-tuple-element.79), channel_id=1, source_target_pairs={{0,1},{1,0},{2,3},{3,2},{4,5},{5,4},{6,7},{7,6},{8,9},{9,8},{10,11... | collective-permute-start | bytes 1376264 | tf_op jit(solution)/shard_map/ppermute | solution.py:20
  159.0 4.4 %collective-permute-start.38 = (bf16[64,3584]{1,0:T(8,128)(2,1)S(1)}, bf16[64,3584]{1,0:T(8,128)(2,1)S(1)}, u32[]{:S(2)}, u32[]{:S(2)}) collective-permute-start(bf16[64,3584]{1,0:T(8,128)(2,1)S(1)} %get-tuple-element.81), channel_id=1, source_target_pairs={{0,1},{1,0},{2,3},{3,2},{4,5},{5,4},{6,7},{7,6},{8,9},{9,8},{10,11... | collective-permute-start | bytes 1376264 | tf_op jit(solution)/shard_map/ppermute | solution.py:20
  159.3 4.0 %collective-permute-start.39 = (bf16[256,512]{1,0:T(8,128)(2,1)S(1)}, bf16[256,512]{1,0:T(8,128)(2,1)S(1)}, u32[]{:S(2)}, u32[]{:S(2)}) collective-permute-start(bf16[256,512]{1,0:T(8,128)(2,1)S(1)} %bitcast.40), channel_id=1, source_target_pairs={{4,8},{8,4},{5,9},{9,5},{6,10},{10,6},{7,11},{11,7},{20,24},{24,20... | collective-permute-start | bytes 786440 | tf_op jit(solution)/shard_map/ppermute | solution.py:30
  160.1 10.2 %collective-permute-start.40 = (bf16[256,512]{1,0:T(8,128)(2,1)S(1)}, bf16[256,512]{1,0:T(8,128)(2,1)S(1)}, u32[]{:S(2)}, u32[]{:S(2)}) collective-permute-start(bf16[256,512]{1,0:T(8,128)(2,1)S(1)} %collective-permute-done.29.refs_2_), channel_id=1, source_target_pairs={{4,0},{8,12},{5,1},{9,13},{6,2},{10,14},{7,3},{11,15},{20,16},{24,... | collective-permute-start | bytes 786440 | tf_op jit(solution)/shard_map/ppermute | solution.py:30
  161.6 40.7 %collective-permute-start.45 = (bf16[128,3584]{1,0:T(8,128)(2,1)S(1)}, bf16[128,3584]{1,0:T(8,128)(2,1)S(1)}, u32[]{:S(2)}, u32[]{:S(2)}) collective-permute-start(bf16[128,3584]{1,0:T(8,128)(2,1)S(1)} %pair.7), channel_id=1, source_target_pairs={{0,2},{1,3},{2,0},{3,1},{4,6},{5,7},{6,4},{7,5},{8,10},{9,11},{10,... | collective-permute-start | bytes 2752520 | tf_op jit(solution)/shard_map/ppermute | solution.py:20
  189.4 1.9 collective-permute-start.41
  189.4 2.5 %collective-permute-start.42 = (bf16[64,3584]{1,0:T(8,128)(2,1)S(1)}, bf16[64,3584]{1,0:T(8,128)(2,1)S(1)}, u32[]{:S(2)}, u32[]{:S(2)}) collective-permute-start(bf16[64,3584]{1,0:T(8,128)(2,1)S(1)} %get-tuple-element.86), channel_id=1, source_target_pairs={{0,1},{1,0},{2,3},{3,2},{4,5},{5,4},{6,7},{7,6},{8,9},{9,8},{10,11... | collective-permute-start | bytes 1376264 | tf_op jit(solution)/shard_map/ppermute | solution.py:20
  189.9 8.9 %collective-permute-start.43 = (bf16[64,3584]{1,0:T(8,128)(2,1)S(1)}, bf16[64,3584]{1,0:T(8,128)(2,1)S(1)}, u32[]{:S(2)}, u32[]{:S(2)}) collective-permute-start(bf16[64,3584]{1,0:T(8,128)(2,1)S(1)} %get-tuple-element.87), channel_id=1, source_target_pairs={{0,1},{1,0},{2,3},{3,2},{4,5},{5,4},{6,7},{7,6},{8,9},{9,8},{10,11... | collective-permute-start | bytes 1376264 | tf_op jit(solution)/shard_map/ppermute | solution.py:20
  190.0 8.8 %collective-permute-start.44 = (bf16[64,3584]{1,0:T(8,128)(2,1)S(1)}, bf16[64,3584]{1,0:T(8,128)(2,1)S(1)}, u32[]{:S(2)}, u32[]{:S(2)}) collective-permute-start(bf16[64,3584]{1,0:T(8,128)(2,1)S(1)} %get-tuple-element.88), channel_id=1, source_target_pairs={{0,1},{1,0},{2,3},{3,2},{4,5},{5,4},{6,7},{7,6},{8,9},{9,8},{10,11... | collective-permute-start | bytes 1376264 | tf_op jit(solution)/shard_map/ppermute | solution.py:20
  (13 other events, 31.5 us)

commit v6 on v5

v6 whole, which is shorter than its diff:
```python
import functools

import jax
import jax.numpy as jnp
from jax import lax
from jax.experimental import pallas as pl
from jax.experimental.pallas import tpu as pltpu
from jax.sharding import PartitionSpec as P

GROUPS = 8

highest = lax.Precision.HIGHEST
f32, bf16 = jnp.float32, jnp.bfloat16


def swap(value, step):
    size = lax.axis_size("dp")
    return lax.ppermute(value, "dp", [(d, d ^ step) for d in range(size)])


def after(value, *earlier):
    return lax.optimization_barrier((value,) + earlier)[0]


def across(value, step, places=None):
    size = lax.axis_size("tensor")
    pairs = [(t, t ^ step) for t in range(size) if places is None or t in places]
    return lax.ppermute(value, "tensor", pairs)


def spread_first(block):
    second = across(block, 2)
    return [block, across(block, 1), second]


def spread_last(blocks, *earlier):
    block, _, second = blocks
    middle = across(after(block, second, *earlier), 3, (1, 2))
    ends = across(after(second, *earlier), 1, (1, 2))
    return blocks + [middle, ends]


def terms_kernel(size, count, first, adds, per_part, place_ref, *refs):
    total = 5 * count
    groups = [refs[5 * group : 5 * group + 5] for group in range(count)]
    w_ref, add_refs, outs = refs[total], refs[total + 1 :][: len(adds)], refs[total + 1 + len(adds) : -4]
    feats, held, sems, held_sems = refs[-4:]
    width, tile = feats.shape[1] // size, outs[0].shape[1]
    tall = feats.shape[0] // len(groups)
    j, steps = pl.program_id(0), pl.num_programs(0)
    slots = held.shape[0]

    def put(value, group, source, slot):
        at = pl.ds(pl.multiple_of(source * width, width), width)
        rows = pl.ds(group * tall, tall)
        return pltpu.make_async_copy(value, feats.at[rows, at], sems.at[group * size + slot])

    def fetch(step):
        slot = lax.rem(step, slots)
        at = pl.ds(pl.multiple_of(first + step * tile, tile), tile)
        return pltpu.make_async_copy(w_ref.at[:, 0, :, at], held.at[slot], held_sems.at[slot])

    @pl.when(j == 0)
    def _():
        copies = []
        place = place_ref[0]
        for group, blocks in enumerate(groups):
            copies += [put(blocks[k], group, lax.bitwise_xor(place, k), k) for k in range(3)]
        for copy in copies:
            copy.start()
        for step in range(slots):
            fetch(step).start()
        inside = jnp.logical_or(place == 1, place == 2)
        for group, blocks in enumerate(groups):
            for chosen, block in ((inside, blocks[3]), (jnp.logical_not(inside), blocks[4])):

                @pl.when(chosen)
                def _():
                    last = put(block, group, lax.bitwise_xor(place, 3), 3)
                    last.start()
                    last.wait()

        for copy in copies:
            copy.wait()

    fetch(j).wait()
    weight = held[lax.rem(j, slots)].reshape(size * width, tile)
    terms = jnp.dot(feats[...], weight, preferred_element_type=f32)
    row = 0
    for out_ref in outs:
        if not adds:
            out_ref[...] = terms[row : row + out_ref.shape[0]].astype(bf16)
        row += out_ref.shape[0]

    def add_part(part):
        here = [(ref, at) for ref, (at, of) in zip(add_refs, adds) if of == part]
        cut = min(ref.shape[0] for ref, _ in here)
        for row in range(0, feats.shape[0], cut):
            total = terms[row : row + cut]
            for ref, at in here:
                if at <= row < at + ref.shape[0]:
                    total = total + ref[row - at : row - at + cut].astype(f32)
            outs[0][row : row + cut] = total.astype(bf16)

    for part in sorted({of for _, of in adds}):
        pl.when(j // per_part == part)(functools.partial(add_part, part))

    @pl.when(j + slots < steps)
    def _():
        fetch(j + slots).start()


def block_terms(groups, down_weight, col_start, cols, outs, adds=()):
    size, _, width, _ = down_weight.shape
    rows = sum(outs)
    tile = max(n for n in range(128, 513, 128) if cols % n == 0)
    slots = min(4, cols // tile)
    blocks = [block for group in groups for block in group]
    per_part = adds[0][0].shape[1] // tile if adds else 1

    def add_spec(value, part):
        return pl.BlockSpec(
            (value.shape[0], tile),
            lambda j, place: (0, jnp.clip(j - part * per_part, 0, per_part - 1)),
        )

    return pl.pallas_call(
        functools.partial(
            terms_kernel,
            size,
            len(groups),
            col_start,
            [add[1:] for add in adds],
            per_part,
        ),
        out_shape=[jax.ShapeDtypeStruct((tall, cols), bf16) for tall in outs],
        grid_spec=pltpu.PrefetchScalarGridSpec(
            num_scalar_prefetch=1,
            grid=(cols // tile,),
            in_specs=[pl.BlockSpec(memory_space=pl.ANY)] * (len(blocks) + 1)
            + [add_spec(value, part) for value, _, part in adds],
            out_specs=[pl.BlockSpec((tall, tile), lambda j, place: (0, j)) for tall in outs],
            scratch_shapes=[
                pltpu.VMEM((rows, size * width), bf16),
                pltpu.VMEM((slots, size, width, tile), bf16),
                pltpu.SemaphoreType.DMA((len(groups) * size,)),
                pltpu.SemaphoreType.DMA((slots,)),
            ],
        ),
        compiler_params=pltpu.CompilerParams(vmem_limit_bytes=40 << 20),
        cost_estimate=pl.CostEstimate(
            flops=8 * rows * size * width * cols, bytes_accessed=1000, transcendentals=0
        ),
        name="terms",
    )(
        lax.axis_index("tensor").reshape(1),
        *blocks,
        down_weight,
        *[value for value, _, _ in adds],
    )


def add_kernel(kept_ref, first_ref, second_ref, out_ref):
    rows = first_ref.shape[0]
    for index, other in enumerate((first_ref, second_ref)):
        cut = slice(index * rows, (index + 1) * rows)
        out_ref[cut] = (kept_ref[cut].astype(f32) + other[...].astype(f32)).astype(bf16)


def add_halves(kept, first, second):
    rows, cols = kept.shape
    tile = max(n for n in range(128, 1025, 128) if cols % n == 0)

    def spec(tall):
        return pl.BlockSpec((tall, tile), lambda j: (0, j))

    return pl.pallas_call(
        add_kernel,
        out_shape=jax.ShapeDtypeStruct((rows, cols), bf16),
        grid=(cols // tile,),
        in_specs=[spec(rows), spec(rows // 2), spec(rows // 2)],
        out_specs=spec(rows),
        compiler_params=pltpu.CompilerParams(vmem_limit_bytes=16 << 20),
        cost_estimate=pl.CostEstimate(flops=1000, bytes_accessed=1000, transcendentals=0),
        name="pair",
    )(kept, first, second)


def finish_kernel(own_ref, other_ref, out_ref):
    out_ref[...] = (own_ref[...].astype(f32) + other_ref[...].astype(f32)).astype(bf16)


def finish(result, other, row, col):
    rows, cols = other.shape
    tile = max(n for n in range(128, 2049, 128) if cols % n == 0)
    part = pl.BlockSpec((rows, tile), lambda j: (row // rows, col // tile + j))
    return pl.pallas_call(
        finish_kernel,
        out_shape=jax.ShapeDtypeStruct(result.shape, bf16),
        grid=(cols // tile,),
        in_specs=[part, pl.BlockSpec((rows, tile), lambda j: (0, j))],
        out_specs=part,
        input_output_aliases={0: 0},
        compiler_params=pltpu.CompilerParams(vmem_limit_bytes=16 << 20),
        cost_estimate=pl.CostEstimate(flops=1000, bytes_accessed=1000, transcendentals=0),
        name="finish",
    )(result, other)


def example_gradients(acts_low, grads_low, local_ids, examples):
    onehot = (local_ids[:, None] == jnp.arange(examples, dtype=jnp.int32)[None, :]).astype(f32)
    counts = jnp.sum(onehot, axis=0)
    spread = (onehot[:, :, None] * acts_low[:, None, :]).reshape(onehot.shape[0], -1)
    outer_sum = lax.dot_general(
        spread,
        grads_low,
        (((0,), (0,)), ((), ())),
        precision=highest,
        preferred_element_type=f32,
    )
    basis_rank = acts_low.shape[1]
    outer_sum = outer_sum.reshape(examples, basis_rank * grads_low.shape[1]) / counts[:, None]
    return outer_sum.astype(bf16)


def gather_examples(example_grad, example_group):
    count = example_grad.shape[0]
    group_column = jnp.broadcast_to(example_group.astype(bf16)[:, None], (count, 128))
    held = jnp.concatenate([example_grad, group_column], axis=1)
    return [held] + [swap(held, step) for step in range(1, lax.axis_size("dp"))]


def order_examples(values):
    groups, place = lax.axis_size("dp"), lax.axis_index("dp")
    ordered = []
    for group in range(groups):
        value = values[0]
        for step in range(1, groups):
            value = jnp.where((place ^ group) == step, values[step], value)
        ordered.append(value)
    return jnp.concatenate(ordered, axis=0)


def fisher_and_groups(every, flat_width):
    row_count = flat_width // lax.axis_size("dp")
    col_count = flat_width // lax.axis_size("tensor")
    col_start = lax.axis_index("tensor") * col_count
    row_start = lax.axis_index("dp") * row_count
    every_group = every[:, flat_width].astype(jnp.int32)
    rows_part = lax.dynamic_slice_in_dim(every, row_start, row_count, 1)
    cols_part = lax.dynamic_slice_in_dim(every, col_start, col_count, 1)
    fisher = lax.dot_general(
        rows_part, cols_part, (((0,), (0,)), ((), ())), preferred_element_type=f32
    )
    member = (every_group[:, None] == jnp.arange(GROUPS, dtype=jnp.int32)[None, :]).astype(bf16)
    group_grad = lax.dot_general(
        member, cols_part, (((0,), (0,)), ((), ())), preferred_element_type=f32
    )
    return fisher, group_grad


def small_sums(hidden_acts, output_grad, input_basis, output_basis):
    acts_part = jnp.dot(hidden_acts, input_basis, preferred_element_type=f32)
    grads_part = lax.dot_general(
        output_grad,
        output_basis,
        (((0, 1, 2), (0, 1, 2)), ((), ())),
        preferred_element_type=f32,
    )
    return jnp.concatenate([acts_part, grads_part], axis=1)


def any_mesh(
    hidden_acts, output_grad, down_weight, input_basis, output_basis, token_example, example_group
):
    pieces = lax.all_to_all(output_grad, "dp", split_axis=1, concat_axis=3, tiled=True)
    columns = lax.all_gather(pieces, "tensor", axis=0, tiled=True)
    parts = small_sums(hidden_acts, output_grad, input_basis, output_basis)
    terms = lax.dot_general(
        columns, down_weight, (((0, 1, 2), (0, 1, 2)), ((), ())), preferred_element_type=f32
    )
    hidden_grad = lax.psum_scatter(terms.astype(bf16), "dp", scatter_dimension=0, tiled=True)
    acts_low, grads_low = jnp.split(lax.psum(parts, "tensor"), 2, axis=1)
    example_grad = example_gradients(
        acts_low, grads_low, token_example[0], example_group.shape[0]
    )
    every = order_examples(gather_examples(example_grad, example_group))
    fisher, group_grad = fisher_and_groups(every, example_grad.shape[1])
    return (hidden_grad, fisher, group_grad)


def line_of_four(
    hidden_acts, output_grad, down_weight, input_basis, output_basis, token_example, example_group
):
    tokens, cols = hidden_acts.shape
    part, rows = cols // 2, tokens // 2
    place = lax.axis_index("dp")
    turned = jnp.transpose(output_grad[0], (0, 2, 1))
    pieces = [lax.dynamic_index_in_dim(turned, place ^ k, 0, keepdims=False) for k in range(4)]
    far = []
    for half in range(2):
        cut = slice(half * rows, (half + 1) * rows)
        far.append(jnp.concatenate([swap(pieces[3][cut], 3), swap(pieces[2][cut], 2)]))
    beside, own = swap(pieces[1], 1), pieces[0]
    parts = small_sums(hidden_acts, output_grad, input_basis, output_basis)
    low = parts + across(parts, 1)

    blocks = spread_first(after(far[0], parts))
    later = spread_first(after(far[1], blocks[2]))
    blocks = spread_last(blocks, low, beside, far[1])
    low = after(low, blocks[4])

    def far_terms(chunks, at, *earlier):
        chunks = [[after(chunks[0][0], *earlier)] + chunks[0][1:]] + chunks[1:]
        outs = [rows // 2, rows // 2, rows] + [rows // 2] * 4 * (len(chunks) - 1)
        return block_terms(chunks, down_weight, at * part, part, outs)

    def pair_sum(first, last, kept, *earlier):
        pair = add_halves(kept, swap(after(first, *earlier), 1), swap(after(last, *earlier), 1))
        return pair, swap(pair, 2)

    first, last, kept = far_terms([blocks], 0, *later)
    pair0, sum0 = pair_sum(first, last, kept)

    low = low + across(after(low, pair0), 2)
    later = spread_last(later, pair0)
    beside = spread_first(after(beside, pair0))
    first, last, kept = far_terms([blocks], 1, pair0)
    pair1, sum1 = pair_sum(first, last, kept, *later, *beside)

    beside = spread_last(beside, pair1)
    own = spread_first(after(own, pair1))
    acts_low, grads_low = jnp.split(after(low, pair1, sum0), 2, axis=1)
    example_grad = example_gradients(
        acts_low, grads_low, token_example[0], example_group.shape[0]
    )
    gathered = gather_examples(example_grad, example_group)
    first, last, kept, *near0 = far_terms([later, beside], 0, pair1, example_grad)
    pair2, sum2 = pair_sum(first, last, kept, *own)

    own = spread_last(own, pair2)
    near0 = [swap(after(term, sum1, pair2), 1) for term in near0]
    every = order_examples(after(gathered, sum1, pair2))
    fisher, group_grad = fisher_and_groups(every, example_grad.shape[1])
    first, last, kept, *near1 = far_terms([later, beside], 1, fisher, group_grad, *near0)
    pair3, sum3 = pair_sum(first, last, kept, *own)

    near1 = [swap(after(term, sum2, pair3), 1) for term in near1]
    adds = [(term, row * (rows // 2), 0) for row, term in enumerate(near0)]
    adds += [(term, row * (rows // 2), 1) for row, term in enumerate(near1)]
    adds += [(sum0, 0, 0), (sum1, 0, 1), (sum2, rows, 0)]
    (result,) = block_terms([own], down_weight, 0, cols, [tokens], adds)
    return (finish(result, sum3, rows, part), fisher, group_grad)


def per_device(hidden_acts, output_grad, down_weight, *rest):
    fits = lax.axis_size("tensor") == 4 and lax.axis_size("dp") == 4
    fits = fits and down_weight.shape[2] % 128 == 0 and down_weight.shape[3] % 1024 == 0
    fits = fits and hidden_acts.shape[0] % 64 == 0
    return (line_of_four if fits else any_mesh)(hidden_acts, output_grad, down_weight, *rest)


def solution(mesh):
    return jax.shard_map(
        per_device,
        mesh=mesh,
        in_specs=(
            P(("parts", "dp"), "tensor"),
            P("tensor", None, None, ("parts", "dp")),
            P(None, "dp", None, "tensor"),
            P("tensor", None),
            P("tensor", None, None, None),
            P(("parts", "dp"), None),
            P(("parts", "dp")),
        ),
        out_specs=(
            P(("parts", "dp"), "tensor"),
            P(("parts", "dp"), "tensor"),
            P("parts", "tensor"),
        ),
        check_vma=False,
    )
```

time: 207 us -> 194 us (0.937)
  waiting for transfers between devices: 63.3 us -> 48.9 us
  Pallas kernels: 69.4 us -> 61 us
  local copies, waits for them, and re-layouts: 16.9 us -> 22.8 us
  starting transfers between devices: 43.8 us -> 47.1 us
    ppermute x18, waiting for transfers between devices: 59 us -> 41.3 us  [across(): return lax.ppermute(value, 'tensor', pairs)]
    pallas_call x4 -> x1, Pallas kernels: 13.9 us -> 2.06 us  [finish(): pl.pallas_call(finish_kernel, out_shape=jax.ShapeDtypeStruct(result.shape...]
    unnamed x63 -> x97, local copies, waits for them, and re-layouts: 10.2 us -> 17.6 us
    ppermute x18, starting transfers between devices: 20.7 us -> 28.1 us  [across(): return lax.ppermute(value, 'tensor', pairs)]
    pallas_call x5, Pallas kernels: 51.6 us -> 56.9 us  [block_terms(): pl.pallas_call(functools.partial(terms_kernel, size, len(groups), col_sta...]
    ppermute x28, starting transfers between devices: 23.1 us -> 19 us  [swap(): return lax.ppermute(value, 'dp', [(d, d ^ step) for d in range(size)])]
    ppermute x28, waiting for transfers between devices: 4.31 us -> 7.59 us  [swap(): return lax.ppermute(value, 'dp', [(d, d ^ step) for d in range(size)])]
  transfers between devices with their start and end apart: 46 -> 46, of which waited for: 17 -> 15; matrix products, arithmetic and copies ran while one was open for 8% -> 7% of each run, Pallas kernels for 29% -> 27%
where the time goes in v6:
time: 194 us; the launch traced here: 192 us
  Pallas kernels  61 us (31%)
  waiting for transfers between devices  48.9 us (25%)
  starting transfers between devices  47.1 us (24%)
  local copies, waits for them, and re-layouts  22.8 us (12%)
  matrix products  7.54 us (4%)
  other arithmetic  3.01 us (2%)
    pallas_call x5, Pallas kernels, block_terms(): pl.pallas_call(functools.partial(terms_kernel, size, len(groups), col_sta...  56.9 us
    ppermute x18, waiting for transfers between devices, across(): return lax.ppermute(value, 'tensor', pairs)  41.3 us
    ppermute x18, starting transfers between devices, across(): return lax.ppermute(value, 'tensor', pairs)  28.1 us
    ppermute x28, starting transfers between devices, swap(): return lax.ppermute(value, 'dp', [(d, d ^ step) for d in range(size)])  19 us
    unnamed x97, local copies, waits for them, and re-layouts  17.6 us
    ppermute x28, waiting for transfers between devices, swap(): return lax.ppermute(value, 'dp', [(d, d ^ step) for d in range(size)])  7.59 us
  transfers between devices with their start and end apart: 46, of which 15 were waited for; matrix products, arithmetic and copies ran while one was open for 7% of the time, Pallas kernels for 27%

profile of v6, /device:TPU:0, one launch (start us, length us, event | category | flops | bytes accessed | tf_op | source)
XLA Modules:
  0.0 191.9 jit_solution(5176068019322147402)
XLA Ops:
  0.7 2.1 %constant_dynamic-slice_fusion = (bf16[1,1,512,256]{3,2,1,0:T(8,128)(2,1)S(1)}, bf16[1,1,512,256]{3,2,1,0:T(8,128)(2,1)S(1)}, bf16[1,1,512,256]{3,2,1,0:T(8,128)(2,1)S(1)}, bf16[1,1,512,256]{3,2,1,0:T(8,128)(2,1)}) fusion(bf16[1,4,512,256]{3,2,1,0:T(8,128)(2,1)} %param.8, s32[]{:T(128)S(6)} %select_n.96, s32[]{:T(128)S(6)} %select_n.95, s32[]{:T(128)S(6)} %select_n.94, ...), kind=kLoop, calls=%fused_computation.33 | loop fusion | bytes 2097168 | tf_op jit(solution)/shard_map/dynamic-slice.7
  2.9 0.7 slice_bitcast_fusion
  3.6 2.9 %collective-permute-start.1 = (bf16[128,512]{1,0:T(8,128)(2,1)}, bf16[128,512]{1,0:T(8,128)(2,1)S(1)}, u32[]{:S(2)}, u32[]{:S(2)}) collective-permute-start(bf16[128,512]{1,0:T(8,128)(2,1)} %get-tuple-element.122), channel_id=1, source_target_pairs={{0,2},{1,3},{2,0},{3,1},{4,6},{5,7},{6,4},{7,5},{8,10},{9,11},{10,... | collective-permute-start | bytes 393224 | tf_op jit(solution)/shard_map/ppermute | solution.py:18
  7.4 1.7 collective-permute-start
  9.1 3.3 %fusion.15 = f32[256,64]{0,1:T(8,128)S(1)} fusion(bf16[256,7168]{1,0:T(8,128)(2,1)} %param.7, bf16[7168,64]{0,1:T(8,128)(2,1)S(1)} %copy-done), kind=kOutput, calls=%fused_computation.39 | convolution fusion | flops 234881024 | bytes 4653056 | tf_op jit(solution)/shard_map/dot_general | solution.py:263
  12.7 1.6 collective-permute-start.8
  15.1 0.8 collective-permute-done
  16.0 0.9 pad_maximum_fusion.refs_0_
  16.9 2.0 %collective-permute-start.7 = (bf16[256,512]{1,0:T(8,128)(2,1)S(1)}, bf16[256,512]{1,0:T(8,128)(2,1)S(1)}, u32[]{:S(2)}, u32[]{:S(2)}) collective-permute-start(bf16[256,512]{1,0:T(8,128)(2,1)S(1)} %pad_maximum_fusion.refs_0_), channel_id=1, source_target_pairs={{0,4},{4,0},{8,12},{12,8},{1,5},{5,1},{9,13},{13,9},{2,6},{6,2},{1... | collective-permute-start | bytes 786440 | tf_op jit(solution)/shard_map/ppermute | solution.py:28
  18.9 2.6 %collective-permute-start.4 = (bf16[256,512]{1,0:T(8,128)(2,1)S(1)}, bf16[256,512]{1,0:T(8,128)(2,1)S(1)}, u32[]{:S(2)}, u32[]{:S(2)}) collective-permute-start(bf16[256,512]{1,0:T(8,128)(2,1)S(1)} %pad_maximum_fusion.refs_0_), channel_id=1, source_target_pairs={{0,8},{4,12},{8,0},{12,4},{1,9},{5,13},{9,1},{13,5},{2,10},{6,14},... | collective-permute-start | bytes 786440 | tf_op jit(solution)/shard_map/ppermute | solution.py:28
  21.5 0.7 fusion.14
  22.3 11.0 %collective-permute-done.4.refs_2_ = bf16[256,512]{1,0:T(8,128)(2,1)S(1)} collective-permute-done((bf16[256,512]{1,0:T(8,128)(2,1)S(1)}, bf16[256,512]{1,0:T(8,128)(2,1)S(1)}, u32[]{:S(2)}, u32[]{:S(2)}) %collective-permute-start.4) | collective-permute-done | bytes 262176 | tf_op jit(solution)/shard_map/ppermute | solution.py:28
  33.6 2.7 %collective-permute-start.5 = (bf16[256,512]{1,0:T(8,128)(2,1)S(1)}, bf16[256,512]{1,0:T(8,128)(2,1)S(1)}, u32[]{:S(2)}, u32[]{:S(2)}) collective-permute-start(bf16[256,512]{1,0:T(8,128)(2,1)S(1)} %constant_dynamic-update-slice_fusion.refs_0_), channel_id=1, source_target_pairs={{0,4},{4,0},{8,12},{12,8},{1,5},{5,1},{9,13},{13,9},{2,6},{6,2},{1... | collective-permute-start | bytes 786440 | tf_op jit(solution)/shard_map/ppermute | solution.py:28
  37.0 1.3 collective-permute-start.11
  38.3 9.0 %collective-permute-done.6.refs_2_ = bf16[256,512]{1,0:T(8,128)(2,1)S(1)} collective-permute-done((bf16[256,512]{1,0:T(8,128)(2,1)S(1)}, bf16[256,512]{1,0:T(8,128)(2,1)S(1)}, u32[]{:S(2)}, u32[]{:S(2)}) %collective-permute-start.6) | collective-permute-done | bytes 262176 | tf_op jit(solution)/shard_map/ppermute | solution.py:28
  47.4 3.0 %collective-permute-done.11.refs_4_ = bf16[256,512]{1,0:T(8,128)(2,1)S(1)} collective-permute-done((bf16[256,512]{1,0:T(8,128)(2,1)S(1)}, bf16[256,512]{1,0:T(8,128)(2,1)S(1)}, u32[]{:S(2)}, u32[]{:S(2)}) %collective-permute-start.11) | collective-permute-done | bytes 262176 | tf_op jit(solution)/shard_map/ppermute | solution.py:28
  50.4 6.9 %terms.5 = (bf16[64,3584]{1,0:T(8,128)(2,1)S(1)}, bf16[64,3584]{1,0:T(8,128)(2,1)S(1)}, bf16[128,3584]{1,0:T(8,128)(2,1)S(1)}) custom-call(s32[1]{0:T(128)} %bitcast.place_ref, bf16[256,512]{1,0:T(8,128)(2,1)S(1)} %pad_maximum_fusion.refs_0_, bf16[256,512]{1,0:T(8,128)(2,1)S(1)} %collective-permute-done.7.refs_1_, ...), custom_call_target="tpu_custom_call" | custom-call | flops 15032385536 | bytes 1000 | tf_op jit(solution)/shard_map/terms/pallas_call | solution.py:127
  57.9 1.3 collective-permute-done.12.first_ref
  60.4 2.8 %collective-permute-start.17 = (bf16[256,512]{1,0:T(8,128)(2,1)S(1)}, bf16[256,512]{1,0:T(8,128)(2,1)S(1)}, u32[]{:S(2)}, u32[]{:S(2)}) collective-permute-start(bf16[256,512]{1,0:T(8,128)(2,1)S(1)} %collective-permute-done.9.refs_5_), channel_id=1, source_target_pairs={{0,8},{4,12},{8,0},{12,4},{1,9},{5,13},{9,1},{13,5},{2,10},{6,14},... | collective-permute-start | bytes 786440 | tf_op jit(solution)/shard_map/ppermute | solution.py:28
  63.2 1.9 %collective-permute-start.16 = (bf16[256,512]{1,0:T(8,128)(2,1)S(1)}, bf16[256,512]{1,0:T(8,128)(2,1)S(1)}, u32[]{:S(2)}, u32[]{:S(2)}) collective-permute-start(bf16[256,512]{1,0:T(8,128)(2,1)S(1)} %collective-permute-done.9.refs_5_), channel_id=1, source_target_pairs={{0,4},{4,0},{8,12},{12,8},{1,5},{5,1},{9,13},{13,9},{2,6},{6,2},{1... | collective-permute-start | bytes 786440 | tf_op jit(solution)/shard_map/ppermute | solution.py:28
  65.2 2.2 %collective-permute-start.23 = (bf16[128,3584]{1,0:T(8,128)(2,1)S(1)}, bf16[128,3584]{1,0:T(8,128)(2,1)}, u32[]{:S(2)}, u32[]{:S(2)}) collective-permute-start(bf16[128,3584]{1,0:T(8,128)(2,1)S(1)} %pair.4), channel_id=1, source_target_pairs={{0,2},{1,3},{2,0},{3,1},{4,6},{5,7},{6,4},{7,5},{8,10},{9,11},{10,... | collective-permute-start | bytes 2752520 | tf_op jit(solution)/shard_map/ppermute | solution.py:18
  68.1 1.3 collective-permute-start.15
  69.4 0.9 copy-done.40
  70.3 0.9 copy-done.42
  71.3 7.5 %terms.6 = (bf16[64,3584]{1,0:T(8,128)(2,1)}, bf16[64,3584]{1,0:T(8,128)(2,1)}, bf16[128,3584]{1,0:T(8,128)(2,1)S(1)}) custom-call(s32[1]{0:T(128)} %bitcast.place_ref, bf16[256,512]{1,0:T(8,128)(2,1)S(1)} %pad_maximum_fusion.refs_0_, bf16[256,512]{1,0:T(8,128)(2,1)S(1)} %collective-permute-done.7.refs_1_, ...), custom_call_target="tpu_custom_call" | custom-call | flops 15032385536 | bytes 1000 | tf_op jit(solution)/shard_map/terms/pallas_call | solution.py:127
  78.8 0.7 copy-done.27
  79.4 1.8 collective-permute-done.15.refs_4_
  81.3 0.7 copy-done.30
  82.0 0.7 copy-done.24
  83.2 3.2 %collective-permute-start.22 = (f32[256,128]{0,1:T(8,128)S(1)}, f32[256,128]{0,1:T(8,128)S(1)}, u32[]{:S(2)}, u32[]{:S(2)}) collective-permute-start(f32[256,128]{0,1:T(8,128)S(1)} %copy-done.44), channel_id=1, source_target_pairs={{0,8},{4,12},{8,0},{12,4},{1,9},{5,13},{9,1},{13,5},{2,10},{6,14},... | collective-permute-start | bytes 393224 | tf_op jit(solution)/shard_map/ppermute | solution.py:28
  86.5 1.1 copy.21
  87.7 5.4 %collective-permute-done.22 = f32[256,128]{0,1:T(8,128)S(1)} collective-permute-done((f32[256,128]{0,1:T(8,128)S(1)}, f32[256,128]{0,1:T(8,128)S(1)}, u32[]{:S(2)}, u32[]{:S(2)}) %collective-permute-start.22) | collective-permute-done | bytes 131104 | tf_op jit(solution)/shard_map/ppermute | solution.py:28
  93.1 0.8 copy-done.2
  93.9 1.0 copy-done.3
  95.5 2.9 %collective-permute-start.20 = (bf16[256,512]{1,0:T(8,128)(2,1)S(1)}, bf16[256,512]{1,0:T(8,128)(2,1)}, u32[]{:S(2)}, u32[]{:S(2)}) collective-permute-start(bf16[256,512]{1,0:T(8,128)(2,1)S(1)} %bitcast.39), channel_id=1, source_target_pairs={{0,4},{4,0},{8,12},{12,8},{1,5},{5,1},{9,13},{13,9},{2,6},{6,2},{1... | collective-permute-start | bytes 786440 | tf_op jit(solution)/shard_map/ppermute | solution.py:28
  98.4 2.2 %collective-permute-start.30 = (bf16[128,3584]{1,0:T(8,128)(2,1)S(1)}, bf16[128,3584]{1,0:T(8,128)(2,1)}, u32[]{:S(2)}, u32[]{:S(2)}) collective-permute-start(bf16[128,3584]{1,0:T(8,128)(2,1)S(1)} %pair.5), channel_id=1, source_target_pairs={{0,2},{1,3},{2,0},{3,1},{4,6},{5,7},{6,4},{7,5},{8,10},{9,11},{10,... | collective-permute-start | bytes 2752520 | tf_op jit(solution)/shard_map/ppermute | solution.py:18
  101.3 1.3 collective-permute-start.25
  103.2 0.7 copy-done.33
  103.9 11.1 %collective-permute-done.25.refs_9_ = bf16[256,512]{1,0:T(8,128)(2,1)S(1)} collective-permute-done((bf16[256,512]{1,0:T(8,128)(2,1)}, bf16[256,512]{1,0:T(8,128)(2,1)S(1)}, u32[]{:S(2)}, u32[]{:S(2)}) %collective-permute-start.25) | collective-permute-done | bytes 262176 | tf_op jit(solution)/shard_map/ppermute | solution.py:28
  115.0 0.7 copy-done.36
  115.7 0.9 copy-done.5
  116.7 0.9 copy-done.11
  117.6 0.9 copy-done.14
  118.6 0.9 copy-done.17
  119.5 0.9 copy-done.20
  120.5 0.9 copy-done.25
  121.4 0.9 copy-done.28
  122.4 0.9 copy-done.31
  123.3 0.9 copy-done.34
  124.3 0.9 copy-done.37
  125.2 11.5 %terms.7 = (bf16[64,3584]{1,0:T(8,128)(2,1)}, bf16[64,3584]{1,0:T(8,128)(2,1)S(1)}, bf16[128,3584]{1,0:T(8,128)(2,1)S(1)}, bf16[64,3584]{1,0:T(8,128)(2,1)S(1)},...) custom-call(s32[1]{0:T(128)} %bitcast.place_ref, ...), custom_call_target="tpu_custom_call" | custom-call | flops 30064771072 | bytes 1000 | tf_op jit(solution)/shard_map/terms/pallas_call | solution.py:127
  136.8 0.8 copy-done.9
  138.2 1.8 collective-permute-start.37
  141.3 1.8 collective-permute-start.38
  143.1 0.9 collective-permute-done.36
  145.1 0.9 select_select_fusion.3
  146.1 2.7 %fusion.4 = f32[1024,1024]{1,0:T(8,128)} fusion(bf16[16,4224]{1,0:T(8,128)(2,1)S(1)} %pad_maximum_fusion.1, s32[]{:T(128)S(6)} %select_n.121, s32[]{:T(128)S(6)} %select_n.122), kind=kOutput, calls=%fused_computation.19 | convolution fusion | flops 33554432 | bytes 4259848 | tf_op jit(solution)/shard_map/dot_general | solution.py:252
  148.9 0.9 fusion.6
  150.4 1.3 collective-permute-start.29
  151.9 11.1 %terms.8 = (bf16[64,3584]{1,0:T(8,128)(2,1)S(1)}, bf16[64,3584]{1,0:T(8,128)(2,1)S(1)}, bf16[128,3584]{1,0:T(8,128)(2,1)S(1)}, bf16[64,3584]{1,0:T(8,128)(2,1)S(...) custom-call(s32[1]{0:T(128)} %bitcast.place_ref, ...), custom_call_target="tpu_custom_call" | custom-call | flops 30064771072 | bytes 1000 | tf_op jit(solution)/shard_map/terms/pallas_call | solution.py:127
  163.6 1.3 collective-permute-done.40.second_ref
  167.2 0.9 collective-permute-start.45
  169.9 19.9 %terms.9.own_ref = bf16[256,7168]{1,0:T(8,128)(2,1)} custom-call(s32[1]{0:T(128)} %bitcast.place_ref, bf16[256,512]{1,0:T(8,128)(2,1)S(1)} %bitcast.41, bf16[256,512]{1,0:T(8,128)(2,1)} %collective-permute-done.20.refs_1_, bf16[256,512]{1,0:T(8,128)(2,1)S(1)} %copy-done.23, bf16[256,512]{1,0:T(8,128)(2,1)S(1)} %collective-permute-done.28.refs_3_, ...), custom_call_target="tpu_custom_call" | custom-call | flops 30064771072 | bytes 1000 | tf_op jit(solution)/shard_map/terms/pallas_call | solution.py:127
  189.8 2.1 %finish.1 = bf16[256,7168]{1,0:T(8,128)(2,1)} custom-call(bf16[256,7168]{1,0:T(8,128)(2,1)} %terms.9.own_ref, bf16[128,3584]{1,0:T(8,128)(2,1)S(1)} %collective-permute-done.45.other_ref), custom_call_target="tpu_custom_call", output_to_operand_aliasing={{}: (0, {})} | custom-call | flops 1000 | bytes 1000 | tf_op jit(solution)/shard_map/finish/pallas_call | solution.py:197
  (164 shorter events, 16.5 us)
Async XLA Ops:
  3.6 11.4 %collective-permute-start.1 = (bf16[128,512]{1,0:T(8,128)(2,1)}, bf16[128,512]{1,0:T(8,128)(2,1)S(1)}, u32[]{:S(2)}, u32[]{:S(2)}) collective-permute-start(bf16[128,512]{1,0:T(8,128)(2,1)} %get-tuple-element.122), channel_id=1, source_target_pairs={{0,2},{1,3},{2,0},{3,1},{4,6},{5,7},{6,4},{7,5},{8,10},{9,11},{10,... | collective-permute-start | bytes 393224 | tf_op jit(solution)/shard_map/ppermute | solution.py:18
  7.4 11.5 %collective-permute-start.2 = (bf16[128,512]{1,0:T(8,128)(2,1)S(1)}, bf16[128,512]{1,0:T(8,128)(2,1)S(1)}, u32[]{:S(2)}, u32[]{:S(2)}) collective-permute-start(bf16[128,512]{1,0:T(8,128)(2,1)S(1)} %get-tuple-element.123), channel_id=1, source_target_pairs={{0,3},{1,2},{2,1},{3,0},{4,7},{5,6},{6,5},{7,4},{8,11},{9,10},{10,... | collective-permute-start | bytes 393224 | tf_op jit(solution)/shard_map/ppermute | solution.py:18
  7.4 8.6 %collective-permute-start = (bf16[128,512]{1,0:T(8,128)(2,1)}, bf16[128,512]{1,0:T(8,128)(2,1)}, u32[]{:S(2)}, u32[]{:S(2)}) collective-permute-start(bf16[128,512]{1,0:T(8,128)(2,1)} %get-tuple-element.124), channel_id=1, source_target_pairs={{0,3},{1,2},{2,1},{3,0},{4,7},{5,6},{6,5},{7,4},{8,11},{9,10},{10,... | collective-permute-start | bytes 393224 | tf_op jit(solution)/shard_map/ppermute | solution.py:18
  12.7 8.8 %collective-permute-start.8 = (f32[256,128]{0,1:T(8,128)S(1)}, f32[256,128]{0,1:T(8,128)S(1)}, u32[]{:S(2)}, u32[]{:S(2)}) collective-permute-start(f32[256,128]{0,1:T(8,128)S(1)} %pad_maximum_fusion.2), channel_id=1, source_target_pairs={{0,4},{4,0},{8,12},{12,8},{1,5},{5,1},{9,13},{13,9},{2,6},{6,2},{1... | collective-permute-start | bytes 393224 | tf_op jit(solution)/shard_map/ppermute | solution.py:28
  14.4 7.1 %collective-permute-start.3 = (bf16[128,512]{1,0:T(8,128)(2,1)}, bf16[128,512]{1,0:T(8,128)(2,1)S(1)}, u32[]{:S(2)}, u32[]{:S(2)}) collective-permute-start(bf16[128,512]{1,0:T(8,128)(2,1)} %get-tuple-element.121), channel_id=1, source_target_pairs={{0,2},{1,3},{2,0},{3,1},{4,6},{5,7},{6,4},{7,5},{8,10},{9,11},{10,... | collective-permute-start | bytes 393224 | tf_op jit(solution)/shard_map/ppermute | solution.py:18
  15.1 21.3 %collective-permute-start.9 = (bf16[256,512]{1,0:T(8,128)(2,1)S(1)}, bf16[256,512]{1,0:T(8,128)(2,1)S(1)}, u32[]{:S(2)}, u32[]{:S(2)}) collective-permute-start(bf16[256,512]{1,0:T(8,128)(2,1)S(1)} %bitcast.45), channel_id=1, source_target_pairs={{0,1},{1,0},{2,3},{3,2},{4,5},{5,4},{6,7},{7,6},{8,9},{9,8},{10,11... | collective-permute-start | bytes 786440 | tf_op jit(solution)/shard_map/ppermute | solution.py:18
  16.9 30.4 %collective-permute-start.7 = (bf16[256,512]{1,0:T(8,128)(2,1)S(1)}, bf16[256,512]{1,0:T(8,128)(2,1)S(1)}, u32[]{:S(2)}, u32[]{:S(2)}) collective-permute-start(bf16[256,512]{1,0:T(8,128)(2,1)S(1)} %pad_maximum_fusion.refs_0_), channel_id=1, source_target_pairs={{0,4},{4,0},{8,12},{12,8},{1,5},{5,1},{9,13},{13,9},{2,6},{6,2},{1... | collective-permute-start | bytes 786440 | tf_op jit(solution)/shard_map/ppermute | solution.py:28
  18.9 14.4 %collective-permute-start.4 = (bf16[256,512]{1,0:T(8,128)(2,1)S(1)}, bf16[256,512]{1,0:T(8,128)(2,1)S(1)}, u32[]{:S(2)}, u32[]{:S(2)}) collective-permute-start(bf16[256,512]{1,0:T(8,128)(2,1)S(1)} %pad_maximum_fusion.refs_0_), channel_id=1, source_target_pairs={{0,8},{4,12},{8,0},{12,4},{1,9},{5,13},{9,1},{13,5},{2,10},{6,14},... | collective-permute-start | bytes 786440 | tf_op jit(solution)/shard_map/ppermute | solution.py:28
  21.5 45.8 %copy-start.4 = (bf16[256,512]{1,0:T(8,128)(2,1)}, bf16[256,512]{1,0:T(8,128)(2,1)S(1)}, u32[]{:S(2)}) copy-start(bf16[256,512]{1,0:T(8,128)(2,1)S(1)} %constant_dynamic-update-slice_fusion.refs_0_) | copy-start | bytes 786436
  33.3 14.0 %collective-permute-start.6 = (bf16[256,512]{1,0:T(8,128)(2,1)S(1)}, bf16[256,512]{1,0:T(8,128)(2,1)S(1)}, u32[]{:S(2)}, u32[]{:S(2)}) collective-permute-start(bf16[256,512]{1,0:T(8,128)(2,1)S(1)} %constant_dynamic-update-slice_fusion.refs_0_), channel_id=1, source_target_pairs={{0,8},{4,12},{8,0},{12,4},{1,9},{5,13},{9,1},{13,5},{2,10},{6,14},... | collective-permute-start | bytes 786440 | tf_op jit(solution)/shard_map/ppermute | solution.py:28
  33.6 13.7 %collective-permute-start.5 = (bf16[256,512]{1,0:T(8,128)(2,1)S(1)}, bf16[256,512]{1,0:T(8,128)(2,1)S(1)}, u32[]{:S(2)}, u32[]{:S(2)}) collective-permute-start(bf16[256,512]{1,0:T(8,128)(2,1)S(1)} %constant_dynamic-update-slice_fusion.refs_0_), channel_id=1, source_target_pairs={{0,4},{4,0},{8,12},{12,8},{1,5},{5,1},{9,13},{13,9},{2,6},{6,2},{1... | collective-permute-start | bytes 786440 | tf_op jit(solution)/shard_map/ppermute | solution.py:28
  36.4 26.9 %copy-start.10 = (bf16[256,512]{1,0:T(8,128)(2,1)}, bf16[256,512]{1,0:T(8,128)(2,1)S(1)}, u32[]{:S(2)}) copy-start(bf16[256,512]{1,0:T(8,128)(2,1)S(1)} %collective-permute-done.9.refs_5_) | copy-start | bytes 786436
  36.4 11.0 %collective-permute-start.10 = (bf16[256,512]{1,0:T(8,128)(2,1)S(1)}, bf16[256,512]{1,0:T(8,128)(2,1)S(1)}, u32[]{:S(2)}, u32[]{:S(2)}) collective-permute-start(bf16[256,512]{1,0:T(8,128)(2,1)S(1)} %pad_maximum_fusion.refs_0_), channel_id=1, source_target_pairs={{4,8},{8,4},{5,9},{9,5},{6,10},{10,6},{7,11},{11,7},{20,24},{24,20... | collective-permute-start | bytes 786440 | tf_op jit(solution)/shard_map/ppermute | solution.py:28
  37.0 13.3 %collective-permute-start.11 = (bf16[256,512]{1,0:T(8,128)(2,1)S(1)}, bf16[256,512]{1,0:T(8,128)(2,1)S(1)}, u32[]{:S(2)}, u32[]{:S(2)}) collective-permute-start(bf16[256,512]{1,0:T(8,128)(2,1)S(1)} %collective-permute-done.4.refs_2_), channel_id=1, source_target_pairs={{4,0},{8,12},{5,1},{9,13},{6,2},{10,14},{7,3},{11,15},{20,16},{24,... | collective-permute-start | bytes 786440 | tf_op jit(solution)/shard_map/ppermute | solution.py:28
  47.3 20.7 %copy-start.13 = (bf16[256,512]{1,0:T(8,128)(2,1)}, bf16[256,512]{1,0:T(8,128)(2,1)S(1)}, u32[]{:S(2)}) copy-start(bf16[256,512]{1,0:T(8,128)(2,1)S(1)} %collective-permute-done.6.refs_2_) | copy-start | bytes 786436
  47.3 10.0 %copy-start.16 = (bf16[256,512]{1,0:T(8,128)(2,1)}, bf16[256,512]{1,0:T(8,128)(2,1)S(1)}, u32[]{:S(2)}) copy-start(bf16[256,512]{1,0:T(8,128)(2,1)S(1)} %collective-permute-done.5.refs_1_) | copy-start | bytes 786436
  57.3 1.9 collective-permute-start.12
  57.4 2.5 %collective-permute-start.13 = (bf16[64,3584]{1,0:T(8,128)(2,1)S(1)}, bf16[64,3584]{1,0:T(8,128)(2,1)S(1)}, u32[]{:S(2)}, u32[]{:S(2)}) collective-permute-start(bf16[64,3584]{1,0:T(8,128)(2,1)S(1)} %get-tuple-element.67), channel_id=1, source_target_pairs={{0,1},{1,0},{2,3},{3,2},{4,5},{5,4},{6,7},{7,6},{8,9},{9,8},{10,11... | collective-permute-start | bytes 1376264 | tf_op jit(solution)/shard_map/ppermute | solution.py:18
  59.9 23.4 %copy-start.44 = (f32[256,128]{0,1:T(8,128)S(1)}, f32[256,128]{0,1:T(8,128)}, u32[]{:S(2)}) copy-start(f32[256,128]{0,1:T(8,128)} %fusion.14) | copy-start | bytes 393220
  59.9 26.6 %copy-start.46 = (s32[1,256]{1,0:T(1,128)S(1)}, s32[1,256]{1,0:T(1,128)}, u32[]{:S(2)}) copy-start(s32[1,256]{1,0:T(1,128)} %param.12) | copy-start | bytes 3076
  59.9 26.6 %copy-start.47 = (s32[4]{0:T(128)S(1)}, s32[4]{0:T(128)}, u32[]{:S(2)}) copy-start(s32[4]{0:T(128)} %param.13) | copy-start | bytes 52
  60.4 21.6 %collective-permute-start.17 = (bf16[256,512]{1,0:T(8,128)(2,1)S(1)}, bf16[256,512]{1,0:T(8,128)(2,1)S(1)}, u32[]{:S(2)}, u32[]{:S(2)}) collective-permute-start(bf16[256,512]{1,0:T(8,128)(2,1)S(1)} %collective-permute-done.9.refs_5_), channel_id=1, source_target_pairs={{0,8},{4,12},{8,0},{12,4},{1,9},{5,13},{9,1},{13,5},{2,10},{6,14},... | collective-permute-start | bytes 786440 | tf_op jit(solution)/shard_map/ppermute | solution.py:28
  63.2 18.7 %collective-permute-start.16 = (bf16[256,512]{1,0:T(8,128)(2,1)S(1)}, bf16[256,512]{1,0:T(8,128)(2,1)S(1)}, u32[]{:S(2)}, u32[]{:S(2)}) collective-permute-start(bf16[256,512]{1,0:T(8,128)(2,1)S(1)} %collective-permute-done.9.refs_5_), channel_id=1, source_target_pairs={{0,4},{4,0},{8,12},{12,8},{1,5},{5,1},{9,13},{13,9},{2,6},{6,2},{1... | collective-permute-start | bytes 786440 | tf_op jit(solution)/shard_map/ppermute | solution.py:28
  65.2 36.1 %collective-permute-start.23 = (bf16[128,3584]{1,0:T(8,128)(2,1)S(1)}, bf16[128,3584]{1,0:T(8,128)(2,1)}, u32[]{:S(2)}, u32[]{:S(2)}) collective-permute-start(bf16[128,3584]{1,0:T(8,128)(2,1)S(1)} %pair.4), channel_id=1, source_target_pairs={{0,2},{1,3},{2,0},{3,1},{4,6},{5,7},{6,4},{7,5},{8,10},{9,11},{10,... | collective-permute-start | bytes 2752520 | tf_op jit(solution)/shard_map/ppermute | solution.py:18
  67.4 11.4 %collective-permute-start.14 = (bf16[256,512]{1,0:T(8,128)(2,1)S(1)}, bf16[256,512]{1,0:T(8,128)(2,1)S(1)}, u32[]{:S(2)}, u32[]{:S(2)}) collective-permute-start(bf16[256,512]{1,0:T(8,128)(2,1)S(1)} %constant_dynamic-update-slice_fusion.refs_0_), channel_id=1, source_target_pairs={{4,8},{8,4},{5,9},{9,5},{6,10},{10,6},{7,11},{11,7},{20,24},{24,20... | collective-permute-start | bytes 786440 | tf_op jit(solution)/shard_map/ppermute | solution.py:28
  68.1 13.2 %collective-permute-start.15 = (bf16[256,512]{1,0:T(8,128)(2,1)S(1)}, bf16[256,512]{1,0:T(8,128)(2,1)S(1)}, u32[]{:S(2)}, u32[]{:S(2)}) collective-permute-start(bf16[256,512]{1,0:T(8,128)(2,1)S(1)} %collective-permute-done.6.refs_2_), channel_id=1, source_target_pairs={{4,0},{8,12},{5,1},{9,13},{6,2},{10,14},{7,3},{11,15},{20,16},{24,... | collective-permute-start | bytes 786440 | tf_op jit(solution)/shard_map/ppermute | solution.py:28
  82.7 10.3 %collective-permute-start.19 = (bf16[64,3584]{1,0:T(8,128)(2,1)}, bf16[64,3584]{1,0:T(8,128)(2,1)S(1)}, u32[]{:S(2)}, u32[]{:S(2)}) collective-permute-start(bf16[64,3584]{1,0:T(8,128)(2,1)} %get-tuple-element.76), channel_id=1, source_target_pairs={{0,1},{1,0},{2,3},{3,2},{4,5},{5,4},{6,7},{7,6},{8,9},{9,8},{10,11... | collective-permute-start | bytes 1376264 | tf_op jit(solution)/shard_map/ppermute | solution.py:18
  82.9 10.2 %collective-permute-start.18 = (bf16[64,3584]{1,0:T(8,128)(2,1)}, bf16[64,3584]{1,0:T(8,128)(2,1)S(1)}, u32[]{:S(2)}, u32[]{:S(2)}) collective-permute-start(bf16[64,3584]{1,0:T(8,128)(2,1)} %get-tuple-element.74), channel_id=1, source_target_pairs={{0,1},{1,0},{2,3},{3,2},{4,5},{5,4},{6,7},{7,6},{8,9},{9,8},{10,11... | collective-permute-start | bytes 1376264 | tf_op jit(solution)/shard_map/ppermute | solution.py:18
  83.2 9.8 %collective-permute-start.22 = (f32[256,128]{0,1:T(8,128)S(1)}, f32[256,128]{0,1:T(8,128)S(1)}, u32[]{:S(2)}, u32[]{:S(2)}) collective-permute-start(f32[256,128]{0,1:T(8,128)S(1)} %copy-done.44), channel_id=1, source_target_pairs={{0,8},{4,12},{8,0},{12,4},{1,9},{5,13},{9,1},{13,5},{2,10},{6,14},... | collective-permute-start | bytes 393224 | tf_op jit(solution)/shard_map/ppermute | solution.py:28
  95.4 41.3 %collective-permute-start.21 = (bf16[256,512]{1,0:T(8,128)(2,1)S(1)}, bf16[256,512]{1,0:T(8,128)(2,1)S(1)}, u32[]{:S(2)}, u32[]{:S(2)}) collective-permute-start(bf16[256,512]{1,0:T(8,128)(2,1)S(1)} %bitcast.38), channel_id=1, source_target_pairs={{0,8},{4,12},{8,0},{12,4},{1,9},{5,13},{9,1},{13,5},{2,10},{6,14},... | collective-permute-start | bytes 786440 | tf_op jit(solution)/shard_map/ppermute | solution.py:28
  95.5 41.3 %collective-permute-start.20 = (bf16[256,512]{1,0:T(8,128)(2,1)S(1)}, bf16[256,512]{1,0:T(8,128)(2,1)}, u32[]{:S(2)}, u32[]{:S(2)}) collective-permute-start(bf16[256,512]{1,0:T(8,128)(2,1)S(1)} %bitcast.39), channel_id=1, source_target_pairs={{0,4},{4,0},{8,12},{12,8},{1,5},{5,1},{9,13},{13,9},{2,6},{6,2},{1... | collective-permute-start | bytes 786440 | tf_op jit(solution)/shard_map/ppermute | solution.py:28
  98.4 45.6 %collective-permute-start.30 = (bf16[128,3584]{1,0:T(8,128)(2,1)S(1)}, bf16[128,3584]{1,0:T(8,128)(2,1)}, u32[]{:S(2)}, u32[]{:S(2)}) collective-permute-start(bf16[128,3584]{1,0:T(8,128)(2,1)S(1)} %pair.5), channel_id=1, source_target_pairs={{0,2},{1,3},{2,0},{3,1},{4,6},{5,7},{6,4},{7,5},{8,10},{9,11},{10,... | collective-permute-start | bytes 2752520 | tf_op jit(solution)/shard_map/ppermute | solution.py:18
  100.6 2.6 %collective-permute-start.24 = (bf16[256,512]{1,0:T(8,128)(2,1)}, bf16[256,512]{1,0:T(8,128)(2,1)S(1)}, u32[]{:S(2)}, u32[]{:S(2)}) collective-permute-start(bf16[256,512]{1,0:T(8,128)(2,1)} %copy-done.10), channel_id=1, source_target_pairs={{4,8},{8,4},{5,9},{9,5},{6,10},{10,6},{7,11},{11,7},{20,24},{24,20... | collective-permute-start | bytes 786440 | tf_op jit(solution)/shard_map/ppermute | solution.py:28
  101.3 13.7 %collective-permute-start.25 = (bf16[256,512]{1,0:T(8,128)(2,1)}, bf16[256,512]{1,0:T(8,128)(2,1)S(1)}, u32[]{:S(2)}, u32[]{:S(2)}) collective-permute-start(bf16[256,512]{1,0:T(8,128)(2,1)} %copy-done.19), channel_id=1, source_target_pairs={{4,0},{8,12},{5,1},{9,13},{6,2},{10,14},{7,3},{11,15},{20,16},{24,... | collective-permute-start | bytes 786440 | tf_op jit(solution)/shard_map/ppermute | solution.py:28
  137.6 2.9 %collective-permute-start.27 = (bf16[64,3584]{1,0:T(8,128)(2,1)S(1)}, bf16[64,3584]{1,0:T(8,128)(2,1)S(1)}, u32[]{:S(2)}, u32[]{:S(2)}) collective-permute-start(bf16[64,3584]{1,0:T(8,128)(2,1)S(1)} %get-tuple-element.88), channel_id=1, source_target_pairs={{0,1},{1,0},{2,3},{3,2},{4,5},{5,4},{6,7},{7,6},{8,9},{9,8},{10,11... | collective-permute-start | bytes 1376264 | tf_op jit(solution)/shard_map/ppermute | solution.py:18
  137.6 3.0 %collective-permute-start.26 = (bf16[64,3584]{1,0:T(8,128)(2,1)}, bf16[64,3584]{1,0:T(8,128)(2,1)S(1)}, u32[]{:S(2)}, u32[]{:S(2)}) collective-permute-start(bf16[64,3584]{1,0:T(8,128)(2,1)} %get-tuple-element.86), channel_id=1, source_target_pairs={{0,1},{1,0},{2,3},{3,2},{4,5},{5,4},{6,7},{7,6},{8,9},{9,8},{10,11... | collective-permute-start | bytes 1376264 | tf_op jit(solution)/shard_map/ppermute | solution.py:18
  138.2 4.9 %collective-permute-start.37 = (bf16[4,4224]{1,0:T(4,128)(2,1)S(1)}, bf16[4,4224]{1,0:T(4,128)(2,1)S(1)}, u32[]{:S(2)}, u32[]{:S(2)}) collective-permute-start(bf16[4,4224]{1,0:T(4,128)(2,1)S(1)} %pad_maximum_fusion.3), channel_id=1, source_target_pairs={{0,3},{1,2},{2,1},{3,0},{4,7},{5,6},{6,5},{7,4},{8,11},{9,10},{10,... | collective-permute-start | bytes 101384 | tf_op jit(solution)/shard_map/ppermute | solution.py:18
  140.0 4.0 %collective-permute-start.36 = (bf16[4,4224]{1,0:T(4,128)(2,1)S(1)}, bf16[4,4224]{1,0:T(4,128)(2,1)}, u32[]{:S(2)}, u32[]{:S(2)}) collective-permute-start(bf16[4,4224]{1,0:T(4,128)(2,1)S(1)} %pad_maximum_fusion.3), channel_id=1, source_target_pairs={{0,2},{1,3},{2,0},{3,1},{4,6},{5,7},{6,4},{7,5},{8,10},{9,11},{10,... | collective-permute-start | bytes 101384 | tf_op jit(solution)/shard_map/ppermute | solution.py:18
  140.5 3.6 %collective-permute-start.35 = (bf16[4,4224]{1,0:T(4,128)(2,1)S(1)}, bf16[4,4224]{1,0:T(4,128)(2,1)}, u32[]{:S(2)}, u32[]{:S(2)}) collective-permute-start(bf16[4,4224]{1,0:T(4,128)(2,1)S(1)} %pad_maximum_fusion.3), channel_id=1, source_target_pairs={{0,1},{1,0},{2,3},{3,2},{4,5},{5,4},{6,7},{7,6},{8,9},{9,8},{10,11... | collective-permute-start | bytes 101384 | tf_op jit(solution)/shard_map/ppermute | solution.py:18
  140.6 11.2 %copy-start.6 = (bf16[256,512]{1,0:T(8,128)(2,1)S(1)}, bf16[256,512]{1,0:T(8,128)(2,1)}, u32[]{:S(2)}) copy-start(bf16[256,512]{1,0:T(8,128)(2,1)} %copy-done.4) | copy-start | bytes 786436
  140.6 11.2 %copy-start.12 = (bf16[256,512]{1,0:T(8,128)(2,1)S(1)}, bf16[256,512]{1,0:T(8,128)(2,1)}, u32[]{:S(2)}) copy-start(bf16[256,512]{1,0:T(8,128)(2,1)} %copy-done.10) | copy-start | bytes 786436
  140.6 11.2 %copy-start.15 = (bf16[256,512]{1,0:T(8,128)(2,1)S(1)}, bf16[256,512]{1,0:T(8,128)(2,1)}, u32[]{:S(2)}) copy-start(bf16[256,512]{1,0:T(8,128)(2,1)} %copy-done.13) | copy-start | bytes 786436
  140.6 11.2 %copy-start.18 = (bf16[256,512]{1,0:T(8,128)(2,1)S(1)}, bf16[256,512]{1,0:T(8,128)(2,1)}, u32[]{:S(2)}) copy-start(bf16[256,512]{1,0:T(8,128)(2,1)} %copy-done.16) | copy-start | bytes 786436
  140.7 11.2 %copy-start.21 = (bf16[256,512]{1,0:T(8,128)(2,1)S(1)}, bf16[256,512]{1,0:T(8,128)(2,1)}, u32[]{:S(2)}) copy-start(bf16[256,512]{1,0:T(8,128)(2,1)} %copy-done.19) | copy-start | bytes 786436
  140.7 11.2 %copy-start.26 = (bf16[256,512]{1,0:T(8,128)(2,1)S(1)}, bf16[256,512]{1,0:T(8,128)(2,1)}, u32[]{:S(2)}) copy-start(bf16[256,512]{1,0:T(8,128)(2,1)} %copy-done.24) | copy-start | bytes 786436
  140.7 11.2 %copy-start.29 = (bf16[256,512]{1,0:T(8,128)(2,1)S(1)}, bf16[256,512]{1,0:T(8,128)(2,1)}, u32[]{:S(2)}) copy-start(bf16[256,512]{1,0:T(8,128)(2,1)} %copy-done.27) | copy-start | bytes 786436
  140.7 11.2 %copy-start.32 = (bf16[256,512]{1,0:T(8,128)(2,1)S(1)}, bf16[256,512]{1,0:T(8,128)(2,1)}, u32[]{:S(2)}) copy-start(bf16[256,512]{1,0:T(8,128)(2,1)} %copy-done.30) | copy-start | bytes 786436
  140.7 11.2 %copy-start.35 = (bf16[256,512]{1,0:T(8,128)(2,1)S(1)}, bf16[256,512]{1,0:T(8,128)(2,1)}, u32[]{:S(2)}) copy-start(bf16[256,512]{1,0:T(8,128)(2,1)} %copy-done.33) | copy-start | bytes 786436
  140.7 11.2 %copy-start.38 = (bf16[256,512]{1,0:T(8,128)(2,1)S(1)}, bf16[256,512]{1,0:T(8,128)(2,1)}, u32[]{:S(2)}) copy-start(bf16[256,512]{1,0:T(8,128)(2,1)} %copy-done.36) | copy-start | bytes 786436
  141.3 24.8 %collective-permute-start.38 = (bf16[128,3584]{1,0:T(8,128)(2,1)S(1)}, bf16[128,3584]{1,0:T(8,128)(2,1)S(1)}, u32[]{:S(2)}, u32[]{:S(2)}) collective-permute-start(bf16[128,3584]{1,0:T(8,128)(2,1)S(1)} %pair.6), channel_id=1, source_target_pairs={{0,2},{1,3},{2,0},{3,1},{4,6},{5,7},{6,4},{7,5},{8,10},{9,11},{10,... | collective-permute-start | bytes 2752520 | tf_op jit(solution)/shard_map/ppermute | solution.py:18
  144.0 5.7 %collective-permute-start.31 = (bf16[64,3584]{1,0:T(8,128)(2,1)}, bf16[64,3584]{1,0:T(8,128)(2,1)S(1)}, u32[]{:S(2)}, u32[]{:S(2)}) collective-permute-start(bf16[64,3584]{1,0:T(8,128)(2,1)} %copy-done.9), channel_id=1, source_target_pairs={{0,1},{1,0},{2,3},{3,2},{4,5},{5,4},{6,7},{7,6},{8,9},{9,8},{10,11... | collective-permute-start | bytes 1376264 | tf_op jit(solution)/shard_map/ppermute | solution.py:18
  144.0 6.4 %collective-permute-start.32 = (bf16[64,3584]{1,0:T(8,128)(2,1)}, bf16[64,3584]{1,0:T(8,128)(2,1)S(1)}, u32[]{:S(2)}, u32[]{:S(2)}) collective-permute-start(bf16[64,3584]{1,0:T(8,128)(2,1)} %copy-done.8), channel_id=1, source_target_pairs={{0,1},{1,0},{2,3},{3,2},{4,5},{5,4},{6,7},{7,6},{8,9},{9,8},{10,11... | collective-permute-start | bytes 1376264 | tf_op jit(solution)/shard_map/ppermute | solution.py:18
  144.5 7.2 %collective-permute-start.33 = (bf16[64,3584]{1,0:T(8,128)(2,1)}, bf16[64,3584]{1,0:T(8,128)(2,1)S(1)}, u32[]{:S(2)}, u32[]{:S(2)}) collective-permute-start(bf16[64,3584]{1,0:T(8,128)(2,1)} %copy-done.7), channel_id=1, source_target_pairs={{0,1},{1,0},{2,3},{3,2},{4,5},{5,4},{6,7},{7,6},{8,9},{9,8},{10,11... | collective-permute-start | bytes 1376264 | tf_op jit(solution)/shard_map/ppermute | solution.py:18
  144.6 7.1 %collective-permute-start.34 = (bf16[64,3584]{1,0:T(8,128)(2,1)S(1)}, bf16[64,3584]{1,0:T(8,128)(2,1)S(1)}, u32[]{:S(2)}, u32[]{:S(2)}) collective-permute-start(bf16[64,3584]{1,0:T(8,128)(2,1)S(1)} %get-tuple-element.98), channel_id=1, source_target_pairs={{0,1},{1,0},{2,3},{3,2},{4,5},{5,4},{6,7},{7,6},{8,9},{9,8},{10,11... | collective-permute-start | bytes 1376264 | tf_op jit(solution)/shard_map/ppermute | solution.py:18
  149.7 13.2 %collective-permute-start.28 = (bf16[256,512]{1,0:T(8,128)(2,1)S(1)}, bf16[256,512]{1,0:T(8,128)(2,1)S(1)}, u32[]{:S(2)}, u32[]{:S(2)}) collective-permute-start(bf16[256,512]{1,0:T(8,128)(2,1)S(1)} %bitcast.40), channel_id=1, source_target_pairs={{4,8},{8,4},{5,9},{9,5},{6,10},{10,6},{7,11},{11,7},{20,24},{24,20... | collective-permute-start | bytes 786440 | tf_op jit(solution)/shard_map/ppermute | solution.py:28
  150.4 12.5 %collective-permute-start.29 = (bf16[256,512]{1,0:T(8,128)(2,1)S(1)}, bf16[256,512]{1,0:T(8,128)(2,1)S(1)}, u32[]{:S(2)}, u32[]{:S(2)}) collective-permute-start(bf16[256,512]{1,0:T(8,128)(2,1)S(1)} %copy-done.23), channel_id=1, source_target_pairs={{4,0},{8,12},{5,1},{9,13},{6,2},{10,14},{7,3},{11,15},{20,16},{24,... | collective-permute-start | bytes 786440 | tf_op jit(solution)/shard_map/ppermute | solution.py:28
  163.0 1.9 collective-permute-start.40
  163.1 2.4 %collective-permute-start.39 = (bf16[64,3584]{1,0:T(8,128)(2,1)S(1)}, bf16[64,3584]{1,0:T(8,128)(2,1)S(1)}, u32[]{:S(2)}, u32[]{:S(2)}) collective-permute-start(bf16[64,3584]{1,0:T(8,128)(2,1)S(1)} %get-tuple-element.107), channel_id=1, source_target_pairs={{0,1},{1,0},{2,3},{3,2},{4,5},{5,4},{6,7},{7,6},{8,9},{9,8},{10,11... | collective-permute-start | bytes 1376264 | tf_op jit(solution)/shard_map/ppermute | solution.py:18
  166.1 2.0 %collective-permute-start.41 = (bf16[64,3584]{1,0:T(8,128)(2,1)S(1)}, bf16[64,3584]{1,0:T(8,128)(2,1)S(1)}, u32[]{:S(2)}, u32[]{:S(2)}) collective-permute-start(bf16[64,3584]{1,0:T(8,128)(2,1)S(1)} %get-tuple-element.110), channel_id=1, source_target_pairs={{0,1},{1,0},{2,3},{3,2},{4,5},{5,4},{6,7},{7,6},{8,9},{9,8},{10,11... | collective-permute-start | bytes 1376264 | tf_op jit(solution)/shard_map/ppermute | solution.py:18
  166.3 2.3 %collective-permute-start.42 = (bf16[64,3584]{1,0:T(8,128)(2,1)S(1)}, bf16[64,3584]{1,0:T(8,128)(2,1)S(1)}, u32[]{:S(2)}, u32[]{:S(2)}) collective-permute-start(bf16[64,3584]{1,0:T(8,128)(2,1)S(1)} %get-tuple-element.112), channel_id=1, source_target_pairs={{0,1},{1,0},{2,3},{3,2},{4,5},{5,4},{6,7},{7,6},{8,9},{9,8},{10,11... | collective-permute-start | bytes 1376264 | tf_op jit(solution)/shard_map/ppermute | solution.py:18
  166.6 2.6 %collective-permute-start.43 = (bf16[64,3584]{1,0:T(8,128)(2,1)S(1)}, bf16[64,3584]{1,0:T(8,128)(2,1)S(1)}, u32[]{:S(2)}, u32[]{:S(2)}) collective-permute-start(bf16[64,3584]{1,0:T(8,128)(2,1)S(1)} %get-tuple-element.114), channel_id=1, source_target_pairs={{0,1},{1,0},{2,3},{3,2},{4,5},{5,4},{6,7},{7,6},{8,9},{9,8},{10,11... | collective-permute-start | bytes 1376264 | tf_op jit(solution)/shard_map/ppermute | solution.py:18
  166.8 3.1 %collective-permute-start.44 = (bf16[64,3584]{1,0:T(8,128)(2,1)S(1)}, bf16[64,3584]{1,0:T(8,128)(2,1)S(1)}, u32[]{:S(2)}, u32[]{:S(2)}) collective-permute-start(bf16[64,3584]{1,0:T(8,128)(2,1)S(1)} %get-tuple-element.116), channel_id=1, source_target_pairs={{0,1},{1,0},{2,3},{3,2},{4,5},{5,4},{6,7},{7,6},{8,9},{9,8},{10,11... | collective-permute-start | bytes 1376264 | tf_op jit(solution)/shard_map/ppermute | solution.py:18
  167.2 22.7 %collective-permute-start.45 = (bf16[128,3584]{1,0:T(8,128)(2,1)S(1)}, bf16[128,3584]{1,0:T(8,128)(2,1)S(1)}, u32[]{:S(2)}, u32[]{:S(2)}) collective-permute-start(bf16[128,3584]{1,0:T(8,128)(2,1)S(1)} %pair.7), channel_id=1, source_target_pairs={{0,2},{1,3},{2,0},{3,1},{4,6},{5,7},{6,4},{7,5},{8,10},{9,11},{10,... | collective-permute-start | bytes 2752520 | tf_op jit(solution)/shard_map/ppermute | solution.py:18
  169.9 22.0 %copy-start.1 = (bf16[7168,64]{0,1:T(8,128)(2,1)S(1)}, bf16[7168,64]{0,1:T(8,128)(2,1)}, u32[]{:S(2)}) copy-start(bf16[7168,64]{0,1:T(8,128)(2,1)} %param.10) | copy-start | bytes 2752516
  (30 other events, 84.9 us)

commit v7 on v6

--- a/solution.py
+++ b/solution.py
@@ -95,11 +95,12 @@
     def add_part(part):
         here = [(ref, at) for ref, (at, of) in zip(add_refs, adds) if of == part]
         cut = min(ref.shape[0] for ref, _ in here)
+        cols = pl.ds(pl.multiple_of((j - part * per_part) * tile, tile), tile)
         for row in range(0, feats.shape[0], cut):
             total = terms[row : row + cut]
             for ref, at in here:
                 if at <= row < at + ref.shape[0]:
-                    total = total + ref[row - at : row - at + cut].astype(f32)
+                    total = total + ref[row - at : row - at + cut, cols].astype(f32)
             outs[0][row : row + cut] = total.astype(bf16)
 
     for part in sorted({of for _, of in adds}):
@@ -117,12 +118,6 @@
     slots = min(4, cols // tile)
     blocks = [block for group in groups for block in group]
     per_part = adds[0][0].shape[1] // tile if adds else 1
-
-    def add_spec(value, part):
-        return pl.BlockSpec(
-            (value.shape[0], tile),
-            lambda j, place: (0, jnp.clip(j - part * per_part, 0, per_part - 1)),
-        )
 
     return pl.pallas_call(
         functools.partial(
@@ -137,8 +132,9 @@
         grid_spec=pltpu.PrefetchScalarGridSpec(
             num_scalar_prefetch=1,
             grid=(cols // tile,),
-            in_specs=[pl.BlockSpec(memory_space=pl.ANY)] * (len(blocks) + 1)
-            + [add_spec(value, part) for value, _, part in adds],
+            in_specs=[pl.BlockSpec(memory_space=pl.ANY)] * len(blocks)
+            + [pl.BlockSpec(memory_space=pltpu.HBM)]
+            + [pl.BlockSpec(memory_space=pltpu.VMEM)] * len(adds),
             out_specs=[pl.BlockSpec((tall, tile), lambda j, place: (0, j)) for tall in outs],
             scratch_shapes=[
                 pltpu.VMEM((rows, size * width), bf16),
@@ -147,7 +143,7 @@
                 pltpu.SemaphoreType.DMA((slots,)),
             ],
         ),
-        compiler_params=pltpu.CompilerParams(vmem_limit_bytes=40 << 20),
+        compiler_params=pltpu.CompilerParams(vmem_limit_bytes=24 << 20),
         cost_estimate=pl.CostEstimate(
             flops=8 * rows * size * width * cols, bytes_accessed=1000, transcendentals=0
         ),
@@ -330,22 +326,23 @@
 
     beside = spread_last(beside, pair1)
     own = spread_first(after(own, pair1))
-    acts_low, grads_low = jnp.split(after(low, pair1, sum0), 2, axis=1)
+    first, last, kept, *near0 = far_terms([later, beside], 0, pair1, sum0)
+    pair2, sum2 = pair_sum(first, last, kept, *own)
+
+    own = spread_last(own, pair2)
+    near0 = [swap(after(term, sum1, pair2), 1) for term in near0]
+    acts_low, grads_low = jnp.split(after(low, pair2, sum1), 2, axis=1)
     example_grad = example_gradients(
         acts_low, grads_low, token_example[0], example_group.shape[0]
     )
     gathered = gather_examples(example_grad, example_group)
-    first, last, kept, *near0 = far_terms([later, beside], 0, pair1, example_grad)
-    pair2, sum2 = pair_sum(first, last, kept, *own)
-
-    own = spread_last(own, pair2)
-    near0 = [swap(after(term, sum1, pair2), 1) for term in near0]
-    every = order_examples(after(gathered, sum1, pair2))
+    first, last, kept, *near1 = far_terms([later, beside], 1, example_grad, *near0)
+    pair3, sum3 = pair_sum(first, last, kept, *own)
+
+    near1 = [swap(after(term, sum2, pair3), 1) for term in near1]
+    every = order_examples(after(gathered, sum2, pair3))
     fisher, group_grad = fisher_and_groups(every, example_grad.shape[1])
-    first, last, kept, *near1 = far_terms([later, beside], 1, fisher, group_grad, *near0)
-    pair3, sum3 = pair_sum(first, last, kept, *own)
-
-    near1 = [swap(after(term, sum2, pair3), 1) for term in near1]
+    own = [after(own[0], fisher, group_grad)] + own[1:]
     adds = [(term, row * (rows // 2), 0) for row, term in enumerate(near0)]
     adds += [(term, row * (rows // 2), 1) for row, term in enumerate(near1)]
     adds += [(sum0, 0, 0), (sum1, 0, 1), (sum2, rows, 0)]

time: 194 us -> 195 us (level)
  local copies, waits for them, and re-layouts: 22.8 us -> 28.7 us
  Pallas kernels: 61 us -> 58.5 us
    unnamed x97 -> x105, local copies, waits for them, and re-layouts: 17.6 us -> 24.9 us
    ppermute x18, starting transfers between devices: 28.1 us -> 32.4 us  [across(): return lax.ppermute(value, 'tensor', pairs)]
    ppermute x28, starting transfers between devices: 19 us -> 15.8 us  [swap(): return lax.ppermute(value, 'dp', [(d, d ^ step) for d in range(size)])]
    pallas_call x5, Pallas kernels: 56.9 us -> 54.3 us  [block_terms(): pl.pallas_call(functools.partial(terms_kernel, size, len(groups), col_sta...]
  transfers between devices with their start and end apart: 46 -> 46, of which waited for: 15 -> 14; matrix products, arithmetic and copies ran while one was open for 7% -> 6% of each run, Pallas kernels for 27% -> 25%
where the time goes in v7:
time: 195 us; the launch traced here: 194 us
  Pallas kernels  58.5 us (30%)
  starting transfers between devices  48.2 us (25%)
  waiting for transfers between devices  48.1 us (25%)
  local copies, waits for them, and re-layouts  28.7 us (15%)
  matrix products  7.54 us (4%)
  other arithmetic  2.02 us (1%)
    pallas_call x5, Pallas kernels, block_terms(): pl.pallas_call(functools.partial(terms_kernel, size, len(groups), col_sta...  54.3 us
    ppermute x18, waiting for transfers between devices, across(): return lax.ppermute(value, 'tensor', pairs)  40.9 us
    ppermute x18, starting transfers between devices, across(): return lax.ppermute(value, 'tensor', pairs)  32.4 us
    unnamed x105, local copies, waits for them, and re-layouts  24.9 us
    ppermute x28, starting transfers between devices, swap(): return lax.ppermute(value, 'dp', [(d, d ^ step) for d in range(size)])  15.8 us
    ppermute x28, waiting for transfers between devices, swap(): return lax.ppermute(value, 'dp', [(d, d ^ step) for d in range(size)])  7.25 us
  transfers between devices with their start and end apart: 46, of which 14 were waited for; matrix products, arithmetic and copies ran while one was open for 6% of the time, Pallas kernels for 25%

profile of v7, /device:TPU:0, one launch (start us, length us, event | category | flops | bytes accessed | tf_op | source)
XLA Modules:
  0.0 194.5 jit_solution(5889171057338855782)
XLA Ops:
  0.7 2.0 %constant_dynamic-slice_fusion = (bf16[1,1,512,256]{3,2,1,0:T(8,128)(2,1)S(1)}, bf16[1,1,512,256]{3,2,1,0:T(8,128)(2,1)S(1)}, bf16[1,1,512,256]{3,2,1,0:T(8,128)(2,1)S(1)}, bf16[1,1,512,256]{3,2,1,0:T(8,128)(2,1)}) fusion(bf16[1,4,512,256]{3,2,1,0:T(8,128)(2,1)} %param.8, s32[]{:T(128)S(6)} %select_n.96, s32[]{:T(128)S(6)} %select_n.95, s32[]{:T(128)S(6)} %select_n.94, ...), kind=kLoop, calls=%fused_computation.33 | loop fusion | bytes 2097168 | tf_op jit(solution)/shard_map/dynamic-slice.7
  2.9 3.0 %collective-permute-start.1 = (bf16[128,512]{1,0:T(8,128)(2,1)S(1)}, bf16[128,512]{1,0:T(8,128)(2,1)S(1)}, u32[]{:S(2)}, u32[]{:S(2)}) collective-permute-start(bf16[128,512]{1,0:T(8,128)(2,1)S(1)} %get-tuple-element.124), channel_id=1, source_target_pairs={{0,2},{1,3},{2,0},{3,1},{4,6},{5,7},{6,4},{7,5},{8,10},{9,11},{10,... | collective-permute-start | bytes 393224 | tf_op jit(solution)/shard_map/ppermute | solution.py:18
  6.1 1.7 collective-permute-start
  7.9 3.3 %fusion.15 = f32[256,64]{0,1:T(8,128)S(1)} fusion(bf16[256,7168]{1,0:T(8,128)(2,1)} %param.7, bf16[7168,64]{0,1:T(8,128)(2,1)S(1)} %copy-done), kind=kOutput, calls=%fused_computation.39 | convolution fusion | flops 234881024 | bytes 4653056 | tf_op jit(solution)/shard_map/dot_general | solution.py:259
  11.5 1.6 collective-permute-start.8
  13.9 1.1 collective-permute-done
  15.0 2.0 %collective-permute-start.7 = (bf16[256,512]{1,0:T(8,128)(2,1)S(1)}, bf16[256,512]{1,0:T(8,128)(2,1)S(1)}, u32[]{:S(2)}, u32[]{:S(2)}) collective-permute-start(bf16[256,512]{1,0:T(8,128)(2,1)S(1)} %pad_maximum_fusion.refs_0_), channel_id=1, source_target_pairs={{0,4},{4,0},{8,12},{12,8},{1,5},{5,1},{9,13},{13,9},{2,6},{6,2},{1... | collective-permute-start | bytes 786440 | tf_op jit(solution)/shard_map/ppermute | solution.py:28
  17.1 2.6 %collective-permute-start.4 = (bf16[256,512]{1,0:T(8,128)(2,1)S(1)}, bf16[256,512]{1,0:T(8,128)(2,1)S(1)}, u32[]{:S(2)}, u32[]{:S(2)}) collective-permute-start(bf16[256,512]{1,0:T(8,128)(2,1)S(1)} %pad_maximum_fusion.refs_0_), channel_id=1, source_target_pairs={{0,8},{4,12},{8,0},{12,4},{1,9},{5,13},{9,1},{13,5},{2,10},{6,14},... | collective-permute-start | bytes 786440 | tf_op jit(solution)/shard_map/ppermute | solution.py:28
  20.4 11.6 %collective-permute-done.4.refs_2_ = bf16[256,512]{1,0:T(8,128)(2,1)S(1)} collective-permute-done((bf16[256,512]{1,0:T(8,128)(2,1)S(1)}, bf16[256,512]{1,0:T(8,128)(2,1)S(1)}, u32[]{:S(2)}, u32[]{:S(2)}) %collective-permute-start.4) | collective-permute-done | bytes 262176 | tf_op jit(solution)/shard_map/ppermute | solution.py:28
  32.4 2.6 %collective-permute-start.5 = (bf16[256,512]{1,0:T(8,128)(2,1)S(1)}, bf16[256,512]{1,0:T(8,128)(2,1)S(1)}, u32[]{:S(2)}, u32[]{:S(2)}) collective-permute-start(bf16[256,512]{1,0:T(8,128)(2,1)S(1)} %constant_dynamic-update-slice_fusion.refs_0_), channel_id=1, source_target_pairs={{0,4},{4,0},{8,12},{12,8},{1,5},{5,1},{9,13},{13,9},{2,6},{6,2},{1... | collective-permute-start | bytes 786440 | tf_op jit(solution)/shard_map/ppermute | solution.py:28
  35.7 1.3 collective-permute-start.11
  37.0 9.4 %collective-permute-done.6.refs_2_ = bf16[256,512]{1,0:T(8,128)(2,1)S(1)} collective-permute-done((bf16[256,512]{1,0:T(8,128)(2,1)S(1)}, bf16[256,512]{1,0:T(8,128)(2,1)S(1)}, u32[]{:S(2)}, u32[]{:S(2)}) %collective-permute-start.6) | collective-permute-done | bytes 262176 | tf_op jit(solution)/shard_map/ppermute | solution.py:28
  47.2 2.6 %collective-permute-done.11.refs_4_ = bf16[256,512]{1,0:T(8,128)(2,1)S(1)} collective-permute-done((bf16[256,512]{1,0:T(8,128)(2,1)S(1)}, bf16[256,512]{1,0:T(8,128)(2,1)S(1)}, u32[]{:S(2)}, u32[]{:S(2)}) %collective-permute-start.11) | collective-permute-done | bytes 262176 | tf_op jit(solution)/shard_map/ppermute | solution.py:28
  49.8 6.9 %terms.5 = (bf16[64,3584]{1,0:T(8,128)(2,1)S(1)}, bf16[64,3584]{1,0:T(8,128)(2,1)S(1)}, bf16[128,3584]{1,0:T(8,128)(2,1)S(1)}) custom-call(s32[1]{0:T(128)} %bitcast.place_ref, bf16[256,512]{1,0:T(8,128)(2,1)S(1)} %pad_maximum_fusion.refs_0_, bf16[256,512]{1,0:T(8,128)(2,1)S(1)} %collective-permute-done.7.refs_1_, ...), custom_call_target="tpu_custom_call" | custom-call | flops 15032385536 | bytes 1000 | tf_op jit(solution)/shard_map/terms/pallas_call | solution.py:122
  57.2 1.3 collective-permute-done.12.first_ref
  59.7 2.7 %collective-permute-start.17 = (bf16[256,512]{1,0:T(8,128)(2,1)}, bf16[256,512]{1,0:T(8,128)(2,1)}, u32[]{:S(2)}, u32[]{:S(2)}) collective-permute-start(bf16[256,512]{1,0:T(8,128)(2,1)} %collective-permute-done.9.refs_5_), channel_id=1, source_target_pairs={{0,8},{4,12},{8,0},{12,4},{1,9},{5,13},{9,1},{13,5},{2,10},{6,14},... | collective-permute-start | bytes 786440 | tf_op jit(solution)/shard_map/ppermute | solution.py:28
  62.4 1.8 collective-permute-start.16
  64.2 1.1 collective-permute-start.21
  66.0 1.3 collective-permute-start.15
  67.3 6.9 %terms.6 = (bf16[64,3584]{1,0:T(8,128)(2,1)S(1)}, bf16[64,3584]{1,0:T(8,128)(2,1)S(1)}, bf16[128,3584]{1,0:T(8,128)(2,1)S(1)}) custom-call(s32[1]{0:T(128)} %bitcast.place_ref, bf16[256,512]{1,0:T(8,128)(2,1)S(1)} %pad_maximum_fusion.refs_0_, bf16[256,512]{1,0:T(8,128)(2,1)S(1)} %collective-permute-done.7.refs_1_, ...), custom_call_target="tpu_custom_call" | custom-call | flops 15032385536 | bytes 1000 | tf_op jit(solution)/shard_map/terms/pallas_call | solution.py:122
  74.2 6.5 %collective-permute-done.15.refs_4_ = bf16[256,512]{1,0:T(8,128)(2,1)S(1)} collective-permute-done((bf16[256,512]{1,0:T(8,128)(2,1)S(1)}, bf16[256,512]{1,0:T(8,128)(2,1)S(1)}, u32[]{:S(2)}, u32[]{:S(2)}) %collective-permute-start.15) | collective-permute-done | bytes 262176 | tf_op jit(solution)/shard_map/ppermute | solution.py:28
  81.3 1.3 collective-permute-done.19.second_ref
  84.5 1.3 collective-permute-start.23
  85.8 1.1 copy.21
  87.0 4.1 %collective-permute-start.25 = (bf16[256,512]{1,0:T(8,128)(2,1)S(1)}, bf16[256,512]{1,0:T(8,128)(2,1)S(1)}, u32[]{:S(2)}, u32[]{:S(2)}) collective-permute-start(bf16[256,512]{1,0:T(8,128)(2,1)S(1)} %bitcast.38), channel_id=1, source_target_pairs={{0,8},{4,12},{8,0},{12,4},{1,9},{5,13},{9,1},{13,5},{2,10},{6,14},... | collective-permute-start | bytes 786440 | tf_op jit(solution)/shard_map/ppermute | solution.py:28
  91.4 0.9 collective-permute-start.28
  93.0 4.4 %collective-permute-done.23.refs_9_ = bf16[256,512]{1,0:T(8,128)(2,1)S(1)} collective-permute-done((bf16[256,512]{1,0:T(8,128)(2,1)}, bf16[256,512]{1,0:T(8,128)(2,1)S(1)}, u32[]{:S(2)}, u32[]{:S(2)}) %collective-permute-start.23) | collective-permute-done | bytes 262176 | tf_op jit(solution)/shard_map/ppermute | solution.py:28
  98.0 0.9 copy-done.23
  99.0 0.9 copy-done.26
  99.9 0.9 copy-done.31
  100.9 0.9 copy-done.36
  101.9 0.9 copy-done.39
  102.8 0.9 copy-done.42
  103.8 0.9 copy-done.45
  104.7 12.4 %terms.7 = (bf16[64,3584]{1,0:T(8,128)(2,1)S(1)}, bf16[64,3584]{1,0:T(8,128)(2,1)S(1)}, bf16[128,3584]{1,0:T(8,128)(2,1)S(1)}, bf16[64,3584]{1,0:T(8,128)(2,1)S(...) custom-call(s32[1]{0:T(128)} %bitcast.place_ref, ...), custom_call_target="tpu_custom_call" | custom-call | flops 30064771072 | bytes 1000 | tf_op jit(solution)/shard_map/terms/pallas_call | solution.py:122
  119.9 6.5 %collective-permute-start.20 = (f32[256,128]{0,1:T(8,128)S(1)}, f32[256,128]{0,1:T(8,128)S(1)}, u32[]{:S(2)}, u32[]{:S(2)}) collective-permute-start(f32[256,128]{0,1:T(8,128)S(1)} %copy-done.48), channel_id=1, source_target_pairs={{0,8},{4,12},{8,0},{12,4},{1,9},{5,13},{9,1},{13,5},{2,10},{6,14},... | collective-permute-start | bytes 393224 | tf_op jit(solution)/shard_map/ppermute | solution.py:28
  126.5 6.3 %collective-permute-done.20 = f32[256,128]{0,1:T(8,128)S(1)} collective-permute-done((f32[256,128]{0,1:T(8,128)S(1)}, f32[256,128]{0,1:T(8,128)S(1)}, u32[]{:S(2)}, u32[]{:S(2)}) %collective-permute-start.20) | collective-permute-done | bytes 131104 | tf_op jit(solution)/shard_map/ppermute | solution.py:28
  133.4 1.0 collective-permute-start.32
  134.4 0.9 copy-done.2
  137.0 0.9 collective-permute-done.33.refs_6_
  138.6 1.3 collective-permute-start.38
  139.9 0.8 copy-done.6
  140.7 0.8 copy-done.8
  141.5 0.9 copy-done.24
  142.4 0.9 copy-done.27
  143.4 0.9 copy-done.32
  144.3 0.9 copy-done.37
  145.3 0.9 copy-done.40
  146.2 0.9 copy-done.43
  147.2 0.9 copy-done.46
  148.1 12.8 %terms.8 = (bf16[64,3584]{1,0:T(8,128)(2,1)}, bf16[64,3584]{1,0:T(8,128)(2,1)S(1)}, bf16[128,3584]{1,0:T(8,128)(2,1)S(1)}, bf16[64,3584]{1,0:T(8,128)(2,1)S(1)},...) custom-call(s32[1]{0:T(128)} %bitcast.place_ref, ...), custom_call_target="tpu_custom_call" | custom-call | flops 30064771072 | bytes 1000 | tf_op jit(solution)/shard_map/terms/pallas_call | solution.py:122
  161.0 0.8 copy-done.10
  161.7 0.8 copy-done.11
  162.5 0.8 copy-done.12
  163.3 0.8 copy-done.13
  166.1 0.9 collective-permute-start.31
  167.1 0.9 collective-permute-start.30
  168.8 1.2 collective-permute-start.45
  170.0 1.1 collective-permute-done.30
  172.1 0.9 select_select_fusion.3
  173.2 2.7 %fusion.4 = f32[1024,1024]{1,0:T(8,128)} fusion(bf16[16,4224]{1,0:T(8,128)(2,1)S(1)} %pad_maximum_fusion.1, s32[]{:T(128)S(6)} %select_n.121, s32[]{:T(128)S(6)} %select_n.122), kind=kOutput, calls=%fused_computation.19 | convolution fusion | flops 33554432 | bytes 4259848 | tf_op jit(solution)/shard_map/dot_general | solution.py:248
  176.0 0.9 fusion.6
  177.0 15.4 %terms.9.own_ref = bf16[256,7168]{1,0:T(8,128)(2,1)} custom-call(s32[1]{0:T(128)} %bitcast.place_ref, bf16[256,512]{1,0:T(8,128)(2,1)S(1)} %bitcast.41, bf16[256,512]{1,0:T(8,128)(2,1)S(1)} %copy-done.21, bf16[256,512]{1,0:T(8,128)(2,1)S(1)} %copy-done.19, bf16[256,512]{1,0:T(8,128)(2,1)S(1)} %copy-done.29, bf16[256,512]{1,0:T(8,128)(2,1)S(1)} %copy-done.34, ...), custom_call_target="tpu_custom_call" | custom-call | flops 30064771072 | bytes 1000 | tf_op jit(solution)/shard_map/terms/pallas_call | solution.py:122
  192.4 2.1 %finish.1 = bf16[256,7168]{1,0:T(8,128)(2,1)} custom-call(bf16[256,7168]{1,0:T(8,128)(2,1)} %terms.9.own_ref, bf16[128,3584]{1,0:T(8,128)(2,1)S(1)} %collective-permute-done.45.other_ref), custom_call_target="tpu_custom_call", output_to_operand_aliasing={{}: (0, {})} | custom-call | flops 1000 | bytes 1000 | tf_op jit(solution)/shard_map/finish/pallas_call | solution.py:193
  (172 shorter events, 20.5 us)
Async XLA Ops:
  2.9 10.9 %collective-permute-start.1 = (bf16[128,512]{1,0:T(8,128)(2,1)S(1)}, bf16[128,512]{1,0:T(8,128)(2,1)S(1)}, u32[]{:S(2)}, u32[]{:S(2)}) collective-permute-start(bf16[128,512]{1,0:T(8,128)(2,1)S(1)} %get-tuple-element.124), channel_id=1, source_target_pairs={{0,2},{1,3},{2,0},{3,1},{4,6},{5,7},{6,4},{7,5},{8,10},{9,11},{10,... | collective-permute-start | bytes 393224 | tf_op jit(solution)/shard_map/ppermute | solution.py:18
  6.1 11.0 %collective-permute-start.2 = (bf16[128,512]{1,0:T(8,128)(2,1)S(1)}, bf16[128,512]{1,0:T(8,128)(2,1)S(1)}, u32[]{:S(2)}, u32[]{:S(2)}) collective-permute-start(bf16[128,512]{1,0:T(8,128)(2,1)S(1)} %get-tuple-element.125), channel_id=1, source_target_pairs={{0,3},{1,2},{2,1},{3,0},{4,7},{5,6},{6,5},{7,4},{8,11},{9,10},{10,... | collective-permute-start | bytes 393224 | tf_op jit(solution)/shard_map/ppermute | solution.py:18
  6.1 8.9 %collective-permute-start = (bf16[128,512]{1,0:T(8,128)(2,1)S(1)}, bf16[128,512]{1,0:T(8,128)(2,1)S(1)}, u32[]{:S(2)}, u32[]{:S(2)}) collective-permute-start(bf16[128,512]{1,0:T(8,128)(2,1)S(1)} %get-tuple-element.126), channel_id=1, source_target_pairs={{0,3},{1,2},{2,1},{3,0},{4,7},{5,6},{6,5},{7,4},{8,11},{9,10},{10,... | collective-permute-start | bytes 393224 | tf_op jit(solution)/shard_map/ppermute | solution.py:18
  11.5 8.2 %collective-permute-start.8 = (f32[256,128]{0,1:T(8,128)S(1)}, f32[256,128]{0,1:T(8,128)S(1)}, u32[]{:S(2)}, u32[]{:S(2)}) collective-permute-start(f32[256,128]{0,1:T(8,128)S(1)} %pad_maximum_fusion.2), channel_id=1, source_target_pairs={{0,4},{4,0},{8,12},{12,8},{1,5},{5,1},{9,13},{13,9},{2,6},{6,2},{1... | collective-permute-start | bytes 393224 | tf_op jit(solution)/shard_map/ppermute | solution.py:28
  13.1 6.5 %collective-permute-start.3 = (bf16[128,512]{1,0:T(8,128)(2,1)S(1)}, bf16[128,512]{1,0:T(8,128)(2,1)S(1)}, u32[]{:S(2)}, u32[]{:S(2)}) collective-permute-start(bf16[128,512]{1,0:T(8,128)(2,1)S(1)} %get-tuple-element.123), channel_id=1, source_target_pairs={{0,2},{1,3},{2,0},{3,1},{4,6},{5,7},{6,4},{7,5},{8,10},{9,11},{10,... | collective-permute-start | bytes 393224 | tf_op jit(solution)/shard_map/ppermute | solution.py:18
  13.8 21.2 %collective-permute-start.9 = (bf16[256,512]{1,0:T(8,128)(2,1)S(1)}, bf16[256,512]{1,0:T(8,128)(2,1)}, u32[]{:S(2)}, u32[]{:S(2)}) collective-permute-start(bf16[256,512]{1,0:T(8,128)(2,1)S(1)} %bitcast.45), channel_id=1, source_target_pairs={{0,1},{1,0},{2,3},{3,2},{4,5},{5,4},{6,7},{7,6},{8,9},{9,8},{10,11... | collective-permute-start | bytes 786440 | tf_op jit(solution)/shard_map/ppermute | solution.py:18
  15.0 32.1 %collective-permute-start.7 = (bf16[256,512]{1,0:T(8,128)(2,1)S(1)}, bf16[256,512]{1,0:T(8,128)(2,1)S(1)}, u32[]{:S(2)}, u32[]{:S(2)}) collective-permute-start(bf16[256,512]{1,0:T(8,128)(2,1)S(1)} %pad_maximum_fusion.refs_0_), channel_id=1, source_target_pairs={{0,4},{4,0},{8,12},{12,8},{1,5},{5,1},{9,13},{13,9},{2,6},{6,2},{1... | collective-permute-start | bytes 786440 | tf_op jit(solution)/shard_map/ppermute | solution.py:28
  17.1 14.9 %collective-permute-start.4 = (bf16[256,512]{1,0:T(8,128)(2,1)S(1)}, bf16[256,512]{1,0:T(8,128)(2,1)S(1)}, u32[]{:S(2)}, u32[]{:S(2)}) collective-permute-start(bf16[256,512]{1,0:T(8,128)(2,1)S(1)} %pad_maximum_fusion.refs_0_), channel_id=1, source_target_pairs={{0,8},{4,12},{8,0},{12,4},{1,9},{5,13},{9,1},{13,5},{2,10},{6,14},... | collective-permute-start | bytes 786440 | tf_op jit(solution)/shard_map/ppermute | solution.py:28
  32.0 14.4 %collective-permute-start.6 = (bf16[256,512]{1,0:T(8,128)(2,1)S(1)}, bf16[256,512]{1,0:T(8,128)(2,1)S(1)}, u32[]{:S(2)}, u32[]{:S(2)}) collective-permute-start(bf16[256,512]{1,0:T(8,128)(2,1)S(1)} %constant_dynamic-update-slice_fusion.refs_0_), channel_id=1, source_target_pairs={{0,8},{4,12},{8,0},{12,4},{1,9},{5,13},{9,1},{13,5},{2,10},{6,14},... | collective-permute-start | bytes 786440 | tf_op jit(solution)/shard_map/ppermute | solution.py:28
  32.4 14.1 %collective-permute-start.5 = (bf16[256,512]{1,0:T(8,128)(2,1)S(1)}, bf16[256,512]{1,0:T(8,128)(2,1)S(1)}, u32[]{:S(2)}, u32[]{:S(2)}) collective-permute-start(bf16[256,512]{1,0:T(8,128)(2,1)S(1)} %constant_dynamic-update-slice_fusion.refs_0_), channel_id=1, source_target_pairs={{0,4},{4,0},{8,12},{12,8},{1,5},{5,1},{9,13},{13,9},{2,6},{6,2},{1... | collective-permute-start | bytes 786440 | tf_op jit(solution)/shard_map/ppermute | solution.py:28
  35.0 12.2 %collective-permute-start.10 = (bf16[256,512]{1,0:T(8,128)(2,1)S(1)}, bf16[256,512]{1,0:T(8,128)(2,1)S(1)}, u32[]{:S(2)}, u32[]{:S(2)}) collective-permute-start(bf16[256,512]{1,0:T(8,128)(2,1)S(1)} %pad_maximum_fusion.refs_0_), channel_id=1, source_target_pairs={{4,8},{8,4},{5,9},{9,5},{6,10},{10,6},{7,11},{11,7},{20,24},{24,20... | collective-permute-start | bytes 786440 | tf_op jit(solution)/shard_map/ppermute | solution.py:28
  35.7 14.1 %collective-permute-start.11 = (bf16[256,512]{1,0:T(8,128)(2,1)S(1)}, bf16[256,512]{1,0:T(8,128)(2,1)S(1)}, u32[]{:S(2)}, u32[]{:S(2)}) collective-permute-start(bf16[256,512]{1,0:T(8,128)(2,1)S(1)} %collective-permute-done.4.refs_2_), channel_id=1, source_target_pairs={{4,0},{8,12},{5,1},{9,13},{6,2},{10,14},{7,3},{11,15},{20,16},{24,... | collective-permute-start | bytes 786440 | tf_op jit(solution)/shard_map/ppermute | solution.py:28
  46.4 19.6 %copy-start.22 = (bf16[256,512]{1,0:T(8,128)(2,1)}, bf16[256,512]{1,0:T(8,128)(2,1)S(1)}, u32[]{:S(2)}) copy-start(bf16[256,512]{1,0:T(8,128)(2,1)S(1)} %collective-permute-done.6.refs_2_) | copy-start | bytes 786436
  56.7 1.9 collective-permute-start.12
  56.7 2.5 %collective-permute-start.13 = (bf16[64,3584]{1,0:T(8,128)(2,1)S(1)}, bf16[64,3584]{1,0:T(8,128)(2,1)S(1)}, u32[]{:S(2)}, u32[]{:S(2)}) collective-permute-start(bf16[64,3584]{1,0:T(8,128)(2,1)S(1)} %get-tuple-element.68), channel_id=1, source_target_pairs={{0,1},{1,0},{2,3},{3,2},{4,5},{5,4},{6,7},{7,6},{8,9},{9,8},{10,11... | collective-permute-start | bytes 1376264 | tf_op jit(solution)/shard_map/ppermute | solution.py:18
  59.7 21.0 %collective-permute-start.17 = (bf16[256,512]{1,0:T(8,128)(2,1)}, bf16[256,512]{1,0:T(8,128)(2,1)}, u32[]{:S(2)}, u32[]{:S(2)}) collective-permute-start(bf16[256,512]{1,0:T(8,128)(2,1)} %collective-permute-done.9.refs_5_), channel_id=1, source_target_pairs={{0,8},{4,12},{8,0},{12,4},{1,9},{5,13},{9,1},{13,5},{2,10},{6,14},... | collective-permute-start | bytes 786440 | tf_op jit(solution)/shard_map/ppermute | solution.py:28
  62.4 18.3 %collective-permute-start.16 = (bf16[256,512]{1,0:T(8,128)(2,1)}, bf16[256,512]{1,0:T(8,128)(2,1)S(1)}, u32[]{:S(2)}, u32[]{:S(2)}) collective-permute-start(bf16[256,512]{1,0:T(8,128)(2,1)} %collective-permute-done.9.refs_5_), channel_id=1, source_target_pairs={{0,4},{4,0},{8,12},{12,8},{1,5},{5,1},{9,13},{13,9},{2,6},{6,2},{1... | collective-permute-start | bytes 786440 | tf_op jit(solution)/shard_map/ppermute | solution.py:28
  64.2 27.2 %collective-permute-start.21 = (bf16[128,3584]{1,0:T(8,128)(2,1)S(1)}, bf16[128,3584]{1,0:T(8,128)(2,1)}, u32[]{:S(2)}, u32[]{:S(2)}) collective-permute-start(bf16[128,3584]{1,0:T(8,128)(2,1)S(1)} %pair.4), channel_id=1, source_target_pairs={{0,2},{1,3},{2,0},{3,1},{4,6},{5,7},{6,4},{7,5},{8,10},{9,11},{10,... | collective-permute-start | bytes 2752520 | tf_op jit(solution)/shard_map/ppermute | solution.py:18
  65.3 8.9 %collective-permute-start.14 = (bf16[256,512]{1,0:T(8,128)(2,1)S(1)}, bf16[256,512]{1,0:T(8,128)(2,1)S(1)}, u32[]{:S(2)}, u32[]{:S(2)}) collective-permute-start(bf16[256,512]{1,0:T(8,128)(2,1)S(1)} %constant_dynamic-update-slice_fusion.refs_0_), channel_id=1, source_target_pairs={{4,8},{8,4},{5,9},{9,5},{6,10},{10,6},{7,11},{11,7},{20,24},{24,20... | collective-permute-start | bytes 786440 | tf_op jit(solution)/shard_map/ppermute | solution.py:28
  66.0 14.7 %collective-permute-start.15 = (bf16[256,512]{1,0:T(8,128)(2,1)S(1)}, bf16[256,512]{1,0:T(8,128)(2,1)S(1)}, u32[]{:S(2)}, u32[]{:S(2)}) collective-permute-start(bf16[256,512]{1,0:T(8,128)(2,1)S(1)} %collective-permute-done.6.refs_2_), channel_id=1, source_target_pairs={{4,0},{8,12},{5,1},{9,13},{6,2},{10,14},{7,3},{11,15},{20,16},{24,... | collective-permute-start | bytes 786440 | tf_op jit(solution)/shard_map/ppermute | solution.py:28
  74.2 11.6 %copy-start.35 = (bf16[256,512]{1,0:T(8,128)(2,1)}, bf16[256,512]{1,0:T(8,128)(2,1)S(1)}, u32[]{:S(2)}) copy-start(bf16[256,512]{1,0:T(8,128)(2,1)S(1)} %collective-permute-done.14.refs_3_) | copy-start | bytes 786436
  80.7 1.9 collective-permute-start.19
  80.8 2.5 %collective-permute-start.18 = (bf16[64,3584]{1,0:T(8,128)(2,1)S(1)}, bf16[64,3584]{1,0:T(8,128)(2,1)S(1)}, u32[]{:S(2)}, u32[]{:S(2)}) collective-permute-start(bf16[64,3584]{1,0:T(8,128)(2,1)S(1)} %get-tuple-element.75), channel_id=1, source_target_pairs={{0,1},{1,0},{2,3},{3,2},{4,5},{5,4},{6,7},{7,6},{8,9},{9,8},{10,11... | collective-permute-start | bytes 1376264 | tf_op jit(solution)/shard_map/ppermute | solution.py:18
  83.8 8.5 %collective-permute-start.22 = (bf16[256,512]{1,0:T(8,128)(2,1)}, bf16[256,512]{1,0:T(8,128)(2,1)S(1)}, u32[]{:S(2)}, u32[]{:S(2)}) collective-permute-start(bf16[256,512]{1,0:T(8,128)(2,1)} %collective-permute-done.9.refs_5_), channel_id=1, source_target_pairs={{4,8},{8,4},{5,9},{9,5},{6,10},{10,6},{7,11},{11,7},{20,24},{24,20... | collective-permute-start | bytes 786440 | tf_op jit(solution)/shard_map/ppermute | solution.py:28
  84.5 12.8 %collective-permute-start.23 = (bf16[256,512]{1,0:T(8,128)(2,1)}, bf16[256,512]{1,0:T(8,128)(2,1)S(1)}, u32[]{:S(2)}, u32[]{:S(2)}) collective-permute-start(bf16[256,512]{1,0:T(8,128)(2,1)} %collective-permute-done.17.refs_7_), channel_id=1, source_target_pairs={{4,0},{8,12},{5,1},{9,13},{6,2},{10,14},{7,3},{11,15},{20,16},{24,... | collective-permute-start | bytes 786440 | tf_op jit(solution)/shard_map/ppermute | solution.py:28
  85.8 34.0 %copy-start.48 = (f32[256,128]{0,1:T(8,128)S(1)}, f32[256,128]{0,1:T(8,128)}, u32[]{:S(2)}) copy-start(f32[256,128]{0,1:T(8,128)} %fusion.14) | copy-start | bytes 393220
  87.0 39.4 %copy-start.50 = (s32[1,256]{1,0:T(1,128)S(1)}, s32[1,256]{1,0:T(1,128)}, u32[]{:S(2)}) copy-start(s32[1,256]{1,0:T(1,128)} %param.12) | copy-start | bytes 3076
  87.0 39.4 %copy-start.51 = (s32[4]{0:T(128)S(1)}, s32[4]{0:T(128)}, u32[]{:S(2)}) copy-start(s32[4]{0:T(128)} %param.13) | copy-start | bytes 52
  87.0 31.6 %collective-permute-start.25 = (bf16[256,512]{1,0:T(8,128)(2,1)S(1)}, bf16[256,512]{1,0:T(8,128)(2,1)S(1)}, u32[]{:S(2)}, u32[]{:S(2)}) collective-permute-start(bf16[256,512]{1,0:T(8,128)(2,1)S(1)} %bitcast.38), channel_id=1, source_target_pairs={{0,8},{4,12},{8,0},{12,4},{1,9},{5,13},{9,1},{13,5},{2,10},{6,14},... | collective-permute-start | bytes 786440 | tf_op jit(solution)/shard_map/ppermute | solution.py:28
  91.0 27.6 %collective-permute-start.24 = (bf16[256,512]{1,0:T(8,128)(2,1)S(1)}, bf16[256,512]{1,0:T(8,128)(2,1)S(1)}, u32[]{:S(2)}, u32[]{:S(2)}) collective-permute-start(bf16[256,512]{1,0:T(8,128)(2,1)S(1)} %bitcast.39), channel_id=1, source_target_pairs={{0,4},{4,0},{8,12},{12,8},{1,5},{5,1},{9,13},{13,9},{2,6},{6,2},{1... | collective-permute-start | bytes 786440 | tf_op jit(solution)/shard_map/ppermute | solution.py:28
  91.4 43.0 %collective-permute-start.28 = (bf16[128,3584]{1,0:T(8,128)(2,1)S(1)}, bf16[128,3584]{1,0:T(8,128)(2,1)S(1)}, u32[]{:S(2)}, u32[]{:S(2)}) collective-permute-start(bf16[128,3584]{1,0:T(8,128)(2,1)S(1)} %pair.5), channel_id=1, source_target_pairs={{0,2},{1,3},{2,0},{3,1},{4,6},{5,7},{6,4},{7,5},{8,10},{9,11},{10,... | collective-permute-start | bytes 2752520 | tf_op jit(solution)/shard_map/ppermute | solution.py:18
  118.6 15.8 %copy-start.14 = (bf16[64,3584]{1,0:T(8,128)(2,1)}, bf16[64,3584]{1,0:T(8,128)(2,1)S(1)}, u32[]{:S(2)}) copy-start(bf16[64,3584]{1,0:T(8,128)(2,1)S(1)} %get-tuple-element.97) | copy-start | bytes 1376260
  118.6 16.7 %copy-start.15 = (bf16[64,3584]{1,0:T(8,128)(2,1)}, bf16[64,3584]{1,0:T(8,128)(2,1)S(1)}, u32[]{:S(2)}) copy-start(bf16[64,3584]{1,0:T(8,128)(2,1)S(1)} %get-tuple-element.95) | copy-start | bytes 1376260
  118.6 16.7 %copy-start.20 = (bf16[256,512]{1,0:T(8,128)(2,1)}, bf16[256,512]{1,0:T(8,128)(2,1)S(1)}, u32[]{:S(2)}) copy-start(bf16[256,512]{1,0:T(8,128)(2,1)S(1)} %collective-permute-done.24.refs_1_) | copy-start | bytes 786436
  119.3 13.5 %collective-permute-start.27 = (bf16[64,3584]{1,0:T(8,128)(2,1)S(1)}, bf16[64,3584]{1,0:T(8,128)(2,1)S(1)}, u32[]{:S(2)}, u32[]{:S(2)}) collective-permute-start(bf16[64,3584]{1,0:T(8,128)(2,1)S(1)} %get-tuple-element.88), channel_id=1, source_target_pairs={{0,1},{1,0},{2,3},{3,2},{4,5},{5,4},{6,7},{7,6},{8,9},{9,8},{10,11... | collective-permute-start | bytes 1376264 | tf_op jit(solution)/shard_map/ppermute | solution.py:18
  119.3 13.5 %collective-permute-start.26 = (bf16[64,3584]{1,0:T(8,128)(2,1)S(1)}, bf16[64,3584]{1,0:T(8,128)(2,1)S(1)}, u32[]{:S(2)}, u32[]{:S(2)}) collective-permute-start(bf16[64,3584]{1,0:T(8,128)(2,1)S(1)} %get-tuple-element.86), channel_id=1, source_target_pairs={{0,1},{1,0},{2,3},{3,2},{4,5},{5,4},{6,7},{7,6},{8,9},{9,8},{10,11... | collective-permute-start | bytes 1376264 | tf_op jit(solution)/shard_map/ppermute | solution.py:18
  119.9 13.0 %collective-permute-start.20 = (f32[256,128]{0,1:T(8,128)S(1)}, f32[256,128]{0,1:T(8,128)S(1)}, u32[]{:S(2)}, u32[]{:S(2)}) collective-permute-start(f32[256,128]{0,1:T(8,128)S(1)} %copy-done.48), channel_id=1, source_target_pairs={{0,8},{4,12},{8,0},{12,4},{1,9},{5,13},{9,1},{13,5},{2,10},{6,14},... | collective-permute-start | bytes 393224 | tf_op jit(solution)/shard_map/ppermute | solution.py:28
  133.4 36.6 %collective-permute-start.32 = (bf16[128,3584]{1,0:T(8,128)(2,1)S(1)}, bf16[128,3584]{1,0:T(8,128)(2,1)}, u32[]{:S(2)}, u32[]{:S(2)}) collective-permute-start(bf16[128,3584]{1,0:T(8,128)(2,1)S(1)} %pair.6), channel_id=1, source_target_pairs={{0,2},{1,3},{2,0},{3,1},{4,6},{5,7},{6,4},{7,5},{8,10},{9,11},{10,... | collective-permute-start | bytes 2752520 | tf_op jit(solution)/shard_map/ppermute | solution.py:18
  135.8 2.1 %collective-permute-start.33 = (bf16[64,3584]{1,0:T(8,128)(2,1)}, bf16[64,3584]{1,0:T(8,128)(2,1)S(1)}, u32[]{:S(2)}, u32[]{:S(2)}) collective-permute-start(bf16[64,3584]{1,0:T(8,128)(2,1)} %copy-done.17), channel_id=1, source_target_pairs={{0,1},{1,0},{2,3},{3,2},{4,5},{5,4},{6,7},{7,6},{8,9},{9,8},{10,11... | collective-permute-start | bytes 1376264 | tf_op jit(solution)/shard_map/ppermute | solution.py:18
  135.9 2.7 %collective-permute-start.34 = (bf16[64,3584]{1,0:T(8,128)(2,1)}, bf16[64,3584]{1,0:T(8,128)(2,1)S(1)}, u32[]{:S(2)}, u32[]{:S(2)}) collective-permute-start(bf16[64,3584]{1,0:T(8,128)(2,1)} %copy-done.16), channel_id=1, source_target_pairs={{0,1},{1,0},{2,3},{3,2},{4,5},{5,4},{6,7},{7,6},{8,9},{9,8},{10,11... | collective-permute-start | bytes 1376264 | tf_op jit(solution)/shard_map/ppermute | solution.py:18
  136.4 3.5 %collective-permute-start.35 = (bf16[64,3584]{1,0:T(8,128)(2,1)}, bf16[64,3584]{1,0:T(8,128)(2,1)S(1)}, u32[]{:S(2)}, u32[]{:S(2)}) collective-permute-start(bf16[64,3584]{1,0:T(8,128)(2,1)} %copy-done.15), channel_id=1, source_target_pairs={{0,1},{1,0},{2,3},{3,2},{4,5},{5,4},{6,7},{7,6},{8,9},{9,8},{10,11... | collective-permute-start | bytes 1376264 | tf_op jit(solution)/shard_map/ppermute | solution.py:18
  136.5 4.2 %collective-permute-start.36 = (bf16[64,3584]{1,0:T(8,128)(2,1)}, bf16[64,3584]{1,0:T(8,128)(2,1)S(1)}, u32[]{:S(2)}, u32[]{:S(2)}) collective-permute-start(bf16[64,3584]{1,0:T(8,128)(2,1)} %copy-done.14), channel_id=1, source_target_pairs={{0,1},{1,0},{2,3},{3,2},{4,5},{5,4},{6,7},{7,6},{8,9},{9,8},{10,11... | collective-permute-start | bytes 1376264 | tf_op jit(solution)/shard_map/ppermute | solution.py:18
  137.9 26.2 %collective-permute-start.37 = (bf16[256,512]{1,0:T(8,128)(2,1)S(1)}, bf16[256,512]{1,0:T(8,128)(2,1)S(1)}, u32[]{:S(2)}, u32[]{:S(2)}) collective-permute-start(bf16[256,512]{1,0:T(8,128)(2,1)S(1)} %bitcast.40), channel_id=1, source_target_pairs={{4,8},{8,4},{5,9},{9,5},{6,10},{10,6},{7,11},{11,7},{20,24},{24,20... | collective-permute-start | bytes 786440 | tf_op jit(solution)/shard_map/ppermute | solution.py:28
  138.6 22.4 %copy-start.4 = (bf16[64,3584]{1,0:T(8,128)(2,1)}, bf16[64,3584]{1,0:T(8,128)(2,1)S(1)}, u32[]{:S(2)}) copy-start(bf16[64,3584]{1,0:T(8,128)(2,1)S(1)} %collective-permute-done.34.refs_7_) | copy-start | bytes 1376260
  138.6 26.2 %collective-permute-start.38 = (bf16[256,512]{1,0:T(8,128)(2,1)}, bf16[256,512]{1,0:T(8,128)(2,1)S(1)}, u32[]{:S(2)}, u32[]{:S(2)}) collective-permute-start(bf16[256,512]{1,0:T(8,128)(2,1)} %copy-done.18), channel_id=1, source_target_pairs={{4,0},{8,12},{5,1},{9,13},{6,2},{10,14},{7,3},{11,15},{20,16},{24,... | collective-permute-start | bytes 786440 | tf_op jit(solution)/shard_map/ppermute | solution.py:28
  165.5 2.5 %collective-permute-start.40 = (bf16[64,3584]{1,0:T(8,128)(2,1)S(1)}, bf16[64,3584]{1,0:T(8,128)(2,1)S(1)}, u32[]{:S(2)}, u32[]{:S(2)}) collective-permute-start(bf16[64,3584]{1,0:T(8,128)(2,1)S(1)} %get-tuple-element.105), channel_id=1, source_target_pairs={{0,1},{1,0},{2,3},{3,2},{4,5},{5,4},{6,7},{7,6},{8,9},{9,8},{10,11... | collective-permute-start | bytes 1376264 | tf_op jit(solution)/shard_map/ppermute | solution.py:18
  165.7 2.5 %collective-permute-start.39 = (bf16[64,3584]{1,0:T(8,128)(2,1)}, bf16[64,3584]{1,0:T(8,128)(2,1)S(1)}, u32[]{:S(2)}, u32[]{:S(2)}) collective-permute-start(bf16[64,3584]{1,0:T(8,128)(2,1)} %get-tuple-element.103), channel_id=1, source_target_pairs={{0,1},{1,0},{2,3},{3,2},{4,5},{5,4},{6,7},{7,6},{8,9},{9,8},{10,11... | collective-permute-start | bytes 1376264 | tf_op jit(solution)/shard_map/ppermute | solution.py:18
  166.1 3.9 %collective-permute-start.31 = (bf16[4,4224]{1,0:T(4,128)(2,1)S(1)}, bf16[4,4224]{1,0:T(4,128)(2,1)S(1)}, u32[]{:S(2)}, u32[]{:S(2)}) collective-permute-start(bf16[4,4224]{1,0:T(4,128)(2,1)S(1)} %pad_maximum_fusion.3), channel_id=1, source_target_pairs={{0,3},{1,2},{2,1},{3,0},{4,7},{5,6},{6,5},{7,4},{8,11},{9,10},{10,... | collective-permute-start | bytes 101384 | tf_op jit(solution)/shard_map/ppermute | solution.py:18
  167.1 4.0 %collective-permute-start.30 = (bf16[4,4224]{1,0:T(4,128)(2,1)S(1)}, bf16[4,4224]{1,0:T(4,128)(2,1)}, u32[]{:S(2)}, u32[]{:S(2)}) collective-permute-start(bf16[4,4224]{1,0:T(4,128)(2,1)S(1)} %pad_maximum_fusion.3), channel_id=1, source_target_pairs={{0,2},{1,3},{2,0},{3,1},{4,6},{5,7},{6,4},{7,5},{8,10},{9,11},{10,... | collective-permute-start | bytes 101384 | tf_op jit(solution)/shard_map/ppermute | solution.py:18
  168.0 3.1 %collective-permute-start.29 = (bf16[4,4224]{1,0:T(4,128)(2,1)S(1)}, bf16[4,4224]{1,0:T(4,128)(2,1)}, u32[]{:S(2)}, u32[]{:S(2)}) collective-permute-start(bf16[4,4224]{1,0:T(4,128)(2,1)S(1)} %pad_maximum_fusion.3), channel_id=1, source_target_pairs={{0,1},{1,0},{2,3},{3,2},{4,5},{5,4},{6,7},{7,6},{8,9},{9,8},{10,11... | collective-permute-start | bytes 101384 | tf_op jit(solution)/shard_map/ppermute | solution.py:18
  168.2 8.6 %copy-start.3 = (bf16[128,3584]{1,0:T(8,128)(2,1)S(1)}, bf16[128,3584]{1,0:T(8,128)(2,1)}, u32[]{:S(2)}) copy-start(bf16[128,3584]{1,0:T(8,128)(2,1)} %copy-done.2) | copy-start | bytes 2752516
  168.2 8.7 %copy-start.5 = (bf16[64,3584]{1,0:T(8,128)(2,1)S(1)}, bf16[64,3584]{1,0:T(8,128)(2,1)}, u32[]{:S(2)}) copy-start(bf16[64,3584]{1,0:T(8,128)(2,1)} %copy-done.4) | copy-start | bytes 1376260
  168.2 8.7 %copy-start.7 = (bf16[64,3584]{1,0:T(8,128)(2,1)S(1)}, bf16[64,3584]{1,0:T(8,128)(2,1)}, u32[]{:S(2)}) copy-start(bf16[64,3584]{1,0:T(8,128)(2,1)} %copy-done.6) | copy-start | bytes 1376260
  168.2 8.7 %copy-start.9 = (bf16[64,3584]{1,0:T(8,128)(2,1)S(1)}, bf16[64,3584]{1,0:T(8,128)(2,1)}, u32[]{:S(2)}) copy-start(bf16[64,3584]{1,0:T(8,128)(2,1)} %copy-done.8) | copy-start | bytes 1376260
  168.2 8.7 %copy-start.19 = (bf16[256,512]{1,0:T(8,128)(2,1)S(1)}, bf16[256,512]{1,0:T(8,128)(2,1)}, u32[]{:S(2)}) copy-start(bf16[256,512]{1,0:T(8,128)(2,1)} %copy-done.18) | copy-start | bytes 786436
  168.2 8.7 %copy-start.21 = (bf16[256,512]{1,0:T(8,128)(2,1)S(1)}, bf16[256,512]{1,0:T(8,128)(2,1)}, u32[]{:S(2)}) copy-start(bf16[256,512]{1,0:T(8,128)(2,1)} %copy-done.20) | copy-start | bytes 786436
  168.2 8.7 %copy-start.29 = (bf16[256,512]{1,0:T(8,128)(2,1)S(1)}, bf16[256,512]{1,0:T(8,128)(2,1)}, u32[]{:S(2)}) copy-start(bf16[256,512]{1,0:T(8,128)(2,1)} %copy-done.28) | copy-start | bytes 786436
  168.3 8.7 %copy-start.34 = (bf16[256,512]{1,0:T(8,128)(2,1)S(1)}, bf16[256,512]{1,0:T(8,128)(2,1)}, u32[]{:S(2)}) copy-start(bf16[256,512]{1,0:T(8,128)(2,1)} %copy-done.33) | copy-start | bytes 786436
  168.8 23.6 %collective-permute-start.45 = (bf16[128,3584]{1,0:T(8,128)(2,1)S(1)}, bf16[128,3584]{1,0:T(8,128)(2,1)S(1)}, u32[]{:S(2)}, u32[]{:S(2)}) collective-permute-start(bf16[128,3584]{1,0:T(8,128)(2,1)S(1)} %pair.7), channel_id=1, source_target_pairs={{0,2},{1,3},{2,0},{3,1},{4,6},{5,7},{6,4},{7,5},{8,10},{9,11},{10,... | collective-permute-start | bytes 2752520 | tf_op jit(solution)/shard_map/ppermute | solution.py:18
  171.1 5.7 %collective-permute-start.41 = (bf16[64,3584]{1,0:T(8,128)(2,1)}, bf16[64,3584]{1,0:T(8,128)(2,1)S(1)}, u32[]{:S(2)}, u32[]{:S(2)}) collective-permute-start(bf16[64,3584]{1,0:T(8,128)(2,1)} %copy-done.13), channel_id=1, source_target_pairs={{0,1},{1,0},{2,3},{3,2},{4,5},{5,4},{6,7},{7,6},{8,9},{9,8},{10,11... | collective-permute-start | bytes 1376264 | tf_op jit(solution)/shard_map/ppermute | solution.py:18
  171.1 5.7 %collective-permute-start.42 = (bf16[64,3584]{1,0:T(8,128)(2,1)}, bf16[64,3584]{1,0:T(8,128)(2,1)S(1)}, u32[]{:S(2)}, u32[]{:S(2)}) collective-permute-start(bf16[64,3584]{1,0:T(8,128)(2,1)} %copy-done.12), channel_id=1, source_target_pairs={{0,1},{1,0},{2,3},{3,2},{4,5},{5,4},{6,7},{7,6},{8,9},{9,8},{10,11... | collective-permute-start | bytes 1376264 | tf_op jit(solution)/shard_map/ppermute | solution.py:18
  171.6 5.2 %collective-permute-start.43 = (bf16[64,3584]{1,0:T(8,128)(2,1)}, bf16[64,3584]{1,0:T(8,128)(2,1)S(1)}, u32[]{:S(2)}, u32[]{:S(2)}) collective-permute-start(bf16[64,3584]{1,0:T(8,128)(2,1)} %copy-done.11), channel_id=1, source_target_pairs={{0,1},{1,0},{2,3},{3,2},{4,5},{5,4},{6,7},{7,6},{8,9},{9,8},{10,11... | collective-permute-start | bytes 1376264 | tf_op jit(solution)/shard_map/ppermute | solution.py:18
  171.6 5.2 %collective-permute-start.44 = (bf16[64,3584]{1,0:T(8,128)(2,1)}, bf16[64,3584]{1,0:T(8,128)(2,1)S(1)}, u32[]{:S(2)}, u32[]{:S(2)}) collective-permute-start(bf16[64,3584]{1,0:T(8,128)(2,1)} %copy-done.10), channel_id=1, source_target_pairs={{0,1},{1,0},{2,3},{3,2},{4,5},{5,4},{6,7},{7,6},{8,9},{9,8},{10,11... | collective-permute-start | bytes 1376264 | tf_op jit(solution)/shard_map/ppermute | solution.py:18
  176.9 17.5 %copy-start.1 = (bf16[7168,64]{0,1:T(8,128)(2,1)S(1)}, bf16[7168,64]{0,1:T(8,128)(2,1)}, u32[]{:S(2)}) copy-start(bf16[7168,64]{0,1:T(8,128)(2,1)} %param.10) | copy-start | bytes 2752516
  (34 other events, 59.2 us)

commit v8 on v7

--- a/solution.py
+++ b/solution.py
@@ -132,8 +132,7 @@
         grid_spec=pltpu.PrefetchScalarGridSpec(
             num_scalar_prefetch=1,
             grid=(cols // tile,),
-            in_specs=[pl.BlockSpec(memory_space=pl.ANY)] * len(blocks)
-            + [pl.BlockSpec(memory_space=pltpu.HBM)]
+            in_specs=[pl.BlockSpec(memory_space=pltpu.HBM)] * (len(blocks) + 1)
             + [pl.BlockSpec(memory_space=pltpu.VMEM)] * len(adds),
             out_specs=[pl.BlockSpec((tall, tile), lambda j, place: (0, j)) for tall in outs],
             scratch_shapes=[
@@ -145,7 +144,7 @@
         ),
         compiler_params=pltpu.CompilerParams(vmem_limit_bytes=24 << 20),
         cost_estimate=pl.CostEstimate(
-            flops=8 * rows * size * width * cols, bytes_accessed=1000, transcendentals=0
+            flops=rows * size * width * cols // 4, bytes_accessed=1000, transcendentals=0
         ),
         name="terms",
     )(
@@ -318,7 +317,6 @@
     first, last, kept = far_terms([blocks], 0, *later)
     pair0, sum0 = pair_sum(first, last, kept)
 
-    low = low + across(after(low, pair0), 2)
     later = spread_last(later, pair0)
     beside = spread_first(after(beside, pair0))
     first, last, kept = far_terms([blocks], 1, pair0)
@@ -331,7 +329,8 @@
 
     own = spread_last(own, pair2)
     near0 = [swap(after(term, sum1, pair2), 1) for term in near0]
-    acts_low, grads_low = jnp.split(after(low, pair2, sum1), 2, axis=1)
+    partner = across(after(low, pair0), 2)
+    acts_low, grads_low = jnp.split(after(low, pair2, sum1) + partner, 2, axis=1)
     example_grad = example_gradients(
         acts_low, grads_low, token_example[0], example_group.shape[0]
     )

time: 195 us -> 178 us (0.913)
  local copies, waits for them, and re-layouts: 28.7 us -> 8.22 us
  Pallas kernels: 58.5 us -> 62.5 us
  starting transfers between devices: 48.2 us -> 46 us
  waiting for transfers between devices: 48.1 us -> 50.1 us
    unnamed x105 -> x41, local copies, waits for them, and re-layouts: 24.9 us -> 3.77 us
    pallas_call x4, Pallas kernels: 2.15 us -> 5.66 us  [add_halves(): pl.pallas_call(add_kernel, out_shape=jax.ShapeDtypeStruct((rows, cols), b...]
  transfers between devices with their start and end apart: 46 -> 46, of which waited for: 14 -> 16; matrix products, arithmetic and copies ran while one was open for 6% -> 6% of each run, Pallas kernels for 25% -> 29%
where the time goes in v8:
time: 178 us; the launch traced here: 177 us
  Pallas kernels  62.5 us (35%)
  waiting for transfers between devices  50.1 us (28%)
  starting transfers between devices  46 us (26%)
  local copies, waits for them, and re-layouts  8.22 us (5%)
  matrix products  7.54 us (4%)
    pallas_call x5, Pallas kernels, block_terms(): pl.pallas_call(functools.partial(terms_kernel, size, len(groups), col_sta...  54.8 us
    ppermute x18, waiting for transfers between devices, across(): return lax.ppermute(value, 'tensor', pairs)  41.9 us
    ppermute x18, starting transfers between devices, across(): return lax.ppermute(value, 'tensor', pairs)  30.9 us
    ppermute x28, starting transfers between devices, swap(): return lax.ppermute(value, 'dp', [(d, d ^ step) for d in range(size)])  15.1 us
    ppermute x28, waiting for transfers between devices, swap(): return lax.ppermute(value, 'dp', [(d, d ^ step) for d in range(size)])  8.24 us
    pallas_call x4, Pallas kernels, add_halves(): pl.pallas_call(add_kernel, out_shape=jax.ShapeDtypeStruct((rows, cols), b...  5.66 us
    unnamed x41, local copies, waits for them, and re-layouts  3.77 us
    another operation x5, local copies, waits for them, and re-layouts  3.57 us
  transfers between devices with their start and end apart: 46, of which 16 were waited for; matrix products, arithmetic and copies ran while one was open for 6% of the time, Pallas kernels for 29%

profile of v8, /device:TPU:0, one launch (start us, length us, event | category | flops | bytes accessed | tf_op | source)
XLA Modules:
  0.0 177.2 jit_solution(17713947336959546047)
XLA Ops:
  0.7 2.1 %constant_dynamic-slice_fusion = (bf16[1,1,512,256]{3,2,1,0:T(8,128)(2,1)S(1)}, bf16[1,1,512,256]{3,2,1,0:T(8,128)(2,1)S(1)}, bf16[1,1,512,256]{3,2,1,0:T(8,128)(2,1)S(1)}, bf16[1,1,512,256]{3,2,1,0:T(8,128)(2,1)}) fusion(bf16[1,4,512,256]{3,2,1,0:T(8,128)(2,1)} %param.8, s32[]{:T(128)S(6)} %select_n.96, s32[]{:T(128)S(6)} %select_n.95, s32[]{:T(128)S(6)} %select_n.94, ...), kind=kLoop, calls=%fused_computation.33 | loop fusion | bytes 2097168 | tf_op jit(solution)/shard_map/dynamic-slice.7
  2.9 0.7 slice_bitcast_fusion
  3.6 2.9 %collective-permute-start.1 = (bf16[128,512]{1,0:T(8,128)(2,1)}, bf16[128,512]{1,0:T(8,128)(2,1)}, u32[]{:S(2)}, u32[]{:S(2)}) collective-permute-start(bf16[128,512]{1,0:T(8,128)(2,1)} %get-tuple-element.124), channel_id=1, source_target_pairs={{0,2},{1,3},{2,0},{3,1},{4,6},{5,7},{6,4},{7,5},{8,10},{9,11},{10,... | collective-permute-start | bytes 393224 | tf_op jit(solution)/shard_map/ppermute | solution.py:18
  6.7 1.7 collective-permute-start
  8.5 3.3 %fusion.15 = f32[256,64]{0,1:T(8,128)S(1)} fusion(bf16[256,7168]{1,0:T(8,128)(2,1)} %param.7, bf16[7168,64]{0,1:T(8,128)(2,1)S(1)} %copy-done), kind=kOutput, calls=%fused_computation.39 | convolution fusion | flops 234881024 | bytes 4653056 | tf_op jit(solution)/shard_map/dot_general | solution.py:258
  12.1 1.6 collective-permute-start.8
  13.7 0.5 collective-permute-start.3
  14.5 1.5 collective-permute-done
  16.0 0.9 pad_maximum_fusion.refs_0_
  17.0 1.8 %collective-permute-start.7 = (bf16[256,512]{1,0:T(8,128)(2,1)S(1)}, bf16[256,512]{1,0:T(8,128)(2,1)S(1)}, u32[]{:S(2)}, u32[]{:S(2)}) collective-permute-start(bf16[256,512]{1,0:T(8,128)(2,1)S(1)} %pad_maximum_fusion.refs_0_), channel_id=1, source_target_pairs={{0,4},{4,0},{8,12},{12,8},{1,5},{5,1},{9,13},{13,9},{2,6},{6,2},{1... | collective-permute-start | bytes 786440 | tf_op jit(solution)/shard_map/ppermute | solution.py:28
  18.8 2.6 %collective-permute-start.4 = (bf16[256,512]{1,0:T(8,128)(2,1)S(1)}, bf16[256,512]{1,0:T(8,128)(2,1)S(1)}, u32[]{:S(2)}, u32[]{:S(2)}) collective-permute-start(bf16[256,512]{1,0:T(8,128)(2,1)S(1)} %pad_maximum_fusion.refs_0_), channel_id=1, source_target_pairs={{0,8},{4,12},{8,0},{12,4},{1,9},{5,13},{9,1},{13,5},{2,10},{6,14},... | collective-permute-start | bytes 786440 | tf_op jit(solution)/shard_map/ppermute | solution.py:28
  21.5 12.5 %collective-permute-done.4.refs_2_ = bf16[256,512]{1,0:T(8,128)(2,1)S(1)} collective-permute-done((bf16[256,512]{1,0:T(8,128)(2,1)S(1)}, bf16[256,512]{1,0:T(8,128)(2,1)S(1)}, u32[]{:S(2)}, u32[]{:S(2)}) %collective-permute-start.4) | collective-permute-done | bytes 262176 | tf_op jit(solution)/shard_map/ppermute | solution.py:28
  34.3 2.6 %collective-permute-start.5 = (bf16[256,512]{1,0:T(8,128)(2,1)S(1)}, bf16[256,512]{1,0:T(8,128)(2,1)S(1)}, u32[]{:S(2)}, u32[]{:S(2)}) collective-permute-start(bf16[256,512]{1,0:T(8,128)(2,1)S(1)} %constant_dynamic-update-slice_fusion.refs_0_), channel_id=1, source_target_pairs={{0,4},{4,0},{8,12},{12,8},{1,5},{5,1},{9,13},{13,9},{2,6},{6,2},{1... | collective-permute-start | bytes 786440 | tf_op jit(solution)/shard_map/ppermute | solution.py:28
  36.9 0.7 collective-permute-start.10
  37.6 1.3 collective-permute-start.11
  38.9 9.5 %collective-permute-done.6.refs_2_ = bf16[256,512]{1,0:T(8,128)(2,1)S(1)} collective-permute-done((bf16[256,512]{1,0:T(8,128)(2,1)S(1)}, bf16[256,512]{1,0:T(8,128)(2,1)S(1)}, u32[]{:S(2)}, u32[]{:S(2)}) %collective-permute-start.6) | collective-permute-done | bytes 262176 | tf_op jit(solution)/shard_map/ppermute | solution.py:28
  48.4 3.5 %collective-permute-done.11.refs_4_ = bf16[256,512]{1,0:T(8,128)(2,1)S(1)} collective-permute-done((bf16[256,512]{1,0:T(8,128)(2,1)S(1)}, bf16[256,512]{1,0:T(8,128)(2,1)S(1)}, u32[]{:S(2)}, u32[]{:S(2)}) %collective-permute-start.11) | collective-permute-done | bytes 262176 | tf_op jit(solution)/shard_map/ppermute | solution.py:28
  51.9 6.9 %terms.5 = (bf16[64,3584]{1,0:T(8,128)(2,1)S(1)}, bf16[64,3584]{1,0:T(8,128)(2,1)S(1)}, bf16[128,3584]{1,0:T(8,128)(2,1)S(1)}) custom-call(s32[1]{0:T(128)} %bitcast.place_ref, bf16[256,512]{1,0:T(8,128)(2,1)S(1)} %pad_maximum_fusion.refs_0_, bf16[256,512]{1,0:T(8,128)(2,1)S(1)} %collective-permute-done.7.refs_1_, ...), custom_call_target="tpu_custom_call" | custom-call | flops 469762048 | bytes 1000 | tf_op jit(solution)/shard_map/terms/pallas_call | solution.py:122
  58.9 0.5 collective-permute-start.13
  59.4 1.3 collective-permute-done.12.first_ref
  60.7 0.7 collective-permute-done.13.second_ref
  61.4 1.7 pair.4
  63.3 0.7 collective-permute-start.14
  64.0 1.3 collective-permute-start.15
  65.3 5.5 %collective-permute-start.17 = (bf16[256,512]{1,0:T(8,128)(2,1)S(1)}, bf16[256,512]{1,0:T(8,128)(2,1)S(1)}, u32[]{:S(2)}, u32[]{:S(2)}) collective-permute-start(bf16[256,512]{1,0:T(8,128)(2,1)S(1)} %collective-permute-done.9.refs_5_), channel_id=1, source_target_pairs={{0,8},{4,12},{8,0},{12,4},{1,9},{5,13},{9,1},{13,5},{2,10},{6,14},... | collective-permute-start | bytes 786440 | tf_op jit(solution)/shard_map/ppermute | solution.py:28
  70.8 6.9 %terms.6 = (bf16[64,3584]{1,0:T(8,128)(2,1)S(1)}, bf16[64,3584]{1,0:T(8,128)(2,1)S(1)}, bf16[128,3584]{1,0:T(8,128)(2,1)S(1)}) custom-call(s32[1]{0:T(128)} %bitcast.place_ref, bf16[256,512]{1,0:T(8,128)(2,1)S(1)} %pad_maximum_fusion.refs_0_, bf16[256,512]{1,0:T(8,128)(2,1)S(1)} %collective-permute-done.7.refs_1_, ...), custom_call_target="tpu_custom_call" | custom-call | flops 469762048 | bytes 1000 | tf_op jit(solution)/shard_map/terms/pallas_call | solution.py:122
  77.7 7.9 %collective-permute-done.17.refs_7_ = bf16[256,512]{1,0:T(8,128)(2,1)S(1)} collective-permute-done((bf16[256,512]{1,0:T(8,128)(2,1)S(1)}, bf16[256,512]{1,0:T(8,128)(2,1)S(1)}, u32[]{:S(2)}, u32[]{:S(2)}) %collective-permute-start.17) | collective-permute-done | bytes 262176 | tf_op jit(solution)/shard_map/ppermute | solution.py:28
  85.6 1.5 collective-permute-done.16.refs_6_
  87.1 0.5 collective-permute-start.18
  87.6 1.3 collective-permute-done.19.second_ref
  88.9 0.7 collective-permute-done.18.first_ref
  89.6 1.7 pair.5
  91.3 1.5 collective-permute-start.27
  92.8 0.7 collective-permute-start.21
  93.5 1.3 collective-permute-start.22
  94.8 1.1 copy.21
  95.9 3.2 %collective-permute-start.24 = (bf16[256,512]{1,0:T(8,128)(2,1)S(1)}, bf16[256,512]{1,0:T(8,128)(2,1)}, u32[]{:S(2)}, u32[]{:S(2)}) collective-permute-start(bf16[256,512]{1,0:T(8,128)(2,1)S(1)} %bitcast.38), channel_id=1, source_target_pairs={{0,8},{4,12},{8,0},{12,4},{1,9},{5,13},{9,1},{13,5},{2,10},{6,14},... | collective-permute-start | bytes 786440 | tf_op jit(solution)/shard_map/ppermute | solution.py:28
  99.2 5.8 %collective-permute-done.22.refs_9_ = bf16[256,512]{1,0:T(8,128)(2,1)S(1)} collective-permute-done((bf16[256,512]{1,0:T(8,128)(2,1)S(1)}, bf16[256,512]{1,0:T(8,128)(2,1)S(1)}, u32[]{:S(2)}, u32[]{:S(2)}) %collective-permute-start.22) | collective-permute-done | bytes 262176 | tf_op jit(solution)/shard_map/ppermute | solution.py:28
  104.9 11.7 %terms.7 = (bf16[64,3584]{1,0:T(8,128)(2,1)S(1)}, bf16[64,3584]{1,0:T(8,128)(2,1)S(1)}, bf16[128,3584]{1,0:T(8,128)(2,1)S(1)}, bf16[64,3584]{1,0:T(8,128)(2,1)},...) custom-call(s32[1]{0:T(128)} %bitcast.place_ref, ...), custom_call_target="tpu_custom_call" | custom-call | flops 939524096 | bytes 1000 | tf_op jit(solution)/shard_map/terms/pallas_call | solution.py:122
  116.7 0.5 collective-permute-start.25
  117.2 4.7 %collective-permute-start.28 = (f32[256,128]{0,1:T(8,128)S(1)}, f32[256,128]{0,1:T(8,128)S(1)}, u32[]{:S(2)}, u32[]{:S(2)}) collective-permute-start(f32[256,128]{0,1:T(8,128)S(1)} %fusion.14), channel_id=1, source_target_pairs={{0,8},{4,12},{8,0},{12,4},{1,9},{5,13},{9,1},{13,5},{2,10},{6,14},... | collective-permute-start | bytes 393224 | tf_op jit(solution)/shard_map/ppermute | solution.py:28
  122.0 1.7 pair.6
  123.7 0.9 collective-permute-start.32
  124.6 1.4 collective-permute-start.37
  126.0 1.3 collective-permute-start.38
  127.3 1.1 collective-permute-done.28
  128.6 0.5 collective-permute-start.34
  129.5 1.0 collective-permute-done.33.refs_6_
  130.7 0.7 collective-permute-done.34.refs_7_
  131.6 1.0 collective-permute-done.35.refs_8_
  132.6 0.8 copy-done.4
  133.4 0.8 copy-done.6
  134.2 11.5 %terms.8 = (bf16[64,3584]{1,0:T(8,128)(2,1)}, bf16[64,3584]{1,0:T(8,128)(2,1)S(1)}, bf16[128,3584]{1,0:T(8,128)(2,1)S(1)}, bf16[64,3584]{1,0:T(8,128)(2,1)S(1)},...) custom-call(s32[1]{0:T(128)} %bitcast.place_ref, ...), custom_call_target="tpu_custom_call" | custom-call | flops 939524096 | bytes 1000 | tf_op jit(solution)/shard_map/terms/pallas_call | solution.py:122
  145.7 0.9 copy-done.2
  147.3 0.7 collective-permute-start.31
  148.0 1.2 collective-permute-start.30
  149.4 1.2 copy-done.3
  150.6 0.5 pair.7
  151.1 1.0 collective-permute-start.45
  152.2 0.4 collective-permute-start.42
  153.5 2.7 %fusion.4 = f32[1024,1024]{1,0:T(8,128)} fusion(bf16[16,4224]{1,0:T(8,128)(2,1)S(1)} %pad_maximum_fusion.1, s32[]{:T(128)S(6)} %select_n.121, s32[]{:T(128)S(6)} %select_n.122), kind=kOutput, calls=%fused_computation.19 | convolution fusion | flops 33554432 | bytes 4259848 | tf_op jit(solution)/shard_map/dot_general | solution.py:247
  156.2 0.9 fusion.6
  157.2 17.9 %terms.9.own_ref = bf16[256,7168]{1,0:T(8,128)(2,1)} custom-call(s32[1]{0:T(128)} %bitcast.place_ref, bf16[256,512]{1,0:T(8,128)(2,1)S(1)} %bitcast.41, bf16[256,512]{1,0:T(8,128)(2,1)S(1)} %copy-done.9, bf16[256,512]{1,0:T(8,128)(2,1)} %collective-permute-done.24.refs_2_, bf16[256,512]{1,0:T(8,128)(2,1)} %collective-permute-done.37.refs_3_, ...), custom_call_target="tpu_custom_call" | custom-call | flops 939524096 | bytes 1000 | tf_op jit(solution)/shard_map/terms/pallas_call | solution.py:122
  175.1 2.1 %finish.1 = bf16[256,7168]{1,0:T(8,128)(2,1)} custom-call(bf16[256,7168]{1,0:T(8,128)(2,1)} %terms.9.own_ref, bf16[128,3584]{1,0:T(8,128)(2,1)S(1)} %collective-permute-done.45.other_ref), custom_call_target="tpu_custom_call", output_to_operand_aliasing={{}: (0, {})} | custom-call | flops 1000 | bytes 1000 | tf_op jit(solution)/shard_map/finish/pallas_call | solution.py:192
  (108 shorter events, 4.7 us)
Async XLA Ops:
  0.6 7.9 %copy-start = (bf16[7168,64]{0,1:T(8,128)(2,1)S(1)}, bf16[7168,64]{0,1:T(8,128)(2,1)}, u32[]{:S(2)}) copy-start(bf16[7168,64]{0,1:T(8,128)(2,1)} %param.10) | copy-start | bytes 2752516
  2.7 9.0 %copy-start.16 = (bf16[1,4,512,256]{3,2,1,0:T(8,128)(2,1)S(1)}, bf16[1,4,512,256]{3,2,1,0:T(8,128)(2,1)}, u32[]{:S(2)}) copy-start(bf16[1,4,512,256]{3,2,1,0:T(8,128)(2,1)} %param.8) | copy-start | bytes 3145732
  2.7 9.0 %copy-start.17 = (bf16[1,4,512,64]{2,3,1,0:T(8,128)(2,1)S(1)}, bf16[1,4,512,64]{2,3,1,0:T(8,128)(2,1)}, u32[]{:S(2)}) copy-start(bf16[1,4,512,64]{2,3,1,0:T(8,128)(2,1)} %param.11) | copy-start | bytes 786436
  3.6 10.9 %collective-permute-start.1 = (bf16[128,512]{1,0:T(8,128)(2,1)}, bf16[128,512]{1,0:T(8,128)(2,1)}, u32[]{:S(2)}, u32[]{:S(2)}) collective-permute-start(bf16[128,512]{1,0:T(8,128)(2,1)} %get-tuple-element.124), channel_id=1, source_target_pairs={{0,2},{1,3},{2,0},{3,1},{4,6},{5,7},{6,4},{7,5},{8,10},{9,11},{10,... | collective-permute-start | bytes 393224 | tf_op jit(solution)/shard_map/ppermute | solution.py:18
  6.7 12.1 %collective-permute-start.2 = (bf16[128,512]{1,0:T(8,128)(2,1)S(1)}, bf16[128,512]{1,0:T(8,128)(2,1)S(1)}, u32[]{:S(2)}, u32[]{:S(2)}) collective-permute-start(bf16[128,512]{1,0:T(8,128)(2,1)S(1)} %get-tuple-element.125), channel_id=1, source_target_pairs={{0,3},{1,2},{2,1},{3,0},{4,7},{5,6},{6,5},{7,4},{8,11},{9,10},{10,... | collective-permute-start | bytes 393224 | tf_op jit(solution)/shard_map/ppermute | solution.py:18
  6.7 9.3 %collective-permute-start = (bf16[128,512]{1,0:T(8,128)(2,1)S(1)}, bf16[128,512]{1,0:T(8,128)(2,1)S(1)}, u32[]{:S(2)}, u32[]{:S(2)}) collective-permute-start(bf16[128,512]{1,0:T(8,128)(2,1)S(1)} %get-tuple-element.126), channel_id=1, source_target_pairs={{0,3},{1,2},{2,1},{3,0},{4,7},{5,6},{6,5},{7,4},{8,11},{9,10},{10,... | collective-permute-start | bytes 393224 | tf_op jit(solution)/shard_map/ppermute | solution.py:18
  12.1 9.3 %collective-permute-start.8 = (f32[256,128]{0,1:T(8,128)S(1)}, f32[256,128]{0,1:T(8,128)S(1)}, u32[]{:S(2)}, u32[]{:S(2)}) collective-permute-start(f32[256,128]{0,1:T(8,128)S(1)} %pad_maximum_fusion.2), channel_id=1, source_target_pairs={{0,4},{4,0},{8,12},{12,8},{1,5},{5,1},{9,13},{13,9},{2,6},{6,2},{1... | collective-permute-start | bytes 393224 | tf_op jit(solution)/shard_map/ppermute | solution.py:28
  13.7 7.7 %collective-permute-start.3 = (bf16[128,512]{1,0:T(8,128)(2,1)S(1)}, bf16[128,512]{1,0:T(8,128)(2,1)S(1)}, u32[]{:S(2)}, u32[]{:S(2)}) collective-permute-start(bf16[128,512]{1,0:T(8,128)(2,1)S(1)} %get-tuple-element.123), channel_id=1, source_target_pairs={{0,2},{1,3},{2,0},{3,1},{4,6},{5,7},{6,4},{7,5},{8,10},{9,11},{10,... | collective-permute-start | bytes 393224 | tf_op jit(solution)/shard_map/ppermute | solution.py:18
  14.4 22.5 %collective-permute-start.9 = (bf16[256,512]{1,0:T(8,128)(2,1)S(1)}, bf16[256,512]{1,0:T(8,128)(2,1)S(1)}, u32[]{:S(2)}, u32[]{:S(2)}) collective-permute-start(bf16[256,512]{1,0:T(8,128)(2,1)S(1)} %bitcast.45), channel_id=1, source_target_pairs={{0,1},{1,0},{2,3},{3,2},{4,5},{5,4},{6,7},{7,6},{8,9},{9,8},{10,11... | collective-permute-start | bytes 786440 | tf_op jit(solution)/shard_map/ppermute | solution.py:18
  17.0 31.4 %collective-permute-start.7 = (bf16[256,512]{1,0:T(8,128)(2,1)S(1)}, bf16[256,512]{1,0:T(8,128)(2,1)S(1)}, u32[]{:S(2)}, u32[]{:S(2)}) collective-permute-start(bf16[256,512]{1,0:T(8,128)(2,1)S(1)} %pad_maximum_fusion.refs_0_), channel_id=1, source_target_pairs={{0,4},{4,0},{8,12},{12,8},{1,5},{5,1},{9,13},{13,9},{2,6},{6,2},{1... | collective-permute-start | bytes 786440 | tf_op jit(solution)/shard_map/ppermute | solution.py:28
  18.8 15.2 %collective-permute-start.4 = (bf16[256,512]{1,0:T(8,128)(2,1)S(1)}, bf16[256,512]{1,0:T(8,128)(2,1)S(1)}, u32[]{:S(2)}, u32[]{:S(2)}) collective-permute-start(bf16[256,512]{1,0:T(8,128)(2,1)S(1)} %pad_maximum_fusion.refs_0_), channel_id=1, source_target_pairs={{0,8},{4,12},{8,0},{12,4},{1,9},{5,13},{9,1},{13,5},{2,10},{6,14},... | collective-permute-start | bytes 786440 | tf_op jit(solution)/shard_map/ppermute | solution.py:28
  34.0 14.4 %collective-permute-start.6 = (bf16[256,512]{1,0:T(8,128)(2,1)S(1)}, bf16[256,512]{1,0:T(8,128)(2,1)S(1)}, u32[]{:S(2)}, u32[]{:S(2)}) collective-permute-start(bf16[256,512]{1,0:T(8,128)(2,1)S(1)} %constant_dynamic-update-slice_fusion.refs_0_), channel_id=1, source_target_pairs={{0,8},{4,12},{8,0},{12,4},{1,9},{5,13},{9,1},{13,5},{2,10},{6,14},... | collective-permute-start | bytes 786440 | tf_op jit(solution)/shard_map/ppermute | solution.py:28
  34.3 14.1 %collective-permute-start.5 = (bf16[256,512]{1,0:T(8,128)(2,1)S(1)}, bf16[256,512]{1,0:T(8,128)(2,1)S(1)}, u32[]{:S(2)}, u32[]{:S(2)}) collective-permute-start(bf16[256,512]{1,0:T(8,128)(2,1)S(1)} %constant_dynamic-update-slice_fusion.refs_0_), channel_id=1, source_target_pairs={{0,4},{4,0},{8,12},{12,8},{1,5},{5,1},{9,13},{13,9},{2,6},{6,2},{1... | collective-permute-start | bytes 786440 | tf_op jit(solution)/shard_map/ppermute | solution.py:28
  36.9 11.5 %collective-permute-start.10 = (bf16[256,512]{1,0:T(8,128)(2,1)S(1)}, bf16[256,512]{1,0:T(8,128)(2,1)S(1)}, u32[]{:S(2)}, u32[]{:S(2)}) collective-permute-start(bf16[256,512]{1,0:T(8,128)(2,1)S(1)} %pad_maximum_fusion.refs_0_), channel_id=1, source_target_pairs={{4,8},{8,4},{5,9},{9,5},{6,10},{10,6},{7,11},{11,7},{20,24},{24,20... | collective-permute-start | bytes 786440 | tf_op jit(solution)/shard_map/ppermute | solution.py:28
  37.6 14.3 %collective-permute-start.11 = (bf16[256,512]{1,0:T(8,128)(2,1)S(1)}, bf16[256,512]{1,0:T(8,128)(2,1)S(1)}, u32[]{:S(2)}, u32[]{:S(2)}) collective-permute-start(bf16[256,512]{1,0:T(8,128)(2,1)S(1)} %collective-permute-done.4.refs_2_), channel_id=1, source_target_pairs={{4,0},{8,12},{5,1},{9,13},{6,2},{10,14},{7,3},{11,15},{20,16},{24,... | collective-permute-start | bytes 786440 | tf_op jit(solution)/shard_map/ppermute | solution.py:28
  58.8 1.9 %collective-permute-start.12 = (bf16[64,3584]{1,0:T(8,128)(2,1)S(1)}, bf16[64,3584]{1,0:T(8,128)(2,1)S(1)}, u32[]{:S(2)}, u32[]{:S(2)}) collective-permute-start(bf16[64,3584]{1,0:T(8,128)(2,1)S(1)} %get-tuple-element.67), channel_id=1, source_target_pairs={{0,1},{1,0},{2,3},{3,2},{4,5},{5,4},{6,7},{7,6},{8,9},{9,8},{10,11... | collective-permute-start | bytes 1376264 | tf_op jit(solution)/shard_map/ppermute | solution.py:18
  58.9 2.5 %collective-permute-start.13 = (bf16[64,3584]{1,0:T(8,128)(2,1)S(1)}, bf16[64,3584]{1,0:T(8,128)(2,1)S(1)}, u32[]{:S(2)}, u32[]{:S(2)}) collective-permute-start(bf16[64,3584]{1,0:T(8,128)(2,1)S(1)} %get-tuple-element.68), channel_id=1, source_target_pairs={{0,1},{1,0},{2,3},{3,2},{4,5},{5,4},{6,7},{7,6},{8,9},{9,8},{10,11... | collective-permute-start | bytes 1376264 | tf_op jit(solution)/shard_map/ppermute | solution.py:18
  63.1 36.1 %collective-permute-start.20 = (bf16[128,3584]{1,0:T(8,128)(2,1)}, bf16[128,3584]{1,0:T(8,128)(2,1)}, u32[]{:S(2)}, u32[]{:S(2)}) collective-permute-start(bf16[128,3584]{1,0:T(8,128)(2,1)} %pair.4), channel_id=1, source_target_pairs={{0,2},{1,3},{2,0},{3,1},{4,6},{5,7},{6,4},{7,5},{8,10},{9,11},{10,... | collective-permute-start | bytes 2752520 | tf_op jit(solution)/shard_map/ppermute | solution.py:18
  63.3 14.4 %collective-permute-start.14 = (bf16[256,512]{1,0:T(8,128)(2,1)S(1)}, bf16[256,512]{1,0:T(8,128)(2,1)S(1)}, u32[]{:S(2)}, u32[]{:S(2)}) collective-permute-start(bf16[256,512]{1,0:T(8,128)(2,1)S(1)} %constant_dynamic-update-slice_fusion.refs_0_), channel_id=1, source_target_pairs={{4,8},{8,4},{5,9},{9,5},{6,10},{10,6},{7,11},{11,7},{20,24},{24,20... | collective-permute-start | bytes 786440 | tf_op jit(solution)/shard_map/ppermute | solution.py:28
  64.0 13.7 %collective-permute-start.15 = (bf16[256,512]{1,0:T(8,128)(2,1)S(1)}, bf16[256,512]{1,0:T(8,128)(2,1)S(1)}, u32[]{:S(2)}, u32[]{:S(2)}) collective-permute-start(bf16[256,512]{1,0:T(8,128)(2,1)S(1)} %collective-permute-done.6.refs_2_), channel_id=1, source_target_pairs={{4,0},{8,12},{5,1},{9,13},{6,2},{10,14},{7,3},{11,15},{20,16},{24,... | collective-permute-start | bytes 786440 | tf_op jit(solution)/shard_map/ppermute | solution.py:28
  65.3 20.4 %collective-permute-start.17 = (bf16[256,512]{1,0:T(8,128)(2,1)S(1)}, bf16[256,512]{1,0:T(8,128)(2,1)S(1)}, u32[]{:S(2)}, u32[]{:S(2)}) collective-permute-start(bf16[256,512]{1,0:T(8,128)(2,1)S(1)} %collective-permute-done.9.refs_5_), channel_id=1, source_target_pairs={{0,8},{4,12},{8,0},{12,4},{1,9},{5,13},{9,1},{13,5},{2,10},{6,14},... | collective-permute-start | bytes 786440 | tf_op jit(solution)/shard_map/ppermute | solution.py:28
  70.8 16.3 %collective-permute-start.16 = (bf16[256,512]{1,0:T(8,128)(2,1)S(1)}, bf16[256,512]{1,0:T(8,128)(2,1)S(1)}, u32[]{:S(2)}, u32[]{:S(2)}) collective-permute-start(bf16[256,512]{1,0:T(8,128)(2,1)S(1)} %collective-permute-done.9.refs_5_), channel_id=1, source_target_pairs={{0,4},{4,0},{8,12},{12,8},{1,5},{5,1},{9,13},{13,9},{2,6},{6,2},{1... | collective-permute-start | bytes 786440 | tf_op jit(solution)/shard_map/ppermute | solution.py:28
  87.1 1.8 %collective-permute-start.19 = (bf16[64,3584]{1,0:T(8,128)(2,1)S(1)}, bf16[64,3584]{1,0:T(8,128)(2,1)S(1)}, u32[]{:S(2)}, u32[]{:S(2)}) collective-permute-start(bf16[64,3584]{1,0:T(8,128)(2,1)S(1)} %get-tuple-element.77), channel_id=1, source_target_pairs={{0,1},{1,0},{2,3},{3,2},{4,5},{5,4},{6,7},{7,6},{8,9},{9,8},{10,11... | collective-permute-start | bytes 1376264 | tf_op jit(solution)/shard_map/ppermute | solution.py:18
  87.1 2.5 %collective-permute-start.18 = (bf16[64,3584]{1,0:T(8,128)(2,1)S(1)}, bf16[64,3584]{1,0:T(8,128)(2,1)S(1)}, u32[]{:S(2)}, u32[]{:S(2)}) collective-permute-start(bf16[64,3584]{1,0:T(8,128)(2,1)S(1)} %get-tuple-element.75), channel_id=1, source_target_pairs={{0,1},{1,0},{2,3},{3,2},{4,5},{5,4},{6,7},{7,6},{8,9},{9,8},{10,11... | collective-permute-start | bytes 1376264 | tf_op jit(solution)/shard_map/ppermute | solution.py:18
  91.3 36.0 %collective-permute-start.27 = (bf16[128,3584]{1,0:T(8,128)(2,1)}, bf16[128,3584]{1,0:T(8,128)(2,1)}, u32[]{:S(2)}, u32[]{:S(2)}) collective-permute-start(bf16[128,3584]{1,0:T(8,128)(2,1)} %pair.5), channel_id=1, source_target_pairs={{0,2},{1,3},{2,0},{3,1},{4,6},{5,7},{6,4},{7,5},{8,10},{9,11},{10,... | collective-permute-start | bytes 2752520 | tf_op jit(solution)/shard_map/ppermute | solution.py:18
  92.8 6.3 %collective-permute-start.21 = (bf16[256,512]{1,0:T(8,128)(2,1)S(1)}, bf16[256,512]{1,0:T(8,128)(2,1)S(1)}, u32[]{:S(2)}, u32[]{:S(2)}) collective-permute-start(bf16[256,512]{1,0:T(8,128)(2,1)S(1)} %collective-permute-done.9.refs_5_), channel_id=1, source_target_pairs={{4,8},{8,4},{5,9},{9,5},{6,10},{10,6},{7,11},{11,7},{20,24},{24,20... | collective-permute-start | bytes 786440 | tf_op jit(solution)/shard_map/ppermute | solution.py:28
  93.5 11.4 %collective-permute-start.22 = (bf16[256,512]{1,0:T(8,128)(2,1)S(1)}, bf16[256,512]{1,0:T(8,128)(2,1)S(1)}, u32[]{:S(2)}, u32[]{:S(2)}) collective-permute-start(bf16[256,512]{1,0:T(8,128)(2,1)S(1)} %collective-permute-done.17.refs_7_), channel_id=1, source_target_pairs={{4,0},{8,12},{5,1},{9,13},{6,2},{10,14},{7,3},{11,15},{20,16},{24,... | collective-permute-start | bytes 786440 | tf_op jit(solution)/shard_map/ppermute | solution.py:28
  95.9 26.0 %copy-start.18 = (s32[1,256]{1,0:T(1,128)S(1)}, s32[1,256]{1,0:T(1,128)}, u32[]{:S(2)}) copy-start(s32[1,256]{1,0:T(1,128)} %param.12) | copy-start | bytes 3076
  95.9 26.0 %copy-start.19 = (s32[4]{0:T(128)S(1)}, s32[4]{0:T(128)}, u32[]{:S(2)}) copy-start(s32[4]{0:T(128)} %param.13) | copy-start | bytes 52
  95.9 20.7 %collective-permute-start.24 = (bf16[256,512]{1,0:T(8,128)(2,1)S(1)}, bf16[256,512]{1,0:T(8,128)(2,1)}, u32[]{:S(2)}, u32[]{:S(2)}) collective-permute-start(bf16[256,512]{1,0:T(8,128)(2,1)S(1)} %bitcast.38), channel_id=1, source_target_pairs={{0,8},{4,12},{8,0},{12,4},{1,9},{5,13},{9,1},{13,5},{2,10},{6,14},... | collective-permute-start | bytes 786440 | tf_op jit(solution)/shard_map/ppermute | solution.py:28
  99.1 17.5 %collective-permute-start.23 = (bf16[256,512]{1,0:T(8,128)(2,1)S(1)}, bf16[256,512]{1,0:T(8,128)(2,1)S(1)}, u32[]{:S(2)}, u32[]{:S(2)}) collective-permute-start(bf16[256,512]{1,0:T(8,128)(2,1)S(1)} %bitcast.39), channel_id=1, source_target_pairs={{0,4},{4,0},{8,12},{12,8},{1,5},{5,1},{9,13},{13,9},{2,6},{6,2},{1... | collective-permute-start | bytes 786440 | tf_op jit(solution)/shard_map/ppermute | solution.py:28
  116.6 11.9 %copy-start.14 = (bf16[64,3584]{1,0:T(8,128)(2,1)}, bf16[64,3584]{1,0:T(8,128)(2,1)S(1)}, u32[]{:S(2)}) copy-start(bf16[64,3584]{1,0:T(8,128)(2,1)S(1)} %get-tuple-element.97) | copy-start | bytes 1376260
  116.6 12.0 %copy-start.15 = (bf16[64,3584]{1,0:T(8,128)(2,1)}, bf16[64,3584]{1,0:T(8,128)(2,1)S(1)}, u32[]{:S(2)}) copy-start(bf16[64,3584]{1,0:T(8,128)(2,1)S(1)} %get-tuple-element.95) | copy-start | bytes 1376260
  116.6 11.8 %copy-start.8 = (bf16[256,512]{1,0:T(8,128)(2,1)}, bf16[256,512]{1,0:T(8,128)(2,1)S(1)}, u32[]{:S(2)}) copy-start(bf16[256,512]{1,0:T(8,128)(2,1)S(1)} %collective-permute-done.23.refs_1_) | copy-start | bytes 786436
  116.6 5.4 %collective-permute-start.26 = (bf16[64,3584]{1,0:T(8,128)(2,1)S(1)}, bf16[64,3584]{1,0:T(8,128)(2,1)S(1)}, u32[]{:S(2)}, u32[]{:S(2)}) collective-permute-start(bf16[64,3584]{1,0:T(8,128)(2,1)S(1)} %get-tuple-element.87), channel_id=1, source_target_pairs={{0,1},{1,0},{2,3},{3,2},{4,5},{5,4},{6,7},{7,6},{8,9},{9,8},{10,11... | collective-permute-start | bytes 1376264 | tf_op jit(solution)/shard_map/ppermute | solution.py:18
  116.7 5.3 %collective-permute-start.25 = (bf16[64,3584]{1,0:T(8,128)(2,1)S(1)}, bf16[64,3584]{1,0:T(8,128)(2,1)S(1)}, u32[]{:S(2)}, u32[]{:S(2)}) collective-permute-start(bf16[64,3584]{1,0:T(8,128)(2,1)S(1)} %get-tuple-element.85), channel_id=1, source_target_pairs={{0,1},{1,0},{2,3},{3,2},{4,5},{5,4},{6,7},{7,6},{8,9},{9,8},{10,11... | collective-permute-start | bytes 1376264 | tf_op jit(solution)/shard_map/ppermute | solution.py:18
  117.2 11.2 %collective-permute-start.28 = (f32[256,128]{0,1:T(8,128)S(1)}, f32[256,128]{0,1:T(8,128)S(1)}, u32[]{:S(2)}, u32[]{:S(2)}) collective-permute-start(f32[256,128]{0,1:T(8,128)S(1)} %fusion.14), channel_id=1, source_target_pairs={{0,8},{4,12},{8,0},{12,4},{1,9},{5,13},{9,1},{13,5},{2,10},{6,14},... | collective-permute-start | bytes 393224 | tf_op jit(solution)/shard_map/ppermute | solution.py:28
  123.7 28.3 %collective-permute-start.32 = (bf16[128,3584]{1,0:T(8,128)(2,1)}, bf16[128,3584]{1,0:T(8,128)(2,1)}, u32[]{:S(2)}, u32[]{:S(2)}) collective-permute-start(bf16[128,3584]{1,0:T(8,128)(2,1)} %pair.6), channel_id=1, source_target_pairs={{0,2},{1,3},{2,0},{3,1},{4,6},{5,7},{6,4},{7,5},{8,10},{9,11},{10,... | collective-permute-start | bytes 2752520 | tf_op jit(solution)/shard_map/ppermute | solution.py:18
  124.6 22.0 %collective-permute-start.37 = (bf16[256,512]{1,0:T(8,128)(2,1)S(1)}, bf16[256,512]{1,0:T(8,128)(2,1)}, u32[]{:S(2)}, u32[]{:S(2)}) collective-permute-start(bf16[256,512]{1,0:T(8,128)(2,1)S(1)} %bitcast.40), channel_id=1, source_target_pairs={{4,8},{8,4},{5,9},{9,5},{6,10},{10,6},{7,11},{11,7},{20,24},{24,20... | collective-permute-start | bytes 786440 | tf_op jit(solution)/shard_map/ppermute | solution.py:28
  126.0 20.6 %collective-permute-start.38 = (bf16[256,512]{1,0:T(8,128)(2,1)}, bf16[256,512]{1,0:T(8,128)(2,1)}, u32[]{:S(2)}, u32[]{:S(2)}) collective-permute-start(bf16[256,512]{1,0:T(8,128)(2,1)} %collective-permute-done.24.refs_2_), channel_id=1, source_target_pairs={{4,0},{8,12},{5,1},{9,13},{6,2},{10,14},{7,3},{11,15},{20,16},{24,... | collective-permute-start | bytes 786440 | tf_op jit(solution)/shard_map/ppermute | solution.py:28
  128.5 2.1 %collective-permute-start.33 = (bf16[64,3584]{1,0:T(8,128)(2,1)}, bf16[64,3584]{1,0:T(8,128)(2,1)S(1)}, u32[]{:S(2)}, u32[]{:S(2)}) collective-permute-start(bf16[64,3584]{1,0:T(8,128)(2,1)} %get-tuple-element.91), channel_id=1, source_target_pairs={{0,1},{1,0},{2,3},{3,2},{4,5},{5,4},{6,7},{7,6},{8,9},{9,8},{10,11... | collective-permute-start | bytes 1376264 | tf_op jit(solution)/shard_map/ppermute | solution.py:18
  128.6 2.8 %collective-permute-start.34 = (bf16[64,3584]{1,0:T(8,128)(2,1)}, bf16[64,3584]{1,0:T(8,128)(2,1)}, u32[]{:S(2)}, u32[]{:S(2)}) collective-permute-start(bf16[64,3584]{1,0:T(8,128)(2,1)} %get-tuple-element.93), channel_id=1, source_target_pairs={{0,1},{1,0},{2,3},{3,2},{4,5},{5,4},{6,7},{7,6},{8,9},{9,8},{10,11... | collective-permute-start | bytes 1376264 | tf_op jit(solution)/shard_map/ppermute | solution.py:18
  130.6 2.0 %collective-permute-start.35 = (bf16[64,3584]{1,0:T(8,128)(2,1)}, bf16[64,3584]{1,0:T(8,128)(2,1)S(1)}, u32[]{:S(2)}, u32[]{:S(2)}) collective-permute-start(bf16[64,3584]{1,0:T(8,128)(2,1)} %copy-done.15), channel_id=1, source_target_pairs={{0,1},{1,0},{2,3},{3,2},{4,5},{5,4},{6,7},{7,6},{8,9},{9,8},{10,11... | collective-permute-start | bytes 1376264 | tf_op jit(solution)/shard_map/ppermute | solution.py:18
  131.4 2.0 %collective-permute-start.36 = (bf16[64,3584]{1,0:T(8,128)(2,1)}, bf16[64,3584]{1,0:T(8,128)(2,1)S(1)}, u32[]{:S(2)}, u32[]{:S(2)}) collective-permute-start(bf16[64,3584]{1,0:T(8,128)(2,1)} %copy-done.14), channel_id=1, source_target_pairs={{0,1},{1,0},{2,3},{3,2},{4,5},{5,4},{6,7},{7,6},{8,9},{9,8},{10,11... | collective-permute-start | bytes 1376264 | tf_op jit(solution)/shard_map/ppermute | solution.py:18
  145.7 0.9 copy-start.2
  146.6 2.6 %copy-start.10 = (bf16[64,3584]{1,0:T(8,128)(2,1)}, bf16[64,3584]{1,0:T(8,128)(2,1)S(1)}, u32[]{:S(2)}) copy-start(bf16[64,3584]{1,0:T(8,128)(2,1)S(1)} %get-tuple-element.118) | copy-start | bytes 1376260
  146.6 2.6 %copy-start.11 = (bf16[64,3584]{1,0:T(8,128)(2,1)}, bf16[64,3584]{1,0:T(8,128)(2,1)S(1)}, u32[]{:S(2)}) copy-start(bf16[64,3584]{1,0:T(8,128)(2,1)S(1)} %get-tuple-element.116) | copy-start | bytes 1376260
  146.6 2.6 %copy-start.12 = (bf16[64,3584]{1,0:T(8,128)(2,1)}, bf16[64,3584]{1,0:T(8,128)(2,1)S(1)}, u32[]{:S(2)}) copy-start(bf16[64,3584]{1,0:T(8,128)(2,1)S(1)} %get-tuple-element.114) | copy-start | bytes 1376260
  146.6 2.6 %copy-start.13 = (bf16[64,3584]{1,0:T(8,128)(2,1)}, bf16[64,3584]{1,0:T(8,128)(2,1)S(1)}, u32[]{:S(2)}) copy-start(bf16[64,3584]{1,0:T(8,128)(2,1)S(1)} %get-tuple-element.112) | copy-start | bytes 1376260
  146.6 2.5 %collective-permute-start.40 = (bf16[64,3584]{1,0:T(8,128)(2,1)S(1)}, bf16[64,3584]{1,0:T(8,128)(2,1)S(1)}, u32[]{:S(2)}, u32[]{:S(2)}) collective-permute-start(bf16[64,3584]{1,0:T(8,128)(2,1)S(1)} %get-tuple-element.105), channel_id=1, source_target_pairs={{0,1},{1,0},{2,3},{3,2},{4,5},{5,4},{6,7},{7,6},{8,9},{9,8},{10,11... | collective-permute-start | bytes 1376264 | tf_op jit(solution)/shard_map/ppermute | solution.py:18
  146.8 2.5 %collective-permute-start.39 = (bf16[64,3584]{1,0:T(8,128)(2,1)}, bf16[64,3584]{1,0:T(8,128)(2,1)S(1)}, u32[]{:S(2)}, u32[]{:S(2)}) collective-permute-start(bf16[64,3584]{1,0:T(8,128)(2,1)} %get-tuple-element.103), channel_id=1, source_target_pairs={{0,1},{1,0},{2,3},{3,2},{4,5},{5,4},{6,7},{7,6},{8,9},{9,8},{10,11... | collective-permute-start | bytes 1376264 | tf_op jit(solution)/shard_map/ppermute | solution.py:18
  147.3 4.8 %collective-permute-start.31 = (bf16[4,4224]{1,0:T(4,128)(2,1)S(1)}, bf16[4,4224]{1,0:T(4,128)(2,1)S(1)}, u32[]{:S(2)}, u32[]{:S(2)}) collective-permute-start(bf16[4,4224]{1,0:T(4,128)(2,1)S(1)} %pad_maximum_fusion.3), channel_id=1, source_target_pairs={{0,3},{1,2},{2,1},{3,0},{4,7},{5,6},{6,5},{7,4},{8,11},{9,10},{10,... | collective-permute-start | bytes 101384 | tf_op jit(solution)/shard_map/ppermute | solution.py:18
  148.0 4.1 %collective-permute-start.30 = (bf16[4,4224]{1,0:T(4,128)(2,1)S(1)}, bf16[4,4224]{1,0:T(4,128)(2,1)S(1)}, u32[]{:S(2)}, u32[]{:S(2)}) collective-permute-start(bf16[4,4224]{1,0:T(4,128)(2,1)S(1)} %pad_maximum_fusion.3), channel_id=1, source_target_pairs={{0,2},{1,3},{2,0},{3,1},{4,6},{5,7},{6,4},{7,5},{8,10},{9,11},{10,... | collective-permute-start | bytes 101384 | tf_op jit(solution)/shard_map/ppermute | solution.py:18
  149.2 2.9 %collective-permute-start.29 = (bf16[4,4224]{1,0:T(4,128)(2,1)S(1)}, bf16[4,4224]{1,0:T(4,128)(2,1)S(1)}, u32[]{:S(2)}, u32[]{:S(2)}) collective-permute-start(bf16[4,4224]{1,0:T(4,128)(2,1)S(1)} %pad_maximum_fusion.3), channel_id=1, source_target_pairs={{0,1},{1,0},{2,3},{3,2},{4,5},{5,4},{6,7},{7,6},{8,9},{9,8},{10,11... | collective-permute-start | bytes 101384 | tf_op jit(solution)/shard_map/ppermute | solution.py:18
  149.4 1.2 copy-start.3
  150.6 6.5 %copy-start.5 = (bf16[64,3584]{1,0:T(8,128)(2,1)S(1)}, bf16[64,3584]{1,0:T(8,128)(2,1)}, u32[]{:S(2)}) copy-start(bf16[64,3584]{1,0:T(8,128)(2,1)} %copy-done.4) | copy-start | bytes 1376260
  150.6 6.6 %copy-start.7 = (bf16[64,3584]{1,0:T(8,128)(2,1)S(1)}, bf16[64,3584]{1,0:T(8,128)(2,1)}, u32[]{:S(2)}) copy-start(bf16[64,3584]{1,0:T(8,128)(2,1)} %copy-done.6) | copy-start | bytes 1376260
  150.6 6.6 %copy-start.9 = (bf16[256,512]{1,0:T(8,128)(2,1)S(1)}, bf16[256,512]{1,0:T(8,128)(2,1)}, u32[]{:S(2)}) copy-start(bf16[256,512]{1,0:T(8,128)(2,1)} %copy-done.8) | copy-start | bytes 786436
  151.1 24.0 %collective-permute-start.45 = (bf16[128,3584]{1,0:T(8,128)(2,1)S(1)}, bf16[128,3584]{1,0:T(8,128)(2,1)S(1)}, u32[]{:S(2)}, u32[]{:S(2)}) collective-permute-start(bf16[128,3584]{1,0:T(8,128)(2,1)S(1)} %pair.7), channel_id=1, source_target_pairs={{0,2},{1,3},{2,0},{3,1},{4,6},{5,7},{6,4},{7,5},{8,10},{9,11},{10,... | collective-permute-start | bytes 2752520 | tf_op jit(solution)/shard_map/ppermute | solution.py:18
  152.1 5.0 %collective-permute-start.41 = (bf16[64,3584]{1,0:T(8,128)(2,1)}, bf16[64,3584]{1,0:T(8,128)(2,1)S(1)}, u32[]{:S(2)}, u32[]{:S(2)}) collective-permute-start(bf16[64,3584]{1,0:T(8,128)(2,1)} %copy-done.13), channel_id=1, source_target_pairs={{0,1},{1,0},{2,3},{3,2},{4,5},{5,4},{6,7},{7,6},{8,9},{9,8},{10,11... | collective-permute-start | bytes 1376264 | tf_op jit(solution)/shard_map/ppermute | solution.py:18
  152.2 4.9 %collective-permute-start.42 = (bf16[64,3584]{1,0:T(8,128)(2,1)}, bf16[64,3584]{1,0:T(8,128)(2,1)S(1)}, u32[]{:S(2)}, u32[]{:S(2)}) collective-permute-start(bf16[64,3584]{1,0:T(8,128)(2,1)} %copy-done.12), channel_id=1, source_target_pairs={{0,1},{1,0},{2,3},{3,2},{4,5},{5,4},{6,7},{7,6},{8,9},{9,8},{10,11... | collective-permute-start | bytes 1376264 | tf_op jit(solution)/shard_map/ppermute | solution.py:18
  152.7 4.4 %collective-permute-start.43 = (bf16[64,3584]{1,0:T(8,128)(2,1)}, bf16[64,3584]{1,0:T(8,128)(2,1)S(1)}, u32[]{:S(2)}, u32[]{:S(2)}) collective-permute-start(bf16[64,3584]{1,0:T(8,128)(2,1)} %copy-done.11), channel_id=1, source_target_pairs={{0,1},{1,0},{2,3},{3,2},{4,5},{5,4},{6,7},{7,6},{8,9},{9,8},{10,11... | collective-permute-start | bytes 1376264 | tf_op jit(solution)/shard_map/ppermute | solution.py:18
  152.7 4.4 %collective-permute-start.44 = (bf16[64,3584]{1,0:T(8,128)(2,1)}, bf16[64,3584]{1,0:T(8,128)(2,1)S(1)}, u32[]{:S(2)}, u32[]{:S(2)}) collective-permute-start(bf16[64,3584]{1,0:T(8,128)(2,1)} %copy-done.10), channel_id=1, source_target_pairs={{0,1},{1,0},{2,3},{3,2},{4,5},{5,4},{6,7},{7,6},{8,9},{9,8},{10,11... | collective-permute-start | bytes 1376264 | tf_op jit(solution)/shard_map/ppermute | solution.py:18
  157.1 20.0 %copy-start.1 = (bf16[7168,64]{0,1:T(8,128)(2,1)S(1)}, bf16[7168,64]{0,1:T(8,128)(2,1)}, u32[]{:S(2)}) copy-start(bf16[7168,64]{0,1:T(8,128)(2,1)} %param.10) | copy-start | bytes 2752516
  (2 other events, 1.6 us)

commit v9 on v8

--- a/solution.py
+++ b/solution.py
@@ -33,6 +33,11 @@
     return [block, across(block, 1), second]
 
 
+def spread_direct(block):
+    second, third = across(block, 2), across(block, 3)
+    return [block, across(block, 1), second, third]
+
+
 def spread_last(blocks, *earlier):
     block, _, second = blocks
     middle = across(after(block, second, *earlier), 3, (1, 2))
@@ -40,10 +45,10 @@
     return blocks + [middle, ends]
 
 
-def terms_kernel(size, count, first, adds, per_part, place_ref, *refs):
-    total = 5 * count
-    groups = [refs[5 * group : 5 * group + 5] for group in range(count)]
-    w_ref, add_refs, outs = refs[total], refs[total + 1 :][: len(adds)], refs[total + 1 + len(adds) : -4]
+def terms_kernel(size, per_group, count, first, adds, per_part, parts, place_ref, *refs):
+    total = per_group * count
+    groups = [refs[per_group * group :][:per_group] for group in range(count)]
+    w_ref, add_refs, outs = refs[total], refs[total + 1 :][:adds], refs[total + 1 + adds : -4]
     feats, held, sems, held_sems = refs[-4:]
     width, tile = feats.shape[1] // size, outs[0].shape[1]
     tall = feats.shape[0] // len(groups)
@@ -65,13 +70,16 @@
         copies = []
         place = place_ref[0]
         for group, blocks in enumerate(groups):
-            copies += [put(blocks[k], group, lax.bitwise_xor(place, k), k) for k in range(3)]
+            straight = 3 if per_group == 5 else 4
+            copies += [
+                put(blocks[k], group, lax.bitwise_xor(place, k), k) for k in range(straight)
+            ]
         for copy in copies:
             copy.start()
         for step in range(slots):
             fetch(step).start()
         inside = jnp.logical_or(place == 1, place == 2)
-        for group, blocks in enumerate(groups):
+        for group, blocks in enumerate(groups if per_group == 5 else ()):
             for chosen, block in ((inside, blocks[3]), (jnp.logical_not(inside), blocks[4])):
 
                 @pl.when(chosen)
@@ -86,55 +94,85 @@
     fetch(j).wait()
     weight = held[lax.rem(j, slots)].reshape(size * width, tile)
     terms = jnp.dot(feats[...], weight, preferred_element_type=f32)
-    row = 0
-    for out_ref in outs:
-        if not adds:
+    if adds:
+        wide_refs, low_refs = add_refs[:-2], add_refs[-2:]
+        tall = low_refs[0].shape[0]
+        top = feats.shape[0] - 2 * tall
+        for part, ref in enumerate(wide_refs):
+
+            @pl.when(j // per_part == part)
+            def _():
+                total = terms + ref[...].astype(f32)
+                if part == len(wide_refs) - 1:
+                    outs[0][:top] = total[:top].astype(bf16)
+                    for row, low_ref in zip((top, top + tall), low_refs):
+                        low = total[row : row + tall] + low_ref[...].astype(f32)
+                        outs[0][row : row + tall] = low.astype(bf16)
+                else:
+                    outs[0][...] = total.astype(bf16)
+
+
+    def write(some):
+        row = 0
+        for out_ref in some:
             out_ref[...] = terms[row : row + out_ref.shape[0]].astype(bf16)
-        row += out_ref.shape[0]
-
-    def add_part(part):
-        here = [(ref, at) for ref, (at, of) in zip(add_refs, adds) if of == part]
-        cut = min(ref.shape[0] for ref, _ in here)
-        cols = pl.ds(pl.multiple_of((j - part * per_part) * tile, tile), tile)
-        for row in range(0, feats.shape[0], cut):
-            total = terms[row : row + cut]
-            for ref, at in here:
-                if at <= row < at + ref.shape[0]:
-                    total = total + ref[row - at : row - at + cut, cols].astype(f32)
-            outs[0][row : row + cut] = total.astype(bf16)
-
-    for part in sorted({of for _, of in adds}):
-        pl.when(j // per_part == part)(functools.partial(add_part, part))
+            row += out_ref.shape[0]
+
+    each = len(outs) // parts
+    if parts == 1 and not adds:
+        write(outs)
+    for part in range(parts if parts > 1 else 0):
+        pl.when(j // per_part == part)(
+            functools.partial(write, outs[part * each : (part + 1) * each])
+        )
 
     @pl.when(j + slots < steps)
     def _():
         fetch(j + slots).start()
 
 
-def block_terms(groups, down_weight, col_start, cols, outs, adds=()):
+def block_terms(groups, down_weight, col_start, cols, outs, adds=(), low_adds=(), parts=1):
     size, _, width, _ = down_weight.shape
     rows = sum(outs)
-    tile = max(n for n in range(128, 513, 128) if cols % n == 0)
-    slots = min(4, cols // tile)
+    tile = max(n for n in range(128, 897, 128) if cols % n == 0)
+    slots = min(3, cols // tile)
     blocks = [block for group in groups for block in group]
-    per_part = adds[0][0].shape[1] // tile if adds else 1
+    per_part = adds[0].shape[1] // tile if adds else cols // parts // tile
+
+    def add_spec(part, tall=rows):
+        if parts == 1 and not adds or part is None:
+            return pl.BlockSpec((tall, tile), lambda j, place: (0, j))
+        return pl.BlockSpec(
+            (tall, tile), lambda j, place: (0, jnp.clip(j - part * per_part, 0, per_part - 1))
+        )
+
+    add_specs = [add_spec(part) for part in range(len(adds))]
+    if adds:
+        add_specs += [add_spec(len(adds) - 1, value.shape[0]) for value in low_adds]
+        adds = [*adds, *low_adds]
 
     return pl.pallas_call(
         functools.partial(
             terms_kernel,
             size,
+            len(groups[0]),
             len(groups),
             col_start,
-            [add[1:] for add in adds],
+            len(adds),
             per_part,
+            parts,
         ),
-        out_shape=[jax.ShapeDtypeStruct((tall, cols), bf16) for tall in outs],
+        out_shape=[jax.ShapeDtypeStruct((tall, cols // parts), bf16) for tall in outs] * parts,
         grid_spec=pltpu.PrefetchScalarGridSpec(
             num_scalar_prefetch=1,
             grid=(cols // tile,),
             in_specs=[pl.BlockSpec(memory_space=pltpu.HBM)] * (len(blocks) + 1)
-            + [pl.BlockSpec(memory_space=pltpu.VMEM)] * len(adds),
-            out_specs=[pl.BlockSpec((tall, tile), lambda j, place: (0, j)) for tall in outs],
+            + add_specs,
+            out_specs=[
+                add_spec(None if parts == 1 else part, tall)
+                for part in range(parts)
+                for tall in outs
+            ],
             scratch_shapes=[
                 pltpu.VMEM((rows, size * width), bf16),
                 pltpu.VMEM((slots, size, width, tile), bf16),
@@ -151,18 +189,19 @@
         lax.axis_index("tensor").reshape(1),
         *blocks,
         down_weight,
-        *[value for value, _, _ in adds],
-    )
-
-
-def add_kernel(kept_ref, first_ref, second_ref, out_ref):
-    rows = first_ref.shape[0]
+        *adds,
+    )
+
+
+def add_kernel(kept_ref, first_ref, second_ref, *outs):
+    rows, tall = first_ref.shape[0], outs[0].shape[0]
     for index, other in enumerate((first_ref, second_ref)):
-        cut = slice(index * rows, (index + 1) * rows)
-        out_ref[cut] = (kept_ref[cut].astype(f32) + other[...].astype(f32)).astype(bf16)
-
-
-def add_halves(kept, first, second):
+        total = kept_ref[index * rows : (index + 1) * rows].astype(f32) + other[...].astype(f32)
+        at = index * rows % tall
+        outs[index * rows // tall][at : at + rows] = total.astype(bf16)
+
+
+def add_halves(kept, first, second, outs=1):
     rows, cols = kept.shape
     tile = max(n for n in range(128, 1025, 128) if cols % n == 0)
 
@@ -171,35 +210,45 @@
 
     return pl.pallas_call(
         add_kernel,
-        out_shape=jax.ShapeDtypeStruct((rows, cols), bf16),
+        out_shape=[jax.ShapeDtypeStruct((rows // outs, cols), bf16)] * outs,
         grid=(cols // tile,),
         in_specs=[spec(rows), spec(rows // 2), spec(rows // 2)],
-        out_specs=spec(rows),
+        out_specs=[spec(rows // outs)] * outs,
         compiler_params=pltpu.CompilerParams(vmem_limit_bytes=16 << 20),
         cost_estimate=pl.CostEstimate(flops=1000, bytes_accessed=1000, transcendentals=0),
         name="pair",
     )(kept, first, second)
 
 
-def finish_kernel(own_ref, other_ref, out_ref):
-    out_ref[...] = (own_ref[...].astype(f32) + other_ref[...].astype(f32)).astype(bf16)
-
-
-def finish(result, other, row, col):
-    rows, cols = other.shape
+def gather_sums_kernel(*refs):
+    quarters, sums, out_ref = refs[:4], refs[4:-1], refs[-1]
+    rows = quarters[0].shape[0]
+    for index, ref in enumerate(quarters):
+        value = ref[...]
+        if index // 2 < len(sums):
+            at = (index % 2) * rows
+            other = sums[index // 2][at : at + rows]
+            value = (value.astype(f32) + other.astype(f32)).astype(bf16)
+        out_ref[index * rows : (index + 1) * rows] = value
+
+
+def gather_sums(quarters, sums):
+    rows, cols = quarters[0].shape
     tile = max(n for n in range(128, 2049, 128) if cols % n == 0)
-    part = pl.BlockSpec((rows, tile), lambda j: (row // rows, col // tile + j))
+
+    def spec(tall):
+        return pl.BlockSpec((tall, tile), lambda j: (0, j))
+
     return pl.pallas_call(
-        finish_kernel,
-        out_shape=jax.ShapeDtypeStruct(result.shape, bf16),
+        gather_sums_kernel,
+        out_shape=jax.ShapeDtypeStruct((4 * rows, cols), bf16),
         grid=(cols // tile,),
-        in_specs=[part, pl.BlockSpec((rows, tile), lambda j: (0, j))],
-        out_specs=part,
-        input_output_aliases={0: 0},
-        compiler_params=pltpu.CompilerParams(vmem_limit_bytes=16 << 20),
+        in_specs=[spec(rows)] * 4 + [spec(2 * rows)] * len(sums),
+        out_specs=spec(4 * rows),
+        compiler_params=pltpu.CompilerParams(vmem_limit_bytes=24 << 20),
         cost_estimate=pl.CostEstimate(flops=1000, bytes_accessed=1000, transcendentals=0),
-        name="finish",
-    )(result, other)
+        name="sums",
+    )(*quarters, *sums)
 
 
 def example_gradients(acts_low, grads_low, local_ids, examples):
@@ -300,53 +349,55 @@
     parts = small_sums(hidden_acts, output_grad, input_basis, output_basis)
     low = parts + across(parts, 1)
 
-    blocks = spread_first(after(far[0], parts))
-    later = spread_first(after(far[1], blocks[2]))
-    blocks = spread_last(blocks, low, beside, far[1])
-    low = after(low, blocks[4])
-
-    def far_terms(chunks, at, *earlier):
-        chunks = [[after(chunks[0][0], *earlier)] + chunks[0][1:]] + chunks[1:]
-        outs = [rows // 2, rows // 2, rows] + [rows // 2] * 4 * (len(chunks) - 1)
-        return block_terms(chunks, down_weight, at * part, part, outs)
+    blocks = spread_direct(after(far[0], parts))
+    low = after(low, *blocks[1:])
+    partner = across(low, 2)
+    far[1] = after(far[1], *blocks[1:])
+    later_first = across(far[1], 1)
+
+    def far_terms(chunk, at, *earlier):
+        chunk = [after(chunk[0], *earlier)] + chunk[1:] if earlier else chunk
+        return block_terms([chunk], down_weight, at * part, part, [rows // 2, rows // 2, rows])
 
     def pair_sum(first, last, kept, *earlier):
-        pair = add_halves(kept, swap(after(first, *earlier), 1), swap(after(last, *earlier), 1))
+        (pair,) = add_halves(kept, swap(after(first, *earlier), 1), swap(after(last, *earlier), 1))
         return pair, swap(pair, 2)
 
-    first, last, kept = far_terms([blocks], 0, *later)
-    pair0, sum0 = pair_sum(first, last, kept)
-
-    later = spread_last(later, pair0)
-    beside = spread_first(after(beside, pair0))
-    first, last, kept = far_terms([blocks], 1, pair0)
-    pair1, sum1 = pair_sum(first, last, kept, *later, *beside)
-
-    beside = spread_last(beside, pair1)
-    own = spread_first(after(own, pair1))
-    first, last, kept, *near0 = far_terms([later, beside], 0, pair1, sum0)
-    pair2, sum2 = pair_sum(first, last, kept, *own)
-
-    own = spread_last(own, pair2)
-    near0 = [swap(after(term, sum1, pair2), 1) for term in near0]
-    partner = across(after(low, pair0), 2)
-    acts_low, grads_low = jnp.split(after(low, pair2, sum1) + partner, 2, axis=1)
+    first, last, kept = far_terms(blocks, 0)
+    pair0, sum0 = pair_sum(first, last, kept, partner, later_first)
+
+    later = [far[1], later_first, across(after(far[1], pair0), 2)]
+    first, last, kept = far_terms(blocks, 1, pair0)
+    pair1, sum1 = pair_sum(first, last, kept, later[2])
+
+    later = spread_last(later, pair1)
+    beside = spread_first(after(beside, pair1, *later[3:]))
+    acts_low, grads_low = jnp.split(after(low, pair1, sum0) + partner, 2, axis=1)
     example_grad = example_gradients(
         acts_low, grads_low, token_example[0], example_group.shape[0]
     )
     gathered = gather_examples(example_grad, example_group)
-    first, last, kept, *near1 = far_terms([later, beside], 1, example_grad, *near0)
-    pair3, sum3 = pair_sum(first, last, kept, *own)
-
-    near1 = [swap(after(term, sum2, pair3), 1) for term in near1]
-    every = order_examples(after(gathered, sum2, pair3))
+    first, last, kept = far_terms(later, 0, example_grad)
+    pair2, sum2 = pair_sum(first, last, kept, *beside)
+
+    beside = spread_last(beside, pair2)
+    own = after(own, pair2)
+    own_first = across(own, 1)
+    every = order_examples(after(gathered, pair2, sum1))
     fisher, group_grad = fisher_and_groups(every, example_grad.shape[1])
-    own = [after(own[0], fisher, group_grad)] + own[1:]
-    adds = [(term, row * (rows // 2), 0) for row, term in enumerate(near0)]
-    adds += [(term, row * (rows // 2), 1) for row, term in enumerate(near1)]
-    adds += [(sum0, 0, 0), (sum1, 0, 1), (sum2, rows, 0)]
-    (result,) = block_terms([own], down_weight, 0, cols, [tokens], adds)
-    return (finish(result, sum3, rows, part), fisher, group_grad)
+    first, last, kept = far_terms(later, 1, fisher, group_grad)
+    first, last = (swap(after(term, own_first, *beside), 1) for term in (first, last))
+    pair3 = add_halves(kept, first, last, 2)
+    sum3 = [swap(term, 2) for term in pair3]
+
+    own = [own, own_first, across(after(own, pair3[0]), 2)]
+    beside = [after(beside[0], pair3[0], sum2)] + beside[1:]
+    near = block_terms([beside], down_weight, 0, cols, [rows // 2] * 4, parts=2)
+    near = [swap(after(term, own[2], sum3[0]), 1) for term in near]
+    own = spread_last(own, *near[:1])
+    adds = [gather_sums(near[:4], [sum0, sum2]), gather_sums(near[4:], [sum1])]
+    (result,) = block_terms([own], down_weight, 0, cols, [tokens], adds, sum3)
+    return (result, fisher, group_grad)
 
 
 def per_device(hidden_acts, output_grad, down_weight, *rest):

time: 178 us -> 178 us (level)
  starting transfers between devices: 46 us -> 38.6 us
  Pallas kernels: 62.5 us -> 67.2 us
  waiting for transfers between devices: 50.1 us -> 52 us
    ppermute x28 -> x29, waiting for transfers between devices: 8.24 us -> 22 us  [swap(): return lax.ppermute(value, 'dp', [(d, d ^ step) for d in range(size)])]
    ppermute x18 -> x17, waiting for transfers between devices: 41.9 us -> 30 us  [across(): return lax.ppermute(value, 'tensor', pairs)]
    ppermute x18 -> x17, starting transfers between devices: 30.9 us -> 22.8 us  [across(): return lax.ppermute(value, 'tensor', pairs)]
    pallas_call x10 -> x12, Pallas kernels: 62.5 us -> 67.2 us  [the longest x6 58.8 us: block_terms(): pl.pallas_call(functools.partial(terms_kernel, size, len(groups[0]), len(...]
    unnamed x41 -> x24, local copies, waits for them, and re-layouts: 3.77 us -> 4.94 us
    ppermute x28 -> x29, starting transfers between devices: 15.1 us -> 15.8 us  [swap(): return lax.ppermute(value, 'dp', [(d, d ^ step) for d in range(size)])]
  transfers between devices with their start and end apart: 46 -> 46, of which waited for: 16 -> 21; matrix products, arithmetic and copies ran while one was open for 6% -> 6% of each run, Pallas kernels for 29% -> 29%
where the time goes in v9:
time: 178 us; the launch traced here: 177 us
  Pallas kernels  67.2 us (38%)
  waiting for transfers between devices  52 us (29%)
  starting transfers between devices  38.6 us (22%)
  local copies, waits for them, and re-layouts  9.37 us (5%)
  matrix products  7.54 us (4%)
    pallas_call x6, Pallas kernels, block_terms(): pl.pallas_call(functools.partial(terms_kernel, size, len(groups[0]), len(...  58.8 us
    ppermute x17, waiting for transfers between devices, across(): return lax.ppermute(value, 'tensor', pairs)  30 us
    ppermute x17, starting transfers between devices, across(): return lax.ppermute(value, 'tensor', pairs)  22.8 us
    ppermute x29, waiting for transfers between devices, swap(): return lax.ppermute(value, 'dp', [(d, d ^ step) for d in range(size)])  22 us
    ppermute x29, starting transfers between devices, swap(): return lax.ppermute(value, 'dp', [(d, d ^ step) for d in range(size)])  15.8 us
    pallas_call x4, Pallas kernels, add_halves(): pl.pallas_call(add_kernel, out_shape=[jax.ShapeDtypeStruct((rows // outs,...  6.08 us
    unnamed x24, local copies, waits for them, and re-layouts  4.94 us
  transfers between devices with their start and end apart: 46, of which 21 were waited for; matrix products, arithmetic and copies ran while one was open for 6% of the time, Pallas kernels for 29%

profile of v9, /device:TPU:0, one launch (start us, length us, event | category | flops | bytes accessed | tf_op | source)
XLA Modules:
  0.0 177.5 jit_solution(8688864037544932738)
XLA Ops:
  0.7 2.0 %constant_dynamic-slice_fusion = (bf16[1,1,512,256]{3,2,1,0:T(8,128)(2,1)S(1)}, bf16[1,1,512,256]{3,2,1,0:T(8,128)(2,1)S(1)}, bf16[1,1,512,256]{3,2,1,0:T(8,128)(2,1)S(1)}, bf16[1,1,512,256]{3,2,1,0:T(8,128)(2,1)}) fusion(bf16[1,4,512,256]{3,2,1,0:T(8,128)(2,1)} %param.8, s32[]{:T(128)S(6)} %select_n.96, s32[]{:T(128)S(6)} %select_n.95, s32[]{:T(128)S(6)} %select_n.94, ...), kind=kLoop, calls=%fused_computation.32 | loop fusion | bytes 2097168 | tf_op jit(solution)/shard_map/dynamic-slice.7
  2.9 0.7 slice_bitcast_fusion
  3.5 2.9 %collective-permute-start.3 = (bf16[128,512]{1,0:T(8,128)(2,1)}, bf16[128,512]{1,0:T(8,128)(2,1)S(1)}, u32[]{:S(2)}, u32[]{:S(2)}) collective-permute-start(bf16[128,512]{1,0:T(8,128)(2,1)} %get-tuple-element.129), channel_id=1, source_target_pairs={{0,2},{1,3},{2,0},{3,1},{4,6},{5,7},{6,4},{7,5},{8,10},{9,11},{10,... | collective-permute-start | bytes 393224 | tf_op jit(solution)/shard_map/ppermute | solution.py:18
  6.7 3.3 %fusion.15 = f32[256,64]{0,1:T(8,128)S(1)} fusion(bf16[256,7168]{1,0:T(8,128)(2,1)} %param.7, bf16[7168,64]{0,1:T(8,128)(2,1)S(1)} %copy-done), kind=kOutput, calls=%fused_computation.38 | convolution fusion | flops 234881024 | bytes 4653056 | tf_op jit(solution)/shard_map/dot_general | solution.py:307
  10.7 1.9 %collective-permute-done.2 = bf16[128,512]{1,0:T(8,128)(2,1)S(1)} collective-permute-done((bf16[128,512]{1,0:T(8,128)(2,1)S(1)}, bf16[128,512]{1,0:T(8,128)(2,1)S(1)}, u32[]{:S(2)}, u32[]{:S(2)}) %collective-permute-start.2) | collective-permute-done | bytes 131104 | tf_op jit(solution)/shard_map/ppermute | solution.py:18
  12.6 3.6 %collective-permute-start.6 = (bf16[256,512]{1,0:T(8,128)(2,1)S(1)}, bf16[256,512]{1,0:T(8,128)(2,1)S(1)}, u32[]{:S(2)}, u32[]{:S(2)}) collective-permute-start(bf16[256,512]{1,0:T(8,128)(2,1)S(1)} %pad_maximum_fusion.1.refs_0_), channel_id=1, source_target_pairs={{0,12},{4,8},{8,4},{12,0},{1,13},{5,9},{9,5},{13,1},{2,14},{6,10},... | collective-permute-start | bytes 786440 | tf_op jit(solution)/shard_map/ppermute | solution.py:28
  16.2 0.9 collective-permute-start.4
  17.1 1.0 collective-permute-start.1
  18.2 5.2 %collective-permute-done.1 = bf16[128,512]{1,0:T(8,128)(2,1)S(1)} collective-permute-done((bf16[128,512]{1,0:T(8,128)(2,1)S(1)}, bf16[128,512]{1,0:T(8,128)(2,1)S(1)}, u32[]{:S(2)}, u32[]{:S(2)}) %collective-permute-start.1) | collective-permute-done | bytes 131104 | tf_op jit(solution)/shard_map/ppermute | solution.py:18
  23.4 1.2 collective-permute-start.7
  24.6 14.6 %collective-permute-done.5.refs_2_ = bf16[256,512]{1,0:T(8,128)(2,1)S(1)} collective-permute-done((bf16[256,512]{1,0:T(8,128)(2,1)S(1)}, bf16[256,512]{1,0:T(8,128)(2,1)S(1)}, u32[]{:S(2)}, u32[]{:S(2)}) %collective-permute-start.5) | collective-permute-done | bytes 262176 | tf_op jit(solution)/shard_map/ppermute | solution.py:28
  39.3 3.1 %collective-permute-start.8 = (f32[256,128]{0,1:T(8,128)S(1)}, f32[256,128]{0,1:T(8,128)S(1)}, u32[]{:S(2)}, u32[]{:S(2)}) collective-permute-start(f32[256,128]{0,1:T(8,128)S(1)} %fusion.14), channel_id=1, source_target_pairs={{0,8},{4,12},{8,0},{12,4},{1,9},{5,13},{9,1},{13,5},{2,10},{6,14},... | collective-permute-start | bytes 393224 | tf_op jit(solution)/shard_map/ppermute | solution.py:28
  42.4 7.4 %terms.6 = (bf16[64,3584]{1,0:T(8,128)(2,1)S(1)}, bf16[64,3584]{1,0:T(8,128)(2,1)S(1)}, bf16[128,3584]{1,0:T(8,128)(2,1)S(1)}) custom-call(s32[1]{0:T(128)} %bitcast.place_ref, bf16[256,512]{1,0:T(8,128)(2,1)S(1)} %pad_maximum_fusion.1.refs_0_, bf16[256,512]{1,0:T(8,128)(2,1)S(1)} %collective-permute-done.4.refs_1_, ...), custom_call_target="tpu_custom_call" | custom-call | flops 469762048 | bytes 1000 | tf_op jit(solution)/shard_map/terms/pallas_call | solution.py:154
  50.0 0.5 collective-permute-start.10
  50.6 1.3 collective-permute-done.11.second_ref
  51.9 0.7 collective-permute-done.10.first_ref
  52.5 1.7 pair.4
  54.2 1.8 %collective-permute-start.15 = (bf16[128,3584]{1,0:T(8,128)(2,1)}, bf16[128,3584]{1,0:T(8,128)(2,1)S(1)}, u32[]{:S(2)}, u32[]{:S(2)}) collective-permute-start(bf16[128,3584]{1,0:T(8,128)(2,1)} %pair.4), channel_id=1, source_target_pairs={{0,2},{1,3},{2,0},{3,1},{4,6},{5,7},{6,4},{7,5},{8,10},{9,11},{10,... | collective-permute-start | bytes 2752520 | tf_op jit(solution)/shard_map/ppermute | solution.py:18
  56.0 1.2 collective-permute-start.12
  57.2 8.0 %terms.7 = (bf16[64,3584]{1,0:T(8,128)(2,1)}, bf16[64,3584]{1,0:T(8,128)(2,1)}, bf16[128,3584]{1,0:T(8,128)(2,1)S(1)}) custom-call(s32[1]{0:T(128)} %bitcast.place_ref, bf16[256,512]{1,0:T(8,128)(2,1)S(1)} %pad_maximum_fusion.1.refs_0_, bf16[256,512]{1,0:T(8,128)(2,1)S(1)} %collective-permute-done.4.refs_1_, ...), custom_call_target="tpu_custom_call" | custom-call | flops 469762048 | bytes 1000 | tf_op jit(solution)/shard_map/terms/pallas_call | solution.py:154
  65.2 0.9 copy-done.4
  66.1 4.5 %collective-permute-done.12.refs_2_ = bf16[256,512]{1,0:T(8,128)(2,1)S(1)} collective-permute-done((bf16[256,512]{1,0:T(8,128)(2,1)S(1)}, bf16[256,512]{1,0:T(8,128)(2,1)S(1)}, u32[]{:S(2)}, u32[]{:S(2)}) %collective-permute-start.12) | collective-permute-done | bytes 262176 | tf_op jit(solution)/shard_map/ppermute | solution.py:28
  70.6 0.5 collective-permute-start.13
  71.5 1.1 collective-permute-done.14.second_ref
  72.6 0.7 collective-permute-done.13.first_ref
  73.3 1.2 copy-done.5
  74.5 1.7 pair.5
  76.5 0.7 collective-permute-start.16
  77.2 1.3 collective-permute-start.17
  79.1 8.1 %collective-permute-done.17.refs_4_ = bf16[256,512]{1,0:T(8,128)(2,1)S(1)} collective-permute-done((bf16[256,512]{1,0:T(8,128)(2,1)S(1)}, bf16[256,512]{1,0:T(8,128)(2,1)S(1)}, u32[]{:S(2)}, u32[]{:S(2)}) %collective-permute-start.17) | collective-permute-done | bytes 262176 | tf_op jit(solution)/shard_map/ppermute | solution.py:28
  87.3 2.5 %collective-permute-start.19 = (bf16[256,512]{1,0:T(8,128)(2,1)S(1)}, bf16[256,512]{1,0:T(8,128)(2,1)S(1)}, u32[]{:S(2)}, u32[]{:S(2)}) collective-permute-start(bf16[256,512]{1,0:T(8,128)(2,1)S(1)} %collective-permute-done.18.refs_0_), channel_id=1, source_target_pairs={{0,4},{4,0},{8,12},{12,8},{1,5},{5,1},{9,13},{13,9},{2,6},{6,2},{1... | collective-permute-start | bytes 786440 | tf_op jit(solution)/shard_map/ppermute | solution.py:28
  89.9 8.0 %terms.8 = (bf16[64,3584]{1,0:T(8,128)(2,1)}, bf16[64,3584]{1,0:T(8,128)(2,1)S(1)}, bf16[128,3584]{1,0:T(8,128)(2,1)S(1)}) custom-call(s32[1]{0:T(128)} %bitcast.place_ref, bf16[256,512]{1,0:T(8,128)(2,1)S(1)} %pad_maximum_fusion.refs_0_, bf16[256,512]{1,0:T(8,128)(2,1)S(1)} %collective-permute-done.9.refs_1_, ...), custom_call_target="tpu_custom_call" | custom-call | flops 469762048 | bytes 1000 | tf_op jit(solution)/shard_map/terms/pallas_call | solution.py:154
  97.9 0.9 copy-done.2
  98.8 1.7 collective-permute-done.20.refs_2_
  100.7 0.7 copy-done.6
  101.4 0.5 collective-permute-start.21
  102.0 1.4 collective-permute-start.26
  104.0 1.1 copy.20
  105.1 1.2 copy-done.3
  106.3 2.1 %pair.6 = bf16[128,3584]{1,0:T(8,128)(2,1)S(1)} custom-call(bf16[128,3584]{1,0:T(8,128)(2,1)S(1)} %copy-done.3, bf16[64,3584]{1,0:T(8,128)(2,1)} %collective-permute-done.21.first_ref, bf16[64,3584]{1,0:T(8,128)(2,1)S(1)} %collective-permute-done.22.second_ref), custom_call_target="tpu_custom_call" | custom-call | flops 1000 | bytes 1000 | tf_op jit(solution)/shard_map/pair/pallas_call | solution.py:211
  108.4 1.8 collective-permute-start.33
  110.2 0.9 select_select_fusion.3
  111.4 0.7 collective-permute-start.28
  112.1 1.5 collective-permute-start.29
  113.5 0.9 fusion.6
  114.4 2.7 %fusion.4 = f32[1024,1024]{1,0:T(8,128)} fusion(bf16[16,4224]{1,0:T(8,128)(2,1)S(1)} %pad_maximum_fusion.2, s32[]{:T(128)S(6)} %select_n.121, s32[]{:T(128)S(6)} %select_n.122), kind=kOutput, calls=%fused_computation.20 | convolution fusion | flops 33554432 | bytes 4259848 | tf_op jit(solution)/shard_map/dot_general | solution.py:296
  117.2 7.4 %terms.9 = (bf16[64,3584]{1,0:T(8,128)(2,1)S(1)}, bf16[64,3584]{1,0:T(8,128)(2,1)S(1)}, bf16[128,3584]{1,0:T(8,128)(2,1)S(1)}) custom-call(s32[1]{0:T(128)} %bitcast.place_ref, bf16[256,512]{1,0:T(8,128)(2,1)S(1)} %pad_maximum_fusion.refs_0_, bf16[256,512]{1,0:T(8,128)(2,1)S(1)} %collective-permute-done.9.refs_1_, ...), custom_call_target="tpu_custom_call" | custom-call | flops 469762048 | bytes 1000 | tf_op jit(solution)/shard_map/terms/pallas_call | solution.py:154
  124.6 0.7 collective-permute-done.29.refs_4_
  125.8 1.3 collective-permute-done.31.second_ref
  127.1 0.7 collective-permute-done.30.first_ref
  127.8 0.5 pair.7
  128.7 4.1 %collective-permute-start.32 = (bf16[256,512]{1,0:T(8,128)(2,1)S(1)}, bf16[256,512]{1,0:T(8,128)(2,1)S(1)}, u32[]{:S(2)}, u32[]{:S(2)}) collective-permute-start(bf16[256,512]{1,0:T(8,128)(2,1)S(1)} %bitcast.39), channel_id=1, source_target_pairs={{0,8},{4,12},{8,0},{12,4},{1,9},{5,13},{9,1},{13,5},{2,10},{6,14},... | collective-permute-start | bytes 786440 | tf_op jit(solution)/shard_map/ppermute | solution.py:28
  132.8 13.4 %terms.10 = (bf16[64,3584]{1,0:T(8,128)(2,1)S(1)}, bf16[64,3584]{1,0:T(8,128)(2,1)S(1)}, bf16[64,3584]{1,0:T(8,128)(2,1)S(1)}, bf16[64,3584]{1,0:T(8,128)(2,1)S(...) custom-call(s32[1]{0:T(128)} %bitcast.place_ref, ...), custom_call_target="tpu_custom_call" | custom-call | flops 939524096 | bytes 1000 | tf_op jit(solution)/shard_map/terms/pallas_call | solution.py:154
  147.4 0.7 collective-permute-done.44.refs_3_
  148.3 0.5 collective-permute-done.43.refs_2_
  148.9 0.5 collective-permute-done.40.refs_3_
  149.6 0.5 collective-permute-done.35.refs_0_
  150.1 1.7 collective-permute-start.45
  151.8 0.7 collective-permute-start.36
  152.5 1.3 collective-permute-start.37
  153.8 0.9 sums.2.refs_6_
  154.6 1.5 sums.3.refs_7_
  156.1 6.5 %collective-permute-done.45.refs_9_ = bf16[64,3584]{1,0:T(8,128)(2,1)S(1)} collective-permute-done((bf16[64,3584]{1,0:T(8,128)(2,1)S(1)}, bf16[64,3584]{1,0:T(8,128)(2,1)S(1)}, u32[]{:S(2)}, u32[]{:S(2)}) %collective-permute-start.45) | collective-permute-done | bytes 458784 | tf_op jit(solution)/shard_map/ppermute | solution.py:18
  162.7 14.7 %terms.11 = bf16[256,7168]{1,0:T(8,128)(2,1)} custom-call(s32[1]{0:T(128)} %bitcast.place_ref, bf16[256,512]{1,0:T(8,128)(2,1)S(1)} %bitcast.41, bf16[256,512]{1,0:T(8,128)(2,1)S(1)} %collective-permute-done.23.refs_1_, bf16[256,512]{1,0:T(8,128)(2,1)S(1)} %collective-permute-done.32.refs_2_, bf16[256,512]{1,0:T(8,128)(2,1)S(1)} %collective-permute-done.36.refs_3_, ...), custom_call_target="tpu_custom_call" | custom-call | flops 939524096 | bytes 1000 | tf_op jit(solution)/shard_map/terms/pallas_call | solution.py:154
  (93 shorter events, 6.7 us)
Async XLA Ops:
  0.6 6.1 %copy-start = (bf16[7168,64]{0,1:T(8,128)(2,1)S(1)}, bf16[7168,64]{0,1:T(8,128)(2,1)}, u32[]{:S(2)}) copy-start(bf16[7168,64]{0,1:T(8,128)(2,1)} %param.10) | copy-start | bytes 2752516
  2.7 7.3 %copy-start.8 = (bf16[1,4,512,256]{3,2,1,0:T(8,128)(2,1)S(1)}, bf16[1,4,512,256]{3,2,1,0:T(8,128)(2,1)}, u32[]{:S(2)}) copy-start(bf16[1,4,512,256]{3,2,1,0:T(8,128)(2,1)} %param.8) | copy-start | bytes 3145732
  2.7 7.3 %copy-start.9 = (bf16[1,4,512,64]{2,3,1,0:T(8,128)(2,1)S(1)}, bf16[1,4,512,64]{2,3,1,0:T(8,128)(2,1)}, u32[]{:S(2)}) copy-start(bf16[1,4,512,64]{2,3,1,0:T(8,128)(2,1)} %param.11) | copy-start | bytes 786436
  3.5 7.2 %collective-permute-start.3 = (bf16[128,512]{1,0:T(8,128)(2,1)}, bf16[128,512]{1,0:T(8,128)(2,1)S(1)}, u32[]{:S(2)}, u32[]{:S(2)}) collective-permute-start(bf16[128,512]{1,0:T(8,128)(2,1)} %get-tuple-element.129), channel_id=1, source_target_pairs={{0,2},{1,3},{2,0},{3,1},{4,6},{5,7},{6,4},{7,5},{8,10},{9,11},{10,... | collective-permute-start | bytes 393224 | tf_op jit(solution)/shard_map/ppermute | solution.py:18
  6.6 5.9 %collective-permute-start.2 = (bf16[128,512]{1,0:T(8,128)(2,1)S(1)}, bf16[128,512]{1,0:T(8,128)(2,1)S(1)}, u32[]{:S(2)}, u32[]{:S(2)}) collective-permute-start(bf16[128,512]{1,0:T(8,128)(2,1)S(1)} %get-tuple-element.127), channel_id=1, source_target_pairs={{0,3},{1,2},{2,1},{3,0},{4,7},{5,6},{6,5},{7,4},{8,11},{9,10},{10,... | collective-permute-start | bytes 393224 | tf_op jit(solution)/shard_map/ppermute | solution.py:18
  12.6 12.0 %collective-permute-start.6 = (bf16[256,512]{1,0:T(8,128)(2,1)S(1)}, bf16[256,512]{1,0:T(8,128)(2,1)S(1)}, u32[]{:S(2)}, u32[]{:S(2)}) collective-permute-start(bf16[256,512]{1,0:T(8,128)(2,1)S(1)} %pad_maximum_fusion.1.refs_0_), channel_id=1, source_target_pairs={{0,12},{4,8},{8,4},{12,0},{1,13},{5,9},{9,5},{13,1},{2,14},{6,10},... | collective-permute-start | bytes 786440 | tf_op jit(solution)/shard_map/ppermute | solution.py:28
  16.2 23.0 %collective-permute-start.5 = (bf16[256,512]{1,0:T(8,128)(2,1)S(1)}, bf16[256,512]{1,0:T(8,128)(2,1)S(1)}, u32[]{:S(2)}, u32[]{:S(2)}) collective-permute-start(bf16[256,512]{1,0:T(8,128)(2,1)S(1)} %pad_maximum_fusion.1.refs_0_), channel_id=1, source_target_pairs={{0,8},{4,12},{8,0},{12,4},{1,9},{5,13},{9,1},{13,5},{2,10},{6,14},... | collective-permute-start | bytes 786440 | tf_op jit(solution)/shard_map/ppermute | solution.py:28
  16.2 23.0 %collective-permute-start.4 = (bf16[256,512]{1,0:T(8,128)(2,1)S(1)}, bf16[256,512]{1,0:T(8,128)(2,1)S(1)}, u32[]{:S(2)}, u32[]{:S(2)}) collective-permute-start(bf16[256,512]{1,0:T(8,128)(2,1)S(1)} %pad_maximum_fusion.1.refs_0_), channel_id=1, source_target_pairs={{0,4},{4,0},{8,12},{12,8},{1,5},{5,1},{9,13},{13,9},{2,6},{6,2},{1... | collective-permute-start | bytes 786440 | tf_op jit(solution)/shard_map/ppermute | solution.py:28
  17.1 6.4 %collective-permute-start.1 = (bf16[128,512]{1,0:T(8,128)(2,1)S(1)}, bf16[128,512]{1,0:T(8,128)(2,1)S(1)}, u32[]{:S(2)}, u32[]{:S(2)}) collective-permute-start(bf16[128,512]{1,0:T(8,128)(2,1)S(1)} %get-tuple-element.130), channel_id=1, source_target_pairs={{0,2},{1,3},{2,0},{3,1},{4,6},{5,7},{6,4},{7,5},{8,10},{9,11},{10,... | collective-permute-start | bytes 393224 | tf_op jit(solution)/shard_map/ppermute | solution.py:18
  18.1 6.5 %collective-permute-start = (bf16[128,512]{1,0:T(8,128)(2,1)S(1)}, bf16[128,512]{1,0:T(8,128)(2,1)S(1)}, u32[]{:S(2)}, u32[]{:S(2)}) collective-permute-start(bf16[128,512]{1,0:T(8,128)(2,1)S(1)} %get-tuple-element.128), channel_id=1, source_target_pairs={{0,3},{1,2},{2,1},{3,0},{4,7},{5,6},{6,5},{7,4},{8,11},{9,10},{10,... | collective-permute-start | bytes 393224 | tf_op jit(solution)/shard_map/ppermute | solution.py:18
  23.4 15.8 %collective-permute-start.7 = (f32[256,128]{0,1:T(8,128)S(1)}, f32[256,128]{0,1:T(8,128)S(1)}, u32[]{:S(2)}, u32[]{:S(2)}) collective-permute-start(f32[256,128]{0,1:T(8,128)S(1)} %pad_maximum_fusion.3), channel_id=1, source_target_pairs={{0,4},{4,0},{8,12},{12,8},{1,5},{5,1},{9,13},{13,9},{2,6},{6,2},{1... | collective-permute-start | bytes 393224 | tf_op jit(solution)/shard_map/ppermute | solution.py:28
  39.2 10.8 %collective-permute-start.9 = (bf16[256,512]{1,0:T(8,128)(2,1)S(1)}, bf16[256,512]{1,0:T(8,128)(2,1)S(1)}, u32[]{:S(2)}, u32[]{:S(2)}) collective-permute-start(bf16[256,512]{1,0:T(8,128)(2,1)S(1)} %pad_maximum_fusion.refs_0_), channel_id=1, source_target_pairs={{0,4},{4,0},{8,12},{12,8},{1,5},{5,1},{9,13},{13,9},{2,6},{6,2},{1... | collective-permute-start | bytes 786440 | tf_op jit(solution)/shard_map/ppermute | solution.py:28
  39.3 10.5 %collective-permute-start.8 = (f32[256,128]{0,1:T(8,128)S(1)}, f32[256,128]{0,1:T(8,128)S(1)}, u32[]{:S(2)}, u32[]{:S(2)}) collective-permute-start(f32[256,128]{0,1:T(8,128)S(1)} %fusion.14), channel_id=1, source_target_pairs={{0,8},{4,12},{8,0},{12,4},{1,9},{5,13},{9,1},{13,5},{2,10},{6,14},... | collective-permute-start | bytes 393224 | tf_op jit(solution)/shard_map/ppermute | solution.py:28
  50.0 1.8 %collective-permute-start.11 = (bf16[64,3584]{1,0:T(8,128)(2,1)S(1)}, bf16[64,3584]{1,0:T(8,128)(2,1)S(1)}, u32[]{:S(2)}, u32[]{:S(2)}) collective-permute-start(bf16[64,3584]{1,0:T(8,128)(2,1)S(1)} %get-tuple-element.70), channel_id=1, source_target_pairs={{0,1},{1,0},{2,3},{3,2},{4,5},{5,4},{6,7},{7,6},{8,9},{9,8},{10,11... | collective-permute-start | bytes 1376264 | tf_op jit(solution)/shard_map/ppermute | solution.py:18
  50.0 2.5 %collective-permute-start.10 = (bf16[64,3584]{1,0:T(8,128)(2,1)S(1)}, bf16[64,3584]{1,0:T(8,128)(2,1)S(1)}, u32[]{:S(2)}, u32[]{:S(2)}) collective-permute-start(bf16[64,3584]{1,0:T(8,128)(2,1)S(1)} %get-tuple-element.68), channel_id=1, source_target_pairs={{0,1},{1,0},{2,3},{3,2},{4,5},{5,4},{6,7},{7,6},{8,9},{9,8},{10,11... | collective-permute-start | bytes 1376264 | tf_op jit(solution)/shard_map/ppermute | solution.py:18
  54.2 17.1 %copy-start.11 = (s32[4]{0:T(128)S(1)}, s32[4]{0:T(128)}, u32[]{:S(2)}) copy-start(s32[4]{0:T(128)} %param.13) | copy-start | bytes 52
  54.2 17.2 %copy-start.10 = (s32[1,256]{1,0:T(1,128)S(1)}, s32[1,256]{1,0:T(1,128)}, u32[]{:S(2)}) copy-start(s32[1,256]{1,0:T(1,128)} %param.12) | copy-start | bytes 3076
  54.2 24.3 %collective-permute-start.15 = (bf16[128,3584]{1,0:T(8,128)(2,1)}, bf16[128,3584]{1,0:T(8,128)(2,1)S(1)}, u32[]{:S(2)}, u32[]{:S(2)}) collective-permute-start(bf16[128,3584]{1,0:T(8,128)(2,1)} %pair.4), channel_id=1, source_target_pairs={{0,2},{1,3},{2,0},{3,1},{4,6},{5,7},{6,4},{7,5},{8,10},{9,11},{10,... | collective-permute-start | bytes 2752520 | tf_op jit(solution)/shard_map/ppermute | solution.py:18
  56.0 14.6 %collective-permute-start.12 = (bf16[256,512]{1,0:T(8,128)(2,1)S(1)}, bf16[256,512]{1,0:T(8,128)(2,1)S(1)}, u32[]{:S(2)}, u32[]{:S(2)}) collective-permute-start(bf16[256,512]{1,0:T(8,128)(2,1)S(1)} %pad_maximum_fusion.refs_0_), channel_id=1, source_target_pairs={{0,8},{4,12},{8,0},{12,4},{1,9},{5,13},{9,1},{13,5},{2,10},{6,14},... | collective-permute-start | bytes 786440 | tf_op jit(solution)/shard_map/ppermute | solution.py:28
  65.2 0.9 copy-start.4
  70.6 2.0 %collective-permute-start.14 = (bf16[64,3584]{1,0:T(8,128)(2,1)}, bf16[64,3584]{1,0:T(8,128)(2,1)S(1)}, u32[]{:S(2)}, u32[]{:S(2)}) collective-permute-start(bf16[64,3584]{1,0:T(8,128)(2,1)} %get-tuple-element.77), channel_id=1, source_target_pairs={{0,1},{1,0},{2,3},{3,2},{4,5},{5,4},{6,7},{7,6},{8,9},{9,8},{10,11... | collective-permute-start | bytes 1376264 | tf_op jit(solution)/shard_map/ppermute | solution.py:18
  70.6 2.7 %collective-permute-start.13 = (bf16[64,3584]{1,0:T(8,128)(2,1)}, bf16[64,3584]{1,0:T(8,128)(2,1)S(1)}, u32[]{:S(2)}, u32[]{:S(2)}) collective-permute-start(bf16[64,3584]{1,0:T(8,128)(2,1)} %get-tuple-element.75), channel_id=1, source_target_pairs={{0,1},{1,0},{2,3},{3,2},{4,5},{5,4},{6,7},{7,6},{8,9},{9,8},{10,11... | collective-permute-start | bytes 1376264 | tf_op jit(solution)/shard_map/ppermute | solution.py:18
  71.3 7.8 %collective-permute-start.18 = (bf16[256,512]{1,0:T(8,128)(2,1)S(1)}, bf16[256,512]{1,0:T(8,128)(2,1)S(1)}, u32[]{:S(2)}, u32[]{:S(2)}) collective-permute-start(bf16[256,512]{1,0:T(8,128)(2,1)S(1)} %bitcast.45), channel_id=1, source_target_pairs={{0,1},{1,0},{2,3},{3,2},{4,5},{5,4},{6,7},{7,6},{8,9},{9,8},{10,11... | collective-permute-start | bytes 786440 | tf_op jit(solution)/shard_map/ppermute | solution.py:18
  73.3 1.2 copy-start.5
  76.2 34.0 %collective-permute-start.27 = (bf16[128,3584]{1,0:T(8,128)(2,1)}, bf16[128,3584]{1,0:T(8,128)(2,1)}, u32[]{:S(2)}, u32[]{:S(2)}) collective-permute-start(bf16[128,3584]{1,0:T(8,128)(2,1)} %pair.5), channel_id=1, source_target_pairs={{0,2},{1,3},{2,0},{3,1},{4,6},{5,7},{6,4},{7,5},{8,10},{9,11},{10,... | collective-permute-start | bytes 2752520 | tf_op jit(solution)/shard_map/ppermute | solution.py:18
  76.5 2.5 %collective-permute-start.16 = (bf16[256,512]{1,0:T(8,128)(2,1)S(1)}, bf16[256,512]{1,0:T(8,128)(2,1)S(1)}, u32[]{:S(2)}, u32[]{:S(2)}) collective-permute-start(bf16[256,512]{1,0:T(8,128)(2,1)S(1)} %pad_maximum_fusion.refs_0_), channel_id=1, source_target_pairs={{4,8},{8,4},{5,9},{9,5},{6,10},{10,6},{7,11},{11,7},{20,24},{24,20... | collective-permute-start | bytes 786440 | tf_op jit(solution)/shard_map/ppermute | solution.py:28
  77.2 10.0 %collective-permute-start.17 = (bf16[256,512]{1,0:T(8,128)(2,1)S(1)}, bf16[256,512]{1,0:T(8,128)(2,1)S(1)}, u32[]{:S(2)}, u32[]{:S(2)}) collective-permute-start(bf16[256,512]{1,0:T(8,128)(2,1)S(1)} %collective-permute-done.12.refs_2_), channel_id=1, source_target_pairs={{4,0},{8,12},{5,1},{9,13},{6,2},{10,14},{7,3},{11,15},{20,16},{24,... | collective-permute-start | bytes 786440 | tf_op jit(solution)/shard_map/ppermute | solution.py:28
  87.2 13.4 %collective-permute-start.20 = (bf16[256,512]{1,0:T(8,128)(2,1)S(1)}, bf16[256,512]{1,0:T(8,128)(2,1)S(1)}, u32[]{:S(2)}, u32[]{:S(2)}) collective-permute-start(bf16[256,512]{1,0:T(8,128)(2,1)S(1)} %collective-permute-done.18.refs_0_), channel_id=1, source_target_pairs={{0,8},{4,12},{8,0},{12,4},{1,9},{5,13},{9,1},{13,5},{2,10},{6,14},... | collective-permute-start | bytes 786440 | tf_op jit(solution)/shard_map/ppermute | solution.py:28
  87.3 13.4 %collective-permute-start.19 = (bf16[256,512]{1,0:T(8,128)(2,1)S(1)}, bf16[256,512]{1,0:T(8,128)(2,1)S(1)}, u32[]{:S(2)}, u32[]{:S(2)}) collective-permute-start(bf16[256,512]{1,0:T(8,128)(2,1)S(1)} %collective-permute-done.18.refs_0_), channel_id=1, source_target_pairs={{0,4},{4,0},{8,12},{12,8},{1,5},{5,1},{9,13},{13,9},{2,6},{6,2},{1... | collective-permute-start | bytes 786440 | tf_op jit(solution)/shard_map/ppermute | solution.py:28
  97.9 0.9 copy-start.2
  100.7 0.7 copy-start.6
  101.4 2.5 %collective-permute-start.22 = (bf16[64,3584]{1,0:T(8,128)(2,1)S(1)}, bf16[64,3584]{1,0:T(8,128)(2,1)S(1)}, u32[]{:S(2)}, u32[]{:S(2)}) collective-permute-start(bf16[64,3584]{1,0:T(8,128)(2,1)S(1)} %get-tuple-element.87), channel_id=1, source_target_pairs={{0,1},{1,0},{2,3},{3,2},{4,5},{5,4},{6,7},{7,6},{8,9},{9,8},{10,11... | collective-permute-start | bytes 1376264 | tf_op jit(solution)/shard_map/ppermute | solution.py:18
  101.4 3.7 %collective-permute-start.21 = (bf16[64,3584]{1,0:T(8,128)(2,1)}, bf16[64,3584]{1,0:T(8,128)(2,1)}, u32[]{:S(2)}, u32[]{:S(2)}) collective-permute-start(bf16[64,3584]{1,0:T(8,128)(2,1)} %get-tuple-element.85), channel_id=1, source_target_pairs={{0,1},{1,0},{2,3},{3,2},{4,5},{5,4},{6,7},{7,6},{8,9},{9,8},{10,11... | collective-permute-start | bytes 1376264 | tf_op jit(solution)/shard_map/ppermute | solution.py:18
  102.0 8.2 %collective-permute-start.26 = (bf16[4,4224]{1,0:T(4,128)(2,1)S(1)}, bf16[4,4224]{1,0:T(4,128)(2,1)S(1)}, u32[]{:S(2)}, u32[]{:S(2)}) collective-permute-start(bf16[4,4224]{1,0:T(4,128)(2,1)S(1)} %pad_maximum_fusion.4), channel_id=1, source_target_pairs={{0,3},{1,2},{2,1},{3,0},{4,7},{5,6},{6,5},{7,4},{8,11},{9,10},{10,... | collective-permute-start | bytes 101384 | tf_op jit(solution)/shard_map/ppermute | solution.py:18
  103.4 6.8 %collective-permute-start.25 = (bf16[4,4224]{1,0:T(4,128)(2,1)S(1)}, bf16[4,4224]{1,0:T(4,128)(2,1)}, u32[]{:S(2)}, u32[]{:S(2)}) collective-permute-start(bf16[4,4224]{1,0:T(4,128)(2,1)S(1)} %pad_maximum_fusion.4), channel_id=1, source_target_pairs={{0,2},{1,3},{2,0},{3,1},{4,6},{5,7},{6,4},{7,5},{8,10},{9,11},{10,... | collective-permute-start | bytes 101384 | tf_op jit(solution)/shard_map/ppermute | solution.py:18
  103.9 6.3 %collective-permute-start.24 = (bf16[4,4224]{1,0:T(4,128)(2,1)S(1)}, bf16[4,4224]{1,0:T(4,128)(2,1)}, u32[]{:S(2)}, u32[]{:S(2)}) collective-permute-start(bf16[4,4224]{1,0:T(4,128)(2,1)S(1)} %pad_maximum_fusion.4), channel_id=1, source_target_pairs={{0,1},{1,0},{2,3},{3,2},{4,5},{5,4},{6,7},{7,6},{8,9},{9,8},{10,11... | collective-permute-start | bytes 101384 | tf_op jit(solution)/shard_map/ppermute | solution.py:18
  105.1 1.2 copy-start.3
  108.4 24.4 %collective-permute-start.33 = (bf16[128,3584]{1,0:T(8,128)(2,1)S(1)}, bf16[128,3584]{1,0:T(8,128)(2,1)S(1)}, u32[]{:S(2)}, u32[]{:S(2)}) collective-permute-start(bf16[128,3584]{1,0:T(8,128)(2,1)S(1)} %pair.6), channel_id=1, source_target_pairs={{0,2},{1,3},{2,0},{3,1},{4,6},{5,7},{6,4},{7,5},{8,10},{9,11},{10,... | collective-permute-start | bytes 2752520 | tf_op jit(solution)/shard_map/ppermute | solution.py:18
  111.3 13.3 %collective-permute-start.23 = (bf16[256,512]{1,0:T(8,128)(2,1)S(1)}, bf16[256,512]{1,0:T(8,128)(2,1)S(1)}, u32[]{:S(2)}, u32[]{:S(2)}) collective-permute-start(bf16[256,512]{1,0:T(8,128)(2,1)S(1)} %bitcast.38), channel_id=1, source_target_pairs={{0,4},{4,0},{8,12},{12,8},{1,5},{5,1},{9,13},{13,9},{2,6},{6,2},{1... | collective-permute-start | bytes 786440 | tf_op jit(solution)/shard_map/ppermute | solution.py:28
  111.4 13.2 %collective-permute-start.28 = (bf16[256,512]{1,0:T(8,128)(2,1)S(1)}, bf16[256,512]{1,0:T(8,128)(2,1)S(1)}, u32[]{:S(2)}, u32[]{:S(2)}) collective-permute-start(bf16[256,512]{1,0:T(8,128)(2,1)S(1)} %collective-permute-done.18.refs_0_), channel_id=1, source_target_pairs={{4,8},{8,4},{5,9},{9,5},{6,10},{10,6},{7,11},{11,7},{20,24},{24,20... | collective-permute-start | bytes 786440 | tf_op jit(solution)/shard_map/ppermute | solution.py:28
  112.1 13.2 %collective-permute-start.29 = (bf16[256,512]{1,0:T(8,128)(2,1)S(1)}, bf16[256,512]{1,0:T(8,128)(2,1)S(1)}, u32[]{:S(2)}, u32[]{:S(2)}) collective-permute-start(bf16[256,512]{1,0:T(8,128)(2,1)S(1)} %collective-permute-done.20.refs_2_), channel_id=1, source_target_pairs={{4,0},{8,12},{5,1},{9,13},{6,2},{10,14},{7,3},{11,15},{20,16},{24,... | collective-permute-start | bytes 786440 | tf_op jit(solution)/shard_map/ppermute | solution.py:28
  117.2 15.7 %copy-start.7 = (bf16[256,512]{1,0:T(8,128)(2,1)S(1)}, bf16[256,512]{1,0:T(8,128)(2,1)}, u32[]{:S(2)}) copy-start(bf16[256,512]{1,0:T(8,128)(2,1)} %copy-done.6) | copy-start | bytes 786436
  125.3 1.8 %collective-permute-start.31 = (bf16[64,3584]{1,0:T(8,128)(2,1)S(1)}, bf16[64,3584]{1,0:T(8,128)(2,1)S(1)}, u32[]{:S(2)}, u32[]{:S(2)}) collective-permute-start(bf16[64,3584]{1,0:T(8,128)(2,1)S(1)} %get-tuple-element.100), channel_id=1, source_target_pairs={{0,1},{1,0},{2,3},{3,2},{4,5},{5,4},{6,7},{7,6},{8,9},{9,8},{10,11... | collective-permute-start | bytes 1376264 | tf_op jit(solution)/shard_map/ppermute | solution.py:18
  125.3 2.5 %collective-permute-start.30 = (bf16[64,3584]{1,0:T(8,128)(2,1)S(1)}, bf16[64,3584]{1,0:T(8,128)(2,1)S(1)}, u32[]{:S(2)}, u32[]{:S(2)}) collective-permute-start(bf16[64,3584]{1,0:T(8,128)(2,1)S(1)} %get-tuple-element.98), channel_id=1, source_target_pairs={{0,1},{1,0},{2,3},{3,2},{4,5},{5,4},{6,7},{7,6},{8,9},{9,8},{10,11... | collective-permute-start | bytes 1376264 | tf_op jit(solution)/shard_map/ppermute | solution.py:18
  128.3 17.9 %collective-permute-start.34 = (bf16[64,3584]{1,0:T(8,128)(2,1)S(1)}, bf16[64,3584]{1,0:T(8,128)(2,1)S(1)}, u32[]{:S(2)}, u32[]{:S(2)}) collective-permute-start(bf16[64,3584]{1,0:T(8,128)(2,1)S(1)} %get-tuple-element.101), channel_id=1, source_target_pairs={{0,2},{1,3},{2,0},{3,1},{4,6},{5,7},{6,4},{7,5},{8,10},{9,11},{10,... | collective-permute-start | bytes 1376264 | tf_op jit(solution)/shard_map/ppermute | solution.py:18
  128.7 17.5 %collective-permute-start.32 = (bf16[256,512]{1,0:T(8,128)(2,1)S(1)}, bf16[256,512]{1,0:T(8,128)(2,1)S(1)}, u32[]{:S(2)}, u32[]{:S(2)}) collective-permute-start(bf16[256,512]{1,0:T(8,128)(2,1)S(1)} %bitcast.39), channel_id=1, source_target_pairs={{0,8},{4,12},{8,0},{12,4},{1,9},{5,13},{9,1},{13,5},{2,10},{6,14},... | collective-permute-start | bytes 786440 | tf_op jit(solution)/shard_map/ppermute | solution.py:28
  146.2 1.9 %collective-permute-start.44 = (bf16[64,3584]{1,0:T(8,128)(2,1)S(1)}, bf16[64,3584]{1,0:T(8,128)(2,1)S(1)}, u32[]{:S(2)}, u32[]{:S(2)}) collective-permute-start(bf16[64,3584]{1,0:T(8,128)(2,1)S(1)} %get-tuple-element.121), channel_id=1, source_target_pairs={{0,1},{1,0},{2,3},{3,2},{4,5},{5,4},{6,7},{7,6},{8,9},{9,8},{10,11... | collective-permute-start | bytes 1376264 | tf_op jit(solution)/shard_map/ppermute | solution.py:18
  146.3 2.5 %collective-permute-start.43 = (bf16[64,3584]{1,0:T(8,128)(2,1)S(1)}, bf16[64,3584]{1,0:T(8,128)(2,1)S(1)}, u32[]{:S(2)}, u32[]{:S(2)}) collective-permute-start(bf16[64,3584]{1,0:T(8,128)(2,1)S(1)} %get-tuple-element.119), channel_id=1, source_target_pairs={{0,1},{1,0},{2,3},{3,2},{4,5},{5,4},{6,7},{7,6},{8,9},{9,8},{10,11... | collective-permute-start | bytes 1376264 | tf_op jit(solution)/shard_map/ppermute | solution.py:18
  146.8 2.6 %collective-permute-start.40 = (bf16[64,3584]{1,0:T(8,128)(2,1)S(1)}, bf16[64,3584]{1,0:T(8,128)(2,1)S(1)}, u32[]{:S(2)}, u32[]{:S(2)}) collective-permute-start(bf16[64,3584]{1,0:T(8,128)(2,1)S(1)} %get-tuple-element.113), channel_id=1, source_target_pairs={{0,1},{1,0},{2,3},{3,2},{4,5},{5,4},{6,7},{7,6},{8,9},{9,8},{10,11... | collective-permute-start | bytes 1376264 | tf_op jit(solution)/shard_map/ppermute | solution.py:18
  146.9 3.2 %collective-permute-start.35 = (bf16[64,3584]{1,0:T(8,128)(2,1)S(1)}, bf16[64,3584]{1,0:T(8,128)(2,1)S(1)}, u32[]{:S(2)}, u32[]{:S(2)}) collective-permute-start(bf16[64,3584]{1,0:T(8,128)(2,1)S(1)} %get-tuple-element.105), channel_id=1, source_target_pairs={{0,1},{1,0},{2,3},{3,2},{4,5},{5,4},{6,7},{7,6},{8,9},{9,8},{10,11... | collective-permute-start | bytes 1376264 | tf_op jit(solution)/shard_map/ppermute | solution.py:18
  147.3 4.4 %collective-permute-start.39 = (bf16[64,3584]{1,0:T(8,128)(2,1)S(1)}, bf16[64,3584]{1,0:T(8,128)(2,1)S(1)}, u32[]{:S(2)}, u32[]{:S(2)}) collective-permute-start(bf16[64,3584]{1,0:T(8,128)(2,1)S(1)} %get-tuple-element.111), channel_id=1, source_target_pairs={{0,1},{1,0},{2,3},{3,2},{4,5},{5,4},{6,7},{7,6},{8,9},{9,8},{10,11... | collective-permute-start | bytes 1376264 | tf_op jit(solution)/shard_map/ppermute | solution.py:18
  148.1 4.3 %collective-permute-start.38 = (bf16[64,3584]{1,0:T(8,128)(2,1)S(1)}, bf16[64,3584]{1,0:T(8,128)(2,1)S(1)}, u32[]{:S(2)}, u32[]{:S(2)}) collective-permute-start(bf16[64,3584]{1,0:T(8,128)(2,1)S(1)} %get-tuple-element.109), channel_id=1, source_target_pairs={{0,1},{1,0},{2,3},{3,2},{4,5},{5,4},{6,7},{7,6},{8,9},{9,8},{10,11... | collective-permute-start | bytes 1376264 | tf_op jit(solution)/shard_map/ppermute | solution.py:18
  148.8 5.9 %collective-permute-start.42 = (bf16[64,3584]{1,0:T(8,128)(2,1)S(1)}, bf16[64,3584]{1,0:T(8,128)(2,1)S(1)}, u32[]{:S(2)}, u32[]{:S(2)}) collective-permute-start(bf16[64,3584]{1,0:T(8,128)(2,1)S(1)} %get-tuple-element.117), channel_id=1, source_target_pairs={{0,1},{1,0},{2,3},{3,2},{4,5},{5,4},{6,7},{7,6},{8,9},{9,8},{10,11... | collective-permute-start | bytes 1376264 | tf_op jit(solution)/shard_map/ppermute | solution.py:18
  149.4 5.2 %collective-permute-start.41 = (bf16[64,3584]{1,0:T(8,128)(2,1)S(1)}, bf16[64,3584]{1,0:T(8,128)(2,1)S(1)}, u32[]{:S(2)}, u32[]{:S(2)}) collective-permute-start(bf16[64,3584]{1,0:T(8,128)(2,1)S(1)} %get-tuple-element.115), channel_id=1, source_target_pairs={{0,1},{1,0},{2,3},{3,2},{4,5},{5,4},{6,7},{7,6},{8,9},{9,8},{10,11... | collective-permute-start | bytes 1376264 | tf_op jit(solution)/shard_map/ppermute | solution.py:18
  150.1 12.6 %collective-permute-start.45 = (bf16[64,3584]{1,0:T(8,128)(2,1)S(1)}, bf16[64,3584]{1,0:T(8,128)(2,1)S(1)}, u32[]{:S(2)}, u32[]{:S(2)}) collective-permute-start(bf16[64,3584]{1,0:T(8,128)(2,1)S(1)} %get-tuple-element.122), channel_id=1, source_target_pairs={{0,2},{1,3},{2,0},{3,1},{4,6},{5,7},{6,4},{7,5},{8,10},{9,11},{10,... | collective-permute-start | bytes 1376264 | tf_op jit(solution)/shard_map/ppermute | solution.py:18
  151.8 10.9 %collective-permute-start.36 = (bf16[256,512]{1,0:T(8,128)(2,1)S(1)}, bf16[256,512]{1,0:T(8,128)(2,1)S(1)}, u32[]{:S(2)}, u32[]{:S(2)}) collective-permute-start(bf16[256,512]{1,0:T(8,128)(2,1)S(1)} %bitcast.40), channel_id=1, source_target_pairs={{4,8},{8,4},{5,9},{9,5},{6,10},{10,6},{7,11},{11,7},{20,24},{24,20... | collective-permute-start | bytes 786440 | tf_op jit(solution)/shard_map/ppermute | solution.py:28
  152.5 10.2 %collective-permute-start.37 = (bf16[256,512]{1,0:T(8,128)(2,1)S(1)}, bf16[256,512]{1,0:T(8,128)(2,1)S(1)}, u32[]{:S(2)}, u32[]{:S(2)}) collective-permute-start(bf16[256,512]{1,0:T(8,128)(2,1)S(1)} %collective-permute-done.32.refs_2_), channel_id=1, source_target_pairs={{4,0},{8,12},{5,1},{9,13},{6,2},{10,14},{7,3},{11,15},{20,16},{24,... | collective-permute-start | bytes 786440 | tf_op jit(solution)/shard_map/ppermute | solution.py:28
  162.7 14.7 %copy-start.1 = (bf16[7168,64]{0,1:T(8,128)(2,1)S(1)}, bf16[7168,64]{0,1:T(8,128)(2,1)}, u32[]{:S(2)}) copy-start(bf16[7168,64]{0,1:T(8,128)(2,1)} %param.10) | copy-start | bytes 2752516

commit v10 on v9

--- a/solution.py
+++ b/solution.py
@@ -45,20 +45,20 @@
     return blocks + [middle, ends]
 
 
-def terms_kernel(size, per_group, count, first, adds, per_part, parts, place_ref, *refs):
-    total = per_group * count
-    groups = [refs[per_group * group :][:per_group] for group in range(count)]
-    w_ref, add_refs, outs = refs[total], refs[total + 1 :][:adds], refs[total + 1 + adds : -4]
+def terms_kernel(size, count, first, lows, place_ref, *refs):
+    blocks, w_ref = refs[:count], refs[count]
     feats, held, sems, held_sems = refs[-4:]
+    outs = refs[count + 1 : -4]
+    add_refs = []
+    if lows is not None:
+        add_refs, outs = outs[: 1 + lows], outs[-1:]
     width, tile = feats.shape[1] // size, outs[0].shape[1]
-    tall = feats.shape[0] // len(groups)
     j, steps = pl.program_id(0), pl.num_programs(0)
     slots = held.shape[0]
 
-    def put(value, group, source, slot):
+    def put(value, source, slot):
         at = pl.ds(pl.multiple_of(source * width, width), width)
-        rows = pl.ds(group * tall, tall)
-        return pltpu.make_async_copy(value, feats.at[rows, at], sems.at[group * size + slot])
+        return pltpu.make_async_copy(value, feats.at[:, at], sems.at[slot])
 
     def fetch(step):
         slot = lax.rem(step, slots)
@@ -67,26 +67,22 @@
 
     @pl.when(j == 0)
     def _():
-        copies = []
         place = place_ref[0]
-        for group, blocks in enumerate(groups):
-            straight = 3 if per_group == 5 else 4
-            copies += [
-                put(blocks[k], group, lax.bitwise_xor(place, k), k) for k in range(straight)
-            ]
+        straight = 3 if count == 5 else 4
+        copies = [put(blocks[k], lax.bitwise_xor(place, k), k) for k in range(straight)]
         for copy in copies:
             copy.start()
         for step in range(slots):
             fetch(step).start()
         inside = jnp.logical_or(place == 1, place == 2)
-        for group, blocks in enumerate(groups if per_group == 5 else ()):
-            for chosen, block in ((inside, blocks[3]), (jnp.logical_not(inside), blocks[4])):
-
-                @pl.when(chosen)
-                def _():
-                    last = put(block, group, lax.bitwise_xor(place, 3), 3)
-                    last.start()
-                    last.wait()
+        relayed = ((inside, 3), (jnp.logical_not(inside), 4)) if count == 5 else ()
+        for chosen, k in relayed:
+
+            @pl.when(chosen)
+            def _():
+                last = put(blocks[k], lax.bitwise_xor(place, 3), 3)
+                last.start()
+                last.wait()
 
         for copy in copies:
             copy.wait()
@@ -94,114 +90,88 @@
     fetch(j).wait()
     weight = held[lax.rem(j, slots)].reshape(size * width, tile)
     terms = jnp.dot(feats[...], weight, preferred_element_type=f32)
-    if adds:
-        wide_refs, low_refs = add_refs[:-2], add_refs[-2:]
-        tall = low_refs[0].shape[0]
-        top = feats.shape[0] - 2 * tall
-        for part, ref in enumerate(wide_refs):
-
-            @pl.when(j // per_part == part)
-            def _():
-                total = terms + ref[...].astype(f32)
-                if part == len(wide_refs) - 1:
-                    outs[0][:top] = total[:top].astype(bf16)
-                    for row, low_ref in zip((top, top + tall), low_refs):
-                        low = total[row : row + tall] + low_ref[...].astype(f32)
-                        outs[0][row : row + tall] = low.astype(bf16)
-                else:
-                    outs[0][...] = total.astype(bf16)
-
-
-    def write(some):
-        row = 0
-        for out_ref in some:
+    if add_refs:
+        terms = terms + add_refs[0][...].astype(f32)
+    row = 0
+    for low_ref in reversed(add_refs[1:]):
+        row += low_ref.shape[0]
+        cut = slice(feats.shape[0] - row, feats.shape[0] - row + low_ref.shape[0])
+        outs[0][cut] = (terms[cut] + low_ref[...].astype(f32)).astype(bf16)
+    if add_refs:
+        outs[0][: feats.shape[0] - row] = terms[: feats.shape[0] - row].astype(bf16)
+    else:
+        for out_ref in outs:
             out_ref[...] = terms[row : row + out_ref.shape[0]].astype(bf16)
             row += out_ref.shape[0]
-
-    each = len(outs) // parts
-    if parts == 1 and not adds:
-        write(outs)
-    for part in range(parts if parts > 1 else 0):
-        pl.when(j // per_part == part)(
-            functools.partial(write, outs[part * each : (part + 1) * each])
-        )
 
     @pl.when(j + slots < steps)
     def _():
         fetch(j + slots).start()
 
 
-def block_terms(groups, down_weight, col_start, cols, outs, adds=(), low_adds=(), parts=1):
-    size, _, width, _ = down_weight.shape
-    rows = sum(outs)
-    tile = max(n for n in range(128, 897, 128) if cols % n == 0)
-    slots = min(3, cols // tile)
-    blocks = [block for group in groups for block in group]
-    per_part = adds[0].shape[1] // tile if adds else cols // parts // tile
-
-    def add_spec(part, tall=rows):
-        if parts == 1 and not adds or part is None:
-            return pl.BlockSpec((tall, tile), lambda j, place: (0, j))
-        return pl.BlockSpec(
-            (tall, tile), lambda j, place: (0, jnp.clip(j - part * per_part, 0, per_part - 1))
-        )
-
-    add_specs = [add_spec(part) for part in range(len(adds))]
-    if adds:
-        add_specs += [add_spec(len(adds) - 1, value.shape[0]) for value in low_adds]
-        adds = [*adds, *low_adds]
-
+def block_terms(blocks, down_weight, part, parts, outs, adds=None, into=None):
+    size, _, width, every = down_weight.shape
+    rows, cols = sum(outs), every // parts
+    tile = max(n for n in range(128, 513, 128) if cols % n == 0)
+    slots = min(4, cols // tile)
+
+    def spec(tall, first=0):
+        return pl.BlockSpec((tall, tile), lambda j, place: (0, first + j))
+
+    operands = [*blocks, down_weight]
+    in_specs = [pl.BlockSpec(memory_space=pltpu.HBM)] * len(operands)
+    out_shape = [jax.ShapeDtypeStruct((tall, cols), bf16) for tall in outs]
+    out_specs = [spec(tall) for tall in outs]
+    aliases = {}
+    if adds is not None:
+        operands += adds
+        in_specs += [spec(value.shape[0]) for value in adds]
+        out_shape = [jax.ShapeDtypeStruct((rows, every), bf16)]
+        out_specs = [spec(rows, part * (cols // tile))]
+    if into is not None:
+        operands.append(into)
+        in_specs.append(pl.BlockSpec(memory_space=pltpu.HBM))
+        aliases = {len(operands): 0}
     return pl.pallas_call(
         functools.partial(
             terms_kernel,
             size,
-            len(groups[0]),
-            len(groups),
-            col_start,
-            len(adds),
-            per_part,
-            parts,
+            len(blocks),
+            part * cols,
+            None if adds is None else len(adds) - 1,
         ),
-        out_shape=[jax.ShapeDtypeStruct((tall, cols // parts), bf16) for tall in outs] * parts,
+        out_shape=out_shape,
         grid_spec=pltpu.PrefetchScalarGridSpec(
             num_scalar_prefetch=1,
             grid=(cols // tile,),
-            in_specs=[pl.BlockSpec(memory_space=pltpu.HBM)] * (len(blocks) + 1)
-            + add_specs,
-            out_specs=[
-                add_spec(None if parts == 1 else part, tall)
-                for part in range(parts)
-                for tall in outs
-            ],
+            in_specs=in_specs,
+            out_specs=out_specs,
             scratch_shapes=[
                 pltpu.VMEM((rows, size * width), bf16),
                 pltpu.VMEM((slots, size, width, tile), bf16),
-                pltpu.SemaphoreType.DMA((len(groups) * size,)),
+                pltpu.SemaphoreType.DMA((size,)),
                 pltpu.SemaphoreType.DMA((slots,)),
             ],
         ),
+        input_output_aliases=aliases,
         compiler_params=pltpu.CompilerParams(vmem_limit_bytes=24 << 20),
         cost_estimate=pl.CostEstimate(
             flops=rows * size * width * cols // 4, bytes_accessed=1000, transcendentals=0
         ),
         name="terms",
-    )(
-        lax.axis_index("tensor").reshape(1),
-        *blocks,
-        down_weight,
-        *adds,
-    )
-
-
-def add_kernel(kept_ref, first_ref, second_ref, *outs):
-    rows, tall = first_ref.shape[0], outs[0].shape[0]
-    for index, other in enumerate((first_ref, second_ref)):
-        total = kept_ref[index * rows : (index + 1) * rows].astype(f32) + other[...].astype(f32)
-        at = index * rows % tall
-        outs[index * rows // tall][at : at + rows] = total.astype(bf16)
-
-
-def add_halves(kept, first, second, outs=1):
+    )(lax.axis_index("tensor").reshape(1), *operands)
+
+
+def add_kernel(count, kept_ref, *refs):
+    pieces, outs = refs[:count], refs[count:]
+    rows, tall = pieces[0].shape[0], outs[0].shape[0]
+    for index, piece in enumerate(pieces):
+        row = index * rows
+        total = kept_ref[row : row + rows].astype(f32) + piece[...].astype(f32)
+        outs[row // tall][row % tall : row % tall + rows] = total.astype(bf16)
+
+
+def add_pieces(kept, pieces, outs=1):
     rows, cols = kept.shape
     tile = max(n for n in range(128, 1025, 128) if cols % n == 0)
 
@@ -209,15 +179,15 @@
         return pl.BlockSpec((tall, tile), lambda j: (0, j))
 
     return pl.pallas_call(
-        add_kernel,
+        functools.partial(add_kernel, len(pieces)),
         out_shape=[jax.ShapeDtypeStruct((rows // outs, cols), bf16)] * outs,
         grid=(cols // tile,),
-        in_specs=[spec(rows), spec(rows // 2), spec(rows // 2)],
+        in_specs=[spec(rows)] + [spec(rows // len(pieces))] * len(pieces),
         out_specs=[spec(rows // outs)] * outs,
         compiler_params=pltpu.CompilerParams(vmem_limit_bytes=16 << 20),
         cost_estimate=pl.CostEstimate(flops=1000, bytes_accessed=1000, transcendentals=0),
         name="pair",
-    )(kept, first, second)
+    )(kept, *pieces)
 
 
 def gather_sums_kernel(*refs):
@@ -336,8 +306,8 @@
 def line_of_four(
     hidden_acts, output_grad, down_weight, input_basis, output_basis, token_example, example_group
 ):
-    tokens, cols = hidden_acts.shape
-    part, rows = cols // 2, tokens // 2
+    tokens = hidden_acts.shape[0]
+    rows = tokens // 2
     place = lax.axis_index("dp")
     turned = jnp.transpose(output_grad[0], (0, 2, 1))
     pieces = [lax.dynamic_index_in_dim(turned, place ^ k, 0, keepdims=False) for k in range(4)]
@@ -355,48 +325,53 @@
     far[1] = after(far[1], *blocks[1:])
     later_first = across(far[1], 1)
 
-    def far_terms(chunk, at, *earlier):
+    def far_terms(chunk, at, pieces, *earlier):
         chunk = [after(chunk[0], *earlier)] + chunk[1:] if earlier else chunk
-        return block_terms([chunk], down_weight, at * part, part, [rows // 2, rows // 2, rows])
-
-    def pair_sum(first, last, kept, *earlier):
-        (pair,) = add_halves(kept, swap(after(first, *earlier), 1), swap(after(last, *earlier), 1))
-        return pair, swap(pair, 2)
-
-    first, last, kept = far_terms(blocks, 0)
-    pair0, sum0 = pair_sum(first, last, kept, partner, later_first)
-
-    later = [far[1], later_first, across(after(far[1], pair0), 2)]
-    first, last, kept = far_terms(blocks, 1, pair0)
-    pair1, sum1 = pair_sum(first, last, kept, later[2])
-
-    later = spread_last(later, pair1)
-    beside = spread_first(after(beside, pair1, *later[3:]))
-    acts_low, grads_low = jnp.split(after(low, pair1, sum0) + partner, 2, axis=1)
-    example_grad = example_gradients(
-        acts_low, grads_low, token_example[0], example_group.shape[0]
-    )
-    gathered = gather_examples(example_grad, example_group)
-    first, last, kept = far_terms(later, 0, example_grad)
-    pair2, sum2 = pair_sum(first, last, kept, *beside)
+        outs = [rows // pieces] * pieces + [rows]
+        *sent, kept = block_terms(chunk, down_weight, at, 2, outs)
+        return sent, kept
+
+    def pair_sum(sent, kept, *earlier, outs=1):
+        pair = add_pieces(kept, [swap(after(term, *earlier), 1) for term in sent], outs)
+        return pair[0], [swap(term, 2) for term in pair]
+
+    sent, kept = far_terms(blocks, 0, 2, beside)
+    pair0, sum0 = pair_sum(sent, kept, partner, later_first)
+
+    later = after(far[1], pair0)
+    later = [far[1], later_first, across(later, 2), across(later, 3)]
+    sent, kept = far_terms(blocks, 1, 2, pair0)
+    pair1, sum1 = pair_sum(sent, kept, *later[2:])
+
+    beside = spread_first(after(beside, pair1))
+    sent, kept = far_terms(later, 0, 2, pair1, *sum0)
+    pair2, sum2 = pair_sum(sent, kept, *beside[1:])
 
     beside = spread_last(beside, pair2)
     own = after(own, pair2)
     own_first = across(own, 1)
-    every = order_examples(after(gathered, pair2, sum1))
+    acts_low, grads_low = jnp.split(after(low, pair2, *sum1) + partner, 2, axis=1)
+    example_grad = example_gradients(
+        acts_low, grads_low, token_example[0], example_group.shape[0]
+    )
+    gathered = gather_examples(example_grad, example_group)
+    sent, kept = far_terms(later, 1, 2, example_grad)
+    pair3, sum3 = pair_sum(sent, kept, own_first, *beside, outs=2)
+
+    own = [own, own_first, across(after(own, pair3), 2)]
+    every = order_examples(after(gathered, pair3, *sum2))
     fisher, group_grad = fisher_and_groups(every, example_grad.shape[1])
-    first, last, kept = far_terms(later, 1, fisher, group_grad)
-    first, last = (swap(after(term, own_first, *beside), 1) for term in (first, last))
-    pair3 = add_halves(kept, first, last, 2)
-    sum3 = [swap(term, 2) for term in pair3]
-
-    own = [own, own_first, across(after(own, pair3[0]), 2)]
-    beside = [after(beside[0], pair3[0], sum2)] + beside[1:]
-    near = block_terms([beside], down_weight, 0, cols, [rows // 2] * 4, parts=2)
-    near = [swap(after(term, own[2], sum3[0]), 1) for term in near]
-    own = spread_last(own, *near[:1])
-    adds = [gather_sums(near[:4], [sum0, sum2]), gather_sums(near[4:], [sum1])]
-    (result,) = block_terms([own], down_weight, 0, cols, [tokens], adds, sum3)
+    beside = [after(beside[0], fisher, group_grad)] + beside[1:]
+    near0 = block_terms(beside, down_weight, 0, 2, [rows // 2] * 4)
+    near0 = [swap(after(term, own[2], sum3[0]), 1) for term in near0]
+    own = spread_last(own, *near0[:1])
+    beside = [after(beside[0], *near0[:1])] + beside[1:]
+    near1 = block_terms(beside, down_weight, 1, 2, [rows // 2] * 4)
+    near1 = [swap(after(term, sum3[1]), 1) for term in near1]
+    adds = [gather_sums(near0, sum0 + sum2)]
+    (result,) = block_terms(own, down_weight, 0, 2, [tokens], adds)
+    adds = [gather_sums(near1, sum1)] + sum3
+    (result,) = block_terms(own, down_weight, 1, 2, [tokens], adds, result)
     return (result, fisher, group_grad)
 
 

time: 178 us -> 184 us (1.034)
  waiting for transfers between devices: 52 us -> 64.2 us
  starting transfers between devices: 38.6 us -> 35.2 us
    ppermute x17 -> x16, waiting for transfers between devices: 30 us -> 43.1 us  [across(): return lax.ppermute(value, 'tensor', pairs)]
    ppermute x17 -> x16, starting transfers between devices: 22.8 us -> 18.4 us  [across(): return lax.ppermute(value, 'tensor', pairs)]
    pallas_call x10 -> x12, Pallas kernels: 64.9 us -> 63.2 us  [the longest x8 58.7 us: block_terms(): pl.pallas_call(functools.partial(terms_kernel, size, len(blocks), part *...]
    unnamed x24 -> x32, local copies, waits for them, and re-layouts: 4.94 us -> 4.25 us
  transfers between devices with their start and end apart: 46 -> 45, of which waited for: 21 -> 23; matrix products, arithmetic and copies ran while one was open for 6% -> 5% of each run, Pallas kernels for 29% -> 31%
where the time goes in v10:
time: 184 us
  Pallas kernels  66.3 us (36%)
  waiting for transfers between devices  64.2 us (35%)
  starting transfers between devices  35.2 us (19%)
  local copies, waits for them, and re-layouts  7.74 us (4%)
  matrix products  7.55 us (4%)
    pallas_call x8, Pallas kernels, block_terms(): pl.pallas_call(functools.partial(terms_kernel, size, len(blocks), part *...  58.7 us
    ppermute x16, waiting for transfers between devices, across(): return lax.ppermute(value, 'tensor', pairs)  43.1 us
    ppermute x29, waiting for transfers between devices, swap(): return lax.ppermute(value, 'dp', [(d, d ^ step) for d in range(size)])  21.1 us
    ppermute x16, starting transfers between devices, across(): return lax.ppermute(value, 'tensor', pairs)  18.4 us
    ppermute x29, starting transfers between devices, swap(): return lax.ppermute(value, 'dp', [(d, d ^ step) for d in range(size)])  16.8 us
    pallas_call x4, Pallas kernels, add_pieces(): pl.pallas_call(functools.partial(add_kernel, len(pieces)), out_shape=[jax...  4.48 us
    unnamed x32, local copies, waits for them, and re-layouts  4.25 us
  transfers between devices with their start and end apart: 45, of which 23 were waited for; matrix products, arithmetic and copies ran while one was open for 5% of the time, Pallas kernels for 31%

profile of v10, /device:TPU:0, one launch (start us, length us, event | category | flops | bytes accessed | tf_op | source)
XLA Modules:
  0.0 183.7 jit_solution(8891617703612561127)
XLA Ops:
  0.7 2.1 %constant_dynamic-slice_fusion = (bf16[1,1,512,256]{3,2,1,0:T(8,128)(2,1)S(1)}, bf16[1,1,512,256]{3,2,1,0:T(8,128)(2,1)S(1)}, bf16[1,1,512,256]{3,2,1,0:T(8,128)(2,1)S(1)}, bf16[1,1,512,256]{3,2,1,0:T(8,128)(2,1)}) fusion(bf16[1,4,512,256]{3,2,1,0:T(8,128)(2,1)} %param.8, s32[]{:T(128)S(6)} %select_n.96, s32[]{:T(128)S(6)} %select_n.95, s32[]{:T(128)S(6)} %select_n.94, ...), kind=kLoop, calls=%fused_computation.32 | loop fusion | bytes 2097168 | tf_op jit(solution)/shard_map/dynamic-slice.7
  2.9 0.7 slice_bitcast_fusion
  3.5 2.9 %collective-permute-start.3 = (bf16[128,512]{1,0:T(8,128)(2,1)}, bf16[128,512]{1,0:T(8,128)(2,1)S(1)}, u32[]{:S(2)}, u32[]{:S(2)}) collective-permute-start(bf16[128,512]{1,0:T(8,128)(2,1)} %get-tuple-element.129), channel_id=1, source_target_pairs={{0,2},{1,3},{2,0},{3,1},{4,6},{5,7},{6,4},{7,5},{8,10},{9,11},{10,... | collective-permute-start | bytes 393224 | tf_op jit(solution)/shard_map/ppermute | solution.py:18
  6.7 3.3 %fusion.15 = f32[256,64]{0,1:T(8,128)S(1)} fusion(bf16[256,7168]{1,0:T(8,128)(2,1)} %param.7, bf16[7168,64]{0,1:T(8,128)(2,1)S(1)} %copy-done), kind=kOutput, calls=%fused_computation.38 | convolution fusion | flops 234881024 | bytes 4653056 | tf_op jit(solution)/shard_map/dot_general | solution.py:277
  10.7 1.9 %collective-permute-done.2 = bf16[128,512]{1,0:T(8,128)(2,1)S(1)} collective-permute-done((bf16[128,512]{1,0:T(8,128)(2,1)S(1)}, bf16[128,512]{1,0:T(8,128)(2,1)S(1)}, u32[]{:S(2)}, u32[]{:S(2)}) %collective-permute-start.2) | collective-permute-done | bytes 131104 | tf_op jit(solution)/shard_map/ppermute | solution.py:18
  12.6 3.6 %collective-permute-start.6 = (bf16[256,512]{1,0:T(8,128)(2,1)S(1)}, bf16[256,512]{1,0:T(8,128)(2,1)S(1)}, u32[]{:S(2)}, u32[]{:S(2)}) collective-permute-start(bf16[256,512]{1,0:T(8,128)(2,1)S(1)} %pad_maximum_fusion.1.refs_0_), channel_id=1, source_target_pairs={{0,12},{4,8},{8,4},{12,0},{1,13},{5,9},{9,5},{13,1},{2,14},{6,10},... | collective-permute-start | bytes 786440 | tf_op jit(solution)/shard_map/ppermute | solution.py:28
  16.2 0.9 collective-permute-start.4
  17.1 1.0 collective-permute-start.1
  18.2 5.2 %collective-permute-done.1 = bf16[128,512]{1,0:T(8,128)(2,1)S(1)} collective-permute-done((bf16[128,512]{1,0:T(8,128)(2,1)S(1)}, bf16[128,512]{1,0:T(8,128)(2,1)S(1)}, u32[]{:S(2)}, u32[]{:S(2)}) %collective-permute-start.1) | collective-permute-done | bytes 131104 | tf_op jit(solution)/shard_map/ppermute | solution.py:18
  23.4 1.2 collective-permute-start.8
  25.2 14.0 %collective-permute-done.5.refs_2_ = bf16[256,512]{1,0:T(8,128)(2,1)S(1)} collective-permute-done((bf16[256,512]{1,0:T(8,128)(2,1)S(1)}, bf16[256,512]{1,0:T(8,128)(2,1)S(1)}, u32[]{:S(2)}, u32[]{:S(2)}) %collective-permute-start.5) | collective-permute-done | bytes 262176 | tf_op jit(solution)/shard_map/ppermute | solution.py:28
  39.3 3.1 %collective-permute-start.9 = (f32[256,128]{0,1:T(8,128)S(1)}, f32[256,128]{0,1:T(8,128)S(1)}, u32[]{:S(2)}, u32[]{:S(2)}) collective-permute-start(f32[256,128]{0,1:T(8,128)S(1)} %fusion.14), channel_id=1, source_target_pairs={{0,8},{4,12},{8,0},{12,4},{1,9},{5,13},{9,1},{13,5},{2,10},{6,14},... | collective-permute-start | bytes 393224 | tf_op jit(solution)/shard_map/ppermute | solution.py:28
  42.4 6.9 %terms.8 = (bf16[64,3584]{1,0:T(8,128)(2,1)S(1)}, bf16[64,3584]{1,0:T(8,128)(2,1)S(1)}, bf16[128,3584]{1,0:T(8,128)(2,1)S(1)}) custom-call(s32[1]{0:T(128)} %bitcast.place_ref, bf16[256,512]{1,0:T(8,128)(2,1)S(1)} %pad_maximum_fusion.1.refs_0_, bf16[256,512]{1,0:T(8,128)(2,1)S(1)} %collective-permute-done.4.refs_1_, ...), custom_call_target="tpu_custom_call" | custom-call | flops 469762048 | bytes 1000 | tf_op jit(solution)/shard_map/terms/pallas_call | solution.py:135
  49.3 0.7 collective-permute-done.10.refs_1_
  50.1 0.5 collective-permute-start.11
  50.6 1.3 collective-permute-done.12.refs_1_
  51.9 0.7 collective-permute-done.11.refs_0_
  52.5 0.5 pair.4
  53.1 2.5 %collective-permute-start.14 = (bf16[256,512]{1,0:T(8,128)(2,1)S(1)}, bf16[256,512]{1,0:T(8,128)(2,1)S(1)}, u32[]{:S(2)}, u32[]{:S(2)}) collective-permute-start(bf16[256,512]{1,0:T(8,128)(2,1)S(1)} %pad_maximum_fusion.refs_0_), channel_id=1, source_target_pairs={{0,12},{4,8},{8,4},{12,0},{1,13},{5,9},{9,5},{13,1},{2,14},{6,10},... | collective-permute-start | bytes 786440 | tf_op jit(solution)/shard_map/ppermute | solution.py:28
  55.9 1.8 collective-permute-start.17
  57.7 6.9 %terms.9 = (bf16[64,3584]{1,0:T(8,128)(2,1)S(1)}, bf16[64,3584]{1,0:T(8,128)(2,1)S(1)}, bf16[128,3584]{1,0:T(8,128)(2,1)S(1)}) custom-call(s32[1]{0:T(128)} %bitcast.place_ref, bf16[256,512]{1,0:T(8,128)(2,1)S(1)} %pad_maximum_fusion.1.refs_0_, bf16[256,512]{1,0:T(8,128)(2,1)S(1)} %collective-permute-done.4.refs_1_, ...), custom_call_target="tpu_custom_call" | custom-call | flops 469762048 | bytes 1000 | tf_op jit(solution)/shard_map/terms/pallas_call | solution.py:135
  64.6 14.4 %collective-permute-done.13.refs_2_ = bf16[256,512]{1,0:T(8,128)(2,1)S(1)} collective-permute-done((bf16[256,512]{1,0:T(8,128)(2,1)S(1)}, bf16[256,512]{1,0:T(8,128)(2,1)S(1)}, u32[]{:S(2)}, u32[]{:S(2)}) %collective-permute-start.13) | collective-permute-done | bytes 262176 | tf_op jit(solution)/shard_map/ppermute | solution.py:28
  79.1 0.5 collective-permute-start.15
  79.6 1.3 collective-permute-done.16.refs_1_
  80.9 0.7 collective-permute-done.15.refs_0_
  81.5 1.7 pair.5
  83.3 1.9 %collective-permute-start.23 = (bf16[128,3584]{1,0:T(8,128)(2,1)}, bf16[128,3584]{1,0:T(8,128)(2,1)}, u32[]{:S(2)}, u32[]{:S(2)}) collective-permute-start(bf16[128,3584]{1,0:T(8,128)(2,1)} %pair.5), channel_id=1, source_target_pairs={{0,2},{1,3},{2,0},{3,1},{4,6},{5,7},{6,4},{7,5},{8,10},{9,11},{10,... | collective-permute-start | bytes 2752520 | tf_op jit(solution)/shard_map/ppermute | solution.py:18
  85.1 1.9 %collective-permute-start.18 = (bf16[256,512]{1,0:T(8,128)(2,1)S(1)}, bf16[256,512]{1,0:T(8,128)(2,1)S(1)}, u32[]{:S(2)}, u32[]{:S(2)}) collective-permute-start(bf16[256,512]{1,0:T(8,128)(2,1)S(1)} %collective-permute-done.7.refs_0_), channel_id=1, source_target_pairs={{0,4},{4,0},{8,12},{12,8},{1,5},{5,1},{9,13},{13,9},{2,6},{6,2},{1... | collective-permute-start | bytes 786440 | tf_op jit(solution)/shard_map/ppermute | solution.py:28
  87.0 7.8 %terms.10 = (bf16[64,3584]{1,0:T(8,128)(2,1)}, bf16[64,3584]{1,0:T(8,128)(2,1)}, bf16[128,3584]{1,0:T(8,128)(2,1)S(1)}) custom-call(s32[1]{0:T(128)} %bitcast.place_ref, bf16[256,512]{1,0:T(8,128)(2,1)S(1)} %pad_maximum_fusion.refs_0_, bf16[256,512]{1,0:T(8,128)(2,1)S(1)} %collective-permute-done.10.refs_1_, ...), custom_call_target="tpu_custom_call" | custom-call | flops 469762048 | bytes 1000 | tf_op jit(solution)/shard_map/terms/pallas_call | solution.py:135
  94.9 0.9 copy-done.6
  95.8 2.8 %collective-permute-done.19.refs_2_ = bf16[256,512]{1,0:T(8,128)(2,1)S(1)} collective-permute-done((bf16[256,512]{1,0:T(8,128)(2,1)S(1)}, bf16[256,512]{1,0:T(8,128)(2,1)S(1)}, u32[]{:S(2)}, u32[]{:S(2)}) %collective-permute-start.19) | collective-permute-done | bytes 262176 | tf_op jit(solution)/shard_map/ppermute | solution.py:28
  98.8 0.5 collective-permute-start.20
  99.6 1.2 collective-permute-done.21.refs_1_
  100.8 0.7 collective-permute-done.20.refs_0_
  101.5 1.2 copy-done.7
  102.7 1.7 pair.6
  105.1 0.7 collective-permute-start.24
  105.8 1.3 collective-permute-start.25
  107.1 0.9 add.30
  108.6 7.5 %terms.11 = (bf16[64,3584]{1,0:T(8,128)(2,1)}, bf16[64,3584]{1,0:T(8,128)(2,1)S(1)}, bf16[128,3584]{1,0:T(8,128)(2,1)S(1)}) custom-call(s32[1]{0:T(128)} %bitcast.place_ref, bf16[256,512]{1,0:T(8,128)(2,1)S(1)} %pad_maximum_fusion.refs_0_, bf16[256,512]{1,0:T(8,128)(2,1)S(1)} %collective-permute-done.10.refs_1_, ...), custom_call_target="tpu_custom_call" | custom-call | flops 469762048 | bytes 1000 | tf_op jit(solution)/shard_map/terms/pallas_call | solution.py:135
  116.2 0.9 copy-done.2
  117.1 1.4 collective-permute-done.25.refs_4_
  119.1 1.3 collective-permute-start.31
  121.2 1.2 copy-done.3
  122.4 0.5 pair.7
  122.9 1.7 collective-permute-start.33
  124.6 2.3 %collective-permute-done.31 = bf16[4,4224]{1,0:T(4,128)(2,1)S(1)} collective-permute-done((bf16[4,4224]{1,0:T(4,128)(2,1)S(1)}, bf16[4,4224]{1,0:T(4,128)(2,1)S(1)}, u32[]{:S(2)}, u32[]{:S(2)}) %collective-permute-start.31) | collective-permute-done | bytes 33824 | tf_op jit(solution)/shard_map/ppermute | solution.py:18
  126.9 0.8 collective-permute-start.28
  127.7 1.5 collective-permute-done.30
  129.6 0.9 fusion.6
  130.4 2.7 %fusion.4 = f32[1024,1024]{1,0:T(8,128)} fusion(bf16[16,4224]{1,0:T(8,128)(2,1)S(1)} %pad_maximum_fusion.2, s32[]{:T(128)S(6)} %select_n.121, s32[]{:T(128)S(6)} %select_n.122), kind=kOutput, calls=%fused_computation.20 | convolution fusion | flops 33554432 | bytes 4259848 | tf_op jit(solution)/shard_map/dot_general | solution.py:266
  133.2 6.9 %terms.12 = (bf16[64,3584]{1,0:T(8,128)(2,1)S(1)}, bf16[64,3584]{1,0:T(8,128)(2,1)S(1)}, bf16[64,3584]{1,0:T(8,128)(2,1)S(1)}, bf16[64,3584]{1,0:T(8,128)(2,1)S(1)}) custom-call(s32[1]{0:T(128)} %bitcast.place_ref, bf16[256,512]{1,0:T(8,128)(2,1)S(1)} %collective-permute-done.7.refs_0_, bf16[256,512]{1,0:T(8,128)(2,1)S(1)} %collective-permute-done.18.refs_1_, ...), custom_call_target="tpu_custom_call" | custom-call | flops 469762048 | bytes 1000 | tf_op jit(solution)/shard_map/terms/pallas_call | solution.py:135
  140.1 2.2 %collective-permute-done.28.refs_2_ = bf16[256,512]{1,0:T(8,128)(2,1)S(1)} collective-permute-done((bf16[256,512]{1,0:T(8,128)(2,1)S(1)}, bf16[256,512]{1,0:T(8,128)(2,1)S(1)}, u32[]{:S(2)}, u32[]{:S(2)}) %collective-permute-start.28) | collective-permute-done | bytes 262176 | tf_op jit(solution)/shard_map/ppermute | solution.py:28
  142.5 0.8 collective-permute-start.37
  144.2 0.7 collective-permute-start.35
  144.8 6.9 %terms.13 = (bf16[64,3584]{1,0:T(8,128)(2,1)S(1)}, bf16[64,3584]{1,0:T(8,128)(2,1)S(1)}, bf16[64,3584]{1,0:T(8,128)(2,1)S(1)}, bf16[64,3584]{1,0:T(8,128)(2,1)S(1)}) custom-call(s32[1]{0:T(128)} %bitcast.place_ref, bf16[256,512]{1,0:T(8,128)(2,1)S(1)} %collective-permute-done.7.refs_0_, bf16[256,512]{1,0:T(8,128)(2,1)S(1)} %collective-permute-done.18.refs_1_, ...), custom_call_target="tpu_custom_call" | custom-call | flops 469762048 | bytes 1000 | tf_op jit(solution)/shard_map/terms/pallas_call | solution.py:135
  151.8 3.5 %collective-permute-done.37.refs_8_ = bf16[64,3584]{1,0:T(8,128)(2,1)S(1)} collective-permute-done((bf16[64,3584]{1,0:T(8,128)(2,1)S(1)}, bf16[64,3584]{1,0:T(8,128)(2,1)S(1)}, u32[]{:S(2)}, u32[]{:S(2)}) %collective-permute-start.37) | collective-permute-done | bytes 458784 | tf_op jit(solution)/shard_map/ppermute | solution.py:18
  155.3 0.5 collective-permute-start.40
  156.3 1.3 collective-permute-start.36
  157.6 1.7 sums.3.refs_6_
  159.3 7.2 %collective-permute-done.36.refs_4_ = bf16[256,512]{1,0:T(8,128)(2,1)S(1)} collective-permute-done((bf16[256,512]{1,0:T(8,128)(2,1)S(1)}, bf16[256,512]{1,0:T(8,128)(2,1)S(1)}, u32[]{:S(2)}, u32[]{:S(2)}) %collective-permute-start.36) | collective-permute-done | bytes 262176 | tf_op jit(solution)/shard_map/ppermute | solution.py:28
  166.5 7.7 %terms.14.refs_9_ = bf16[256,7168]{1,0:T(8,128)(2,1)} custom-call(s32[1]{0:T(128)} %bitcast.place_ref, bf16[256,512]{1,0:T(8,128)(2,1)S(1)} %bitcast.41, bf16[256,512]{1,0:T(8,128)(2,1)S(1)} %collective-permute-done.22.refs_1_, bf16[256,512]{1,0:T(8,128)(2,1)S(1)} %collective-permute-done.28.refs_2_, bf16[256,512]{1,0:T(8,128)(2,1)S(1)} %collective-permute-done.35.refs_3_, ...), custom_call_target="tpu_custom_call" | custom-call | flops 469762048 | bytes 1000 | tf_op jit(solution)/shard_map/terms/pallas_call | solution.py:135
  174.2 1.5 sums.2.refs_6_
  175.7 8.0 %terms.15 = bf16[256,7168]{1,0:T(8,128)(2,1)} custom-call(s32[1]{0:T(128)} %bitcast.place_ref, bf16[256,512]{1,0:T(8,128)(2,1)S(1)} %bitcast.42, bf16[256,512]{1,0:T(8,128)(2,1)S(1)} %collective-permute-done.22.refs_1_, bf16[256,512]{1,0:T(8,128)(2,1)S(1)} %collective-permute-done.28.refs_2_, ...), custom_call_target="tpu_custom_call", output_to_operand_aliasing={{}: (10, {})} | custom-call | flops 469762048 | bytes 1000 | tf_op jit(solution)/shard_map/terms/pallas_call | solution.py:135
  (101 shorter events, 7.3 us)
Async XLA Ops:
  0.6 6.1 %copy-start = (bf16[7168,64]{0,1:T(8,128)(2,1)S(1)}, bf16[7168,64]{0,1:T(8,128)(2,1)}, u32[]{:S(2)}) copy-start(bf16[7168,64]{0,1:T(8,128)(2,1)} %param.10) | copy-start | bytes 2752516
  2.7 7.3 %copy-start.8 = (bf16[1,4,512,256]{3,2,1,0:T(8,128)(2,1)S(1)}, bf16[1,4,512,256]{3,2,1,0:T(8,128)(2,1)}, u32[]{:S(2)}) copy-start(bf16[1,4,512,256]{3,2,1,0:T(8,128)(2,1)} %param.8) | copy-start | bytes 3145732
  2.7 7.3 %copy-start.12 = (bf16[1,4,512,64]{2,3,1,0:T(8,128)(2,1)S(1)}, bf16[1,4,512,64]{2,3,1,0:T(8,128)(2,1)}, u32[]{:S(2)}) copy-start(bf16[1,4,512,64]{2,3,1,0:T(8,128)(2,1)} %param.11) | copy-start | bytes 786436
  3.5 7.2 %collective-permute-start.3 = (bf16[128,512]{1,0:T(8,128)(2,1)}, bf16[128,512]{1,0:T(8,128)(2,1)S(1)}, u32[]{:S(2)}, u32[]{:S(2)}) collective-permute-start(bf16[128,512]{1,0:T(8,128)(2,1)} %get-tuple-element.129), channel_id=1, source_target_pairs={{0,2},{1,3},{2,0},{3,1},{4,6},{5,7},{6,4},{7,5},{8,10},{9,11},{10,... | collective-permute-start | bytes 393224 | tf_op jit(solution)/shard_map/ppermute | solution.py:18
  6.7 5.9 %collective-permute-start.2 = (bf16[128,512]{1,0:T(8,128)(2,1)S(1)}, bf16[128,512]{1,0:T(8,128)(2,1)S(1)}, u32[]{:S(2)}, u32[]{:S(2)}) collective-permute-start(bf16[128,512]{1,0:T(8,128)(2,1)S(1)} %get-tuple-element.127), channel_id=1, source_target_pairs={{0,3},{1,2},{2,1},{3,0},{4,7},{5,6},{6,5},{7,4},{8,11},{9,10},{10,... | collective-permute-start | bytes 393224 | tf_op jit(solution)/shard_map/ppermute | solution.py:18
  12.6 12.6 %collective-permute-start.6 = (bf16[256,512]{1,0:T(8,128)(2,1)S(1)}, bf16[256,512]{1,0:T(8,128)(2,1)S(1)}, u32[]{:S(2)}, u32[]{:S(2)}) collective-permute-start(bf16[256,512]{1,0:T(8,128)(2,1)S(1)} %pad_maximum_fusion.1.refs_0_), channel_id=1, source_target_pairs={{0,12},{4,8},{8,4},{12,0},{1,13},{5,9},{9,5},{13,1},{2,14},{6,10},... | collective-permute-start | bytes 786440 | tf_op jit(solution)/shard_map/ppermute | solution.py:28
  16.2 23.0 %collective-permute-start.5 = (bf16[256,512]{1,0:T(8,128)(2,1)S(1)}, bf16[256,512]{1,0:T(8,128)(2,1)S(1)}, u32[]{:S(2)}, u32[]{:S(2)}) collective-permute-start(bf16[256,512]{1,0:T(8,128)(2,1)S(1)} %pad_maximum_fusion.1.refs_0_), channel_id=1, source_target_pairs={{0,8},{4,12},{8,0},{12,4},{1,9},{5,13},{9,1},{13,5},{2,10},{6,14},... | collective-permute-start | bytes 786440 | tf_op jit(solution)/shard_map/ppermute | solution.py:28
  16.2 23.0 %collective-permute-start.4 = (bf16[256,512]{1,0:T(8,128)(2,1)S(1)}, bf16[256,512]{1,0:T(8,128)(2,1)S(1)}, u32[]{:S(2)}, u32[]{:S(2)}) collective-permute-start(bf16[256,512]{1,0:T(8,128)(2,1)S(1)} %pad_maximum_fusion.1.refs_0_), channel_id=1, source_target_pairs={{0,4},{4,0},{8,12},{12,8},{1,5},{5,1},{9,13},{13,9},{2,6},{6,2},{1... | collective-permute-start | bytes 786440 | tf_op jit(solution)/shard_map/ppermute | solution.py:28
  17.1 6.4 %collective-permute-start.1 = (bf16[128,512]{1,0:T(8,128)(2,1)S(1)}, bf16[128,512]{1,0:T(8,128)(2,1)S(1)}, u32[]{:S(2)}, u32[]{:S(2)}) collective-permute-start(bf16[128,512]{1,0:T(8,128)(2,1)S(1)} %get-tuple-element.130), channel_id=1, source_target_pairs={{0,2},{1,3},{2,0},{3,1},{4,6},{5,7},{6,4},{7,5},{8,10},{9,11},{10,... | collective-permute-start | bytes 393224 | tf_op jit(solution)/shard_map/ppermute | solution.py:18
  18.1 6.7 %collective-permute-start = (bf16[128,512]{1,0:T(8,128)(2,1)S(1)}, bf16[128,512]{1,0:T(8,128)(2,1)S(1)}, u32[]{:S(2)}, u32[]{:S(2)}) collective-permute-start(bf16[128,512]{1,0:T(8,128)(2,1)S(1)} %get-tuple-element.128), channel_id=1, source_target_pairs={{0,3},{1,2},{2,1},{3,0},{4,7},{5,6},{6,5},{7,4},{8,11},{9,10},{10,... | collective-permute-start | bytes 393224 | tf_op jit(solution)/shard_map/ppermute | solution.py:18
  23.4 15.8 %collective-permute-start.8 = (f32[256,128]{0,1:T(8,128)S(1)}, f32[256,128]{0,1:T(8,128)S(1)}, u32[]{:S(2)}, u32[]{:S(2)}) collective-permute-start(f32[256,128]{0,1:T(8,128)S(1)} %pad_maximum_fusion.3), channel_id=1, source_target_pairs={{0,4},{4,0},{8,12},{12,8},{1,5},{5,1},{9,13},{13,9},{2,6},{6,2},{1... | collective-permute-start | bytes 393224 | tf_op jit(solution)/shard_map/ppermute | solution.py:28
  24.7 17.6 %collective-permute-start.7 = (bf16[256,512]{1,0:T(8,128)(2,1)S(1)}, bf16[256,512]{1,0:T(8,128)(2,1)S(1)}, u32[]{:S(2)}, u32[]{:S(2)}) collective-permute-start(bf16[256,512]{1,0:T(8,128)(2,1)S(1)} %bitcast.46), channel_id=1, source_target_pairs={{0,1},{1,0},{2,3},{3,2},{4,5},{5,4},{6,7},{7,6},{8,9},{9,8},{10,11... | collective-permute-start | bytes 786440 | tf_op jit(solution)/shard_map/ppermute | solution.py:18
  39.2 10.8 %collective-permute-start.10 = (bf16[256,512]{1,0:T(8,128)(2,1)S(1)}, bf16[256,512]{1,0:T(8,128)(2,1)S(1)}, u32[]{:S(2)}, u32[]{:S(2)}) collective-permute-start(bf16[256,512]{1,0:T(8,128)(2,1)S(1)} %pad_maximum_fusion.refs_0_), channel_id=1, source_target_pairs={{0,4},{4,0},{8,12},{12,8},{1,5},{5,1},{9,13},{13,9},{2,6},{6,2},{1... | collective-permute-start | bytes 786440 | tf_op jit(solution)/shard_map/ppermute | solution.py:28
  39.3 10.0 %copy-start.10 = (f32[256,128]{0,1:T(8,128)}, f32[256,128]{0,1:T(8,128)S(1)}, u32[]{:S(2)}) copy-start(f32[256,128]{0,1:T(8,128)S(1)} %fusion.14) | copy-start | bytes 393220
  39.3 10.0 %collective-permute-start.9 = (f32[256,128]{0,1:T(8,128)S(1)}, f32[256,128]{0,1:T(8,128)S(1)}, u32[]{:S(2)}, u32[]{:S(2)}) collective-permute-start(f32[256,128]{0,1:T(8,128)S(1)} %fusion.14), channel_id=1, source_target_pairs={{0,8},{4,12},{8,0},{12,4},{1,9},{5,13},{9,1},{13,5},{2,10},{6,14},... | collective-permute-start | bytes 393224 | tf_op jit(solution)/shard_map/ppermute | solution.py:28
  49.3 15.3 %copy-start.13 = (f32[256,128]{0,1:T(8,128)}, f32[256,128]{0,1:T(8,128)S(1)}, u32[]{:S(2)}) copy-start(f32[256,128]{0,1:T(8,128)S(1)} %collective-permute-done.9) | copy-start | bytes 393220
  50.0 1.8 collective-permute-start.12
  50.1 2.5 %collective-permute-start.11 = (bf16[64,3584]{1,0:T(8,128)(2,1)S(1)}, bf16[64,3584]{1,0:T(8,128)(2,1)S(1)}, u32[]{:S(2)}, u32[]{:S(2)}) collective-permute-start(bf16[64,3584]{1,0:T(8,128)(2,1)S(1)} %get-tuple-element.69), channel_id=1, source_target_pairs={{0,1},{1,0},{2,3},{3,2},{4,5},{5,4},{6,7},{7,6},{8,9},{9,8},{10,11... | collective-permute-start | bytes 1376264 | tf_op jit(solution)/shard_map/ppermute | solution.py:18
  53.1 11.6 %collective-permute-start.14 = (bf16[256,512]{1,0:T(8,128)(2,1)S(1)}, bf16[256,512]{1,0:T(8,128)(2,1)S(1)}, u32[]{:S(2)}, u32[]{:S(2)}) collective-permute-start(bf16[256,512]{1,0:T(8,128)(2,1)S(1)} %pad_maximum_fusion.refs_0_), channel_id=1, source_target_pairs={{0,12},{4,8},{8,4},{12,0},{1,13},{5,9},{9,5},{13,1},{2,14},{6,10},... | collective-permute-start | bytes 786440 | tf_op jit(solution)/shard_map/ppermute | solution.py:28
  55.6 23.5 %collective-permute-start.13 = (bf16[256,512]{1,0:T(8,128)(2,1)S(1)}, bf16[256,512]{1,0:T(8,128)(2,1)S(1)}, u32[]{:S(2)}, u32[]{:S(2)}) collective-permute-start(bf16[256,512]{1,0:T(8,128)(2,1)S(1)} %pad_maximum_fusion.refs_0_), channel_id=1, source_target_pairs={{0,8},{4,12},{8,0},{12,4},{1,9},{5,13},{9,1},{13,5},{2,10},{6,14},... | collective-permute-start | bytes 786440 | tf_op jit(solution)/shard_map/ppermute | solution.py:28
  55.9 31.2 %collective-permute-start.17 = (bf16[128,3584]{1,0:T(8,128)(2,1)S(1)}, bf16[128,3584]{1,0:T(8,128)(2,1)S(1)}, u32[]{:S(2)}, u32[]{:S(2)}) collective-permute-start(bf16[128,3584]{1,0:T(8,128)(2,1)S(1)} %pair.4), channel_id=1, source_target_pairs={{0,2},{1,3},{2,0},{3,1},{4,6},{5,7},{6,4},{7,5},{8,10},{9,11},{10,... | collective-permute-start | bytes 2752520 | tf_op jit(solution)/shard_map/ppermute | solution.py:18
  79.1 1.8 collective-permute-start.16
  79.1 2.5 %collective-permute-start.15 = (bf16[64,3584]{1,0:T(8,128)(2,1)S(1)}, bf16[64,3584]{1,0:T(8,128)(2,1)S(1)}, u32[]{:S(2)}, u32[]{:S(2)}) collective-permute-start(bf16[64,3584]{1,0:T(8,128)(2,1)S(1)} %get-tuple-element.76), channel_id=1, source_target_pairs={{0,1},{1,0},{2,3},{3,2},{4,5},{5,4},{6,7},{7,6},{8,9},{9,8},{10,11... | collective-permute-start | bytes 1376264 | tf_op jit(solution)/shard_map/ppermute | solution.py:18
  83.2 16.1 %copy-start.15 = (s32[4]{0:T(128)S(1)}, s32[4]{0:T(128)}, u32[]{:S(2)}) copy-start(s32[4]{0:T(128)} %param.13) | copy-start | bytes 52
  83.2 16.1 %copy-start.9 = (bf16[1,1,512,256]{3,2,1,0:T(8,128)(2,1)S(1)}, bf16[1,1,512,256]{3,2,1,0:T(8,128)(2,1)}, u32[]{:S(2)}) copy-start(bf16[1,1,512,256]{3,2,1,0:T(8,128)(2,1)} %get-tuple-element.126) | copy-start | bytes 786436
  83.3 16.2 %copy-start.14 = (s32[1,256]{1,0:T(1,128)S(1)}, s32[1,256]{1,0:T(1,128)}, u32[]{:S(2)}) copy-start(s32[1,256]{1,0:T(1,128)} %param.12) | copy-start | bytes 3076
  83.3 23.8 %copy-start.11 = (f32[256,128]{0,1:T(8,128)S(1)}, f32[256,128]{0,1:T(8,128)}, u32[]{:S(2)}) copy-start(f32[256,128]{0,1:T(8,128)} %copy-done.10) | copy-start | bytes 393220
  83.3 23.8 %collective-permute-start.23 = (bf16[128,3584]{1,0:T(8,128)(2,1)}, bf16[128,3584]{1,0:T(8,128)(2,1)}, u32[]{:S(2)}, u32[]{:S(2)}) collective-permute-start(bf16[128,3584]{1,0:T(8,128)(2,1)} %pair.5), channel_id=1, source_target_pairs={{0,2},{1,3},{2,0},{3,1},{4,6},{5,7},{6,4},{7,5},{8,10},{9,11},{10,... | collective-permute-start | bytes 2752520 | tf_op jit(solution)/shard_map/ppermute | solution.py:18
  85.1 13.4 %collective-permute-start.19 = (bf16[256,512]{1,0:T(8,128)(2,1)S(1)}, bf16[256,512]{1,0:T(8,128)(2,1)S(1)}, u32[]{:S(2)}, u32[]{:S(2)}) collective-permute-start(bf16[256,512]{1,0:T(8,128)(2,1)S(1)} %collective-permute-done.7.refs_0_), channel_id=1, source_target_pairs={{0,8},{4,12},{8,0},{12,4},{1,9},{5,13},{9,1},{13,5},{2,10},{6,14},... | collective-permute-start | bytes 786440 | tf_op jit(solution)/shard_map/ppermute | solution.py:28
  85.1 13.7 %collective-permute-start.18 = (bf16[256,512]{1,0:T(8,128)(2,1)S(1)}, bf16[256,512]{1,0:T(8,128)(2,1)S(1)}, u32[]{:S(2)}, u32[]{:S(2)}) collective-permute-start(bf16[256,512]{1,0:T(8,128)(2,1)S(1)} %collective-permute-done.7.refs_0_), channel_id=1, source_target_pairs={{0,4},{4,0},{8,12},{12,8},{1,5},{5,1},{9,13},{13,9},{2,6},{6,2},{1... | collective-permute-start | bytes 786440 | tf_op jit(solution)/shard_map/ppermute | solution.py:28
  87.0 7.8 %copy-start.4 = (bf16[128,3584]{1,0:T(8,128)(2,1)}, bf16[128,3584]{1,0:T(8,128)(2,1)S(1)}, u32[]{:S(2)}) copy-start(bf16[128,3584]{1,0:T(8,128)(2,1)S(1)} %collective-permute-done.17.refs_4_) | copy-start | bytes 2752516
  94.8 0.9 copy-start.6
  98.8 2.0 %collective-permute-start.21 = (bf16[64,3584]{1,0:T(8,128)(2,1)}, bf16[64,3584]{1,0:T(8,128)(2,1)S(1)}, u32[]{:S(2)}, u32[]{:S(2)}) collective-permute-start(bf16[64,3584]{1,0:T(8,128)(2,1)} %get-tuple-element.85), channel_id=1, source_target_pairs={{0,1},{1,0},{2,3},{3,2},{4,5},{5,4},{6,7},{7,6},{8,9},{9,8},{10,11... | collective-permute-start | bytes 1376264 | tf_op jit(solution)/shard_map/ppermute | solution.py:18
  98.8 2.7 %collective-permute-start.20 = (bf16[64,3584]{1,0:T(8,128)(2,1)}, bf16[64,3584]{1,0:T(8,128)(2,1)S(1)}, u32[]{:S(2)}, u32[]{:S(2)}) collective-permute-start(bf16[64,3584]{1,0:T(8,128)(2,1)} %get-tuple-element.83), channel_id=1, source_target_pairs={{0,1},{1,0},{2,3},{3,2},{4,5},{5,4},{6,7},{7,6},{8,9},{9,8},{10,11... | collective-permute-start | bytes 1376264 | tf_op jit(solution)/shard_map/ppermute | solution.py:18
  101.5 1.2 copy-start.7
  104.4 24.9 %collective-permute-start.32 = (bf16[128,3584]{1,0:T(8,128)(2,1)}, bf16[128,3584]{1,0:T(8,128)(2,1)}, u32[]{:S(2)}, u32[]{:S(2)}) collective-permute-start(bf16[128,3584]{1,0:T(8,128)(2,1)} %pair.6), channel_id=1, source_target_pairs={{0,2},{1,3},{2,0},{3,1},{4,6},{5,7},{6,4},{7,5},{8,10},{9,11},{10,... | collective-permute-start | bytes 2752520 | tf_op jit(solution)/shard_map/ppermute | solution.py:18
  104.8 12.2 %collective-permute-start.22 = (bf16[256,512]{1,0:T(8,128)(2,1)S(1)}, bf16[256,512]{1,0:T(8,128)(2,1)S(1)}, u32[]{:S(2)}, u32[]{:S(2)}) collective-permute-start(bf16[256,512]{1,0:T(8,128)(2,1)S(1)} %bitcast.38), channel_id=1, source_target_pairs={{0,4},{4,0},{8,12},{12,8},{1,5},{5,1},{9,13},{13,9},{2,6},{6,2},{1... | collective-permute-start | bytes 786440 | tf_op jit(solution)/shard_map/ppermute | solution.py:28
  105.1 12.0 %collective-permute-start.24 = (bf16[256,512]{1,0:T(8,128)(2,1)S(1)}, bf16[256,512]{1,0:T(8,128)(2,1)S(1)}, u32[]{:S(2)}, u32[]{:S(2)}) collective-permute-start(bf16[256,512]{1,0:T(8,128)(2,1)S(1)} %collective-permute-done.7.refs_0_), channel_id=1, source_target_pairs={{4,8},{8,4},{5,9},{9,5},{6,10},{10,6},{7,11},{11,7},{20,24},{24,20... | collective-permute-start | bytes 786440 | tf_op jit(solution)/shard_map/ppermute | solution.py:28
  105.8 12.8 %collective-permute-start.25 = (bf16[256,512]{1,0:T(8,128)(2,1)S(1)}, bf16[256,512]{1,0:T(8,128)(2,1)S(1)}, u32[]{:S(2)}, u32[]{:S(2)}) collective-permute-start(bf16[256,512]{1,0:T(8,128)(2,1)S(1)} %collective-permute-done.19.refs_2_), channel_id=1, source_target_pairs={{4,0},{8,12},{5,1},{9,13},{6,2},{10,14},{7,3},{11,15},{20,16},{24,... | collective-permute-start | bytes 786440 | tf_op jit(solution)/shard_map/ppermute | solution.py:28
  116.1 0.9 copy-start.2
  118.5 2.4 %collective-permute-start.27 = (bf16[64,3584]{1,0:T(8,128)(2,1)S(1)}, bf16[64,3584]{1,0:T(8,128)(2,1)S(1)}, u32[]{:S(2)}, u32[]{:S(2)}) collective-permute-start(bf16[64,3584]{1,0:T(8,128)(2,1)S(1)} %get-tuple-element.95), channel_id=1, source_target_pairs={{0,1},{1,0},{2,3},{3,2},{4,5},{5,4},{6,7},{7,6},{8,9},{9,8},{10,11... | collective-permute-start | bytes 1376264 | tf_op jit(solution)/shard_map/ppermute | solution.py:18
  118.5 2.7 %collective-permute-start.26 = (bf16[64,3584]{1,0:T(8,128)(2,1)}, bf16[64,3584]{1,0:T(8,128)(2,1)S(1)}, u32[]{:S(2)}, u32[]{:S(2)}) collective-permute-start(bf16[64,3584]{1,0:T(8,128)(2,1)} %get-tuple-element.93), channel_id=1, source_target_pairs={{0,1},{1,0},{2,3},{3,2},{4,5},{5,4},{6,7},{7,6},{8,9},{9,8},{10,11... | collective-permute-start | bytes 1376264 | tf_op jit(solution)/shard_map/ppermute | solution.py:18
  119.1 7.8 %collective-permute-start.31 = (bf16[4,4224]{1,0:T(4,128)(2,1)S(1)}, bf16[4,4224]{1,0:T(4,128)(2,1)S(1)}, u32[]{:S(2)}, u32[]{:S(2)}) collective-permute-start(bf16[4,4224]{1,0:T(4,128)(2,1)S(1)} %pad_maximum_fusion.4), channel_id=1, source_target_pairs={{0,3},{1,2},{2,1},{3,0},{4,7},{5,6},{6,5},{7,4},{8,11},{9,10},{10,... | collective-permute-start | bytes 101384 | tf_op jit(solution)/shard_map/ppermute | solution.py:18
  120.4 8.9 %collective-permute-start.30 = (bf16[4,4224]{1,0:T(4,128)(2,1)S(1)}, bf16[4,4224]{1,0:T(4,128)(2,1)S(1)}, u32[]{:S(2)}, u32[]{:S(2)}) collective-permute-start(bf16[4,4224]{1,0:T(4,128)(2,1)S(1)} %pad_maximum_fusion.4), channel_id=1, source_target_pairs={{0,2},{1,3},{2,0},{3,1},{4,6},{5,7},{6,4},{7,5},{8,10},{9,11},{10,... | collective-permute-start | bytes 101384 | tf_op jit(solution)/shard_map/ppermute | solution.py:18
  120.9 8.3 %collective-permute-start.29 = (bf16[4,4224]{1,0:T(4,128)(2,1)S(1)}, bf16[4,4224]{1,0:T(4,128)(2,1)S(1)}, u32[]{:S(2)}, u32[]{:S(2)}) collective-permute-start(bf16[4,4224]{1,0:T(4,128)(2,1)S(1)} %pad_maximum_fusion.4), channel_id=1, source_target_pairs={{0,1},{1,0},{2,3},{3,2},{4,5},{5,4},{6,7},{7,6},{8,9},{9,8},{10,11... | collective-permute-start | bytes 101384 | tf_op jit(solution)/shard_map/ppermute | solution.py:18
  121.2 1.2 copy-start.3
  122.9 19.4 %collective-permute-start.33 = (bf16[64,3584]{1,0:T(8,128)(2,1)S(1)}, bf16[64,3584]{1,0:T(8,128)(2,1)S(1)}, u32[]{:S(2)}, u32[]{:S(2)}) collective-permute-start(bf16[64,3584]{1,0:T(8,128)(2,1)S(1)} %get-tuple-element.96), channel_id=1, source_target_pairs={{0,2},{1,3},{2,0},{3,1},{4,6},{5,7},{6,4},{7,5},{8,10},{9,11},{10,... | collective-permute-start | bytes 1376264 | tf_op jit(solution)/shard_map/ppermute | solution.py:18
  126.9 15.4 %collective-permute-start.28 = (bf16[256,512]{1,0:T(8,128)(2,1)S(1)}, bf16[256,512]{1,0:T(8,128)(2,1)S(1)}, u32[]{:S(2)}, u32[]{:S(2)}) collective-permute-start(bf16[256,512]{1,0:T(8,128)(2,1)S(1)} %bitcast.39), channel_id=1, source_target_pairs={{0,8},{4,12},{8,0},{12,4},{1,9},{5,13},{9,1},{13,5},{2,10},{6,14},... | collective-permute-start | bytes 786440 | tf_op jit(solution)/shard_map/ppermute | solution.py:28
  142.3 1.8 collective-permute-start.34
  142.5 12.8 %collective-permute-start.37 = (bf16[64,3584]{1,0:T(8,128)(2,1)S(1)}, bf16[64,3584]{1,0:T(8,128)(2,1)S(1)}, u32[]{:S(2)}, u32[]{:S(2)}) collective-permute-start(bf16[64,3584]{1,0:T(8,128)(2,1)S(1)} %get-tuple-element.109), channel_id=1, source_target_pairs={{0,2},{1,3},{2,0},{3,1},{4,6},{5,7},{6,4},{7,5},{8,10},{9,11},{10,... | collective-permute-start | bytes 1376264 | tf_op jit(solution)/shard_map/ppermute | solution.py:18
  143.2 12.1 %collective-permute-start.44 = (bf16[64,3584]{1,0:T(8,128)(2,1)S(1)}, bf16[64,3584]{1,0:T(8,128)(2,1)S(1)}, u32[]{:S(2)}, u32[]{:S(2)}) collective-permute-start(bf16[64,3584]{1,0:T(8,128)(2,1)S(1)} %get-tuple-element.122), channel_id=1, source_target_pairs={{0,1},{1,0},{2,3},{3,2},{4,5},{5,4},{6,7},{7,6},{8,9},{9,8},{10,11... | collective-permute-start | bytes 1376264 | tf_op jit(solution)/shard_map/ppermute | solution.py:18
  143.4 12.4 %collective-permute-start.43 = (bf16[64,3584]{1,0:T(8,128)(2,1)S(1)}, bf16[64,3584]{1,0:T(8,128)(2,1)S(1)}, u32[]{:S(2)}, u32[]{:S(2)}) collective-permute-start(bf16[64,3584]{1,0:T(8,128)(2,1)S(1)} %get-tuple-element.120), channel_id=1, source_target_pairs={{0,1},{1,0},{2,3},{3,2},{4,5},{5,4},{6,7},{7,6},{8,9},{9,8},{10,11... | collective-permute-start | bytes 1376264 | tf_op jit(solution)/shard_map/ppermute | solution.py:18
  143.7 13.9 %copy-start.5 = (bf16[128,3584]{1,0:T(8,128)(2,1)S(1)}, bf16[128,3584]{1,0:T(8,128)(2,1)}, u32[]{:S(2)}) copy-start(bf16[128,3584]{1,0:T(8,128)(2,1)} %copy-done.4) | copy-start | bytes 2752516
  143.7 12.1 %collective-permute-start.42 = (bf16[64,3584]{1,0:T(8,128)(2,1)S(1)}, bf16[64,3584]{1,0:T(8,128)(2,1)S(1)}, u32[]{:S(2)}, u32[]{:S(2)}) collective-permute-start(bf16[64,3584]{1,0:T(8,128)(2,1)S(1)} %get-tuple-element.118), channel_id=1, source_target_pairs={{0,1},{1,0},{2,3},{3,2},{4,5},{5,4},{6,7},{7,6},{8,9},{9,8},{10,11... | collective-permute-start | bytes 1376264 | tf_op jit(solution)/shard_map/ppermute | solution.py:18
  144.2 12.2 %collective-permute-start.35 = (bf16[256,512]{1,0:T(8,128)(2,1)S(1)}, bf16[256,512]{1,0:T(8,128)(2,1)S(1)}, u32[]{:S(2)}, u32[]{:S(2)}) collective-permute-start(bf16[256,512]{1,0:T(8,128)(2,1)S(1)} %bitcast.40), channel_id=1, source_target_pairs={{4,8},{8,4},{5,9},{9,5},{6,10},{10,6},{7,11},{11,7},{20,24},{24,20... | collective-permute-start | bytes 786440 | tf_op jit(solution)/shard_map/ppermute | solution.py:28
  155.3 18.9 %collective-permute-start.41 = (bf16[64,3584]{1,0:T(8,128)(2,1)S(1)}, bf16[64,3584]{1,0:T(8,128)(2,1)S(1)}, u32[]{:S(2)}, u32[]{:S(2)}) collective-permute-start(bf16[64,3584]{1,0:T(8,128)(2,1)S(1)} %get-tuple-element.116), channel_id=1, source_target_pairs={{0,1},{1,0},{2,3},{3,2},{4,5},{5,4},{6,7},{7,6},{8,9},{9,8},{10,11... | collective-permute-start | bytes 1376264 | tf_op jit(solution)/shard_map/ppermute | solution.py:18
  155.3 18.9 %collective-permute-start.40 = (bf16[64,3584]{1,0:T(8,128)(2,1)S(1)}, bf16[64,3584]{1,0:T(8,128)(2,1)S(1)}, u32[]{:S(2)}, u32[]{:S(2)}) collective-permute-start(bf16[64,3584]{1,0:T(8,128)(2,1)S(1)} %get-tuple-element.114), channel_id=1, source_target_pairs={{0,1},{1,0},{2,3},{3,2},{4,5},{5,4},{6,7},{7,6},{8,9},{9,8},{10,11... | collective-permute-start | bytes 1376264 | tf_op jit(solution)/shard_map/ppermute | solution.py:18
  155.8 18.4 %collective-permute-start.39 = (bf16[64,3584]{1,0:T(8,128)(2,1)S(1)}, bf16[64,3584]{1,0:T(8,128)(2,1)S(1)}, u32[]{:S(2)}, u32[]{:S(2)}) collective-permute-start(bf16[64,3584]{1,0:T(8,128)(2,1)S(1)} %get-tuple-element.112), channel_id=1, source_target_pairs={{0,1},{1,0},{2,3},{3,2},{4,5},{5,4},{6,7},{7,6},{8,9},{9,8},{10,11... | collective-permute-start | bytes 1376264 | tf_op jit(solution)/shard_map/ppermute | solution.py:18
  155.9 18.3 %collective-permute-start.38 = (bf16[64,3584]{1,0:T(8,128)(2,1)S(1)}, bf16[64,3584]{1,0:T(8,128)(2,1)S(1)}, u32[]{:S(2)}, u32[]{:S(2)}) collective-permute-start(bf16[64,3584]{1,0:T(8,128)(2,1)S(1)} %get-tuple-element.110), channel_id=1, source_target_pairs={{0,1},{1,0},{2,3},{3,2},{4,5},{5,4},{6,7},{7,6},{8,9},{9,8},{10,11... | collective-permute-start | bytes 1376264 | tf_op jit(solution)/shard_map/ppermute | solution.py:18
  156.3 10.2 %collective-permute-start.36 = (bf16[256,512]{1,0:T(8,128)(2,1)S(1)}, bf16[256,512]{1,0:T(8,128)(2,1)S(1)}, u32[]{:S(2)}, u32[]{:S(2)}) collective-permute-start(bf16[256,512]{1,0:T(8,128)(2,1)S(1)} %collective-permute-done.28.refs_2_), channel_id=1, source_target_pairs={{4,0},{8,12},{5,1},{9,13},{6,2},{10,14},{7,3},{11,15},{20,16},{24,... | collective-permute-start | bytes 786440 | tf_op jit(solution)/shard_map/ppermute | solution.py:28
  175.7 8.0 %copy-start.1 = (bf16[7168,64]{0,1:T(8,128)(2,1)S(1)}, bf16[7168,64]{0,1:T(8,128)(2,1)}, u32[]{:S(2)}) copy-start(bf16[7168,64]{0,1:T(8,128)(2,1)} %param.10) | copy-start | bytes 2752516

commit v11 on v10

--- a/solution.py
+++ b/solution.py
@@ -355,22 +355,24 @@
         acts_low, grads_low, token_example[0], example_group.shape[0]
     )
     gathered = gather_examples(example_grad, example_group)
-    sent, kept = far_terms(later, 1, 2, example_grad)
-    pair3, sum3 = pair_sum(sent, kept, own_first, *beside, outs=2)
-
-    own = [own, own_first, across(after(own, pair3), 2)]
-    every = order_examples(after(gathered, pair3, *sum2))
-    fisher, group_grad = fisher_and_groups(every, example_grad.shape[1])
-    beside = [after(beside[0], fisher, group_grad)] + beside[1:]
+    sent, kept = far_terms(later, 1, 4, example_grad)
+    own = [own, own_first, across(own, 2)]
+    pair3, sum3 = pair_sum(sent, after(kept, own[2]), own_first, *beside, outs=2)
+
+    own = spread_last(own, pair3)
+    beside = [after(beside[0], pair3, *sum2)] + beside[1:]
     near0 = block_terms(beside, down_weight, 0, 2, [rows // 2] * 4)
-    near0 = [swap(after(term, own[2], sum3[0]), 1) for term in near0]
-    own = spread_last(own, *near0[:1])
+    near0 = [swap(after(term, sum3[0]), 1) for term in near0]
     beside = [after(beside[0], *near0[:1])] + beside[1:]
     near1 = block_terms(beside, down_weight, 1, 2, [rows // 2] * 4)
-    near1 = [swap(after(term, sum3[1]), 1) for term in near1]
+    every = order_examples(after(gathered, near1[0]))
+    fisher, group_grad = fisher_and_groups(every, example_grad.shape[1])
+    own = [after(own[0], near1[0])] + own[1:]
+    near1 = [swap(after(term, sum3[1], *own[3:]), 1) for term in near1]
     adds = [gather_sums(near0, sum0 + sum2)]
     (result,) = block_terms(own, down_weight, 0, 2, [tokens], adds)
     adds = [gather_sums(near1, sum1)] + sum3
+    own = [after(own[0], fisher, group_grad, result)] + own[1:]
     (result,) = block_terms(own, down_weight, 1, 2, [tokens], adds, result)
     return (result, fisher, group_grad)
 

time: 184 us -> 176 us (0.957)
  waiting for transfers between devices: 64.2 us -> 55.5 us
  starting transfers between devices: 35.2 us -> 37.4 us
    ppermute x16, waiting for transfers between devices: 43.1 us -> 37.4 us  [across(): return lax.ppermute(value, 'tensor', pairs)]
    ppermute x29 -> x31, waiting for transfers between devices: 21.1 us -> 18.1 us  [swap(): return lax.ppermute(value, 'dp', [(d, d ^ step) for d in range(size)])]
    ppermute x16, starting transfers between devices: 18.4 us -> 20.7 us  [across(): return lax.ppermute(value, 'tensor', pairs)]
    unnamed x32 -> x26, local copies, waits for them, and re-layouts: 4.25 us -> 2.19 us
    ppermute x29 -> x31, starting transfers between devices: 16.8 us -> 16.7 us  [swap(): return lax.ppermute(value, 'dp', [(d, d ^ step) for d in range(size)])]
  transfers between devices with their start and end apart: 45 -> 47, of which waited for: 23 -> 24; matrix products, arithmetic and copies ran while one was open for 5% -> 6% of each run, Pallas kernels for 31% -> 32%
where the time goes in v11:
time: 176 us
  Pallas kernels  66.9 us (38%)
  waiting for transfers between devices  55.5 us (32%)
  starting transfers between devices  37.4 us (21%)
  matrix products  7.55 us (4%)
  local copies, waits for them, and re-layouts  5.95 us (3%)
    pallas_call x8, Pallas kernels, block_terms(): pl.pallas_call(functools.partial(terms_kernel, size, len(blocks), part *...  58.2 us
    ppermute x16, waiting for transfers between devices, across(): return lax.ppermute(value, 'tensor', pairs)  37.4 us
    ppermute x16, starting transfers between devices, across(): return lax.ppermute(value, 'tensor', pairs)  20.7 us
    ppermute x31, waiting for transfers between devices, swap(): return lax.ppermute(value, 'dp', [(d, d ^ step) for d in range(size)])  18.1 us
    ppermute x31, starting transfers between devices, swap(): return lax.ppermute(value, 'dp', [(d, d ^ step) for d in range(size)])  16.7 us
    pallas_call x4, Pallas kernels, add_pieces(): pl.pallas_call(functools.partial(add_kernel, len(pieces)), out_shape=[jax...  5.57 us
    another operation x5, local copies, waits for them, and re-layouts  3.54 us
  transfers between devices with their start and end apart: 47, of which 24 were waited for; matrix products, arithmetic and copies ran while one was open for 6% of the time, Pallas kernels for 32%

profile of v11, /device:TPU:0, one launch (start us, length us, event | category | flops | bytes accessed | tf_op | source)
XLA Modules:
  0.0 176.1 jit_solution(4854152356827465222)
XLA Ops:
  0.7 2.0 %constant_dynamic-slice_fusion = (bf16[1,1,512,256]{3,2,1,0:T(8,128)(2,1)S(1)}, bf16[1,1,512,256]{3,2,1,0:T(8,128)(2,1)S(1)}, bf16[1,1,512,256]{3,2,1,0:T(8,128)(2,1)S(1)}, bf16[1,1,512,256]{3,2,1,0:T(8,128)(2,1)}) fusion(bf16[1,4,512,256]{3,2,1,0:T(8,128)(2,1)} %param.8, s32[]{:T(128)S(6)} %select_n.96, s32[]{:T(128)S(6)} %select_n.95, s32[]{:T(128)S(6)} %select_n.94, ...), kind=kLoop, calls=%fused_computation.32 | loop fusion | bytes 2097168 | tf_op jit(solution)/shard_map/dynamic-slice.7
  2.9 3.0 %collective-permute-start.3 = (bf16[128,512]{1,0:T(8,128)(2,1)S(1)}, bf16[128,512]{1,0:T(8,128)(2,1)S(1)}, u32[]{:S(2)}, u32[]{:S(2)}) collective-permute-start(bf16[128,512]{1,0:T(8,128)(2,1)S(1)} %get-tuple-element.141), channel_id=1, source_target_pairs={{0,2},{1,3},{2,0},{3,1},{4,6},{5,7},{6,4},{7,5},{8,10},{9,11},{10,... | collective-permute-start | bytes 393224 | tf_op jit(solution)/shard_map/ppermute | solution.py:18
  6.2 3.3 %fusion.15 = f32[256,64]{0,1:T(8,128)S(1)} fusion(bf16[256,7168]{1,0:T(8,128)(2,1)} %param.7, bf16[7168,64]{0,1:T(8,128)(2,1)S(1)} %copy-done), kind=kOutput, calls=%fused_computation.38 | convolution fusion | flops 234881024 | bytes 4653056 | tf_op jit(solution)/shard_map/dot_general | solution.py:277
  9.8 2.2 %collective-permute-done.2 = bf16[128,512]{1,0:T(8,128)(2,1)S(1)} collective-permute-done((bf16[128,512]{1,0:T(8,128)(2,1)S(1)}, bf16[128,512]{1,0:T(8,128)(2,1)S(1)}, u32[]{:S(2)}, u32[]{:S(2)}) %collective-permute-start.2) | collective-permute-done | bytes 131104 | tf_op jit(solution)/shard_map/ppermute | solution.py:18
  12.0 3.6 %collective-permute-start.6 = (bf16[256,512]{1,0:T(8,128)(2,1)S(1)}, bf16[256,512]{1,0:T(8,128)(2,1)S(1)}, u32[]{:S(2)}, u32[]{:S(2)}) collective-permute-start(bf16[256,512]{1,0:T(8,128)(2,1)S(1)} %pad_maximum_fusion.1.refs_0_), channel_id=1, source_target_pairs={{0,12},{4,8},{8,4},{12,0},{1,13},{5,9},{9,5},{13,1},{2,14},{6,10},... | collective-permute-start | bytes 786440 | tf_op jit(solution)/shard_map/ppermute | solution.py:28
  15.6 0.8 collective-permute-start.4
  16.5 0.8 collective-permute-start.1
  17.4 5.2 %collective-permute-done.1 = bf16[128,512]{1,0:T(8,128)(2,1)S(1)} collective-permute-done((bf16[128,512]{1,0:T(8,128)(2,1)S(1)}, bf16[128,512]{1,0:T(8,128)(2,1)S(1)}, u32[]{:S(2)}, u32[]{:S(2)}) %collective-permute-start.1) | collective-permute-done | bytes 131104 | tf_op jit(solution)/shard_map/ppermute | solution.py:18
  22.6 1.4 collective-permute-start.8
  24.4 14.0 %collective-permute-done.5.refs_2_ = bf16[256,512]{1,0:T(8,128)(2,1)S(1)} collective-permute-done((bf16[256,512]{1,0:T(8,128)(2,1)S(1)}, bf16[256,512]{1,0:T(8,128)(2,1)S(1)}, u32[]{:S(2)}, u32[]{:S(2)}) %collective-permute-start.5) | collective-permute-done | bytes 262176 | tf_op jit(solution)/shard_map/ppermute | solution.py:28
  38.5 3.1 %collective-permute-start.9 = (f32[256,128]{0,1:T(8,128)S(1)}, f32[256,128]{0,1:T(8,128)S(1)}, u32[]{:S(2)}, u32[]{:S(2)}) collective-permute-start(f32[256,128]{0,1:T(8,128)S(1)} %fusion.14), channel_id=1, source_target_pairs={{0,8},{4,12},{8,0},{12,4},{1,9},{5,13},{9,1},{13,5},{2,10},{6,14},... | collective-permute-start | bytes 393224 | tf_op jit(solution)/shard_map/ppermute | solution.py:28
  41.6 6.9 %terms.8 = (bf16[64,3584]{1,0:T(8,128)(2,1)S(1)}, bf16[64,3584]{1,0:T(8,128)(2,1)S(1)}, bf16[128,3584]{1,0:T(8,128)(2,1)S(1)}) custom-call(s32[1]{0:T(128)} %bitcast.place_ref, bf16[256,512]{1,0:T(8,128)(2,1)S(1)} %pad_maximum_fusion.1.refs_0_, bf16[256,512]{1,0:T(8,128)(2,1)S(1)} %collective-permute-done.4.refs_1_, ...), custom_call_target="tpu_custom_call" | custom-call | flops 469762048 | bytes 1000 | tf_op jit(solution)/shard_map/terms/pallas_call | solution.py:135
  48.5 0.4 collective-permute-done.10.refs_1_
  49.0 0.5 collective-permute-start.11
  49.5 1.3 collective-permute-done.12.refs_1_
  50.8 0.7 collective-permute-done.11.refs_0_
  51.4 0.5 pair.4
  52.0 2.5 %collective-permute-start.14 = (bf16[256,512]{1,0:T(8,128)(2,1)S(1)}, bf16[256,512]{1,0:T(8,128)(2,1)S(1)}, u32[]{:S(2)}, u32[]{:S(2)}) collective-permute-start(bf16[256,512]{1,0:T(8,128)(2,1)S(1)} %pad_maximum_fusion.refs_0_), channel_id=1, source_target_pairs={{0,12},{4,8},{8,4},{12,0},{1,13},{5,9},{9,5},{13,1},{2,14},{6,10},... | collective-permute-start | bytes 786440 | tf_op jit(solution)/shard_map/ppermute | solution.py:28
  54.8 2.1 %collective-permute-start.17 = (bf16[128,3584]{1,0:T(8,128)(2,1)S(1)}, bf16[128,3584]{1,0:T(8,128)(2,1)S(1)}, u32[]{:S(2)}, u32[]{:S(2)}) collective-permute-start(bf16[128,3584]{1,0:T(8,128)(2,1)S(1)} %pair.4), channel_id=1, source_target_pairs={{0,2},{1,3},{2,0},{3,1},{4,6},{5,7},{6,4},{7,5},{8,10},{9,11},{10,... | collective-permute-start | bytes 2752520 | tf_op jit(solution)/shard_map/ppermute | solution.py:18
  56.9 6.9 %terms.9 = (bf16[64,3584]{1,0:T(8,128)(2,1)S(1)}, bf16[64,3584]{1,0:T(8,128)(2,1)S(1)}, bf16[128,3584]{1,0:T(8,128)(2,1)S(1)}) custom-call(s32[1]{0:T(128)} %bitcast.place_ref, bf16[256,512]{1,0:T(8,128)(2,1)S(1)} %pad_maximum_fusion.1.refs_0_, bf16[256,512]{1,0:T(8,128)(2,1)S(1)} %collective-permute-done.4.refs_1_, ...), custom_call_target="tpu_custom_call" | custom-call | flops 469762048 | bytes 1000 | tf_op jit(solution)/shard_map/terms/pallas_call | solution.py:135
  63.8 14.1 %collective-permute-done.13.refs_2_ = bf16[256,512]{1,0:T(8,128)(2,1)S(1)} collective-permute-done((bf16[256,512]{1,0:T(8,128)(2,1)S(1)}, bf16[256,512]{1,0:T(8,128)(2,1)S(1)}, u32[]{:S(2)}, u32[]{:S(2)}) %collective-permute-start.13) | collective-permute-done | bytes 262176 | tf_op jit(solution)/shard_map/ppermute | solution.py:28
  78.0 0.5 collective-permute-start.15
  78.5 1.3 collective-permute-done.16.refs_1_
  79.8 0.7 collective-permute-done.15.refs_0_
  80.5 1.7 pair.5
  82.2 2.1 %collective-permute-start.22 = (bf16[128,3584]{1,0:T(8,128)(2,1)}, bf16[128,3584]{1,0:T(8,128)(2,1)}, u32[]{:S(2)}, u32[]{:S(2)}) collective-permute-start(bf16[128,3584]{1,0:T(8,128)(2,1)} %pair.5), channel_id=1, source_target_pairs={{0,2},{1,3},{2,0},{3,1},{4,6},{5,7},{6,4},{7,5},{8,10},{9,11},{10,... | collective-permute-start | bytes 2752520 | tf_op jit(solution)/shard_map/ppermute | solution.py:18
  84.3 1.9 %collective-permute-start.18 = (bf16[256,512]{1,0:T(8,128)(2,1)S(1)}, bf16[256,512]{1,0:T(8,128)(2,1)S(1)}, u32[]{:S(2)}, u32[]{:S(2)}) collective-permute-start(bf16[256,512]{1,0:T(8,128)(2,1)S(1)} %collective-permute-done.7.refs_0_), channel_id=1, source_target_pairs={{0,4},{4,0},{8,12},{12,8},{1,5},{5,1},{9,13},{13,9},{2,6},{6,2},{1... | collective-permute-start | bytes 786440 | tf_op jit(solution)/shard_map/ppermute | solution.py:28
  86.2 7.8 %terms.10 = (bf16[64,3584]{1,0:T(8,128)(2,1)}, bf16[64,3584]{1,0:T(8,128)(2,1)}, bf16[128,3584]{1,0:T(8,128)(2,1)S(1)}) custom-call(s32[1]{0:T(128)} %bitcast.place_ref, bf16[256,512]{1,0:T(8,128)(2,1)S(1)} %pad_maximum_fusion.refs_0_, bf16[256,512]{1,0:T(8,128)(2,1)S(1)} %collective-permute-done.10.refs_1_, ...), custom_call_target="tpu_custom_call" | custom-call | flops 469762048 | bytes 1000 | tf_op jit(solution)/shard_map/terms/pallas_call | solution.py:135
  94.0 0.9 copy-done.4
  94.9 2.7 %collective-permute-done.19.refs_2_ = bf16[256,512]{1,0:T(8,128)(2,1)S(1)} collective-permute-done((bf16[256,512]{1,0:T(8,128)(2,1)S(1)}, bf16[256,512]{1,0:T(8,128)(2,1)S(1)}, u32[]{:S(2)}, u32[]{:S(2)}) %collective-permute-start.19) | collective-permute-done | bytes 262176 | tf_op jit(solution)/shard_map/ppermute | solution.py:28
  97.9 0.5 collective-permute-start.20
  98.5 1.1 copy.21
  100.0 0.7 collective-permute-done.20.refs_0_
  100.6 1.2 copy-done.5
  101.8 1.7 pair.6
  103.9 2.6 %collective-permute-start.23 = (bf16[256,512]{1,0:T(8,128)(2,1)S(1)}, bf16[256,512]{1,0:T(8,128)(2,1)S(1)}, u32[]{:S(2)}, u32[]{:S(2)}) collective-permute-start(bf16[256,512]{1,0:T(8,128)(2,1)S(1)} %bitcast.39), channel_id=1, source_target_pairs={{0,8},{4,12},{8,0},{12,4},{1,9},{5,13},{9,1},{13,5},{2,10},{6,14},... | collective-permute-start | bytes 786440 | tf_op jit(solution)/shard_map/ppermute | solution.py:28
  106.8 0.7 collective-permute-start.25
  107.5 1.3 collective-permute-start.26
  108.8 0.9 add.30
  110.3 7.0 %terms.11 = (bf16[32,3584]{1,0:T(8,128)(2,1)S(1)}, bf16[32,3584]{1,0:T(8,128)(2,1)S(1)}, bf16[32,3584]{1,0:T(8,128)(2,1)S(1)}, bf16[32,3584]{1,0:T(8,128)(2,1)S(1)}, bf16[128,3584]{1,0:T(8,128)(2,1)S(1)}) custom-call(s32[1]{0:T(128)} %bitcast.place_ref, bf16[256,512]{1,0:T(8,128)(2,1)S(1)} %pad_maximum_fusion.refs_0_, ...), custom_call_target="tpu_custom_call" | custom-call | flops 469762048 | bytes 1000 | tf_op jit(solution)/shard_map/terms/pallas_call | solution.py:135
  117.6 5.5 %collective-permute-done.26.refs_4_ = bf16[256,512]{1,0:T(8,128)(2,1)S(1)} collective-permute-done((bf16[256,512]{1,0:T(8,128)(2,1)S(1)}, bf16[256,512]{1,0:T(8,128)(2,1)S(1)}, u32[]{:S(2)}, u32[]{:S(2)}) %collective-permute-start.26) | collective-permute-done | bytes 262176 | tf_op jit(solution)/shard_map/ppermute | solution.py:28
  123.1 0.5 collective-permute-start.29
  123.7 0.5 collective-permute-start.27
  124.2 0.5 collective-permute-done.30.refs_3_
  125.6 1.6 pair.7
  127.2 0.4 collective-permute-start.32
  127.6 0.7 collective-permute-start.37
  128.3 1.5 collective-permute-start.38
  129.8 1.7 collective-permute-start.42
  131.5 6.9 %terms.12 = (bf16[64,3584]{1,0:T(8,128)(2,1)S(1)}, bf16[64,3584]{1,0:T(8,128)(2,1)S(1)}, bf16[64,3584]{1,0:T(8,128)(2,1)S(1)}, bf16[64,3584]{1,0:T(8,128)(2,1)S(1)}) custom-call(s32[1]{0:T(128)} %bitcast.place_ref, bf16[256,512]{1,0:T(8,128)(2,1)S(1)} %collective-permute-done.7.refs_0_, bf16[256,512]{1,0:T(8,128)(2,1)S(1)} %collective-permute-done.18.refs_1_, ...), custom_call_target="tpu_custom_call" | custom-call | flops 469762048 | bytes 1000 | tf_op jit(solution)/shard_map/terms/pallas_call | solution.py:135
  138.4 2.4 %collective-permute-done.32.refs_7_ = bf16[64,3584]{1,0:T(8,128)(2,1)S(1)} collective-permute-done((bf16[64,3584]{1,0:T(8,128)(2,1)}, bf16[64,3584]{1,0:T(8,128)(2,1)S(1)}, u32[]{:S(2)}, u32[]{:S(2)}) %collective-permute-start.32) | collective-permute-done | bytes 458784 | tf_op jit(solution)/shard_map/ppermute | solution.py:18
  140.9 0.6 collective-permute-start.36
  141.5 1.1 collective-permute-done.33.refs_0_
  142.6 0.5 collective-permute-start.35
  143.1 6.9 %terms.13 = (bf16[64,3584]{1,0:T(8,128)(2,1)S(1)}, bf16[64,3584]{1,0:T(8,128)(2,1)S(1)}, bf16[64,3584]{1,0:T(8,128)(2,1)S(1)}, bf16[64,3584]{1,0:T(8,128)(2,1)S(1)}) custom-call(s32[1]{0:T(128)} %bitcast.place_ref, bf16[256,512]{1,0:T(8,128)(2,1)S(1)} %collective-permute-done.7.refs_0_, bf16[256,512]{1,0:T(8,128)(2,1)S(1)} %collective-permute-done.18.refs_1_, ...), custom_call_target="tpu_custom_call" | custom-call | flops 469762048 | bytes 1000 | tf_op jit(solution)/shard_map/terms/pallas_call | solution.py:135
  150.0 0.6 collective-permute-start.41
  150.7 0.4 collective-permute-start.39
  151.3 0.5 collective-permute-start.46
  153.4 1.7 sums.2.refs_6_
  155.0 7.7 %terms.14.refs_9_ = bf16[256,7168]{1,0:T(8,128)(2,1)} custom-call(s32[1]{0:T(128)} %bitcast.place_ref, bf16[256,512]{1,0:T(8,128)(2,1)S(1)} %bitcast.41, bf16[256,512]{1,0:T(8,128)(2,1)S(1)} %collective-permute-done.24.refs_1_, bf16[256,512]{1,0:T(8,128)(2,1)S(1)} %collective-permute-done.23.refs_2_, bf16[256,512]{1,0:T(8,128)(2,1)S(1)} %collective-permute-done.37.refs_3_, ...), custom_call_target="tpu_custom_call" | custom-call | flops 469762048 | bytes 1000 | tf_op jit(solution)/shard_map/terms/pallas_call | solution.py:135
  162.8 2.7 %fusion.4 = f32[1024,1024]{1,0:T(8,128)} fusion(bf16[16,4224]{1,0:T(8,128)(2,1)S(1)} %pad_maximum_fusion.2, s32[]{:T(128)S(6)} %select_n.121, s32[]{:T(128)S(6)} %select_n.122), kind=kOutput, calls=%fused_computation.20 | convolution fusion | flops 33554432 | bytes 4259848 | tf_op jit(solution)/shard_map/dot_general | solution.py:266
  165.5 0.9 fusion.6
  166.4 1.5 sums.3.refs_6_
  167.9 8.0 %terms.15 = bf16[256,7168]{1,0:T(8,128)(2,1)} custom-call(s32[1]{0:T(128)} %bitcast.place_ref, bf16[256,512]{1,0:T(8,128)(2,1)S(1)} %bitcast.42, bf16[256,512]{1,0:T(8,128)(2,1)S(1)} %collective-permute-done.24.refs_1_, bf16[256,512]{1,0:T(8,128)(2,1)S(1)} %collective-permute-done.23.refs_2_, ...), custom_call_target="tpu_custom_call", output_to_operand_aliasing={{}: (10, {})} | custom-call | flops 469762048 | bytes 1000 | tf_op jit(solution)/shard_map/terms/pallas_call | solution.py:135
  (99 shorter events, 6.7 us)
Async XLA Ops:
  0.6 5.5 %copy-start = (bf16[7168,64]{0,1:T(8,128)(2,1)S(1)}, bf16[7168,64]{0,1:T(8,128)(2,1)}, u32[]{:S(2)}) copy-start(bf16[7168,64]{0,1:T(8,128)(2,1)} %param.10) | copy-start | bytes 2752516
  2.7 6.7 %copy-start.6 = (bf16[1,4,512,256]{3,2,1,0:T(8,128)(2,1)S(1)}, bf16[1,4,512,256]{3,2,1,0:T(8,128)(2,1)}, u32[]{:S(2)}) copy-start(bf16[1,4,512,256]{3,2,1,0:T(8,128)(2,1)} %param.8) | copy-start | bytes 3145732
  2.7 6.7 %copy-start.9 = (bf16[1,4,512,64]{2,3,1,0:T(8,128)(2,1)S(1)}, bf16[1,4,512,64]{2,3,1,0:T(8,128)(2,1)}, u32[]{:S(2)}) copy-start(bf16[1,4,512,64]{2,3,1,0:T(8,128)(2,1)} %param.11) | copy-start | bytes 786436
  2.9 6.9 %collective-permute-start.3 = (bf16[128,512]{1,0:T(8,128)(2,1)S(1)}, bf16[128,512]{1,0:T(8,128)(2,1)S(1)}, u32[]{:S(2)}, u32[]{:S(2)}) collective-permute-start(bf16[128,512]{1,0:T(8,128)(2,1)S(1)} %get-tuple-element.141), channel_id=1, source_target_pairs={{0,2},{1,3},{2,0},{3,1},{4,6},{5,7},{6,4},{7,5},{8,10},{9,11},{10,... | collective-permute-start | bytes 393224 | tf_op jit(solution)/shard_map/ppermute | solution.py:18
  6.1 5.9 %collective-permute-start.2 = (bf16[128,512]{1,0:T(8,128)(2,1)S(1)}, bf16[128,512]{1,0:T(8,128)(2,1)S(1)}, u32[]{:S(2)}, u32[]{:S(2)}) collective-permute-start(bf16[128,512]{1,0:T(8,128)(2,1)S(1)} %get-tuple-element.139), channel_id=1, source_target_pairs={{0,3},{1,2},{2,1},{3,0},{4,7},{5,6},{6,5},{7,4},{8,11},{9,10},{10,... | collective-permute-start | bytes 393224 | tf_op jit(solution)/shard_map/ppermute | solution.py:18
  12.0 12.4 %collective-permute-start.6 = (bf16[256,512]{1,0:T(8,128)(2,1)S(1)}, bf16[256,512]{1,0:T(8,128)(2,1)S(1)}, u32[]{:S(2)}, u32[]{:S(2)}) collective-permute-start(bf16[256,512]{1,0:T(8,128)(2,1)S(1)} %pad_maximum_fusion.1.refs_0_), channel_id=1, source_target_pairs={{0,12},{4,8},{8,4},{12,0},{1,13},{5,9},{9,5},{13,1},{2,14},{6,10},... | collective-permute-start | bytes 786440 | tf_op jit(solution)/shard_map/ppermute | solution.py:28
  15.6 22.8 %collective-permute-start.5 = (bf16[256,512]{1,0:T(8,128)(2,1)S(1)}, bf16[256,512]{1,0:T(8,128)(2,1)S(1)}, u32[]{:S(2)}, u32[]{:S(2)}) collective-permute-start(bf16[256,512]{1,0:T(8,128)(2,1)S(1)} %pad_maximum_fusion.1.refs_0_), channel_id=1, source_target_pairs={{0,8},{4,12},{8,0},{12,4},{1,9},{5,13},{9,1},{13,5},{2,10},{6,14},... | collective-permute-start | bytes 786440 | tf_op jit(solution)/shard_map/ppermute | solution.py:28
  15.6 22.8 %collective-permute-start.4 = (bf16[256,512]{1,0:T(8,128)(2,1)S(1)}, bf16[256,512]{1,0:T(8,128)(2,1)S(1)}, u32[]{:S(2)}, u32[]{:S(2)}) collective-permute-start(bf16[256,512]{1,0:T(8,128)(2,1)S(1)} %pad_maximum_fusion.1.refs_0_), channel_id=1, source_target_pairs={{0,4},{4,0},{8,12},{12,8},{1,5},{5,1},{9,13},{13,9},{2,6},{6,2},{1... | collective-permute-start | bytes 786440 | tf_op jit(solution)/shard_map/ppermute | solution.py:28
  16.5 6.2 %collective-permute-start.1 = (bf16[128,512]{1,0:T(8,128)(2,1)S(1)}, bf16[128,512]{1,0:T(8,128)(2,1)S(1)}, u32[]{:S(2)}, u32[]{:S(2)}) collective-permute-start(bf16[128,512]{1,0:T(8,128)(2,1)S(1)} %get-tuple-element.142), channel_id=1, source_target_pairs={{0,2},{1,3},{2,0},{3,1},{4,6},{5,7},{6,4},{7,5},{8,10},{9,11},{10,... | collective-permute-start | bytes 393224 | tf_op jit(solution)/shard_map/ppermute | solution.py:18
  17.3 7.0 %collective-permute-start = (bf16[128,512]{1,0:T(8,128)(2,1)S(1)}, bf16[128,512]{1,0:T(8,128)(2,1)S(1)}, u32[]{:S(2)}, u32[]{:S(2)}) collective-permute-start(bf16[128,512]{1,0:T(8,128)(2,1)S(1)} %get-tuple-element.140), channel_id=1, source_target_pairs={{0,3},{1,2},{2,1},{3,0},{4,7},{5,6},{6,5},{7,4},{8,11},{9,10},{10,... | collective-permute-start | bytes 393224 | tf_op jit(solution)/shard_map/ppermute | solution.py:18
  22.6 15.8 %collective-permute-start.8 = (f32[256,128]{0,1:T(8,128)S(1)}, f32[256,128]{0,1:T(8,128)S(1)}, u32[]{:S(2)}, u32[]{:S(2)}) collective-permute-start(f32[256,128]{0,1:T(8,128)S(1)} %pad_maximum_fusion.3), channel_id=1, source_target_pairs={{0,4},{4,0},{8,12},{12,8},{1,5},{5,1},{9,13},{13,9},{2,6},{6,2},{1... | collective-permute-start | bytes 393224 | tf_op jit(solution)/shard_map/ppermute | solution.py:28
  24.2 17.4 %collective-permute-start.7 = (bf16[256,512]{1,0:T(8,128)(2,1)S(1)}, bf16[256,512]{1,0:T(8,128)(2,1)S(1)}, u32[]{:S(2)}, u32[]{:S(2)}) collective-permute-start(bf16[256,512]{1,0:T(8,128)(2,1)S(1)} %bitcast.46), channel_id=1, source_target_pairs={{0,1},{1,0},{2,3},{3,2},{4,5},{5,4},{6,7},{7,6},{8,9},{9,8},{10,11... | collective-permute-start | bytes 786440 | tf_op jit(solution)/shard_map/ppermute | solution.py:18
  38.4 10.5 %collective-permute-start.10 = (bf16[256,512]{1,0:T(8,128)(2,1)S(1)}, bf16[256,512]{1,0:T(8,128)(2,1)S(1)}, u32[]{:S(2)}, u32[]{:S(2)}) collective-permute-start(bf16[256,512]{1,0:T(8,128)(2,1)S(1)} %pad_maximum_fusion.refs_0_), channel_id=1, source_target_pairs={{0,4},{4,0},{8,12},{12,8},{1,5},{5,1},{9,13},{13,9},{2,6},{6,2},{1... | collective-permute-start | bytes 786440 | tf_op jit(solution)/shard_map/ppermute | solution.py:28
  38.5 10.0 %copy-start.7 = (f32[256,128]{0,1:T(8,128)}, f32[256,128]{0,1:T(8,128)S(1)}, u32[]{:S(2)}) copy-start(f32[256,128]{0,1:T(8,128)S(1)} %fusion.14) | copy-start | bytes 393220
  38.5 10.0 %collective-permute-start.9 = (f32[256,128]{0,1:T(8,128)S(1)}, f32[256,128]{0,1:T(8,128)S(1)}, u32[]{:S(2)}, u32[]{:S(2)}) collective-permute-start(f32[256,128]{0,1:T(8,128)S(1)} %fusion.14), channel_id=1, source_target_pairs={{0,8},{4,12},{8,0},{12,4},{1,9},{5,13},{9,1},{13,5},{2,10},{6,14},... | collective-permute-start | bytes 393224 | tf_op jit(solution)/shard_map/ppermute | solution.py:28
  48.5 15.3 %copy-start.10 = (f32[256,128]{0,1:T(8,128)}, f32[256,128]{0,1:T(8,128)S(1)}, u32[]{:S(2)}) copy-start(f32[256,128]{0,1:T(8,128)S(1)} %collective-permute-done.9) | copy-start | bytes 393220
  49.0 1.8 %collective-permute-start.12 = (bf16[64,3584]{1,0:T(8,128)(2,1)S(1)}, bf16[64,3584]{1,0:T(8,128)(2,1)S(1)}, u32[]{:S(2)}, u32[]{:S(2)}) collective-permute-start(bf16[64,3584]{1,0:T(8,128)(2,1)S(1)} %get-tuple-element.77), channel_id=1, source_target_pairs={{0,1},{1,0},{2,3},{3,2},{4,5},{5,4},{6,7},{7,6},{8,9},{9,8},{10,11... | collective-permute-start | bytes 1376264 | tf_op jit(solution)/shard_map/ppermute | solution.py:18
  49.0 2.5 %collective-permute-start.11 = (bf16[64,3584]{1,0:T(8,128)(2,1)S(1)}, bf16[64,3584]{1,0:T(8,128)(2,1)S(1)}, u32[]{:S(2)}, u32[]{:S(2)}) collective-permute-start(bf16[64,3584]{1,0:T(8,128)(2,1)S(1)} %get-tuple-element.75), channel_id=1, source_target_pairs={{0,1},{1,0},{2,3},{3,2},{4,5},{5,4},{6,7},{7,6},{8,9},{9,8},{10,11... | collective-permute-start | bytes 1376264 | tf_op jit(solution)/shard_map/ppermute | solution.py:18
  52.0 11.8 %collective-permute-start.14 = (bf16[256,512]{1,0:T(8,128)(2,1)S(1)}, bf16[256,512]{1,0:T(8,128)(2,1)S(1)}, u32[]{:S(2)}, u32[]{:S(2)}) collective-permute-start(bf16[256,512]{1,0:T(8,128)(2,1)S(1)} %pad_maximum_fusion.refs_0_), channel_id=1, source_target_pairs={{0,12},{4,8},{8,4},{12,0},{1,13},{5,9},{9,5},{13,1},{2,14},{6,10},... | collective-permute-start | bytes 786440 | tf_op jit(solution)/shard_map/ppermute | solution.py:28
  54.5 23.5 %collective-permute-start.13 = (bf16[256,512]{1,0:T(8,128)(2,1)S(1)}, bf16[256,512]{1,0:T(8,128)(2,1)S(1)}, u32[]{:S(2)}, u32[]{:S(2)}) collective-permute-start(bf16[256,512]{1,0:T(8,128)(2,1)S(1)} %pad_maximum_fusion.refs_0_), channel_id=1, source_target_pairs={{0,8},{4,12},{8,0},{12,4},{1,9},{5,13},{9,1},{13,5},{2,10},{6,14},... | collective-permute-start | bytes 786440 | tf_op jit(solution)/shard_map/ppermute | solution.py:28
  54.8 31.4 %collective-permute-start.17 = (bf16[128,3584]{1,0:T(8,128)(2,1)S(1)}, bf16[128,3584]{1,0:T(8,128)(2,1)S(1)}, u32[]{:S(2)}, u32[]{:S(2)}) collective-permute-start(bf16[128,3584]{1,0:T(8,128)(2,1)S(1)} %pair.4), channel_id=1, source_target_pairs={{0,2},{1,3},{2,0},{3,1},{4,6},{5,7},{6,4},{7,5},{8,10},{9,11},{10,... | collective-permute-start | bytes 2752520 | tf_op jit(solution)/shard_map/ppermute | solution.py:18
  78.0 1.8 %collective-permute-start.16 = (bf16[64,3584]{1,0:T(8,128)(2,1)S(1)}, bf16[64,3584]{1,0:T(8,128)(2,1)S(1)}, u32[]{:S(2)}, u32[]{:S(2)}) collective-permute-start(bf16[64,3584]{1,0:T(8,128)(2,1)S(1)} %get-tuple-element.84), channel_id=1, source_target_pairs={{0,1},{1,0},{2,3},{3,2},{4,5},{5,4},{6,7},{7,6},{8,9},{9,8},{10,11... | collective-permute-start | bytes 1376264 | tf_op jit(solution)/shard_map/ppermute | solution.py:18
  78.0 2.5 %collective-permute-start.15 = (bf16[64,3584]{1,0:T(8,128)(2,1)S(1)}, bf16[64,3584]{1,0:T(8,128)(2,1)S(1)}, u32[]{:S(2)}, u32[]{:S(2)}) collective-permute-start(bf16[64,3584]{1,0:T(8,128)(2,1)S(1)} %get-tuple-element.82), channel_id=1, source_target_pairs={{0,1},{1,0},{2,3},{3,2},{4,5},{5,4},{6,7},{7,6},{8,9},{9,8},{10,11... | collective-permute-start | bytes 1376264 | tf_op jit(solution)/shard_map/ppermute | solution.py:18
  82.2 17.4 %copy-start.11 = (s32[1,256]{1,0:T(1,128)S(1)}, s32[1,256]{1,0:T(1,128)}, u32[]{:S(2)}) copy-start(s32[1,256]{1,0:T(1,128)} %param.12) | copy-start | bytes 3076
  82.2 26.6 %copy-start.8 = (f32[256,128]{0,1:T(8,128)S(1)}, f32[256,128]{0,1:T(8,128)}, u32[]{:S(2)}) copy-start(f32[256,128]{0,1:T(8,128)} %copy-done.7) | copy-start | bytes 393220
  82.2 25.3 %collective-permute-start.22 = (bf16[128,3584]{1,0:T(8,128)(2,1)}, bf16[128,3584]{1,0:T(8,128)(2,1)}, u32[]{:S(2)}, u32[]{:S(2)}) collective-permute-start(bf16[128,3584]{1,0:T(8,128)(2,1)} %pair.5), channel_id=1, source_target_pairs={{0,2},{1,3},{2,0},{3,1},{4,6},{5,7},{6,4},{7,5},{8,10},{9,11},{10,... | collective-permute-start | bytes 2752520 | tf_op jit(solution)/shard_map/ppermute | solution.py:18
  84.3 13.4 %collective-permute-start.19 = (bf16[256,512]{1,0:T(8,128)(2,1)S(1)}, bf16[256,512]{1,0:T(8,128)(2,1)S(1)}, u32[]{:S(2)}, u32[]{:S(2)}) collective-permute-start(bf16[256,512]{1,0:T(8,128)(2,1)S(1)} %collective-permute-done.7.refs_0_), channel_id=1, source_target_pairs={{0,8},{4,12},{8,0},{12,4},{1,9},{5,13},{9,1},{13,5},{2,10},{6,14},... | collective-permute-start | bytes 786440 | tf_op jit(solution)/shard_map/ppermute | solution.py:28
  84.3 13.7 %collective-permute-start.18 = (bf16[256,512]{1,0:T(8,128)(2,1)S(1)}, bf16[256,512]{1,0:T(8,128)(2,1)S(1)}, u32[]{:S(2)}, u32[]{:S(2)}) collective-permute-start(bf16[256,512]{1,0:T(8,128)(2,1)S(1)} %collective-permute-done.7.refs_0_), channel_id=1, source_target_pairs={{0,4},{4,0},{8,12},{12,8},{1,5},{5,1},{9,13},{13,9},{2,6},{6,2},{1... | collective-permute-start | bytes 786440 | tf_op jit(solution)/shard_map/ppermute | solution.py:28
  86.2 7.8 %copy-start.2 = (bf16[128,3584]{1,0:T(8,128)(2,1)}, bf16[128,3584]{1,0:T(8,128)(2,1)S(1)}, u32[]{:S(2)}) copy-start(bf16[128,3584]{1,0:T(8,128)(2,1)S(1)} %collective-permute-done.17.refs_4_) | copy-start | bytes 2752516
  94.0 1.0 copy-start.4
  97.9 2.0 %collective-permute-start.21 = (bf16[64,3584]{1,0:T(8,128)(2,1)}, bf16[64,3584]{1,0:T(8,128)(2,1)S(1)}, u32[]{:S(2)}, u32[]{:S(2)}) collective-permute-start(bf16[64,3584]{1,0:T(8,128)(2,1)} %get-tuple-element.91), channel_id=1, source_target_pairs={{0,1},{1,0},{2,3},{3,2},{4,5},{5,4},{6,7},{7,6},{8,9},{9,8},{10,11... | collective-permute-start | bytes 1376264 | tf_op jit(solution)/shard_map/ppermute | solution.py:18
  97.9 2.7 %collective-permute-start.20 = (bf16[64,3584]{1,0:T(8,128)(2,1)}, bf16[64,3584]{1,0:T(8,128)(2,1)S(1)}, u32[]{:S(2)}, u32[]{:S(2)}) collective-permute-start(bf16[64,3584]{1,0:T(8,128)(2,1)} %get-tuple-element.89), channel_id=1, source_target_pairs={{0,1},{1,0},{2,3},{3,2},{4,5},{5,4},{6,7},{7,6},{8,9},{9,8},{10,11... | collective-permute-start | bytes 1376264 | tf_op jit(solution)/shard_map/ppermute | solution.py:18
  100.6 1.2 copy-start.5
  103.6 14.1 %collective-permute-start.24 = (bf16[256,512]{1,0:T(8,128)(2,1)S(1)}, bf16[256,512]{1,0:T(8,128)(2,1)S(1)}, u32[]{:S(2)}, u32[]{:S(2)}) collective-permute-start(bf16[256,512]{1,0:T(8,128)(2,1)S(1)} %bitcast.38), channel_id=1, source_target_pairs={{0,4},{4,0},{8,12},{12,8},{1,5},{5,1},{9,13},{13,9},{2,6},{6,2},{1... | collective-permute-start | bytes 786440 | tf_op jit(solution)/shard_map/ppermute | solution.py:28
  103.9 19.8 %collective-permute-start.23 = (bf16[256,512]{1,0:T(8,128)(2,1)S(1)}, bf16[256,512]{1,0:T(8,128)(2,1)S(1)}, u32[]{:S(2)}, u32[]{:S(2)}) collective-permute-start(bf16[256,512]{1,0:T(8,128)(2,1)S(1)} %bitcast.39), channel_id=1, source_target_pairs={{0,8},{4,12},{8,0},{12,4},{1,9},{5,13},{9,1},{13,5},{2,10},{6,14},... | collective-permute-start | bytes 786440 | tf_op jit(solution)/shard_map/ppermute | solution.py:28
  106.5 25.0 %collective-permute-start.31 = (bf16[128,3584]{1,0:T(8,128)(2,1)}, bf16[128,3584]{1,0:T(8,128)(2,1)}, u32[]{:S(2)}, u32[]{:S(2)}) collective-permute-start(bf16[128,3584]{1,0:T(8,128)(2,1)} %pair.6), channel_id=1, source_target_pairs={{0,2},{1,3},{2,0},{3,1},{4,6},{5,7},{6,4},{7,5},{8,10},{9,11},{10,... | collective-permute-start | bytes 2752520 | tf_op jit(solution)/shard_map/ppermute | solution.py:18
  106.8 10.8 %collective-permute-start.25 = (bf16[256,512]{1,0:T(8,128)(2,1)S(1)}, bf16[256,512]{1,0:T(8,128)(2,1)S(1)}, u32[]{:S(2)}, u32[]{:S(2)}) collective-permute-start(bf16[256,512]{1,0:T(8,128)(2,1)S(1)} %collective-permute-done.7.refs_0_), channel_id=1, source_target_pairs={{4,8},{8,4},{5,9},{9,5},{6,10},{10,6},{7,11},{11,7},{20,24},{24,20... | collective-permute-start | bytes 786440 | tf_op jit(solution)/shard_map/ppermute | solution.py:28
  107.5 15.6 %collective-permute-start.26 = (bf16[256,512]{1,0:T(8,128)(2,1)S(1)}, bf16[256,512]{1,0:T(8,128)(2,1)S(1)}, u32[]{:S(2)}, u32[]{:S(2)}) collective-permute-start(bf16[256,512]{1,0:T(8,128)(2,1)S(1)} %collective-permute-done.19.refs_2_), channel_id=1, source_target_pairs={{4,0},{8,12},{5,1},{9,13},{6,2},{10,14},{7,3},{11,15},{20,16},{24,... | collective-permute-start | bytes 786440 | tf_op jit(solution)/shard_map/ppermute | solution.py:28
  110.3 17.3 %copy-start.12 = (s32[4]{0:T(128)S(1)}, s32[4]{0:T(128)}, u32[]{:S(2)}) copy-start(s32[4]{0:T(128)} %param.13) | copy-start | bytes 52
  123.1 1.5 collective-permute-start.30
  123.1 1.8 %collective-permute-start.29 = (bf16[32,3584]{1,0:T(8,128)(2,1)S(1)}, bf16[32,3584]{1,0:T(8,128)(2,1)S(1)}, u32[]{:S(2)}, u32[]{:S(2)}) collective-permute-start(bf16[32,3584]{1,0:T(8,128)(2,1)S(1)} %get-tuple-element.104), channel_id=1, source_target_pairs={{0,1},{1,0},{2,3},{3,2},{4,5},{5,4},{6,7},{7,6},{8,9},{9,8},{10,11... | collective-permute-start | bytes 688136 | tf_op jit(solution)/shard_map/ppermute | solution.py:18
  123.6 1.6 collective-permute-start.28
  123.7 2.0 %collective-permute-start.27 = (bf16[32,3584]{1,0:T(8,128)(2,1)S(1)}, bf16[32,3584]{1,0:T(8,128)(2,1)S(1)}, u32[]{:S(2)}, u32[]{:S(2)}) collective-permute-start(bf16[32,3584]{1,0:T(8,128)(2,1)S(1)} %get-tuple-element.100), channel_id=1, source_target_pairs={{0,1},{1,0},{2,3},{3,2},{4,5},{5,4},{6,7},{7,6},{8,9},{9,8},{10,11... | collective-permute-start | bytes 688136 | tf_op jit(solution)/shard_map/ppermute | solution.py:18
  127.2 13.6 %collective-permute-start.32 = (bf16[64,3584]{1,0:T(8,128)(2,1)}, bf16[64,3584]{1,0:T(8,128)(2,1)S(1)}, u32[]{:S(2)}, u32[]{:S(2)}) collective-permute-start(bf16[64,3584]{1,0:T(8,128)(2,1)} %get-tuple-element.107), channel_id=1, source_target_pairs={{0,2},{1,3},{2,0},{3,1},{4,6},{5,7},{6,4},{7,5},{8,10},{9,11},{10,... | collective-permute-start | bytes 1376264 | tf_op jit(solution)/shard_map/ppermute | solution.py:18
  127.6 15.5 %collective-permute-start.37 = (bf16[256,512]{1,0:T(8,128)(2,1)S(1)}, bf16[256,512]{1,0:T(8,128)(2,1)S(1)}, u32[]{:S(2)}, u32[]{:S(2)}) collective-permute-start(bf16[256,512]{1,0:T(8,128)(2,1)S(1)} %bitcast.40), channel_id=1, source_target_pairs={{4,8},{8,4},{5,9},{9,5},{6,10},{10,6},{7,11},{11,7},{20,24},{24,20... | collective-permute-start | bytes 786440 | tf_op jit(solution)/shard_map/ppermute | solution.py:28
  128.3 21.7 %collective-permute-start.38 = (bf16[256,512]{1,0:T(8,128)(2,1)S(1)}, bf16[256,512]{1,0:T(8,128)(2,1)S(1)}, u32[]{:S(2)}, u32[]{:S(2)}) collective-permute-start(bf16[256,512]{1,0:T(8,128)(2,1)S(1)} %collective-permute-done.23.refs_2_), channel_id=1, source_target_pairs={{4,0},{8,12},{5,1},{9,13},{6,2},{10,14},{7,3},{11,15},{20,16},{24,... | collective-permute-start | bytes 786440 | tf_op jit(solution)/shard_map/ppermute | solution.py:28
  129.8 20.8 %collective-permute-start.42 = (bf16[64,3584]{1,0:T(8,128)(2,1)S(1)}, bf16[64,3584]{1,0:T(8,128)(2,1)S(1)}, u32[]{:S(2)}, u32[]{:S(2)}) collective-permute-start(bf16[64,3584]{1,0:T(8,128)(2,1)S(1)} %get-tuple-element.127), channel_id=1, source_target_pairs={{0,2},{1,3},{2,0},{3,1},{4,6},{5,7},{6,4},{7,5},{8,10},{9,11},{10,... | collective-permute-start | bytes 1376264 | tf_op jit(solution)/shard_map/ppermute | solution.py:18
  140.8 1.8 %collective-permute-start.33 = (bf16[64,3584]{1,0:T(8,128)(2,1)S(1)}, bf16[64,3584]{1,0:T(8,128)(2,1)S(1)}, u32[]{:S(2)}, u32[]{:S(2)}) collective-permute-start(bf16[64,3584]{1,0:T(8,128)(2,1)S(1)} %get-tuple-element.110), channel_id=1, source_target_pairs={{0,1},{1,0},{2,3},{3,2},{4,5},{5,4},{6,7},{7,6},{8,9},{9,8},{10,11... | collective-permute-start | bytes 1376264 | tf_op jit(solution)/shard_map/ppermute | solution.py:18
  140.9 9.8 %collective-permute-start.36 = (bf16[4,4224]{1,0:T(4,128)(2,1)S(1)}, bf16[4,4224]{1,0:T(4,128)(2,1)S(1)}, u32[]{:S(2)}, u32[]{:S(2)}) collective-permute-start(bf16[4,4224]{1,0:T(4,128)(2,1)S(1)} %pad_maximum_fusion.4), channel_id=1, source_target_pairs={{0,3},{1,2},{2,1},{3,0},{4,7},{5,6},{6,5},{7,4},{8,11},{9,10},{10,... | collective-permute-start | bytes 101384 | tf_op jit(solution)/shard_map/ppermute | solution.py:18
  141.5 11.9 %copy-start.3 = (bf16[128,3584]{1,0:T(8,128)(2,1)S(1)}, bf16[128,3584]{1,0:T(8,128)(2,1)}, u32[]{:S(2)}) copy-start(bf16[128,3584]{1,0:T(8,128)(2,1)} %copy-done.2) | copy-start | bytes 2752516
  142.6 8.7 %collective-permute-start.35 = (bf16[4,4224]{1,0:T(4,128)(2,1)S(1)}, bf16[4,4224]{1,0:T(4,128)(2,1)S(1)}, u32[]{:S(2)}, u32[]{:S(2)}) collective-permute-start(bf16[4,4224]{1,0:T(4,128)(2,1)S(1)} %pad_maximum_fusion.4), channel_id=1, source_target_pairs={{0,2},{1,3},{2,0},{3,1},{4,6},{5,7},{6,4},{7,5},{8,10},{9,11},{10,... | collective-permute-start | bytes 101384 | tf_op jit(solution)/shard_map/ppermute | solution.py:18
  143.1 8.2 %collective-permute-start.34 = (bf16[4,4224]{1,0:T(4,128)(2,1)S(1)}, bf16[4,4224]{1,0:T(4,128)(2,1)S(1)}, u32[]{:S(2)}, u32[]{:S(2)}) collective-permute-start(bf16[4,4224]{1,0:T(4,128)(2,1)S(1)} %pad_maximum_fusion.4), channel_id=1, source_target_pairs={{0,1},{1,0},{2,3},{3,2},{4,5},{5,4},{6,7},{7,6},{8,9},{9,8},{10,11... | collective-permute-start | bytes 101384 | tf_op jit(solution)/shard_map/ppermute | solution.py:18
  150.0 2.1 %collective-permute-start.41 = (bf16[64,3584]{1,0:T(8,128)(2,1)S(1)}, bf16[64,3584]{1,0:T(8,128)(2,1)S(1)}, u32[]{:S(2)}, u32[]{:S(2)}) collective-permute-start(bf16[64,3584]{1,0:T(8,128)(2,1)S(1)} %get-tuple-element.125), channel_id=1, source_target_pairs={{0,1},{1,0},{2,3},{3,2},{4,5},{5,4},{6,7},{7,6},{8,9},{9,8},{10,11... | collective-permute-start | bytes 1376264 | tf_op jit(solution)/shard_map/ppermute | solution.py:18
  150.6 2.1 %collective-permute-start.40 = (bf16[64,3584]{1,0:T(8,128)(2,1)S(1)}, bf16[64,3584]{1,0:T(8,128)(2,1)S(1)}, u32[]{:S(2)}, u32[]{:S(2)}) collective-permute-start(bf16[64,3584]{1,0:T(8,128)(2,1)S(1)} %get-tuple-element.123), channel_id=1, source_target_pairs={{0,1},{1,0},{2,3},{3,2},{4,5},{5,4},{6,7},{7,6},{8,9},{9,8},{10,11... | collective-permute-start | bytes 1376264 | tf_op jit(solution)/shard_map/ppermute | solution.py:18
  150.7 2.7 %collective-permute-start.39 = (bf16[64,3584]{1,0:T(8,128)(2,1)S(1)}, bf16[64,3584]{1,0:T(8,128)(2,1)S(1)}, u32[]{:S(2)}, u32[]{:S(2)}) collective-permute-start(bf16[64,3584]{1,0:T(8,128)(2,1)S(1)} %get-tuple-element.121), channel_id=1, source_target_pairs={{0,1},{1,0},{2,3},{3,2},{4,5},{5,4},{6,7},{7,6},{8,9},{9,8},{10,11... | collective-permute-start | bytes 1376264 | tf_op jit(solution)/shard_map/ppermute | solution.py:18
  151.3 15.1 %collective-permute-start.43 = (bf16[64,3584]{1,0:T(8,128)(2,1)S(1)}, bf16[64,3584]{1,0:T(8,128)(2,1)S(1)}, u32[]{:S(2)}, u32[]{:S(2)}) collective-permute-start(bf16[64,3584]{1,0:T(8,128)(2,1)S(1)} %get-tuple-element.128), channel_id=1, source_target_pairs={{0,1},{1,0},{2,3},{3,2},{4,5},{5,4},{6,7},{7,6},{8,9},{9,8},{10,11... | collective-permute-start | bytes 1376264 | tf_op jit(solution)/shard_map/ppermute | solution.py:18
  151.3 15.1 %collective-permute-start.46 = (bf16[64,3584]{1,0:T(8,128)(2,1)S(1)}, bf16[64,3584]{1,0:T(8,128)(2,1)S(1)}, u32[]{:S(2)}, u32[]{:S(2)}) collective-permute-start(bf16[64,3584]{1,0:T(8,128)(2,1)S(1)} %get-tuple-element.134), channel_id=1, source_target_pairs={{0,1},{1,0},{2,3},{3,2},{4,5},{5,4},{6,7},{7,6},{8,9},{9,8},{10,11... | collective-permute-start | bytes 1376264 | tf_op jit(solution)/shard_map/ppermute | solution.py:18
  152.1 14.3 %collective-permute-start.45 = (bf16[64,3584]{1,0:T(8,128)(2,1)S(1)}, bf16[64,3584]{1,0:T(8,128)(2,1)S(1)}, u32[]{:S(2)}, u32[]{:S(2)}) collective-permute-start(bf16[64,3584]{1,0:T(8,128)(2,1)S(1)} %get-tuple-element.132), channel_id=1, source_target_pairs={{0,1},{1,0},{2,3},{3,2},{4,5},{5,4},{6,7},{7,6},{8,9},{9,8},{10,11... | collective-permute-start | bytes 1376264 | tf_op jit(solution)/shard_map/ppermute | solution.py:18
  152.7 13.7 %collective-permute-start.44 = (bf16[64,3584]{1,0:T(8,128)(2,1)S(1)}, bf16[64,3584]{1,0:T(8,128)(2,1)S(1)}, u32[]{:S(2)}, u32[]{:S(2)}) collective-permute-start(bf16[64,3584]{1,0:T(8,128)(2,1)S(1)} %get-tuple-element.130), channel_id=1, source_target_pairs={{0,1},{1,0},{2,3},{3,2},{4,5},{5,4},{6,7},{7,6},{8,9},{9,8},{10,11... | collective-permute-start | bytes 1376264 | tf_op jit(solution)/shard_map/ppermute | solution.py:18
  167.9 8.0 %copy-start.1 = (bf16[7168,64]{0,1:T(8,128)(2,1)S(1)}, bf16[7168,64]{0,1:T(8,128)(2,1)}, u32[]{:S(2)}) copy-start(bf16[7168,64]{0,1:T(8,128)(2,1)} %param.10) | copy-start | bytes 2752516

commit v12 on v11

--- a/solution.py
+++ b/solution.py
@@ -323,7 +323,7 @@
     low = after(low, *blocks[1:])
     partner = across(low, 2)
     far[1] = after(far[1], *blocks[1:])
-    later_first = across(far[1], 1)
+    later = spread_direct(far[1])
 
     def far_terms(chunk, at, pieces, *earlier):
         chunk = [after(chunk[0], *earlier)] + chunk[1:] if earlier else chunk
@@ -335,41 +335,39 @@
         pair = add_pieces(kept, [swap(after(term, *earlier), 1) for term in sent], outs)
         return pair[0], [swap(term, 2) for term in pair]
 
-    sent, kept = far_terms(blocks, 0, 2, beside)
-    pair0, sum0 = pair_sum(sent, kept, partner, later_first)
-
-    later = after(far[1], pair0)
-    later = [far[1], later_first, across(later, 2), across(later, 3)]
-    sent, kept = far_terms(blocks, 1, 2, pair0)
-    pair1, sum1 = pair_sum(sent, kept, *later[2:])
+    sent0, kept0 = far_terms(blocks, 0, 2, beside)
+    sent1, kept1 = far_terms(blocks, 1, 2, sent0[0])
+    pair0, sum0 = pair_sum(sent0, kept0, partner, *later[1:], sent1[0])
+    pair1, sum1 = pair_sum(sent1, kept1, *later[1:])
 
     beside = spread_first(after(beside, pair1))
-    sent, kept = far_terms(later, 0, 2, pair1, *sum0)
+    sent, kept = far_terms(later, 0, 2, pair0, pair1)
     pair2, sum2 = pair_sum(sent, kept, *beside[1:])
 
     beside = spread_last(beside, pair2)
     own = after(own, pair2)
     own_first = across(own, 1)
-    acts_low, grads_low = jnp.split(after(low, pair2, *sum1) + partner, 2, axis=1)
+    acts_low, grads_low = jnp.split(after(low, pair2, *sum0) + partner, 2, axis=1)
     example_grad = example_gradients(
         acts_low, grads_low, token_example[0], example_group.shape[0]
     )
     gathered = gather_examples(example_grad, example_group)
-    sent, kept = far_terms(later, 1, 4, example_grad)
-    own = [own, own_first, across(own, 2)]
-    pair3, sum3 = pair_sum(sent, after(kept, own[2]), own_first, *beside, outs=2)
-
-    own = spread_last(own, pair3)
-    beside = [after(beside[0], pair3, *sum2)] + beside[1:]
+    sent, kept = far_terms(later, 1, 2, example_grad)
+    pair3, sum3 = pair_sum(sent, kept, own_first, *beside, outs=2)
+
+    own = [own, own_first, across(after(own, pair3), 2)]
+    beside = [after(beside[0], pair3, *sum1)] + beside[1:]
     near0 = block_terms(beside, down_weight, 0, 2, [rows // 2] * 4)
-    near0 = [swap(after(term, sum3[0]), 1) for term in near0]
-    beside = [after(beside[0], *near0[:1])] + beside[1:]
+    near0 = [swap(after(term, own[2]), 1) for term in near0]
+    own = spread_last(own, *near0[:1])
+    beside = [after(beside[0], *near0[:1], *sum2)] + beside[1:]
     near1 = block_terms(beside, down_weight, 1, 2, [rows // 2] * 4)
+    near1 = [swap(after(term, *own[3:]), 1) for term in near1]
     every = order_examples(after(gathered, near1[0]))
     fisher, group_grad = fisher_and_groups(every, example_grad.shape[1])
-    own = [after(own[0], near1[0])] + own[1:]
-    near1 = [swap(after(term, sum3[1], *own[3:]), 1) for term in near1]
+    near0 = [after(near0[0], near1[0])] + near0[1:]
     adds = [gather_sums(near0, sum0 + sum2)]
+    own = [after(own[0], sum3[0])] + own[1:]
     (result,) = block_terms(own, down_weight, 0, 2, [tokens], adds)
     adds = [gather_sums(near1, sum1)] + sum3
     own = [after(own[0], fisher, group_grad, result)] + own[1:]

time: 176 us -> 182 us (1.034)
  starting transfers between devices: 37.4 us -> 32.4 us
  local copies, waits for them, and re-layouts: 5.95 us -> 10.6 us
  waiting for transfers between devices: 55.5 us -> 58.8 us
  Pallas kernels: 66.9 us -> 69.2 us
    unnamed x26 -> x42, local copies, waits for them, and re-layouts: 2.19 us -> 7.05 us
    ppermute x31 -> x29, waiting for transfers between devices: 18.1 us -> 21.6 us  [swap(): return lax.ppermute(value, 'dp', [(d, d ^ step) for d in range(size)])]
    ppermute x31 -> x29, starting transfers between devices: 16.7 us -> 13.6 us  [swap(): return lax.ppermute(value, 'dp', [(d, d ^ step) for d in range(size)])]
    ppermute x16, starting transfers between devices: 20.7 us -> 18.7 us  [across(): return lax.ppermute(value, 'tensor', pairs)]
  transfers between devices with their start and end apart: 47 -> 45, of which waited for: 24 -> 22; matrix products, arithmetic and copies ran while one was open for 6% -> 5% of each run, Pallas kernels for 32% -> 34%
where the time goes in v12:
time: 182 us; the launch traced here: 181 us
  Pallas kernels  69.2 us (38%)
  waiting for transfers between devices  58.8 us (32%)
  starting transfers between devices  32.4 us (18%)
  local copies, waits for them, and re-layouts  10.6 us (6%)
  matrix products  7.55 us (4%)
    pallas_call x8, Pallas kernels, block_terms(): pl.pallas_call(functools.partial(terms_kernel, size, len(blocks), part *...  58.8 us
    ppermute x16, waiting for transfers between devices, across(): return lax.ppermute(value, 'tensor', pairs)  37.2 us
    ppermute x29, waiting for transfers between devices, swap(): return lax.ppermute(value, 'dp', [(d, d ^ step) for d in range(size)])  21.6 us
    ppermute x16, starting transfers between devices, across(): return lax.ppermute(value, 'tensor', pairs)  18.7 us
    ppermute x29, starting transfers between devices, swap(): return lax.ppermute(value, 'dp', [(d, d ^ step) for d in range(size)])  13.6 us
    pallas_call x4, Pallas kernels, add_pieces(): pl.pallas_call(functools.partial(add_kernel, len(pieces)), out_shape=[jax...  7.28 us
    unnamed x42, local copies, waits for them, and re-layouts  7.05 us
  transfers between devices with their start and end apart: 45, of which 22 were waited for; matrix products, arithmetic and copies ran while one was open for 5% of the time, Pallas kernels for 34%

profile of v12, /device:TPU:0, one launch (start us, length us, event | category | flops | bytes accessed | tf_op | source)
XLA Modules:
  0.0 181.2 jit_solution(7688618212246200230)
XLA Ops:
  0.7 2.1 %constant_dynamic-slice_fusion = (bf16[1,1,512,256]{3,2,1,0:T(8,128)(2,1)S(1)}, bf16[1,1,512,256]{3,2,1,0:T(8,128)(2,1)S(1)}, bf16[1,1,512,256]{3,2,1,0:T(8,128)(2,1)S(1)}, bf16[1,1,512,256]{3,2,1,0:T(8,128)(2,1)}) fusion(bf16[1,4,512,256]{3,2,1,0:T(8,128)(2,1)} %param.8, s32[]{:T(128)S(6)} %select_n.96, s32[]{:T(128)S(6)} %select_n.95, s32[]{:T(128)S(6)} %select_n.94, ...), kind=kLoop, calls=%fused_computation.32 | loop fusion | bytes 2097168 | tf_op jit(solution)/shard_map/dynamic-slice.7
  2.9 0.7 slice_bitcast_fusion
  3.6 2.9 %collective-permute-start.3 = (bf16[128,512]{1,0:T(8,128)(2,1)}, bf16[128,512]{1,0:T(8,128)(2,1)S(1)}, u32[]{:S(2)}, u32[]{:S(2)}) collective-permute-start(bf16[128,512]{1,0:T(8,128)(2,1)} %get-tuple-element.133), channel_id=1, source_target_pairs={{0,2},{1,3},{2,0},{3,1},{4,6},{5,7},{6,4},{7,5},{8,10},{9,11},{10,... | collective-permute-start | bytes 393224 | tf_op jit(solution)/shard_map/ppermute | solution.py:18
  6.8 3.3 %fusion.15 = f32[256,64]{0,1:T(8,128)S(1)} fusion(bf16[256,7168]{1,0:T(8,128)(2,1)} %param.7, bf16[7168,64]{0,1:T(8,128)(2,1)S(1)} %copy-done), kind=kOutput, calls=%fused_computation.38 | convolution fusion | flops 234881024 | bytes 4653056 | tf_op jit(solution)/shard_map/dot_general | solution.py:277
  10.7 1.9 %collective-permute-done.2 = bf16[128,512]{1,0:T(8,128)(2,1)S(1)} collective-permute-done((bf16[128,512]{1,0:T(8,128)(2,1)S(1)}, bf16[128,512]{1,0:T(8,128)(2,1)S(1)}, u32[]{:S(2)}, u32[]{:S(2)}) %collective-permute-start.2) | collective-permute-done | bytes 131104 | tf_op jit(solution)/shard_map/ppermute | solution.py:18
  12.6 3.6 %collective-permute-start.6 = (bf16[256,512]{1,0:T(8,128)(2,1)S(1)}, bf16[256,512]{1,0:T(8,128)(2,1)S(1)}, u32[]{:S(2)}, u32[]{:S(2)}) collective-permute-start(bf16[256,512]{1,0:T(8,128)(2,1)S(1)} %pad_maximum_fusion.1.refs_0_), channel_id=1, source_target_pairs={{0,12},{4,8},{8,4},{12,0},{1,13},{5,9},{9,5},{13,1},{2,14},{6,10},... | collective-permute-start | bytes 786440 | tf_op jit(solution)/shard_map/ppermute | solution.py:28
  16.2 0.9 collective-permute-start.4
  17.1 1.0 collective-permute-start.1
  18.2 5.2 %collective-permute-done.1 = bf16[128,512]{1,0:T(8,128)(2,1)S(1)} collective-permute-done((bf16[128,512]{1,0:T(8,128)(2,1)S(1)}, bf16[128,512]{1,0:T(8,128)(2,1)S(1)}, u32[]{:S(2)}, u32[]{:S(2)}) %collective-permute-start.1) | collective-permute-done | bytes 131104 | tf_op jit(solution)/shard_map/ppermute | solution.py:18
  23.4 1.2 collective-permute-start.8
  25.2 14.0 %collective-permute-done.5.refs_2_ = bf16[256,512]{1,0:T(8,128)(2,1)S(1)} collective-permute-done((bf16[256,512]{1,0:T(8,128)(2,1)S(1)}, bf16[256,512]{1,0:T(8,128)(2,1)S(1)}, u32[]{:S(2)}, u32[]{:S(2)}) %collective-permute-start.5) | collective-permute-done | bytes 262176 | tf_op jit(solution)/shard_map/ppermute | solution.py:28
  39.2 2.5 %collective-permute-start.12 = (bf16[256,512]{1,0:T(8,128)(2,1)S(1)}, bf16[256,512]{1,0:T(8,128)(2,1)S(1)}, u32[]{:S(2)}, u32[]{:S(2)}) collective-permute-start(bf16[256,512]{1,0:T(8,128)(2,1)S(1)} %pad_maximum_fusion.refs_0_), channel_id=1, source_target_pairs={{0,12},{4,8},{8,4},{12,0},{1,13},{5,9},{9,5},{13,1},{2,14},{6,10},... | collective-permute-start | bytes 786440 | tf_op jit(solution)/shard_map/ppermute | solution.py:28
  41.7 1.9 %collective-permute-start.10 = (bf16[256,512]{1,0:T(8,128)(2,1)S(1)}, bf16[256,512]{1,0:T(8,128)(2,1)S(1)}, u32[]{:S(2)}, u32[]{:S(2)}) collective-permute-start(bf16[256,512]{1,0:T(8,128)(2,1)S(1)} %pad_maximum_fusion.refs_0_), channel_id=1, source_target_pairs={{0,4},{4,0},{8,12},{12,8},{1,5},{5,1},{9,13},{13,9},{2,6},{6,2},{1... | collective-permute-start | bytes 786440 | tf_op jit(solution)/shard_map/ppermute | solution.py:28
  43.7 1.1 collective-permute-start.9
  44.7 6.9 %terms.8 = (bf16[64,3584]{1,0:T(8,128)(2,1)S(1)}, bf16[64,3584]{1,0:T(8,128)(2,1)S(1)}, bf16[128,3584]{1,0:T(8,128)(2,1)S(1)}) custom-call(s32[1]{0:T(128)} %bitcast.place_ref, bf16[256,512]{1,0:T(8,128)(2,1)S(1)} %pad_maximum_fusion.1.refs_0_, bf16[256,512]{1,0:T(8,128)(2,1)S(1)} %collective-permute-done.4.refs_1_, ...), custom_call_target="tpu_custom_call" | custom-call | flops 469762048 | bytes 1000 | tf_op jit(solution)/shard_map/terms/pallas_call | solution.py:135
  51.7 6.9 %terms.9 = (bf16[64,3584]{1,0:T(8,128)(2,1)S(1)}, bf16[64,3584]{1,0:T(8,128)(2,1)S(1)}, bf16[128,3584]{1,0:T(8,128)(2,1)S(1)}) custom-call(s32[1]{0:T(128)} %bitcast.place_ref, bf16[256,512]{1,0:T(8,128)(2,1)S(1)} %pad_maximum_fusion.1.refs_0_, bf16[256,512]{1,0:T(8,128)(2,1)S(1)} %collective-permute-done.4.refs_1_, ...), custom_call_target="tpu_custom_call" | custom-call | flops 469762048 | bytes 1000 | tf_op jit(solution)/shard_map/terms/pallas_call | solution.py:135
  58.6 10.2 %collective-permute-done.9 = f32[256,128]{0,1:T(8,128)S(1)} collective-permute-done((f32[256,128]{0,1:T(8,128)S(1)}, f32[256,128]{0,1:T(8,128)S(1)}, u32[]{:S(2)}, u32[]{:S(2)}) %collective-permute-start.9) | collective-permute-done | bytes 131104 | tf_op jit(solution)/shard_map/ppermute | solution.py:28
  69.9 0.8 collective-permute-done.13.refs_0_
  70.7 0.7 collective-permute-done.14.refs_1_
  71.4 1.7 pair.4
  73.1 1.8 collective-permute-start.21
  74.9 1.7 pair.5
  76.6 1.9 %collective-permute-start.17 = (bf16[256,512]{1,0:T(8,128)(2,1)S(1)}, bf16[256,512]{1,0:T(8,128)(2,1)S(1)}, u32[]{:S(2)}, u32[]{:S(2)}) collective-permute-start(bf16[256,512]{1,0:T(8,128)(2,1)S(1)} %collective-permute-done.7.refs_0_), channel_id=1, source_target_pairs={{0,4},{4,0},{8,12},{12,8},{1,5},{5,1},{9,13},{13,9},{2,6},{6,2},{1... | collective-permute-start | bytes 786440 | tf_op jit(solution)/shard_map/ppermute | solution.py:28
  78.6 7.5 %terms.10 = (bf16[64,3584]{1,0:T(8,128)(2,1)}, bf16[64,3584]{1,0:T(8,128)(2,1)}, bf16[128,3584]{1,0:T(8,128)(2,1)S(1)}) custom-call(s32[1]{0:T(128)} %bitcast.place_ref, bf16[256,512]{1,0:T(8,128)(2,1)S(1)} %pad_maximum_fusion.refs_0_, bf16[256,512]{1,0:T(8,128)(2,1)S(1)} %collective-permute-done.10.refs_1_, ...), custom_call_target="tpu_custom_call" | custom-call | flops 469762048 | bytes 1000 | tf_op jit(solution)/shard_map/terms/pallas_call | solution.py:135
  86.1 4.0 %collective-permute-done.18.refs_2_ = bf16[256,512]{1,0:T(8,128)(2,1)S(1)} collective-permute-done((bf16[256,512]{1,0:T(8,128)(2,1)S(1)}, bf16[256,512]{1,0:T(8,128)(2,1)S(1)}, u32[]{:S(2)}, u32[]{:S(2)}) %collective-permute-start.18) | collective-permute-done | bytes 262176 | tf_op jit(solution)/shard_map/ppermute | solution.py:28
  91.5 1.0 collective-permute-done.20.refs_1_
  92.5 0.7 collective-permute-done.19.refs_0_
  93.2 2.3 %pair.6 = bf16[128,3584]{1,0:T(8,128)(2,1)S(1)} custom-call(bf16[128,3584]{1,0:T(8,128)(2,1)S(1)} %get-tuple-element.81.kept_ref, bf16[64,3584]{1,0:T(8,128)(2,1)} %collective-permute-done.19.refs_0_, bf16[64,3584]{1,0:T(8,128)(2,1)} %collective-permute-done.20.refs_1_), custom_call_target="tpu_custom_call" | custom-call | flops 1000 | bytes 1000 | tf_op jit(solution)/shard_map/pair/pallas_call | solution.py:181
  95.5 0.9 copy-done.4
  96.7 0.7 collective-permute-start.23
  97.3 1.3 collective-permute-start.24
  98.6 0.9 add.30
  100.2 7.0 %terms.11 = (bf16[64,3584]{1,0:T(8,128)(2,1)S(1)}, bf16[64,3584]{1,0:T(8,128)(2,1)S(1)}, bf16[128,3584]{1,0:T(8,128)(2,1)S(1)}) custom-call(s32[1]{0:T(128)} %bitcast.place_ref, bf16[256,512]{1,0:T(8,128)(2,1)S(1)} %pad_maximum_fusion.refs_0_, bf16[256,512]{1,0:T(8,128)(2,1)S(1)} %collective-permute-done.10.refs_1_, ...), custom_call_target="tpu_custom_call" | custom-call | flops 469762048 | bytes 1000 | tf_op jit(solution)/shard_map/terms/pallas_call | solution.py:135
  107.2 3.2 %collective-permute-done.24.refs_4_ = bf16[256,512]{1,0:T(8,128)(2,1)S(1)} collective-permute-done((bf16[256,512]{1,0:T(8,128)(2,1)S(1)}, bf16[256,512]{1,0:T(8,128)(2,1)S(1)}, u32[]{:S(2)}, u32[]{:S(2)}) %collective-permute-start.24) | collective-permute-done | bytes 262176 | tf_op jit(solution)/shard_map/ppermute | solution.py:28
  110.9 1.3 collective-permute-done.26.refs_1_
  112.2 0.7 collective-permute-done.25.refs_0_
  112.8 1.6 pair.7
  114.4 1.4 collective-permute-start.32
  116.1 6.9 %terms.12 = (bf16[64,3584]{1,0:T(8,128)(2,1)S(1)}, bf16[64,3584]{1,0:T(8,128)(2,1)S(1)}, bf16[64,3584]{1,0:T(8,128)(2,1)S(1)}, bf16[64,3584]{1,0:T(8,128)(2,1)S(1)}) custom-call(s32[1]{0:T(128)} %bitcast.place_ref, bf16[256,512]{1,0:T(8,128)(2,1)S(1)} %collective-permute-done.7.refs_0_, bf16[256,512]{1,0:T(8,128)(2,1)S(1)} %collective-permute-done.17.refs_1_, ...), custom_call_target="tpu_custom_call" | custom-call | flops 469762048 | bytes 1000 | tf_op jit(solution)/shard_map/terms/pallas_call | solution.py:135
  123.1 0.8 copy-done.14
  123.9 5.4 %collective-permute-done.32.refs_2_ = bf16[256,512]{1,0:T(8,128)(2,1)S(1)} collective-permute-done((bf16[256,512]{1,0:T(8,128)(2,1)S(1)}, bf16[256,512]{1,0:T(8,128)(2,1)S(1)}, u32[]{:S(2)}, u32[]{:S(2)}) %collective-permute-start.32) | collective-permute-done | bytes 262176 | tf_op jit(solution)/shard_map/ppermute | solution.py:28
  129.3 1.8 %collective-permute-done.33.refs_0_ = bf16[64,3584]{1,0:T(8,128)(2,1)S(1)} collective-permute-done((bf16[64,3584]{1,0:T(8,128)(2,1)S(1)}, bf16[64,3584]{1,0:T(8,128)(2,1)S(1)}, u32[]{:S(2)}, u32[]{:S(2)}) %collective-permute-start.33) | collective-permute-done | bytes 458784 | tf_op jit(solution)/shard_map/ppermute | solution.py:18
  131.1 0.8 copy-done.6
  131.9 0.7 collective-permute-start.35
  132.6 1.5 collective-permute-start.36
  134.4 4.3 %collective-permute-done.34.refs_5_ = bf16[128,3584]{1,0:T(8,128)(2,1)S(1)} collective-permute-done((bf16[128,3584]{1,0:T(8,128)(2,1)S(1)}, bf16[128,3584]{1,0:T(8,128)(2,1)S(1)}, u32[]{:S(2)}, u32[]{:S(2)}) %collective-permute-start.34) | collective-permute-done | bytes 917536 | tf_op jit(solution)/shard_map/ppermute | solution.py:18
  138.7 7.8 %terms.13 = (bf16[64,3584]{1,0:T(8,128)(2,1)}, bf16[64,3584]{1,0:T(8,128)(2,1)S(1)}, bf16[64,3584]{1,0:T(8,128)(2,1)S(1)}, bf16[64,3584]{1,0:T(8,128)(2,1)S(1)}) custom-call(s32[1]{0:T(128)} %bitcast.place_ref, bf16[256,512]{1,0:T(8,128)(2,1)S(1)} %collective-permute-done.7.refs_0_, bf16[256,512]{1,0:T(8,128)(2,1)S(1)} %collective-permute-done.17.refs_1_, ...), custom_call_target="tpu_custom_call" | custom-call | flops 469762048 | bytes 1000 | tf_op jit(solution)/shard_map/terms/pallas_call | solution.py:135
  146.5 0.8 copy-done.12
  147.3 0.8 copy-done.13
  148.1 0.8 copy-done.10
  149.4 1.7 collective-permute-start.29
  151.5 0.9 collective-permute-done.30
  152.4 0.5 collective-permute-start.40
  152.9 0.5 collective-permute-done.29
  155.0 0.5 collective-permute-done.39.refs_2_
  155.6 0.5 collective-permute-done.38.refs_1_
  156.2 1.2 copy-done.3
  157.3 1.0 copy-done.7
  158.3 1.6 sums.2.refs_6_
  160.2 7.7 %terms.14.refs_9_ = bf16[256,7168]{1,0:T(8,128)(2,1)} custom-call(s32[1]{0:T(128)} %bitcast.place_ref, bf16[256,512]{1,0:T(8,128)(2,1)S(1)} %bitcast.41, bf16[256,512]{1,0:T(8,128)(2,1)S(1)} %collective-permute-done.22.refs_1_, bf16[256,512]{1,0:T(8,128)(2,1)S(1)} %collective-permute-done.32.refs_2_, bf16[256,512]{1,0:T(8,128)(2,1)S(1)} %collective-permute-done.35.refs_3_, ...), custom_call_target="tpu_custom_call" | custom-call | flops 469762048 | bytes 1000 | tf_op jit(solution)/shard_map/terms/pallas_call | solution.py:135
  168.0 1.5 sums.3.refs_6_
  169.5 2.7 %fusion.4 = f32[1024,1024]{1,0:T(8,128)} fusion(bf16[16,4224]{1,0:T(8,128)(2,1)S(1)} %pad_maximum_fusion.2, s32[]{:T(128)S(6)} %select_n.121, s32[]{:T(128)S(6)} %select_n.122), kind=kOutput, calls=%fused_computation.20 | convolution fusion | flops 33554432 | bytes 4259848 | tf_op jit(solution)/shard_map/dot_general | solution.py:266
  172.2 0.9 fusion.6
  173.1 8.0 %terms.15 = bf16[256,7168]{1,0:T(8,128)(2,1)} custom-call(s32[1]{0:T(128)} %bitcast.place_ref, bf16[256,512]{1,0:T(8,128)(2,1)S(1)} %bitcast.42, bf16[256,512]{1,0:T(8,128)(2,1)S(1)} %collective-permute-done.22.refs_1_, bf16[256,512]{1,0:T(8,128)(2,1)S(1)} %collective-permute-done.32.refs_2_, ...), custom_call_target="tpu_custom_call", output_to_operand_aliasing={{}: (10, {})} | custom-call | flops 469762048 | bytes 1000 | tf_op jit(solution)/shard_map/terms/pallas_call | solution.py:135
  (111 shorter events, 9.1 us)
Async XLA Ops:
  0.6 6.1 %copy-start = (bf16[7168,64]{0,1:T(8,128)(2,1)S(1)}, bf16[7168,64]{0,1:T(8,128)(2,1)}, u32[]{:S(2)}) copy-start(bf16[7168,64]{0,1:T(8,128)(2,1)} %param.10) | copy-start | bytes 2752516
  2.7 7.3 %copy-start.15 = (bf16[1,4,512,256]{3,2,1,0:T(8,128)(2,1)S(1)}, bf16[1,4,512,256]{3,2,1,0:T(8,128)(2,1)}, u32[]{:S(2)}) copy-start(bf16[1,4,512,256]{3,2,1,0:T(8,128)(2,1)} %param.8) | copy-start | bytes 3145732
  2.7 7.3 %copy-start.17 = (bf16[1,4,512,64]{2,3,1,0:T(8,128)(2,1)S(1)}, bf16[1,4,512,64]{2,3,1,0:T(8,128)(2,1)}, u32[]{:S(2)}) copy-start(bf16[1,4,512,64]{2,3,1,0:T(8,128)(2,1)} %param.11) | copy-start | bytes 786436
  3.6 7.2 %collective-permute-start.3 = (bf16[128,512]{1,0:T(8,128)(2,1)}, bf16[128,512]{1,0:T(8,128)(2,1)S(1)}, u32[]{:S(2)}, u32[]{:S(2)}) collective-permute-start(bf16[128,512]{1,0:T(8,128)(2,1)} %get-tuple-element.133), channel_id=1, source_target_pairs={{0,2},{1,3},{2,0},{3,1},{4,6},{5,7},{6,4},{7,5},{8,10},{9,11},{10,... | collective-permute-start | bytes 393224 | tf_op jit(solution)/shard_map/ppermute | solution.py:18
  6.7 5.9 %collective-permute-start.2 = (bf16[128,512]{1,0:T(8,128)(2,1)S(1)}, bf16[128,512]{1,0:T(8,128)(2,1)S(1)}, u32[]{:S(2)}, u32[]{:S(2)}) collective-permute-start(bf16[128,512]{1,0:T(8,128)(2,1)S(1)} %get-tuple-element.131), channel_id=1, source_target_pairs={{0,3},{1,2},{2,1},{3,0},{4,7},{5,6},{6,5},{7,4},{8,11},{9,10},{10,... | collective-permute-start | bytes 393224 | tf_op jit(solution)/shard_map/ppermute | solution.py:18
  12.6 12.6 %collective-permute-start.6 = (bf16[256,512]{1,0:T(8,128)(2,1)S(1)}, bf16[256,512]{1,0:T(8,128)(2,1)S(1)}, u32[]{:S(2)}, u32[]{:S(2)}) collective-permute-start(bf16[256,512]{1,0:T(8,128)(2,1)S(1)} %pad_maximum_fusion.1.refs_0_), channel_id=1, source_target_pairs={{0,12},{4,8},{8,4},{12,0},{1,13},{5,9},{9,5},{13,1},{2,14},{6,10},... | collective-permute-start | bytes 786440 | tf_op jit(solution)/shard_map/ppermute | solution.py:28
  16.2 23.0 %collective-permute-start.5 = (bf16[256,512]{1,0:T(8,128)(2,1)S(1)}, bf16[256,512]{1,0:T(8,128)(2,1)S(1)}, u32[]{:S(2)}, u32[]{:S(2)}) collective-permute-start(bf16[256,512]{1,0:T(8,128)(2,1)S(1)} %pad_maximum_fusion.1.refs_0_), channel_id=1, source_target_pairs={{0,8},{4,12},{8,0},{12,4},{1,9},{5,13},{9,1},{13,5},{2,10},{6,14},... | collective-permute-start | bytes 786440 | tf_op jit(solution)/shard_map/ppermute | solution.py:28
  16.2 23.0 %collective-permute-start.4 = (bf16[256,512]{1,0:T(8,128)(2,1)S(1)}, bf16[256,512]{1,0:T(8,128)(2,1)S(1)}, u32[]{:S(2)}, u32[]{:S(2)}) collective-permute-start(bf16[256,512]{1,0:T(8,128)(2,1)S(1)} %pad_maximum_fusion.1.refs_0_), channel_id=1, source_target_pairs={{0,4},{4,0},{8,12},{12,8},{1,5},{5,1},{9,13},{13,9},{2,6},{6,2},{1... | collective-permute-start | bytes 786440 | tf_op jit(solution)/shard_map/ppermute | solution.py:28
  17.1 6.4 %collective-permute-start.1 = (bf16[128,512]{1,0:T(8,128)(2,1)S(1)}, bf16[128,512]{1,0:T(8,128)(2,1)S(1)}, u32[]{:S(2)}, u32[]{:S(2)}) collective-permute-start(bf16[128,512]{1,0:T(8,128)(2,1)S(1)} %get-tuple-element.134), channel_id=1, source_target_pairs={{0,2},{1,3},{2,0},{3,1},{4,6},{5,7},{6,4},{7,5},{8,10},{9,11},{10,... | collective-permute-start | bytes 393224 | tf_op jit(solution)/shard_map/ppermute | solution.py:18
  18.1 6.7 %collective-permute-start = (bf16[128,512]{1,0:T(8,128)(2,1)S(1)}, bf16[128,512]{1,0:T(8,128)(2,1)S(1)}, u32[]{:S(2)}, u32[]{:S(2)}) collective-permute-start(bf16[128,512]{1,0:T(8,128)(2,1)S(1)} %get-tuple-element.132), channel_id=1, source_target_pairs={{0,3},{1,2},{2,1},{3,0},{4,7},{5,6},{6,5},{7,4},{8,11},{9,10},{10,... | collective-permute-start | bytes 393224 | tf_op jit(solution)/shard_map/ppermute | solution.py:18
  23.4 20.2 %collective-permute-start.8 = (f32[256,128]{0,1:T(8,128)S(1)}, f32[256,128]{0,1:T(8,128)S(1)}, u32[]{:S(2)}, u32[]{:S(2)}) collective-permute-start(f32[256,128]{0,1:T(8,128)S(1)} %pad_maximum_fusion.3), channel_id=1, source_target_pairs={{0,4},{4,0},{8,12},{12,8},{1,5},{5,1},{9,13},{13,9},{2,6},{6,2},{1... | collective-permute-start | bytes 393224 | tf_op jit(solution)/shard_map/ppermute | solution.py:28
  24.8 20.0 %collective-permute-start.7 = (bf16[256,512]{1,0:T(8,128)(2,1)S(1)}, bf16[256,512]{1,0:T(8,128)(2,1)S(1)}, u32[]{:S(2)}, u32[]{:S(2)}) collective-permute-start(bf16[256,512]{1,0:T(8,128)(2,1)S(1)} %bitcast.46), channel_id=1, source_target_pairs={{0,1},{1,0},{2,3},{3,2},{4,5},{5,4},{6,7},{7,6},{8,9},{9,8},{10,11... | collective-permute-start | bytes 786440 | tf_op jit(solution)/shard_map/ppermute | solution.py:18
  39.2 29.6 %collective-permute-start.12 = (bf16[256,512]{1,0:T(8,128)(2,1)S(1)}, bf16[256,512]{1,0:T(8,128)(2,1)S(1)}, u32[]{:S(2)}, u32[]{:S(2)}) collective-permute-start(bf16[256,512]{1,0:T(8,128)(2,1)S(1)} %pad_maximum_fusion.refs_0_), channel_id=1, source_target_pairs={{0,12},{4,8},{8,4},{12,0},{1,13},{5,9},{9,5},{13,1},{2,14},{6,10},... | collective-permute-start | bytes 786440 | tf_op jit(solution)/shard_map/ppermute | solution.py:28
  41.7 27.1 %collective-permute-start.11 = (bf16[256,512]{1,0:T(8,128)(2,1)S(1)}, bf16[256,512]{1,0:T(8,128)(2,1)S(1)}, u32[]{:S(2)}, u32[]{:S(2)}) collective-permute-start(bf16[256,512]{1,0:T(8,128)(2,1)S(1)} %pad_maximum_fusion.refs_0_), channel_id=1, source_target_pairs={{0,8},{4,12},{8,0},{12,4},{1,9},{5,13},{9,1},{13,5},{2,10},{6,14},... | collective-permute-start | bytes 786440 | tf_op jit(solution)/shard_map/ppermute | solution.py:28
  41.7 27.1 %collective-permute-start.10 = (bf16[256,512]{1,0:T(8,128)(2,1)S(1)}, bf16[256,512]{1,0:T(8,128)(2,1)S(1)}, u32[]{:S(2)}, u32[]{:S(2)}) collective-permute-start(bf16[256,512]{1,0:T(8,128)(2,1)S(1)} %pad_maximum_fusion.refs_0_), channel_id=1, source_target_pairs={{0,4},{4,0},{8,12},{12,8},{1,5},{5,1},{9,13},{13,9},{2,6},{6,2},{1... | collective-permute-start | bytes 786440 | tf_op jit(solution)/shard_map/ppermute | solution.py:28
  43.7 25.2 %collective-permute-start.9 = (f32[256,128]{0,1:T(8,128)S(1)}, f32[256,128]{0,1:T(8,128)S(1)}, u32[]{:S(2)}, u32[]{:S(2)}) collective-permute-start(f32[256,128]{0,1:T(8,128)S(1)} %fusion.14), channel_id=1, source_target_pairs={{0,8},{4,12},{8,0},{12,4},{1,9},{5,13},{9,1},{13,5},{2,10},{6,14},... | collective-permute-start | bytes 393224 | tf_op jit(solution)/shard_map/ppermute | solution.py:28
  68.8 6.1 %copy-start.18 = (f32[256,128]{0,1:T(8,128)}, f32[256,128]{0,1:T(8,128)S(1)}, u32[]{:S(2)}) copy-start(f32[256,128]{0,1:T(8,128)S(1)} %collective-permute-done.9) | copy-start | bytes 393220
  68.8 1.9 %collective-permute-start.13 = (bf16[64,3584]{1,0:T(8,128)(2,1)S(1)}, bf16[64,3584]{1,0:T(8,128)(2,1)S(1)}, u32[]{:S(2)}, u32[]{:S(2)}) collective-permute-start(bf16[64,3584]{1,0:T(8,128)(2,1)S(1)} %get-tuple-element.73), channel_id=1, source_target_pairs={{0,1},{1,0},{2,3},{3,2},{4,5},{5,4},{6,7},{7,6},{8,9},{9,8},{10,11... | collective-permute-start | bytes 1376264 | tf_op jit(solution)/shard_map/ppermute | solution.py:18
  68.9 2.5 %collective-permute-start.14 = (bf16[64,3584]{1,0:T(8,128)(2,1)S(1)}, bf16[64,3584]{1,0:T(8,128)(2,1)S(1)}, u32[]{:S(2)}, u32[]{:S(2)}) collective-permute-start(bf16[64,3584]{1,0:T(8,128)(2,1)S(1)} %get-tuple-element.75), channel_id=1, source_target_pairs={{0,1},{1,0},{2,3},{3,2},{4,5},{5,4},{6,7},{7,6},{8,9},{9,8},{10,11... | collective-permute-start | bytes 1376264 | tf_op jit(solution)/shard_map/ppermute | solution.py:18
  69.4 5.5 %collective-permute-start.15 = (bf16[64,3584]{1,0:T(8,128)(2,1)S(1)}, bf16[64,3584]{1,0:T(8,128)(2,1)S(1)}, u32[]{:S(2)}, u32[]{:S(2)}) collective-permute-start(bf16[64,3584]{1,0:T(8,128)(2,1)S(1)} %get-tuple-element.77), channel_id=1, source_target_pairs={{0,1},{1,0},{2,3},{3,2},{4,5},{5,4},{6,7},{7,6},{8,9},{9,8},{10,11... | collective-permute-start | bytes 1376264 | tf_op jit(solution)/shard_map/ppermute | solution.py:18
  69.5 5.4 %collective-permute-start.16 = (bf16[64,3584]{1,0:T(8,128)(2,1)S(1)}, bf16[64,3584]{1,0:T(8,128)(2,1)S(1)}, u32[]{:S(2)}, u32[]{:S(2)}) collective-permute-start(bf16[64,3584]{1,0:T(8,128)(2,1)S(1)} %get-tuple-element.79), channel_id=1, source_target_pairs={{0,1},{1,0},{2,3},{3,2},{4,5},{5,4},{6,7},{7,6},{8,9},{9,8},{10,11... | collective-permute-start | bytes 1376264 | tf_op jit(solution)/shard_map/ppermute | solution.py:18
  73.1 25.6 %collective-permute-start.21 = (bf16[128,3584]{1,0:T(8,128)(2,1)}, bf16[128,3584]{1,0:T(8,128)(2,1)}, u32[]{:S(2)}, u32[]{:S(2)}) collective-permute-start(bf16[128,3584]{1,0:T(8,128)(2,1)} %pair.4), channel_id=1, source_target_pairs={{0,2},{1,3},{2,0},{3,1},{4,6},{5,7},{6,4},{7,5},{8,10},{9,11},{10,... | collective-permute-start | bytes 2752520 | tf_op jit(solution)/shard_map/ppermute | solution.py:18
  76.6 14.3 %copy-start.16 = (bf16[1,1,512,256]{3,2,1,0:T(8,128)(2,1)S(1)}, bf16[1,1,512,256]{3,2,1,0:T(8,128)(2,1)}, u32[]{:S(2)}) copy-start(bf16[1,1,512,256]{3,2,1,0:T(8,128)(2,1)} %get-tuple-element.130) | copy-start | bytes 786436
  76.6 14.4 %copy-start.19 = (s32[1,256]{1,0:T(1,128)S(1)}, s32[1,256]{1,0:T(1,128)}, u32[]{:S(2)}) copy-start(s32[1,256]{1,0:T(1,128)} %param.12) | copy-start | bytes 3076
  76.6 13.4 %collective-permute-start.18 = (bf16[256,512]{1,0:T(8,128)(2,1)S(1)}, bf16[256,512]{1,0:T(8,128)(2,1)S(1)}, u32[]{:S(2)}, u32[]{:S(2)}) collective-permute-start(bf16[256,512]{1,0:T(8,128)(2,1)S(1)} %collective-permute-done.7.refs_0_), channel_id=1, source_target_pairs={{0,8},{4,12},{8,0},{12,4},{1,9},{5,13},{9,1},{13,5},{2,10},{6,14},... | collective-permute-start | bytes 786440 | tf_op jit(solution)/shard_map/ppermute | solution.py:28
  76.6 13.7 %collective-permute-start.17 = (bf16[256,512]{1,0:T(8,128)(2,1)S(1)}, bf16[256,512]{1,0:T(8,128)(2,1)S(1)}, u32[]{:S(2)}, u32[]{:S(2)}) collective-permute-start(bf16[256,512]{1,0:T(8,128)(2,1)S(1)} %collective-permute-done.7.refs_0_), channel_id=1, source_target_pairs={{0,4},{4,0},{8,12},{12,8},{1,5},{5,1},{9,13},{13,9},{2,6},{6,2},{1... | collective-permute-start | bytes 786440 | tf_op jit(solution)/shard_map/ppermute | solution.py:28
  90.4 2.2 %collective-permute-start.20 = (bf16[64,3584]{1,0:T(8,128)(2,1)}, bf16[64,3584]{1,0:T(8,128)(2,1)}, u32[]{:S(2)}, u32[]{:S(2)}) collective-permute-start(bf16[64,3584]{1,0:T(8,128)(2,1)} %get-tuple-element.86), channel_id=1, source_target_pairs={{0,1},{1,0},{2,3},{3,2},{4,5},{5,4},{6,7},{7,6},{8,9},{9,8},{10,11... | collective-permute-start | bytes 1376264 | tf_op jit(solution)/shard_map/ppermute | solution.py:18
  90.4 2.8 %collective-permute-start.19 = (bf16[64,3584]{1,0:T(8,128)(2,1)}, bf16[64,3584]{1,0:T(8,128)(2,1)}, u32[]{:S(2)}, u32[]{:S(2)}) collective-permute-start(bf16[64,3584]{1,0:T(8,128)(2,1)} %get-tuple-element.84), channel_id=1, source_target_pairs={{0,1},{1,0},{2,3},{3,2},{4,5},{5,4},{6,7},{7,6},{8,9},{9,8},{10,11... | collective-permute-start | bytes 1376264 | tf_op jit(solution)/shard_map/ppermute | solution.py:18
  91.2 24.9 %collective-permute-start.31 = (bf16[128,3584]{1,0:T(8,128)(2,1)}, bf16[128,3584]{1,0:T(8,128)(2,1)}, u32[]{:S(2)}, u32[]{:S(2)}) collective-permute-start(bf16[128,3584]{1,0:T(8,128)(2,1)} %pair.5), channel_id=1, source_target_pairs={{0,2},{1,3},{2,0},{3,1},{4,6},{5,7},{6,4},{7,5},{8,10},{9,11},{10,... | collective-permute-start | bytes 2752520 | tf_op jit(solution)/shard_map/ppermute | solution.py:18
  95.5 0.9 copy-start.4
  96.4 10.8 %collective-permute-start.22 = (bf16[256,512]{1,0:T(8,128)(2,1)S(1)}, bf16[256,512]{1,0:T(8,128)(2,1)S(1)}, u32[]{:S(2)}, u32[]{:S(2)}) collective-permute-start(bf16[256,512]{1,0:T(8,128)(2,1)S(1)} %bitcast.38), channel_id=1, source_target_pairs={{0,4},{4,0},{8,12},{12,8},{1,5},{5,1},{9,13},{13,9},{2,6},{6,2},{1... | collective-permute-start | bytes 786440 | tf_op jit(solution)/shard_map/ppermute | solution.py:28
  96.7 10.5 %collective-permute-start.23 = (bf16[256,512]{1,0:T(8,128)(2,1)S(1)}, bf16[256,512]{1,0:T(8,128)(2,1)S(1)}, u32[]{:S(2)}, u32[]{:S(2)}) collective-permute-start(bf16[256,512]{1,0:T(8,128)(2,1)S(1)} %collective-permute-done.7.refs_0_), channel_id=1, source_target_pairs={{4,8},{8,4},{5,9},{9,5},{6,10},{10,6},{7,11},{11,7},{20,24},{24,20... | collective-permute-start | bytes 786440 | tf_op jit(solution)/shard_map/ppermute | solution.py:28
  97.3 13.0 %collective-permute-start.24 = (bf16[256,512]{1,0:T(8,128)(2,1)S(1)}, bf16[256,512]{1,0:T(8,128)(2,1)S(1)}, u32[]{:S(2)}, u32[]{:S(2)}) collective-permute-start(bf16[256,512]{1,0:T(8,128)(2,1)S(1)} %collective-permute-done.18.refs_2_), channel_id=1, source_target_pairs={{4,0},{8,12},{5,1},{9,13},{6,2},{10,14},{7,3},{11,15},{20,16},{24,... | collective-permute-start | bytes 786440 | tf_op jit(solution)/shard_map/ppermute | solution.py:28
  100.2 15.7 %copy-start.5 = (bf16[128,3584]{1,0:T(8,128)(2,1)S(1)}, bf16[128,3584]{1,0:T(8,128)(2,1)}, u32[]{:S(2)}) copy-start(bf16[128,3584]{1,0:T(8,128)(2,1)} %copy-done.4) | copy-start | bytes 2752516
  110.4 1.8 %collective-permute-start.26 = (bf16[64,3584]{1,0:T(8,128)(2,1)S(1)}, bf16[64,3584]{1,0:T(8,128)(2,1)S(1)}, u32[]{:S(2)}, u32[]{:S(2)}) collective-permute-start(bf16[64,3584]{1,0:T(8,128)(2,1)S(1)} %get-tuple-element.96), channel_id=1, source_target_pairs={{0,1},{1,0},{2,3},{3,2},{4,5},{5,4},{6,7},{7,6},{8,9},{9,8},{10,11... | collective-permute-start | bytes 1376264 | tf_op jit(solution)/shard_map/ppermute | solution.py:18
  110.4 2.5 %collective-permute-start.25 = (bf16[64,3584]{1,0:T(8,128)(2,1)S(1)}, bf16[64,3584]{1,0:T(8,128)(2,1)S(1)}, u32[]{:S(2)}, u32[]{:S(2)}) collective-permute-start(bf16[64,3584]{1,0:T(8,128)(2,1)S(1)} %get-tuple-element.94), channel_id=1, source_target_pairs={{0,1},{1,0},{2,3},{3,2},{4,5},{5,4},{6,7},{7,6},{8,9},{9,8},{10,11... | collective-permute-start | bytes 1376264 | tf_op jit(solution)/shard_map/ppermute | solution.py:18
  114.4 1.7 copy-start.8
  114.4 19.6 %copy-start.20 = (s32[4]{0:T(128)S(1)}, s32[4]{0:T(128)}, u32[]{:S(2)}) copy-start(s32[4]{0:T(128)} %param.13) | copy-start | bytes 52
  114.4 14.9 %collective-permute-start.32 = (bf16[256,512]{1,0:T(8,128)(2,1)S(1)}, bf16[256,512]{1,0:T(8,128)(2,1)S(1)}, u32[]{:S(2)}, u32[]{:S(2)}) collective-permute-start(bf16[256,512]{1,0:T(8,128)(2,1)S(1)} %bitcast.39), channel_id=1, source_target_pairs={{0,8},{4,12},{8,0},{12,4},{1,9},{5,13},{9,1},{13,5},{2,10},{6,14},... | collective-permute-start | bytes 786440 | tf_op jit(solution)/shard_map/ppermute | solution.py:28
  115.8 22.9 %collective-permute-start.34 = (bf16[128,3584]{1,0:T(8,128)(2,1)S(1)}, bf16[128,3584]{1,0:T(8,128)(2,1)S(1)}, u32[]{:S(2)}, u32[]{:S(2)}) collective-permute-start(bf16[128,3584]{1,0:T(8,128)(2,1)S(1)} %copy-done.5), channel_id=1, source_target_pairs={{0,2},{1,3},{2,0},{3,1},{4,6},{5,7},{6,4},{7,5},{8,10},{9,11},{10,... | collective-permute-start | bytes 2752520 | tf_op jit(solution)/shard_map/ppermute | solution.py:18
  123.1 0.8 copy-start.14
  123.9 10.2 %copy-start.9 = (bf16[64,3584]{1,0:T(8,128)(2,1)}, bf16[64,3584]{1,0:T(8,128)(2,1)S(1)}, u32[]{:S(2)}) copy-start(bf16[64,3584]{1,0:T(8,128)(2,1)S(1)} %get-tuple-element.114) | copy-start | bytes 1376260
  123.9 10.6 %copy-start.11 = (bf16[64,3584]{1,0:T(8,128)(2,1)}, bf16[64,3584]{1,0:T(8,128)(2,1)S(1)}, u32[]{:S(2)}) copy-start(bf16[64,3584]{1,0:T(8,128)(2,1)S(1)} %get-tuple-element.116) | copy-start | bytes 1376260
  129.3 1.8 %collective-permute-start.33 = (bf16[64,3584]{1,0:T(8,128)(2,1)S(1)}, bf16[64,3584]{1,0:T(8,128)(2,1)S(1)}, u32[]{:S(2)}, u32[]{:S(2)}) collective-permute-start(bf16[64,3584]{1,0:T(8,128)(2,1)S(1)} %get-tuple-element.102), channel_id=1, source_target_pairs={{0,1},{1,0},{2,3},{3,2},{4,5},{5,4},{6,7},{7,6},{8,9},{9,8},{10,11... | collective-permute-start | bytes 1376264 | tf_op jit(solution)/shard_map/ppermute | solution.py:18
  131.9 16.2 %collective-permute-start.35 = (bf16[256,512]{1,0:T(8,128)(2,1)S(1)}, bf16[256,512]{1,0:T(8,128)(2,1)S(1)}, u32[]{:S(2)}, u32[]{:S(2)}) collective-permute-start(bf16[256,512]{1,0:T(8,128)(2,1)S(1)} %bitcast.40), channel_id=1, source_target_pairs={{4,8},{8,4},{5,9},{9,5},{6,10},{10,6},{7,11},{11,7},{20,24},{24,20... | collective-permute-start | bytes 786440 | tf_op jit(solution)/shard_map/ppermute | solution.py:28
  132.6 15.5 %collective-permute-start.36 = (bf16[256,512]{1,0:T(8,128)(2,1)S(1)}, bf16[256,512]{1,0:T(8,128)(2,1)S(1)}, u32[]{:S(2)}, u32[]{:S(2)}) collective-permute-start(bf16[256,512]{1,0:T(8,128)(2,1)S(1)} %collective-permute-done.32.refs_2_), channel_id=1, source_target_pairs={{4,0},{8,12},{5,1},{9,13},{6,2},{10,14},{7,3},{11,15},{20,16},{24,... | collective-permute-start | bytes 786440 | tf_op jit(solution)/shard_map/ppermute | solution.py:28
  134.1 17.1 %collective-permute-start.27 = (bf16[64,3584]{1,0:T(8,128)(2,1)}, bf16[64,3584]{1,0:T(8,128)(2,1)S(1)}, u32[]{:S(2)}, u32[]{:S(2)}) collective-permute-start(bf16[64,3584]{1,0:T(8,128)(2,1)} %get-tuple-element.97), channel_id=1, source_target_pairs={{0,2},{1,3},{2,0},{3,1},{4,6},{5,7},{6,4},{7,5},{8,10},{9,11},{10,... | collective-permute-start | bytes 1376264 | tf_op jit(solution)/shard_map/ppermute | solution.py:18
  138.7 7.8 %copy-start.2 = (bf16[128,3584]{1,0:T(8,128)(2,1)}, bf16[128,3584]{1,0:T(8,128)(2,1)S(1)}, u32[]{:S(2)}) copy-start(bf16[128,3584]{1,0:T(8,128)(2,1)S(1)} %collective-permute-done.34.refs_5_) | copy-start | bytes 2752516
  147.3 0.8 copy-start.13
  148.1 0.8 copy-start.10
  148.9 5.1 %collective-permute-start.37 = (bf16[64,3584]{1,0:T(8,128)(2,1)}, bf16[64,3584]{1,0:T(8,128)(2,1)S(1)}, u32[]{:S(2)}, u32[]{:S(2)}) collective-permute-start(bf16[64,3584]{1,0:T(8,128)(2,1)} %get-tuple-element.107), channel_id=1, source_target_pairs={{0,1},{1,0},{2,3},{3,2},{4,5},{5,4},{6,7},{7,6},{8,9},{9,8},{10,11... | collective-permute-start | bytes 1376264 | tf_op jit(solution)/shard_map/ppermute | solution.py:18
  149.0 3.4 %collective-permute-start.30 = (bf16[4,4224]{1,0:T(4,128)(2,1)S(1)}, bf16[4,4224]{1,0:T(4,128)(2,1)S(1)}, u32[]{:S(2)}, u32[]{:S(2)}) collective-permute-start(bf16[4,4224]{1,0:T(4,128)(2,1)S(1)} %pad_maximum_fusion.4), channel_id=1, source_target_pairs={{0,3},{1,2},{2,1},{3,0},{4,7},{5,6},{6,5},{7,4},{8,11},{9,10},{10,... | collective-permute-start | bytes 101384 | tf_op jit(solution)/shard_map/ppermute | solution.py:18
  149.4 4.0 %collective-permute-start.29 = (bf16[4,4224]{1,0:T(4,128)(2,1)S(1)}, bf16[4,4224]{1,0:T(4,128)(2,1)S(1)}, u32[]{:S(2)}, u32[]{:S(2)}) collective-permute-start(bf16[4,4224]{1,0:T(4,128)(2,1)S(1)} %pad_maximum_fusion.4), channel_id=1, source_target_pairs={{0,2},{1,3},{2,0},{3,1},{4,6},{5,7},{6,4},{7,5},{8,10},{9,11},{10,... | collective-permute-start | bytes 101384 | tf_op jit(solution)/shard_map/ppermute | solution.py:18
  151.2 2.3 %collective-permute-start.28 = (bf16[4,4224]{1,0:T(4,128)(2,1)S(1)}, bf16[4,4224]{1,0:T(4,128)(2,1)S(1)}, u32[]{:S(2)}, u32[]{:S(2)}) collective-permute-start(bf16[4,4224]{1,0:T(4,128)(2,1)S(1)} %pad_maximum_fusion.4), channel_id=1, source_target_pairs={{0,1},{1,0},{2,3},{3,2},{4,5},{5,4},{6,7},{7,6},{8,9},{9,8},{10,11... | collective-permute-start | bytes 101384 | tf_op jit(solution)/shard_map/ppermute | solution.py:18
  151.2 21.9 %collective-permute-start.44 = (bf16[64,3584]{1,0:T(8,128)(2,1)}, bf16[64,3584]{1,0:T(8,128)(2,1)S(1)}, u32[]{:S(2)}, u32[]{:S(2)}) collective-permute-start(bf16[64,3584]{1,0:T(8,128)(2,1)} %copy-done.8), channel_id=1, source_target_pairs={{0,2},{1,3},{2,0},{3,1},{4,6},{5,7},{6,4},{7,5},{8,10},{9,11},{10,... | collective-permute-start | bytes 1376264 | tf_op jit(solution)/shard_map/ppermute | solution.py:18
  152.4 2.2 %collective-permute-start.40 = (bf16[64,3584]{1,0:T(8,128)(2,1)}, bf16[64,3584]{1,0:T(8,128)(2,1)S(1)}, u32[]{:S(2)}, u32[]{:S(2)}) collective-permute-start(bf16[64,3584]{1,0:T(8,128)(2,1)} %copy-done.14), channel_id=1, source_target_pairs={{0,1},{1,0},{2,3},{3,2},{4,5},{5,4},{6,7},{7,6},{8,9},{9,8},{10,11... | collective-permute-start | bytes 1376264 | tf_op jit(solution)/shard_map/ppermute | solution.py:18
  153.5 2.0 %collective-permute-start.39 = (bf16[64,3584]{1,0:T(8,128)(2,1)}, bf16[64,3584]{1,0:T(8,128)(2,1)S(1)}, u32[]{:S(2)}, u32[]{:S(2)}) collective-permute-start(bf16[64,3584]{1,0:T(8,128)(2,1)} %copy-done.11), channel_id=1, source_target_pairs={{0,1},{1,0},{2,3},{3,2},{4,5},{5,4},{6,7},{7,6},{8,9},{9,8},{10,11... | collective-permute-start | bytes 1376264 | tf_op jit(solution)/shard_map/ppermute | solution.py:18
  153.5 2.7 %collective-permute-start.38 = (bf16[64,3584]{1,0:T(8,128)(2,1)}, bf16[64,3584]{1,0:T(8,128)(2,1)S(1)}, u32[]{:S(2)}, u32[]{:S(2)}) collective-permute-start(bf16[64,3584]{1,0:T(8,128)(2,1)} %copy-done.9), channel_id=1, source_target_pairs={{0,1},{1,0},{2,3},{3,2},{4,5},{5,4},{6,7},{7,6},{8,9},{9,8},{10,11... | collective-permute-start | bytes 1376264 | tf_op jit(solution)/shard_map/ppermute | solution.py:18
  154.0 14.0 %collective-permute-start.43 = (bf16[64,3584]{1,0:T(8,128)(2,1)}, bf16[64,3584]{1,0:T(8,128)(2,1)S(1)}, u32[]{:S(2)}, u32[]{:S(2)}) collective-permute-start(bf16[64,3584]{1,0:T(8,128)(2,1)} %copy-done.13), channel_id=1, source_target_pairs={{0,1},{1,0},{2,3},{3,2},{4,5},{5,4},{6,7},{7,6},{8,9},{9,8},{10,11... | collective-permute-start | bytes 1376264 | tf_op jit(solution)/shard_map/ppermute | solution.py:18
  154.6 13.4 %collective-permute-start.42 = (bf16[64,3584]{1,0:T(8,128)(2,1)}, bf16[64,3584]{1,0:T(8,128)(2,1)S(1)}, u32[]{:S(2)}, u32[]{:S(2)}) collective-permute-start(bf16[64,3584]{1,0:T(8,128)(2,1)} %copy-done.12), channel_id=1, source_target_pairs={{0,1},{1,0},{2,3},{3,2},{4,5},{5,4},{6,7},{7,6},{8,9},{9,8},{10,11... | collective-permute-start | bytes 1376264 | tf_op jit(solution)/shard_map/ppermute | solution.py:18
  155.5 12.5 %collective-permute-start.41 = (bf16[64,3584]{1,0:T(8,128)(2,1)}, bf16[64,3584]{1,0:T(8,128)(2,1)S(1)}, u32[]{:S(2)}, u32[]{:S(2)}) collective-permute-start(bf16[64,3584]{1,0:T(8,128)(2,1)} %copy-done.10), channel_id=1, source_target_pairs={{0,1},{1,0},{2,3},{3,2},{4,5},{5,4},{6,7},{7,6},{8,9},{9,8},{10,11... | collective-permute-start | bytes 1376264 | tf_op jit(solution)/shard_map/ppermute | solution.py:18
  156.1 1.2 copy-start.3
  157.3 1.0 copy-start.7
  173.1 8.0 %copy-start.1 = (bf16[7168,64]{0,1:T(8,128)(2,1)S(1)}, bf16[7168,64]{0,1:T(8,128)(2,1)}, u32[]{:S(2)}) copy-start(bf16[7168,64]{0,1:T(8,128)(2,1)} %param.10) | copy-start | bytes 2752516
  (2 other events, 1.6 us)

commit v13 on v12

--- a/solution.py
+++ b/solution.py
@@ -190,30 +190,31 @@
     )(kept, *pieces)
 
 
-def gather_sums_kernel(*refs):
+def gather_sums_kernel(places, *refs):
     quarters, sums, out_ref = refs[:4], refs[4:-1], refs[-1]
     rows = quarters[0].shape[0]
     for index, ref in enumerate(quarters):
-        value = ref[...]
-        if index // 2 < len(sums):
-            at = (index % 2) * rows
-            other = sums[index // 2][at : at + rows]
-            value = (value.astype(f32) + other.astype(f32)).astype(bf16)
-        out_ref[index * rows : (index + 1) * rows] = value
+        value = ref[...].astype(f32)
+        for place, other in zip(places, sums):
+            at = (index - place) * rows
+            if 0 <= at < other.shape[0]:
+                value = value + other[at : at + rows].astype(f32)
+        out_ref[index * rows : (index + 1) * rows] = value.astype(bf16)
 
 
 def gather_sums(quarters, sums):
     rows, cols = quarters[0].shape
     tile = max(n for n in range(128, 2049, 128) if cols % n == 0)
+    places = [sum(value.shape[0] for value in sums[:k]) // rows for k in range(len(sums))]
 
     def spec(tall):
         return pl.BlockSpec((tall, tile), lambda j: (0, j))
 
     return pl.pallas_call(
-        gather_sums_kernel,
+        functools.partial(gather_sums_kernel, places),
         out_shape=jax.ShapeDtypeStruct((4 * rows, cols), bf16),
         grid=(cols // tile,),
-        in_specs=[spec(rows)] * 4 + [spec(2 * rows)] * len(sums),
+        in_specs=[spec(rows)] * 4 + [spec(value.shape[0]) for value in sums],
         out_specs=spec(4 * rows),
         compiler_params=pltpu.CompilerParams(vmem_limit_bytes=24 << 20),
         cost_estimate=pl.CostEstimate(flops=1000, bytes_accessed=1000, transcendentals=0),
@@ -342,32 +343,31 @@
 
     beside = spread_first(after(beside, pair1))
     sent, kept = far_terms(later, 0, 2, pair0, pair1)
-    pair2, sum2 = pair_sum(sent, kept, *beside[1:])
+    pair2, sum2 = pair_sum(sent, kept, *beside[1:], outs=2)
 
     beside = spread_last(beside, pair2)
     own = after(own, pair2)
     own_first = across(own, 1)
+    own = [own, own_first, across(own, 2)]
     acts_low, grads_low = jnp.split(after(low, pair2, *sum0) + partner, 2, axis=1)
     example_grad = example_gradients(
         acts_low, grads_low, token_example[0], example_group.shape[0]
     )
     gathered = gather_examples(example_grad, example_group)
-    sent, kept = far_terms(later, 1, 2, example_grad)
-    pair3, sum3 = pair_sum(sent, kept, own_first, *beside, outs=2)
-
-    own = [own, own_first, across(after(own, pair3), 2)]
+    sent, kept = far_terms(later, 1, 4, example_grad)
+    pair3, sum3 = pair_sum(sent, after(kept, own[2]), own_first, *beside, outs=2)
+
+    own = spread_last(own, pair3)
     beside = [after(beside[0], pair3, *sum1)] + beside[1:]
     near0 = block_terms(beside, down_weight, 0, 2, [rows // 2] * 4)
-    near0 = [swap(after(term, own[2]), 1) for term in near0]
-    own = spread_last(own, *near0[:1])
-    beside = [after(beside[0], *near0[:1], *sum2)] + beside[1:]
+    near0 = [swap(term, 1) for term in near0]
+    beside = [after(beside[0], near0[0], sum2[0])] + beside[1:]
     near1 = block_terms(beside, down_weight, 1, 2, [rows // 2] * 4)
-    near1 = [swap(after(term, *own[3:]), 1) for term in near1]
     every = order_examples(after(gathered, near1[0]))
     fisher, group_grad = fisher_and_groups(every, example_grad.shape[1])
-    near0 = [after(near0[0], near1[0])] + near0[1:]
+    own = [after(own[0], near1[0], sum3[0])] + own[1:]
+    near1 = [swap(after(term, *own[3:]), 1) for term in near1]
     adds = [gather_sums(near0, sum0 + sum2)]
-    own = [after(own[0], sum3[0])] + own[1:]
     (result,) = block_terms(own, down_weight, 0, 2, [tokens], adds)
     adds = [gather_sums(near1, sum1)] + sum3
     own = [after(own[0], fisher, group_grad, result)] + own[1:]

time: 182 us -> 184 us (1.011)
  local copies, waits for them, and re-layouts: 10.6 us -> 16 us
  waiting for transfers between devices: 58.8 us -> 53.5 us
  starting transfers between devices: 32.4 us -> 36.8 us
  Pallas kernels: 69.2 us -> 65 us
    ppermute x16, waiting for transfers between devices: 37.2 us -> 32.1 us  [across(): return lax.ppermute(value, 'tensor', pairs)]
    unnamed x42 -> x46, local copies, waits for them, and re-layouts: 7.05 us -> 11.5 us
    pallas_call x4, Pallas kernels: 7.28 us -> 3.33 us  [add_pieces(): pl.pallas_call(functools.partial(add_kernel, len(pieces)), out_shape=[jax...]
    ppermute x29 -> x32, starting transfers between devices: 13.6 us -> 16.8 us  [swap(): return lax.ppermute(value, 'dp', [(d, d ^ step) for d in range(size)])]
    ppermute x29 -> x32, waiting for transfers between devices: 21.6 us -> 21.4 us  [swap(): return lax.ppermute(value, 'dp', [(d, d ^ step) for d in range(size)])]
  transfers between devices with their start and end apart: 45 -> 48, of which waited for: 22 -> 14; matrix products, arithmetic and copies ran while one was open for 5% -> 6% of each run, Pallas kernels for 34% -> 31%
where the time goes in v13:
time: 184 us; the launch traced here: 182 us
  Pallas kernels  65 us (35%)
  waiting for transfers between devices  53.5 us (29%)
  starting transfers between devices  36.8 us (20%)
  local copies, waits for them, and re-layouts  16 us (9%)
  matrix products  7.55 us (4%)
    pallas_call x8, Pallas kernels, block_terms(): pl.pallas_call(functools.partial(terms_kernel, size, len(blocks), part *...  58.6 us
    ppermute x16, waiting for transfers between devices, across(): return lax.ppermute(value, 'tensor', pairs)  32.1 us
    ppermute x32, waiting for transfers between devices, swap(): return lax.ppermute(value, 'dp', [(d, d ^ step) for d in range(size)])  21.4 us
    ppermute x16, starting transfers between devices, across(): return lax.ppermute(value, 'tensor', pairs)  20 us
    ppermute x32, starting transfers between devices, swap(): return lax.ppermute(value, 'dp', [(d, d ^ step) for d in range(size)])  16.8 us
    unnamed x46, local copies, waits for them, and re-layouts  11.5 us
  transfers between devices with their start and end apart: 48, of which 14 were waited for; matrix products, arithmetic and copies ran while one was open for 6% of the time, Pallas kernels for 31%

profile of v13, /device:TPU:0, one launch (start us, length us, event | category | flops | bytes accessed | tf_op | source)
XLA Modules:
  0.0 181.8 jit_solution(12533928286223245181)
XLA Ops:
  0.7 2.0 %constant_dynamic-slice_fusion = (bf16[1,1,512,256]{3,2,1,0:T(8,128)(2,1)S(1)}, bf16[1,1,512,256]{3,2,1,0:T(8,128)(2,1)S(1)}, bf16[1,1,512,256]{3,2,1,0:T(8,128)(2,1)S(1)}, bf16[1,1,512,256]{3,2,1,0:T(8,128)(2,1)}) fusion(bf16[1,4,512,256]{3,2,1,0:T(8,128)(2,1)} %param.8, s32[]{:T(128)S(6)} %select_n.96, s32[]{:T(128)S(6)} %select_n.95, s32[]{:T(128)S(6)} %select_n.94, ...), kind=kLoop, calls=%fused_computation.32 | loop fusion | bytes 2097168 | tf_op jit(solution)/shard_map/dynamic-slice.7
  2.9 0.7 slice_bitcast_fusion
  3.5 2.9 %collective-permute-start.3 = (bf16[128,512]{1,0:T(8,128)(2,1)}, bf16[128,512]{1,0:T(8,128)(2,1)S(1)}, u32[]{:S(2)}, u32[]{:S(2)}) collective-permute-start(bf16[128,512]{1,0:T(8,128)(2,1)} %get-tuple-element.135), channel_id=1, source_target_pairs={{0,2},{1,3},{2,0},{3,1},{4,6},{5,7},{6,4},{7,5},{8,10},{9,11},{10,... | collective-permute-start | bytes 393224 | tf_op jit(solution)/shard_map/ppermute | solution.py:18
  6.7 3.3 %fusion.15 = f32[256,64]{0,1:T(8,128)S(1)} fusion(bf16[256,7168]{1,0:T(8,128)(2,1)} %param.7, bf16[7168,64]{0,1:T(8,128)(2,1)S(1)} %copy-done), kind=kOutput, calls=%fused_computation.38 | convolution fusion | flops 234881024 | bytes 4653056 | tf_op jit(solution)/shard_map/dot_general | solution.py:278
  10.7 1.9 %collective-permute-done.2 = bf16[128,512]{1,0:T(8,128)(2,1)S(1)} collective-permute-done((bf16[128,512]{1,0:T(8,128)(2,1)S(1)}, bf16[128,512]{1,0:T(8,128)(2,1)S(1)}, u32[]{:S(2)}, u32[]{:S(2)}) %collective-permute-start.2) | collective-permute-done | bytes 131104 | tf_op jit(solution)/shard_map/ppermute | solution.py:18
  12.6 3.6 %collective-permute-start.6 = (bf16[256,512]{1,0:T(8,128)(2,1)S(1)}, bf16[256,512]{1,0:T(8,128)(2,1)S(1)}, u32[]{:S(2)}, u32[]{:S(2)}) collective-permute-start(bf16[256,512]{1,0:T(8,128)(2,1)S(1)} %pad_maximum_fusion.1.refs_0_), channel_id=1, source_target_pairs={{0,12},{4,8},{8,4},{12,0},{1,13},{5,9},{9,5},{13,1},{2,14},{6,10},... | collective-permute-start | bytes 786440 | tf_op jit(solution)/shard_map/ppermute | solution.py:28
  16.2 0.9 collective-permute-start.4
  17.1 1.0 collective-permute-start.1
  18.2 5.2 %collective-permute-done.1 = bf16[128,512]{1,0:T(8,128)(2,1)S(1)} collective-permute-done((bf16[128,512]{1,0:T(8,128)(2,1)S(1)}, bf16[128,512]{1,0:T(8,128)(2,1)S(1)}, u32[]{:S(2)}, u32[]{:S(2)}) %collective-permute-start.1) | collective-permute-done | bytes 131104 | tf_op jit(solution)/shard_map/ppermute | solution.py:18
  23.4 1.2 collective-permute-start.8
  25.2 14.0 %collective-permute-done.5.refs_2_ = bf16[256,512]{1,0:T(8,128)(2,1)S(1)} collective-permute-done((bf16[256,512]{1,0:T(8,128)(2,1)S(1)}, bf16[256,512]{1,0:T(8,128)(2,1)S(1)}, u32[]{:S(2)}, u32[]{:S(2)}) %collective-permute-start.5) | collective-permute-done | bytes 262176 | tf_op jit(solution)/shard_map/ppermute | solution.py:28
  39.2 2.5 %collective-permute-start.12 = (bf16[256,512]{1,0:T(8,128)(2,1)S(1)}, bf16[256,512]{1,0:T(8,128)(2,1)S(1)}, u32[]{:S(2)}, u32[]{:S(2)}) collective-permute-start(bf16[256,512]{1,0:T(8,128)(2,1)S(1)} %pad_maximum_fusion.refs_0_), channel_id=1, source_target_pairs={{0,12},{4,8},{8,4},{12,0},{1,13},{5,9},{9,5},{13,1},{2,14},{6,10},... | collective-permute-start | bytes 786440 | tf_op jit(solution)/shard_map/ppermute | solution.py:28
  41.7 1.9 %collective-permute-start.10 = (bf16[256,512]{1,0:T(8,128)(2,1)S(1)}, bf16[256,512]{1,0:T(8,128)(2,1)S(1)}, u32[]{:S(2)}, u32[]{:S(2)}) collective-permute-start(bf16[256,512]{1,0:T(8,128)(2,1)S(1)} %pad_maximum_fusion.refs_0_), channel_id=1, source_target_pairs={{0,4},{4,0},{8,12},{12,8},{1,5},{5,1},{9,13},{13,9},{2,6},{6,2},{1... | collective-permute-start | bytes 786440 | tf_op jit(solution)/shard_map/ppermute | solution.py:28
  43.7 1.1 collective-permute-start.9
  44.7 6.9 %terms.8 = (bf16[64,3584]{1,0:T(8,128)(2,1)S(1)}, bf16[64,3584]{1,0:T(8,128)(2,1)S(1)}, bf16[128,3584]{1,0:T(8,128)(2,1)S(1)}) custom-call(s32[1]{0:T(128)} %bitcast.place_ref, bf16[256,512]{1,0:T(8,128)(2,1)S(1)} %pad_maximum_fusion.1.refs_0_, bf16[256,512]{1,0:T(8,128)(2,1)S(1)} %collective-permute-done.4.refs_1_, ...), custom_call_target="tpu_custom_call" | custom-call | flops 469762048 | bytes 1000 | tf_op jit(solution)/shard_map/terms/pallas_call | solution.py:135
  51.7 6.9 %terms.9 = (bf16[64,3584]{1,0:T(8,128)(2,1)S(1)}, bf16[64,3584]{1,0:T(8,128)(2,1)S(1)}, bf16[128,3584]{1,0:T(8,128)(2,1)S(1)}) custom-call(s32[1]{0:T(128)} %bitcast.place_ref, bf16[256,512]{1,0:T(8,128)(2,1)S(1)} %pad_maximum_fusion.1.refs_0_, bf16[256,512]{1,0:T(8,128)(2,1)S(1)} %collective-permute-done.4.refs_1_, ...), custom_call_target="tpu_custom_call" | custom-call | flops 469762048 | bytes 1000 | tf_op jit(solution)/shard_map/terms/pallas_call | solution.py:135
  58.6 10.2 %collective-permute-done.9 = f32[256,128]{0,1:T(8,128)S(1)} collective-permute-done((f32[256,128]{0,1:T(8,128)S(1)}, f32[256,128]{0,1:T(8,128)S(1)}, u32[]{:S(2)}, u32[]{:S(2)}) %collective-permute-start.9) | collective-permute-done | bytes 131104 | tf_op jit(solution)/shard_map/ppermute | solution.py:28
  69.9 0.8 collective-permute-done.13.refs_0_
  70.7 0.7 collective-permute-done.14.refs_1_
  71.4 1.7 pair.4
  73.1 1.8 collective-permute-start.21
  75.4 0.9 copy-done.6
  76.4 1.9 %collective-permute-start.17 = (bf16[256,512]{1,0:T(8,128)(2,1)S(1)}, bf16[256,512]{1,0:T(8,128)(2,1)S(1)}, u32[]{:S(2)}, u32[]{:S(2)}) collective-permute-start(bf16[256,512]{1,0:T(8,128)(2,1)S(1)} %collective-permute-done.7.refs_0_), channel_id=1, source_target_pairs={{0,4},{4,0},{8,12},{12,8},{1,5},{5,1},{9,13},{13,9},{2,6},{6,2},{1... | collective-permute-start | bytes 786440 | tf_op jit(solution)/shard_map/ppermute | solution.py:28
  78.3 7.5 %terms.10 = (bf16[64,3584]{1,0:T(8,128)(2,1)}, bf16[64,3584]{1,0:T(8,128)(2,1)}, bf16[128,3584]{1,0:T(8,128)(2,1)S(1)}) custom-call(s32[1]{0:T(128)} %bitcast.place_ref, bf16[256,512]{1,0:T(8,128)(2,1)S(1)} %pad_maximum_fusion.refs_0_, bf16[256,512]{1,0:T(8,128)(2,1)S(1)} %collective-permute-done.10.refs_1_, ...), custom_call_target="tpu_custom_call" | custom-call | flops 469762048 | bytes 1000 | tf_op jit(solution)/shard_map/terms/pallas_call | solution.py:135
  85.8 0.9 copy-done.4
  86.7 3.0 %collective-permute-done.18.refs_2_ = bf16[256,512]{1,0:T(8,128)(2,1)S(1)} collective-permute-done((bf16[256,512]{1,0:T(8,128)(2,1)S(1)}, bf16[256,512]{1,0:T(8,128)(2,1)S(1)}, u32[]{:S(2)}, u32[]{:S(2)}) %collective-permute-start.18) | collective-permute-done | bytes 262176 | tf_op jit(solution)/shard_map/ppermute | solution.py:28
  90.6 1.1 copy.21
  92.2 0.6 collective-permute-done.19.refs_0_
  92.7 1.2 copy-done.5
  94.5 0.8 copy-done.13
  95.2 0.7 copy-done.15
  96.3 2.6 %collective-permute-start.22 = (bf16[256,512]{1,0:T(8,128)(2,1)S(1)}, bf16[256,512]{1,0:T(8,128)(2,1)S(1)}, u32[]{:S(2)}, u32[]{:S(2)}) collective-permute-start(bf16[256,512]{1,0:T(8,128)(2,1)S(1)} %bitcast.39), channel_id=1, source_target_pairs={{0,8},{4,12},{8,0},{12,4},{1,9},{5,13},{9,1},{13,5},{2,10},{6,14},... | collective-permute-start | bytes 786440 | tf_op jit(solution)/shard_map/ppermute | solution.py:28
  98.9 0.7 collective-permute-start.24
  99.6 1.3 collective-permute-start.25
  100.9 0.9 add.30
  102.4 7.6 %terms.11 = (bf16[32,3584]{1,0:T(8,128)(2,1)S(1)}, bf16[32,3584]{1,0:T(8,128)(2,1)}, bf16[32,3584]{1,0:T(8,128)(2,1)}, bf16[32,3584]{1,0:T(8,128)(2,1)}, bf16[128,3584]{1,0:T(8,128)(2,1)S(1)}) custom-call(s32[1]{0:T(128)} %bitcast.place_ref, bf16[256,512]{1,0:T(8,128)(2,1)S(1)} %pad_maximum_fusion.refs_0_, ...), custom_call_target="tpu_custom_call" | custom-call | flops 469762048 | bytes 1000 | tf_op jit(solution)/shard_map/terms/pallas_call | solution.py:135
  110.1 0.9 copy-done.2
  111.0 4.5 %collective-permute-done.25.refs_4_ = bf16[256,512]{1,0:T(8,128)(2,1)S(1)} collective-permute-done((bf16[256,512]{1,0:T(8,128)(2,1)S(1)}, bf16[256,512]{1,0:T(8,128)(2,1)S(1)}, u32[]{:S(2)}, u32[]{:S(2)}) %collective-permute-start.25) | collective-permute-done | bytes 262176 | tf_op jit(solution)/shard_map/ppermute | solution.py:28
  116.6 0.7 collective-permute-done.29.refs_3_
  117.3 0.7 collective-permute-start.32
  118.0 0.7 copy-done.7
  118.7 0.7 copy-done.9
  119.4 0.7 copy-done.11
  120.1 1.2 copy-done.3
  121.3 0.9 copy-done.8
  122.2 0.9 copy-done.10
  123.1 0.9 copy-done.12
  124.6 1.4 collective-permute-start.33
  126.0 0.7 collective-permute-start.37
  126.7 1.5 collective-permute-start.38
  128.1 6.9 %terms.12 = (bf16[64,3584]{1,0:T(8,128)(2,1)S(1)}, bf16[64,3584]{1,0:T(8,128)(2,1)S(1)}, bf16[64,3584]{1,0:T(8,128)(2,1)S(1)}, bf16[64,3584]{1,0:T(8,128)(2,1)S(1)}) custom-call(s32[1]{0:T(128)} %bitcast.place_ref, bf16[256,512]{1,0:T(8,128)(2,1)S(1)} %collective-permute-done.7.refs_0_, bf16[256,512]{1,0:T(8,128)(2,1)S(1)} %collective-permute-done.17.refs_1_, ...), custom_call_target="tpu_custom_call" | custom-call | flops 469762048 | bytes 1000 | tf_op jit(solution)/shard_map/terms/pallas_call | solution.py:135
  135.3 0.9 collective-permute-start.36
  136.2 0.8 collective-permute-done.31.refs_0_
  137.0 0.7 collective-permute-start.35
  137.7 6.9 %terms.13 = (bf16[64,3584]{1,0:T(8,128)(2,1)S(1)}, bf16[64,3584]{1,0:T(8,128)(2,1)S(1)}, bf16[64,3584]{1,0:T(8,128)(2,1)S(1)}, bf16[64,3584]{1,0:T(8,128)(2,1)S(1)}) custom-call(s32[1]{0:T(128)} %bitcast.place_ref, bf16[256,512]{1,0:T(8,128)(2,1)S(1)} %collective-permute-done.7.refs_0_, bf16[256,512]{1,0:T(8,128)(2,1)S(1)} %collective-permute-done.17.refs_1_, ...), custom_call_target="tpu_custom_call" | custom-call | flops 469762048 | bytes 1000 | tf_op jit(solution)/shard_map/terms/pallas_call | solution.py:135
  144.7 1.4 collective-permute-start.42
  146.0 0.7 collective-permute-start.47
  147.7 10.4 %collective-permute-done.42.refs_6_ = bf16[64,3584]{1,0:T(8,128)(2,1)S(1)} collective-permute-done((bf16[64,3584]{1,0:T(8,128)(2,1)S(1)}, bf16[64,3584]{1,0:T(8,128)(2,1)S(1)}, u32[]{:S(2)}, u32[]{:S(2)}) %collective-permute-start.42) | collective-permute-done | bytes 458784 | tf_op jit(solution)/shard_map/ppermute | solution.py:18
  159.1 1.7 sums.2.refs_6_
  160.8 7.7 %terms.14.refs_9_ = bf16[256,7168]{1,0:T(8,128)(2,1)} custom-call(s32[1]{0:T(128)} %bitcast.place_ref, bf16[256,512]{1,0:T(8,128)(2,1)S(1)} %bitcast.41, bf16[256,512]{1,0:T(8,128)(2,1)S(1)} %collective-permute-done.23.refs_1_, bf16[256,512]{1,0:T(8,128)(2,1)S(1)} %collective-permute-done.22.refs_2_, bf16[256,512]{1,0:T(8,128)(2,1)S(1)} %collective-permute-done.37.refs_3_, ...), custom_call_target="tpu_custom_call" | custom-call | flops 469762048 | bytes 1000 | tf_op jit(solution)/shard_map/terms/pallas_call | solution.py:135
  168.5 2.7 %fusion.4 = f32[1024,1024]{1,0:T(8,128)} fusion(bf16[16,4224]{1,0:T(8,128)(2,1)S(1)} %pad_maximum_fusion.2, s32[]{:T(128)S(6)} %select_n.121, s32[]{:T(128)S(6)} %select_n.122), kind=kOutput, calls=%fused_computation.20 | convolution fusion | flops 33554432 | bytes 4259848 | tf_op jit(solution)/shard_map/dot_general | solution.py:267
  171.2 0.9 fusion.6
  172.1 1.5 sums.3.refs_6_
  173.6 8.0 %terms.15 = bf16[256,7168]{1,0:T(8,128)(2,1)} custom-call(s32[1]{0:T(128)} %bitcast.place_ref, bf16[256,512]{1,0:T(8,128)(2,1)S(1)} %bitcast.42, bf16[256,512]{1,0:T(8,128)(2,1)S(1)} %collective-permute-done.23.refs_1_, bf16[256,512]{1,0:T(8,128)(2,1)S(1)} %collective-permute-done.22.refs_2_, ...), custom_call_target="tpu_custom_call", output_to_operand_aliasing={{}: (10, {})} | custom-call | flops 469762048 | bytes 1000 | tf_op jit(solution)/shard_map/terms/pallas_call | solution.py:135
  (121 shorter events, 9.9 us)
Async XLA Ops:
  0.6 6.1 %copy-start = (bf16[7168,64]{0,1:T(8,128)(2,1)S(1)}, bf16[7168,64]{0,1:T(8,128)(2,1)}, u32[]{:S(2)}) copy-start(bf16[7168,64]{0,1:T(8,128)(2,1)} %param.10) | copy-start | bytes 2752516
  2.7 7.3 %copy-start.16 = (bf16[1,4,512,256]{3,2,1,0:T(8,128)(2,1)S(1)}, bf16[1,4,512,256]{3,2,1,0:T(8,128)(2,1)}, u32[]{:S(2)}) copy-start(bf16[1,4,512,256]{3,2,1,0:T(8,128)(2,1)} %param.8) | copy-start | bytes 3145732
  2.7 7.3 %copy-start.19 = (bf16[1,4,512,64]{2,3,1,0:T(8,128)(2,1)S(1)}, bf16[1,4,512,64]{2,3,1,0:T(8,128)(2,1)}, u32[]{:S(2)}) copy-start(bf16[1,4,512,64]{2,3,1,0:T(8,128)(2,1)} %param.11) | copy-start | bytes 786436
  3.5 7.2 %collective-permute-start.3 = (bf16[128,512]{1,0:T(8,128)(2,1)}, bf16[128,512]{1,0:T(8,128)(2,1)S(1)}, u32[]{:S(2)}, u32[]{:S(2)}) collective-permute-start(bf16[128,512]{1,0:T(8,128)(2,1)} %get-tuple-element.135), channel_id=1, source_target_pairs={{0,2},{1,3},{2,0},{3,1},{4,6},{5,7},{6,4},{7,5},{8,10},{9,11},{10,... | collective-permute-start | bytes 393224 | tf_op jit(solution)/shard_map/ppermute | solution.py:18
  6.6 5.9 %collective-permute-start.2 = (bf16[128,512]{1,0:T(8,128)(2,1)S(1)}, bf16[128,512]{1,0:T(8,128)(2,1)S(1)}, u32[]{:S(2)}, u32[]{:S(2)}) collective-permute-start(bf16[128,512]{1,0:T(8,128)(2,1)S(1)} %get-tuple-element.133), channel_id=1, source_target_pairs={{0,3},{1,2},{2,1},{3,0},{4,7},{5,6},{6,5},{7,4},{8,11},{9,10},{10,... | collective-permute-start | bytes 393224 | tf_op jit(solution)/shard_map/ppermute | solution.py:18
  12.6 12.6 %collective-permute-start.6 = (bf16[256,512]{1,0:T(8,128)(2,1)S(1)}, bf16[256,512]{1,0:T(8,128)(2,1)S(1)}, u32[]{:S(2)}, u32[]{:S(2)}) collective-permute-start(bf16[256,512]{1,0:T(8,128)(2,1)S(1)} %pad_maximum_fusion.1.refs_0_), channel_id=1, source_target_pairs={{0,12},{4,8},{8,4},{12,0},{1,13},{5,9},{9,5},{13,1},{2,14},{6,10},... | collective-permute-start | bytes 786440 | tf_op jit(solution)/shard_map/ppermute | solution.py:28
  16.2 23.0 %collective-permute-start.5 = (bf16[256,512]{1,0:T(8,128)(2,1)S(1)}, bf16[256,512]{1,0:T(8,128)(2,1)S(1)}, u32[]{:S(2)}, u32[]{:S(2)}) collective-permute-start(bf16[256,512]{1,0:T(8,128)(2,1)S(1)} %pad_maximum_fusion.1.refs_0_), channel_id=1, source_target_pairs={{0,8},{4,12},{8,0},{12,4},{1,9},{5,13},{9,1},{13,5},{2,10},{6,14},... | collective-permute-start | bytes 786440 | tf_op jit(solution)/shard_map/ppermute | solution.py:28
  16.2 23.0 %collective-permute-start.4 = (bf16[256,512]{1,0:T(8,128)(2,1)S(1)}, bf16[256,512]{1,0:T(8,128)(2,1)S(1)}, u32[]{:S(2)}, u32[]{:S(2)}) collective-permute-start(bf16[256,512]{1,0:T(8,128)(2,1)S(1)} %pad_maximum_fusion.1.refs_0_), channel_id=1, source_target_pairs={{0,4},{4,0},{8,12},{12,8},{1,5},{5,1},{9,13},{13,9},{2,6},{6,2},{1... | collective-permute-start | bytes 786440 | tf_op jit(solution)/shard_map/ppermute | solution.py:28
  17.1 6.4 %collective-permute-start.1 = (bf16[128,512]{1,0:T(8,128)(2,1)S(1)}, bf16[128,512]{1,0:T(8,128)(2,1)S(1)}, u32[]{:S(2)}, u32[]{:S(2)}) collective-permute-start(bf16[128,512]{1,0:T(8,128)(2,1)S(1)} %get-tuple-element.136), channel_id=1, source_target_pairs={{0,2},{1,3},{2,0},{3,1},{4,6},{5,7},{6,4},{7,5},{8,10},{9,11},{10,... | collective-permute-start | bytes 393224 | tf_op jit(solution)/shard_map/ppermute | solution.py:18
  18.1 6.7 %collective-permute-start = (bf16[128,512]{1,0:T(8,128)(2,1)S(1)}, bf16[128,512]{1,0:T(8,128)(2,1)S(1)}, u32[]{:S(2)}, u32[]{:S(2)}) collective-permute-start(bf16[128,512]{1,0:T(8,128)(2,1)S(1)} %get-tuple-element.134), channel_id=1, source_target_pairs={{0,3},{1,2},{2,1},{3,0},{4,7},{5,6},{6,5},{7,4},{8,11},{9,10},{10,... | collective-permute-start | bytes 393224 | tf_op jit(solution)/shard_map/ppermute | solution.py:18
  23.4 20.2 %collective-permute-start.8 = (f32[256,128]{0,1:T(8,128)S(1)}, f32[256,128]{0,1:T(8,128)S(1)}, u32[]{:S(2)}, u32[]{:S(2)}) collective-permute-start(f32[256,128]{0,1:T(8,128)S(1)} %pad_maximum_fusion.3), channel_id=1, source_target_pairs={{0,4},{4,0},{8,12},{12,8},{1,5},{5,1},{9,13},{13,9},{2,6},{6,2},{1... | collective-permute-start | bytes 393224 | tf_op jit(solution)/shard_map/ppermute | solution.py:28
  24.7 20.0 %collective-permute-start.7 = (bf16[256,512]{1,0:T(8,128)(2,1)S(1)}, bf16[256,512]{1,0:T(8,128)(2,1)S(1)}, u32[]{:S(2)}, u32[]{:S(2)}) collective-permute-start(bf16[256,512]{1,0:T(8,128)(2,1)S(1)} %bitcast.46), channel_id=1, source_target_pairs={{0,1},{1,0},{2,3},{3,2},{4,5},{5,4},{6,7},{7,6},{8,9},{9,8},{10,11... | collective-permute-start | bytes 786440 | tf_op jit(solution)/shard_map/ppermute | solution.py:18
  39.2 29.6 %collective-permute-start.12 = (bf16[256,512]{1,0:T(8,128)(2,1)S(1)}, bf16[256,512]{1,0:T(8,128)(2,1)S(1)}, u32[]{:S(2)}, u32[]{:S(2)}) collective-permute-start(bf16[256,512]{1,0:T(8,128)(2,1)S(1)} %pad_maximum_fusion.refs_0_), channel_id=1, source_target_pairs={{0,12},{4,8},{8,4},{12,0},{1,13},{5,9},{9,5},{13,1},{2,14},{6,10},... | collective-permute-start | bytes 786440 | tf_op jit(solution)/shard_map/ppermute | solution.py:28
  41.7 27.1 %collective-permute-start.11 = (bf16[256,512]{1,0:T(8,128)(2,1)S(1)}, bf16[256,512]{1,0:T(8,128)(2,1)S(1)}, u32[]{:S(2)}, u32[]{:S(2)}) collective-permute-start(bf16[256,512]{1,0:T(8,128)(2,1)S(1)} %pad_maximum_fusion.refs_0_), channel_id=1, source_target_pairs={{0,8},{4,12},{8,0},{12,4},{1,9},{5,13},{9,1},{13,5},{2,10},{6,14},... | collective-permute-start | bytes 786440 | tf_op jit(solution)/shard_map/ppermute | solution.py:28
  41.7 27.1 %collective-permute-start.10 = (bf16[256,512]{1,0:T(8,128)(2,1)S(1)}, bf16[256,512]{1,0:T(8,128)(2,1)S(1)}, u32[]{:S(2)}, u32[]{:S(2)}) collective-permute-start(bf16[256,512]{1,0:T(8,128)(2,1)S(1)} %pad_maximum_fusion.refs_0_), channel_id=1, source_target_pairs={{0,4},{4,0},{8,12},{12,8},{1,5},{5,1},{9,13},{13,9},{2,6},{6,2},{1... | collective-permute-start | bytes 786440 | tf_op jit(solution)/shard_map/ppermute | solution.py:28
  43.6 8.0 %copy-start.17 = (f32[256,128]{0,1:T(8,128)}, f32[256,128]{0,1:T(8,128)S(1)}, u32[]{:S(2)}) copy-start(f32[256,128]{0,1:T(8,128)S(1)} %fusion.14) | copy-start | bytes 393220
  43.7 25.1 %collective-permute-start.9 = (f32[256,128]{0,1:T(8,128)S(1)}, f32[256,128]{0,1:T(8,128)S(1)}, u32[]{:S(2)}, u32[]{:S(2)}) collective-permute-start(f32[256,128]{0,1:T(8,128)S(1)} %fusion.14), channel_id=1, source_target_pairs={{0,8},{4,12},{8,0},{12,4},{1,9},{5,13},{9,1},{13,5},{2,10},{6,14},... | collective-permute-start | bytes 393224 | tf_op jit(solution)/shard_map/ppermute | solution.py:28
  68.8 17.0 %copy-start.20 = (f32[256,128]{0,1:T(8,128)}, f32[256,128]{0,1:T(8,128)S(1)}, u32[]{:S(2)}) copy-start(f32[256,128]{0,1:T(8,128)S(1)} %collective-permute-done.9) | copy-start | bytes 393220
  68.8 1.9 %collective-permute-start.13 = (bf16[64,3584]{1,0:T(8,128)(2,1)S(1)}, bf16[64,3584]{1,0:T(8,128)(2,1)S(1)}, u32[]{:S(2)}, u32[]{:S(2)}) collective-permute-start(bf16[64,3584]{1,0:T(8,128)(2,1)S(1)} %get-tuple-element.74), channel_id=1, source_target_pairs={{0,1},{1,0},{2,3},{3,2},{4,5},{5,4},{6,7},{7,6},{8,9},{9,8},{10,11... | collective-permute-start | bytes 1376264 | tf_op jit(solution)/shard_map/ppermute | solution.py:18
  68.9 2.5 %collective-permute-start.14 = (bf16[64,3584]{1,0:T(8,128)(2,1)S(1)}, bf16[64,3584]{1,0:T(8,128)(2,1)S(1)}, u32[]{:S(2)}, u32[]{:S(2)}) collective-permute-start(bf16[64,3584]{1,0:T(8,128)(2,1)S(1)} %get-tuple-element.76), channel_id=1, source_target_pairs={{0,1},{1,0},{2,3},{3,2},{4,5},{5,4},{6,7},{7,6},{8,9},{9,8},{10,11... | collective-permute-start | bytes 1376264 | tf_op jit(solution)/shard_map/ppermute | solution.py:18
  69.4 5.5 %collective-permute-start.15 = (bf16[64,3584]{1,0:T(8,128)(2,1)S(1)}, bf16[64,3584]{1,0:T(8,128)(2,1)S(1)}, u32[]{:S(2)}, u32[]{:S(2)}) collective-permute-start(bf16[64,3584]{1,0:T(8,128)(2,1)S(1)} %get-tuple-element.78), channel_id=1, source_target_pairs={{0,1},{1,0},{2,3},{3,2},{4,5},{5,4},{6,7},{7,6},{8,9},{9,8},{10,11... | collective-permute-start | bytes 1376264 | tf_op jit(solution)/shard_map/ppermute | solution.py:18
  69.5 5.4 %collective-permute-start.16 = (bf16[64,3584]{1,0:T(8,128)(2,1)S(1)}, bf16[64,3584]{1,0:T(8,128)(2,1)S(1)}, u32[]{:S(2)}, u32[]{:S(2)}) collective-permute-start(bf16[64,3584]{1,0:T(8,128)(2,1)S(1)} %get-tuple-element.80), channel_id=1, source_target_pairs={{0,1},{1,0},{2,3},{3,2},{4,5},{5,4},{6,7},{7,6},{8,9},{9,8},{10,11... | collective-permute-start | bytes 1376264 | tf_op jit(solution)/shard_map/ppermute | solution.py:18
  73.1 26.5 %collective-permute-start.21 = (bf16[128,3584]{1,0:T(8,128)(2,1)}, bf16[128,3584]{1,0:T(8,128)(2,1)}, u32[]{:S(2)}, u32[]{:S(2)}) collective-permute-start(bf16[128,3584]{1,0:T(8,128)(2,1)} %pair.4), channel_id=1, source_target_pairs={{0,2},{1,3},{2,0},{3,1},{4,6},{5,7},{6,4},{7,5},{8,10},{9,11},{10,... | collective-permute-start | bytes 2752520 | tf_op jit(solution)/shard_map/ppermute | solution.py:18
  76.4 15.3 %copy-start.21 = (s32[1,256]{1,0:T(1,128)S(1)}, s32[1,256]{1,0:T(1,128)}, u32[]{:S(2)}) copy-start(s32[1,256]{1,0:T(1,128)} %param.12) | copy-start | bytes 3076
  76.4 24.5 %copy-start.18 = (f32[256,128]{0,1:T(8,128)S(1)}, f32[256,128]{0,1:T(8,128)}, u32[]{:S(2)}) copy-start(f32[256,128]{0,1:T(8,128)} %copy-done.17) | copy-start | bytes 393220
  76.4 13.4 %collective-permute-start.18 = (bf16[256,512]{1,0:T(8,128)(2,1)S(1)}, bf16[256,512]{1,0:T(8,128)(2,1)S(1)}, u32[]{:S(2)}, u32[]{:S(2)}) collective-permute-start(bf16[256,512]{1,0:T(8,128)(2,1)S(1)} %collective-permute-done.7.refs_0_), channel_id=1, source_target_pairs={{0,8},{4,12},{8,0},{12,4},{1,9},{5,13},{9,1},{13,5},{2,10},{6,14},... | collective-permute-start | bytes 786440 | tf_op jit(solution)/shard_map/ppermute | solution.py:28
  76.4 13.7 %collective-permute-start.17 = (bf16[256,512]{1,0:T(8,128)(2,1)S(1)}, bf16[256,512]{1,0:T(8,128)(2,1)S(1)}, u32[]{:S(2)}, u32[]{:S(2)}) collective-permute-start(bf16[256,512]{1,0:T(8,128)(2,1)S(1)} %collective-permute-done.7.refs_0_), channel_id=1, source_target_pairs={{0,4},{4,0},{8,12},{12,8},{1,5},{5,1},{9,13},{13,9},{2,6},{6,2},{1... | collective-permute-start | bytes 786440 | tf_op jit(solution)/shard_map/ppermute | solution.py:28
  90.0 2.1 %collective-permute-start.20 = (bf16[64,3584]{1,0:T(8,128)(2,1)}, bf16[64,3584]{1,0:T(8,128)(2,1)S(1)}, u32[]{:S(2)}, u32[]{:S(2)}) collective-permute-start(bf16[64,3584]{1,0:T(8,128)(2,1)} %get-tuple-element.87), channel_id=1, source_target_pairs={{0,1},{1,0},{2,3},{3,2},{4,5},{5,4},{6,7},{7,6},{8,9},{9,8},{10,11... | collective-permute-start | bytes 1376264 | tf_op jit(solution)/shard_map/ppermute | solution.py:18
  90.0 2.7 %collective-permute-start.19 = (bf16[64,3584]{1,0:T(8,128)(2,1)}, bf16[64,3584]{1,0:T(8,128)(2,1)S(1)}, u32[]{:S(2)}, u32[]{:S(2)}) collective-permute-start(bf16[64,3584]{1,0:T(8,128)(2,1)} %get-tuple-element.85), channel_id=1, source_target_pairs={{0,1},{1,0},{2,3},{3,2},{4,5},{5,4},{6,7},{7,6},{8,9},{9,8},{10,11... | collective-permute-start | bytes 1376264 | tf_op jit(solution)/shard_map/ppermute | solution.py:18
  91.8 34.2 %collective-permute-start.30 = (bf16[128,3584]{1,0:T(8,128)(2,1)}, bf16[128,3584]{1,0:T(8,128)(2,1)}, u32[]{:S(2)}, u32[]{:S(2)}) collective-permute-start(bf16[128,3584]{1,0:T(8,128)(2,1)} %copy-done.6), channel_id=1, source_target_pairs={{0,2},{1,3},{2,0},{3,1},{4,6},{5,7},{6,4},{7,5},{8,10},{9,11},{10,... | collective-permute-start | bytes 2752520 | tf_op jit(solution)/shard_map/ppermute | solution.py:18
  92.7 1.2 copy-start.5
  96.0 15.0 %collective-permute-start.23 = (bf16[256,512]{1,0:T(8,128)(2,1)S(1)}, bf16[256,512]{1,0:T(8,128)(2,1)S(1)}, u32[]{:S(2)}, u32[]{:S(2)}) collective-permute-start(bf16[256,512]{1,0:T(8,128)(2,1)S(1)} %bitcast.38), channel_id=1, source_target_pairs={{0,4},{4,0},{8,12},{12,8},{1,5},{5,1},{9,13},{13,9},{2,6},{6,2},{1... | collective-permute-start | bytes 786440 | tf_op jit(solution)/shard_map/ppermute | solution.py:28
  96.3 19.8 %collective-permute-start.22 = (bf16[256,512]{1,0:T(8,128)(2,1)S(1)}, bf16[256,512]{1,0:T(8,128)(2,1)S(1)}, u32[]{:S(2)}, u32[]{:S(2)}) collective-permute-start(bf16[256,512]{1,0:T(8,128)(2,1)S(1)} %bitcast.39), channel_id=1, source_target_pairs={{0,8},{4,12},{8,0},{12,4},{1,9},{5,13},{9,1},{13,5},{2,10},{6,14},... | collective-permute-start | bytes 786440 | tf_op jit(solution)/shard_map/ppermute | solution.py:28
  98.9 12.1 %collective-permute-start.24 = (bf16[256,512]{1,0:T(8,128)(2,1)S(1)}, bf16[256,512]{1,0:T(8,128)(2,1)S(1)}, u32[]{:S(2)}, u32[]{:S(2)}) collective-permute-start(bf16[256,512]{1,0:T(8,128)(2,1)S(1)} %collective-permute-done.7.refs_0_), channel_id=1, source_target_pairs={{4,8},{8,4},{5,9},{9,5},{6,10},{10,6},{7,11},{11,7},{20,24},{24,20... | collective-permute-start | bytes 786440 | tf_op jit(solution)/shard_map/ppermute | solution.py:28
  99.6 16.0 %collective-permute-start.25 = (bf16[256,512]{1,0:T(8,128)(2,1)S(1)}, bf16[256,512]{1,0:T(8,128)(2,1)S(1)}, u32[]{:S(2)}, u32[]{:S(2)}) collective-permute-start(bf16[256,512]{1,0:T(8,128)(2,1)S(1)} %collective-permute-done.18.refs_2_), channel_id=1, source_target_pairs={{4,0},{8,12},{5,1},{9,13},{6,2},{10,14},{7,3},{11,15},{20,16},{24,... | collective-permute-start | bytes 786440 | tf_op jit(solution)/shard_map/ppermute | solution.py:28
  102.4 14.2 %copy-start.22 = (s32[4]{0:T(128)S(1)}, s32[4]{0:T(128)}, u32[]{:S(2)}) copy-start(s32[4]{0:T(128)} %param.13) | copy-start | bytes 52
  110.1 0.9 copy-start.2
  115.6 1.7 collective-permute-start.29
  115.6 2.4 %collective-permute-start.28 = (bf16[32,3584]{1,0:T(8,128)(2,1)}, bf16[32,3584]{1,0:T(8,128)(2,1)S(1)}, u32[]{:S(2)}, u32[]{:S(2)}) collective-permute-start(bf16[32,3584]{1,0:T(8,128)(2,1)} %get-tuple-element.101), channel_id=1, source_target_pairs={{0,1},{1,0},{2,3},{3,2},{4,5},{5,4},{6,7},{7,6},{8,9},{9,8},{10,11... | collective-permute-start | bytes 688136 | tf_op jit(solution)/shard_map/ppermute | solution.py:18
  116.1 2.6 %collective-permute-start.27 = (bf16[32,3584]{1,0:T(8,128)(2,1)}, bf16[32,3584]{1,0:T(8,128)(2,1)S(1)}, u32[]{:S(2)}, u32[]{:S(2)}) collective-permute-start(bf16[32,3584]{1,0:T(8,128)(2,1)} %get-tuple-element.99), channel_id=1, source_target_pairs={{0,1},{1,0},{2,3},{3,2},{4,5},{5,4},{6,7},{7,6},{8,9},{9,8},{10,11... | collective-permute-start | bytes 688136 | tf_op jit(solution)/shard_map/ppermute | solution.py:18
  116.1 3.3 %collective-permute-start.26 = (bf16[32,3584]{1,0:T(8,128)(2,1)S(1)}, bf16[32,3584]{1,0:T(8,128)(2,1)S(1)}, u32[]{:S(2)}, u32[]{:S(2)}) collective-permute-start(bf16[32,3584]{1,0:T(8,128)(2,1)S(1)} %get-tuple-element.97), channel_id=1, source_target_pairs={{0,1},{1,0},{2,3},{3,2},{4,5},{5,4},{6,7},{7,6},{8,9},{9,8},{10,11... | collective-permute-start | bytes 688136 | tf_op jit(solution)/shard_map/ppermute | solution.py:18
  117.3 18.0 %collective-permute-start.32 = (bf16[64,3584]{1,0:T(8,128)(2,1)}, bf16[64,3584]{1,0:T(8,128)(2,1)S(1)}, u32[]{:S(2)}, u32[]{:S(2)}) collective-permute-start(bf16[64,3584]{1,0:T(8,128)(2,1)} %copy-done.15), channel_id=1, source_target_pairs={{0,2},{1,3},{2,0},{3,1},{4,6},{5,7},{6,4},{7,5},{8,10},{9,11},{10,... | collective-permute-start | bytes 1376264 | tf_op jit(solution)/shard_map/ppermute | solution.py:18
  120.1 1.2 copy-start.3
  121.3 0.9 copy-start.8
  122.2 0.9 copy-start.10
  123.1 0.9 copy-start.12
  124.6 22.7 %collective-permute-start.33 = (bf16[64,3584]{1,0:T(8,128)(2,1)S(1)}, bf16[64,3584]{1,0:T(8,128)(2,1)S(1)}, u32[]{:S(2)}, u32[]{:S(2)}) collective-permute-start(bf16[64,3584]{1,0:T(8,128)(2,1)S(1)} %get-tuple-element.104), channel_id=1, source_target_pairs={{0,2},{1,3},{2,0},{3,1},{4,6},{5,7},{6,4},{7,5},{8,10},{9,11},{10,... | collective-permute-start | bytes 1376264 | tf_op jit(solution)/shard_map/ppermute | solution.py:18
  126.0 11.7 %collective-permute-start.37 = (bf16[256,512]{1,0:T(8,128)(2,1)S(1)}, bf16[256,512]{1,0:T(8,128)(2,1)S(1)}, u32[]{:S(2)}, u32[]{:S(2)}) collective-permute-start(bf16[256,512]{1,0:T(8,128)(2,1)S(1)} %bitcast.40), channel_id=1, source_target_pairs={{4,8},{8,4},{5,9},{9,5},{6,10},{10,6},{7,11},{11,7},{20,24},{24,20... | collective-permute-start | bytes 786440 | tf_op jit(solution)/shard_map/ppermute | solution.py:28
  126.7 18.0 %collective-permute-start.38 = (bf16[256,512]{1,0:T(8,128)(2,1)S(1)}, bf16[256,512]{1,0:T(8,128)(2,1)S(1)}, u32[]{:S(2)}, u32[]{:S(2)}) collective-permute-start(bf16[256,512]{1,0:T(8,128)(2,1)S(1)} %collective-permute-done.22.refs_2_), channel_id=1, source_target_pairs={{4,0},{8,12},{5,1},{9,13},{6,2},{10,14},{7,3},{11,15},{20,16},{24,... | collective-permute-start | bytes 786440 | tf_op jit(solution)/shard_map/ppermute | solution.py:28
  135.1 1.9 %collective-permute-start.31 = (bf16[64,3584]{1,0:T(8,128)(2,1)S(1)}, bf16[64,3584]{1,0:T(8,128)(2,1)S(1)}, u32[]{:S(2)}, u32[]{:S(2)}) collective-permute-start(bf16[64,3584]{1,0:T(8,128)(2,1)S(1)} %get-tuple-element.106), channel_id=1, source_target_pairs={{0,1},{1,0},{2,3},{3,2},{4,5},{5,4},{6,7},{7,6},{8,9},{9,8},{10,11... | collective-permute-start | bytes 1376264 | tf_op jit(solution)/shard_map/ppermute | solution.py:18
  135.3 9.4 %copy-start.14 = (bf16[64,3584]{1,0:T(8,128)(2,1)S(1)}, bf16[64,3584]{1,0:T(8,128)(2,1)}, u32[]{:S(2)}) copy-start(bf16[64,3584]{1,0:T(8,128)(2,1)} %copy-done.13) | copy-start | bytes 1376260
  135.3 10.7 %collective-permute-start.36 = (bf16[4,4224]{1,0:T(4,128)(2,1)S(1)}, bf16[4,4224]{1,0:T(4,128)(2,1)S(1)}, u32[]{:S(2)}, u32[]{:S(2)}) collective-permute-start(bf16[4,4224]{1,0:T(4,128)(2,1)S(1)} %pad_maximum_fusion.4), channel_id=1, source_target_pairs={{0,3},{1,2},{2,1},{3,0},{4,7},{5,6},{6,5},{7,4},{8,11},{9,10},{10,... | collective-permute-start | bytes 101384 | tf_op jit(solution)/shard_map/ppermute | solution.py:18
  137.0 9.8 %collective-permute-start.35 = (bf16[4,4224]{1,0:T(4,128)(2,1)S(1)}, bf16[4,4224]{1,0:T(4,128)(2,1)S(1)}, u32[]{:S(2)}, u32[]{:S(2)}) collective-permute-start(bf16[4,4224]{1,0:T(4,128)(2,1)S(1)} %pad_maximum_fusion.4), channel_id=1, source_target_pairs={{0,2},{1,3},{2,0},{3,1},{4,6},{5,7},{6,4},{7,5},{8,10},{9,11},{10,... | collective-permute-start | bytes 101384 | tf_op jit(solution)/shard_map/ppermute | solution.py:18
  137.7 9.1 %collective-permute-start.34 = (bf16[4,4224]{1,0:T(4,128)(2,1)S(1)}, bf16[4,4224]{1,0:T(4,128)(2,1)S(1)}, u32[]{:S(2)}, u32[]{:S(2)}) collective-permute-start(bf16[4,4224]{1,0:T(4,128)(2,1)S(1)} %pad_maximum_fusion.4), channel_id=1, source_target_pairs={{0,1},{1,0},{2,3},{3,2},{4,5},{5,4},{6,7},{7,6},{8,9},{9,8},{10,11... | collective-permute-start | bytes 101384 | tf_op jit(solution)/shard_map/ppermute | solution.py:18
  144.7 13.4 %collective-permute-start.42 = (bf16[64,3584]{1,0:T(8,128)(2,1)S(1)}, bf16[64,3584]{1,0:T(8,128)(2,1)S(1)}, u32[]{:S(2)}, u32[]{:S(2)}) collective-permute-start(bf16[64,3584]{1,0:T(8,128)(2,1)S(1)} %copy-done.14), channel_id=1, source_target_pairs={{0,2},{1,3},{2,0},{3,1},{4,6},{5,7},{6,4},{7,5},{8,10},{9,11},{10,... | collective-permute-start | bytes 1376264 | tf_op jit(solution)/shard_map/ppermute | solution.py:18
  146.0 27.6 %collective-permute-start.47 = (bf16[64,3584]{1,0:T(8,128)(2,1)S(1)}, bf16[64,3584]{1,0:T(8,128)(2,1)S(1)}, u32[]{:S(2)}, u32[]{:S(2)}) collective-permute-start(bf16[64,3584]{1,0:T(8,128)(2,1)S(1)} %get-tuple-element.128), channel_id=1, source_target_pairs={{0,2},{1,3},{2,0},{3,1},{4,6},{5,7},{6,4},{7,5},{8,10},{9,11},{10,... | collective-permute-start | bytes 1376264 | tf_op jit(solution)/shard_map/ppermute | solution.py:18
  146.8 11.3 %collective-permute-start.39 = (bf16[64,3584]{1,0:T(8,128)(2,1)S(1)}, bf16[64,3584]{1,0:T(8,128)(2,1)S(1)}, u32[]{:S(2)}, u32[]{:S(2)}) collective-permute-start(bf16[64,3584]{1,0:T(8,128)(2,1)S(1)} %get-tuple-element.116), channel_id=1, source_target_pairs={{0,1},{1,0},{2,3},{3,2},{4,5},{5,4},{6,7},{7,6},{8,9},{9,8},{10,11... | collective-permute-start | bytes 1376264 | tf_op jit(solution)/shard_map/ppermute | solution.py:18
  146.8 11.8 %collective-permute-start.40 = (bf16[64,3584]{1,0:T(8,128)(2,1)S(1)}, bf16[64,3584]{1,0:T(8,128)(2,1)S(1)}, u32[]{:S(2)}, u32[]{:S(2)}) collective-permute-start(bf16[64,3584]{1,0:T(8,128)(2,1)S(1)} %get-tuple-element.117), channel_id=1, source_target_pairs={{0,1},{1,0},{2,3},{3,2},{4,5},{5,4},{6,7},{7,6},{8,9},{9,8},{10,11... | collective-permute-start | bytes 1376264 | tf_op jit(solution)/shard_map/ppermute | solution.py:18
  147.3 11.4 %collective-permute-start.41 = (bf16[64,3584]{1,0:T(8,128)(2,1)S(1)}, bf16[64,3584]{1,0:T(8,128)(2,1)S(1)}, u32[]{:S(2)}, u32[]{:S(2)}) collective-permute-start(bf16[64,3584]{1,0:T(8,128)(2,1)S(1)} %get-tuple-element.118), channel_id=1, source_target_pairs={{0,1},{1,0},{2,3},{3,2},{4,5},{5,4},{6,7},{7,6},{8,9},{9,8},{10,11... | collective-permute-start | bytes 1376264 | tf_op jit(solution)/shard_map/ppermute | solution.py:18
  158.1 14.0 %collective-permute-start.43 = (bf16[64,3584]{1,0:T(8,128)(2,1)S(1)}, bf16[64,3584]{1,0:T(8,128)(2,1)S(1)}, u32[]{:S(2)}, u32[]{:S(2)}) collective-permute-start(bf16[64,3584]{1,0:T(8,128)(2,1)S(1)} %get-tuple-element.121), channel_id=1, source_target_pairs={{0,1},{1,0},{2,3},{3,2},{4,5},{5,4},{6,7},{7,6},{8,9},{9,8},{10,11... | collective-permute-start | bytes 1376264 | tf_op jit(solution)/shard_map/ppermute | solution.py:18
  158.1 14.0 %collective-permute-start.46 = (bf16[64,3584]{1,0:T(8,128)(2,1)S(1)}, bf16[64,3584]{1,0:T(8,128)(2,1)S(1)}, u32[]{:S(2)}, u32[]{:S(2)}) collective-permute-start(bf16[64,3584]{1,0:T(8,128)(2,1)S(1)} %get-tuple-element.127), channel_id=1, source_target_pairs={{0,1},{1,0},{2,3},{3,2},{4,5},{5,4},{6,7},{7,6},{8,9},{9,8},{10,11... | collective-permute-start | bytes 1376264 | tf_op jit(solution)/shard_map/ppermute | solution.py:18
  158.6 13.5 %collective-permute-start.45 = (bf16[64,3584]{1,0:T(8,128)(2,1)S(1)}, bf16[64,3584]{1,0:T(8,128)(2,1)S(1)}, u32[]{:S(2)}, u32[]{:S(2)}) collective-permute-start(bf16[64,3584]{1,0:T(8,128)(2,1)S(1)} %get-tuple-element.125), channel_id=1, source_target_pairs={{0,1},{1,0},{2,3},{3,2},{4,5},{5,4},{6,7},{7,6},{8,9},{9,8},{10,11... | collective-permute-start | bytes 1376264 | tf_op jit(solution)/shard_map/ppermute | solution.py:18
  158.6 13.5 %collective-permute-start.44 = (bf16[64,3584]{1,0:T(8,128)(2,1)S(1)}, bf16[64,3584]{1,0:T(8,128)(2,1)S(1)}, u32[]{:S(2)}, u32[]{:S(2)}) collective-permute-start(bf16[64,3584]{1,0:T(8,128)(2,1)S(1)} %get-tuple-element.123), channel_id=1, source_target_pairs={{0,1},{1,0},{2,3},{3,2},{4,5},{5,4},{6,7},{7,6},{8,9},{9,8},{10,11... | collective-permute-start | bytes 1376264 | tf_op jit(solution)/shard_map/ppermute | solution.py:18
  173.6 8.0 %copy-start.1 = (bf16[7168,64]{0,1:T(8,128)(2,1)S(1)}, bf16[7168,64]{0,1:T(8,128)(2,1)}, u32[]{:S(2)}) copy-start(bf16[7168,64]{0,1:T(8,128)(2,1)} %param.10) | copy-start | bytes 2752516
  (7 other events, 5.4 us)

commit v14 on v13

--- a/solution.py
+++ b/solution.py
@@ -346,32 +346,31 @@
     pair2, sum2 = pair_sum(sent, kept, *beside[1:], outs=2)
 
     beside = spread_last(beside, pair2)
-    own = after(own, pair2)
-    own_first = across(own, 1)
-    own = [own, own_first, across(own, 2)]
+    own = spread_first(after(own, pair2))
     acts_low, grads_low = jnp.split(after(low, pair2, *sum0) + partner, 2, axis=1)
     example_grad = example_gradients(
         acts_low, grads_low, token_example[0], example_group.shape[0]
     )
     gathered = gather_examples(example_grad, example_group)
-    sent, kept = far_terms(later, 1, 4, example_grad)
-    pair3, sum3 = pair_sum(sent, after(kept, own[2]), own_first, *beside, outs=2)
+    sent, kept = far_terms(later, 1, 2, example_grad)
+    pair3, sum3 = pair_sum(sent, kept, *own, *beside, outs=2)
 
     own = spread_last(own, pair3)
     beside = [after(beside[0], pair3, *sum1)] + beside[1:]
     near0 = block_terms(beside, down_weight, 0, 2, [rows // 2] * 4)
-    near0 = [swap(term, 1) for term in near0]
-    beside = [after(beside[0], near0[0], sum2[0])] + beside[1:]
+    near0 = [swap(after(term, sum2[0], *own[3:]), 1) for term in near0]
+    adds0 = gather_sums(near0, sum0 + sum2)
+    every = order_examples(after(gathered, near0[0]))
+    fisher, group_grad = fisher_and_groups(every, example_grad.shape[1])
+    beside = [after(beside[0], near0[0], fisher, group_grad)] + beside[1:]
     near1 = block_terms(beside, down_weight, 1, 2, [rows // 2] * 4)
-    every = order_examples(after(gathered, near1[0]))
-    fisher, group_grad = fisher_and_groups(every, example_grad.shape[1])
-    own = [after(own[0], near1[0], sum3[0])] + own[1:]
-    near1 = [swap(after(term, *own[3:]), 1) for term in near1]
-    adds = [gather_sums(near0, sum0 + sum2)]
-    (result,) = block_terms(own, down_weight, 0, 2, [tokens], adds)
-    adds = [gather_sums(near1, sum1)] + sum3
-    own = [after(own[0], fisher, group_grad, result)] + own[1:]
-    (result,) = block_terms(own, down_weight, 1, 2, [tokens], adds, result)
+
+    near1 = [swap(after(term, sum3[0]), 1) for term in near1]
+    adds1 = gather_sums(near1, sum1)
+    own = [after(own[0], adds1)] + own[1:]
+    (result,) = block_terms(own, down_weight, 0, 2, [tokens], [adds0])
+    own = [after(own[0], result)] + own[1:]
+    (result,) = block_terms(own, down_weight, 1, 2, [tokens], [adds1] + sum3, result)
     return (result, fisher, group_grad)
 
 

time: 184 us -> 182 us (0.989)
  local copies, waits for them, and re-layouts: 16 us -> 11.3 us
  waiting for transfers between devices: 53.5 us -> 56.9 us
  starting transfers between devices: 36.8 us -> 34.5 us
    unnamed x46 -> x40, local copies, waits for them, and re-layouts: 11.5 us -> 8.53 us
    ppermute x32 -> x30, waiting for transfers between devices: 21.4 us -> 23.7 us  [swap(): return lax.ppermute(value, 'dp', [(d, d ^ step) for d in range(size)])]
    ppermute x32 -> x30, starting transfers between devices: 16.8 us -> 14.6 us  [swap(): return lax.ppermute(value, 'dp', [(d, d ^ step) for d in range(size)])]
  transfers between devices with their start and end apart: 48 -> 46, of which waited for: 14 -> 21; matrix products, arithmetic and copies ran while one was open for 6% -> 6% of each run, Pallas kernels for 31% -> 32%
where the time goes in v14:
time: 182 us; the launch traced here: 181 us
  Pallas kernels  66.6 us (37%)
  waiting for transfers between devices  56.9 us (31%)
  starting transfers between devices  34.5 us (19%)
  local copies, waits for them, and re-layouts  11.3 us (6%)
  matrix products  7.56 us (4%)
  other arithmetic  3.07 us (2%)
    pallas_call x8, Pallas kernels, block_terms(): pl.pallas_call(functools.partial(terms_kernel, size, len(blocks), part *...  58.5 us
    ppermute x16, waiting for transfers between devices, across(): return lax.ppermute(value, 'tensor', pairs)  33.2 us
    ppermute x30, waiting for transfers between devices, swap(): return lax.ppermute(value, 'dp', [(d, d ^ step) for d in range(size)])  23.7 us
    ppermute x16, starting transfers between devices, across(): return lax.ppermute(value, 'tensor', pairs)  19.9 us
    ppermute x30, starting transfers between devices, swap(): return lax.ppermute(value, 'dp', [(d, d ^ step) for d in range(size)])  14.6 us
    unnamed x40, local copies, waits for them, and re-layouts  8.53 us
    pallas_call x4, Pallas kernels, add_pieces(): pl.pallas_call(functools.partial(add_kernel, len(pieces)), out_shape=[jax...  4.91 us
  transfers between devices with their start and end apart: 46, of which 21 were waited for; matrix products, arithmetic and copies ran while one was open for 6% of the time, Pallas kernels for 32%

profile of v14, /device:TPU:0, one launch (start us, length us, event | category | flops | bytes accessed | tf_op | source)
XLA Modules:
  0.0 181.4 jit_solution(6277385656878597525)
XLA Ops:
  0.7 1.3 constant_dynamic-slice_fusion
  2.2 0.7 slice_bitcast_fusion
  2.9 2.9 %collective-permute-start.3 = (bf16[128,512]{1,0:T(8,128)(2,1)}, bf16[128,512]{1,0:T(8,128)(2,1)S(1)}, u32[]{:S(2)}, u32[]{:S(2)}) collective-permute-start(bf16[128,512]{1,0:T(8,128)(2,1)} %get-tuple-element.133), channel_id=1, source_target_pairs={{0,2},{1,3},{2,0},{3,1},{4,6},{5,7},{6,4},{7,5},{8,10},{9,11},{10,... | collective-permute-start | bytes 393224 | tf_op jit(solution)/shard_map/ppermute | solution.py:18
  6.1 3.3 %fusion.15 = f32[256,64]{0,1:T(8,128)S(1)} fusion(bf16[256,7168]{1,0:T(8,128)(2,1)} %param.7, bf16[7168,64]{0,1:T(8,128)(2,1)S(1)} %copy-done), kind=kOutput, calls=%fused_computation.38 | convolution fusion | flops 234881024 | bytes 4653056 | tf_op jit(solution)/shard_map/dot_general | solution.py:278
  10.1 1.9 %collective-permute-done.2 = bf16[128,512]{1,0:T(8,128)(2,1)S(1)} collective-permute-done((bf16[128,512]{1,0:T(8,128)(2,1)S(1)}, bf16[128,512]{1,0:T(8,128)(2,1)S(1)}, u32[]{:S(2)}, u32[]{:S(2)}) %collective-permute-start.2) | collective-permute-done | bytes 131104 | tf_op jit(solution)/shard_map/ppermute | solution.py:18
  12.0 3.6 %collective-permute-start.6 = (bf16[256,512]{1,0:T(8,128)(2,1)S(1)}, bf16[256,512]{1,0:T(8,128)(2,1)S(1)}, u32[]{:S(2)}, u32[]{:S(2)}) collective-permute-start(bf16[256,512]{1,0:T(8,128)(2,1)S(1)} %pad_maximum_fusion.1.refs_0_), channel_id=1, source_target_pairs={{0,12},{4,8},{8,4},{12,0},{1,13},{5,9},{9,5},{13,1},{2,14},{6,10},... | collective-permute-start | bytes 786440 | tf_op jit(solution)/shard_map/ppermute | solution.py:28
  15.6 0.9 collective-permute-start.4
  16.4 1.0 collective-permute-start.1
  17.6 5.2 %collective-permute-done.1 = bf16[128,512]{1,0:T(8,128)(2,1)S(1)} collective-permute-done((bf16[128,512]{1,0:T(8,128)(2,1)S(1)}, bf16[128,512]{1,0:T(8,128)(2,1)S(1)}, u32[]{:S(2)}, u32[]{:S(2)}) %collective-permute-start.1) | collective-permute-done | bytes 131104 | tf_op jit(solution)/shard_map/ppermute | solution.py:18
  22.8 1.2 collective-permute-start.8
  24.6 14.0 %collective-permute-done.5.refs_2_ = bf16[256,512]{1,0:T(8,128)(2,1)S(1)} collective-permute-done((bf16[256,512]{1,0:T(8,128)(2,1)S(1)}, bf16[256,512]{1,0:T(8,128)(2,1)S(1)}, u32[]{:S(2)}, u32[]{:S(2)}) %collective-permute-start.5) | collective-permute-done | bytes 262176 | tf_op jit(solution)/shard_map/ppermute | solution.py:28
  38.6 2.5 %collective-permute-start.12 = (bf16[256,512]{1,0:T(8,128)(2,1)S(1)}, bf16[256,512]{1,0:T(8,128)(2,1)S(1)}, u32[]{:S(2)}, u32[]{:S(2)}) collective-permute-start(bf16[256,512]{1,0:T(8,128)(2,1)S(1)} %pad_maximum_fusion.refs_0_), channel_id=1, source_target_pairs={{0,12},{4,8},{8,4},{12,0},{1,13},{5,9},{9,5},{13,1},{2,14},{6,10},... | collective-permute-start | bytes 786440 | tf_op jit(solution)/shard_map/ppermute | solution.py:28
  41.1 1.9 %collective-permute-start.10 = (bf16[256,512]{1,0:T(8,128)(2,1)S(1)}, bf16[256,512]{1,0:T(8,128)(2,1)S(1)}, u32[]{:S(2)}, u32[]{:S(2)}) collective-permute-start(bf16[256,512]{1,0:T(8,128)(2,1)S(1)} %pad_maximum_fusion.refs_0_), channel_id=1, source_target_pairs={{0,4},{4,0},{8,12},{12,8},{1,5},{5,1},{9,13},{13,9},{2,6},{6,2},{1... | collective-permute-start | bytes 786440 | tf_op jit(solution)/shard_map/ppermute | solution.py:28
  43.0 1.5 fusion.14
  44.5 1.0 collective-permute-start.9
  45.5 6.9 %terms.8 = (bf16[64,3584]{1,0:T(8,128)(2,1)S(1)}, bf16[64,3584]{1,0:T(8,128)(2,1)S(1)}, bf16[128,3584]{1,0:T(8,128)(2,1)S(1)}) custom-call(s32[1]{0:T(128)} %bitcast.place_ref, bf16[256,512]{1,0:T(8,128)(2,1)S(1)} %pad_maximum_fusion.1.refs_0_, bf16[256,512]{1,0:T(8,128)(2,1)S(1)} %collective-permute-done.4.refs_1_, ...), custom_call_target="tpu_custom_call" | custom-call | flops 469762048 | bytes 1000 | tf_op jit(solution)/shard_map/terms/pallas_call | solution.py:135
  52.4 6.9 %terms.9 = (bf16[64,3584]{1,0:T(8,128)(2,1)S(1)}, bf16[64,3584]{1,0:T(8,128)(2,1)S(1)}, bf16[128,3584]{1,0:T(8,128)(2,1)S(1)}) custom-call(s32[1]{0:T(128)} %bitcast.place_ref, bf16[256,512]{1,0:T(8,128)(2,1)S(1)} %pad_maximum_fusion.1.refs_0_, bf16[256,512]{1,0:T(8,128)(2,1)S(1)} %collective-permute-done.4.refs_1_, ...), custom_call_target="tpu_custom_call" | custom-call | flops 469762048 | bytes 1000 | tf_op jit(solution)/shard_map/terms/pallas_call | solution.py:135
  59.4 8.9 %collective-permute-done.9 = f32[256,128]{0,1:T(8,128)} collective-permute-done((f32[256,128]{0,1:T(8,128)}, f32[256,128]{0,1:T(8,128)}, u32[]{:S(2)}, u32[]{:S(2)}) %collective-permute-start.9) | collective-permute-done | bytes 131104 | tf_op jit(solution)/shard_map/ppermute | solution.py:28
  69.4 0.8 collective-permute-done.13.refs_0_
  70.1 0.7 collective-permute-done.14.refs_1_
  70.8 1.7 pair.4
  72.5 1.8 %collective-permute-start.21 = (bf16[128,3584]{1,0:T(8,128)(2,1)}, bf16[128,3584]{1,0:T(8,128)(2,1)}, u32[]{:S(2)}, u32[]{:S(2)}) collective-permute-start(bf16[128,3584]{1,0:T(8,128)(2,1)} %pair.4), channel_id=1, source_target_pairs={{0,2},{1,3},{2,0},{3,1},{4,6},{5,7},{6,4},{7,5},{8,10},{9,11},{10,... | collective-permute-start | bytes 2752520 | tf_op jit(solution)/shard_map/ppermute | solution.py:18
  74.9 0.9 copy-done.4
  75.8 1.9 %collective-permute-start.17 = (bf16[256,512]{1,0:T(8,128)(2,1)S(1)}, bf16[256,512]{1,0:T(8,128)(2,1)S(1)}, u32[]{:S(2)}, u32[]{:S(2)}) collective-permute-start(bf16[256,512]{1,0:T(8,128)(2,1)S(1)} %collective-permute-done.7.refs_0_), channel_id=1, source_target_pairs={{0,4},{4,0},{8,12},{12,8},{1,5},{5,1},{9,13},{13,9},{2,6},{6,2},{1... | collective-permute-start | bytes 786440 | tf_op jit(solution)/shard_map/ppermute | solution.py:28
  77.7 7.5 %terms.10 = (bf16[64,3584]{1,0:T(8,128)(2,1)}, bf16[64,3584]{1,0:T(8,128)(2,1)}, bf16[128,3584]{1,0:T(8,128)(2,1)S(1)}) custom-call(s32[1]{0:T(128)} %bitcast.place_ref, bf16[256,512]{1,0:T(8,128)(2,1)S(1)} %pad_maximum_fusion.refs_0_, bf16[256,512]{1,0:T(8,128)(2,1)S(1)} %collective-permute-done.10.refs_1_, ...), custom_call_target="tpu_custom_call" | custom-call | flops 469762048 | bytes 1000 | tf_op jit(solution)/shard_map/terms/pallas_call | solution.py:135
  85.3 0.9 copy-done.2
  86.2 3.0 %collective-permute-done.18.refs_2_ = bf16[256,512]{1,0:T(8,128)(2,1)S(1)} collective-permute-done((bf16[256,512]{1,0:T(8,128)(2,1)S(1)}, bf16[256,512]{1,0:T(8,128)(2,1)S(1)}, u32[]{:S(2)}, u32[]{:S(2)}) %collective-permute-start.18) | collective-permute-done | bytes 262176 | tf_op jit(solution)/shard_map/ppermute | solution.py:28
  90.7 1.5 collective-permute-done.20.refs_1_
  92.3 1.2 copy-done.3
  93.5 2.1 %pair.6 = (bf16[64,3584]{1,0:T(8,128)(2,1)S(1)}, bf16[64,3584]{1,0:T(8,128)(2,1)S(1)}) custom-call(bf16[128,3584]{1,0:T(8,128)(2,1)S(1)} %copy-done.3, bf16[64,3584]{1,0:T(8,128)(2,1)} %collective-permute-done.19.refs_0_, bf16[64,3584]{1,0:T(8,128)(2,1)S(1)} %collective-permute-done.20.refs_1_), custom_call_target="tpu_custom_call" | custom-call | flops 1000 | bytes 1000 | tf_op jit(solution)/shard_map/pair/pallas_call | solution.py:181
  95.7 0.8 copy-done.5
  96.4 0.8 copy-done.12
  97.4 2.7 %collective-permute-start.22 = (bf16[256,512]{1,0:T(8,128)(2,1)S(1)}, bf16[256,512]{1,0:T(8,128)(2,1)S(1)}, u32[]{:S(2)}, u32[]{:S(2)}) collective-permute-start(bf16[256,512]{1,0:T(8,128)(2,1)S(1)} %bitcast.39), channel_id=1, source_target_pairs={{0,4},{4,0},{8,12},{12,8},{1,5},{5,1},{9,13},{13,9},{2,6},{6,2},{1... | collective-permute-start | bytes 786440 | tf_op jit(solution)/shard_map/ppermute | solution.py:28
  100.1 0.7 collective-permute-start.24
  100.8 1.3 collective-permute-start.25
  102.1 1.0 add.30
  103.7 7.0 %terms.11 = (bf16[64,3584]{1,0:T(8,128)(2,1)S(1)}, bf16[64,3584]{1,0:T(8,128)(2,1)S(1)}, bf16[128,3584]{1,0:T(8,128)(2,1)S(1)}) custom-call(s32[1]{0:T(128)} %bitcast.place_ref, bf16[256,512]{1,0:T(8,128)(2,1)S(1)} %pad_maximum_fusion.refs_0_, bf16[256,512]{1,0:T(8,128)(2,1)S(1)} %collective-permute-done.10.refs_1_, ...), custom_call_target="tpu_custom_call" | custom-call | flops 469762048 | bytes 1000 | tf_op jit(solution)/shard_map/terms/pallas_call | solution.py:135
  110.7 1.3 collective-permute-done.23.refs_2_
  111.9 0.8 collective-permute-done.22.refs_1_
  112.8 4.9 %collective-permute-done.25.refs_4_ = bf16[256,512]{1,0:T(8,128)(2,1)S(1)} collective-permute-done((bf16[256,512]{1,0:T(8,128)(2,1)S(1)}, bf16[256,512]{1,0:T(8,128)(2,1)S(1)}, u32[]{:S(2)}, u32[]{:S(2)}) %collective-permute-start.25) | collective-permute-done | bytes 262176 | tf_op jit(solution)/shard_map/ppermute | solution.py:28
  118.5 1.0 collective-permute-done.27.refs_1_
  119.5 0.7 collective-permute-done.26.refs_0_
  120.1 0.5 pair.7
  120.7 0.8 copy-done.6
  121.5 0.8 copy-done.10
  122.2 0.7 collective-permute-start.30
  122.9 1.5 collective-permute-start.31
  124.4 7.5 %terms.12 = (bf16[64,3584]{1,0:T(8,128)(2,1)}, bf16[64,3584]{1,0:T(8,128)(2,1)S(1)}, bf16[64,3584]{1,0:T(8,128)(2,1)S(1)}, bf16[64,3584]{1,0:T(8,128)(2,1)S(1)}) custom-call(s32[1]{0:T(128)} %bitcast.place_ref, bf16[256,512]{1,0:T(8,128)(2,1)S(1)} %collective-permute-done.7.refs_0_, bf16[256,512]{1,0:T(8,128)(2,1)S(1)} %collective-permute-done.17.refs_1_, ...), custom_call_target="tpu_custom_call" | custom-call | flops 469762048 | bytes 1000 | tf_op jit(solution)/shard_map/terms/pallas_call | solution.py:135
  132.0 0.8 copy-done.8
  132.7 0.8 copy-done.9
  133.5 0.8 copy-done.11
  135.0 1.7 collective-permute-start.34
  137.0 1.1 collective-permute-done.35
  138.1 0.7 collective-permute-start.36
  139.9 2.8 %fusion.4 = f32[1024,1024]{1,0:T(8,128)} fusion(bf16[16,4224]{1,0:T(8,128)(2,1)S(1)} %pad_maximum_fusion.2, s32[]{:T(128)S(6)} %select_n.121, s32[]{:T(128)S(6)} %select_n.122), kind=kOutput, calls=%fused_computation.20 | convolution fusion | flops 33554432 | bytes 4259848 | tf_op jit(solution)/shard_map/dot_general | solution.py:267
  142.8 0.9 fusion.6
  143.7 7.0 %terms.13 = (bf16[64,3584]{1,0:T(8,128)(2,1)S(1)}, bf16[64,3584]{1,0:T(8,128)(2,1)S(1)}, bf16[64,3584]{1,0:T(8,128)(2,1)S(1)}, bf16[64,3584]{1,0:T(8,128)(2,1)S(1)}) custom-call(s32[1]{0:T(128)} %bitcast.place_ref, bf16[256,512]{1,0:T(8,128)(2,1)S(1)} %collective-permute-done.7.refs_0_, bf16[256,512]{1,0:T(8,128)(2,1)S(1)} %collective-permute-done.17.refs_1_, ...), custom_call_target="tpu_custom_call" | custom-call | flops 469762048 | bytes 1000 | tf_op jit(solution)/shard_map/terms/pallas_call | solution.py:135
  150.6 9.0 %collective-permute-done.36.refs_7_ = bf16[64,3584]{1,0:T(8,128)(2,1)S(1)} collective-permute-done((bf16[64,3584]{1,0:T(8,128)(2,1)}, bf16[64,3584]{1,0:T(8,128)(2,1)S(1)}, u32[]{:S(2)}, u32[]{:S(2)}) %collective-permute-start.36) | collective-permute-done | bytes 458784 | tf_op jit(solution)/shard_map/ppermute | solution.py:18
  160.7 0.6 collective-permute-start.45
  161.3 1.7 sums.3.refs_6_
  163.5 1.5 sums.2.refs_6_
  164.9 7.7 %terms.14.refs_9_ = bf16[256,7168]{1,0:T(8,128)(2,1)} custom-call(s32[1]{0:T(128)} %bitcast.place_ref, bf16[256,512]{1,0:T(8,128)(2,1)S(1)} %bitcast.41, bf16[256,512]{1,0:T(8,128)(2,1)S(1)} %collective-permute-done.22.refs_1_, bf16[256,512]{1,0:T(8,128)(2,1)S(1)} %collective-permute-done.23.refs_2_, bf16[256,512]{1,0:T(8,128)(2,1)S(1)} %collective-permute-done.30.refs_3_, ...), custom_call_target="tpu_custom_call" | custom-call | flops 469762048 | bytes 1000 | tf_op jit(solution)/shard_map/terms/pallas_call | solution.py:135
  172.7 0.6 collective-permute-done.45.refs_8_
  173.2 8.0 %terms.15 = bf16[256,7168]{1,0:T(8,128)(2,1)} custom-call(s32[1]{0:T(128)} %bitcast.place_ref, bf16[256,512]{1,0:T(8,128)(2,1)S(1)} %bitcast.42, bf16[256,512]{1,0:T(8,128)(2,1)S(1)} %collective-permute-done.22.refs_1_, bf16[256,512]{1,0:T(8,128)(2,1)S(1)} %collective-permute-done.23.refs_2_, ...), custom_call_target="tpu_custom_call", output_to_operand_aliasing={{}: (10, {})} | custom-call | flops 469762048 | bytes 1000 | tf_op jit(solution)/shard_map/terms/pallas_call | solution.py:135
  (111 shorter events, 10.3 us)
Async XLA Ops:
  0.6 5.5 %copy-start = (bf16[7168,64]{0,1:T(8,128)(2,1)S(1)}, bf16[7168,64]{0,1:T(8,128)(2,1)}, u32[]{:S(2)}) copy-start(bf16[7168,64]{0,1:T(8,128)(2,1)} %param.10) | copy-start | bytes 2752516
  2.0 7.4 %copy-start.14 = (bf16[1,4,512,256]{3,2,1,0:T(8,128)(2,1)S(1)}, bf16[1,4,512,256]{3,2,1,0:T(8,128)(2,1)}, u32[]{:S(2)}) copy-start(bf16[1,4,512,256]{3,2,1,0:T(8,128)(2,1)} %param.8) | copy-start | bytes 3145732
  2.0 7.4 %copy-start.16 = (bf16[1,4,512,64]{2,3,1,0:T(8,128)(2,1)S(1)}, bf16[1,4,512,64]{2,3,1,0:T(8,128)(2,1)}, u32[]{:S(2)}) copy-start(bf16[1,4,512,64]{2,3,1,0:T(8,128)(2,1)} %param.11) | copy-start | bytes 786436
  2.9 7.2 %collective-permute-start.3 = (bf16[128,512]{1,0:T(8,128)(2,1)}, bf16[128,512]{1,0:T(8,128)(2,1)S(1)}, u32[]{:S(2)}, u32[]{:S(2)}) collective-permute-start(bf16[128,512]{1,0:T(8,128)(2,1)} %get-tuple-element.133), channel_id=1, source_target_pairs={{0,2},{1,3},{2,0},{3,1},{4,6},{5,7},{6,4},{7,5},{8,10},{9,11},{10,... | collective-permute-start | bytes 393224 | tf_op jit(solution)/shard_map/ppermute | solution.py:18
  6.0 10.4 %copy-start.17 = (bf16[128,512]{1,0:T(8,128)(2,1)S(1)}, bf16[128,512]{1,0:T(8,128)(2,1)}, u32[]{:S(2)}) copy-start(bf16[128,512]{1,0:T(8,128)(2,1)} %get-tuple-element.134) | copy-start | bytes 393220
  6.0 5.9 %collective-permute-start.2 = (bf16[128,512]{1,0:T(8,128)(2,1)S(1)}, bf16[128,512]{1,0:T(8,128)(2,1)S(1)}, u32[]{:S(2)}, u32[]{:S(2)}) collective-permute-start(bf16[128,512]{1,0:T(8,128)(2,1)S(1)} %get-tuple-element.131), channel_id=1, source_target_pairs={{0,3},{1,2},{2,1},{3,0},{4,7},{5,6},{6,5},{7,4},{8,11},{9,10},{10,... | collective-permute-start | bytes 393224 | tf_op jit(solution)/shard_map/ppermute | solution.py:18
  9.4 29.2 %copy-start.15 = (f32[256,64]{0,1:T(8,128)}, f32[256,64]{0,1:T(8,128)S(1)}, u32[]{:S(2)}) copy-start(f32[256,64]{0,1:T(8,128)S(1)} %fusion.15) | copy-start | bytes 196612
  12.0 12.6 %collective-permute-start.6 = (bf16[256,512]{1,0:T(8,128)(2,1)S(1)}, bf16[256,512]{1,0:T(8,128)(2,1)S(1)}, u32[]{:S(2)}, u32[]{:S(2)}) collective-permute-start(bf16[256,512]{1,0:T(8,128)(2,1)S(1)} %pad_maximum_fusion.1.refs_0_), channel_id=1, source_target_pairs={{0,12},{4,8},{8,4},{12,0},{1,13},{5,9},{9,5},{13,1},{2,14},{6,10},... | collective-permute-start | bytes 786440 | tf_op jit(solution)/shard_map/ppermute | solution.py:28
  15.6 23.0 %collective-permute-start.5 = (bf16[256,512]{1,0:T(8,128)(2,1)S(1)}, bf16[256,512]{1,0:T(8,128)(2,1)S(1)}, u32[]{:S(2)}, u32[]{:S(2)}) collective-permute-start(bf16[256,512]{1,0:T(8,128)(2,1)S(1)} %pad_maximum_fusion.1.refs_0_), channel_id=1, source_target_pairs={{0,8},{4,12},{8,0},{12,4},{1,9},{5,13},{9,1},{13,5},{2,10},{6,14},... | collective-permute-start | bytes 786440 | tf_op jit(solution)/shard_map/ppermute | solution.py:28
  15.6 23.0 %collective-permute-start.4 = (bf16[256,512]{1,0:T(8,128)(2,1)S(1)}, bf16[256,512]{1,0:T(8,128)(2,1)S(1)}, u32[]{:S(2)}, u32[]{:S(2)}) collective-permute-start(bf16[256,512]{1,0:T(8,128)(2,1)S(1)} %pad_maximum_fusion.1.refs_0_), channel_id=1, source_target_pairs={{0,4},{4,0},{8,12},{12,8},{1,5},{5,1},{9,13},{13,9},{2,6},{6,2},{1... | collective-permute-start | bytes 786440 | tf_op jit(solution)/shard_map/ppermute | solution.py:28
  16.4 6.4 %collective-permute-start.1 = (bf16[128,512]{1,0:T(8,128)(2,1)S(1)}, bf16[128,512]{1,0:T(8,128)(2,1)S(1)}, u32[]{:S(2)}, u32[]{:S(2)}) collective-permute-start(bf16[128,512]{1,0:T(8,128)(2,1)S(1)} %copy-done.17), channel_id=1, source_target_pairs={{0,2},{1,3},{2,0},{3,1},{4,6},{5,7},{6,4},{7,5},{8,10},{9,11},{10,... | collective-permute-start | bytes 393224 | tf_op jit(solution)/shard_map/ppermute | solution.py:18
  17.4 6.7 %collective-permute-start = (bf16[128,512]{1,0:T(8,128)(2,1)S(1)}, bf16[128,512]{1,0:T(8,128)(2,1)S(1)}, u32[]{:S(2)}, u32[]{:S(2)}) collective-permute-start(bf16[128,512]{1,0:T(8,128)(2,1)S(1)} %get-tuple-element.132), channel_id=1, source_target_pairs={{0,3},{1,2},{2,1},{3,0},{4,7},{5,6},{6,5},{7,4},{8,11},{9,10},{10,... | collective-permute-start | bytes 393224 | tf_op jit(solution)/shard_map/ppermute | solution.py:18
  22.8 20.2 %collective-permute-start.8 = (f32[256,128]{0,1:T(8,128)S(1)}, f32[256,128]{0,1:T(8,128)S(1)}, u32[]{:S(2)}, u32[]{:S(2)}) collective-permute-start(f32[256,128]{0,1:T(8,128)S(1)} %pad_maximum_fusion.3), channel_id=1, source_target_pairs={{0,4},{4,0},{8,12},{12,8},{1,5},{5,1},{9,13},{13,9},{2,6},{6,2},{1... | collective-permute-start | bytes 393224 | tf_op jit(solution)/shard_map/ppermute | solution.py:28
  24.1 21.4 %collective-permute-start.7 = (bf16[256,512]{1,0:T(8,128)(2,1)S(1)}, bf16[256,512]{1,0:T(8,128)(2,1)S(1)}, u32[]{:S(2)}, u32[]{:S(2)}) collective-permute-start(bf16[256,512]{1,0:T(8,128)(2,1)S(1)} %bitcast.46), channel_id=1, source_target_pairs={{0,1},{1,0},{2,3},{3,2},{4,5},{5,4},{6,7},{7,6},{8,9},{9,8},{10,11... | collective-permute-start | bytes 786440 | tf_op jit(solution)/shard_map/ppermute | solution.py:18
  38.6 29.7 %collective-permute-start.12 = (bf16[256,512]{1,0:T(8,128)(2,1)S(1)}, bf16[256,512]{1,0:T(8,128)(2,1)S(1)}, u32[]{:S(2)}, u32[]{:S(2)}) collective-permute-start(bf16[256,512]{1,0:T(8,128)(2,1)S(1)} %pad_maximum_fusion.refs_0_), channel_id=1, source_target_pairs={{0,12},{4,8},{8,4},{12,0},{1,13},{5,9},{9,5},{13,1},{2,14},{6,10},... | collective-permute-start | bytes 786440 | tf_op jit(solution)/shard_map/ppermute | solution.py:28
  41.1 27.2 %collective-permute-start.11 = (bf16[256,512]{1,0:T(8,128)(2,1)S(1)}, bf16[256,512]{1,0:T(8,128)(2,1)S(1)}, u32[]{:S(2)}, u32[]{:S(2)}) collective-permute-start(bf16[256,512]{1,0:T(8,128)(2,1)S(1)} %pad_maximum_fusion.refs_0_), channel_id=1, source_target_pairs={{0,8},{4,12},{8,0},{12,4},{1,9},{5,13},{9,1},{13,5},{2,10},{6,14},... | collective-permute-start | bytes 786440 | tf_op jit(solution)/shard_map/ppermute | solution.py:28
  41.1 27.2 %collective-permute-start.10 = (bf16[256,512]{1,0:T(8,128)(2,1)S(1)}, bf16[256,512]{1,0:T(8,128)(2,1)S(1)}, u32[]{:S(2)}, u32[]{:S(2)}) collective-permute-start(bf16[256,512]{1,0:T(8,128)(2,1)S(1)} %pad_maximum_fusion.refs_0_), channel_id=1, source_target_pairs={{0,4},{4,0},{8,12},{12,8},{1,5},{5,1},{9,13},{13,9},{2,6},{6,2},{1... | collective-permute-start | bytes 786440 | tf_op jit(solution)/shard_map/ppermute | solution.py:28
  44.5 23.8 %collective-permute-start.9 = (f32[256,128]{0,1:T(8,128)}, f32[256,128]{0,1:T(8,128)}, u32[]{:S(2)}, u32[]{:S(2)}) collective-permute-start(f32[256,128]{0,1:T(8,128)} %fusion.14), channel_id=1, source_target_pairs={{0,8},{4,12},{8,0},{12,4},{1,9},{5,13},{9,1},{13,5},{2,10},{6,14},... | collective-permute-start | bytes 393224 | tf_op jit(solution)/shard_map/ppermute | solution.py:28
  68.3 1.9 %collective-permute-start.13 = (bf16[64,3584]{1,0:T(8,128)(2,1)S(1)}, bf16[64,3584]{1,0:T(8,128)(2,1)S(1)}, u32[]{:S(2)}, u32[]{:S(2)}) collective-permute-start(bf16[64,3584]{1,0:T(8,128)(2,1)S(1)} %get-tuple-element.73), channel_id=1, source_target_pairs={{0,1},{1,0},{2,3},{3,2},{4,5},{5,4},{6,7},{7,6},{8,9},{9,8},{10,11... | collective-permute-start | bytes 1376264 | tf_op jit(solution)/shard_map/ppermute | solution.py:18
  68.3 2.5 %collective-permute-start.14 = (bf16[64,3584]{1,0:T(8,128)(2,1)S(1)}, bf16[64,3584]{1,0:T(8,128)(2,1)S(1)}, u32[]{:S(2)}, u32[]{:S(2)}) collective-permute-start(bf16[64,3584]{1,0:T(8,128)(2,1)S(1)} %get-tuple-element.75), channel_id=1, source_target_pairs={{0,1},{1,0},{2,3},{3,2},{4,5},{5,4},{6,7},{7,6},{8,9},{9,8},{10,11... | collective-permute-start | bytes 1376264 | tf_op jit(solution)/shard_map/ppermute | solution.py:18
  68.8 5.5 %collective-permute-start.15 = (bf16[64,3584]{1,0:T(8,128)(2,1)S(1)}, bf16[64,3584]{1,0:T(8,128)(2,1)S(1)}, u32[]{:S(2)}, u32[]{:S(2)}) collective-permute-start(bf16[64,3584]{1,0:T(8,128)(2,1)S(1)} %get-tuple-element.77), channel_id=1, source_target_pairs={{0,1},{1,0},{2,3},{3,2},{4,5},{5,4},{6,7},{7,6},{8,9},{9,8},{10,11... | collective-permute-start | bytes 1376264 | tf_op jit(solution)/shard_map/ppermute | solution.py:18
  68.9 5.4 %collective-permute-start.16 = (bf16[64,3584]{1,0:T(8,128)(2,1)S(1)}, bf16[64,3584]{1,0:T(8,128)(2,1)S(1)}, u32[]{:S(2)}, u32[]{:S(2)}) collective-permute-start(bf16[64,3584]{1,0:T(8,128)(2,1)S(1)} %get-tuple-element.79), channel_id=1, source_target_pairs={{0,1},{1,0},{2,3},{3,2},{4,5},{5,4},{6,7},{7,6},{8,9},{9,8},{10,11... | collective-permute-start | bytes 1376264 | tf_op jit(solution)/shard_map/ppermute | solution.py:18
  72.5 28.3 %collective-permute-start.21 = (bf16[128,3584]{1,0:T(8,128)(2,1)}, bf16[128,3584]{1,0:T(8,128)(2,1)}, u32[]{:S(2)}, u32[]{:S(2)}) collective-permute-start(bf16[128,3584]{1,0:T(8,128)(2,1)} %pair.4), channel_id=1, source_target_pairs={{0,2},{1,3},{2,0},{3,1},{4,6},{5,7},{6,4},{7,5},{8,10},{9,11},{10,... | collective-permute-start | bytes 2752520 | tf_op jit(solution)/shard_map/ppermute | solution.py:18
  74.9 0.9 copy-start.4
  75.8 14.3 %copy-start.18 = (s32[1,256]{1,0:T(1,128)S(1)}, s32[1,256]{1,0:T(1,128)}, u32[]{:S(2)}) copy-start(s32[1,256]{1,0:T(1,128)} %param.12) | copy-start | bytes 3076
  75.8 13.4 %collective-permute-start.18 = (bf16[256,512]{1,0:T(8,128)(2,1)S(1)}, bf16[256,512]{1,0:T(8,128)(2,1)S(1)}, u32[]{:S(2)}, u32[]{:S(2)}) collective-permute-start(bf16[256,512]{1,0:T(8,128)(2,1)S(1)} %collective-permute-done.7.refs_0_), channel_id=1, source_target_pairs={{0,8},{4,12},{8,0},{12,4},{1,9},{5,13},{9,1},{13,5},{2,10},{6,14},... | collective-permute-start | bytes 786440 | tf_op jit(solution)/shard_map/ppermute | solution.py:28
  75.8 13.7 %collective-permute-start.17 = (bf16[256,512]{1,0:T(8,128)(2,1)S(1)}, bf16[256,512]{1,0:T(8,128)(2,1)S(1)}, u32[]{:S(2)}, u32[]{:S(2)}) collective-permute-start(bf16[256,512]{1,0:T(8,128)(2,1)S(1)} %collective-permute-done.7.refs_0_), channel_id=1, source_target_pairs={{0,4},{4,0},{8,12},{12,8},{1,5},{5,1},{9,13},{13,9},{2,6},{6,2},{1... | collective-permute-start | bytes 786440 | tf_op jit(solution)/shard_map/ppermute | solution.py:28
  85.2 0.9 copy-start.2
  89.5 2.6 %collective-permute-start.20 = (bf16[64,3584]{1,0:T(8,128)(2,1)}, bf16[64,3584]{1,0:T(8,128)(2,1)S(1)}, u32[]{:S(2)}, u32[]{:S(2)}) collective-permute-start(bf16[64,3584]{1,0:T(8,128)(2,1)} %get-tuple-element.86), channel_id=1, source_target_pairs={{0,1},{1,0},{2,3},{3,2},{4,5},{5,4},{6,7},{7,6},{8,9},{9,8},{10,11... | collective-permute-start | bytes 1376264 | tf_op jit(solution)/shard_map/ppermute | solution.py:18
  89.5 2.8 %collective-permute-start.19 = (bf16[64,3584]{1,0:T(8,128)(2,1)}, bf16[64,3584]{1,0:T(8,128)(2,1)}, u32[]{:S(2)}, u32[]{:S(2)}) collective-permute-start(bf16[64,3584]{1,0:T(8,128)(2,1)} %get-tuple-element.84), channel_id=1, source_target_pairs={{0,1},{1,0},{2,3},{3,2},{4,5},{5,4},{6,7},{7,6},{8,9},{9,8},{10,11... | collective-permute-start | bytes 1376264 | tf_op jit(solution)/shard_map/ppermute | solution.py:18
  90.3 34.1 %collective-permute-start.28 = (bf16[128,3584]{1,0:T(8,128)(2,1)}, bf16[128,3584]{1,0:T(8,128)(2,1)}, u32[]{:S(2)}, u32[]{:S(2)}) collective-permute-start(bf16[128,3584]{1,0:T(8,128)(2,1)} %copy-done.4), channel_id=1, source_target_pairs={{0,2},{1,3},{2,0},{3,1},{4,6},{5,7},{6,4},{7,5},{8,10},{9,11},{10,... | collective-permute-start | bytes 2752520 | tf_op jit(solution)/shard_map/ppermute | solution.py:18
  92.3 1.2 copy-start.3
  97.2 14.7 %collective-permute-start.23 = (bf16[256,512]{1,0:T(8,128)(2,1)S(1)}, bf16[256,512]{1,0:T(8,128)(2,1)S(1)}, u32[]{:S(2)}, u32[]{:S(2)}) collective-permute-start(bf16[256,512]{1,0:T(8,128)(2,1)S(1)} %bitcast.38), channel_id=1, source_target_pairs={{0,8},{4,12},{8,0},{12,4},{1,9},{5,13},{9,1},{13,5},{2,10},{6,14},... | collective-permute-start | bytes 786440 | tf_op jit(solution)/shard_map/ppermute | solution.py:28
  97.4 15.4 %collective-permute-start.22 = (bf16[256,512]{1,0:T(8,128)(2,1)S(1)}, bf16[256,512]{1,0:T(8,128)(2,1)S(1)}, u32[]{:S(2)}, u32[]{:S(2)}) collective-permute-start(bf16[256,512]{1,0:T(8,128)(2,1)S(1)} %bitcast.39), channel_id=1, source_target_pairs={{0,4},{4,0},{8,12},{12,8},{1,5},{5,1},{9,13},{13,9},{2,6},{6,2},{1... | collective-permute-start | bytes 786440 | tf_op jit(solution)/shard_map/ppermute | solution.py:28
  100.1 12.7 %collective-permute-start.24 = (bf16[256,512]{1,0:T(8,128)(2,1)S(1)}, bf16[256,512]{1,0:T(8,128)(2,1)S(1)}, u32[]{:S(2)}, u32[]{:S(2)}) collective-permute-start(bf16[256,512]{1,0:T(8,128)(2,1)S(1)} %collective-permute-done.7.refs_0_), channel_id=1, source_target_pairs={{4,8},{8,4},{5,9},{9,5},{6,10},{10,6},{7,11},{11,7},{20,24},{24,20... | collective-permute-start | bytes 786440 | tf_op jit(solution)/shard_map/ppermute | solution.py:28
  100.8 16.9 %collective-permute-start.25 = (bf16[256,512]{1,0:T(8,128)(2,1)S(1)}, bf16[256,512]{1,0:T(8,128)(2,1)S(1)}, u32[]{:S(2)}, u32[]{:S(2)}) collective-permute-start(bf16[256,512]{1,0:T(8,128)(2,1)S(1)} %collective-permute-done.18.refs_2_), channel_id=1, source_target_pairs={{4,0},{8,12},{5,1},{9,13},{6,2},{10,14},{7,3},{11,15},{20,16},{24,... | collective-permute-start | bytes 786440 | tf_op jit(solution)/shard_map/ppermute | solution.py:28
  103.7 14.5 %copy-start.13 = (bf16[64,3584]{1,0:T(8,128)(2,1)S(1)}, bf16[64,3584]{1,0:T(8,128)(2,1)}, u32[]{:S(2)}) copy-start(bf16[64,3584]{1,0:T(8,128)(2,1)} %copy-done.12) | copy-start | bytes 1376260
  103.7 20.7 %copy-start.19 = (s32[4]{0:T(128)S(1)}, s32[4]{0:T(128)}, u32[]{:S(2)}) copy-start(s32[4]{0:T(128)} %param.13) | copy-start | bytes 52
  117.7 1.8 %collective-permute-start.27 = (bf16[64,3584]{1,0:T(8,128)(2,1)S(1)}, bf16[64,3584]{1,0:T(8,128)(2,1)S(1)}, u32[]{:S(2)}, u32[]{:S(2)}) collective-permute-start(bf16[64,3584]{1,0:T(8,128)(2,1)S(1)} %get-tuple-element.97), channel_id=1, source_target_pairs={{0,1},{1,0},{2,3},{3,2},{4,5},{5,4},{6,7},{7,6},{8,9},{9,8},{10,11... | collective-permute-start | bytes 1376264 | tf_op jit(solution)/shard_map/ppermute | solution.py:18
  117.7 2.5 %collective-permute-start.26 = (bf16[64,3584]{1,0:T(8,128)(2,1)S(1)}, bf16[64,3584]{1,0:T(8,128)(2,1)S(1)}, u32[]{:S(2)}, u32[]{:S(2)}) collective-permute-start(bf16[64,3584]{1,0:T(8,128)(2,1)S(1)} %get-tuple-element.95), channel_id=1, source_target_pairs={{0,1},{1,0},{2,3},{3,2},{4,5},{5,4},{6,7},{7,6},{8,9},{9,8},{10,11... | collective-permute-start | bytes 1376264 | tf_op jit(solution)/shard_map/ppermute | solution.py:18
  118.2 16.1 %collective-permute-start.29 = (bf16[64,3584]{1,0:T(8,128)(2,1)S(1)}, bf16[64,3584]{1,0:T(8,128)(2,1)S(1)}, u32[]{:S(2)}, u32[]{:S(2)}) collective-permute-start(bf16[64,3584]{1,0:T(8,128)(2,1)S(1)} %copy-done.13), channel_id=1, source_target_pairs={{0,2},{1,3},{2,0},{3,1},{4,6},{5,7},{6,4},{7,5},{8,10},{9,11},{10,... | collective-permute-start | bytes 1376264 | tf_op jit(solution)/shard_map/ppermute | solution.py:18
  120.7 0.8 copy-start.6
  121.5 0.8 copy-start.10
  122.2 12.1 %collective-permute-start.30 = (bf16[256,512]{1,0:T(8,128)(2,1)S(1)}, bf16[256,512]{1,0:T(8,128)(2,1)S(1)}, u32[]{:S(2)}, u32[]{:S(2)}) collective-permute-start(bf16[256,512]{1,0:T(8,128)(2,1)S(1)} %bitcast.40), channel_id=1, source_target_pairs={{4,8},{8,4},{5,9},{9,5},{6,10},{10,6},{7,11},{11,7},{20,24},{24,20... | collective-permute-start | bytes 786440 | tf_op jit(solution)/shard_map/ppermute | solution.py:28
  122.9 11.4 %collective-permute-start.31 = (bf16[256,512]{1,0:T(8,128)(2,1)S(1)}, bf16[256,512]{1,0:T(8,128)(2,1)S(1)}, u32[]{:S(2)}, u32[]{:S(2)}) collective-permute-start(bf16[256,512]{1,0:T(8,128)(2,1)S(1)} %collective-permute-done.23.refs_2_), channel_id=1, source_target_pairs={{4,0},{8,12},{5,1},{9,13},{6,2},{10,14},{7,3},{11,15},{20,16},{24,... | collective-permute-start | bytes 786440 | tf_op jit(solution)/shard_map/ppermute | solution.py:28
  131.9 0.8 copy-start.8
  132.7 0.8 copy-start.9
  133.5 0.8 copy-start.11
  134.3 5.3 %collective-permute-start.32 = (bf16[64,3584]{1,0:T(8,128)(2,1)}, bf16[64,3584]{1,0:T(8,128)(2,1)}, u32[]{:S(2)}, u32[]{:S(2)}) collective-permute-start(bf16[64,3584]{1,0:T(8,128)(2,1)} %get-tuple-element.103), channel_id=1, source_target_pairs={{0,1},{1,0},{2,3},{3,2},{4,5},{5,4},{6,7},{7,6},{8,9},{9,8},{10,11... | collective-permute-start | bytes 1376264 | tf_op jit(solution)/shard_map/ppermute | solution.py:18
  134.6 3.4 %collective-permute-start.35 = (bf16[4,4224]{1,0:T(4,128)(2,1)S(1)}, bf16[4,4224]{1,0:T(4,128)(2,1)S(1)}, u32[]{:S(2)}, u32[]{:S(2)}) collective-permute-start(bf16[4,4224]{1,0:T(4,128)(2,1)S(1)} %pad_maximum_fusion.4), channel_id=1, source_target_pairs={{0,3},{1,2},{2,1},{3,0},{4,7},{5,6},{6,5},{7,4},{8,11},{9,10},{10,... | collective-permute-start | bytes 101384 | tf_op jit(solution)/shard_map/ppermute | solution.py:18
  135.0 4.2 %collective-permute-start.34 = (bf16[4,4224]{1,0:T(4,128)(2,1)S(1)}, bf16[4,4224]{1,0:T(4,128)(2,1)S(1)}, u32[]{:S(2)}, u32[]{:S(2)}) collective-permute-start(bf16[4,4224]{1,0:T(4,128)(2,1)S(1)} %pad_maximum_fusion.4), channel_id=1, source_target_pairs={{0,2},{1,3},{2,0},{3,1},{4,6},{5,7},{6,4},{7,5},{8,10},{9,11},{10,... | collective-permute-start | bytes 101384 | tf_op jit(solution)/shard_map/ppermute | solution.py:18
  136.7 2.5 %collective-permute-start.33 = (bf16[4,4224]{1,0:T(4,128)(2,1)S(1)}, bf16[4,4224]{1,0:T(4,128)(2,1)S(1)}, u32[]{:S(2)}, u32[]{:S(2)}) collective-permute-start(bf16[4,4224]{1,0:T(4,128)(2,1)S(1)} %pad_maximum_fusion.4), channel_id=1, source_target_pairs={{0,1},{1,0},{2,3},{3,2},{4,5},{5,4},{6,7},{7,6},{8,9},{9,8},{10,11... | collective-permute-start | bytes 101384 | tf_op jit(solution)/shard_map/ppermute | solution.py:18
  136.7 23.0 %collective-permute-start.44 = (bf16[64,3584]{1,0:T(8,128)(2,1)}, bf16[64,3584]{1,0:T(8,128)(2,1)S(1)}, u32[]{:S(2)}, u32[]{:S(2)}) collective-permute-start(bf16[64,3584]{1,0:T(8,128)(2,1)} %copy-done.5), channel_id=1, source_target_pairs={{0,2},{1,3},{2,0},{3,1},{4,6},{5,7},{6,4},{7,5},{8,10},{9,11},{10,... | collective-permute-start | bytes 1376264 | tf_op jit(solution)/shard_map/ppermute | solution.py:18
  138.1 21.6 %collective-permute-start.36 = (bf16[64,3584]{1,0:T(8,128)(2,1)}, bf16[64,3584]{1,0:T(8,128)(2,1)S(1)}, u32[]{:S(2)}, u32[]{:S(2)}) collective-permute-start(bf16[64,3584]{1,0:T(8,128)(2,1)} %copy-done.10), channel_id=1, source_target_pairs={{0,2},{1,3},{2,0},{3,1},{4,6},{5,7},{6,4},{7,5},{8,10},{9,11},{10,... | collective-permute-start | bytes 1376264 | tf_op jit(solution)/shard_map/ppermute | solution.py:18
  139.2 21.0 %collective-permute-start.43 = (bf16[64,3584]{1,0:T(8,128)(2,1)}, bf16[64,3584]{1,0:T(8,128)(2,1)S(1)}, u32[]{:S(2)}, u32[]{:S(2)}) collective-permute-start(bf16[64,3584]{1,0:T(8,128)(2,1)} %copy-done.11), channel_id=1, source_target_pairs={{0,1},{1,0},{2,3},{3,2},{4,5},{5,4},{6,7},{7,6},{8,9},{9,8},{10,11... | collective-permute-start | bytes 1376264 | tf_op jit(solution)/shard_map/ppermute | solution.py:18
  139.2 21.1 %collective-permute-start.42 = (bf16[64,3584]{1,0:T(8,128)(2,1)}, bf16[64,3584]{1,0:T(8,128)(2,1)S(1)}, u32[]{:S(2)}, u32[]{:S(2)}) collective-permute-start(bf16[64,3584]{1,0:T(8,128)(2,1)} %copy-done.9), channel_id=1, source_target_pairs={{0,1},{1,0},{2,3},{3,2},{4,5},{5,4},{6,7},{7,6},{8,9},{9,8},{10,11... | collective-permute-start | bytes 1376264 | tf_op jit(solution)/shard_map/ppermute | solution.py:18
  139.7 21.0 %collective-permute-start.41 = (bf16[64,3584]{1,0:T(8,128)(2,1)}, bf16[64,3584]{1,0:T(8,128)(2,1)S(1)}, u32[]{:S(2)}, u32[]{:S(2)}) collective-permute-start(bf16[64,3584]{1,0:T(8,128)(2,1)} %copy-done.8), channel_id=1, source_target_pairs={{0,1},{1,0},{2,3},{3,2},{4,5},{5,4},{6,7},{7,6},{8,9},{9,8},{10,11... | collective-permute-start | bytes 1376264 | tf_op jit(solution)/shard_map/ppermute | solution.py:18
  143.7 17.1 %copy-start.7 = (bf16[64,3584]{1,0:T(8,128)(2,1)S(1)}, bf16[64,3584]{1,0:T(8,128)(2,1)}, u32[]{:S(2)}) copy-start(bf16[64,3584]{1,0:T(8,128)(2,1)} %copy-done.6) | copy-start | bytes 1376260
  159.7 3.4 %collective-permute-start.40 = (bf16[64,3584]{1,0:T(8,128)(2,1)S(1)}, bf16[64,3584]{1,0:T(8,128)(2,1)S(1)}, u32[]{:S(2)}, u32[]{:S(2)}) collective-permute-start(bf16[64,3584]{1,0:T(8,128)(2,1)S(1)} %get-tuple-element.116), channel_id=1, source_target_pairs={{0,1},{1,0},{2,3},{3,2},{4,5},{5,4},{6,7},{7,6},{8,9},{9,8},{10,11... | collective-permute-start | bytes 1376264 | tf_op jit(solution)/shard_map/ppermute | solution.py:18
  159.7 3.4 %collective-permute-start.39 = (bf16[64,3584]{1,0:T(8,128)(2,1)S(1)}, bf16[64,3584]{1,0:T(8,128)(2,1)S(1)}, u32[]{:S(2)}, u32[]{:S(2)}) collective-permute-start(bf16[64,3584]{1,0:T(8,128)(2,1)S(1)} %get-tuple-element.114), channel_id=1, source_target_pairs={{0,1},{1,0},{2,3},{3,2},{4,5},{5,4},{6,7},{7,6},{8,9},{9,8},{10,11... | collective-permute-start | bytes 1376264 | tf_op jit(solution)/shard_map/ppermute | solution.py:18
  160.2 2.9 %collective-permute-start.38 = (bf16[64,3584]{1,0:T(8,128)(2,1)S(1)}, bf16[64,3584]{1,0:T(8,128)(2,1)S(1)}, u32[]{:S(2)}, u32[]{:S(2)}) collective-permute-start(bf16[64,3584]{1,0:T(8,128)(2,1)S(1)} %get-tuple-element.112), channel_id=1, source_target_pairs={{0,1},{1,0},{2,3},{3,2},{4,5},{5,4},{6,7},{7,6},{8,9},{9,8},{10,11... | collective-permute-start | bytes 1376264 | tf_op jit(solution)/shard_map/ppermute | solution.py:18
  160.3 3.2 %collective-permute-start.37 = (bf16[64,3584]{1,0:T(8,128)(2,1)S(1)}, bf16[64,3584]{1,0:T(8,128)(2,1)S(1)}, u32[]{:S(2)}, u32[]{:S(2)}) collective-permute-start(bf16[64,3584]{1,0:T(8,128)(2,1)S(1)} %get-tuple-element.110), channel_id=1, source_target_pairs={{0,1},{1,0},{2,3},{3,2},{4,5},{5,4},{6,7},{7,6},{8,9},{9,8},{10,11... | collective-permute-start | bytes 1376264 | tf_op jit(solution)/shard_map/ppermute | solution.py:18
  160.7 12.5 %collective-permute-start.45 = (bf16[64,3584]{1,0:T(8,128)(2,1)S(1)}, bf16[64,3584]{1,0:T(8,128)(2,1)S(1)}, u32[]{:S(2)}, u32[]{:S(2)}) collective-permute-start(bf16[64,3584]{1,0:T(8,128)(2,1)S(1)} %copy-done.7), channel_id=1, source_target_pairs={{0,2},{1,3},{2,0},{3,1},{4,6},{5,7},{6,4},{7,5},{8,10},{9,11},{10,... | collective-permute-start | bytes 1376264 | tf_op jit(solution)/shard_map/ppermute | solution.py:18
  173.2 8.0 %copy-start.1 = (bf16[7168,64]{0,1:T(8,128)(2,1)S(1)}, bf16[7168,64]{0,1:T(8,128)(2,1)}, u32[]{:S(2)}) copy-start(bf16[7168,64]{0,1:T(8,128)(2,1)} %param.10) | copy-start | bytes 2752516
  (2 other events, 1.5 us)

commit v15 on v11

--- a/solution.py
+++ b/solution.py
@@ -120,13 +120,13 @@
 
     operands = [*blocks, down_weight]
     in_specs = [pl.BlockSpec(memory_space=pltpu.HBM)] * len(operands)
-    out_shape = [jax.ShapeDtypeStruct((tall, cols), bf16) for tall in outs]
+    out_shape = [pltpu.HBM((tall, cols), bf16) for tall in outs]
     out_specs = [spec(tall) for tall in outs]
     aliases = {}
     if adds is not None:
         operands += adds
         in_specs += [spec(value.shape[0]) for value in adds]
-        out_shape = [jax.ShapeDtypeStruct((rows, every), bf16)]
+        out_shape = [pltpu.HBM((rows, every), bf16)]
         out_specs = [spec(rows, part * (cols // tile))]
     if into is not None:
         operands.append(into)
@@ -343,7 +343,7 @@
     sent, kept = far_terms(blocks, 1, 2, pair0)
     pair1, sum1 = pair_sum(sent, kept, *later[2:])
 
-    beside = spread_first(after(beside, pair1))
+    beside = spread_first(after(beside, *later[2:]))
     sent, kept = far_terms(later, 0, 2, pair1, *sum0)
     pair2, sum2 = pair_sum(sent, kept, *beside[1:])
 

time: 176 us -> 207 us (1.18); the launches traced: 176 us -> 205 us
  local copies, waits for them, and re-layouts: 5.95 us -> 35.6 us
  waiting for transfers between devices: 55.5 us -> 49.1 us
  Pallas kernels: 66.9 us -> 72.2 us
    unnamed x26 -> x42, local copies, waits for them, and re-layouts: 2.19 us -> 32.8 us
    ppermute x16, waiting for transfers between devices: 37.4 us -> 31.4 us  [across(): return lax.ppermute(value, 'tensor', pairs)]
    pallas_call x8, Pallas kernels: 58.2 us -> 63.4 us  [block_terms(): pl.pallas_call(functools.partial(terms_kernel, size, len(blocks), part *...]
  transfers between devices with their start and end apart: 47 -> 47, of which waited for: 24 -> 21; matrix products, arithmetic and copies ran while one was open for 6% -> 5% of each run, Pallas kernels for 32% -> 30%
where the time goes in v15:
time: 207 us; the launch traced here: 205 us
  Pallas kernels  72.2 us (35%)
  waiting for transfers between devices  49.1 us (24%)
  starting transfers between devices  37.5 us (18%)
  local copies, waits for them, and re-layouts  35.6 us (17%)
  matrix products  7.56 us (4%)
    pallas_call x8, Pallas kernels, block_terms(): pl.pallas_call(functools.partial(terms_kernel, size, len(blocks), part *...  63.4 us
    unnamed x42, local copies, waits for them, and re-layouts  32.8 us
    ppermute x16, waiting for transfers between devices, across(): return lax.ppermute(value, 'tensor', pairs)  31.4 us
    ppermute x16, starting transfers between devices, across(): return lax.ppermute(value, 'tensor', pairs)  19.6 us
    ppermute x31, starting transfers between devices, swap(): return lax.ppermute(value, 'dp', [(d, d ^ step) for d in range(size)])  17.9 us
    ppermute x31, waiting for transfers between devices, swap(): return lax.ppermute(value, 'dp', [(d, d ^ step) for d in range(size)])  17.6 us
    pallas_call x4, Pallas kernels, add_pieces(): pl.pallas_call(functools.partial(add_kernel, len(pieces)), out_shape=[jax...  5.59 us
  transfers between devices with their start and end apart: 47, of which 21 were waited for; matrix products, arithmetic and copies ran while one was open for 5% of the time, Pallas kernels for 30%

profile of v15, /device:TPU:0, one launch (start us, length us, event | category | flops | bytes accessed | tf_op | source)
XLA Modules:
  0.0 204.9 jit_solution(8706285122826787312)
XLA Ops:
  0.7 2.0 constant_dynamic-slice_fusion
  2.9 3.0 %collective-permute-start.3 = (bf16[128,512]{1,0:T(8,128)(2,1)S(1)}, bf16[128,512]{1,0:T(8,128)(2,1)S(1)}, u32[]{:S(2)}, u32[]{:S(2)}) collective-permute-start(bf16[128,512]{1,0:T(8,128)(2,1)S(1)} %get-tuple-element.141), channel_id=1, source_target_pairs={{0,2},{1,3},{2,0},{3,1},{4,6},{5,7},{6,4},{7,5},{8,10},{9,11},{10,... | collective-permute-start | bytes 393224 | tf_op jit(solution)/shard_map/ppermute | solution.py:18
  6.2 3.3 %fusion.15 = f32[256,64]{0,1:T(8,128)S(1)} fusion(bf16[256,7168]{1,0:T(8,128)(2,1)} %param.7, bf16[7168,64]{0,1:T(8,128)(2,1)S(1)} %copy-done), kind=kOutput, calls=%fused_computation.38 | convolution fusion | flops 234881024 | bytes 4653056 | tf_op jit(solution)/shard_map/dot_general | solution.py:277
  9.8 2.2 %collective-permute-done.2 = bf16[128,512]{1,0:T(8,128)(2,1)S(1)} collective-permute-done((bf16[128,512]{1,0:T(8,128)(2,1)S(1)}, bf16[128,512]{1,0:T(8,128)(2,1)S(1)}, u32[]{:S(2)}, u32[]{:S(2)}) %collective-permute-start.2) | collective-permute-done | bytes 131104 | tf_op jit(solution)/shard_map/ppermute | solution.py:18
  12.0 3.6 %collective-permute-start.6 = (bf16[256,512]{1,0:T(8,128)(2,1)S(1)}, bf16[256,512]{1,0:T(8,128)(2,1)S(1)}, u32[]{:S(2)}, u32[]{:S(2)}) collective-permute-start(bf16[256,512]{1,0:T(8,128)(2,1)S(1)} %pad_maximum_fusion.1.refs_0_), channel_id=1, source_target_pairs={{0,12},{4,8},{8,4},{12,0},{1,13},{5,9},{9,5},{13,1},{2,14},{6,10},... | collective-permute-start | bytes 786440 | tf_op jit(solution)/shard_map/ppermute | solution.py:28
  15.6 0.8 collective-permute-start.4
  16.5 0.8 collective-permute-start.1
  17.4 5.2 %collective-permute-done.1 = bf16[128,512]{1,0:T(8,128)(2,1)S(1)} collective-permute-done((bf16[128,512]{1,0:T(8,128)(2,1)S(1)}, bf16[128,512]{1,0:T(8,128)(2,1)S(1)}, u32[]{:S(2)}, u32[]{:S(2)}) %collective-permute-start.1) | collective-permute-done | bytes 131104 | tf_op jit(solution)/shard_map/ppermute | solution.py:18
  22.6 1.4 collective-permute-start.8
  24.4 14.0 %collective-permute-done.5.refs_2_ = bf16[256,512]{1,0:T(8,128)(2,1)S(1)} collective-permute-done((bf16[256,512]{1,0:T(8,128)(2,1)S(1)}, bf16[256,512]{1,0:T(8,128)(2,1)S(1)}, u32[]{:S(2)}, u32[]{:S(2)}) %collective-permute-start.5) | collective-permute-done | bytes 262176 | tf_op jit(solution)/shard_map/ppermute | solution.py:28
  38.5 3.1 %collective-permute-start.9 = (f32[256,128]{0,1:T(8,128)S(1)}, f32[256,128]{0,1:T(8,128)S(1)}, u32[]{:S(2)}, u32[]{:S(2)}) collective-permute-start(f32[256,128]{0,1:T(8,128)S(1)} %fusion.14), channel_id=1, source_target_pairs={{0,8},{4,12},{8,0},{12,4},{1,9},{5,13},{9,1},{13,5},{2,10},{6,14},... | collective-permute-start | bytes 393224 | tf_op jit(solution)/shard_map/ppermute | solution.py:28
  41.6 9.3 %copy-done.2 = bf16[4,1,512,7168]{3,2,1,0:T(8,128)(2,1)S(1)} copy-done((bf16[4,1,512,7168]{3,2,1,0:T(8,128)(2,1)S(1)}, bf16[4,1,512,7168]{3,2,1,0:T(8,128)(2,1)}, u32[]{:S(2)}) %copy-start.2) | copy-done | bytes 29360152
  50.9 7.9 %terms.8 = (bf16[64,3584]{1,0:T(8,128)(2,1)}, bf16[64,3584]{1,0:T(8,128)(2,1)}, bf16[128,3584]{1,0:T(8,128)(2,1)}) custom-call(s32[1]{0:T(128)} %bitcast.place_ref, bf16[256,512]{1,0:T(8,128)(2,1)S(1)} %pad_maximum_fusion.1.refs_0_, bf16[256,512]{1,0:T(8,128)(2,1)S(1)} %collective-permute-done.4.refs_1_, ...), custom_call_target="tpu_custom_call" | custom-call | flops 469762048 | bytes 1000 | tf_op jit(solution)/shard_map/terms/pallas_call | solution.py:135
  59.0 0.5 collective-permute-start.11
  59.5 1.5 collective-permute-done.12.refs_1_
  61.0 0.7 collective-permute-done.11.refs_0_
  61.6 1.2 copy-done.10
  62.8 0.5 pair.4
  63.3 1.4 collective-permute-start.14
  64.9 1.5 collective-permute-start.17
  66.4 8.0 %terms.9 = (bf16[64,3584]{1,0:T(8,128)(2,1)}, bf16[64,3584]{1,0:T(8,128)(2,1)}, bf16[128,3584]{1,0:T(8,128)(2,1)}) custom-call(s32[1]{0:T(128)} %bitcast.place_ref, bf16[256,512]{1,0:T(8,128)(2,1)S(1)} %pad_maximum_fusion.1.refs_0_, bf16[256,512]{1,0:T(8,128)(2,1)S(1)} %collective-permute-done.4.refs_1_, ...), custom_call_target="tpu_custom_call" | custom-call | flops 469762048 | bytes 1000 | tf_op jit(solution)/shard_map/terms/pallas_call | solution.py:135
  74.5 13.6 %collective-permute-done.13.refs_2_ = bf16[256,512]{1,0:T(8,128)(2,1)S(1)} collective-permute-done((bf16[256,512]{1,0:T(8,128)(2,1)S(1)}, bf16[256,512]{1,0:T(8,128)(2,1)S(1)}, u32[]{:S(2)}, u32[]{:S(2)}) %collective-permute-start.13) | collective-permute-done | bytes 262176 | tf_op jit(solution)/shard_map/ppermute | solution.py:28
  88.1 0.5 collective-permute-start.15
  88.6 1.5 collective-permute-done.16.refs_1_
  90.1 0.7 collective-permute-done.15.refs_0_
  90.7 1.2 copy-done.9
  91.9 1.7 pair.5
  93.6 1.5 collective-permute-start.22
  95.1 2.0 collective-permute-start.18
  97.2 8.0 %terms.10 = (bf16[64,3584]{1,0:T(8,128)(2,1)}, bf16[64,3584]{1,0:T(8,128)(2,1)}, bf16[128,3584]{1,0:T(8,128)(2,1)}) custom-call(s32[1]{0:T(128)} %bitcast.place_ref, bf16[256,512]{1,0:T(8,128)(2,1)S(1)} %pad_maximum_fusion.refs_0_, bf16[256,512]{1,0:T(8,128)(2,1)S(1)} %collective-permute-done.10.refs_1_, ...), custom_call_target="tpu_custom_call" | custom-call | flops 469762048 | bytes 1000 | tf_op jit(solution)/shard_map/terms/pallas_call | solution.py:135
  105.2 3.5 %collective-permute-done.19.refs_2_ = bf16[256,512]{1,0:T(8,128)(2,1)S(1)} collective-permute-done((bf16[256,512]{1,0:T(8,128)(2,1)S(1)}, bf16[256,512]{1,0:T(8,128)(2,1)S(1)}, u32[]{:S(2)}, u32[]{:S(2)}) %collective-permute-start.19) | collective-permute-done | bytes 262176 | tf_op jit(solution)/shard_map/ppermute | solution.py:28
  108.8 0.5 collective-permute-start.20
  109.6 1.2 collective-permute-done.21.refs_1_
  110.9 0.7 collective-permute-done.20.refs_0_
  111.5 1.2 copy-done.8
  112.7 1.8 pair.6
  114.8 2.6 %collective-permute-start.23 = (bf16[256,512]{1,0:T(8,128)(2,1)S(1)}, bf16[256,512]{1,0:T(8,128)(2,1)S(1)}, u32[]{:S(2)}, u32[]{:S(2)}) collective-permute-start(bf16[256,512]{1,0:T(8,128)(2,1)S(1)} %bitcast.39), channel_id=1, source_target_pairs={{0,8},{4,12},{8,0},{12,4},{1,9},{5,13},{9,1},{13,5},{2,10},{6,14},... | collective-permute-start | bytes 786440 | tf_op jit(solution)/shard_map/ppermute | solution.py:28
  117.4 0.5 collective-permute-start.31
  117.9 0.7 collective-permute-start.25
  118.6 1.3 collective-permute-start.26
  119.9 1.0 add.30
  121.5 9.3 %copy-done.3 = bf16[4,1,512,7168]{3,2,1,0:T(8,128)(2,1)S(1)} copy-done((bf16[4,1,512,7168]{3,2,1,0:T(8,128)(2,1)S(1)}, bf16[4,1,512,7168]{3,2,1,0:T(8,128)(2,1)}, u32[]{:S(2)}) %copy-start.3) | copy-done | bytes 29360152
  130.9 7.9 %terms.11 = (bf16[32,3584]{1,0:T(8,128)(2,1)}, bf16[32,3584]{1,0:T(8,128)(2,1)}, bf16[32,3584]{1,0:T(8,128)(2,1)}, bf16[32,3584]{1,0:T(8,128)(2,1)}, bf16[128,3584]{1,0:T(8,128)(2,1)}) custom-call(s32[1]{0:T(128)} %bitcast.place_ref, bf16[256,512]{1,0:T(8,128)(2,1)S(1)} %pad_maximum_fusion.refs_0_, bf16[256,512]{1,0:T(8,128)(2,1)S(1)} %collective-permute-done.10.refs_1_, ...), custom_call_target="tpu_custom_call" | custom-call | flops 469762048 | bytes 1000 | tf_op jit(solution)/shard_map/terms/pallas_call | solution.py:135
  139.9 0.7 collective-permute-done.30.refs_3_
  141.6 1.2 copy-done.5
  142.8 1.6 pair.7
  144.4 1.5 collective-permute-start.32
  145.8 0.7 collective-permute-start.37
  146.5 1.5 collective-permute-start.38
  148.0 0.6 collective-permute-start.42
  148.6 9.3 %copy-done.4 = bf16[4,1,512,7168]{3,2,1,0:T(8,128)(2,1)S(1)} copy-done((bf16[4,1,512,7168]{3,2,1,0:T(8,128)(2,1)S(1)}, bf16[4,1,512,7168]{3,2,1,0:T(8,128)(2,1)}, u32[]{:S(2)}) %copy-start.4) | copy-done | bytes 29360152
  158.0 8.0 %terms.12 = (bf16[64,3584]{1,0:T(8,128)(2,1)}, bf16[64,3584]{1,0:T(8,128)(2,1)}, bf16[64,3584]{1,0:T(8,128)(2,1)}, bf16[64,3584]{1,0:T(8,128)(2,1)}) custom-call(s32[1]{0:T(128)} %bitcast.place_ref, bf16[256,512]{1,0:T(8,128)(2,1)S(1)} %collective-permute-done.7.refs_0_, bf16[256,512]{1,0:T(8,128)(2,1)S(1)} %collective-permute-done.18.refs_1_, ...), custom_call_target="tpu_custom_call" | custom-call | flops 469762048 | bytes 1000 | tf_op jit(solution)/shard_map/terms/pallas_call | solution.py:135
  166.1 1.6 collective-permute-start.36
  168.0 1.5 collective-permute-start.35
  169.5 8.0 %terms.13 = (bf16[64,3584]{1,0:T(8,128)(2,1)}, bf16[64,3584]{1,0:T(8,128)(2,1)}, bf16[64,3584]{1,0:T(8,128)(2,1)}, bf16[64,3584]{1,0:T(8,128)(2,1)}) custom-call(s32[1]{0:T(128)} %bitcast.place_ref, bf16[256,512]{1,0:T(8,128)(2,1)S(1)} %collective-permute-done.7.refs_0_, bf16[256,512]{1,0:T(8,128)(2,1)S(1)} %collective-permute-done.18.refs_1_, ...), custom_call_target="tpu_custom_call" | custom-call | flops 469762048 | bytes 1000 | tf_op jit(solution)/shard_map/terms/pallas_call | solution.py:135
  177.5 0.6 collective-permute-start.41
  179.9 0.9 collective-permute-done.40.refs_2_
  181.2 0.9 collective-permute-done.39.refs_1_
  182.1 1.7 sums.2.refs_6_
  183.8 7.7 %terms.14.refs_9_ = bf16[256,7168]{1,0:T(8,128)(2,1)} custom-call(s32[1]{0:T(128)} %bitcast.place_ref, bf16[256,512]{1,0:T(8,128)(2,1)S(1)} %bitcast.41, bf16[256,512]{1,0:T(8,128)(2,1)S(1)} %collective-permute-done.24.refs_1_, bf16[256,512]{1,0:T(8,128)(2,1)S(1)} %collective-permute-done.23.refs_2_, bf16[256,512]{1,0:T(8,128)(2,1)S(1)} %collective-permute-done.37.refs_3_, ...), custom_call_target="tpu_custom_call" | custom-call | flops 469762048 | bytes 1000 | tf_op jit(solution)/shard_map/terms/pallas_call | solution.py:135
  191.5 2.8 %fusion.4 = f32[1024,1024]{1,0:T(8,128)} fusion(bf16[16,4224]{1,0:T(8,128)(2,1)S(1)} %pad_maximum_fusion.2, s32[]{:T(128)S(6)} %select_n.121, s32[]{:T(128)S(6)} %select_n.122), kind=kOutput, calls=%fused_computation.20 | convolution fusion | flops 33554432 | bytes 4259848 | tf_op jit(solution)/shard_map/dot_general | solution.py:266
  194.3 0.9 fusion.6
  195.2 1.5 sums.3.refs_6_
  196.7 8.0 %terms.15 = bf16[256,7168]{1,0:T(8,128)(2,1)} custom-call(s32[1]{0:T(128)} %bitcast.place_ref, bf16[256,512]{1,0:T(8,128)(2,1)S(1)} %bitcast.42, bf16[256,512]{1,0:T(8,128)(2,1)S(1)} %collective-permute-done.24.refs_1_, bf16[256,512]{1,0:T(8,128)(2,1)S(1)} %collective-permute-done.23.refs_2_, ...), custom_call_target="tpu_custom_call", output_to_operand_aliasing={{}: (10, {})} | custom-call | flops 469762048 | bytes 1000 | tf_op jit(solution)/shard_map/terms/pallas_call | solution.py:135
  (115 shorter events, 7.6 us)
Async XLA Ops:
  0.6 5.5 %copy-start = (bf16[7168,64]{0,1:T(8,128)(2,1)S(1)}, bf16[7168,64]{0,1:T(8,128)(2,1)}, u32[]{:S(2)}) copy-start(bf16[7168,64]{0,1:T(8,128)(2,1)} %param.10) | copy-start | bytes 2752516
  2.7 6.7 %copy-start.11 = (bf16[1,4,512,256]{3,2,1,0:T(8,128)(2,1)S(1)}, bf16[1,4,512,256]{3,2,1,0:T(8,128)(2,1)}, u32[]{:S(2)}) copy-start(bf16[1,4,512,256]{3,2,1,0:T(8,128)(2,1)} %param.8) | copy-start | bytes 3145732
  2.7 6.7 %copy-start.14 = (bf16[1,4,512,64]{2,3,1,0:T(8,128)(2,1)S(1)}, bf16[1,4,512,64]{2,3,1,0:T(8,128)(2,1)}, u32[]{:S(2)}) copy-start(bf16[1,4,512,64]{2,3,1,0:T(8,128)(2,1)} %param.11) | copy-start | bytes 786436
  2.9 6.9 %collective-permute-start.3 = (bf16[128,512]{1,0:T(8,128)(2,1)S(1)}, bf16[128,512]{1,0:T(8,128)(2,1)S(1)}, u32[]{:S(2)}, u32[]{:S(2)}) collective-permute-start(bf16[128,512]{1,0:T(8,128)(2,1)S(1)} %get-tuple-element.141), channel_id=1, source_target_pairs={{0,2},{1,3},{2,0},{3,1},{4,6},{5,7},{6,4},{7,5},{8,10},{9,11},{10,... | collective-permute-start | bytes 393224 | tf_op jit(solution)/shard_map/ppermute | solution.py:18
  6.1 5.9 %collective-permute-start.2 = (bf16[128,512]{1,0:T(8,128)(2,1)S(1)}, bf16[128,512]{1,0:T(8,128)(2,1)S(1)}, u32[]{:S(2)}, u32[]{:S(2)}) collective-permute-start(bf16[128,512]{1,0:T(8,128)(2,1)S(1)} %get-tuple-element.139), channel_id=1, source_target_pairs={{0,3},{1,2},{2,1},{3,0},{4,7},{5,6},{6,5},{7,4},{8,11},{9,10},{10,... | collective-permute-start | bytes 393224 | tf_op jit(solution)/shard_map/ppermute | solution.py:18
  12.0 12.4 %collective-permute-start.6 = (bf16[256,512]{1,0:T(8,128)(2,1)S(1)}, bf16[256,512]{1,0:T(8,128)(2,1)S(1)}, u32[]{:S(2)}, u32[]{:S(2)}) collective-permute-start(bf16[256,512]{1,0:T(8,128)(2,1)S(1)} %pad_maximum_fusion.1.refs_0_), channel_id=1, source_target_pairs={{0,12},{4,8},{8,4},{12,0},{1,13},{5,9},{9,5},{13,1},{2,14},{6,10},... | collective-permute-start | bytes 786440 | tf_op jit(solution)/shard_map/ppermute | solution.py:28
  15.6 22.8 %collective-permute-start.5 = (bf16[256,512]{1,0:T(8,128)(2,1)S(1)}, bf16[256,512]{1,0:T(8,128)(2,1)S(1)}, u32[]{:S(2)}, u32[]{:S(2)}) collective-permute-start(bf16[256,512]{1,0:T(8,128)(2,1)S(1)} %pad_maximum_fusion.1.refs_0_), channel_id=1, source_target_pairs={{0,8},{4,12},{8,0},{12,4},{1,9},{5,13},{9,1},{13,5},{2,10},{6,14},... | collective-permute-start | bytes 786440 | tf_op jit(solution)/shard_map/ppermute | solution.py:28
  15.6 22.8 %collective-permute-start.4 = (bf16[256,512]{1,0:T(8,128)(2,1)S(1)}, bf16[256,512]{1,0:T(8,128)(2,1)S(1)}, u32[]{:S(2)}, u32[]{:S(2)}) collective-permute-start(bf16[256,512]{1,0:T(8,128)(2,1)S(1)} %pad_maximum_fusion.1.refs_0_), channel_id=1, source_target_pairs={{0,4},{4,0},{8,12},{12,8},{1,5},{5,1},{9,13},{13,9},{2,6},{6,2},{1... | collective-permute-start | bytes 786440 | tf_op jit(solution)/shard_map/ppermute | solution.py:28
  16.5 6.2 %collective-permute-start.1 = (bf16[128,512]{1,0:T(8,128)(2,1)S(1)}, bf16[128,512]{1,0:T(8,128)(2,1)S(1)}, u32[]{:S(2)}, u32[]{:S(2)}) collective-permute-start(bf16[128,512]{1,0:T(8,128)(2,1)S(1)} %get-tuple-element.142), channel_id=1, source_target_pairs={{0,2},{1,3},{2,0},{3,1},{4,6},{5,7},{6,4},{7,5},{8,10},{9,11},{10,... | collective-permute-start | bytes 393224 | tf_op jit(solution)/shard_map/ppermute | solution.py:18
  17.3 7.0 %collective-permute-start = (bf16[128,512]{1,0:T(8,128)(2,1)S(1)}, bf16[128,512]{1,0:T(8,128)(2,1)S(1)}, u32[]{:S(2)}, u32[]{:S(2)}) collective-permute-start(bf16[128,512]{1,0:T(8,128)(2,1)S(1)} %get-tuple-element.140), channel_id=1, source_target_pairs={{0,3},{1,2},{2,1},{3,0},{4,7},{5,6},{6,5},{7,4},{8,11},{9,10},{10,... | collective-permute-start | bytes 393224 | tf_op jit(solution)/shard_map/ppermute | solution.py:18
  22.6 15.8 %collective-permute-start.8 = (f32[256,128]{0,1:T(8,128)S(1)}, f32[256,128]{0,1:T(8,128)S(1)}, u32[]{:S(2)}, u32[]{:S(2)}) collective-permute-start(f32[256,128]{0,1:T(8,128)S(1)} %pad_maximum_fusion.3), channel_id=1, source_target_pairs={{0,4},{4,0},{8,12},{12,8},{1,5},{5,1},{9,13},{13,9},{2,6},{6,2},{1... | collective-permute-start | bytes 393224 | tf_op jit(solution)/shard_map/ppermute | solution.py:28
  24.2 17.4 %collective-permute-start.7 = (bf16[256,512]{1,0:T(8,128)(2,1)S(1)}, bf16[256,512]{1,0:T(8,128)(2,1)S(1)}, u32[]{:S(2)}, u32[]{:S(2)}) collective-permute-start(bf16[256,512]{1,0:T(8,128)(2,1)S(1)} %bitcast.46), channel_id=1, source_target_pairs={{0,1},{1,0},{2,3},{3,2},{4,5},{5,4},{6,7},{7,6},{8,9},{9,8},{10,11... | collective-permute-start | bytes 786440 | tf_op jit(solution)/shard_map/ppermute | solution.py:18
  38.4 20.4 %collective-permute-start.10 = (bf16[256,512]{1,0:T(8,128)(2,1)S(1)}, bf16[256,512]{1,0:T(8,128)(2,1)S(1)}, u32[]{:S(2)}, u32[]{:S(2)}) collective-permute-start(bf16[256,512]{1,0:T(8,128)(2,1)S(1)} %pad_maximum_fusion.refs_0_), channel_id=1, source_target_pairs={{0,4},{4,0},{8,12},{12,8},{1,5},{5,1},{9,13},{13,9},{2,6},{6,2},{1... | collective-permute-start | bytes 786440 | tf_op jit(solution)/shard_map/ppermute | solution.py:28
  38.5 20.4 %copy-start.13 = (f32[256,128]{0,1:T(8,128)}, f32[256,128]{0,1:T(8,128)S(1)}, u32[]{:S(2)}) copy-start(f32[256,128]{0,1:T(8,128)S(1)} %fusion.14) | copy-start | bytes 393220
  38.5 20.4 %collective-permute-start.9 = (f32[256,128]{0,1:T(8,128)S(1)}, f32[256,128]{0,1:T(8,128)S(1)}, u32[]{:S(2)}, u32[]{:S(2)}) collective-permute-start(f32[256,128]{0,1:T(8,128)S(1)} %fusion.14), channel_id=1, source_target_pairs={{0,8},{4,12},{8,0},{12,4},{1,9},{5,13},{9,1},{13,5},{2,10},{6,14},... | collective-permute-start | bytes 393224 | tf_op jit(solution)/shard_map/ppermute | solution.py:28
  41.6 9.4 %copy-start.2 = (bf16[4,1,512,7168]{3,2,1,0:T(8,128)(2,1)S(1)}, bf16[4,1,512,7168]{3,2,1,0:T(8,128)(2,1)}, u32[]{:S(2)}) copy-start(bf16[4,1,512,7168]{3,2,1,0:T(8,128)(2,1)} %refs_5_.7) | copy-start | bytes 88080384
  58.9 15.5 %copy-start.15 = (f32[256,128]{0,1:T(8,128)}, f32[256,128]{0,1:T(8,128)S(1)}, u32[]{:S(2)}) copy-start(f32[256,128]{0,1:T(8,128)S(1)} %collective-permute-done.9) | copy-start | bytes 393220
  58.9 2.1 %collective-permute-start.12 = (bf16[64,3584]{1,0:T(8,128)(2,1)}, bf16[64,3584]{1,0:T(8,128)(2,1)S(1)}, u32[]{:S(2)}, u32[]{:S(2)}) collective-permute-start(bf16[64,3584]{1,0:T(8,128)(2,1)} %get-tuple-element.77), channel_id=1, source_target_pairs={{0,1},{1,0},{2,3},{3,2},{4,5},{5,4},{6,7},{7,6},{8,9},{9,8},{10,11... | collective-permute-start | bytes 1376264 | tf_op jit(solution)/shard_map/ppermute | solution.py:18
  59.0 2.7 %collective-permute-start.11 = (bf16[64,3584]{1,0:T(8,128)(2,1)}, bf16[64,3584]{1,0:T(8,128)(2,1)S(1)}, u32[]{:S(2)}, u32[]{:S(2)}) collective-permute-start(bf16[64,3584]{1,0:T(8,128)(2,1)} %get-tuple-element.75), channel_id=1, source_target_pairs={{0,1},{1,0},{2,3},{3,2},{4,5},{5,4},{6,7},{7,6},{8,9},{9,8},{10,11... | collective-permute-start | bytes 1376264 | tf_op jit(solution)/shard_map/ppermute | solution.py:18
  63.3 11.1 %collective-permute-start.14 = (bf16[256,512]{1,0:T(8,128)(2,1)S(1)}, bf16[256,512]{1,0:T(8,128)(2,1)S(1)}, u32[]{:S(2)}, u32[]{:S(2)}) collective-permute-start(bf16[256,512]{1,0:T(8,128)(2,1)S(1)} %pad_maximum_fusion.refs_0_), channel_id=1, source_target_pairs={{0,12},{4,8},{8,4},{12,0},{1,13},{5,9},{9,5},{13,1},{2,14},{6,10},... | collective-permute-start | bytes 786440 | tf_op jit(solution)/shard_map/ppermute | solution.py:28
  64.8 23.3 %collective-permute-start.13 = (bf16[256,512]{1,0:T(8,128)(2,1)S(1)}, bf16[256,512]{1,0:T(8,128)(2,1)S(1)}, u32[]{:S(2)}, u32[]{:S(2)}) collective-permute-start(bf16[256,512]{1,0:T(8,128)(2,1)S(1)} %pad_maximum_fusion.refs_0_), channel_id=1, source_target_pairs={{0,8},{4,12},{8,0},{12,4},{1,9},{5,13},{9,1},{13,5},{2,10},{6,14},... | collective-permute-start | bytes 786440 | tf_op jit(solution)/shard_map/ppermute | solution.py:28
  64.9 32.3 %collective-permute-start.17 = (bf16[128,3584]{1,0:T(8,128)(2,1)S(1)}, bf16[128,3584]{1,0:T(8,128)(2,1)S(1)}, u32[]{:S(2)}, u32[]{:S(2)}) collective-permute-start(bf16[128,3584]{1,0:T(8,128)(2,1)S(1)} %pair.4), channel_id=1, source_target_pairs={{0,2},{1,3},{2,0},{3,1},{4,6},{5,7},{6,4},{7,5},{8,10},{9,11},{10,... | collective-permute-start | bytes 2752520 | tf_op jit(solution)/shard_map/ppermute | solution.py:18
  88.1 2.0 collective-permute-start.16
  88.1 2.7 %collective-permute-start.15 = (bf16[64,3584]{1,0:T(8,128)(2,1)}, bf16[64,3584]{1,0:T(8,128)(2,1)S(1)}, u32[]{:S(2)}, u32[]{:S(2)}) collective-permute-start(bf16[64,3584]{1,0:T(8,128)(2,1)} %get-tuple-element.82), channel_id=1, source_target_pairs={{0,1},{1,0},{2,3},{3,2},{4,5},{5,4},{6,7},{7,6},{8,9},{9,8},{10,11... | collective-permute-start | bytes 1376264 | tf_op jit(solution)/shard_map/ppermute | solution.py:18
  93.6 15.7 %copy-start.12 = (bf16[1,1,512,256]{3,2,1,0:T(8,128)(2,1)S(1)}, bf16[1,1,512,256]{3,2,1,0:T(8,128)(2,1)}, u32[]{:S(2)}) copy-start(bf16[1,1,512,256]{3,2,1,0:T(8,128)(2,1)} %get-tuple-element.138) | copy-start | bytes 786436
  93.6 15.9 %copy-start.16 = (s32[1,256]{1,0:T(1,128)S(1)}, s32[1,256]{1,0:T(1,128)}, u32[]{:S(2)}) copy-start(s32[1,256]{1,0:T(1,128)} %param.12) | copy-start | bytes 3076
  93.6 25.0 %collective-permute-start.22 = (bf16[128,3584]{1,0:T(8,128)(2,1)}, bf16[128,3584]{1,0:T(8,128)(2,1)}, u32[]{:S(2)}, u32[]{:S(2)}) collective-permute-start(bf16[128,3584]{1,0:T(8,128)(2,1)} %pair.5), channel_id=1, source_target_pairs={{0,2},{1,3},{2,0},{3,1},{4,6},{5,7},{6,4},{7,5},{8,10},{9,11},{10,... | collective-permute-start | bytes 2752520 | tf_op jit(solution)/shard_map/ppermute | solution.py:18
  95.1 13.5 %collective-permute-start.19 = (bf16[256,512]{1,0:T(8,128)(2,1)S(1)}, bf16[256,512]{1,0:T(8,128)(2,1)S(1)}, u32[]{:S(2)}, u32[]{:S(2)}) collective-permute-start(bf16[256,512]{1,0:T(8,128)(2,1)S(1)} %collective-permute-done.7.refs_0_), channel_id=1, source_target_pairs={{0,8},{4,12},{8,0},{12,4},{1,9},{5,13},{9,1},{13,5},{2,10},{6,14},... | collective-permute-start | bytes 786440 | tf_op jit(solution)/shard_map/ppermute | solution.py:28
  95.1 13.7 %collective-permute-start.18 = (bf16[256,512]{1,0:T(8,128)(2,1)S(1)}, bf16[256,512]{1,0:T(8,128)(2,1)S(1)}, u32[]{:S(2)}, u32[]{:S(2)}) collective-permute-start(bf16[256,512]{1,0:T(8,128)(2,1)S(1)} %collective-permute-done.7.refs_0_), channel_id=1, source_target_pairs={{0,4},{4,0},{8,12},{12,8},{1,5},{5,1},{9,13},{13,9},{2,6},{6,2},{1... | collective-permute-start | bytes 786440 | tf_op jit(solution)/shard_map/ppermute | solution.py:28
  97.2 8.0 %copy-start.6 = (bf16[128,3584]{1,0:T(8,128)(2,1)}, bf16[128,3584]{1,0:T(8,128)(2,1)S(1)}, u32[]{:S(2)}) copy-start(bf16[128,3584]{1,0:T(8,128)(2,1)S(1)} %collective-permute-done.17.refs_4_) | copy-start | bytes 2752516
  108.8 2.0 collective-permute-start.21
  108.8 2.7 %collective-permute-start.20 = (bf16[64,3584]{1,0:T(8,128)(2,1)}, bf16[64,3584]{1,0:T(8,128)(2,1)S(1)}, u32[]{:S(2)}, u32[]{:S(2)}) collective-permute-start(bf16[64,3584]{1,0:T(8,128)(2,1)} %get-tuple-element.89), channel_id=1, source_target_pairs={{0,1},{1,0},{2,3},{3,2},{4,5},{5,4},{6,7},{7,6},{8,9},{9,8},{10,11... | collective-permute-start | bytes 1376264 | tf_op jit(solution)/shard_map/ppermute | solution.py:18
  114.5 24.3 %collective-permute-start.24 = (bf16[256,512]{1,0:T(8,128)(2,1)S(1)}, bf16[256,512]{1,0:T(8,128)(2,1)S(1)}, u32[]{:S(2)}, u32[]{:S(2)}) collective-permute-start(bf16[256,512]{1,0:T(8,128)(2,1)S(1)} %bitcast.38), channel_id=1, source_target_pairs={{0,4},{4,0},{8,12},{12,8},{1,5},{5,1},{9,13},{13,9},{2,6},{6,2},{1... | collective-permute-start | bytes 786440 | tf_op jit(solution)/shard_map/ppermute | solution.py:28
  114.8 24.7 %collective-permute-start.23 = (bf16[256,512]{1,0:T(8,128)(2,1)S(1)}, bf16[256,512]{1,0:T(8,128)(2,1)S(1)}, u32[]{:S(2)}, u32[]{:S(2)}) collective-permute-start(bf16[256,512]{1,0:T(8,128)(2,1)S(1)} %bitcast.39), channel_id=1, source_target_pairs={{0,8},{4,12},{8,0},{12,4},{1,9},{5,13},{9,1},{13,5},{2,10},{6,14},... | collective-permute-start | bytes 786440 | tf_op jit(solution)/shard_map/ppermute | solution.py:28
  117.4 31.2 %collective-permute-start.31 = (bf16[128,3584]{1,0:T(8,128)(2,1)}, bf16[128,3584]{1,0:T(8,128)(2,1)}, u32[]{:S(2)}, u32[]{:S(2)}) collective-permute-start(bf16[128,3584]{1,0:T(8,128)(2,1)} %pair.6), channel_id=1, source_target_pairs={{0,2},{1,3},{2,0},{3,1},{4,6},{5,7},{6,4},{7,5},{8,10},{9,11},{10,... | collective-permute-start | bytes 2752520 | tf_op jit(solution)/shard_map/ppermute | solution.py:18
  117.9 20.9 %collective-permute-start.25 = (bf16[256,512]{1,0:T(8,128)(2,1)S(1)}, bf16[256,512]{1,0:T(8,128)(2,1)S(1)}, u32[]{:S(2)}, u32[]{:S(2)}) collective-permute-start(bf16[256,512]{1,0:T(8,128)(2,1)S(1)} %collective-permute-done.7.refs_0_), channel_id=1, source_target_pairs={{4,8},{8,4},{5,9},{9,5},{6,10},{10,6},{7,11},{11,7},{20,24},{24,20... | collective-permute-start | bytes 786440 | tf_op jit(solution)/shard_map/ppermute | solution.py:28
  118.6 20.2 %collective-permute-start.26 = (bf16[256,512]{1,0:T(8,128)(2,1)S(1)}, bf16[256,512]{1,0:T(8,128)(2,1)S(1)}, u32[]{:S(2)}, u32[]{:S(2)}) collective-permute-start(bf16[256,512]{1,0:T(8,128)(2,1)S(1)} %collective-permute-done.19.refs_2_), channel_id=1, source_target_pairs={{4,0},{8,12},{5,1},{9,13},{6,2},{10,14},{7,3},{11,15},{20,16},{24,... | collective-permute-start | bytes 786440 | tf_op jit(solution)/shard_map/ppermute | solution.py:28
  121.5 9.4 %copy-start.3 = (bf16[4,1,512,7168]{3,2,1,0:T(8,128)(2,1)S(1)}, bf16[4,1,512,7168]{3,2,1,0:T(8,128)(2,1)}, u32[]{:S(2)}) copy-start(bf16[4,1,512,7168]{3,2,1,0:T(8,128)(2,1)} %refs_5_.7) | copy-start | bytes 88080384
  130.8 15.0 %copy-start.20 = (s32[4]{0:T(128)S(1)}, s32[4]{0:T(128)}, u32[]{:S(2)}) copy-start(s32[4]{0:T(128)} %param.13) | copy-start | bytes 52
  138.8 1.8 collective-permute-start.30
  138.9 2.0 collective-permute-start.29
  139.4 1.8 collective-permute-start.28
  139.5 2.1 %collective-permute-start.27 = (bf16[32,3584]{1,0:T(8,128)(2,1)}, bf16[32,3584]{1,0:T(8,128)(2,1)S(1)}, u32[]{:S(2)}, u32[]{:S(2)}) collective-permute-start(bf16[32,3584]{1,0:T(8,128)(2,1)} %get-tuple-element.100), channel_id=1, source_target_pairs={{0,1},{1,0},{2,3},{3,2},{4,5},{5,4},{6,7},{7,6},{8,9},{9,8},{10,11... | collective-permute-start | bytes 688136 | tf_op jit(solution)/shard_map/ppermute | solution.py:18
  144.4 21.6 %collective-permute-start.32 = (bf16[64,3584]{1,0:T(8,128)(2,1)}, bf16[64,3584]{1,0:T(8,128)(2,1)S(1)}, u32[]{:S(2)}, u32[]{:S(2)}) collective-permute-start(bf16[64,3584]{1,0:T(8,128)(2,1)} %get-tuple-element.107), channel_id=1, source_target_pairs={{0,2},{1,3},{2,0},{3,1},{4,6},{5,7},{6,4},{7,5},{8,10},{9,11},{10,... | collective-permute-start | bytes 1376264 | tf_op jit(solution)/shard_map/ppermute | solution.py:18
  145.8 23.7 %collective-permute-start.37 = (bf16[256,512]{1,0:T(8,128)(2,1)S(1)}, bf16[256,512]{1,0:T(8,128)(2,1)S(1)}, u32[]{:S(2)}, u32[]{:S(2)}) collective-permute-start(bf16[256,512]{1,0:T(8,128)(2,1)S(1)} %bitcast.40), channel_id=1, source_target_pairs={{4,8},{8,4},{5,9},{9,5},{6,10},{10,6},{7,11},{11,7},{20,24},{24,20... | collective-permute-start | bytes 786440 | tf_op jit(solution)/shard_map/ppermute | solution.py:28
  146.5 31.0 %collective-permute-start.38 = (bf16[256,512]{1,0:T(8,128)(2,1)S(1)}, bf16[256,512]{1,0:T(8,128)(2,1)S(1)}, u32[]{:S(2)}, u32[]{:S(2)}) collective-permute-start(bf16[256,512]{1,0:T(8,128)(2,1)S(1)} %collective-permute-done.23.refs_2_), channel_id=1, source_target_pairs={{4,0},{8,12},{5,1},{9,13},{6,2},{10,14},{7,3},{11,15},{20,16},{24,... | collective-permute-start | bytes 786440 | tf_op jit(solution)/shard_map/ppermute | solution.py:28
  148.0 30.1 %collective-permute-start.42 = (bf16[64,3584]{1,0:T(8,128)(2,1)S(1)}, bf16[64,3584]{1,0:T(8,128)(2,1)S(1)}, u32[]{:S(2)}, u32[]{:S(2)}) collective-permute-start(bf16[64,3584]{1,0:T(8,128)(2,1)S(1)} %get-tuple-element.127), channel_id=1, source_target_pairs={{0,2},{1,3},{2,0},{3,1},{4,6},{5,7},{6,4},{7,5},{8,10},{9,11},{10,... | collective-permute-start | bytes 1376264 | tf_op jit(solution)/shard_map/ppermute | solution.py:18
  148.6 9.4 %copy-start.4 = (bf16[4,1,512,7168]{3,2,1,0:T(8,128)(2,1)S(1)}, bf16[4,1,512,7168]{3,2,1,0:T(8,128)(2,1)}, u32[]{:S(2)}) copy-start(bf16[4,1,512,7168]{3,2,1,0:T(8,128)(2,1)} %refs_5_.7) | copy-start | bytes 88080384
  165.9 2.1 %collective-permute-start.33 = (bf16[64,3584]{1,0:T(8,128)(2,1)}, bf16[64,3584]{1,0:T(8,128)(2,1)S(1)}, u32[]{:S(2)}, u32[]{:S(2)}) collective-permute-start(bf16[64,3584]{1,0:T(8,128)(2,1)} %get-tuple-element.110), channel_id=1, source_target_pairs={{0,1},{1,0},{2,3},{3,2},{4,5},{5,4},{6,7},{7,6},{8,9},{9,8},{10,11... | collective-permute-start | bytes 1376264 | tf_op jit(solution)/shard_map/ppermute | solution.py:18
  166.1 12.0 %collective-permute-start.36 = (bf16[4,4224]{1,0:T(4,128)(2,1)S(1)}, bf16[4,4224]{1,0:T(4,128)(2,1)S(1)}, u32[]{:S(2)}, u32[]{:S(2)}) collective-permute-start(bf16[4,4224]{1,0:T(4,128)(2,1)S(1)} %pad_maximum_fusion.4), channel_id=1, source_target_pairs={{0,3},{1,2},{2,1},{3,0},{4,7},{5,6},{6,5},{7,4},{8,11},{9,10},{10,... | collective-permute-start | bytes 101384 | tf_op jit(solution)/shard_map/ppermute | solution.py:18
  167.8 9.7 %copy-start.19 = (bf16[64,3584]{1,0:T(8,128)(2,1)S(1)}, bf16[64,3584]{1,0:T(8,128)(2,1)}, u32[]{:S(2)}) copy-start(bf16[64,3584]{1,0:T(8,128)(2,1)} %get-tuple-element.125) | copy-start | bytes 1376260
  167.8 10.3 %copy-start.18 = (bf16[64,3584]{1,0:T(8,128)(2,1)S(1)}, bf16[64,3584]{1,0:T(8,128)(2,1)}, u32[]{:S(2)}) copy-start(bf16[64,3584]{1,0:T(8,128)(2,1)} %get-tuple-element.123) | copy-start | bytes 1376260
  167.8 10.4 %copy-start.17 = (bf16[64,3584]{1,0:T(8,128)(2,1)S(1)}, bf16[64,3584]{1,0:T(8,128)(2,1)}, u32[]{:S(2)}) copy-start(bf16[64,3584]{1,0:T(8,128)(2,1)} %get-tuple-element.121) | copy-start | bytes 1376260
  167.8 14.4 %copy-start.7 = (bf16[128,3584]{1,0:T(8,128)(2,1)S(1)}, bf16[128,3584]{1,0:T(8,128)(2,1)}, u32[]{:S(2)}) copy-start(bf16[128,3584]{1,0:T(8,128)(2,1)} %copy-done.6) | copy-start | bytes 2752516
  168.0 10.5 %collective-permute-start.35 = (bf16[4,4224]{1,0:T(4,128)(2,1)S(1)}, bf16[4,4224]{1,0:T(4,128)(2,1)S(1)}, u32[]{:S(2)}, u32[]{:S(2)}) collective-permute-start(bf16[4,4224]{1,0:T(4,128)(2,1)S(1)} %pad_maximum_fusion.4), channel_id=1, source_target_pairs={{0,2},{1,3},{2,0},{3,1},{4,6},{5,7},{6,4},{7,5},{8,10},{9,11},{10,... | collective-permute-start | bytes 101384 | tf_op jit(solution)/shard_map/ppermute | solution.py:18
  169.5 9.1 %collective-permute-start.34 = (bf16[4,4224]{1,0:T(4,128)(2,1)S(1)}, bf16[4,4224]{1,0:T(4,128)(2,1)S(1)}, u32[]{:S(2)}, u32[]{:S(2)}) collective-permute-start(bf16[4,4224]{1,0:T(4,128)(2,1)S(1)} %pad_maximum_fusion.4), channel_id=1, source_target_pairs={{0,1},{1,0},{2,3},{3,2},{4,5},{5,4},{6,7},{7,6},{8,9},{9,8},{10,11... | collective-permute-start | bytes 101384 | tf_op jit(solution)/shard_map/ppermute | solution.py:18
  177.5 2.0 collective-permute-start.41
  178.1 2.7 %collective-permute-start.40 = (bf16[64,3584]{1,0:T(8,128)(2,1)S(1)}, bf16[64,3584]{1,0:T(8,128)(2,1)S(1)}, u32[]{:S(2)}, u32[]{:S(2)}) collective-permute-start(bf16[64,3584]{1,0:T(8,128)(2,1)S(1)} %copy-done.18), channel_id=1, source_target_pairs={{0,1},{1,0},{2,3},{3,2},{4,5},{5,4},{6,7},{7,6},{8,9},{9,8},{10,11... | collective-permute-start | bytes 1376264 | tf_op jit(solution)/shard_map/ppermute | solution.py:18
  178.2 4.0 %collective-permute-start.39 = (bf16[64,3584]{1,0:T(8,128)(2,1)S(1)}, bf16[64,3584]{1,0:T(8,128)(2,1)S(1)}, u32[]{:S(2)}, u32[]{:S(2)}) collective-permute-start(bf16[64,3584]{1,0:T(8,128)(2,1)S(1)} %copy-done.17), channel_id=1, source_target_pairs={{0,1},{1,0},{2,3},{3,2},{4,5},{5,4},{6,7},{7,6},{8,9},{9,8},{10,11... | collective-permute-start | bytes 1376264 | tf_op jit(solution)/shard_map/ppermute | solution.py:18
  178.6 16.6 %collective-permute-start.43 = (bf16[64,3584]{1,0:T(8,128)(2,1)}, bf16[64,3584]{1,0:T(8,128)(2,1)S(1)}, u32[]{:S(2)}, u32[]{:S(2)}) collective-permute-start(bf16[64,3584]{1,0:T(8,128)(2,1)} %get-tuple-element.128), channel_id=1, source_target_pairs={{0,1},{1,0},{2,3},{3,2},{4,5},{5,4},{6,7},{7,6},{8,9},{9,8},{10,11... | collective-permute-start | bytes 1376264 | tf_op jit(solution)/shard_map/ppermute | solution.py:18
  178.7 16.5 %collective-permute-start.46 = (bf16[64,3584]{1,0:T(8,128)(2,1)}, bf16[64,3584]{1,0:T(8,128)(2,1)S(1)}, u32[]{:S(2)}, u32[]{:S(2)}) collective-permute-start(bf16[64,3584]{1,0:T(8,128)(2,1)} %get-tuple-element.134), channel_id=1, source_target_pairs={{0,1},{1,0},{2,3},{3,2},{4,5},{5,4},{6,7},{7,6},{8,9},{9,8},{10,11... | collective-permute-start | bytes 1376264 | tf_op jit(solution)/shard_map/ppermute | solution.py:18
  179.5 15.7 %collective-permute-start.45 = (bf16[64,3584]{1,0:T(8,128)(2,1)}, bf16[64,3584]{1,0:T(8,128)(2,1)S(1)}, u32[]{:S(2)}, u32[]{:S(2)}) collective-permute-start(bf16[64,3584]{1,0:T(8,128)(2,1)} %get-tuple-element.132), channel_id=1, source_target_pairs={{0,1},{1,0},{2,3},{3,2},{4,5},{5,4},{6,7},{7,6},{8,9},{9,8},{10,11... | collective-permute-start | bytes 1376264 | tf_op jit(solution)/shard_map/ppermute | solution.py:18
  180.8 14.4 %collective-permute-start.44 = (bf16[64,3584]{1,0:T(8,128)(2,1)}, bf16[64,3584]{1,0:T(8,128)(2,1)S(1)}, u32[]{:S(2)}, u32[]{:S(2)}) collective-permute-start(bf16[64,3584]{1,0:T(8,128)(2,1)} %get-tuple-element.130), channel_id=1, source_target_pairs={{0,1},{1,0},{2,3},{3,2},{4,5},{5,4},{6,7},{7,6},{8,9},{9,8},{10,11... | collective-permute-start | bytes 1376264 | tf_op jit(solution)/shard_map/ppermute | solution.py:18
  196.7 8.0 %copy-start.1 = (bf16[7168,64]{0,1:T(8,128)(2,1)S(1)}, bf16[7168,64]{0,1:T(8,128)(2,1)}, u32[]{:S(2)}) copy-start(bf16[7168,64]{0,1:T(8,128)(2,1)} %param.10) | copy-start | bytes 2752516
  (4 other events, 4.7 us)

commit v16 on v11

--- a/solution.py
+++ b/solution.py
@@ -341,7 +341,11 @@
     later = after(far[1], pair0)
     later = [far[1], later_first, across(later, 2), across(later, 3)]
     sent, kept = far_terms(blocks, 1, 2, pair0)
-    pair1, sum1 = pair_sum(sent, kept, *later[2:])
+    acts_low, grads_low = jnp.split(after(low, sent[0]) + partner, 2, axis=1)
+    example_grad = example_gradients(
+        acts_low, grads_low, token_example[0], example_group.shape[0]
+    )
+    pair1, sum1 = pair_sum(sent, kept, *later[2:], example_grad)
 
     beside = spread_first(after(beside, pair1))
     sent, kept = far_terms(later, 0, 2, pair1, *sum0)
@@ -350,29 +354,27 @@
     beside = spread_last(beside, pair2)
     own = after(own, pair2)
     own_first = across(own, 1)
-    acts_low, grads_low = jnp.split(after(low, pair2, *sum1) + partner, 2, axis=1)
-    example_grad = example_gradients(
-        acts_low, grads_low, token_example[0], example_group.shape[0]
-    )
-    gathered = gather_examples(example_grad, example_group)
-    sent, kept = far_terms(later, 1, 4, example_grad)
+    gathered = gather_examples(after(example_grad, pair1), example_group)
+    sent, kept = far_terms(later, 1, 4, pair2, *sum1, *gathered)
+    every = order_examples(after(gathered, sent[0]))
+    fisher, group_grad = fisher_and_groups(every, example_grad.shape[1])
     own = [own, own_first, across(own, 2)]
-    pair3, sum3 = pair_sum(sent, after(kept, own[2]), own_first, *beside, outs=2)
+    pair3, sum3 = pair_sum(
+        sent, after(kept, own[2]), own_first, *beside, fisher, group_grad, outs=2
+    )
 
     own = spread_last(own, pair3)
     beside = [after(beside[0], pair3, *sum2)] + beside[1:]
     near0 = block_terms(beside, down_weight, 0, 2, [rows // 2] * 4)
-    near0 = [swap(after(term, sum3[0]), 1) for term in near0]
+    near0 = [swap(after(term, sum3[0], *own[3:]), 1) for term in near0]
     beside = [after(beside[0], *near0[:1])] + beside[1:]
     near1 = block_terms(beside, down_weight, 1, 2, [rows // 2] * 4)
-    every = order_examples(after(gathered, near1[0]))
-    fisher, group_grad = fisher_and_groups(every, example_grad.shape[1])
     own = [after(own[0], near1[0])] + own[1:]
     near1 = [swap(after(term, sum3[1], *own[3:]), 1) for term in near1]
     adds = [gather_sums(near0, sum0 + sum2)]
     (result,) = block_terms(own, down_weight, 0, 2, [tokens], adds)
     adds = [gather_sums(near1, sum1)] + sum3
-    own = [after(own[0], fisher, group_grad, result)] + own[1:]
+    own = [after(own[0], result)] + own[1:]
     (result,) = block_terms(own, down_weight, 1, 2, [tokens], adds, result)
     return (result, fisher, group_grad)
 

time: 176 us -> 177 us (level)
  local copies, waits for them, and re-layouts: 5.95 us -> 11.1 us
  waiting for transfers between devices: 55.5 us -> 51.1 us
    unnamed x26 -> x30, local copies, waits for them, and re-layouts: 2.19 us -> 7.61 us
    ppermute x16, waiting for transfers between devices: 37.4 us -> 34.4 us  [across(): return lax.ppermute(value, 'tensor', pairs)]
  transfers between devices with their start and end apart: 47 -> 47, of which waited for: 24 -> 18; matrix products, arithmetic and copies ran while one was open for 6% -> 6% of each run, Pallas kernels for 32% -> 31%
where the time goes in v16:
time: 177 us
  Pallas kernels  66.4 us (38%)
  waiting for transfers between devices  51.1 us (29%)
  starting transfers between devices  36.9 us (21%)
  local copies, waits for them, and re-layouts  11.1 us (6%)
  matrix products  7.55 us (4%)
  other arithmetic  2.25 us (1%)
    pallas_call x8, Pallas kernels, block_terms(): pl.pallas_call(functools.partial(terms_kernel, size, len(blocks), part *...  58 us
    ppermute x16, waiting for transfers between devices, across(): return lax.ppermute(value, 'tensor', pairs)  34.4 us
    ppermute x16, starting transfers between devices, across(): return lax.ppermute(value, 'tensor', pairs)  20.4 us
    ppermute x31, waiting for transfers between devices, swap(): return lax.ppermute(value, 'dp', [(d, d ^ step) for d in range(size)])  16.7 us
    ppermute x31, starting transfers between devices, swap(): return lax.ppermute(value, 'dp', [(d, d ^ step) for d in range(size)])  16.5 us
    unnamed x30, local copies, waits for them, and re-layouts  7.61 us
    pallas_call x4, Pallas kernels, add_pieces(): pl.pallas_call(functools.partial(add_kernel, len(pieces)), out_shape=[jax...  6.1 us
  transfers between devices with their start and end apart: 47, of which 18 were waited for; matrix products, arithmetic and copies ran while one was open for 6% of the time, Pallas kernels for 31%

profile of v16, /device:TPU:0, one launch (start us, length us, event | category | flops | bytes accessed | tf_op | source)
XLA Modules:
  0.0 176.6 jit_solution(7320126730016188649)
XLA Ops:
  0.7 1.3 constant_dynamic-slice_fusion
  2.2 0.7 slice_bitcast_fusion
  2.9 2.9 %collective-permute-start.3 = (bf16[128,512]{1,0:T(8,128)(2,1)}, bf16[128,512]{1,0:T(8,128)(2,1)S(1)}, u32[]{:S(2)}, u32[]{:S(2)}) collective-permute-start(bf16[128,512]{1,0:T(8,128)(2,1)} %get-tuple-element.143), channel_id=1, source_target_pairs={{0,2},{1,3},{2,0},{3,1},{4,6},{5,7},{6,4},{7,5},{8,10},{9,11},{10,... | collective-permute-start | bytes 393224 | tf_op jit(solution)/shard_map/ppermute | solution.py:18
  6.0 0.7 slice_bitcast_fusion.1
  6.7 3.3 %fusion.15 = f32[256,64]{0,1:T(8,128)S(1)} fusion(bf16[256,7168]{1,0:T(8,128)(2,1)} %param.7, bf16[7168,64]{0,1:T(8,128)(2,1)S(1)} %copy-done), kind=kOutput, calls=%fused_computation.38 | convolution fusion | flops 234881024 | bytes 4653056 | tf_op jit(solution)/shard_map/dot_general | solution.py:277
  10.3 2.1 %collective-permute-done.2 = bf16[128,512]{1,0:T(8,128)(2,1)S(1)} collective-permute-done((bf16[128,512]{1,0:T(8,128)(2,1)S(1)}, bf16[128,512]{1,0:T(8,128)(2,1)S(1)}, u32[]{:S(2)}, u32[]{:S(2)}) %collective-permute-start.2) | collective-permute-done | bytes 131104 | tf_op jit(solution)/shard_map/ppermute | solution.py:18
  12.4 3.8 %collective-permute-start.6 = (bf16[256,512]{1,0:T(8,128)(2,1)S(1)}, bf16[256,512]{1,0:T(8,128)(2,1)S(1)}, u32[]{:S(2)}, u32[]{:S(2)}) collective-permute-start(bf16[256,512]{1,0:T(8,128)(2,1)S(1)} %pad_maximum_fusion.1.refs_0_), channel_id=1, source_target_pairs={{0,12},{4,8},{8,4},{12,0},{1,13},{5,9},{9,5},{13,1},{2,14},{6,10},... | collective-permute-start | bytes 786440 | tf_op jit(solution)/shard_map/ppermute | solution.py:28
  16.2 0.6 collective-permute-start.4
  16.9 0.6 collective-permute-start.1
  17.8 5.3 %collective-permute-done.1 = bf16[128,512]{1,0:T(8,128)(2,1)S(1)} collective-permute-done((bf16[128,512]{1,0:T(8,128)(2,1)S(1)}, bf16[128,512]{1,0:T(8,128)(2,1)S(1)}, u32[]{:S(2)}, u32[]{:S(2)}) %collective-permute-start.1) | collective-permute-done | bytes 131104 | tf_op jit(solution)/shard_map/ppermute | solution.py:18
  23.0 1.5 collective-permute-start.8
  24.8 14.0 %collective-permute-done.5.refs_2_ = bf16[256,512]{1,0:T(8,128)(2,1)S(1)} collective-permute-done((bf16[256,512]{1,0:T(8,128)(2,1)S(1)}, bf16[256,512]{1,0:T(8,128)(2,1)S(1)}, u32[]{:S(2)}, u32[]{:S(2)}) %collective-permute-start.5) | collective-permute-done | bytes 262176 | tf_op jit(solution)/shard_map/ppermute | solution.py:28
  38.8 0.7 fusion.14
  39.5 3.0 %collective-permute-start.9 = (f32[256,128]{0,1:T(8,128)}, f32[256,128]{0,1:T(8,128)}, u32[]{:S(2)}, u32[]{:S(2)}) collective-permute-start(f32[256,128]{0,1:T(8,128)} %fusion.14), channel_id=1, source_target_pairs={{0,8},{4,12},{8,0},{12,4},{1,9},{5,13},{9,1},{13,5},{2,10},{6,14},... | collective-permute-start | bytes 393224 | tf_op jit(solution)/shard_map/ppermute | solution.py:28
  42.5 6.9 %terms.8 = (bf16[64,3584]{1,0:T(8,128)(2,1)S(1)}, bf16[64,3584]{1,0:T(8,128)(2,1)S(1)}, bf16[128,3584]{1,0:T(8,128)(2,1)S(1)}) custom-call(s32[1]{0:T(128)} %bitcast.place_ref, bf16[256,512]{1,0:T(8,128)(2,1)S(1)} %pad_maximum_fusion.1.refs_0_, bf16[256,512]{1,0:T(8,128)(2,1)S(1)} %collective-permute-done.4.refs_1_, ...), custom_call_target="tpu_custom_call" | custom-call | flops 469762048 | bytes 1000 | tf_op jit(solution)/shard_map/terms/pallas_call | solution.py:135
  50.2 1.2 collective-permute-done.12.refs_1_
  51.3 0.7 collective-permute-done.11.refs_0_
  52.0 1.7 pair.4
  53.7 2.1 %collective-permute-start.14 = (bf16[256,512]{1,0:T(8,128)(2,1)S(1)}, bf16[256,512]{1,0:T(8,128)(2,1)S(1)}, u32[]{:S(2)}, u32[]{:S(2)}) collective-permute-start(bf16[256,512]{1,0:T(8,128)(2,1)S(1)} %pad_maximum_fusion.refs_0_), channel_id=1, source_target_pairs={{0,12},{4,8},{8,4},{12,0},{1,13},{5,9},{9,5},{13,1},{2,14},{6,10},... | collective-permute-start | bytes 786440 | tf_op jit(solution)/shard_map/ppermute | solution.py:28
  56.2 2.1 %collective-permute-start.17 = (bf16[128,3584]{1,0:T(8,128)(2,1)}, bf16[128,3584]{1,0:T(8,128)(2,1)S(1)}, u32[]{:S(2)}, u32[]{:S(2)}) collective-permute-start(bf16[128,3584]{1,0:T(8,128)(2,1)} %pair.4), channel_id=1, source_target_pairs={{0,2},{1,3},{2,0},{3,1},{4,6},{5,7},{6,4},{7,5},{8,10},{9,11},{10,... | collective-permute-start | bytes 2752520 | tf_op jit(solution)/shard_map/ppermute | solution.py:18
  58.2 6.9 %terms.9 = (bf16[64,3584]{1,0:T(8,128)(2,1)S(1)}, bf16[64,3584]{1,0:T(8,128)(2,1)S(1)}, bf16[128,3584]{1,0:T(8,128)(2,1)S(1)}) custom-call(s32[1]{0:T(128)} %bitcast.place_ref, bf16[256,512]{1,0:T(8,128)(2,1)S(1)} %pad_maximum_fusion.1.refs_0_, bf16[256,512]{1,0:T(8,128)(2,1)S(1)} %collective-permute-done.4.refs_1_, ...), custom_call_target="tpu_custom_call" | custom-call | flops 469762048 | bytes 1000 | tf_op jit(solution)/shard_map/terms/pallas_call | solution.py:135
  65.1 0.9 copy-done.4
  66.1 0.8 copy-done.8
  66.9 0.8 copy-done.9
  67.6 1.0 add.30
  69.3 10.1 %collective-permute-done.13.refs_2_ = bf16[256,512]{1,0:T(8,128)(2,1)S(1)} collective-permute-done((bf16[256,512]{1,0:T(8,128)(2,1)S(1)}, bf16[256,512]{1,0:T(8,128)(2,1)S(1)}, u32[]{:S(2)}, u32[]{:S(2)}) %collective-permute-start.13) | collective-permute-done | bytes 262176 | tf_op jit(solution)/shard_map/ppermute | solution.py:28
  79.3 0.5 collective-permute-start.16
  79.8 1.5 collective-permute-done.15.refs_0_
  81.4 0.7 collective-permute-done.16.refs_1_
  82.0 1.2 copy-done.5
  83.2 1.7 pair.5
  84.9 2.1 %collective-permute-start.22 = (bf16[128,3584]{1,0:T(8,128)(2,1)}, bf16[128,3584]{1,0:T(8,128)(2,1)}, u32[]{:S(2)}, u32[]{:S(2)}) collective-permute-start(bf16[128,3584]{1,0:T(8,128)(2,1)} %pair.5), channel_id=1, source_target_pairs={{0,2},{1,3},{2,0},{3,1},{4,6},{5,7},{6,4},{7,5},{8,10},{9,11},{10,... | collective-permute-start | bytes 2752520 | tf_op jit(solution)/shard_map/ppermute | solution.py:18
  87.0 1.9 %collective-permute-start.18 = (bf16[256,512]{1,0:T(8,128)(2,1)S(1)}, bf16[256,512]{1,0:T(8,128)(2,1)S(1)}, u32[]{:S(2)}, u32[]{:S(2)}) collective-permute-start(bf16[256,512]{1,0:T(8,128)(2,1)S(1)} %collective-permute-done.7.refs_0_), channel_id=1, source_target_pairs={{0,4},{4,0},{8,12},{12,8},{1,5},{5,1},{9,13},{13,9},{2,6},{6,2},{1... | collective-permute-start | bytes 786440 | tf_op jit(solution)/shard_map/ppermute | solution.py:28
  88.9 7.5 %terms.10 = (bf16[64,3584]{1,0:T(8,128)(2,1)}, bf16[64,3584]{1,0:T(8,128)(2,1)S(1)}, bf16[128,3584]{1,0:T(8,128)(2,1)S(1)}) custom-call(s32[1]{0:T(128)} %bitcast.place_ref, bf16[256,512]{1,0:T(8,128)(2,1)S(1)} %pad_maximum_fusion.refs_0_, bf16[256,512]{1,0:T(8,128)(2,1)S(1)} %collective-permute-done.10.refs_1_, ...), custom_call_target="tpu_custom_call" | custom-call | flops 469762048 | bytes 1000 | tf_op jit(solution)/shard_map/terms/pallas_call | solution.py:135
  96.4 0.9 copy-done.2
  97.4 3.0 %collective-permute-done.19.refs_2_ = bf16[256,512]{1,0:T(8,128)(2,1)S(1)} collective-permute-done((bf16[256,512]{1,0:T(8,128)(2,1)S(1)}, bf16[256,512]{1,0:T(8,128)(2,1)S(1)}, u32[]{:S(2)}, u32[]{:S(2)}) %collective-permute-start.19) | collective-permute-done | bytes 262176 | tf_op jit(solution)/shard_map/ppermute | solution.py:28
  100.7 0.5 collective-permute-start.20
  101.3 1.6 collective-permute-start.24
  103.1 0.8 copy-done.6
  104.2 1.2 copy-done.3
  105.4 1.0 copy-done.7
  106.4 2.1 %pair.6 = bf16[128,3584]{1,0:T(8,128)(2,1)S(1)} custom-call(bf16[128,3584]{1,0:T(8,128)(2,1)S(1)} %copy-done.3, bf16[64,3584]{1,0:T(8,128)(2,1)} %collective-permute-done.20.refs_0_, bf16[64,3584]{1,0:T(8,128)(2,1)S(1)} %copy-done.7), custom_call_target="tpu_custom_call" | custom-call | flops 1000 | bytes 1000 | tf_op jit(solution)/shard_map/pair/pallas_call | solution.py:181
  108.9 2.6 %collective-permute-start.26 = (bf16[256,512]{1,0:T(8,128)(2,1)S(1)}, bf16[256,512]{1,0:T(8,128)(2,1)S(1)}, u32[]{:S(2)}, u32[]{:S(2)}) collective-permute-start(bf16[256,512]{1,0:T(8,128)(2,1)S(1)} %bitcast.39), channel_id=1, source_target_pairs={{0,8},{4,12},{8,0},{12,4},{1,9},{5,13},{9,1},{13,5},{2,10},{6,14},... | collective-permute-start | bytes 786440 | tf_op jit(solution)/shard_map/ppermute | solution.py:28
  111.8 0.7 collective-permute-start.28
  112.5 1.3 collective-permute-start.29
  113.8 7.0 %terms.11 = (bf16[32,3584]{1,0:T(8,128)(2,1)S(1)}, bf16[32,3584]{1,0:T(8,128)(2,1)S(1)}, bf16[32,3584]{1,0:T(8,128)(2,1)S(1)}, bf16[32,3584]{1,0:T(8,128)(2,1)S(1)}, bf16[128,3584]{1,0:T(8,128)(2,1)S(1)}) custom-call(s32[1]{0:T(128)} %bitcast.place_ref, bf16[256,512]{1,0:T(8,128)(2,1)S(1)} %pad_maximum_fusion.refs_0_, ...), custom_call_target="tpu_custom_call" | custom-call | flops 469762048 | bytes 1000 | tf_op jit(solution)/shard_map/terms/pallas_call | solution.py:135
  121.0 2.8 %fusion.4 = f32[1024,1024]{1,0:T(8,128)} fusion(bf16[16,4224]{1,0:T(8,128)(2,1)S(1)} %pad_maximum_fusion.2, s32[]{:T(128)S(6)} %select_n.121, s32[]{:T(128)S(6)} %select_n.122), kind=kOutput, calls=%fused_computation.20 | convolution fusion | flops 33554432 | bytes 4259848 | tf_op jit(solution)/shard_map/dot_general | solution.py:266
  123.9 0.9 fusion.6
  124.8 3.6 %collective-permute-done.29.refs_4_ = bf16[256,512]{1,0:T(8,128)(2,1)S(1)} collective-permute-done((bf16[256,512]{1,0:T(8,128)(2,1)S(1)}, bf16[256,512]{1,0:T(8,128)(2,1)S(1)}, u32[]{:S(2)}, u32[]{:S(2)}) %collective-permute-start.29) | collective-permute-done | bytes 262176 | tf_op jit(solution)/shard_map/ppermute | solution.py:28
  128.4 0.5 collective-permute-start.31
  128.9 0.5 collective-permute-start.33
  130.9 0.6 pair.7
  131.9 0.7 collective-permute-start.36
  132.5 1.5 collective-permute-start.37
  134.0 6.9 %terms.12 = (bf16[64,3584]{1,0:T(8,128)(2,1)S(1)}, bf16[64,3584]{1,0:T(8,128)(2,1)S(1)}, bf16[64,3584]{1,0:T(8,128)(2,1)S(1)}, bf16[64,3584]{1,0:T(8,128)(2,1)S(1)}) custom-call(s32[1]{0:T(128)} %bitcast.place_ref, bf16[256,512]{1,0:T(8,128)(2,1)S(1)} %collective-permute-done.7.refs_0_, bf16[256,512]{1,0:T(8,128)(2,1)S(1)} %collective-permute-done.18.refs_1_, ...), custom_call_target="tpu_custom_call" | custom-call | flops 469762048 | bytes 1000 | tf_op jit(solution)/shard_map/terms/pallas_call | solution.py:135
  141.0 3.3 %collective-permute-done.37.refs_4_ = bf16[256,512]{1,0:T(8,128)(2,1)S(1)} collective-permute-done((bf16[256,512]{1,0:T(8,128)(2,1)S(1)}, bf16[256,512]{1,0:T(8,128)(2,1)S(1)}, u32[]{:S(2)}, u32[]{:S(2)}) %collective-permute-start.37) | collective-permute-done | bytes 262176 | tf_op jit(solution)/shard_map/ppermute | solution.py:28
  144.3 1.6 collective-permute-start.42
  146.6 6.9 %terms.13 = (bf16[64,3584]{1,0:T(8,128)(2,1)S(1)}, bf16[64,3584]{1,0:T(8,128)(2,1)S(1)}, bf16[64,3584]{1,0:T(8,128)(2,1)S(1)}, bf16[64,3584]{1,0:T(8,128)(2,1)S(1)}) custom-call(s32[1]{0:T(128)} %bitcast.place_ref, bf16[256,512]{1,0:T(8,128)(2,1)S(1)} %collective-permute-done.7.refs_0_, bf16[256,512]{1,0:T(8,128)(2,1)S(1)} %collective-permute-done.18.refs_1_, ...), custom_call_target="tpu_custom_call" | custom-call | flops 469762048 | bytes 1000 | tf_op jit(solution)/shard_map/terms/pallas_call | solution.py:135
  153.5 3.7 %collective-permute-done.42.refs_8_ = bf16[64,3584]{1,0:T(8,128)(2,1)S(1)} collective-permute-done((bf16[64,3584]{1,0:T(8,128)(2,1)S(1)}, bf16[64,3584]{1,0:T(8,128)(2,1)S(1)}, u32[]{:S(2)}, u32[]{:S(2)}) %collective-permute-start.42) | collective-permute-done | bytes 458784 | tf_op jit(solution)/shard_map/ppermute | solution.py:18
  157.3 0.5 collective-permute-start.46
  158.3 0.8 sums.2.refs_6_
  159.1 7.7 %terms.14.refs_9_ = bf16[256,7168]{1,0:T(8,128)(2,1)} custom-call(s32[1]{0:T(128)} %bitcast.place_ref, bf16[256,512]{1,0:T(8,128)(2,1)S(1)} %bitcast.41, bf16[256,512]{1,0:T(8,128)(2,1)S(1)} %collective-permute-done.27.refs_1_, bf16[256,512]{1,0:T(8,128)(2,1)S(1)} %collective-permute-done.26.refs_2_, bf16[256,512]{1,0:T(8,128)(2,1)S(1)} %collective-permute-done.36.refs_3_, ...), custom_call_target="tpu_custom_call" | custom-call | flops 469762048 | bytes 1000 | tf_op jit(solution)/shard_map/terms/pallas_call | solution.py:135
  166.9 1.5 sums.3.refs_6_
  168.4 8.0 %terms.15 = bf16[256,7168]{1,0:T(8,128)(2,1)} custom-call(s32[1]{0:T(128)} %bitcast.place_ref, bf16[256,512]{1,0:T(8,128)(2,1)S(1)} %bitcast.42, bf16[256,512]{1,0:T(8,128)(2,1)S(1)} %collective-permute-done.27.refs_1_, bf16[256,512]{1,0:T(8,128)(2,1)S(1)} %collective-permute-done.26.refs_2_, ...), custom_call_target="tpu_custom_call", output_to_operand_aliasing={{}: (10, {})} | custom-call | flops 469762048 | bytes 1000 | tf_op jit(solution)/shard_map/terms/pallas_call | solution.py:135
  (103 shorter events, 8.0 us)
Async XLA Ops:
  0.6 6.0 %copy-start = (bf16[7168,64]{0,1:T(8,128)(2,1)S(1)}, bf16[7168,64]{0,1:T(8,128)(2,1)}, u32[]{:S(2)}) copy-start(bf16[7168,64]{0,1:T(8,128)(2,1)} %param.10) | copy-start | bytes 2752516
  2.0 7.9 %copy-start.10 = (bf16[1,4,512,256]{3,2,1,0:T(8,128)(2,1)S(1)}, bf16[1,4,512,256]{3,2,1,0:T(8,128)(2,1)}, u32[]{:S(2)}) copy-start(bf16[1,4,512,256]{3,2,1,0:T(8,128)(2,1)} %param.8) | copy-start | bytes 3145732
  2.0 7.9 %copy-start.11 = (bf16[1,4,512,64]{2,3,1,0:T(8,128)(2,1)S(1)}, bf16[1,4,512,64]{2,3,1,0:T(8,128)(2,1)}, u32[]{:S(2)}) copy-start(bf16[1,4,512,64]{2,3,1,0:T(8,128)(2,1)} %param.11) | copy-start | bytes 786436
  2.9 7.4 %collective-permute-start.3 = (bf16[128,512]{1,0:T(8,128)(2,1)}, bf16[128,512]{1,0:T(8,128)(2,1)S(1)}, u32[]{:S(2)}, u32[]{:S(2)}) collective-permute-start(bf16[128,512]{1,0:T(8,128)(2,1)} %get-tuple-element.143), channel_id=1, source_target_pairs={{0,2},{1,3},{2,0},{3,1},{4,6},{5,7},{6,4},{7,5},{8,10},{9,11},{10,... | collective-permute-start | bytes 393224 | tf_op jit(solution)/shard_map/ppermute | solution.py:18
  6.0 10.9 %copy-start.12 = (bf16[128,512]{1,0:T(8,128)(2,1)S(1)}, bf16[128,512]{1,0:T(8,128)(2,1)}, u32[]{:S(2)}) copy-start(bf16[128,512]{1,0:T(8,128)(2,1)} %get-tuple-element.144) | copy-start | bytes 393220
  6.7 5.7 %collective-permute-start.2 = (bf16[128,512]{1,0:T(8,128)(2,1)S(1)}, bf16[128,512]{1,0:T(8,128)(2,1)S(1)}, u32[]{:S(2)}, u32[]{:S(2)}) collective-permute-start(bf16[128,512]{1,0:T(8,128)(2,1)S(1)} %get-tuple-element.141), channel_id=1, source_target_pairs={{0,3},{1,2},{2,1},{3,0},{4,7},{5,6},{6,5},{7,4},{8,11},{9,10},{10,... | collective-permute-start | bytes 393224 | tf_op jit(solution)/shard_map/ppermute | solution.py:18
  12.4 12.4 %collective-permute-start.6 = (bf16[256,512]{1,0:T(8,128)(2,1)S(1)}, bf16[256,512]{1,0:T(8,128)(2,1)S(1)}, u32[]{:S(2)}, u32[]{:S(2)}) collective-permute-start(bf16[256,512]{1,0:T(8,128)(2,1)S(1)} %pad_maximum_fusion.1.refs_0_), channel_id=1, source_target_pairs={{0,12},{4,8},{8,4},{12,0},{1,13},{5,9},{9,5},{13,1},{2,14},{6,10},... | collective-permute-start | bytes 786440 | tf_op jit(solution)/shard_map/ppermute | solution.py:28
  16.2 22.6 %collective-permute-start.5 = (bf16[256,512]{1,0:T(8,128)(2,1)S(1)}, bf16[256,512]{1,0:T(8,128)(2,1)S(1)}, u32[]{:S(2)}, u32[]{:S(2)}) collective-permute-start(bf16[256,512]{1,0:T(8,128)(2,1)S(1)} %pad_maximum_fusion.1.refs_0_), channel_id=1, source_target_pairs={{0,8},{4,12},{8,0},{12,4},{1,9},{5,13},{9,1},{13,5},{2,10},{6,14},... | collective-permute-start | bytes 786440 | tf_op jit(solution)/shard_map/ppermute | solution.py:28
  16.2 22.6 %collective-permute-start.4 = (bf16[256,512]{1,0:T(8,128)(2,1)S(1)}, bf16[256,512]{1,0:T(8,128)(2,1)S(1)}, u32[]{:S(2)}, u32[]{:S(2)}) collective-permute-start(bf16[256,512]{1,0:T(8,128)(2,1)S(1)} %pad_maximum_fusion.1.refs_0_), channel_id=1, source_target_pairs={{0,4},{4,0},{8,12},{12,8},{1,5},{5,1},{9,13},{13,9},{2,6},{6,2},{1... | collective-permute-start | bytes 786440 | tf_op jit(solution)/shard_map/ppermute | solution.py:28
  16.9 6.2 %collective-permute-start.1 = (bf16[128,512]{1,0:T(8,128)(2,1)S(1)}, bf16[128,512]{1,0:T(8,128)(2,1)S(1)}, u32[]{:S(2)}, u32[]{:S(2)}) collective-permute-start(bf16[128,512]{1,0:T(8,128)(2,1)S(1)} %copy-done.12), channel_id=1, source_target_pairs={{0,2},{1,3},{2,0},{3,1},{4,6},{5,7},{6,4},{7,5},{8,10},{9,11},{10,... | collective-permute-start | bytes 393224 | tf_op jit(solution)/shard_map/ppermute | solution.py:18
  17.4 7.2 %collective-permute-start = (bf16[128,512]{1,0:T(8,128)(2,1)}, bf16[128,512]{1,0:T(8,128)(2,1)S(1)}, u32[]{:S(2)}, u32[]{:S(2)}) collective-permute-start(bf16[128,512]{1,0:T(8,128)(2,1)} %get-tuple-element.142), channel_id=1, source_target_pairs={{0,3},{1,2},{2,1},{3,0},{4,7},{5,6},{6,5},{7,4},{8,11},{9,10},{10,... | collective-permute-start | bytes 393224 | tf_op jit(solution)/shard_map/ppermute | solution.py:18
  23.0 15.8 %collective-permute-start.8 = (f32[256,128]{0,1:T(8,128)S(1)}, f32[256,128]{0,1:T(8,128)S(1)}, u32[]{:S(2)}, u32[]{:S(2)}) collective-permute-start(f32[256,128]{0,1:T(8,128)S(1)} %pad_maximum_fusion.3), channel_id=1, source_target_pairs={{0,4},{4,0},{8,12},{12,8},{1,5},{5,1},{9,13},{13,9},{2,6},{6,2},{1... | collective-permute-start | bytes 393224 | tf_op jit(solution)/shard_map/ppermute | solution.py:28
  24.6 17.9 %collective-permute-start.7 = (bf16[256,512]{1,0:T(8,128)(2,1)S(1)}, bf16[256,512]{1,0:T(8,128)(2,1)S(1)}, u32[]{:S(2)}, u32[]{:S(2)}) collective-permute-start(bf16[256,512]{1,0:T(8,128)(2,1)S(1)} %bitcast.46), channel_id=1, source_target_pairs={{0,1},{1,0},{2,3},{3,2},{4,5},{5,4},{6,7},{7,6},{8,9},{9,8},{10,11... | collective-permute-start | bytes 786440 | tf_op jit(solution)/shard_map/ppermute | solution.py:18
  38.8 10.6 %collective-permute-start.10 = (bf16[256,512]{1,0:T(8,128)(2,1)S(1)}, bf16[256,512]{1,0:T(8,128)(2,1)S(1)}, u32[]{:S(2)}, u32[]{:S(2)}) collective-permute-start(bf16[256,512]{1,0:T(8,128)(2,1)S(1)} %pad_maximum_fusion.refs_0_), channel_id=1, source_target_pairs={{0,4},{4,0},{8,12},{12,8},{1,5},{5,1},{9,13},{13,9},{2,6},{6,2},{1... | collective-permute-start | bytes 786440 | tf_op jit(solution)/shard_map/ppermute | solution.py:28
  39.5 10.0 %collective-permute-start.9 = (f32[256,128]{0,1:T(8,128)}, f32[256,128]{0,1:T(8,128)}, u32[]{:S(2)}, u32[]{:S(2)}) collective-permute-start(f32[256,128]{0,1:T(8,128)} %fusion.14), channel_id=1, source_target_pairs={{0,8},{4,12},{8,0},{12,4},{1,9},{5,13},{9,1},{13,5},{2,10},{6,14},... | collective-permute-start | bytes 393224 | tf_op jit(solution)/shard_map/ppermute | solution.py:28
  42.5 7.5 %copy-start.13 = (s32[1,256]{1,0:T(1,128)S(1)}, s32[1,256]{1,0:T(1,128)}, u32[]{:S(2)}) copy-start(s32[1,256]{1,0:T(1,128)} %param.12) | copy-start | bytes 3076
  49.5 1.9 %collective-permute-start.12 = (bf16[64,3584]{1,0:T(8,128)(2,1)S(1)}, bf16[64,3584]{1,0:T(8,128)(2,1)S(1)}, u32[]{:S(2)}, u32[]{:S(2)}) collective-permute-start(bf16[64,3584]{1,0:T(8,128)(2,1)S(1)} %get-tuple-element.78), channel_id=1, source_target_pairs={{0,1},{1,0},{2,3},{3,2},{4,5},{5,4},{6,7},{7,6},{8,9},{9,8},{10,11... | collective-permute-start | bytes 1376264 | tf_op jit(solution)/shard_map/ppermute | solution.py:18
  49.5 2.5 %collective-permute-start.11 = (bf16[64,3584]{1,0:T(8,128)(2,1)S(1)}, bf16[64,3584]{1,0:T(8,128)(2,1)S(1)}, u32[]{:S(2)}, u32[]{:S(2)}) collective-permute-start(bf16[64,3584]{1,0:T(8,128)(2,1)S(1)} %get-tuple-element.76), channel_id=1, source_target_pairs={{0,1},{1,0},{2,3},{3,2},{4,5},{5,4},{6,7},{7,6},{8,9},{9,8},{10,11... | collective-permute-start | bytes 1376264 | tf_op jit(solution)/shard_map/ppermute | solution.py:18
  53.7 15.5 %collective-permute-start.14 = (bf16[256,512]{1,0:T(8,128)(2,1)S(1)}, bf16[256,512]{1,0:T(8,128)(2,1)S(1)}, u32[]{:S(2)}, u32[]{:S(2)}) collective-permute-start(bf16[256,512]{1,0:T(8,128)(2,1)S(1)} %pad_maximum_fusion.refs_0_), channel_id=1, source_target_pairs={{0,12},{4,8},{8,4},{12,0},{1,13},{5,9},{9,5},{13,1},{2,14},{6,10},... | collective-permute-start | bytes 786440 | tf_op jit(solution)/shard_map/ppermute | solution.py:28
  55.8 23.6 %collective-permute-start.13 = (bf16[256,512]{1,0:T(8,128)(2,1)S(1)}, bf16[256,512]{1,0:T(8,128)(2,1)S(1)}, u32[]{:S(2)}, u32[]{:S(2)}) collective-permute-start(bf16[256,512]{1,0:T(8,128)(2,1)S(1)} %pad_maximum_fusion.refs_0_), channel_id=1, source_target_pairs={{0,8},{4,12},{8,0},{12,4},{1,9},{5,13},{9,1},{13,5},{2,10},{6,14},... | collective-permute-start | bytes 786440 | tf_op jit(solution)/shard_map/ppermute | solution.py:28
  56.2 32.7 %collective-permute-start.17 = (bf16[128,3584]{1,0:T(8,128)(2,1)}, bf16[128,3584]{1,0:T(8,128)(2,1)S(1)}, u32[]{:S(2)}, u32[]{:S(2)}) collective-permute-start(bf16[128,3584]{1,0:T(8,128)(2,1)} %pair.4), channel_id=1, source_target_pairs={{0,2},{1,3},{2,0},{3,1},{4,6},{5,7},{6,4},{7,5},{8,10},{9,11},{10,... | collective-permute-start | bytes 2752520 | tf_op jit(solution)/shard_map/ppermute | solution.py:18
  65.1 0.9 copy-start.4
  66.1 0.8 copy-start.8
  66.9 0.8 copy-start.9
  67.6 21.3 %copy-start.14 = (s32[4]{0:T(128)S(1)}, s32[4]{0:T(128)}, u32[]{:S(2)}) copy-start(s32[4]{0:T(128)} %param.13) | copy-start | bytes 52
  79.3 2.0 %collective-permute-start.15 = (bf16[64,3584]{1,0:T(8,128)(2,1)}, bf16[64,3584]{1,0:T(8,128)(2,1)S(1)}, u32[]{:S(2)}, u32[]{:S(2)}) collective-permute-start(bf16[64,3584]{1,0:T(8,128)(2,1)} %copy-done.9), channel_id=1, source_target_pairs={{0,1},{1,0},{2,3},{3,2},{4,5},{5,4},{6,7},{7,6},{8,9},{9,8},{10,11... | collective-permute-start | bytes 1376264 | tf_op jit(solution)/shard_map/ppermute | solution.py:18
  79.3 2.7 %collective-permute-start.16 = (bf16[64,3584]{1,0:T(8,128)(2,1)}, bf16[64,3584]{1,0:T(8,128)(2,1)S(1)}, u32[]{:S(2)}, u32[]{:S(2)}) collective-permute-start(bf16[64,3584]{1,0:T(8,128)(2,1)} %copy-done.8), channel_id=1, source_target_pairs={{0,1},{1,0},{2,3},{3,2},{4,5},{5,4},{6,7},{7,6},{8,9},{9,8},{10,11... | collective-permute-start | bytes 1376264 | tf_op jit(solution)/shard_map/ppermute | solution.py:18
  82.0 1.2 copy-start.5
  84.9 27.6 %collective-permute-start.22 = (bf16[128,3584]{1,0:T(8,128)(2,1)}, bf16[128,3584]{1,0:T(8,128)(2,1)}, u32[]{:S(2)}, u32[]{:S(2)}) collective-permute-start(bf16[128,3584]{1,0:T(8,128)(2,1)} %pair.5), channel_id=1, source_target_pairs={{0,2},{1,3},{2,0},{3,1},{4,6},{5,7},{6,4},{7,5},{8,10},{9,11},{10,... | collective-permute-start | bytes 2752520 | tf_op jit(solution)/shard_map/ppermute | solution.py:18
  87.0 13.4 %collective-permute-start.19 = (bf16[256,512]{1,0:T(8,128)(2,1)S(1)}, bf16[256,512]{1,0:T(8,128)(2,1)S(1)}, u32[]{:S(2)}, u32[]{:S(2)}) collective-permute-start(bf16[256,512]{1,0:T(8,128)(2,1)S(1)} %collective-permute-done.7.refs_0_), channel_id=1, source_target_pairs={{0,8},{4,12},{8,0},{12,4},{1,9},{5,13},{9,1},{13,5},{2,10},{6,14},... | collective-permute-start | bytes 786440 | tf_op jit(solution)/shard_map/ppermute | solution.py:28
  87.0 13.7 %collective-permute-start.18 = (bf16[256,512]{1,0:T(8,128)(2,1)S(1)}, bf16[256,512]{1,0:T(8,128)(2,1)S(1)}, u32[]{:S(2)}, u32[]{:S(2)}) collective-permute-start(bf16[256,512]{1,0:T(8,128)(2,1)S(1)} %collective-permute-done.7.refs_0_), channel_id=1, source_target_pairs={{0,4},{4,0},{8,12},{12,8},{1,5},{5,1},{9,13},{13,9},{2,6},{6,2},{1... | collective-permute-start | bytes 786440 | tf_op jit(solution)/shard_map/ppermute | solution.py:28
  96.4 0.9 copy-start.2
  100.7 2.4 %collective-permute-start.21 = (bf16[64,3584]{1,0:T(8,128)(2,1)S(1)}, bf16[64,3584]{1,0:T(8,128)(2,1)S(1)}, u32[]{:S(2)}, u32[]{:S(2)}) collective-permute-start(bf16[64,3584]{1,0:T(8,128)(2,1)S(1)} %get-tuple-element.93), channel_id=1, source_target_pairs={{0,1},{1,0},{2,3},{3,2},{4,5},{5,4},{6,7},{7,6},{8,9},{9,8},{10,11... | collective-permute-start | bytes 1376264 | tf_op jit(solution)/shard_map/ppermute | solution.py:18
  100.7 3.5 %collective-permute-start.20 = (bf16[64,3584]{1,0:T(8,128)(2,1)}, bf16[64,3584]{1,0:T(8,128)(2,1)}, u32[]{:S(2)}, u32[]{:S(2)}) collective-permute-start(bf16[64,3584]{1,0:T(8,128)(2,1)} %get-tuple-element.91), channel_id=1, source_target_pairs={{0,1},{1,0},{2,3},{3,2},{4,5},{5,4},{6,7},{7,6},{8,9},{9,8},{10,11... | collective-permute-start | bytes 1376264 | tf_op jit(solution)/shard_map/ppermute | solution.py:18
  101.3 7.7 %collective-permute-start.25 = (bf16[4,4224]{1,0:T(4,128)(2,1)S(1)}, bf16[4,4224]{1,0:T(4,128)(2,1)S(1)}, u32[]{:S(2)}, u32[]{:S(2)}) collective-permute-start(bf16[4,4224]{1,0:T(4,128)(2,1)S(1)} %pad_maximum_fusion.4), channel_id=1, source_target_pairs={{0,3},{1,2},{2,1},{3,0},{4,7},{5,6},{6,5},{7,4},{8,11},{9,10},{10,... | collective-permute-start | bytes 101384 | tf_op jit(solution)/shard_map/ppermute | solution.py:18
  101.3 10.2 %collective-permute-start.24 = (bf16[4,4224]{1,0:T(4,128)(2,1)S(1)}, bf16[4,4224]{1,0:T(4,128)(2,1)S(1)}, u32[]{:S(2)}, u32[]{:S(2)}) collective-permute-start(bf16[4,4224]{1,0:T(4,128)(2,1)S(1)} %pad_maximum_fusion.4), channel_id=1, source_target_pairs={{0,2},{1,3},{2,0},{3,1},{4,6},{5,7},{6,4},{7,5},{8,10},{9,11},{10,... | collective-permute-start | bytes 101384 | tf_op jit(solution)/shard_map/ppermute | solution.py:18
  103.1 0.8 copy-start.6
  103.9 7.9 %collective-permute-start.23 = (bf16[4,4224]{1,0:T(4,128)(2,1)S(1)}, bf16[4,4224]{1,0:T(4,128)(2,1)S(1)}, u32[]{:S(2)}, u32[]{:S(2)}) collective-permute-start(bf16[4,4224]{1,0:T(4,128)(2,1)S(1)} %pad_maximum_fusion.4), channel_id=1, source_target_pairs={{0,1},{1,0},{2,3},{3,2},{4,5},{5,4},{6,7},{7,6},{8,9},{9,8},{10,11... | collective-permute-start | bytes 101384 | tf_op jit(solution)/shard_map/ppermute | solution.py:18
  104.2 1.2 copy-start.3
  105.4 1.0 copy-start.7
  108.5 16.2 %collective-permute-start.27 = (bf16[256,512]{1,0:T(8,128)(2,1)S(1)}, bf16[256,512]{1,0:T(8,128)(2,1)S(1)}, u32[]{:S(2)}, u32[]{:S(2)}) collective-permute-start(bf16[256,512]{1,0:T(8,128)(2,1)S(1)} %bitcast.38), channel_id=1, source_target_pairs={{0,4},{4,0},{8,12},{12,8},{1,5},{5,1},{9,13},{13,9},{2,6},{6,2},{1... | collective-permute-start | bytes 786440 | tf_op jit(solution)/shard_map/ppermute | solution.py:28
  108.9 20.0 %collective-permute-start.26 = (bf16[256,512]{1,0:T(8,128)(2,1)S(1)}, bf16[256,512]{1,0:T(8,128)(2,1)S(1)}, u32[]{:S(2)}, u32[]{:S(2)}) collective-permute-start(bf16[256,512]{1,0:T(8,128)(2,1)S(1)} %bitcast.39), channel_id=1, source_target_pairs={{0,8},{4,12},{8,0},{12,4},{1,9},{5,13},{9,1},{13,5},{2,10},{6,14},... | collective-permute-start | bytes 786440 | tf_op jit(solution)/shard_map/ppermute | solution.py:28
  111.5 22.5 %collective-permute-start.34 = (bf16[128,3584]{1,0:T(8,128)(2,1)S(1)}, bf16[128,3584]{1,0:T(8,128)(2,1)S(1)}, u32[]{:S(2)}, u32[]{:S(2)}) collective-permute-start(bf16[128,3584]{1,0:T(8,128)(2,1)S(1)} %pair.6), channel_id=1, source_target_pairs={{0,2},{1,3},{2,0},{3,1},{4,6},{5,7},{6,4},{7,5},{8,10},{9,11},{10,... | collective-permute-start | bytes 2752520 | tf_op jit(solution)/shard_map/ppermute | solution.py:18
  111.8 13.0 %collective-permute-start.28 = (bf16[256,512]{1,0:T(8,128)(2,1)S(1)}, bf16[256,512]{1,0:T(8,128)(2,1)S(1)}, u32[]{:S(2)}, u32[]{:S(2)}) collective-permute-start(bf16[256,512]{1,0:T(8,128)(2,1)S(1)} %collective-permute-done.7.refs_0_), channel_id=1, source_target_pairs={{4,8},{8,4},{5,9},{9,5},{6,10},{10,6},{7,11},{11,7},{20,24},{24,20... | collective-permute-start | bytes 786440 | tf_op jit(solution)/shard_map/ppermute | solution.py:28
  112.5 15.9 %collective-permute-start.29 = (bf16[256,512]{1,0:T(8,128)(2,1)S(1)}, bf16[256,512]{1,0:T(8,128)(2,1)S(1)}, u32[]{:S(2)}, u32[]{:S(2)}) collective-permute-start(bf16[256,512]{1,0:T(8,128)(2,1)S(1)} %collective-permute-done.19.refs_2_), channel_id=1, source_target_pairs={{4,0},{8,12},{5,1},{9,13},{6,2},{10,14},{7,3},{11,15},{20,16},{24,... | collective-permute-start | bytes 786440 | tf_op jit(solution)/shard_map/ppermute | solution.py:28
  128.4 1.5 collective-permute-start.30
  128.4 1.8 %collective-permute-start.31 = (bf16[32,3584]{1,0:T(8,128)(2,1)S(1)}, bf16[32,3584]{1,0:T(8,128)(2,1)S(1)}, u32[]{:S(2)}, u32[]{:S(2)}) collective-permute-start(bf16[32,3584]{1,0:T(8,128)(2,1)S(1)} %get-tuple-element.108), channel_id=1, source_target_pairs={{0,1},{1,0},{2,3},{3,2},{4,5},{5,4},{6,7},{7,6},{8,9},{9,8},{10,11... | collective-permute-start | bytes 688136 | tf_op jit(solution)/shard_map/ppermute | solution.py:18
  128.9 1.6 collective-permute-start.32
  128.9 2.0 %collective-permute-start.33 = (bf16[32,3584]{1,0:T(8,128)(2,1)S(1)}, bf16[32,3584]{1,0:T(8,128)(2,1)S(1)}, u32[]{:S(2)}, u32[]{:S(2)}) collective-permute-start(bf16[32,3584]{1,0:T(8,128)(2,1)S(1)} %get-tuple-element.112), channel_id=1, source_target_pairs={{0,1},{1,0},{2,3},{3,2},{4,5},{5,4},{6,7},{7,6},{8,9},{9,8},{10,11... | collective-permute-start | bytes 688136 | tf_op jit(solution)/shard_map/ppermute | solution.py:18
  131.4 12.9 %collective-permute-start.35 = (bf16[64,3584]{1,0:T(8,128)(2,1)S(1)}, bf16[64,3584]{1,0:T(8,128)(2,1)S(1)}, u32[]{:S(2)}, u32[]{:S(2)}) collective-permute-start(bf16[64,3584]{1,0:T(8,128)(2,1)S(1)} %get-tuple-element.113), channel_id=1, source_target_pairs={{0,2},{1,3},{2,0},{3,1},{4,6},{5,7},{6,4},{7,5},{8,10},{9,11},{10,... | collective-permute-start | bytes 1376264 | tf_op jit(solution)/shard_map/ppermute | solution.py:18
  131.9 9.1 %collective-permute-start.36 = (bf16[256,512]{1,0:T(8,128)(2,1)S(1)}, bf16[256,512]{1,0:T(8,128)(2,1)S(1)}, u32[]{:S(2)}, u32[]{:S(2)}) collective-permute-start(bf16[256,512]{1,0:T(8,128)(2,1)S(1)} %bitcast.40), channel_id=1, source_target_pairs={{4,8},{8,4},{5,9},{9,5},{6,10},{10,6},{7,11},{11,7},{20,24},{24,20... | collective-permute-start | bytes 786440 | tf_op jit(solution)/shard_map/ppermute | solution.py:28
  132.5 11.8 %collective-permute-start.37 = (bf16[256,512]{1,0:T(8,128)(2,1)S(1)}, bf16[256,512]{1,0:T(8,128)(2,1)S(1)}, u32[]{:S(2)}, u32[]{:S(2)}) collective-permute-start(bf16[256,512]{1,0:T(8,128)(2,1)S(1)} %collective-permute-done.26.refs_2_), channel_id=1, source_target_pairs={{4,0},{8,12},{5,1},{9,13},{6,2},{10,14},{7,3},{11,15},{20,16},{24,... | collective-permute-start | bytes 786440 | tf_op jit(solution)/shard_map/ppermute | solution.py:28
  144.3 2.3 %collective-permute-start.38 = (bf16[64,3584]{1,0:T(8,128)(2,1)S(1)}, bf16[64,3584]{1,0:T(8,128)(2,1)S(1)}, u32[]{:S(2)}, u32[]{:S(2)}) collective-permute-start(bf16[64,3584]{1,0:T(8,128)(2,1)S(1)} %get-tuple-element.118), channel_id=1, source_target_pairs={{0,1},{1,0},{2,3},{3,2},{4,5},{5,4},{6,7},{7,6},{8,9},{9,8},{10,11... | collective-permute-start | bytes 1376264 | tf_op jit(solution)/shard_map/ppermute | solution.py:18
  144.3 12.9 %collective-permute-start.42 = (bf16[64,3584]{1,0:T(8,128)(2,1)S(1)}, bf16[64,3584]{1,0:T(8,128)(2,1)S(1)}, u32[]{:S(2)}, u32[]{:S(2)}) collective-permute-start(bf16[64,3584]{1,0:T(8,128)(2,1)S(1)} %get-tuple-element.129), channel_id=1, source_target_pairs={{0,2},{1,3},{2,0},{3,1},{4,6},{5,7},{6,4},{7,5},{8,10},{9,11},{10,... | collective-permute-start | bytes 1376264 | tf_op jit(solution)/shard_map/ppermute | solution.py:18
  145.9 11.9 %collective-permute-start.41 = (bf16[64,3584]{1,0:T(8,128)(2,1)S(1)}, bf16[64,3584]{1,0:T(8,128)(2,1)S(1)}, u32[]{:S(2)}, u32[]{:S(2)}) collective-permute-start(bf16[64,3584]{1,0:T(8,128)(2,1)S(1)} %get-tuple-element.127), channel_id=1, source_target_pairs={{0,1},{1,0},{2,3},{3,2},{4,5},{5,4},{6,7},{7,6},{8,9},{9,8},{10,11... | collective-permute-start | bytes 1376264 | tf_op jit(solution)/shard_map/ppermute | solution.py:18
  146.1 11.7 %collective-permute-start.40 = (bf16[64,3584]{1,0:T(8,128)(2,1)S(1)}, bf16[64,3584]{1,0:T(8,128)(2,1)S(1)}, u32[]{:S(2)}, u32[]{:S(2)}) collective-permute-start(bf16[64,3584]{1,0:T(8,128)(2,1)S(1)} %get-tuple-element.125), channel_id=1, source_target_pairs={{0,1},{1,0},{2,3},{3,2},{4,5},{5,4},{6,7},{7,6},{8,9},{9,8},{10,11... | collective-permute-start | bytes 1376264 | tf_op jit(solution)/shard_map/ppermute | solution.py:18
  146.4 11.9 %collective-permute-start.39 = (bf16[64,3584]{1,0:T(8,128)(2,1)S(1)}, bf16[64,3584]{1,0:T(8,128)(2,1)S(1)}, u32[]{:S(2)}, u32[]{:S(2)}) collective-permute-start(bf16[64,3584]{1,0:T(8,128)(2,1)S(1)} %get-tuple-element.123), channel_id=1, source_target_pairs={{0,1},{1,0},{2,3},{3,2},{4,5},{5,4},{6,7},{7,6},{8,9},{9,8},{10,11... | collective-permute-start | bytes 1376264 | tf_op jit(solution)/shard_map/ppermute | solution.py:18
  157.3 9.6 %collective-permute-start.43 = (bf16[64,3584]{1,0:T(8,128)(2,1)S(1)}, bf16[64,3584]{1,0:T(8,128)(2,1)S(1)}, u32[]{:S(2)}, u32[]{:S(2)}) collective-permute-start(bf16[64,3584]{1,0:T(8,128)(2,1)S(1)} %get-tuple-element.130), channel_id=1, source_target_pairs={{0,1},{1,0},{2,3},{3,2},{4,5},{5,4},{6,7},{7,6},{8,9},{9,8},{10,11... | collective-permute-start | bytes 1376264 | tf_op jit(solution)/shard_map/ppermute | solution.py:18
  157.3 9.6 %collective-permute-start.46 = (bf16[64,3584]{1,0:T(8,128)(2,1)S(1)}, bf16[64,3584]{1,0:T(8,128)(2,1)S(1)}, u32[]{:S(2)}, u32[]{:S(2)}) collective-permute-start(bf16[64,3584]{1,0:T(8,128)(2,1)S(1)} %get-tuple-element.136), channel_id=1, source_target_pairs={{0,1},{1,0},{2,3},{3,2},{4,5},{5,4},{6,7},{7,6},{8,9},{9,8},{10,11... | collective-permute-start | bytes 1376264 | tf_op jit(solution)/shard_map/ppermute | solution.py:18
  157.8 9.1 %collective-permute-start.45 = (bf16[64,3584]{1,0:T(8,128)(2,1)S(1)}, bf16[64,3584]{1,0:T(8,128)(2,1)S(1)}, u32[]{:S(2)}, u32[]{:S(2)}) collective-permute-start(bf16[64,3584]{1,0:T(8,128)(2,1)S(1)} %get-tuple-element.134), channel_id=1, source_target_pairs={{0,1},{1,0},{2,3},{3,2},{4,5},{5,4},{6,7},{7,6},{8,9},{9,8},{10,11... | collective-permute-start | bytes 1376264 | tf_op jit(solution)/shard_map/ppermute | solution.py:18
  157.8 9.1 %collective-permute-start.44 = (bf16[64,3584]{1,0:T(8,128)(2,1)S(1)}, bf16[64,3584]{1,0:T(8,128)(2,1)S(1)}, u32[]{:S(2)}, u32[]{:S(2)}) collective-permute-start(bf16[64,3584]{1,0:T(8,128)(2,1)S(1)} %get-tuple-element.132), channel_id=1, source_target_pairs={{0,1},{1,0},{2,3},{3,2},{4,5},{5,4},{6,7},{7,6},{8,9},{9,8},{10,11... | collective-permute-start | bytes 1376264 | tf_op jit(solution)/shard_map/ppermute | solution.py:18
  168.4 8.0 %copy-start.1 = (bf16[7168,64]{0,1:T(8,128)(2,1)S(1)}, bf16[7168,64]{0,1:T(8,128)(2,1)}, u32[]{:S(2)}) copy-start(bf16[7168,64]{0,1:T(8,128)(2,1)} %param.10) | copy-start | bytes 2752516

commit v17 on v14

--- a/solution.py
+++ b/solution.py
@@ -338,31 +338,31 @@
 
     sent0, kept0 = far_terms(blocks, 0, 2, beside)
     sent1, kept1 = far_terms(blocks, 1, 2, sent0[0])
-    pair0, sum0 = pair_sum(sent0, kept0, partner, *later[1:], sent1[0])
+    acts_low, grads_low = jnp.split(after(low, sent1[0]) + partner, 2, axis=1)
+    example_grad = example_gradients(
+        acts_low, grads_low, token_example[0], example_group.shape[0]
+    )
+    pair0, sum0 = pair_sum(sent0, kept0, *later[1:], example_grad)
     pair1, sum1 = pair_sum(sent1, kept1, *later[1:])
 
     beside = spread_first(after(beside, pair1))
     sent, kept = far_terms(later, 0, 2, pair0, pair1)
-    pair2, sum2 = pair_sum(sent, kept, *beside[1:], outs=2)
+    pair2, sum2 = pair_sum(sent, kept, *beside[1:])
 
     beside = spread_last(beside, pair2)
     own = spread_first(after(own, pair2))
-    acts_low, grads_low = jnp.split(after(low, pair2, *sum0) + partner, 2, axis=1)
-    example_grad = example_gradients(
-        acts_low, grads_low, token_example[0], example_group.shape[0]
-    )
-    gathered = gather_examples(example_grad, example_group)
-    sent, kept = far_terms(later, 1, 2, example_grad)
-    pair3, sum3 = pair_sum(sent, kept, *own, *beside, outs=2)
+    gathered = gather_examples(after(example_grad, pair1), example_group)
+    sent, kept = far_terms(later, 1, 2, pair2, *sum0, *gathered)
+    every = order_examples(after(gathered, sent[0]))
+    fisher, group_grad = fisher_and_groups(every, example_grad.shape[1])
+    pair3, sum3 = pair_sum(sent, kept, *own, *beside, fisher, group_grad, outs=2)
 
     own = spread_last(own, pair3)
     beside = [after(beside[0], pair3, *sum1)] + beside[1:]
     near0 = block_terms(beside, down_weight, 0, 2, [rows // 2] * 4)
-    near0 = [swap(after(term, sum2[0], *own[3:]), 1) for term in near0]
+    near0 = [swap(after(term, *own[3:]), 1) for term in near0]
     adds0 = gather_sums(near0, sum0 + sum2)
-    every = order_examples(after(gathered, near0[0]))
-    fisher, group_grad = fisher_and_groups(every, example_grad.shape[1])
-    beside = [after(beside[0], near0[0], fisher, group_grad)] + beside[1:]
+    beside = [after(beside[0], near0[0], *sum2)] + beside[1:]
     near1 = block_terms(beside, down_weight, 1, 2, [rows // 2] * 4)
 
     near1 = [swap(after(term, sum3[0]), 1) for term in near1]

time: 182 us -> 172 us (0.945)
  waiting for transfers between devices: 56.9 us -> 51 us
  other arithmetic: 3.07 us -> 0.62 us
  Pallas kernels: 66.6 us -> 64.3 us
  local copies, waits for them, and re-layouts: 11.3 us -> 13.5 us
    ppermute x30 -> x29, waiting for transfers between devices: 23.7 us -> 12 us  [swap(): return lax.ppermute(value, 'dp', [(d, d ^ step) for d in range(size)])]
    ppermute x16, waiting for transfers between devices: 33.2 us -> 38.9 us  [across(): return lax.ppermute(value, 'tensor', pairs)]
    unnamed x40 -> x38, local copies, waits for them, and re-layouts: 8.53 us -> 10.7 us
    ppermute x30 -> x29, starting transfers between devices: 14.6 us -> 13.4 us  [swap(): return lax.ppermute(value, 'dp', [(d, d ^ step) for d in range(size)])]
  transfers between devices with their start and end apart: 46 -> 45, of which waited for: 21 -> 18; matrix products, arithmetic and copies ran while one was open for 6% -> 5% of each run, Pallas kernels for 32% -> 33%
where the time goes in v17:
time: 172 us
  Pallas kernels  64.3 us (37%)
  waiting for transfers between devices  51 us (30%)
  starting transfers between devices  33.6 us (20%)
  local copies, waits for them, and re-layouts  13.5 us (8%)
  matrix products  7.55 us (4%)
    pallas_call x8, Pallas kernels, block_terms(): pl.pallas_call(functools.partial(terms_kernel, size, len(blocks), part *...  58 us
    ppermute x16, waiting for transfers between devices, across(): return lax.ppermute(value, 'tensor', pairs)  38.9 us
    ppermute x16, starting transfers between devices, across(): return lax.ppermute(value, 'tensor', pairs)  20.2 us
    ppermute x29, starting transfers between devices, swap(): return lax.ppermute(value, 'dp', [(d, d ^ step) for d in range(size)])  13.4 us
    ppermute x29, waiting for transfers between devices, swap(): return lax.ppermute(value, 'dp', [(d, d ^ step) for d in range(size)])  12 us
    unnamed x38, local copies, waits for them, and re-layouts  10.7 us
    pallas_call x4, Pallas kernels, add_pieces(): pl.pallas_call(functools.partial(add_kernel, len(pieces)), out_shape=[jax...  4.91 us
  transfers between devices with their start and end apart: 45, of which 18 were waited for; matrix products, arithmetic and copies ran while one was open for 5% of the time, Pallas kernels for 33%

profile of v17, /device:TPU:0, one launch (start us, length us, event | category | flops | bytes accessed | tf_op | source)
XLA Modules:
  0.0 171.9 jit_solution(9072772281827378664)
XLA Ops:
  0.7 2.0 %constant_dynamic-slice_fusion = (bf16[1,1,512,256]{3,2,1,0:T(8,128)(2,1)S(1)}, bf16[1,1,512,256]{3,2,1,0:T(8,128)(2,1)S(1)}, bf16[1,1,512,256]{3,2,1,0:T(8,128)(2,1)S(1)}, bf16[1,1,512,256]{3,2,1,0:T(8,128)(2,1)}) fusion(bf16[1,4,512,256]{3,2,1,0:T(8,128)(2,1)} %param.8, s32[]{:T(128)S(6)} %select_n.96, s32[]{:T(128)S(6)} %select_n.95, s32[]{:T(128)S(6)} %select_n.94, ...), kind=kLoop, calls=%fused_computation.32 | loop fusion | bytes 2097168 | tf_op jit(solution)/shard_map/dynamic-slice.7
  2.9 3.0 %collective-permute-start.3 = (bf16[128,512]{1,0:T(8,128)(2,1)S(1)}, bf16[128,512]{1,0:T(8,128)(2,1)S(1)}, u32[]{:S(2)}, u32[]{:S(2)}) collective-permute-start(bf16[128,512]{1,0:T(8,128)(2,1)S(1)} %get-tuple-element.131), channel_id=1, source_target_pairs={{0,2},{1,3},{2,0},{3,1},{4,6},{5,7},{6,4},{7,5},{8,10},{9,11},{10,... | collective-permute-start | bytes 393224 | tf_op jit(solution)/shard_map/ppermute | solution.py:18
  6.2 3.3 %fusion.15 = f32[256,64]{0,1:T(8,128)S(1)} fusion(bf16[256,7168]{1,0:T(8,128)(2,1)} %param.7, bf16[7168,64]{0,1:T(8,128)(2,1)S(1)} %copy-done), kind=kOutput, calls=%fused_computation.38 | convolution fusion | flops 234881024 | bytes 4653056 | tf_op jit(solution)/shard_map/dot_general | solution.py:278
  9.8 1.6 collective-permute-start.11
  11.4 1.2 collective-permute-start.1
  12.6 3.0 %collective-permute-start.6 = (bf16[256,512]{1,0:T(8,128)(2,1)S(1)}, bf16[256,512]{1,0:T(8,128)(2,1)S(1)}, u32[]{:S(2)}, u32[]{:S(2)}) collective-permute-start(bf16[256,512]{1,0:T(8,128)(2,1)S(1)} %pad_maximum_fusion.1.refs_0_), channel_id=1, source_target_pairs={{0,12},{4,8},{8,4},{12,0},{1,13},{5,9},{9,5},{13,1},{2,14},{6,10},... | collective-permute-start | bytes 786440 | tf_op jit(solution)/shard_map/ppermute | solution.py:28
  15.7 1.4 collective-permute-start.4
  17.5 6.5 %collective-permute-done.6.refs_3_ = bf16[256,512]{1,0:T(8,128)(2,1)S(1)} collective-permute-done((bf16[256,512]{1,0:T(8,128)(2,1)S(1)}, bf16[256,512]{1,0:T(8,128)(2,1)S(1)}, u32[]{:S(2)}, u32[]{:S(2)}) %collective-permute-start.6) | collective-permute-done | bytes 262176 | tf_op jit(solution)/shard_map/ppermute | solution.py:28
  24.0 15.0 %collective-permute-done.5.refs_2_ = bf16[256,512]{1,0:T(8,128)(2,1)S(1)} collective-permute-done((bf16[256,512]{1,0:T(8,128)(2,1)S(1)}, bf16[256,512]{1,0:T(8,128)(2,1)S(1)}, u32[]{:S(2)}, u32[]{:S(2)}) %collective-permute-start.5) | collective-permute-done | bytes 262176 | tf_op jit(solution)/shard_map/ppermute | solution.py:28
  39.1 2.7 %collective-permute-start.10 = (bf16[256,512]{1,0:T(8,128)(2,1)S(1)}, bf16[256,512]{1,0:T(8,128)(2,1)S(1)}, u32[]{:S(2)}, u32[]{:S(2)}) collective-permute-start(bf16[256,512]{1,0:T(8,128)(2,1)S(1)} %pad_maximum_fusion.refs_0_), channel_id=1, source_target_pairs={{0,12},{4,8},{8,4},{12,0},{1,13},{5,9},{9,5},{13,1},{2,14},{6,10},... | collective-permute-start | bytes 786440 | tf_op jit(solution)/shard_map/ppermute | solution.py:28
  41.8 2.0 %collective-permute-start.9 = (bf16[256,512]{1,0:T(8,128)(2,1)S(1)}, bf16[256,512]{1,0:T(8,128)(2,1)S(1)}, u32[]{:S(2)}, u32[]{:S(2)}) collective-permute-start(bf16[256,512]{1,0:T(8,128)(2,1)S(1)} %pad_maximum_fusion.refs_0_), channel_id=1, source_target_pairs={{0,8},{4,12},{8,0},{12,4},{1,9},{5,13},{9,1},{13,5},{2,10},{6,14},... | collective-permute-start | bytes 786440 | tf_op jit(solution)/shard_map/ppermute | solution.py:28
  43.8 6.9 %terms.8 = (bf16[64,3584]{1,0:T(8,128)(2,1)S(1)}, bf16[64,3584]{1,0:T(8,128)(2,1)S(1)}, bf16[128,3584]{1,0:T(8,128)(2,1)S(1)}) custom-call(s32[1]{0:T(128)} %bitcast.place_ref, bf16[256,512]{1,0:T(8,128)(2,1)S(1)} %pad_maximum_fusion.1.refs_0_, bf16[256,512]{1,0:T(8,128)(2,1)S(1)} %collective-permute-done.4.refs_1_, ...), custom_call_target="tpu_custom_call" | custom-call | flops 469762048 | bytes 1000 | tf_op jit(solution)/shard_map/terms/pallas_call | solution.py:135
  50.7 0.9 copy-done.7
  51.6 0.8 copy-done.13
  52.4 7.0 %terms.9 = (bf16[64,3584]{1,0:T(8,128)(2,1)S(1)}, bf16[64,3584]{1,0:T(8,128)(2,1)S(1)}, bf16[128,3584]{1,0:T(8,128)(2,1)S(1)}) custom-call(s32[1]{0:T(128)} %bitcast.place_ref, bf16[256,512]{1,0:T(8,128)(2,1)S(1)} %pad_maximum_fusion.1.refs_0_, bf16[256,512]{1,0:T(8,128)(2,1)S(1)} %collective-permute-done.4.refs_1_, ...), custom_call_target="tpu_custom_call" | custom-call | flops 469762048 | bytes 1000 | tf_op jit(solution)/shard_map/terms/pallas_call | solution.py:135
  59.5 0.9 copy-done.5
  60.4 0.8 copy-done.11
  61.8 8.5 %collective-permute-done.9.refs_2_ = bf16[256,512]{1,0:T(8,128)(2,1)S(1)} collective-permute-done((bf16[256,512]{1,0:T(8,128)(2,1)S(1)}, bf16[256,512]{1,0:T(8,128)(2,1)S(1)}, u32[]{:S(2)}, u32[]{:S(2)}) %collective-permute-start.9) | collective-permute-done | bytes 262176 | tf_op jit(solution)/shard_map/ppermute | solution.py:28
  71.3 1.0 collective-permute-done.13.refs_0_
  72.3 1.3 collective-permute-done.14.refs_1_
  73.6 1.2 copy-done.8
  74.8 1.7 pair.4
  76.5 0.6 collective-permute-start.21
  77.1 1.2 copy-done.6
  78.8 0.9 copy-done.2
  79.8 2.3 %collective-permute-start.17 = (bf16[256,512]{1,0:T(8,128)(2,1)S(1)}, bf16[256,512]{1,0:T(8,128)(2,1)S(1)}, u32[]{:S(2)}, u32[]{:S(2)}) collective-permute-start(bf16[256,512]{1,0:T(8,128)(2,1)S(1)} %collective-permute-done.7.refs_0_), channel_id=1, source_target_pairs={{0,4},{4,0},{8,12},{12,8},{1,5},{5,1},{9,13},{13,9},{2,6},{6,2},{1... | collective-permute-start | bytes 786440 | tf_op jit(solution)/shard_map/ppermute | solution.py:28
  82.1 7.5 %terms.10 = (bf16[64,3584]{1,0:T(8,128)(2,1)}, bf16[64,3584]{1,0:T(8,128)(2,1)S(1)}, bf16[128,3584]{1,0:T(8,128)(2,1)S(1)}) custom-call(s32[1]{0:T(128)} %bitcast.place_ref, bf16[256,512]{1,0:T(8,128)(2,1)S(1)} %pad_maximum_fusion.refs_0_, bf16[256,512]{1,0:T(8,128)(2,1)S(1)} %collective-permute-done.8.refs_1_, ...), custom_call_target="tpu_custom_call" | custom-call | flops 469762048 | bytes 1000 | tf_op jit(solution)/shard_map/terms/pallas_call | solution.py:135
  89.6 1.0 copy-done.3
  90.6 3.0 %collective-permute-done.18.refs_2_ = bf16[256,512]{1,0:T(8,128)(2,1)S(1)} collective-permute-done((bf16[256,512]{1,0:T(8,128)(2,1)S(1)}, bf16[256,512]{1,0:T(8,128)(2,1)S(1)}, u32[]{:S(2)}, u32[]{:S(2)}) %collective-permute-start.18) | collective-permute-done | bytes 262176 | tf_op jit(solution)/shard_map/ppermute | solution.py:28
  94.3 0.8 collective-permute-start.24
  95.2 0.9 collective-permute-start.23
  96.2 0.8 copy-done.9
  97.2 1.2 collective-permute-start.31
  98.5 1.2 copy-done.4
  99.7 1.0 copy-done.10
  100.7 2.1 %pair.6 = bf16[128,3584]{1,0:T(8,128)(2,1)S(1)} custom-call(bf16[128,3584]{1,0:T(8,128)(2,1)S(1)} %copy-done.4, bf16[64,3584]{1,0:T(8,128)(2,1)} %collective-permute-done.19.refs_0_, bf16[64,3584]{1,0:T(8,128)(2,1)S(1)} %copy-done.10), custom_call_target="tpu_custom_call" | custom-call | flops 1000 | bytes 1000 | tf_op jit(solution)/shard_map/pair/pallas_call | solution.py:181
  103.1 2.7 %collective-permute-start.25 = (bf16[256,512]{1,0:T(8,128)(2,1)S(1)}, bf16[256,512]{1,0:T(8,128)(2,1)S(1)}, u32[]{:S(2)}, u32[]{:S(2)}) collective-permute-start(bf16[256,512]{1,0:T(8,128)(2,1)S(1)} %bitcast.39), channel_id=1, source_target_pairs={{0,4},{4,0},{8,12},{12,8},{1,5},{5,1},{9,13},{13,9},{2,6},{6,2},{1... | collective-permute-start | bytes 786440 | tf_op jit(solution)/shard_map/ppermute | solution.py:28
  105.8 0.7 collective-permute-start.27
  106.5 1.3 collective-permute-start.28
  107.8 6.9 %terms.11 = (bf16[64,3584]{1,0:T(8,128)(2,1)S(1)}, bf16[64,3584]{1,0:T(8,128)(2,1)S(1)}, bf16[128,3584]{1,0:T(8,128)(2,1)S(1)}) custom-call(s32[1]{0:T(128)} %bitcast.place_ref, bf16[256,512]{1,0:T(8,128)(2,1)S(1)} %pad_maximum_fusion.refs_0_, bf16[256,512]{1,0:T(8,128)(2,1)S(1)} %collective-permute-done.8.refs_1_, ...), custom_call_target="tpu_custom_call" | custom-call | flops 469762048 | bytes 1000 | tf_op jit(solution)/shard_map/terms/pallas_call | solution.py:135
  115.1 0.9 fusion.6
  115.9 1.7 collective-permute-done.26.refs_2_
  117.6 0.6 collective-permute-start.35
  118.2 2.7 %fusion.4 = f32[1024,1024]{1,0:T(8,128)} fusion(bf16[16,4224]{1,0:T(8,128)(2,1)S(1)} %pad_maximum_fusion.2, s32[]{:T(128)S(6)} %select_n.121, s32[]{:T(128)S(6)} %select_n.122), kind=kOutput, calls=%fused_computation.20 | convolution fusion | flops 33554432 | bytes 4259848 | tf_op jit(solution)/shard_map/dot_general | solution.py:267
  120.9 2.4 %collective-permute-done.28.refs_4_ = bf16[256,512]{1,0:T(8,128)(2,1)S(1)} collective-permute-done((bf16[256,512]{1,0:T(8,128)(2,1)S(1)}, bf16[256,512]{1,0:T(8,128)(2,1)S(1)}, u32[]{:S(2)}, u32[]{:S(2)}) %collective-permute-start.28) | collective-permute-done | bytes 262176 | tf_op jit(solution)/shard_map/ppermute | solution.py:28
  123.8 1.3 collective-permute-done.29.refs_0_
  125.1 0.7 collective-permute-done.30.refs_1_
  125.8 0.5 pair.7
  126.3 0.7 collective-permute-start.32
  127.0 1.5 collective-permute-start.33
  128.5 6.9 %terms.12 = (bf16[64,3584]{1,0:T(8,128)(2,1)S(1)}, bf16[64,3584]{1,0:T(8,128)(2,1)S(1)}, bf16[64,3584]{1,0:T(8,128)(2,1)S(1)}, bf16[64,3584]{1,0:T(8,128)(2,1)S(1)}) custom-call(s32[1]{0:T(128)} %bitcast.place_ref, bf16[256,512]{1,0:T(8,128)(2,1)S(1)} %collective-permute-done.7.refs_0_, bf16[256,512]{1,0:T(8,128)(2,1)S(1)} %collective-permute-done.17.refs_1_, ...), custom_call_target="tpu_custom_call" | custom-call | flops 469762048 | bytes 1000 | tf_op jit(solution)/shard_map/terms/pallas_call | solution.py:135
  135.5 1.8 %collective-permute-done.33.refs_4_ = bf16[256,512]{1,0:T(8,128)(2,1)S(1)} collective-permute-done((bf16[256,512]{1,0:T(8,128)(2,1)S(1)}, bf16[256,512]{1,0:T(8,128)(2,1)S(1)}, u32[]{:S(2)}, u32[]{:S(2)}) %collective-permute-start.33) | collective-permute-done | bytes 262176 | tf_op jit(solution)/shard_map/ppermute | solution.py:28
  137.3 0.6 collective-permute-start.36
  138.4 1.5 collective-permute-done.35.refs_5_
  139.9 6.9 %terms.13 = (bf16[64,3584]{1,0:T(8,128)(2,1)S(1)}, bf16[64,3584]{1,0:T(8,128)(2,1)S(1)}, bf16[64,3584]{1,0:T(8,128)(2,1)S(1)}, bf16[64,3584]{1,0:T(8,128)(2,1)S(1)}) custom-call(s32[1]{0:T(128)} %bitcast.place_ref, bf16[256,512]{1,0:T(8,128)(2,1)S(1)} %collective-permute-done.7.refs_0_, bf16[256,512]{1,0:T(8,128)(2,1)S(1)} %collective-permute-done.17.refs_1_, ...), custom_call_target="tpu_custom_call" | custom-call | flops 469762048 | bytes 1000 | tf_op jit(solution)/shard_map/terms/pallas_call | solution.py:135
  146.8 3.4 %collective-permute-done.36.refs_7_ = bf16[64,3584]{1,0:T(8,128)(2,1)S(1)} collective-permute-done((bf16[64,3584]{1,0:T(8,128)(2,1)S(1)}, bf16[64,3584]{1,0:T(8,128)(2,1)S(1)}, u32[]{:S(2)}, u32[]{:S(2)}) %collective-permute-start.36) | collective-permute-done | bytes 458784 | tf_op jit(solution)/shard_map/ppermute | solution.py:18
  151.2 0.6 collective-permute-start.44
  151.8 0.8 sums.3.refs_6_
  152.7 0.6 collective-permute-done.38.refs_1_
  153.3 0.7 collective-permute-done.37.refs_0_
  154.0 0.6 sums.2.refs_6_
  154.6 7.7 %terms.14.refs_9_ = bf16[256,7168]{1,0:T(8,128)(2,1)} custom-call(s32[1]{0:T(128)} %bitcast.place_ref, bf16[256,512]{1,0:T(8,128)(2,1)S(1)} %bitcast.41, bf16[256,512]{1,0:T(8,128)(2,1)S(1)} %collective-permute-done.25.refs_1_, bf16[256,512]{1,0:T(8,128)(2,1)S(1)} %collective-permute-done.26.refs_2_, bf16[256,512]{1,0:T(8,128)(2,1)S(1)} %collective-permute-done.32.refs_3_, ...), custom_call_target="tpu_custom_call" | custom-call | flops 469762048 | bytes 1000 | tf_op jit(solution)/shard_map/terms/pallas_call | solution.py:135
  162.3 1.4 collective-permute-done.44.refs_8_
  163.7 8.0 %terms.15 = bf16[256,7168]{1,0:T(8,128)(2,1)} custom-call(s32[1]{0:T(128)} %bitcast.place_ref, bf16[256,512]{1,0:T(8,128)(2,1)S(1)} %bitcast.42, bf16[256,512]{1,0:T(8,128)(2,1)S(1)} %collective-permute-done.25.refs_1_, bf16[256,512]{1,0:T(8,128)(2,1)S(1)} %collective-permute-done.26.refs_2_, ...), custom_call_target="tpu_custom_call", output_to_operand_aliasing={{}: (10, {})} | custom-call | flops 469762048 | bytes 1000 | tf_op jit(solution)/shard_map/terms/pallas_call | solution.py:135
  (107 shorter events, 7.2 us)
Async XLA Ops:
  0.6 5.5 %copy-start = (bf16[7168,64]{0,1:T(8,128)(2,1)S(1)}, bf16[7168,64]{0,1:T(8,128)(2,1)}, u32[]{:S(2)}) copy-start(bf16[7168,64]{0,1:T(8,128)(2,1)} %param.10) | copy-start | bytes 2752516
  2.7 6.7 %copy-start.14 = (bf16[1,4,512,256]{3,2,1,0:T(8,128)(2,1)S(1)}, bf16[1,4,512,256]{3,2,1,0:T(8,128)(2,1)}, u32[]{:S(2)}) copy-start(bf16[1,4,512,256]{3,2,1,0:T(8,128)(2,1)} %param.8) | copy-start | bytes 3145732
  2.7 6.7 %copy-start.16 = (bf16[1,4,512,64]{2,3,1,0:T(8,128)(2,1)S(1)}, bf16[1,4,512,64]{2,3,1,0:T(8,128)(2,1)}, u32[]{:S(2)}) copy-start(bf16[1,4,512,64]{2,3,1,0:T(8,128)(2,1)} %param.11) | copy-start | bytes 786436
  2.9 9.7 %collective-permute-start.3 = (bf16[128,512]{1,0:T(8,128)(2,1)S(1)}, bf16[128,512]{1,0:T(8,128)(2,1)S(1)}, u32[]{:S(2)}, u32[]{:S(2)}) collective-permute-start(bf16[128,512]{1,0:T(8,128)(2,1)S(1)} %get-tuple-element.131), channel_id=1, source_target_pairs={{0,2},{1,3},{2,0},{3,1},{4,6},{5,7},{6,4},{7,5},{8,10},{9,11},{10,... | collective-permute-start | bytes 393224 | tf_op jit(solution)/shard_map/ppermute | solution.py:18
  6.0 9.6 %copy-start.17 = (s32[1,256]{1,0:T(1,128)S(1)}, s32[1,256]{1,0:T(1,128)}, u32[]{:S(2)}) copy-start(s32[1,256]{1,0:T(1,128)} %param.12) | copy-start | bytes 3076
  6.1 6.5 %collective-permute-start.2 = (bf16[128,512]{1,0:T(8,128)(2,1)S(1)}, bf16[128,512]{1,0:T(8,128)(2,1)S(1)}, u32[]{:S(2)}, u32[]{:S(2)}) collective-permute-start(bf16[128,512]{1,0:T(8,128)(2,1)S(1)} %get-tuple-element.129), channel_id=1, source_target_pairs={{0,3},{1,2},{2,1},{3,0},{4,7},{5,6},{6,5},{7,4},{8,11},{9,10},{10,... | collective-permute-start | bytes 393224 | tf_op jit(solution)/shard_map/ppermute | solution.py:18
  9.8 7.6 %collective-permute-start.11 = (f32[256,128]{0,1:T(8,128)S(1)}, f32[256,128]{0,1:T(8,128)S(1)}, u32[]{:S(2)}, u32[]{:S(2)}) collective-permute-start(f32[256,128]{0,1:T(8,128)S(1)} %pad_maximum_fusion.3), channel_id=1, source_target_pairs={{0,4},{4,0},{8,12},{12,8},{1,5},{5,1},{9,13},{13,9},{2,6},{6,2},{1... | collective-permute-start | bytes 393224 | tf_op jit(solution)/shard_map/ppermute | solution.py:28
  11.4 27.6 %collective-permute-start.1 = (bf16[128,512]{1,0:T(8,128)(2,1)S(1)}, bf16[128,512]{1,0:T(8,128)(2,1)S(1)}, u32[]{:S(2)}, u32[]{:S(2)}) collective-permute-start(bf16[128,512]{1,0:T(8,128)(2,1)S(1)} %get-tuple-element.132), channel_id=1, source_target_pairs={{0,2},{1,3},{2,0},{3,1},{4,6},{5,7},{6,4},{7,5},{8,10},{9,11},{10,... | collective-permute-start | bytes 393224 | tf_op jit(solution)/shard_map/ppermute | solution.py:18
  12.6 11.4 %collective-permute-start.6 = (bf16[256,512]{1,0:T(8,128)(2,1)S(1)}, bf16[256,512]{1,0:T(8,128)(2,1)S(1)}, u32[]{:S(2)}, u32[]{:S(2)}) collective-permute-start(bf16[256,512]{1,0:T(8,128)(2,1)S(1)} %pad_maximum_fusion.1.refs_0_), channel_id=1, source_target_pairs={{0,12},{4,8},{8,4},{12,0},{1,13},{5,9},{9,5},{13,1},{2,14},{6,10},... | collective-permute-start | bytes 786440 | tf_op jit(solution)/shard_map/ppermute | solution.py:28
  15.7 23.3 %collective-permute-start.5 = (bf16[256,512]{1,0:T(8,128)(2,1)S(1)}, bf16[256,512]{1,0:T(8,128)(2,1)S(1)}, u32[]{:S(2)}, u32[]{:S(2)}) collective-permute-start(bf16[256,512]{1,0:T(8,128)(2,1)S(1)} %pad_maximum_fusion.1.refs_0_), channel_id=1, source_target_pairs={{0,8},{4,12},{8,0},{12,4},{1,9},{5,13},{9,1},{13,5},{2,10},{6,14},... | collective-permute-start | bytes 786440 | tf_op jit(solution)/shard_map/ppermute | solution.py:28
  15.7 23.3 %collective-permute-start.4 = (bf16[256,512]{1,0:T(8,128)(2,1)S(1)}, bf16[256,512]{1,0:T(8,128)(2,1)S(1)}, u32[]{:S(2)}, u32[]{:S(2)}) collective-permute-start(bf16[256,512]{1,0:T(8,128)(2,1)S(1)} %pad_maximum_fusion.1.refs_0_), channel_id=1, source_target_pairs={{0,4},{4,0},{8,12},{12,8},{1,5},{5,1},{9,13},{13,9},{2,6},{6,2},{1... | collective-permute-start | bytes 786440 | tf_op jit(solution)/shard_map/ppermute | solution.py:28
  17.4 21.7 %collective-permute-start = (bf16[128,512]{1,0:T(8,128)(2,1)S(1)}, bf16[128,512]{1,0:T(8,128)(2,1)S(1)}, u32[]{:S(2)}, u32[]{:S(2)}) collective-permute-start(bf16[128,512]{1,0:T(8,128)(2,1)S(1)} %get-tuple-element.130), channel_id=1, source_target_pairs={{0,3},{1,2},{2,1},{3,0},{4,7},{5,6},{6,5},{7,4},{8,11},{9,10},{10,... | collective-permute-start | bytes 393224 | tf_op jit(solution)/shard_map/ppermute | solution.py:18
  24.0 15.0 %collective-permute-start.7 = (bf16[256,512]{1,0:T(8,128)(2,1)S(1)}, bf16[256,512]{1,0:T(8,128)(2,1)S(1)}, u32[]{:S(2)}, u32[]{:S(2)}) collective-permute-start(bf16[256,512]{1,0:T(8,128)(2,1)S(1)} %bitcast.46), channel_id=1, source_target_pairs={{0,1},{1,0},{2,3},{3,2},{4,5},{5,4},{6,7},{7,6},{8,9},{9,8},{10,11... | collective-permute-start | bytes 786440 | tf_op jit(solution)/shard_map/ppermute | solution.py:18
  39.0 22.2 %collective-permute-start.12 = (f32[256,128]{0,1:T(8,128)S(1)}, f32[256,128]{0,1:T(8,128)S(1)}, u32[]{:S(2)}, u32[]{:S(2)}) collective-permute-start(f32[256,128]{0,1:T(8,128)S(1)} %fusion.14), channel_id=1, source_target_pairs={{0,8},{4,12},{8,0},{12,4},{1,9},{5,13},{9,1},{13,5},{2,10},{6,14},... | collective-permute-start | bytes 393224 | tf_op jit(solution)/shard_map/ppermute | solution.py:28
  39.1 22.8 %collective-permute-start.10 = (bf16[256,512]{1,0:T(8,128)(2,1)S(1)}, bf16[256,512]{1,0:T(8,128)(2,1)S(1)}, u32[]{:S(2)}, u32[]{:S(2)}) collective-permute-start(bf16[256,512]{1,0:T(8,128)(2,1)S(1)} %pad_maximum_fusion.refs_0_), channel_id=1, source_target_pairs={{0,12},{4,8},{8,4},{12,0},{1,13},{5,9},{9,5},{13,1},{2,14},{6,10},... | collective-permute-start | bytes 786440 | tf_op jit(solution)/shard_map/ppermute | solution.py:28
  41.8 28.5 %collective-permute-start.9 = (bf16[256,512]{1,0:T(8,128)(2,1)S(1)}, bf16[256,512]{1,0:T(8,128)(2,1)S(1)}, u32[]{:S(2)}, u32[]{:S(2)}) collective-permute-start(bf16[256,512]{1,0:T(8,128)(2,1)S(1)} %pad_maximum_fusion.refs_0_), channel_id=1, source_target_pairs={{0,8},{4,12},{8,0},{12,4},{1,9},{5,13},{9,1},{13,5},{2,10},{6,14},... | collective-permute-start | bytes 786440 | tf_op jit(solution)/shard_map/ppermute | solution.py:28
  43.8 26.5 %collective-permute-start.8 = (bf16[256,512]{1,0:T(8,128)(2,1)S(1)}, bf16[256,512]{1,0:T(8,128)(2,1)S(1)}, u32[]{:S(2)}, u32[]{:S(2)}) collective-permute-start(bf16[256,512]{1,0:T(8,128)(2,1)S(1)} %pad_maximum_fusion.refs_0_), channel_id=1, source_target_pairs={{0,4},{4,0},{8,12},{12,8},{1,5},{5,1},{9,13},{13,9},{2,6},{6,2},{1... | collective-permute-start | bytes 786440 | tf_op jit(solution)/shard_map/ppermute | solution.py:28
  50.7 0.9 copy-start.7
  51.6 0.8 copy-start.13
  52.4 7.0 %copy-start.12 = (bf16[64,3584]{1,0:T(8,128)(2,1)}, bf16[64,3584]{1,0:T(8,128)(2,1)S(1)}, u32[]{:S(2)}) copy-start(bf16[64,3584]{1,0:T(8,128)(2,1)S(1)} %get-tuple-element.75) | copy-start | bytes 1376260
  59.5 0.9 copy-start.5
  60.4 0.8 copy-start.11
  61.2 20.9 %copy-start.18 = (s32[4]{0:T(128)S(1)}, s32[4]{0:T(128)}, u32[]{:S(2)}) copy-start(s32[4]{0:T(128)} %param.13) | copy-start | bytes 52
  70.3 2.0 %collective-permute-start.13 = (bf16[64,3584]{1,0:T(8,128)(2,1)}, bf16[64,3584]{1,0:T(8,128)(2,1)S(1)}, u32[]{:S(2)}, u32[]{:S(2)}) collective-permute-start(bf16[64,3584]{1,0:T(8,128)(2,1)} %copy-done.13), channel_id=1, source_target_pairs={{0,1},{1,0},{2,3},{3,2},{4,5},{5,4},{6,7},{7,6},{8,9},{9,8},{10,11... | collective-permute-start | bytes 1376264 | tf_op jit(solution)/shard_map/ppermute | solution.py:18
  70.3 3.3 %collective-permute-start.14 = (bf16[64,3584]{1,0:T(8,128)(2,1)}, bf16[64,3584]{1,0:T(8,128)(2,1)S(1)}, u32[]{:S(2)}, u32[]{:S(2)}) collective-permute-start(bf16[64,3584]{1,0:T(8,128)(2,1)} %copy-done.12), channel_id=1, source_target_pairs={{0,1},{1,0},{2,3},{3,2},{4,5},{5,4},{6,7},{7,6},{8,9},{9,8},{10,11... | collective-permute-start | bytes 1376264 | tf_op jit(solution)/shard_map/ppermute | solution.py:18
  70.8 6.3 %collective-permute-start.15 = (bf16[64,3584]{1,0:T(8,128)(2,1)}, bf16[64,3584]{1,0:T(8,128)(2,1)S(1)}, u32[]{:S(2)}, u32[]{:S(2)}) collective-permute-start(bf16[64,3584]{1,0:T(8,128)(2,1)} %copy-done.11), channel_id=1, source_target_pairs={{0,1},{1,0},{2,3},{3,2},{4,5},{5,4},{6,7},{7,6},{8,9},{9,8},{10,11... | collective-permute-start | bytes 1376264 | tf_op jit(solution)/shard_map/ppermute | solution.py:18
  70.8 6.3 %collective-permute-start.16 = (bf16[64,3584]{1,0:T(8,128)(2,1)S(1)}, bf16[64,3584]{1,0:T(8,128)(2,1)S(1)}, u32[]{:S(2)}, u32[]{:S(2)}) collective-permute-start(bf16[64,3584]{1,0:T(8,128)(2,1)S(1)} %get-tuple-element.79), channel_id=1, source_target_pairs={{0,1},{1,0},{2,3},{3,2},{4,5},{5,4},{6,7},{7,6},{8,9},{9,8},{10,11... | collective-permute-start | bytes 1376264 | tf_op jit(solution)/shard_map/ppermute | solution.py:18
  73.6 1.2 copy-start.8
  76.5 30.0 %collective-permute-start.21 = (bf16[128,3584]{1,0:T(8,128)(2,1)}, bf16[128,3584]{1,0:T(8,128)(2,1)S(1)}, u32[]{:S(2)}, u32[]{:S(2)}) collective-permute-start(bf16[128,3584]{1,0:T(8,128)(2,1)} %pair.4), channel_id=1, source_target_pairs={{0,2},{1,3},{2,0},{3,1},{4,6},{5,7},{6,4},{7,5},{8,10},{9,11},{10,... | collective-permute-start | bytes 2752520 | tf_op jit(solution)/shard_map/ppermute | solution.py:18
  77.1 1.2 copy-start.6
  78.8 0.9 copy-start.2
  79.8 13.8 %collective-permute-start.18 = (bf16[256,512]{1,0:T(8,128)(2,1)S(1)}, bf16[256,512]{1,0:T(8,128)(2,1)S(1)}, u32[]{:S(2)}, u32[]{:S(2)}) collective-permute-start(bf16[256,512]{1,0:T(8,128)(2,1)S(1)} %collective-permute-done.7.refs_0_), channel_id=1, source_target_pairs={{0,8},{4,12},{8,0},{12,4},{1,9},{5,13},{9,1},{13,5},{2,10},{6,14},... | collective-permute-start | bytes 786440 | tf_op jit(solution)/shard_map/ppermute | solution.py:28
  79.8 14.0 %collective-permute-start.17 = (bf16[256,512]{1,0:T(8,128)(2,1)S(1)}, bf16[256,512]{1,0:T(8,128)(2,1)S(1)}, u32[]{:S(2)}, u32[]{:S(2)}) collective-permute-start(bf16[256,512]{1,0:T(8,128)(2,1)S(1)} %collective-permute-done.7.refs_0_), channel_id=1, source_target_pairs={{0,4},{4,0},{8,12},{12,8},{1,5},{5,1},{9,13},{13,9},{2,6},{6,2},{1... | collective-permute-start | bytes 786440 | tf_op jit(solution)/shard_map/ppermute | solution.py:28
  82.1 15.0 %copy-start.15 = (bf16[1,1,512,256]{3,2,1,0:T(8,128)(2,1)S(1)}, bf16[1,1,512,256]{3,2,1,0:T(8,128)(2,1)}, u32[]{:S(2)}) copy-start(bf16[1,1,512,256]{3,2,1,0:T(8,128)(2,1)} %get-tuple-element.128) | copy-start | bytes 786436
  89.6 1.0 copy-start.3
  93.7 2.4 %collective-permute-start.20 = (bf16[64,3584]{1,0:T(8,128)(2,1)S(1)}, bf16[64,3584]{1,0:T(8,128)(2,1)S(1)}, u32[]{:S(2)}, u32[]{:S(2)}) collective-permute-start(bf16[64,3584]{1,0:T(8,128)(2,1)S(1)} %get-tuple-element.86), channel_id=1, source_target_pairs={{0,1},{1,0},{2,3},{3,2},{4,5},{5,4},{6,7},{7,6},{8,9},{9,8},{10,11... | collective-permute-start | bytes 1376264 | tf_op jit(solution)/shard_map/ppermute | solution.py:18
  93.7 3.5 %collective-permute-start.19 = (bf16[64,3584]{1,0:T(8,128)(2,1)}, bf16[64,3584]{1,0:T(8,128)(2,1)}, u32[]{:S(2)}, u32[]{:S(2)}) collective-permute-start(bf16[64,3584]{1,0:T(8,128)(2,1)} %get-tuple-element.84), channel_id=1, source_target_pairs={{0,1},{1,0},{2,3},{3,2},{4,5},{5,4},{6,7},{7,6},{8,9},{9,8},{10,11... | collective-permute-start | bytes 1376264 | tf_op jit(solution)/shard_map/ppermute | solution.py:18
  94.3 8.5 %collective-permute-start.24 = (bf16[4,4224]{1,0:T(4,128)(2,1)S(1)}, bf16[4,4224]{1,0:T(4,128)(2,1)S(1)}, u32[]{:S(2)}, u32[]{:S(2)}) collective-permute-start(bf16[4,4224]{1,0:T(4,128)(2,1)S(1)} %pad_maximum_fusion.4), channel_id=1, source_target_pairs={{0,3},{1,2},{2,1},{3,0},{4,7},{5,6},{6,5},{7,4},{8,11},{9,10},{10,... | collective-permute-start | bytes 101384 | tf_op jit(solution)/shard_map/ppermute | solution.py:18
  95.2 7.9 %collective-permute-start.23 = (bf16[4,4224]{1,0:T(4,128)(2,1)S(1)}, bf16[4,4224]{1,0:T(4,128)(2,1)S(1)}, u32[]{:S(2)}, u32[]{:S(2)}) collective-permute-start(bf16[4,4224]{1,0:T(4,128)(2,1)S(1)} %pad_maximum_fusion.4), channel_id=1, source_target_pairs={{0,2},{1,3},{2,0},{3,1},{4,6},{5,7},{6,4},{7,5},{8,10},{9,11},{10,... | collective-permute-start | bytes 101384 | tf_op jit(solution)/shard_map/ppermute | solution.py:18
  96.2 0.8 copy-start.9
  96.9 8.9 %collective-permute-start.22 = (bf16[4,4224]{1,0:T(4,128)(2,1)S(1)}, bf16[4,4224]{1,0:T(4,128)(2,1)S(1)}, u32[]{:S(2)}, u32[]{:S(2)}) collective-permute-start(bf16[4,4224]{1,0:T(4,128)(2,1)S(1)} %pad_maximum_fusion.4), channel_id=1, source_target_pairs={{0,1},{1,0},{2,3},{3,2},{4,5},{5,4},{6,7},{7,6},{8,9},{9,8},{10,11... | collective-permute-start | bytes 101384 | tf_op jit(solution)/shard_map/ppermute | solution.py:18
  97.2 31.3 %collective-permute-start.31 = (bf16[128,3584]{1,0:T(8,128)(2,1)}, bf16[128,3584]{1,0:T(8,128)(2,1)S(1)}, u32[]{:S(2)}, u32[]{:S(2)}) collective-permute-start(bf16[128,3584]{1,0:T(8,128)(2,1)} %copy-done.2), channel_id=1, source_target_pairs={{0,2},{1,3},{2,0},{3,1},{4,6},{5,7},{6,4},{7,5},{8,10},{9,11},{10,... | collective-permute-start | bytes 2752520 | tf_op jit(solution)/shard_map/ppermute | solution.py:18
  98.5 1.2 copy-start.4
  99.7 1.0 copy-start.10
  102.8 14.8 %collective-permute-start.26 = (bf16[256,512]{1,0:T(8,128)(2,1)S(1)}, bf16[256,512]{1,0:T(8,128)(2,1)S(1)}, u32[]{:S(2)}, u32[]{:S(2)}) collective-permute-start(bf16[256,512]{1,0:T(8,128)(2,1)S(1)} %bitcast.38), channel_id=1, source_target_pairs={{0,8},{4,12},{8,0},{12,4},{1,9},{5,13},{9,1},{13,5},{2,10},{6,14},... | collective-permute-start | bytes 786440 | tf_op jit(solution)/shard_map/ppermute | solution.py:28
  103.1 17.8 %collective-permute-start.25 = (bf16[256,512]{1,0:T(8,128)(2,1)S(1)}, bf16[256,512]{1,0:T(8,128)(2,1)S(1)}, u32[]{:S(2)}, u32[]{:S(2)}) collective-permute-start(bf16[256,512]{1,0:T(8,128)(2,1)S(1)} %bitcast.39), channel_id=1, source_target_pairs={{0,4},{4,0},{8,12},{12,8},{1,5},{5,1},{9,13},{13,9},{2,6},{6,2},{1... | collective-permute-start | bytes 786440 | tf_op jit(solution)/shard_map/ppermute | solution.py:28
  105.8 15.1 %collective-permute-start.27 = (bf16[256,512]{1,0:T(8,128)(2,1)S(1)}, bf16[256,512]{1,0:T(8,128)(2,1)S(1)}, u32[]{:S(2)}, u32[]{:S(2)}) collective-permute-start(bf16[256,512]{1,0:T(8,128)(2,1)S(1)} %collective-permute-done.7.refs_0_), channel_id=1, source_target_pairs={{4,8},{8,4},{5,9},{9,5},{6,10},{10,6},{7,11},{11,7},{20,24},{24,20... | collective-permute-start | bytes 786440 | tf_op jit(solution)/shard_map/ppermute | solution.py:28
  106.5 16.8 %collective-permute-start.28 = (bf16[256,512]{1,0:T(8,128)(2,1)S(1)}, bf16[256,512]{1,0:T(8,128)(2,1)S(1)}, u32[]{:S(2)}, u32[]{:S(2)}) collective-permute-start(bf16[256,512]{1,0:T(8,128)(2,1)S(1)} %collective-permute-done.18.refs_2_), channel_id=1, source_target_pairs={{4,0},{8,12},{5,1},{9,13},{6,2},{10,14},{7,3},{11,15},{20,16},{24,... | collective-permute-start | bytes 786440 | tf_op jit(solution)/shard_map/ppermute | solution.py:28
  117.6 22.3 %collective-permute-start.35 = (bf16[128,3584]{1,0:T(8,128)(2,1)S(1)}, bf16[128,3584]{1,0:T(8,128)(2,1)S(1)}, u32[]{:S(2)}, u32[]{:S(2)}) collective-permute-start(bf16[128,3584]{1,0:T(8,128)(2,1)S(1)} %pair.6), channel_id=1, source_target_pairs={{0,2},{1,3},{2,0},{3,1},{4,6},{5,7},{6,4},{7,5},{8,10},{9,11},{10,... | collective-permute-start | bytes 2752520 | tf_op jit(solution)/shard_map/ppermute | solution.py:18
  123.3 1.8 %collective-permute-start.29 = (bf16[64,3584]{1,0:T(8,128)(2,1)S(1)}, bf16[64,3584]{1,0:T(8,128)(2,1)S(1)}, u32[]{:S(2)}, u32[]{:S(2)}) collective-permute-start(bf16[64,3584]{1,0:T(8,128)(2,1)S(1)} %get-tuple-element.98), channel_id=1, source_target_pairs={{0,1},{1,0},{2,3},{3,2},{4,5},{5,4},{6,7},{7,6},{8,9},{9,8},{10,11... | collective-permute-start | bytes 1376264 | tf_op jit(solution)/shard_map/ppermute | solution.py:18
  123.3 2.5 %collective-permute-start.30 = (bf16[64,3584]{1,0:T(8,128)(2,1)S(1)}, bf16[64,3584]{1,0:T(8,128)(2,1)S(1)}, u32[]{:S(2)}, u32[]{:S(2)}) collective-permute-start(bf16[64,3584]{1,0:T(8,128)(2,1)S(1)} %get-tuple-element.100), channel_id=1, source_target_pairs={{0,1},{1,0},{2,3},{3,2},{4,5},{5,4},{6,7},{7,6},{8,9},{9,8},{10,11... | collective-permute-start | bytes 1376264 | tf_op jit(solution)/shard_map/ppermute | solution.py:18
  126.3 9.1 %collective-permute-start.32 = (bf16[256,512]{1,0:T(8,128)(2,1)S(1)}, bf16[256,512]{1,0:T(8,128)(2,1)S(1)}, u32[]{:S(2)}, u32[]{:S(2)}) collective-permute-start(bf16[256,512]{1,0:T(8,128)(2,1)S(1)} %bitcast.40), channel_id=1, source_target_pairs={{4,8},{8,4},{5,9},{9,5},{6,10},{10,6},{7,11},{11,7},{20,24},{24,20... | collective-permute-start | bytes 786440 | tf_op jit(solution)/shard_map/ppermute | solution.py:28
  127.0 10.2 %collective-permute-start.33 = (bf16[256,512]{1,0:T(8,128)(2,1)S(1)}, bf16[256,512]{1,0:T(8,128)(2,1)S(1)}, u32[]{:S(2)}, u32[]{:S(2)}) collective-permute-start(bf16[256,512]{1,0:T(8,128)(2,1)S(1)} %collective-permute-done.26.refs_2_), channel_id=1, source_target_pairs={{4,0},{8,12},{5,1},{9,13},{6,2},{10,14},{7,3},{11,15},{20,16},{24,... | collective-permute-start | bytes 786440 | tf_op jit(solution)/shard_map/ppermute | solution.py:28
  137.3 2.6 %collective-permute-start.34 = (bf16[64,3584]{1,0:T(8,128)(2,1)S(1)}, bf16[64,3584]{1,0:T(8,128)(2,1)S(1)}, u32[]{:S(2)}, u32[]{:S(2)}) collective-permute-start(bf16[64,3584]{1,0:T(8,128)(2,1)S(1)} %get-tuple-element.106), channel_id=1, source_target_pairs={{0,1},{1,0},{2,3},{3,2},{4,5},{5,4},{6,7},{7,6},{8,9},{9,8},{10,11... | collective-permute-start | bytes 1376264 | tf_op jit(solution)/shard_map/ppermute | solution.py:18
  137.3 12.9 %collective-permute-start.36 = (bf16[64,3584]{1,0:T(8,128)(2,1)S(1)}, bf16[64,3584]{1,0:T(8,128)(2,1)S(1)}, u32[]{:S(2)}, u32[]{:S(2)}) collective-permute-start(bf16[64,3584]{1,0:T(8,128)(2,1)S(1)} %get-tuple-element.101), channel_id=1, source_target_pairs={{0,2},{1,3},{2,0},{3,1},{4,6},{5,7},{6,4},{7,5},{8,10},{9,11},{10,... | collective-permute-start | bytes 1376264 | tf_op jit(solution)/shard_map/ppermute | solution.py:18
  137.9 12.8 %collective-permute-start.43 = (bf16[64,3584]{1,0:T(8,128)(2,1)S(1)}, bf16[64,3584]{1,0:T(8,128)(2,1)S(1)}, u32[]{:S(2)}, u32[]{:S(2)}) collective-permute-start(bf16[64,3584]{1,0:T(8,128)(2,1)S(1)} %get-tuple-element.122), channel_id=1, source_target_pairs={{0,1},{1,0},{2,3},{3,2},{4,5},{5,4},{6,7},{7,6},{8,9},{9,8},{10,11... | collective-permute-start | bytes 1376264 | tf_op jit(solution)/shard_map/ppermute | solution.py:18
  138.1 12.6 %collective-permute-start.42 = (bf16[64,3584]{1,0:T(8,128)(2,1)S(1)}, bf16[64,3584]{1,0:T(8,128)(2,1)S(1)}, u32[]{:S(2)}, u32[]{:S(2)}) collective-permute-start(bf16[64,3584]{1,0:T(8,128)(2,1)S(1)} %get-tuple-element.120), channel_id=1, source_target_pairs={{0,1},{1,0},{2,3},{3,2},{4,5},{5,4},{6,7},{7,6},{8,9},{9,8},{10,11... | collective-permute-start | bytes 1376264 | tf_op jit(solution)/shard_map/ppermute | solution.py:18
  139.9 11.3 %collective-permute-start.41 = (bf16[64,3584]{1,0:T(8,128)(2,1)S(1)}, bf16[64,3584]{1,0:T(8,128)(2,1)S(1)}, u32[]{:S(2)}, u32[]{:S(2)}) collective-permute-start(bf16[64,3584]{1,0:T(8,128)(2,1)S(1)} %get-tuple-element.118), channel_id=1, source_target_pairs={{0,1},{1,0},{2,3},{3,2},{4,5},{5,4},{6,7},{7,6},{8,9},{9,8},{10,11... | collective-permute-start | bytes 1376264 | tf_op jit(solution)/shard_map/ppermute | solution.py:18
  150.2 2.5 %collective-permute-start.40 = (bf16[64,3584]{1,0:T(8,128)(2,1)S(1)}, bf16[64,3584]{1,0:T(8,128)(2,1)S(1)}, u32[]{:S(2)}, u32[]{:S(2)}) collective-permute-start(bf16[64,3584]{1,0:T(8,128)(2,1)S(1)} %get-tuple-element.115), channel_id=1, source_target_pairs={{0,1},{1,0},{2,3},{3,2},{4,5},{5,4},{6,7},{7,6},{8,9},{9,8},{10,11... | collective-permute-start | bytes 1376264 | tf_op jit(solution)/shard_map/ppermute | solution.py:18
  150.2 2.5 %collective-permute-start.39 = (bf16[64,3584]{1,0:T(8,128)(2,1)S(1)}, bf16[64,3584]{1,0:T(8,128)(2,1)S(1)}, u32[]{:S(2)}, u32[]{:S(2)}) collective-permute-start(bf16[64,3584]{1,0:T(8,128)(2,1)S(1)} %get-tuple-element.113), channel_id=1, source_target_pairs={{0,1},{1,0},{2,3},{3,2},{4,5},{5,4},{6,7},{7,6},{8,9},{9,8},{10,11... | collective-permute-start | bytes 1376264 | tf_op jit(solution)/shard_map/ppermute | solution.py:18
  150.7 2.6 %collective-permute-start.38 = (bf16[64,3584]{1,0:T(8,128)(2,1)S(1)}, bf16[64,3584]{1,0:T(8,128)(2,1)S(1)}, u32[]{:S(2)}, u32[]{:S(2)}) collective-permute-start(bf16[64,3584]{1,0:T(8,128)(2,1)S(1)} %get-tuple-element.111), channel_id=1, source_target_pairs={{0,1},{1,0},{2,3},{3,2},{4,5},{5,4},{6,7},{7,6},{8,9},{9,8},{10,11... | collective-permute-start | bytes 1376264 | tf_op jit(solution)/shard_map/ppermute | solution.py:18
  150.7 3.3 %collective-permute-start.37 = (bf16[64,3584]{1,0:T(8,128)(2,1)S(1)}, bf16[64,3584]{1,0:T(8,128)(2,1)S(1)}, u32[]{:S(2)}, u32[]{:S(2)}) collective-permute-start(bf16[64,3584]{1,0:T(8,128)(2,1)S(1)} %get-tuple-element.109), channel_id=1, source_target_pairs={{0,1},{1,0},{2,3},{3,2},{4,5},{5,4},{6,7},{7,6},{8,9},{9,8},{10,11... | collective-permute-start | bytes 1376264 | tf_op jit(solution)/shard_map/ppermute | solution.py:18
  151.2 12.5 %collective-permute-start.44 = (bf16[64,3584]{1,0:T(8,128)(2,1)S(1)}, bf16[64,3584]{1,0:T(8,128)(2,1)S(1)}, u32[]{:S(2)}, u32[]{:S(2)}) collective-permute-start(bf16[64,3584]{1,0:T(8,128)(2,1)S(1)} %get-tuple-element.124), channel_id=1, source_target_pairs={{0,2},{1,3},{2,0},{3,1},{4,6},{5,7},{6,4},{7,5},{8,10},{9,11},{10,... | collective-permute-start | bytes 1376264 | tf_op jit(solution)/shard_map/ppermute | solution.py:18
  163.7 8.0 %copy-start.1 = (bf16[7168,64]{0,1:T(8,128)(2,1)S(1)}, bf16[7168,64]{0,1:T(8,128)(2,1)}, u32[]{:S(2)}) copy-start(bf16[7168,64]{0,1:T(8,128)(2,1)} %param.10) | copy-start | bytes 2752516

commit v18 on v17

--- a/solution.py
+++ b/solution.py
@@ -63,7 +63,12 @@
     def fetch(step):
         slot = lax.rem(step, slots)
         at = pl.ds(pl.multiple_of(first + step * tile, tile), tile)
-        return pltpu.make_async_copy(w_ref.at[:, 0, :, at], held.at[slot], held_sems.at[slot])
+        return [
+            pltpu.make_async_copy(
+                w_ref.at[source, 0, :, at], held.at[slot, source], held_sems.at[slot, source]
+            )
+            for source in range(size)
+        ]
 
     @pl.when(j == 0)
     def _():
@@ -73,7 +78,8 @@
         for copy in copies:
             copy.start()
         for step in range(slots):
-            fetch(step).start()
+            for copy in fetch(step):
+                copy.start()
         inside = jnp.logical_or(place == 1, place == 2)
         relayed = ((inside, 3), (jnp.logical_not(inside), 4)) if count == 5 else ()
         for chosen, k in relayed:
@@ -87,7 +93,8 @@
         for copy in copies:
             copy.wait()
 
-    fetch(j).wait()
+    for copy in fetch(j):
+        copy.wait()
     weight = held[lax.rem(j, slots)].reshape(size * width, tile)
     terms = jnp.dot(feats[...], weight, preferred_element_type=f32)
     if add_refs:
@@ -106,14 +113,15 @@
 
     @pl.when(j + slots < steps)
     def _():
-        fetch(j + slots).start()
+        for copy in fetch(j + slots):
+            copy.start()
 
 
 def block_terms(blocks, down_weight, part, parts, outs, adds=None, into=None):
     size, _, width, every = down_weight.shape
     rows, cols = sum(outs), every // parts
     tile = max(n for n in range(128, 513, 128) if cols % n == 0)
-    slots = min(4, cols // tile)
+    slots = min(5, cols // tile)
 
     def spec(tall, first=0):
         return pl.BlockSpec((tall, tile), lambda j, place: (0, first + j))
@@ -150,7 +158,7 @@
                 pltpu.VMEM((rows, size * width), bf16),
                 pltpu.VMEM((slots, size, width, tile), bf16),
                 pltpu.SemaphoreType.DMA((size,)),
-                pltpu.SemaphoreType.DMA((slots,)),
+                pltpu.SemaphoreType.DMA((slots, size)),
             ],
         ),
         input_output_aliases=aliases,

time: 172 us -> 172 us (level)
  no operation moved by 1% of the time
where the time goes in v18:
time: 172 us
  Pallas kernels  65.4 us (38%)
  waiting for transfers between devices  50 us (29%)
  starting transfers between devices  33.6 us (20%)
  local copies, waits for them, and re-layouts  13.5 us (8%)
  matrix products  7.54 us (4%)
    pallas_call x8, Pallas kernels, block_terms(): pl.pallas_call(functools.partial(terms_kernel, size, len(blocks), part *...  59.1 us
    ppermute x16, waiting for transfers between devices, across(): return lax.ppermute(value, 'tensor', pairs)  38.3 us
    ppermute x16, starting transfers between devices, across(): return lax.ppermute(value, 'tensor', pairs)  20.2 us
    ppermute x29, starting transfers between devices, swap(): return lax.ppermute(value, 'dp', [(d, d ^ step) for d in range(size)])  13.4 us
    ppermute x29, waiting for transfers between devices, swap(): return lax.ppermute(value, 'dp', [(d, d ^ step) for d in range(size)])  11.8 us
    unnamed x38, local copies, waits for them, and re-layouts  10.7 us
    pallas_call x4, Pallas kernels, add_pieces(): pl.pallas_call(functools.partial(add_kernel, len(pieces)), out_shape=[jax...  4.91 us
  transfers between devices with their start and end apart: 45, of which 18 were waited for; matrix products, arithmetic and copies ran while one was open for 5% of the time, Pallas kernels for 33%

profile of v18, /device:TPU:0, one launch (start us, length us, event | category | flops | bytes accessed | tf_op | source)
XLA Modules:
  0.0 172.0 jit_solution(10216223275766900953)
XLA Ops:
  0.7 2.0 %constant_dynamic-slice_fusion = (bf16[1,1,512,256]{3,2,1,0:T(8,128)(2,1)S(1)}, bf16[1,1,512,256]{3,2,1,0:T(8,128)(2,1)S(1)}, bf16[1,1,512,256]{3,2,1,0:T(8,128)(2,1)S(1)}, bf16[1,1,512,256]{3,2,1,0:T(8,128)(2,1)}) fusion(bf16[1,4,512,256]{3,2,1,0:T(8,128)(2,1)} %param.8, s32[]{:T(128)S(6)} %select_n.96, s32[]{:T(128)S(6)} %select_n.95, s32[]{:T(128)S(6)} %select_n.94, ...), kind=kLoop, calls=%fused_computation.32 | loop fusion | bytes 2097168 | tf_op jit(solution)/shard_map/dynamic-slice.7
  2.9 3.0 %collective-permute-start.3 = (bf16[128,512]{1,0:T(8,128)(2,1)S(1)}, bf16[128,512]{1,0:T(8,128)(2,1)S(1)}, u32[]{:S(2)}, u32[]{:S(2)}) collective-permute-start(bf16[128,512]{1,0:T(8,128)(2,1)S(1)} %get-tuple-element.131), channel_id=1, source_target_pairs={{0,2},{1,3},{2,0},{3,1},{4,6},{5,7},{6,4},{7,5},{8,10},{9,11},{10,... | collective-permute-start | bytes 393224 | tf_op jit(solution)/shard_map/ppermute | solution.py:18
  6.2 3.3 %fusion.15 = f32[256,64]{0,1:T(8,128)S(1)} fusion(bf16[256,7168]{1,0:T(8,128)(2,1)} %param.7, bf16[7168,64]{0,1:T(8,128)(2,1)S(1)} %copy-done), kind=kOutput, calls=%fused_computation.38 | convolution fusion | flops 234881024 | bytes 4653056 | tf_op jit(solution)/shard_map/dot_general | solution.py:286
  9.8 1.6 collective-permute-start.11
  11.4 1.2 collective-permute-start.1
  12.6 3.0 %collective-permute-start.6 = (bf16[256,512]{1,0:T(8,128)(2,1)S(1)}, bf16[256,512]{1,0:T(8,128)(2,1)S(1)}, u32[]{:S(2)}, u32[]{:S(2)}) collective-permute-start(bf16[256,512]{1,0:T(8,128)(2,1)S(1)} %pad_maximum_fusion.1.refs_0_), channel_id=1, source_target_pairs={{0,12},{4,8},{8,4},{12,0},{1,13},{5,9},{9,5},{13,1},{2,14},{6,10},... | collective-permute-start | bytes 786440 | tf_op jit(solution)/shard_map/ppermute | solution.py:28
  15.7 1.4 collective-permute-start.4
  17.5 6.5 %collective-permute-done.6.refs_3_ = bf16[256,512]{1,0:T(8,128)(2,1)S(1)} collective-permute-done((bf16[256,512]{1,0:T(8,128)(2,1)S(1)}, bf16[256,512]{1,0:T(8,128)(2,1)S(1)}, u32[]{:S(2)}, u32[]{:S(2)}) %collective-permute-start.6) | collective-permute-done | bytes 262176 | tf_op jit(solution)/shard_map/ppermute | solution.py:28
  24.0 15.0 %collective-permute-done.5.refs_2_ = bf16[256,512]{1,0:T(8,128)(2,1)S(1)} collective-permute-done((bf16[256,512]{1,0:T(8,128)(2,1)S(1)}, bf16[256,512]{1,0:T(8,128)(2,1)S(1)}, u32[]{:S(2)}, u32[]{:S(2)}) %collective-permute-start.5) | collective-permute-done | bytes 262176 | tf_op jit(solution)/shard_map/ppermute | solution.py:28
  39.1 2.7 %collective-permute-start.10 = (bf16[256,512]{1,0:T(8,128)(2,1)S(1)}, bf16[256,512]{1,0:T(8,128)(2,1)S(1)}, u32[]{:S(2)}, u32[]{:S(2)}) collective-permute-start(bf16[256,512]{1,0:T(8,128)(2,1)S(1)} %pad_maximum_fusion.refs_0_), channel_id=1, source_target_pairs={{0,12},{4,8},{8,4},{12,0},{1,13},{5,9},{9,5},{13,1},{2,14},{6,10},... | collective-permute-start | bytes 786440 | tf_op jit(solution)/shard_map/ppermute | solution.py:28
  41.8 2.0 %collective-permute-start.9 = (bf16[256,512]{1,0:T(8,128)(2,1)S(1)}, bf16[256,512]{1,0:T(8,128)(2,1)S(1)}, u32[]{:S(2)}, u32[]{:S(2)}) collective-permute-start(bf16[256,512]{1,0:T(8,128)(2,1)S(1)} %pad_maximum_fusion.refs_0_), channel_id=1, source_target_pairs={{0,8},{4,12},{8,0},{12,4},{1,9},{5,13},{9,1},{13,5},{2,10},{6,14},... | collective-permute-start | bytes 786440 | tf_op jit(solution)/shard_map/ppermute | solution.py:28
  43.8 7.1 %terms.8 = (bf16[64,3584]{1,0:T(8,128)(2,1)S(1)}, bf16[64,3584]{1,0:T(8,128)(2,1)S(1)}, bf16[128,3584]{1,0:T(8,128)(2,1)S(1)}) custom-call(s32[1]{0:T(128)} %bitcast.place_ref, bf16[256,512]{1,0:T(8,128)(2,1)S(1)} %pad_maximum_fusion.1.refs_0_, bf16[256,512]{1,0:T(8,128)(2,1)S(1)} %collective-permute-done.4.refs_1_, ...), custom_call_target="tpu_custom_call" | custom-call | flops 469762048 | bytes 1000 | tf_op jit(solution)/shard_map/terms/pallas_call | solution.py:143
  50.9 0.9 copy-done.7
  51.8 0.8 copy-done.13
  52.6 7.2 %terms.9 = (bf16[64,3584]{1,0:T(8,128)(2,1)S(1)}, bf16[64,3584]{1,0:T(8,128)(2,1)S(1)}, bf16[128,3584]{1,0:T(8,128)(2,1)S(1)}) custom-call(s32[1]{0:T(128)} %bitcast.place_ref, bf16[256,512]{1,0:T(8,128)(2,1)S(1)} %pad_maximum_fusion.1.refs_0_, bf16[256,512]{1,0:T(8,128)(2,1)S(1)} %collective-permute-done.4.refs_1_, ...), custom_call_target="tpu_custom_call" | custom-call | flops 469762048 | bytes 1000 | tf_op jit(solution)/shard_map/terms/pallas_call | solution.py:143
  59.8 0.9 copy-done.5
  60.7 0.8 copy-done.11
  62.1 8.2 %collective-permute-done.9.refs_2_ = bf16[256,512]{1,0:T(8,128)(2,1)S(1)} collective-permute-done((bf16[256,512]{1,0:T(8,128)(2,1)S(1)}, bf16[256,512]{1,0:T(8,128)(2,1)S(1)}, u32[]{:S(2)}, u32[]{:S(2)}) %collective-permute-start.9) | collective-permute-done | bytes 262176 | tf_op jit(solution)/shard_map/ppermute | solution.py:28
  71.3 1.0 collective-permute-done.13.refs_0_
  72.3 1.3 collective-permute-done.14.refs_1_
  73.6 1.2 copy-done.8
  74.8 1.7 pair.4
  76.5 0.6 collective-permute-start.21
  77.1 1.2 copy-done.6
  78.8 0.9 copy-done.2
  79.8 2.3 %collective-permute-start.17 = (bf16[256,512]{1,0:T(8,128)(2,1)S(1)}, bf16[256,512]{1,0:T(8,128)(2,1)S(1)}, u32[]{:S(2)}, u32[]{:S(2)}) collective-permute-start(bf16[256,512]{1,0:T(8,128)(2,1)S(1)} %collective-permute-done.7.refs_0_), channel_id=1, source_target_pairs={{0,4},{4,0},{8,12},{12,8},{1,5},{5,1},{9,13},{13,9},{2,6},{6,2},{1... | collective-permute-start | bytes 786440 | tf_op jit(solution)/shard_map/ppermute | solution.py:28
  82.1 7.7 %terms.10 = (bf16[64,3584]{1,0:T(8,128)(2,1)}, bf16[64,3584]{1,0:T(8,128)(2,1)S(1)}, bf16[128,3584]{1,0:T(8,128)(2,1)S(1)}) custom-call(s32[1]{0:T(128)} %bitcast.place_ref, bf16[256,512]{1,0:T(8,128)(2,1)S(1)} %pad_maximum_fusion.refs_0_, bf16[256,512]{1,0:T(8,128)(2,1)S(1)} %collective-permute-done.8.refs_1_, ...), custom_call_target="tpu_custom_call" | custom-call | flops 469762048 | bytes 1000 | tf_op jit(solution)/shard_map/terms/pallas_call | solution.py:143
  89.8 1.0 copy-done.3
  90.7 2.8 %collective-permute-done.18.refs_2_ = bf16[256,512]{1,0:T(8,128)(2,1)S(1)} collective-permute-done((bf16[256,512]{1,0:T(8,128)(2,1)S(1)}, bf16[256,512]{1,0:T(8,128)(2,1)S(1)}, u32[]{:S(2)}, u32[]{:S(2)}) %collective-permute-start.18) | collective-permute-done | bytes 262176 | tf_op jit(solution)/shard_map/ppermute | solution.py:28
  94.3 0.8 collective-permute-start.24
  95.2 0.9 collective-permute-start.23
  96.2 0.8 copy-done.9
  97.2 1.2 collective-permute-start.31
  98.5 1.2 copy-done.4
  99.7 1.0 copy-done.10
  100.7 2.1 %pair.6 = bf16[128,3584]{1,0:T(8,128)(2,1)S(1)} custom-call(bf16[128,3584]{1,0:T(8,128)(2,1)S(1)} %copy-done.4, bf16[64,3584]{1,0:T(8,128)(2,1)} %collective-permute-done.19.refs_0_, bf16[64,3584]{1,0:T(8,128)(2,1)S(1)} %copy-done.10), custom_call_target="tpu_custom_call" | custom-call | flops 1000 | bytes 1000 | tf_op jit(solution)/shard_map/pair/pallas_call | solution.py:189
  103.1 2.7 %collective-permute-start.25 = (bf16[256,512]{1,0:T(8,128)(2,1)S(1)}, bf16[256,512]{1,0:T(8,128)(2,1)S(1)}, u32[]{:S(2)}, u32[]{:S(2)}) collective-permute-start(bf16[256,512]{1,0:T(8,128)(2,1)S(1)} %bitcast.39), channel_id=1, source_target_pairs={{0,4},{4,0},{8,12},{12,8},{1,5},{5,1},{9,13},{13,9},{2,6},{6,2},{1... | collective-permute-start | bytes 786440 | tf_op jit(solution)/shard_map/ppermute | solution.py:28
  105.8 0.7 collective-permute-start.27
  106.5 1.3 collective-permute-start.28
  107.8 7.1 %terms.11 = (bf16[64,3584]{1,0:T(8,128)(2,1)S(1)}, bf16[64,3584]{1,0:T(8,128)(2,1)S(1)}, bf16[128,3584]{1,0:T(8,128)(2,1)S(1)}) custom-call(s32[1]{0:T(128)} %bitcast.place_ref, bf16[256,512]{1,0:T(8,128)(2,1)S(1)} %pad_maximum_fusion.refs_0_, bf16[256,512]{1,0:T(8,128)(2,1)S(1)} %collective-permute-done.8.refs_1_, ...), custom_call_target="tpu_custom_call" | custom-call | flops 469762048 | bytes 1000 | tf_op jit(solution)/shard_map/terms/pallas_call | solution.py:143
  115.2 0.9 fusion.6
  116.1 1.5 collective-permute-done.26.refs_2_
  117.6 0.6 collective-permute-start.35
  118.2 2.7 %fusion.4 = f32[1024,1024]{1,0:T(8,128)} fusion(bf16[16,4224]{1,0:T(8,128)(2,1)S(1)} %pad_maximum_fusion.2, s32[]{:T(128)S(6)} %select_n.121, s32[]{:T(128)S(6)} %select_n.122), kind=kOutput, calls=%fused_computation.20 | convolution fusion | flops 33554432 | bytes 4259848 | tf_op jit(solution)/shard_map/dot_general | solution.py:275
  120.9 2.4 %collective-permute-done.28.refs_4_ = bf16[256,512]{1,0:T(8,128)(2,1)S(1)} collective-permute-done((bf16[256,512]{1,0:T(8,128)(2,1)S(1)}, bf16[256,512]{1,0:T(8,128)(2,1)S(1)}, u32[]{:S(2)}, u32[]{:S(2)}) %collective-permute-start.28) | collective-permute-done | bytes 262176 | tf_op jit(solution)/shard_map/ppermute | solution.py:28
  123.8 1.3 collective-permute-done.29.refs_0_
  125.1 0.7 collective-permute-done.30.refs_1_
  125.8 0.5 pair.7
  126.3 0.7 collective-permute-start.32
  127.0 1.5 collective-permute-start.33
  128.5 7.1 %terms.12 = (bf16[64,3584]{1,0:T(8,128)(2,1)S(1)}, bf16[64,3584]{1,0:T(8,128)(2,1)S(1)}, bf16[64,3584]{1,0:T(8,128)(2,1)S(1)}, bf16[64,3584]{1,0:T(8,128)(2,1)S(1)}) custom-call(s32[1]{0:T(128)} %bitcast.place_ref, bf16[256,512]{1,0:T(8,128)(2,1)S(1)} %collective-permute-done.7.refs_0_, bf16[256,512]{1,0:T(8,128)(2,1)S(1)} %collective-permute-done.17.refs_1_, ...), custom_call_target="tpu_custom_call" | custom-call | flops 469762048 | bytes 1000 | tf_op jit(solution)/shard_map/terms/pallas_call | solution.py:143
  135.6 1.7 collective-permute-done.33.refs_4_
  137.3 0.6 collective-permute-start.36
  138.4 1.5 collective-permute-done.35.refs_5_
  139.9 7.1 %terms.13 = (bf16[64,3584]{1,0:T(8,128)(2,1)S(1)}, bf16[64,3584]{1,0:T(8,128)(2,1)S(1)}, bf16[64,3584]{1,0:T(8,128)(2,1)S(1)}, bf16[64,3584]{1,0:T(8,128)(2,1)S(1)}) custom-call(s32[1]{0:T(128)} %bitcast.place_ref, bf16[256,512]{1,0:T(8,128)(2,1)S(1)} %collective-permute-done.7.refs_0_, bf16[256,512]{1,0:T(8,128)(2,1)S(1)} %collective-permute-done.17.refs_1_, ...), custom_call_target="tpu_custom_call" | custom-call | flops 469762048 | bytes 1000 | tf_op jit(solution)/shard_map/terms/pallas_call | solution.py:143
  147.0 3.2 %collective-permute-done.36.refs_7_ = bf16[64,3584]{1,0:T(8,128)(2,1)S(1)} collective-permute-done((bf16[64,3584]{1,0:T(8,128)(2,1)S(1)}, bf16[64,3584]{1,0:T(8,128)(2,1)S(1)}, u32[]{:S(2)}, u32[]{:S(2)}) %collective-permute-start.36) | collective-permute-done | bytes 458784 | tf_op jit(solution)/shard_map/ppermute | solution.py:18
  151.2 0.6 collective-permute-start.44
  151.8 0.8 sums.3.refs_6_
  152.7 0.6 collective-permute-done.38.refs_1_
  153.3 0.7 collective-permute-done.37.refs_0_
  154.0 0.6 sums.2.refs_6_
  154.6 7.8 %terms.14.refs_9_ = bf16[256,7168]{1,0:T(8,128)(2,1)} custom-call(s32[1]{0:T(128)} %bitcast.place_ref, bf16[256,512]{1,0:T(8,128)(2,1)S(1)} %bitcast.41, bf16[256,512]{1,0:T(8,128)(2,1)S(1)} %collective-permute-done.25.refs_1_, bf16[256,512]{1,0:T(8,128)(2,1)S(1)} %collective-permute-done.26.refs_2_, bf16[256,512]{1,0:T(8,128)(2,1)S(1)} %collective-permute-done.32.refs_3_, ...), custom_call_target="tpu_custom_call" | custom-call | flops 469762048 | bytes 1000 | tf_op jit(solution)/shard_map/terms/pallas_call | solution.py:143
  162.4 1.3 collective-permute-done.44.refs_8_
  163.7 8.1 %terms.15 = bf16[256,7168]{1,0:T(8,128)(2,1)} custom-call(s32[1]{0:T(128)} %bitcast.place_ref, bf16[256,512]{1,0:T(8,128)(2,1)S(1)} %bitcast.42, bf16[256,512]{1,0:T(8,128)(2,1)S(1)} %collective-permute-done.25.refs_1_, bf16[256,512]{1,0:T(8,128)(2,1)S(1)} %collective-permute-done.26.refs_2_, ...), custom_call_target="tpu_custom_call", output_to_operand_aliasing={{}: (10, {})} | custom-call | flops 469762048 | bytes 1000 | tf_op jit(solution)/shard_map/terms/pallas_call | solution.py:143
  (107 shorter events, 7.2 us)
Async XLA Ops:
  0.6 5.5 %copy-start = (bf16[7168,64]{0,1:T(8,128)(2,1)S(1)}, bf16[7168,64]{0,1:T(8,128)(2,1)}, u32[]{:S(2)}) copy-start(bf16[7168,64]{0,1:T(8,128)(2,1)} %param.10) | copy-start | bytes 2752516
  2.7 6.7 %copy-start.14 = (bf16[1,4,512,256]{3,2,1,0:T(8,128)(2,1)S(1)}, bf16[1,4,512,256]{3,2,1,0:T(8,128)(2,1)}, u32[]{:S(2)}) copy-start(bf16[1,4,512,256]{3,2,1,0:T(8,128)(2,1)} %param.8) | copy-start | bytes 3145732
  2.7 6.7 %copy-start.16 = (bf16[1,4,512,64]{2,3,1,0:T(8,128)(2,1)S(1)}, bf16[1,4,512,64]{2,3,1,0:T(8,128)(2,1)}, u32[]{:S(2)}) copy-start(bf16[1,4,512,64]{2,3,1,0:T(8,128)(2,1)} %param.11) | copy-start | bytes 786436
  2.9 9.7 %collective-permute-start.3 = (bf16[128,512]{1,0:T(8,128)(2,1)S(1)}, bf16[128,512]{1,0:T(8,128)(2,1)S(1)}, u32[]{:S(2)}, u32[]{:S(2)}) collective-permute-start(bf16[128,512]{1,0:T(8,128)(2,1)S(1)} %get-tuple-element.131), channel_id=1, source_target_pairs={{0,2},{1,3},{2,0},{3,1},{4,6},{5,7},{6,4},{7,5},{8,10},{9,11},{10,... | collective-permute-start | bytes 393224 | tf_op jit(solution)/shard_map/ppermute | solution.py:18
  6.0 9.6 %copy-start.17 = (s32[1,256]{1,0:T(1,128)S(1)}, s32[1,256]{1,0:T(1,128)}, u32[]{:S(2)}) copy-start(s32[1,256]{1,0:T(1,128)} %param.12) | copy-start | bytes 3076
  6.1 6.5 %collective-permute-start.2 = (bf16[128,512]{1,0:T(8,128)(2,1)S(1)}, bf16[128,512]{1,0:T(8,128)(2,1)S(1)}, u32[]{:S(2)}, u32[]{:S(2)}) collective-permute-start(bf16[128,512]{1,0:T(8,128)(2,1)S(1)} %get-tuple-element.129), channel_id=1, source_target_pairs={{0,3},{1,2},{2,1},{3,0},{4,7},{5,6},{6,5},{7,4},{8,11},{9,10},{10,... | collective-permute-start | bytes 393224 | tf_op jit(solution)/shard_map/ppermute | solution.py:18
  9.8 7.6 %collective-permute-start.11 = (f32[256,128]{0,1:T(8,128)S(1)}, f32[256,128]{0,1:T(8,128)S(1)}, u32[]{:S(2)}, u32[]{:S(2)}) collective-permute-start(f32[256,128]{0,1:T(8,128)S(1)} %pad_maximum_fusion.3), channel_id=1, source_target_pairs={{0,4},{4,0},{8,12},{12,8},{1,5},{5,1},{9,13},{13,9},{2,6},{6,2},{1... | collective-permute-start | bytes 393224 | tf_op jit(solution)/shard_map/ppermute | solution.py:28
  11.4 27.6 %collective-permute-start.1 = (bf16[128,512]{1,0:T(8,128)(2,1)S(1)}, bf16[128,512]{1,0:T(8,128)(2,1)S(1)}, u32[]{:S(2)}, u32[]{:S(2)}) collective-permute-start(bf16[128,512]{1,0:T(8,128)(2,1)S(1)} %get-tuple-element.132), channel_id=1, source_target_pairs={{0,2},{1,3},{2,0},{3,1},{4,6},{5,7},{6,4},{7,5},{8,10},{9,11},{10,... | collective-permute-start | bytes 393224 | tf_op jit(solution)/shard_map/ppermute | solution.py:18
  12.6 11.4 %collective-permute-start.6 = (bf16[256,512]{1,0:T(8,128)(2,1)S(1)}, bf16[256,512]{1,0:T(8,128)(2,1)S(1)}, u32[]{:S(2)}, u32[]{:S(2)}) collective-permute-start(bf16[256,512]{1,0:T(8,128)(2,1)S(1)} %pad_maximum_fusion.1.refs_0_), channel_id=1, source_target_pairs={{0,12},{4,8},{8,4},{12,0},{1,13},{5,9},{9,5},{13,1},{2,14},{6,10},... | collective-permute-start | bytes 786440 | tf_op jit(solution)/shard_map/ppermute | solution.py:28
  15.7 23.3 %collective-permute-start.5 = (bf16[256,512]{1,0:T(8,128)(2,1)S(1)}, bf16[256,512]{1,0:T(8,128)(2,1)S(1)}, u32[]{:S(2)}, u32[]{:S(2)}) collective-permute-start(bf16[256,512]{1,0:T(8,128)(2,1)S(1)} %pad_maximum_fusion.1.refs_0_), channel_id=1, source_target_pairs={{0,8},{4,12},{8,0},{12,4},{1,9},{5,13},{9,1},{13,5},{2,10},{6,14},... | collective-permute-start | bytes 786440 | tf_op jit(solution)/shard_map/ppermute | solution.py:28
  15.7 23.3 %collective-permute-start.4 = (bf16[256,512]{1,0:T(8,128)(2,1)S(1)}, bf16[256,512]{1,0:T(8,128)(2,1)S(1)}, u32[]{:S(2)}, u32[]{:S(2)}) collective-permute-start(bf16[256,512]{1,0:T(8,128)(2,1)S(1)} %pad_maximum_fusion.1.refs_0_), channel_id=1, source_target_pairs={{0,4},{4,0},{8,12},{12,8},{1,5},{5,1},{9,13},{13,9},{2,6},{6,2},{1... | collective-permute-start | bytes 786440 | tf_op jit(solution)/shard_map/ppermute | solution.py:28
  17.4 21.7 %collective-permute-start = (bf16[128,512]{1,0:T(8,128)(2,1)S(1)}, bf16[128,512]{1,0:T(8,128)(2,1)S(1)}, u32[]{:S(2)}, u32[]{:S(2)}) collective-permute-start(bf16[128,512]{1,0:T(8,128)(2,1)S(1)} %get-tuple-element.130), channel_id=1, source_target_pairs={{0,3},{1,2},{2,1},{3,0},{4,7},{5,6},{6,5},{7,4},{8,11},{9,10},{10,... | collective-permute-start | bytes 393224 | tf_op jit(solution)/shard_map/ppermute | solution.py:18
  24.0 15.0 %collective-permute-start.7 = (bf16[256,512]{1,0:T(8,128)(2,1)S(1)}, bf16[256,512]{1,0:T(8,128)(2,1)S(1)}, u32[]{:S(2)}, u32[]{:S(2)}) collective-permute-start(bf16[256,512]{1,0:T(8,128)(2,1)S(1)} %bitcast.46), channel_id=1, source_target_pairs={{0,1},{1,0},{2,3},{3,2},{4,5},{5,4},{6,7},{7,6},{8,9},{9,8},{10,11... | collective-permute-start | bytes 786440 | tf_op jit(solution)/shard_map/ppermute | solution.py:18
  39.0 22.5 %collective-permute-start.12 = (f32[256,128]{0,1:T(8,128)S(1)}, f32[256,128]{0,1:T(8,128)S(1)}, u32[]{:S(2)}, u32[]{:S(2)}) collective-permute-start(f32[256,128]{0,1:T(8,128)S(1)} %fusion.14), channel_id=1, source_target_pairs={{0,8},{4,12},{8,0},{12,4},{1,9},{5,13},{9,1},{13,5},{2,10},{6,14},... | collective-permute-start | bytes 393224 | tf_op jit(solution)/shard_map/ppermute | solution.py:28
  39.1 23.0 %collective-permute-start.10 = (bf16[256,512]{1,0:T(8,128)(2,1)S(1)}, bf16[256,512]{1,0:T(8,128)(2,1)S(1)}, u32[]{:S(2)}, u32[]{:S(2)}) collective-permute-start(bf16[256,512]{1,0:T(8,128)(2,1)S(1)} %pad_maximum_fusion.refs_0_), channel_id=1, source_target_pairs={{0,12},{4,8},{8,4},{12,0},{1,13},{5,9},{9,5},{13,1},{2,14},{6,10},... | collective-permute-start | bytes 786440 | tf_op jit(solution)/shard_map/ppermute | solution.py:28
  41.8 28.5 %collective-permute-start.9 = (bf16[256,512]{1,0:T(8,128)(2,1)S(1)}, bf16[256,512]{1,0:T(8,128)(2,1)S(1)}, u32[]{:S(2)}, u32[]{:S(2)}) collective-permute-start(bf16[256,512]{1,0:T(8,128)(2,1)S(1)} %pad_maximum_fusion.refs_0_), channel_id=1, source_target_pairs={{0,8},{4,12},{8,0},{12,4},{1,9},{5,13},{9,1},{13,5},{2,10},{6,14},... | collective-permute-start | bytes 786440 | tf_op jit(solution)/shard_map/ppermute | solution.py:28
  43.8 26.5 %collective-permute-start.8 = (bf16[256,512]{1,0:T(8,128)(2,1)S(1)}, bf16[256,512]{1,0:T(8,128)(2,1)S(1)}, u32[]{:S(2)}, u32[]{:S(2)}) collective-permute-start(bf16[256,512]{1,0:T(8,128)(2,1)S(1)} %pad_maximum_fusion.refs_0_), channel_id=1, source_target_pairs={{0,4},{4,0},{8,12},{12,8},{1,5},{5,1},{9,13},{13,9},{2,6},{6,2},{1... | collective-permute-start | bytes 786440 | tf_op jit(solution)/shard_map/ppermute | solution.py:28
  50.9 0.9 copy-start.7
  51.8 0.8 copy-start.13
  52.6 7.2 %copy-start.12 = (bf16[64,3584]{1,0:T(8,128)(2,1)}, bf16[64,3584]{1,0:T(8,128)(2,1)S(1)}, u32[]{:S(2)}) copy-start(bf16[64,3584]{1,0:T(8,128)(2,1)S(1)} %get-tuple-element.75) | copy-start | bytes 1376260
  59.7 0.9 copy-start.5
  60.7 0.8 copy-start.11
  61.5 20.6 %copy-start.18 = (s32[4]{0:T(128)S(1)}, s32[4]{0:T(128)}, u32[]{:S(2)}) copy-start(s32[4]{0:T(128)} %param.13) | copy-start | bytes 52
  70.3 2.0 %collective-permute-start.13 = (bf16[64,3584]{1,0:T(8,128)(2,1)}, bf16[64,3584]{1,0:T(8,128)(2,1)S(1)}, u32[]{:S(2)}, u32[]{:S(2)}) collective-permute-start(bf16[64,3584]{1,0:T(8,128)(2,1)} %copy-done.13), channel_id=1, source_target_pairs={{0,1},{1,0},{2,3},{3,2},{4,5},{5,4},{6,7},{7,6},{8,9},{9,8},{10,11... | collective-permute-start | bytes 1376264 | tf_op jit(solution)/shard_map/ppermute | solution.py:18
  70.3 3.3 %collective-permute-start.14 = (bf16[64,3584]{1,0:T(8,128)(2,1)}, bf16[64,3584]{1,0:T(8,128)(2,1)S(1)}, u32[]{:S(2)}, u32[]{:S(2)}) collective-permute-start(bf16[64,3584]{1,0:T(8,128)(2,1)} %copy-done.12), channel_id=1, source_target_pairs={{0,1},{1,0},{2,3},{3,2},{4,5},{5,4},{6,7},{7,6},{8,9},{9,8},{10,11... | collective-permute-start | bytes 1376264 | tf_op jit(solution)/shard_map/ppermute | solution.py:18
  70.8 6.3 %collective-permute-start.15 = (bf16[64,3584]{1,0:T(8,128)(2,1)}, bf16[64,3584]{1,0:T(8,128)(2,1)S(1)}, u32[]{:S(2)}, u32[]{:S(2)}) collective-permute-start(bf16[64,3584]{1,0:T(8,128)(2,1)} %copy-done.11), channel_id=1, source_target_pairs={{0,1},{1,0},{2,3},{3,2},{4,5},{5,4},{6,7},{7,6},{8,9},{9,8},{10,11... | collective-permute-start | bytes 1376264 | tf_op jit(solution)/shard_map/ppermute | solution.py:18
  70.8 6.3 %collective-permute-start.16 = (bf16[64,3584]{1,0:T(8,128)(2,1)S(1)}, bf16[64,3584]{1,0:T(8,128)(2,1)S(1)}, u32[]{:S(2)}, u32[]{:S(2)}) collective-permute-start(bf16[64,3584]{1,0:T(8,128)(2,1)S(1)} %get-tuple-element.79), channel_id=1, source_target_pairs={{0,1},{1,0},{2,3},{3,2},{4,5},{5,4},{6,7},{7,6},{8,9},{9,8},{10,11... | collective-permute-start | bytes 1376264 | tf_op jit(solution)/shard_map/ppermute | solution.py:18
  73.6 1.2 copy-start.8
  76.5 30.0 %collective-permute-start.21 = (bf16[128,3584]{1,0:T(8,128)(2,1)}, bf16[128,3584]{1,0:T(8,128)(2,1)S(1)}, u32[]{:S(2)}, u32[]{:S(2)}) collective-permute-start(bf16[128,3584]{1,0:T(8,128)(2,1)} %pair.4), channel_id=1, source_target_pairs={{0,2},{1,3},{2,0},{3,1},{4,6},{5,7},{6,4},{7,5},{8,10},{9,11},{10,... | collective-permute-start | bytes 2752520 | tf_op jit(solution)/shard_map/ppermute | solution.py:18
  77.1 1.2 copy-start.6
  78.8 0.9 copy-start.2
  79.8 13.8 %collective-permute-start.18 = (bf16[256,512]{1,0:T(8,128)(2,1)S(1)}, bf16[256,512]{1,0:T(8,128)(2,1)S(1)}, u32[]{:S(2)}, u32[]{:S(2)}) collective-permute-start(bf16[256,512]{1,0:T(8,128)(2,1)S(1)} %collective-permute-done.7.refs_0_), channel_id=1, source_target_pairs={{0,8},{4,12},{8,0},{12,4},{1,9},{5,13},{9,1},{13,5},{2,10},{6,14},... | collective-permute-start | bytes 786440 | tf_op jit(solution)/shard_map/ppermute | solution.py:28
  79.8 14.0 %collective-permute-start.17 = (bf16[256,512]{1,0:T(8,128)(2,1)S(1)}, bf16[256,512]{1,0:T(8,128)(2,1)S(1)}, u32[]{:S(2)}, u32[]{:S(2)}) collective-permute-start(bf16[256,512]{1,0:T(8,128)(2,1)S(1)} %collective-permute-done.7.refs_0_), channel_id=1, source_target_pairs={{0,4},{4,0},{8,12},{12,8},{1,5},{5,1},{9,13},{13,9},{2,6},{6,2},{1... | collective-permute-start | bytes 786440 | tf_op jit(solution)/shard_map/ppermute | solution.py:28
  82.1 15.0 %copy-start.15 = (bf16[1,1,512,256]{3,2,1,0:T(8,128)(2,1)S(1)}, bf16[1,1,512,256]{3,2,1,0:T(8,128)(2,1)}, u32[]{:S(2)}) copy-start(bf16[1,1,512,256]{3,2,1,0:T(8,128)(2,1)} %get-tuple-element.128) | copy-start | bytes 786436
  89.7 1.0 copy-start.3
  93.7 2.4 %collective-permute-start.20 = (bf16[64,3584]{1,0:T(8,128)(2,1)S(1)}, bf16[64,3584]{1,0:T(8,128)(2,1)S(1)}, u32[]{:S(2)}, u32[]{:S(2)}) collective-permute-start(bf16[64,3584]{1,0:T(8,128)(2,1)S(1)} %get-tuple-element.86), channel_id=1, source_target_pairs={{0,1},{1,0},{2,3},{3,2},{4,5},{5,4},{6,7},{7,6},{8,9},{9,8},{10,11... | collective-permute-start | bytes 1376264 | tf_op jit(solution)/shard_map/ppermute | solution.py:18
  93.7 3.5 %collective-permute-start.19 = (bf16[64,3584]{1,0:T(8,128)(2,1)}, bf16[64,3584]{1,0:T(8,128)(2,1)}, u32[]{:S(2)}, u32[]{:S(2)}) collective-permute-start(bf16[64,3584]{1,0:T(8,128)(2,1)} %get-tuple-element.84), channel_id=1, source_target_pairs={{0,1},{1,0},{2,3},{3,2},{4,5},{5,4},{6,7},{7,6},{8,9},{9,8},{10,11... | collective-permute-start | bytes 1376264 | tf_op jit(solution)/shard_map/ppermute | solution.py:18
  94.3 8.5 %collective-permute-start.24 = (bf16[4,4224]{1,0:T(4,128)(2,1)S(1)}, bf16[4,4224]{1,0:T(4,128)(2,1)S(1)}, u32[]{:S(2)}, u32[]{:S(2)}) collective-permute-start(bf16[4,4224]{1,0:T(4,128)(2,1)S(1)} %pad_maximum_fusion.4), channel_id=1, source_target_pairs={{0,3},{1,2},{2,1},{3,0},{4,7},{5,6},{6,5},{7,4},{8,11},{9,10},{10,... | collective-permute-start | bytes 101384 | tf_op jit(solution)/shard_map/ppermute | solution.py:18
  95.2 7.9 %collective-permute-start.23 = (bf16[4,4224]{1,0:T(4,128)(2,1)S(1)}, bf16[4,4224]{1,0:T(4,128)(2,1)S(1)}, u32[]{:S(2)}, u32[]{:S(2)}) collective-permute-start(bf16[4,4224]{1,0:T(4,128)(2,1)S(1)} %pad_maximum_fusion.4), channel_id=1, source_target_pairs={{0,2},{1,3},{2,0},{3,1},{4,6},{5,7},{6,4},{7,5},{8,10},{9,11},{10,... | collective-permute-start | bytes 101384 | tf_op jit(solution)/shard_map/ppermute | solution.py:18
  96.2 0.8 copy-start.9
  96.9 8.9 %collective-permute-start.22 = (bf16[4,4224]{1,0:T(4,128)(2,1)S(1)}, bf16[4,4224]{1,0:T(4,128)(2,1)S(1)}, u32[]{:S(2)}, u32[]{:S(2)}) collective-permute-start(bf16[4,4224]{1,0:T(4,128)(2,1)S(1)} %pad_maximum_fusion.4), channel_id=1, source_target_pairs={{0,1},{1,0},{2,3},{3,2},{4,5},{5,4},{6,7},{7,6},{8,9},{9,8},{10,11... | collective-permute-start | bytes 101384 | tf_op jit(solution)/shard_map/ppermute | solution.py:18
  97.2 31.3 %collective-permute-start.31 = (bf16[128,3584]{1,0:T(8,128)(2,1)}, bf16[128,3584]{1,0:T(8,128)(2,1)S(1)}, u32[]{:S(2)}, u32[]{:S(2)}) collective-permute-start(bf16[128,3584]{1,0:T(8,128)(2,1)} %copy-done.2), channel_id=1, source_target_pairs={{0,2},{1,3},{2,0},{3,1},{4,6},{5,7},{6,4},{7,5},{8,10},{9,11},{10,... | collective-permute-start | bytes 2752520 | tf_op jit(solution)/shard_map/ppermute | solution.py:18
  98.5 1.2 copy-start.4
  99.7 1.0 copy-start.10
  102.8 14.8 %collective-permute-start.26 = (bf16[256,512]{1,0:T(8,128)(2,1)S(1)}, bf16[256,512]{1,0:T(8,128)(2,1)S(1)}, u32[]{:S(2)}, u32[]{:S(2)}) collective-permute-start(bf16[256,512]{1,0:T(8,128)(2,1)S(1)} %bitcast.38), channel_id=1, source_target_pairs={{0,8},{4,12},{8,0},{12,4},{1,9},{5,13},{9,1},{13,5},{2,10},{6,14},... | collective-permute-start | bytes 786440 | tf_op jit(solution)/shard_map/ppermute | solution.py:28
  103.1 17.8 %collective-permute-start.25 = (bf16[256,512]{1,0:T(8,128)(2,1)S(1)}, bf16[256,512]{1,0:T(8,128)(2,1)S(1)}, u32[]{:S(2)}, u32[]{:S(2)}) collective-permute-start(bf16[256,512]{1,0:T(8,128)(2,1)S(1)} %bitcast.39), channel_id=1, source_target_pairs={{0,4},{4,0},{8,12},{12,8},{1,5},{5,1},{9,13},{13,9},{2,6},{6,2},{1... | collective-permute-start | bytes 786440 | tf_op jit(solution)/shard_map/ppermute | solution.py:28
  105.8 15.1 %collective-permute-start.27 = (bf16[256,512]{1,0:T(8,128)(2,1)S(1)}, bf16[256,512]{1,0:T(8,128)(2,1)S(1)}, u32[]{:S(2)}, u32[]{:S(2)}) collective-permute-start(bf16[256,512]{1,0:T(8,128)(2,1)S(1)} %collective-permute-done.7.refs_0_), channel_id=1, source_target_pairs={{4,8},{8,4},{5,9},{9,5},{6,10},{10,6},{7,11},{11,7},{20,24},{24,20... | collective-permute-start | bytes 786440 | tf_op jit(solution)/shard_map/ppermute | solution.py:28
  106.5 16.8 %collective-permute-start.28 = (bf16[256,512]{1,0:T(8,128)(2,1)S(1)}, bf16[256,512]{1,0:T(8,128)(2,1)S(1)}, u32[]{:S(2)}, u32[]{:S(2)}) collective-permute-start(bf16[256,512]{1,0:T(8,128)(2,1)S(1)} %collective-permute-done.18.refs_2_), channel_id=1, source_target_pairs={{4,0},{8,12},{5,1},{9,13},{6,2},{10,14},{7,3},{11,15},{20,16},{24,... | collective-permute-start | bytes 786440 | tf_op jit(solution)/shard_map/ppermute | solution.py:28
  117.6 22.3 %collective-permute-start.35 = (bf16[128,3584]{1,0:T(8,128)(2,1)S(1)}, bf16[128,3584]{1,0:T(8,128)(2,1)S(1)}, u32[]{:S(2)}, u32[]{:S(2)}) collective-permute-start(bf16[128,3584]{1,0:T(8,128)(2,1)S(1)} %pair.6), channel_id=1, source_target_pairs={{0,2},{1,3},{2,0},{3,1},{4,6},{5,7},{6,4},{7,5},{8,10},{9,11},{10,... | collective-permute-start | bytes 2752520 | tf_op jit(solution)/shard_map/ppermute | solution.py:18
  123.3 1.8 %collective-permute-start.29 = (bf16[64,3584]{1,0:T(8,128)(2,1)S(1)}, bf16[64,3584]{1,0:T(8,128)(2,1)S(1)}, u32[]{:S(2)}, u32[]{:S(2)}) collective-permute-start(bf16[64,3584]{1,0:T(8,128)(2,1)S(1)} %get-tuple-element.98), channel_id=1, source_target_pairs={{0,1},{1,0},{2,3},{3,2},{4,5},{5,4},{6,7},{7,6},{8,9},{9,8},{10,11... | collective-permute-start | bytes 1376264 | tf_op jit(solution)/shard_map/ppermute | solution.py:18
  123.3 2.5 %collective-permute-start.30 = (bf16[64,3584]{1,0:T(8,128)(2,1)S(1)}, bf16[64,3584]{1,0:T(8,128)(2,1)S(1)}, u32[]{:S(2)}, u32[]{:S(2)}) collective-permute-start(bf16[64,3584]{1,0:T(8,128)(2,1)S(1)} %get-tuple-element.100), channel_id=1, source_target_pairs={{0,1},{1,0},{2,3},{3,2},{4,5},{5,4},{6,7},{7,6},{8,9},{9,8},{10,11... | collective-permute-start | bytes 1376264 | tf_op jit(solution)/shard_map/ppermute | solution.py:18
  126.3 9.2 %collective-permute-start.32 = (bf16[256,512]{1,0:T(8,128)(2,1)S(1)}, bf16[256,512]{1,0:T(8,128)(2,1)S(1)}, u32[]{:S(2)}, u32[]{:S(2)}) collective-permute-start(bf16[256,512]{1,0:T(8,128)(2,1)S(1)} %bitcast.40), channel_id=1, source_target_pairs={{4,8},{8,4},{5,9},{9,5},{6,10},{10,6},{7,11},{11,7},{20,24},{24,20... | collective-permute-start | bytes 786440 | tf_op jit(solution)/shard_map/ppermute | solution.py:28
  127.0 10.2 %collective-permute-start.33 = (bf16[256,512]{1,0:T(8,128)(2,1)S(1)}, bf16[256,512]{1,0:T(8,128)(2,1)S(1)}, u32[]{:S(2)}, u32[]{:S(2)}) collective-permute-start(bf16[256,512]{1,0:T(8,128)(2,1)S(1)} %collective-permute-done.26.refs_2_), channel_id=1, source_target_pairs={{4,0},{8,12},{5,1},{9,13},{6,2},{10,14},{7,3},{11,15},{20,16},{24,... | collective-permute-start | bytes 786440 | tf_op jit(solution)/shard_map/ppermute | solution.py:28
  137.3 2.6 %collective-permute-start.34 = (bf16[64,3584]{1,0:T(8,128)(2,1)S(1)}, bf16[64,3584]{1,0:T(8,128)(2,1)S(1)}, u32[]{:S(2)}, u32[]{:S(2)}) collective-permute-start(bf16[64,3584]{1,0:T(8,128)(2,1)S(1)} %get-tuple-element.106), channel_id=1, source_target_pairs={{0,1},{1,0},{2,3},{3,2},{4,5},{5,4},{6,7},{7,6},{8,9},{9,8},{10,11... | collective-permute-start | bytes 1376264 | tf_op jit(solution)/shard_map/ppermute | solution.py:18
  137.3 12.9 %collective-permute-start.36 = (bf16[64,3584]{1,0:T(8,128)(2,1)S(1)}, bf16[64,3584]{1,0:T(8,128)(2,1)S(1)}, u32[]{:S(2)}, u32[]{:S(2)}) collective-permute-start(bf16[64,3584]{1,0:T(8,128)(2,1)S(1)} %get-tuple-element.101), channel_id=1, source_target_pairs={{0,2},{1,3},{2,0},{3,1},{4,6},{5,7},{6,4},{7,5},{8,10},{9,11},{10,... | collective-permute-start | bytes 1376264 | tf_op jit(solution)/shard_map/ppermute | solution.py:18
  137.9 12.8 %collective-permute-start.43 = (bf16[64,3584]{1,0:T(8,128)(2,1)S(1)}, bf16[64,3584]{1,0:T(8,128)(2,1)S(1)}, u32[]{:S(2)}, u32[]{:S(2)}) collective-permute-start(bf16[64,3584]{1,0:T(8,128)(2,1)S(1)} %get-tuple-element.122), channel_id=1, source_target_pairs={{0,1},{1,0},{2,3},{3,2},{4,5},{5,4},{6,7},{7,6},{8,9},{9,8},{10,11... | collective-permute-start | bytes 1376264 | tf_op jit(solution)/shard_map/ppermute | solution.py:18
  138.1 12.6 %collective-permute-start.42 = (bf16[64,3584]{1,0:T(8,128)(2,1)S(1)}, bf16[64,3584]{1,0:T(8,128)(2,1)S(1)}, u32[]{:S(2)}, u32[]{:S(2)}) collective-permute-start(bf16[64,3584]{1,0:T(8,128)(2,1)S(1)} %get-tuple-element.120), channel_id=1, source_target_pairs={{0,1},{1,0},{2,3},{3,2},{4,5},{5,4},{6,7},{7,6},{8,9},{9,8},{10,11... | collective-permute-start | bytes 1376264 | tf_op jit(solution)/shard_map/ppermute | solution.py:18
  139.9 11.3 %collective-permute-start.41 = (bf16[64,3584]{1,0:T(8,128)(2,1)S(1)}, bf16[64,3584]{1,0:T(8,128)(2,1)S(1)}, u32[]{:S(2)}, u32[]{:S(2)}) collective-permute-start(bf16[64,3584]{1,0:T(8,128)(2,1)S(1)} %get-tuple-element.118), channel_id=1, source_target_pairs={{0,1},{1,0},{2,3},{3,2},{4,5},{5,4},{6,7},{7,6},{8,9},{9,8},{10,11... | collective-permute-start | bytes 1376264 | tf_op jit(solution)/shard_map/ppermute | solution.py:18
  150.2 2.5 %collective-permute-start.40 = (bf16[64,3584]{1,0:T(8,128)(2,1)S(1)}, bf16[64,3584]{1,0:T(8,128)(2,1)S(1)}, u32[]{:S(2)}, u32[]{:S(2)}) collective-permute-start(bf16[64,3584]{1,0:T(8,128)(2,1)S(1)} %get-tuple-element.115), channel_id=1, source_target_pairs={{0,1},{1,0},{2,3},{3,2},{4,5},{5,4},{6,7},{7,6},{8,9},{9,8},{10,11... | collective-permute-start | bytes 1376264 | tf_op jit(solution)/shard_map/ppermute | solution.py:18
  150.2 2.5 %collective-permute-start.39 = (bf16[64,3584]{1,0:T(8,128)(2,1)S(1)}, bf16[64,3584]{1,0:T(8,128)(2,1)S(1)}, u32[]{:S(2)}, u32[]{:S(2)}) collective-permute-start(bf16[64,3584]{1,0:T(8,128)(2,1)S(1)} %get-tuple-element.113), channel_id=1, source_target_pairs={{0,1},{1,0},{2,3},{3,2},{4,5},{5,4},{6,7},{7,6},{8,9},{9,8},{10,11... | collective-permute-start | bytes 1376264 | tf_op jit(solution)/shard_map/ppermute | solution.py:18
  150.7 2.6 %collective-permute-start.38 = (bf16[64,3584]{1,0:T(8,128)(2,1)S(1)}, bf16[64,3584]{1,0:T(8,128)(2,1)S(1)}, u32[]{:S(2)}, u32[]{:S(2)}) collective-permute-start(bf16[64,3584]{1,0:T(8,128)(2,1)S(1)} %get-tuple-element.111), channel_id=1, source_target_pairs={{0,1},{1,0},{2,3},{3,2},{4,5},{5,4},{6,7},{7,6},{8,9},{9,8},{10,11... | collective-permute-start | bytes 1376264 | tf_op jit(solution)/shard_map/ppermute | solution.py:18
  150.7 3.3 %collective-permute-start.37 = (bf16[64,3584]{1,0:T(8,128)(2,1)S(1)}, bf16[64,3584]{1,0:T(8,128)(2,1)S(1)}, u32[]{:S(2)}, u32[]{:S(2)}) collective-permute-start(bf16[64,3584]{1,0:T(8,128)(2,1)S(1)} %get-tuple-element.109), channel_id=1, source_target_pairs={{0,1},{1,0},{2,3},{3,2},{4,5},{5,4},{6,7},{7,6},{8,9},{9,8},{10,11... | collective-permute-start | bytes 1376264 | tf_op jit(solution)/shard_map/ppermute | solution.py:18
  151.2 12.5 %collective-permute-start.44 = (bf16[64,3584]{1,0:T(8,128)(2,1)S(1)}, bf16[64,3584]{1,0:T(8,128)(2,1)S(1)}, u32[]{:S(2)}, u32[]{:S(2)}) collective-permute-start(bf16[64,3584]{1,0:T(8,128)(2,1)S(1)} %get-tuple-element.124), channel_id=1, source_target_pairs={{0,2},{1,3},{2,0},{3,1},{4,6},{5,7},{6,4},{7,5},{8,10},{9,11},{10,... | collective-permute-start | bytes 1376264 | tf_op jit(solution)/shard_map/ppermute | solution.py:18
  163.7 8.2 %copy-start.1 = (bf16[7168,64]{0,1:T(8,128)(2,1)S(1)}, bf16[7168,64]{0,1:T(8,128)(2,1)}, u32[]{:S(2)}) copy-start(bf16[7168,64]{0,1:T(8,128)(2,1)} %param.10) | copy-start | bytes 2752516

commit v19 on v17

--- a/solution.py
+++ b/solution.py
@@ -89,7 +89,14 @@
 
     fetch(j).wait()
     weight = held[lax.rem(j, slots)].reshape(size * width, tile)
-    terms = jnp.dot(feats[...], weight, preferred_element_type=f32)
+    narrow = 256 if tile % 256 == 0 else tile
+    terms = jnp.concatenate(
+        [
+            jnp.dot(feats[...], weight[:, at : at + narrow], preferred_element_type=f32)
+            for at in range(0, tile, narrow)
+        ],
+        axis=1,
+    )
     if add_refs:
         terms = terms + add_refs[0][...].astype(f32)
     row = 0

time: 172 us -> 172 us (level)
  no operation moved by 1% of the time
where the time goes in v19:
time: 172 us
  Pallas kernels  64.3 us (37%)
  waiting for transfers between devices  51 us (30%)
  starting transfers between devices  33.6 us (20%)
  local copies, waits for them, and re-layouts  13.5 us (8%)
  matrix products  7.55 us (4%)
    pallas_call x8, Pallas kernels, block_terms(): pl.pallas_call(functools.partial(terms_kernel, size, len(blocks), part *...  58 us
    ppermute x16, waiting for transfers between devices, across(): return lax.ppermute(value, 'tensor', pairs)  38.9 us
    ppermute x16, starting transfers between devices, across(): return lax.ppermute(value, 'tensor', pairs)  20.2 us
    ppermute x29, starting transfers between devices, swap(): return lax.ppermute(value, 'dp', [(d, d ^ step) for d in range(size)])  13.4 us
    ppermute x29, waiting for transfers between devices, swap(): return lax.ppermute(value, 'dp', [(d, d ^ step) for d in range(size)])  12 us
    unnamed x38, local copies, waits for them, and re-layouts  10.7 us
    pallas_call x4, Pallas kernels, add_pieces(): pl.pallas_call(functools.partial(add_kernel, len(pieces)), out_shape=[jax...  4.91 us
  transfers between devices with their start and end apart: 45, of which 18 were waited for; matrix products, arithmetic and copies ran while one was open for 5% of the time, Pallas kernels for 33%

profile of v19, /device:TPU:0, one launch (start us, length us, event | category | flops | bytes accessed | tf_op | source)
XLA Modules:
  0.0 171.9 jit_solution(2076193264185196730)
XLA Ops:
  0.7 2.0 %constant_dynamic-slice_fusion = (bf16[1,1,512,256]{3,2,1,0:T(8,128)(2,1)S(1)}, bf16[1,1,512,256]{3,2,1,0:T(8,128)(2,1)S(1)}, bf16[1,1,512,256]{3,2,1,0:T(8,128)(2,1)S(1)}, bf16[1,1,512,256]{3,2,1,0:T(8,128)(2,1)}) fusion(bf16[1,4,512,256]{3,2,1,0:T(8,128)(2,1)} %param.8, s32[]{:T(128)S(6)} %select_n.96, s32[]{:T(128)S(6)} %select_n.95, s32[]{:T(128)S(6)} %select_n.94, ...), kind=kLoop, calls=%fused_computation.32 | loop fusion | bytes 2097168 | tf_op jit(solution)/shard_map/dynamic-slice.7
  2.9 3.0 %collective-permute-start.3 = (bf16[128,512]{1,0:T(8,128)(2,1)S(1)}, bf16[128,512]{1,0:T(8,128)(2,1)S(1)}, u32[]{:S(2)}, u32[]{:S(2)}) collective-permute-start(bf16[128,512]{1,0:T(8,128)(2,1)S(1)} %get-tuple-element.131), channel_id=1, source_target_pairs={{0,2},{1,3},{2,0},{3,1},{4,6},{5,7},{6,4},{7,5},{8,10},{9,11},{10,... | collective-permute-start | bytes 393224 | tf_op jit(solution)/shard_map/ppermute | solution.py:18
  6.2 3.3 %fusion.15 = f32[256,64]{0,1:T(8,128)S(1)} fusion(bf16[256,7168]{1,0:T(8,128)(2,1)} %param.7, bf16[7168,64]{0,1:T(8,128)(2,1)S(1)} %copy-done), kind=kOutput, calls=%fused_computation.38 | convolution fusion | flops 234881024 | bytes 4653056 | tf_op jit(solution)/shard_map/dot_general | solution.py:285
  9.8 1.6 collective-permute-start.11
  11.4 1.2 collective-permute-start.1
  12.6 3.0 %collective-permute-start.6 = (bf16[256,512]{1,0:T(8,128)(2,1)S(1)}, bf16[256,512]{1,0:T(8,128)(2,1)S(1)}, u32[]{:S(2)}, u32[]{:S(2)}) collective-permute-start(bf16[256,512]{1,0:T(8,128)(2,1)S(1)} %pad_maximum_fusion.1.refs_0_), channel_id=1, source_target_pairs={{0,12},{4,8},{8,4},{12,0},{1,13},{5,9},{9,5},{13,1},{2,14},{6,10},... | collective-permute-start | bytes 786440 | tf_op jit(solution)/shard_map/ppermute | solution.py:28
  15.7 1.4 collective-permute-start.4
  17.5 6.5 %collective-permute-done.6.refs_3_ = bf16[256,512]{1,0:T(8,128)(2,1)S(1)} collective-permute-done((bf16[256,512]{1,0:T(8,128)(2,1)S(1)}, bf16[256,512]{1,0:T(8,128)(2,1)S(1)}, u32[]{:S(2)}, u32[]{:S(2)}) %collective-permute-start.6) | collective-permute-done | bytes 262176 | tf_op jit(solution)/shard_map/ppermute | solution.py:28
  24.0 15.0 %collective-permute-done.5.refs_2_ = bf16[256,512]{1,0:T(8,128)(2,1)S(1)} collective-permute-done((bf16[256,512]{1,0:T(8,128)(2,1)S(1)}, bf16[256,512]{1,0:T(8,128)(2,1)S(1)}, u32[]{:S(2)}, u32[]{:S(2)}) %collective-permute-start.5) | collective-permute-done | bytes 262176 | tf_op jit(solution)/shard_map/ppermute | solution.py:28
  39.1 2.7 %collective-permute-start.10 = (bf16[256,512]{1,0:T(8,128)(2,1)S(1)}, bf16[256,512]{1,0:T(8,128)(2,1)S(1)}, u32[]{:S(2)}, u32[]{:S(2)}) collective-permute-start(bf16[256,512]{1,0:T(8,128)(2,1)S(1)} %pad_maximum_fusion.refs_0_), channel_id=1, source_target_pairs={{0,12},{4,8},{8,4},{12,0},{1,13},{5,9},{9,5},{13,1},{2,14},{6,10},... | collective-permute-start | bytes 786440 | tf_op jit(solution)/shard_map/ppermute | solution.py:28
  41.8 2.0 %collective-permute-start.9 = (bf16[256,512]{1,0:T(8,128)(2,1)S(1)}, bf16[256,512]{1,0:T(8,128)(2,1)S(1)}, u32[]{:S(2)}, u32[]{:S(2)}) collective-permute-start(bf16[256,512]{1,0:T(8,128)(2,1)S(1)} %pad_maximum_fusion.refs_0_), channel_id=1, source_target_pairs={{0,8},{4,12},{8,0},{12,4},{1,9},{5,13},{9,1},{13,5},{2,10},{6,14},... | collective-permute-start | bytes 786440 | tf_op jit(solution)/shard_map/ppermute | solution.py:28
  43.8 6.9 %terms.8 = (bf16[64,3584]{1,0:T(8,128)(2,1)S(1)}, bf16[64,3584]{1,0:T(8,128)(2,1)S(1)}, bf16[128,3584]{1,0:T(8,128)(2,1)S(1)}) custom-call(s32[1]{0:T(128)} %bitcast.place_ref, bf16[256,512]{1,0:T(8,128)(2,1)S(1)} %pad_maximum_fusion.1.refs_0_, bf16[256,512]{1,0:T(8,128)(2,1)S(1)} %collective-permute-done.4.refs_1_, ...), custom_call_target="tpu_custom_call" | custom-call | flops 469762048 | bytes 1000 | tf_op jit(solution)/shard_map/terms/pallas_call | solution.py:142
  50.7 0.9 copy-done.7
  51.6 0.8 copy-done.13
  52.4 7.0 %terms.9 = (bf16[64,3584]{1,0:T(8,128)(2,1)S(1)}, bf16[64,3584]{1,0:T(8,128)(2,1)S(1)}, bf16[128,3584]{1,0:T(8,128)(2,1)S(1)}) custom-call(s32[1]{0:T(128)} %bitcast.place_ref, bf16[256,512]{1,0:T(8,128)(2,1)S(1)} %pad_maximum_fusion.1.refs_0_, bf16[256,512]{1,0:T(8,128)(2,1)S(1)} %collective-permute-done.4.refs_1_, ...), custom_call_target="tpu_custom_call" | custom-call | flops 469762048 | bytes 1000 | tf_op jit(solution)/shard_map/terms/pallas_call | solution.py:142
  59.5 0.9 copy-done.5
  60.4 0.8 copy-done.11
  61.8 8.5 %collective-permute-done.9.refs_2_ = bf16[256,512]{1,0:T(8,128)(2,1)S(1)} collective-permute-done((bf16[256,512]{1,0:T(8,128)(2,1)S(1)}, bf16[256,512]{1,0:T(8,128)(2,1)S(1)}, u32[]{:S(2)}, u32[]{:S(2)}) %collective-permute-start.9) | collective-permute-done | bytes 262176 | tf_op jit(solution)/shard_map/ppermute | solution.py:28
  71.3 1.0 collective-permute-done.13.refs_0_
  72.3 1.3 collective-permute-done.14.refs_1_
  73.6 1.2 copy-done.8
  74.8 1.7 pair.4
  76.5 0.6 collective-permute-start.21
  77.1 1.2 copy-done.6
  78.8 0.9 copy-done.2
  79.8 2.3 %collective-permute-start.17 = (bf16[256,512]{1,0:T(8,128)(2,1)S(1)}, bf16[256,512]{1,0:T(8,128)(2,1)S(1)}, u32[]{:S(2)}, u32[]{:S(2)}) collective-permute-start(bf16[256,512]{1,0:T(8,128)(2,1)S(1)} %collective-permute-done.7.refs_0_), channel_id=1, source_target_pairs={{0,4},{4,0},{8,12},{12,8},{1,5},{5,1},{9,13},{13,9},{2,6},{6,2},{1... | collective-permute-start | bytes 786440 | tf_op jit(solution)/shard_map/ppermute | solution.py:28
  82.1 7.5 %terms.10 = (bf16[64,3584]{1,0:T(8,128)(2,1)}, bf16[64,3584]{1,0:T(8,128)(2,1)S(1)}, bf16[128,3584]{1,0:T(8,128)(2,1)S(1)}) custom-call(s32[1]{0:T(128)} %bitcast.place_ref, bf16[256,512]{1,0:T(8,128)(2,1)S(1)} %pad_maximum_fusion.refs_0_, bf16[256,512]{1,0:T(8,128)(2,1)S(1)} %collective-permute-done.8.refs_1_, ...), custom_call_target="tpu_custom_call" | custom-call | flops 469762048 | bytes 1000 | tf_op jit(solution)/shard_map/terms/pallas_call | solution.py:142
  89.6 1.0 copy-done.3
  90.6 3.0 %collective-permute-done.18.refs_2_ = bf16[256,512]{1,0:T(8,128)(2,1)S(1)} collective-permute-done((bf16[256,512]{1,0:T(8,128)(2,1)S(1)}, bf16[256,512]{1,0:T(8,128)(2,1)S(1)}, u32[]{:S(2)}, u32[]{:S(2)}) %collective-permute-start.18) | collective-permute-done | bytes 262176 | tf_op jit(solution)/shard_map/ppermute | solution.py:28
  94.3 0.8 collective-permute-start.24
  95.2 0.9 collective-permute-start.23
  96.2 0.8 copy-done.9
  97.2 1.2 collective-permute-start.31
  98.5 1.2 copy-done.4
  99.7 1.0 copy-done.10
  100.7 2.1 %pair.6 = bf16[128,3584]{1,0:T(8,128)(2,1)S(1)} custom-call(bf16[128,3584]{1,0:T(8,128)(2,1)S(1)} %copy-done.4, bf16[64,3584]{1,0:T(8,128)(2,1)} %collective-permute-done.19.refs_0_, bf16[64,3584]{1,0:T(8,128)(2,1)S(1)} %copy-done.10), custom_call_target="tpu_custom_call" | custom-call | flops 1000 | bytes 1000 | tf_op jit(solution)/shard_map/pair/pallas_call | solution.py:188
  103.1 2.7 %collective-permute-start.25 = (bf16[256,512]{1,0:T(8,128)(2,1)S(1)}, bf16[256,512]{1,0:T(8,128)(2,1)S(1)}, u32[]{:S(2)}, u32[]{:S(2)}) collective-permute-start(bf16[256,512]{1,0:T(8,128)(2,1)S(1)} %bitcast.39), channel_id=1, source_target_pairs={{0,4},{4,0},{8,12},{12,8},{1,5},{5,1},{9,13},{13,9},{2,6},{6,2},{1... | collective-permute-start | bytes 786440 | tf_op jit(solution)/shard_map/ppermute | solution.py:28
  105.8 0.7 collective-permute-start.27
  106.5 1.3 collective-permute-start.28
  107.8 6.9 %terms.11 = (bf16[64,3584]{1,0:T(8,128)(2,1)S(1)}, bf16[64,3584]{1,0:T(8,128)(2,1)S(1)}, bf16[128,3584]{1,0:T(8,128)(2,1)S(1)}) custom-call(s32[1]{0:T(128)} %bitcast.place_ref, bf16[256,512]{1,0:T(8,128)(2,1)S(1)} %pad_maximum_fusion.refs_0_, bf16[256,512]{1,0:T(8,128)(2,1)S(1)} %collective-permute-done.8.refs_1_, ...), custom_call_target="tpu_custom_call" | custom-call | flops 469762048 | bytes 1000 | tf_op jit(solution)/shard_map/terms/pallas_call | solution.py:142
  115.1 0.9 fusion.6
  115.9 1.7 collective-permute-done.26.refs_2_
  117.6 0.6 collective-permute-start.35
  118.2 2.7 %fusion.4 = f32[1024,1024]{1,0:T(8,128)} fusion(bf16[16,4224]{1,0:T(8,128)(2,1)S(1)} %pad_maximum_fusion.2, s32[]{:T(128)S(6)} %select_n.121, s32[]{:T(128)S(6)} %select_n.122), kind=kOutput, calls=%fused_computation.20 | convolution fusion | flops 33554432 | bytes 4259848 | tf_op jit(solution)/shard_map/dot_general | solution.py:274
  120.9 2.4 %collective-permute-done.28.refs_4_ = bf16[256,512]{1,0:T(8,128)(2,1)S(1)} collective-permute-done((bf16[256,512]{1,0:T(8,128)(2,1)S(1)}, bf16[256,512]{1,0:T(8,128)(2,1)S(1)}, u32[]{:S(2)}, u32[]{:S(2)}) %collective-permute-start.28) | collective-permute-done | bytes 262176 | tf_op jit(solution)/shard_map/ppermute | solution.py:28
  123.8 1.3 collective-permute-done.29.refs_0_
  125.1 0.7 collective-permute-done.30.refs_1_
  125.8 0.5 pair.7
  126.3 0.7 collective-permute-start.32
  127.0 1.5 collective-permute-start.33
  128.5 6.9 %terms.12 = (bf16[64,3584]{1,0:T(8,128)(2,1)S(1)}, bf16[64,3584]{1,0:T(8,128)(2,1)S(1)}, bf16[64,3584]{1,0:T(8,128)(2,1)S(1)}, bf16[64,3584]{1,0:T(8,128)(2,1)S(1)}) custom-call(s32[1]{0:T(128)} %bitcast.place_ref, bf16[256,512]{1,0:T(8,128)(2,1)S(1)} %collective-permute-done.7.refs_0_, bf16[256,512]{1,0:T(8,128)(2,1)S(1)} %collective-permute-done.17.refs_1_, ...), custom_call_target="tpu_custom_call" | custom-call | flops 469762048 | bytes 1000 | tf_op jit(solution)/shard_map/terms/pallas_call | solution.py:142
  135.5 1.8 %collective-permute-done.33.refs_4_ = bf16[256,512]{1,0:T(8,128)(2,1)S(1)} collective-permute-done((bf16[256,512]{1,0:T(8,128)(2,1)S(1)}, bf16[256,512]{1,0:T(8,128)(2,1)S(1)}, u32[]{:S(2)}, u32[]{:S(2)}) %collective-permute-start.33) | collective-permute-done | bytes 262176 | tf_op jit(solution)/shard_map/ppermute | solution.py:28
  137.3 0.6 collective-permute-start.36
  138.4 1.5 collective-permute-done.35.refs_5_
  139.9 6.9 %terms.13 = (bf16[64,3584]{1,0:T(8,128)(2,1)S(1)}, bf16[64,3584]{1,0:T(8,128)(2,1)S(1)}, bf16[64,3584]{1,0:T(8,128)(2,1)S(1)}, bf16[64,3584]{1,0:T(8,128)(2,1)S(1)}) custom-call(s32[1]{0:T(128)} %bitcast.place_ref, bf16[256,512]{1,0:T(8,128)(2,1)S(1)} %collective-permute-done.7.refs_0_, bf16[256,512]{1,0:T(8,128)(2,1)S(1)} %collective-permute-done.17.refs_1_, ...), custom_call_target="tpu_custom_call" | custom-call | flops 469762048 | bytes 1000 | tf_op jit(solution)/shard_map/terms/pallas_call | solution.py:142
  146.8 3.4 %collective-permute-done.36.refs_7_ = bf16[64,3584]{1,0:T(8,128)(2,1)S(1)} collective-permute-done((bf16[64,3584]{1,0:T(8,128)(2,1)S(1)}, bf16[64,3584]{1,0:T(8,128)(2,1)S(1)}, u32[]{:S(2)}, u32[]{:S(2)}) %collective-permute-start.36) | collective-permute-done | bytes 458784 | tf_op jit(solution)/shard_map/ppermute | solution.py:18
  151.2 0.6 collective-permute-start.44
  151.8 0.8 sums.3.refs_6_
  152.7 0.6 collective-permute-done.38.refs_1_
  153.3 0.7 collective-permute-done.37.refs_0_
  154.0 0.6 sums.2.refs_6_
  154.6 7.7 %terms.14.refs_9_ = bf16[256,7168]{1,0:T(8,128)(2,1)} custom-call(s32[1]{0:T(128)} %bitcast.place_ref, bf16[256,512]{1,0:T(8,128)(2,1)S(1)} %bitcast.41, bf16[256,512]{1,0:T(8,128)(2,1)S(1)} %collective-permute-done.25.refs_1_, bf16[256,512]{1,0:T(8,128)(2,1)S(1)} %collective-permute-done.26.refs_2_, bf16[256,512]{1,0:T(8,128)(2,1)S(1)} %collective-permute-done.32.refs_3_, ...), custom_call_target="tpu_custom_call" | custom-call | flops 469762048 | bytes 1000 | tf_op jit(solution)/shard_map/terms/pallas_call | solution.py:142
  162.3 1.4 collective-permute-done.44.refs_8_
  163.7 8.0 %terms.15 = bf16[256,7168]{1,0:T(8,128)(2,1)} custom-call(s32[1]{0:T(128)} %bitcast.place_ref, bf16[256,512]{1,0:T(8,128)(2,1)S(1)} %bitcast.42, bf16[256,512]{1,0:T(8,128)(2,1)S(1)} %collective-permute-done.25.refs_1_, bf16[256,512]{1,0:T(8,128)(2,1)S(1)} %collective-permute-done.26.refs_2_, ...), custom_call_target="tpu_custom_call", output_to_operand_aliasing={{}: (10, {})} | custom-call | flops 469762048 | bytes 1000 | tf_op jit(solution)/shard_map/terms/pallas_call | solution.py:142
  (107 shorter events, 7.2 us)
Async XLA Ops:
  0.6 5.5 %copy-start = (bf16[7168,64]{0,1:T(8,128)(2,1)S(1)}, bf16[7168,64]{0,1:T(8,128)(2,1)}, u32[]{:S(2)}) copy-start(bf16[7168,64]{0,1:T(8,128)(2,1)} %param.10) | copy-start | bytes 2752516
  2.7 6.7 %copy-start.14 = (bf16[1,4,512,256]{3,2,1,0:T(8,128)(2,1)S(1)}, bf16[1,4,512,256]{3,2,1,0:T(8,128)(2,1)}, u32[]{:S(2)}) copy-start(bf16[1,4,512,256]{3,2,1,0:T(8,128)(2,1)} %param.8) | copy-start | bytes 3145732
  2.7 6.7 %copy-start.16 = (bf16[1,4,512,64]{2,3,1,0:T(8,128)(2,1)S(1)}, bf16[1,4,512,64]{2,3,1,0:T(8,128)(2,1)}, u32[]{:S(2)}) copy-start(bf16[1,4,512,64]{2,3,1,0:T(8,128)(2,1)} %param.11) | copy-start | bytes 786436
  2.9 9.7 %collective-permute-start.3 = (bf16[128,512]{1,0:T(8,128)(2,1)S(1)}, bf16[128,512]{1,0:T(8,128)(2,1)S(1)}, u32[]{:S(2)}, u32[]{:S(2)}) collective-permute-start(bf16[128,512]{1,0:T(8,128)(2,1)S(1)} %get-tuple-element.131), channel_id=1, source_target_pairs={{0,2},{1,3},{2,0},{3,1},{4,6},{5,7},{6,4},{7,5},{8,10},{9,11},{10,... | collective-permute-start | bytes 393224 | tf_op jit(solution)/shard_map/ppermute | solution.py:18
  6.0 9.6 %copy-start.17 = (s32[1,256]{1,0:T(1,128)S(1)}, s32[1,256]{1,0:T(1,128)}, u32[]{:S(2)}) copy-start(s32[1,256]{1,0:T(1,128)} %param.12) | copy-start | bytes 3076
  6.1 6.5 %collective-permute-start.2 = (bf16[128,512]{1,0:T(8,128)(2,1)S(1)}, bf16[128,512]{1,0:T(8,128)(2,1)S(1)}, u32[]{:S(2)}, u32[]{:S(2)}) collective-permute-start(bf16[128,512]{1,0:T(8,128)(2,1)S(1)} %get-tuple-element.129), channel_id=1, source_target_pairs={{0,3},{1,2},{2,1},{3,0},{4,7},{5,6},{6,5},{7,4},{8,11},{9,10},{10,... | collective-permute-start | bytes 393224 | tf_op jit(solution)/shard_map/ppermute | solution.py:18
  9.8 7.6 %collective-permute-start.11 = (f32[256,128]{0,1:T(8,128)S(1)}, f32[256,128]{0,1:T(8,128)S(1)}, u32[]{:S(2)}, u32[]{:S(2)}) collective-permute-start(f32[256,128]{0,1:T(8,128)S(1)} %pad_maximum_fusion.3), channel_id=1, source_target_pairs={{0,4},{4,0},{8,12},{12,8},{1,5},{5,1},{9,13},{13,9},{2,6},{6,2},{1... | collective-permute-start | bytes 393224 | tf_op jit(solution)/shard_map/ppermute | solution.py:28
  11.4 27.6 %collective-permute-start.1 = (bf16[128,512]{1,0:T(8,128)(2,1)S(1)}, bf16[128,512]{1,0:T(8,128)(2,1)S(1)}, u32[]{:S(2)}, u32[]{:S(2)}) collective-permute-start(bf16[128,512]{1,0:T(8,128)(2,1)S(1)} %get-tuple-element.132), channel_id=1, source_target_pairs={{0,2},{1,3},{2,0},{3,1},{4,6},{5,7},{6,4},{7,5},{8,10},{9,11},{10,... | collective-permute-start | bytes 393224 | tf_op jit(solution)/shard_map/ppermute | solution.py:18
  12.6 11.4 %collective-permute-start.6 = (bf16[256,512]{1,0:T(8,128)(2,1)S(1)}, bf16[256,512]{1,0:T(8,128)(2,1)S(1)}, u32[]{:S(2)}, u32[]{:S(2)}) collective-permute-start(bf16[256,512]{1,0:T(8,128)(2,1)S(1)} %pad_maximum_fusion.1.refs_0_), channel_id=1, source_target_pairs={{0,12},{4,8},{8,4},{12,0},{1,13},{5,9},{9,5},{13,1},{2,14},{6,10},... | collective-permute-start | bytes 786440 | tf_op jit(solution)/shard_map/ppermute | solution.py:28
  15.7 23.3 %collective-permute-start.5 = (bf16[256,512]{1,0:T(8,128)(2,1)S(1)}, bf16[256,512]{1,0:T(8,128)(2,1)S(1)}, u32[]{:S(2)}, u32[]{:S(2)}) collective-permute-start(bf16[256,512]{1,0:T(8,128)(2,1)S(1)} %pad_maximum_fusion.1.refs_0_), channel_id=1, source_target_pairs={{0,8},{4,12},{8,0},{12,4},{1,9},{5,13},{9,1},{13,5},{2,10},{6,14},... | collective-permute-start | bytes 786440 | tf_op jit(solution)/shard_map/ppermute | solution.py:28
  15.7 23.3 %collective-permute-start.4 = (bf16[256,512]{1,0:T(8,128)(2,1)S(1)}, bf16[256,512]{1,0:T(8,128)(2,1)S(1)}, u32[]{:S(2)}, u32[]{:S(2)}) collective-permute-start(bf16[256,512]{1,0:T(8,128)(2,1)S(1)} %pad_maximum_fusion.1.refs_0_), channel_id=1, source_target_pairs={{0,4},{4,0},{8,12},{12,8},{1,5},{5,1},{9,13},{13,9},{2,6},{6,2},{1... | collective-permute-start | bytes 786440 | tf_op jit(solution)/shard_map/ppermute | solution.py:28
  17.4 21.7 %collective-permute-start = (bf16[128,512]{1,0:T(8,128)(2,1)S(1)}, bf16[128,512]{1,0:T(8,128)(2,1)S(1)}, u32[]{:S(2)}, u32[]{:S(2)}) collective-permute-start(bf16[128,512]{1,0:T(8,128)(2,1)S(1)} %get-tuple-element.130), channel_id=1, source_target_pairs={{0,3},{1,2},{2,1},{3,0},{4,7},{5,6},{6,5},{7,4},{8,11},{9,10},{10,... | collective-permute-start | bytes 393224 | tf_op jit(solution)/shard_map/ppermute | solution.py:18
  24.0 15.0 %collective-permute-start.7 = (bf16[256,512]{1,0:T(8,128)(2,1)S(1)}, bf16[256,512]{1,0:T(8,128)(2,1)S(1)}, u32[]{:S(2)}, u32[]{:S(2)}) collective-permute-start(bf16[256,512]{1,0:T(8,128)(2,1)S(1)} %bitcast.46), channel_id=1, source_target_pairs={{0,1},{1,0},{2,3},{3,2},{4,5},{5,4},{6,7},{7,6},{8,9},{9,8},{10,11... | collective-permute-start | bytes 786440 | tf_op jit(solution)/shard_map/ppermute | solution.py:18
  39.0 22.2 %collective-permute-start.12 = (f32[256,128]{0,1:T(8,128)S(1)}, f32[256,128]{0,1:T(8,128)S(1)}, u32[]{:S(2)}, u32[]{:S(2)}) collective-permute-start(f32[256,128]{0,1:T(8,128)S(1)} %fusion.14), channel_id=1, source_target_pairs={{0,8},{4,12},{8,0},{12,4},{1,9},{5,13},{9,1},{13,5},{2,10},{6,14},... | collective-permute-start | bytes 393224 | tf_op jit(solution)/shard_map/ppermute | solution.py:28
  39.1 22.8 %collective-permute-start.10 = (bf16[256,512]{1,0:T(8,128)(2,1)S(1)}, bf16[256,512]{1,0:T(8,128)(2,1)S(1)}, u32[]{:S(2)}, u32[]{:S(2)}) collective-permute-start(bf16[256,512]{1,0:T(8,128)(2,1)S(1)} %pad_maximum_fusion.refs_0_), channel_id=1, source_target_pairs={{0,12},{4,8},{8,4},{12,0},{1,13},{5,9},{9,5},{13,1},{2,14},{6,10},... | collective-permute-start | bytes 786440 | tf_op jit(solution)/shard_map/ppermute | solution.py:28
  41.8 28.5 %collective-permute-start.9 = (bf16[256,512]{1,0:T(8,128)(2,1)S(1)}, bf16[256,512]{1,0:T(8,128)(2,1)S(1)}, u32[]{:S(2)}, u32[]{:S(2)}) collective-permute-start(bf16[256,512]{1,0:T(8,128)(2,1)S(1)} %pad_maximum_fusion.refs_0_), channel_id=1, source_target_pairs={{0,8},{4,12},{8,0},{12,4},{1,9},{5,13},{9,1},{13,5},{2,10},{6,14},... | collective-permute-start | bytes 786440 | tf_op jit(solution)/shard_map/ppermute | solution.py:28
  43.8 26.5 %collective-permute-start.8 = (bf16[256,512]{1,0:T(8,128)(2,1)S(1)}, bf16[256,512]{1,0:T(8,128)(2,1)S(1)}, u32[]{:S(2)}, u32[]{:S(2)}) collective-permute-start(bf16[256,512]{1,0:T(8,128)(2,1)S(1)} %pad_maximum_fusion.refs_0_), channel_id=1, source_target_pairs={{0,4},{4,0},{8,12},{12,8},{1,5},{5,1},{9,13},{13,9},{2,6},{6,2},{1... | collective-permute-start | bytes 786440 | tf_op jit(solution)/shard_map/ppermute | solution.py:28
  50.7 0.9 copy-start.7
  51.6 0.8 copy-start.13
  52.4 7.0 %copy-start.12 = (bf16[64,3584]{1,0:T(8,128)(2,1)}, bf16[64,3584]{1,0:T(8,128)(2,1)S(1)}, u32[]{:S(2)}) copy-start(bf16[64,3584]{1,0:T(8,128)(2,1)S(1)} %get-tuple-element.75) | copy-start | bytes 1376260
  59.5 0.9 copy-start.5
  60.4 0.8 copy-start.11
  61.2 20.9 %copy-start.18 = (s32[4]{0:T(128)S(1)}, s32[4]{0:T(128)}, u32[]{:S(2)}) copy-start(s32[4]{0:T(128)} %param.13) | copy-start | bytes 52
  70.3 2.0 %collective-permute-start.13 = (bf16[64,3584]{1,0:T(8,128)(2,1)}, bf16[64,3584]{1,0:T(8,128)(2,1)S(1)}, u32[]{:S(2)}, u32[]{:S(2)}) collective-permute-start(bf16[64,3584]{1,0:T(8,128)(2,1)} %copy-done.13), channel_id=1, source_target_pairs={{0,1},{1,0},{2,3},{3,2},{4,5},{5,4},{6,7},{7,6},{8,9},{9,8},{10,11... | collective-permute-start | bytes 1376264 | tf_op jit(solution)/shard_map/ppermute | solution.py:18
  70.3 3.3 %collective-permute-start.14 = (bf16[64,3584]{1,0:T(8,128)(2,1)}, bf16[64,3584]{1,0:T(8,128)(2,1)S(1)}, u32[]{:S(2)}, u32[]{:S(2)}) collective-permute-start(bf16[64,3584]{1,0:T(8,128)(2,1)} %copy-done.12), channel_id=1, source_target_pairs={{0,1},{1,0},{2,3},{3,2},{4,5},{5,4},{6,7},{7,6},{8,9},{9,8},{10,11... | collective-permute-start | bytes 1376264 | tf_op jit(solution)/shard_map/ppermute | solution.py:18
  70.8 6.3 %collective-permute-start.15 = (bf16[64,3584]{1,0:T(8,128)(2,1)}, bf16[64,3584]{1,0:T(8,128)(2,1)S(1)}, u32[]{:S(2)}, u32[]{:S(2)}) collective-permute-start(bf16[64,3584]{1,0:T(8,128)(2,1)} %copy-done.11), channel_id=1, source_target_pairs={{0,1},{1,0},{2,3},{3,2},{4,5},{5,4},{6,7},{7,6},{8,9},{9,8},{10,11... | collective-permute-start | bytes 1376264 | tf_op jit(solution)/shard_map/ppermute | solution.py:18
  70.8 6.3 %collective-permute-start.16 = (bf16[64,3584]{1,0:T(8,128)(2,1)S(1)}, bf16[64,3584]{1,0:T(8,128)(2,1)S(1)}, u32[]{:S(2)}, u32[]{:S(2)}) collective-permute-start(bf16[64,3584]{1,0:T(8,128)(2,1)S(1)} %get-tuple-element.79), channel_id=1, source_target_pairs={{0,1},{1,0},{2,3},{3,2},{4,5},{5,4},{6,7},{7,6},{8,9},{9,8},{10,11... | collective-permute-start | bytes 1376264 | tf_op jit(solution)/shard_map/ppermute | solution.py:18
  73.6 1.2 copy-start.8
  76.5 30.0 %collective-permute-start.21 = (bf16[128,3584]{1,0:T(8,128)(2,1)}, bf16[128,3584]{1,0:T(8,128)(2,1)S(1)}, u32[]{:S(2)}, u32[]{:S(2)}) collective-permute-start(bf16[128,3584]{1,0:T(8,128)(2,1)} %pair.4), channel_id=1, source_target_pairs={{0,2},{1,3},{2,0},{3,1},{4,6},{5,7},{6,4},{7,5},{8,10},{9,11},{10,... | collective-permute-start | bytes 2752520 | tf_op jit(solution)/shard_map/ppermute | solution.py:18
  77.1 1.2 copy-start.6
  78.8 0.9 copy-start.2
  79.8 13.8 %collective-permute-start.18 = (bf16[256,512]{1,0:T(8,128)(2,1)S(1)}, bf16[256,512]{1,0:T(8,128)(2,1)S(1)}, u32[]{:S(2)}, u32[]{:S(2)}) collective-permute-start(bf16[256,512]{1,0:T(8,128)(2,1)S(1)} %collective-permute-done.7.refs_0_), channel_id=1, source_target_pairs={{0,8},{4,12},{8,0},{12,4},{1,9},{5,13},{9,1},{13,5},{2,10},{6,14},... | collective-permute-start | bytes 786440 | tf_op jit(solution)/shard_map/ppermute | solution.py:28
  79.8 14.0 %collective-permute-start.17 = (bf16[256,512]{1,0:T(8,128)(2,1)S(1)}, bf16[256,512]{1,0:T(8,128)(2,1)S(1)}, u32[]{:S(2)}, u32[]{:S(2)}) collective-permute-start(bf16[256,512]{1,0:T(8,128)(2,1)S(1)} %collective-permute-done.7.refs_0_), channel_id=1, source_target_pairs={{0,4},{4,0},{8,12},{12,8},{1,5},{5,1},{9,13},{13,9},{2,6},{6,2},{1... | collective-permute-start | bytes 786440 | tf_op jit(solution)/shard_map/ppermute | solution.py:28
  82.1 15.0 %copy-start.15 = (bf16[1,1,512,256]{3,2,1,0:T(8,128)(2,1)S(1)}, bf16[1,1,512,256]{3,2,1,0:T(8,128)(2,1)}, u32[]{:S(2)}) copy-start(bf16[1,1,512,256]{3,2,1,0:T(8,128)(2,1)} %get-tuple-element.128) | copy-start | bytes 786436
  89.6 1.0 copy-start.3
  93.7 2.4 %collective-permute-start.20 = (bf16[64,3584]{1,0:T(8,128)(2,1)S(1)}, bf16[64,3584]{1,0:T(8,128)(2,1)S(1)}, u32[]{:S(2)}, u32[]{:S(2)}) collective-permute-start(bf16[64,3584]{1,0:T(8,128)(2,1)S(1)} %get-tuple-element.86), channel_id=1, source_target_pairs={{0,1},{1,0},{2,3},{3,2},{4,5},{5,4},{6,7},{7,6},{8,9},{9,8},{10,11... | collective-permute-start | bytes 1376264 | tf_op jit(solution)/shard_map/ppermute | solution.py:18
  93.7 3.5 %collective-permute-start.19 = (bf16[64,3584]{1,0:T(8,128)(2,1)}, bf16[64,3584]{1,0:T(8,128)(2,1)}, u32[]{:S(2)}, u32[]{:S(2)}) collective-permute-start(bf16[64,3584]{1,0:T(8,128)(2,1)} %get-tuple-element.84), channel_id=1, source_target_pairs={{0,1},{1,0},{2,3},{3,2},{4,5},{5,4},{6,7},{7,6},{8,9},{9,8},{10,11... | collective-permute-start | bytes 1376264 | tf_op jit(solution)/shard_map/ppermute | solution.py:18
  94.3 8.5 %collective-permute-start.24 = (bf16[4,4224]{1,0:T(4,128)(2,1)S(1)}, bf16[4,4224]{1,0:T(4,128)(2,1)S(1)}, u32[]{:S(2)}, u32[]{:S(2)}) collective-permute-start(bf16[4,4224]{1,0:T(4,128)(2,1)S(1)} %pad_maximum_fusion.4), channel_id=1, source_target_pairs={{0,3},{1,2},{2,1},{3,0},{4,7},{5,6},{6,5},{7,4},{8,11},{9,10},{10,... | collective-permute-start | bytes 101384 | tf_op jit(solution)/shard_map/ppermute | solution.py:18
  95.2 7.9 %collective-permute-start.23 = (bf16[4,4224]{1,0:T(4,128)(2,1)S(1)}, bf16[4,4224]{1,0:T(4,128)(2,1)S(1)}, u32[]{:S(2)}, u32[]{:S(2)}) collective-permute-start(bf16[4,4224]{1,0:T(4,128)(2,1)S(1)} %pad_maximum_fusion.4), channel_id=1, source_target_pairs={{0,2},{1,3},{2,0},{3,1},{4,6},{5,7},{6,4},{7,5},{8,10},{9,11},{10,... | collective-permute-start | bytes 101384 | tf_op jit(solution)/shard_map/ppermute | solution.py:18
  96.2 0.8 copy-start.9
  96.9 8.9 %collective-permute-start.22 = (bf16[4,4224]{1,0:T(4,128)(2,1)S(1)}, bf16[4,4224]{1,0:T(4,128)(2,1)S(1)}, u32[]{:S(2)}, u32[]{:S(2)}) collective-permute-start(bf16[4,4224]{1,0:T(4,128)(2,1)S(1)} %pad_maximum_fusion.4), channel_id=1, source_target_pairs={{0,1},{1,0},{2,3},{3,2},{4,5},{5,4},{6,7},{7,6},{8,9},{9,8},{10,11... | collective-permute-start | bytes 101384 | tf_op jit(solution)/shard_map/ppermute | solution.py:18
  97.2 31.3 %collective-permute-start.31 = (bf16[128,3584]{1,0:T(8,128)(2,1)}, bf16[128,3584]{1,0:T(8,128)(2,1)S(1)}, u32[]{:S(2)}, u32[]{:S(2)}) collective-permute-start(bf16[128,3584]{1,0:T(8,128)(2,1)} %copy-done.2), channel_id=1, source_target_pairs={{0,2},{1,3},{2,0},{3,1},{4,6},{5,7},{6,4},{7,5},{8,10},{9,11},{10,... | collective-permute-start | bytes 2752520 | tf_op jit(solution)/shard_map/ppermute | solution.py:18
  98.5 1.2 copy-start.4
  99.7 1.0 copy-start.10
  102.8 14.8 %collective-permute-start.26 = (bf16[256,512]{1,0:T(8,128)(2,1)S(1)}, bf16[256,512]{1,0:T(8,128)(2,1)S(1)}, u32[]{:S(2)}, u32[]{:S(2)}) collective-permute-start(bf16[256,512]{1,0:T(8,128)(2,1)S(1)} %bitcast.38), channel_id=1, source_target_pairs={{0,8},{4,12},{8,0},{12,4},{1,9},{5,13},{9,1},{13,5},{2,10},{6,14},... | collective-permute-start | bytes 786440 | tf_op jit(solution)/shard_map/ppermute | solution.py:28
  103.1 17.8 %collective-permute-start.25 = (bf16[256,512]{1,0:T(8,128)(2,1)S(1)}, bf16[256,512]{1,0:T(8,128)(2,1)S(1)}, u32[]{:S(2)}, u32[]{:S(2)}) collective-permute-start(bf16[256,512]{1,0:T(8,128)(2,1)S(1)} %bitcast.39), channel_id=1, source_target_pairs={{0,4},{4,0},{8,12},{12,8},{1,5},{5,1},{9,13},{13,9},{2,6},{6,2},{1... | collective-permute-start | bytes 786440 | tf_op jit(solution)/shard_map/ppermute | solution.py:28
  105.8 15.1 %collective-permute-start.27 = (bf16[256,512]{1,0:T(8,128)(2,1)S(1)}, bf16[256,512]{1,0:T(8,128)(2,1)S(1)}, u32[]{:S(2)}, u32[]{:S(2)}) collective-permute-start(bf16[256,512]{1,0:T(8,128)(2,1)S(1)} %collective-permute-done.7.refs_0_), channel_id=1, source_target_pairs={{4,8},{8,4},{5,9},{9,5},{6,10},{10,6},{7,11},{11,7},{20,24},{24,20... | collective-permute-start | bytes 786440 | tf_op jit(solution)/shard_map/ppermute | solution.py:28
  106.5 16.8 %collective-permute-start.28 = (bf16[256,512]{1,0:T(8,128)(2,1)S(1)}, bf16[256,512]{1,0:T(8,128)(2,1)S(1)}, u32[]{:S(2)}, u32[]{:S(2)}) collective-permute-start(bf16[256,512]{1,0:T(8,128)(2,1)S(1)} %collective-permute-done.18.refs_2_), channel_id=1, source_target_pairs={{4,0},{8,12},{5,1},{9,13},{6,2},{10,14},{7,3},{11,15},{20,16},{24,... | collective-permute-start | bytes 786440 | tf_op jit(solution)/shard_map/ppermute | solution.py:28
  117.6 22.3 %collective-permute-start.35 = (bf16[128,3584]{1,0:T(8,128)(2,1)S(1)}, bf16[128,3584]{1,0:T(8,128)(2,1)S(1)}, u32[]{:S(2)}, u32[]{:S(2)}) collective-permute-start(bf16[128,3584]{1,0:T(8,128)(2,1)S(1)} %pair.6), channel_id=1, source_target_pairs={{0,2},{1,3},{2,0},{3,1},{4,6},{5,7},{6,4},{7,5},{8,10},{9,11},{10,... | collective-permute-start | bytes 2752520 | tf_op jit(solution)/shard_map/ppermute | solution.py:18
  123.3 1.8 %collective-permute-start.29 = (bf16[64,3584]{1,0:T(8,128)(2,1)S(1)}, bf16[64,3584]{1,0:T(8,128)(2,1)S(1)}, u32[]{:S(2)}, u32[]{:S(2)}) collective-permute-start(bf16[64,3584]{1,0:T(8,128)(2,1)S(1)} %get-tuple-element.98), channel_id=1, source_target_pairs={{0,1},{1,0},{2,3},{3,2},{4,5},{5,4},{6,7},{7,6},{8,9},{9,8},{10,11... | collective-permute-start | bytes 1376264 | tf_op jit(solution)/shard_map/ppermute | solution.py:18
  123.3 2.5 %collective-permute-start.30 = (bf16[64,3584]{1,0:T(8,128)(2,1)S(1)}, bf16[64,3584]{1,0:T(8,128)(2,1)S(1)}, u32[]{:S(2)}, u32[]{:S(2)}) collective-permute-start(bf16[64,3584]{1,0:T(8,128)(2,1)S(1)} %get-tuple-element.100), channel_id=1, source_target_pairs={{0,1},{1,0},{2,3},{3,2},{4,5},{5,4},{6,7},{7,6},{8,9},{9,8},{10,11... | collective-permute-start | bytes 1376264 | tf_op jit(solution)/shard_map/ppermute | solution.py:18
  126.3 9.1 %collective-permute-start.32 = (bf16[256,512]{1,0:T(8,128)(2,1)S(1)}, bf16[256,512]{1,0:T(8,128)(2,1)S(1)}, u32[]{:S(2)}, u32[]{:S(2)}) collective-permute-start(bf16[256,512]{1,0:T(8,128)(2,1)S(1)} %bitcast.40), channel_id=1, source_target_pairs={{4,8},{8,4},{5,9},{9,5},{6,10},{10,6},{7,11},{11,7},{20,24},{24,20... | collective-permute-start | bytes 786440 | tf_op jit(solution)/shard_map/ppermute | solution.py:28
  127.0 10.2 %collective-permute-start.33 = (bf16[256,512]{1,0:T(8,128)(2,1)S(1)}, bf16[256,512]{1,0:T(8,128)(2,1)S(1)}, u32[]{:S(2)}, u32[]{:S(2)}) collective-permute-start(bf16[256,512]{1,0:T(8,128)(2,1)S(1)} %collective-permute-done.26.refs_2_), channel_id=1, source_target_pairs={{4,0},{8,12},{5,1},{9,13},{6,2},{10,14},{7,3},{11,15},{20,16},{24,... | collective-permute-start | bytes 786440 | tf_op jit(solution)/shard_map/ppermute | solution.py:28
  137.3 2.6 %collective-permute-start.34 = (bf16[64,3584]{1,0:T(8,128)(2,1)S(1)}, bf16[64,3584]{1,0:T(8,128)(2,1)S(1)}, u32[]{:S(2)}, u32[]{:S(2)}) collective-permute-start(bf16[64,3584]{1,0:T(8,128)(2,1)S(1)} %get-tuple-element.106), channel_id=1, source_target_pairs={{0,1},{1,0},{2,3},{3,2},{4,5},{5,4},{6,7},{7,6},{8,9},{9,8},{10,11... | collective-permute-start | bytes 1376264 | tf_op jit(solution)/shard_map/ppermute | solution.py:18
  137.3 12.9 %collective-permute-start.36 = (bf16[64,3584]{1,0:T(8,128)(2,1)S(1)}, bf16[64,3584]{1,0:T(8,128)(2,1)S(1)}, u32[]{:S(2)}, u32[]{:S(2)}) collective-permute-start(bf16[64,3584]{1,0:T(8,128)(2,1)S(1)} %get-tuple-element.101), channel_id=1, source_target_pairs={{0,2},{1,3},{2,0},{3,1},{4,6},{5,7},{6,4},{7,5},{8,10},{9,11},{10,... | collective-permute-start | bytes 1376264 | tf_op jit(solution)/shard_map/ppermute | solution.py:18
  137.9 12.8 %collective-permute-start.43 = (bf16[64,3584]{1,0:T(8,128)(2,1)S(1)}, bf16[64,3584]{1,0:T(8,128)(2,1)S(1)}, u32[]{:S(2)}, u32[]{:S(2)}) collective-permute-start(bf16[64,3584]{1,0:T(8,128)(2,1)S(1)} %get-tuple-element.122), channel_id=1, source_target_pairs={{0,1},{1,0},{2,3},{3,2},{4,5},{5,4},{6,7},{7,6},{8,9},{9,8},{10,11... | collective-permute-start | bytes 1376264 | tf_op jit(solution)/shard_map/ppermute | solution.py:18
  138.1 12.6 %collective-permute-start.42 = (bf16[64,3584]{1,0:T(8,128)(2,1)S(1)}, bf16[64,3584]{1,0:T(8,128)(2,1)S(1)}, u32[]{:S(2)}, u32[]{:S(2)}) collective-permute-start(bf16[64,3584]{1,0:T(8,128)(2,1)S(1)} %get-tuple-element.120), channel_id=1, source_target_pairs={{0,1},{1,0},{2,3},{3,2},{4,5},{5,4},{6,7},{7,6},{8,9},{9,8},{10,11... | collective-permute-start | bytes 1376264 | tf_op jit(solution)/shard_map/ppermute | solution.py:18
  139.9 11.3 %collective-permute-start.41 = (bf16[64,3584]{1,0:T(8,128)(2,1)S(1)}, bf16[64,3584]{1,0:T(8,128)(2,1)S(1)}, u32[]{:S(2)}, u32[]{:S(2)}) collective-permute-start(bf16[64,3584]{1,0:T(8,128)(2,1)S(1)} %get-tuple-element.118), channel_id=1, source_target_pairs={{0,1},{1,0},{2,3},{3,2},{4,5},{5,4},{6,7},{7,6},{8,9},{9,8},{10,11... | collective-permute-start | bytes 1376264 | tf_op jit(solution)/shard_map/ppermute | solution.py:18
  150.2 2.5 %collective-permute-start.40 = (bf16[64,3584]{1,0:T(8,128)(2,1)S(1)}, bf16[64,3584]{1,0:T(8,128)(2,1)S(1)}, u32[]{:S(2)}, u32[]{:S(2)}) collective-permute-start(bf16[64,3584]{1,0:T(8,128)(2,1)S(1)} %get-tuple-element.115), channel_id=1, source_target_pairs={{0,1},{1,0},{2,3},{3,2},{4,5},{5,4},{6,7},{7,6},{8,9},{9,8},{10,11... | collective-permute-start | bytes 1376264 | tf_op jit(solution)/shard_map/ppermute | solution.py:18
  150.2 2.5 %collective-permute-start.39 = (bf16[64,3584]{1,0:T(8,128)(2,1)S(1)}, bf16[64,3584]{1,0:T(8,128)(2,1)S(1)}, u32[]{:S(2)}, u32[]{:S(2)}) collective-permute-start(bf16[64,3584]{1,0:T(8,128)(2,1)S(1)} %get-tuple-element.113), channel_id=1, source_target_pairs={{0,1},{1,0},{2,3},{3,2},{4,5},{5,4},{6,7},{7,6},{8,9},{9,8},{10,11... | collective-permute-start | bytes 1376264 | tf_op jit(solution)/shard_map/ppermute | solution.py:18
  150.7 2.6 %collective-permute-start.38 = (bf16[64,3584]{1,0:T(8,128)(2,1)S(1)}, bf16[64,3584]{1,0:T(8,128)(2,1)S(1)}, u32[]{:S(2)}, u32[]{:S(2)}) collective-permute-start(bf16[64,3584]{1,0:T(8,128)(2,1)S(1)} %get-tuple-element.111), channel_id=1, source_target_pairs={{0,1},{1,0},{2,3},{3,2},{4,5},{5,4},{6,7},{7,6},{8,9},{9,8},{10,11... | collective-permute-start | bytes 1376264 | tf_op jit(solution)/shard_map/ppermute | solution.py:18
  150.7 3.3 %collective-permute-start.37 = (bf16[64,3584]{1,0:T(8,128)(2,1)S(1)}, bf16[64,3584]{1,0:T(8,128)(2,1)S(1)}, u32[]{:S(2)}, u32[]{:S(2)}) collective-permute-start(bf16[64,3584]{1,0:T(8,128)(2,1)S(1)} %get-tuple-element.109), channel_id=1, source_target_pairs={{0,1},{1,0},{2,3},{3,2},{4,5},{5,4},{6,7},{7,6},{8,9},{9,8},{10,11... | collective-permute-start | bytes 1376264 | tf_op jit(solution)/shard_map/ppermute | solution.py:18
  151.2 12.5 %collective-permute-start.44 = (bf16[64,3584]{1,0:T(8,128)(2,1)S(1)}, bf16[64,3584]{1,0:T(8,128)(2,1)S(1)}, u32[]{:S(2)}, u32[]{:S(2)}) collective-permute-start(bf16[64,3584]{1,0:T(8,128)(2,1)S(1)} %get-tuple-element.124), channel_id=1, source_target_pairs={{0,2},{1,3},{2,0},{3,1},{4,6},{5,7},{6,4},{7,5},{8,10},{9,11},{10,... | collective-permute-start | bytes 1376264 | tf_op jit(solution)/shard_map/ppermute | solution.py:18
  163.7 8.0 %copy-start.1 = (bf16[7168,64]{0,1:T(8,128)(2,1)S(1)}, bf16[7168,64]{0,1:T(8,128)(2,1)}, u32[]{:S(2)}) copy-start(bf16[7168,64]{0,1:T(8,128)(2,1)} %param.10) | copy-start | bytes 2752516
